TPU v7x, 32 devices: a whole 2x2x4 slice. The times are simulated.
32 devices in a mesh: seg: 8 (over z, x), term: 4 (over y, core).
Axes of the slice: x: 2, y: 2, z: 4, core: 2. Of those that a mesh axis runs over, the one named last changes fastest.
Arguments:
- wave_guess: float32 [8, 256, 16, 256], P('seg', 'term'), may hold values from -6 to 6
- left_env: bfloat16 [8, 12, 256, 256], P('seg', 'term'), may hold values from -0.44194174 to 2.6419417, as said below
- right_env: bfloat16 [8, 12, 256, 256], P('seg', 'term'), may hold values from -0.44194174 to 1.2419417, as said below
- site_ops: bfloat16 [8, 12, 16, 16], P('seg', 'term'), may hold values from -0.51031036 to 0.7686437, as said below
- bond_rank: int32 [8], P('seg'), may hold values from 128 to 256, as said below
Outputs:
- ritz_vector: float32 [8, 256, 16, 256], P('seg', 'term')
- energy: float32 [8], P('seg')
Inputs may be any that keep to these rules, and one draw needn't show every extreme that they name: `bond_rank`: the largest rank is 256 in every draw. Every block left_env[s, k] is symmetric. Every block right_env[s, k] is symmetric. Every block site_ops[s, k] is symmetric.
All inputs are finite; a program needn't handle non-finite values.
Results may differ from a plain program's by a relative error of at most 0.005.
Values may be sent and summed in bfloat16 or wider, within the bound.
No kernel may reach another device: no remote copies, remote signals or barrier semaphores. Data moves between devices by JAX's collectives and lax.ppermute only.
A program may use at most 64 MiB of HBM per device.

v0:
```python
import jax
import jax.numpy as jnp
from jax import lax
from jax.sharding import PartitionSpec as P

epsilon = 1e-06


def shifted(block, axis, distance):
    devices = range(lax.axis_size(axis))
    route = [(i - distance, i) for i in devices if i - distance in devices]
    return lax.ppermute(block, axis, route)


def shards(wave_guess, left_env, right_env, site_ops, bond_rank):
    row_count = wave_guess.shape[1]
    local_states = wave_guess.shape[2]
    bond_width = wave_guess.shape[3]
    term_count = left_env.shape[1]
    entry_count = float(row_count * lax.axis_size("term") * local_states * bond_width)
    at_end = lax.axis_index("seg") == lax.axis_size("seg") - 1
    received = shifted(right_env, "seg", -1)
    right_used = jnp.where(at_end, right_env, received)[0]
    left_blocks = left_env[0]
    site_blocks = site_ops[0]
    keep_mask = (lax.iota(jnp.int32, bond_width) < bond_rank[0]).astype(jnp.float32)[None, None, :]

    def spread(piece_bf):
        return lax.all_gather(piece_bf, "term", axis=0, tiled=True)

    def group_rows(full_bf, row_total):
        flat_vector = full_bf.reshape(bond_width, local_states * bond_width)
        running = jnp.zeros((row_total, local_states, bond_width), jnp.float32)
        for term_slot in range(term_count):
            left_rows = left_blocks[term_slot]
            left_mixed = jnp.dot(left_rows, flat_vector, preferred_element_type=jnp.float32).astype(
                jnp.bfloat16
            )
            both_mixed = jnp.dot(
                left_mixed.reshape(row_total * local_states, bond_width),
                right_used[term_slot].T,
                preferred_element_type=jnp.float32,
            ).astype(jnp.bfloat16)
            running = running + jnp.einsum(
                "pq,aqb->apb",
                site_blocks[term_slot],
                both_mixed.reshape(row_total, local_states, bond_width),
                preferred_element_type=jnp.float32,
            )
        return running

    masked = wave_guess[0] * keep_mask
    norm_sq = lax.psum(jnp.sum(masked * masked), "term") / entry_count
    vector_now = masked / jnp.sqrt(norm_sq + epsilon)
    vector_bf = vector_now.astype(jnp.bfloat16)
    full_vector = spread(vector_bf)
    sigma = (
        lax.psum_scatter(
            group_rows(full_vector, lax.axis_size("term") * row_count).astype(jnp.bfloat16),
            "term",
            scatter_dimension=0,
            tiled=True,
        ).astype(jnp.float32)
        * keep_mask
    )
    rayleigh = lax.psum(jnp.sum(vector_now * sigma), "term") / entry_count
    residual = sigma - rayleigh * vector_now
    res_sq = lax.psum(jnp.sum(residual * residual), "term") / entry_count
    res_scale = jnp.sqrt(res_sq + epsilon)
    direction = residual / res_scale
    direction_bf = direction.astype(jnp.bfloat16)
    full_direction = spread(direction_bf)
    partial_value = group_rows(full_direction, bond_width)
    rounded = lax.optimization_barrier(partial_value.astype(jnp.bfloat16)).astype(jnp.float32)
    local_curve = jnp.sum(full_direction.astype(jnp.float32) * keep_mask * rounded)
    curvature = lax.psum(local_curve, "term") / entry_count
    coupling = res_sq / res_scale
    half_gap = 0.5 * (rayleigh - curvature)
    energy = 0.5 * (rayleigh + curvature) - jnp.sqrt(half_gap * half_gap + coupling * coupling)
    coeff_new = energy - rayleigh
    coeff_norm = jnp.sqrt(coupling * coupling + coeff_new * coeff_new + epsilon)
    ritz = (coupling * vector_now + coeff_new * direction) / coeff_norm
    return (ritz[None], energy.reshape(1))


def solution(mesh):
    in_specs = (
        P("seg", "term", None, None),
        P("seg", "term", None, None),
        P("seg", "term", None, None),
        P("seg", "term", None, None),
        P("seg"),
    )
    out_specs = (P("seg", "term", None, None), P("seg"))
    return jax.shard_map(shards, mesh=mesh, in_specs=in_specs, out_specs=out_specs, check_vma=False)
```

profile of v0, /device:TPU:0, one launch (start us, length us, event | category | flops | bytes accessed | tf_op | source)
XLA Modules:
  0.0 222.6 jit_solution(17826545919739028757)
XLA Ops:
  7.2 0.0 copy-start.11
  7.2 0.0 all-gather.3.cloned.1.call-start
  7.9 2.1 multiply_reduce_fusion.3
  10.0 9.0 %psum.28 = f32[]{:T(128)} all-reduce(f32[]{:T(128)} %multiply_reduce_fusion.3), channel_id=1, replica_groups=mesh['seg'=8,'term'=4] {'term'}, use_global_device_ids=true, to_apply=%region_1.2 | all-reduce | flops 1 | bytes 8 | tf_op jit(solution)/shard_map/psum | solution.py:53
  19.7 2.2 fusion.39
  21.8 0.0 all-gather.3.cloned.1.call-update
  21.9 0.0 reduce-scatter.2.cloned.1.call-start
  21.9 0.0 copy-done.11
  21.9 1.3 collective-permute-start
  23.2 10.1 %collective-permute-done = bf16[1,3,256,256]{3,2,1,0:T(8,128)(2,1)S(1)} collective-permute-done((bf16[1,3,256,256]{3,2,1,0:T(8,128)(2,1)S(1)}, bf16[1,3,256,256]{3,2,1,0:T(8,128)(2,1)S(1)}, u32[]{:S(2)}, u32[]{:S(2)}) %collective-permute-start) | collective-permute-done | bytes 393248 | tf_op jit(solution)/shard_map/ppermute | solution.py:12
  33.4 11.5 %all-gather.3.cloned.1.call-done = bf16[256,16,256]{2,1,0:T(8,128)(2,1)} async-done(((bf16[64,16,256]{2,1,0:T(8,128)(2,1)}), bf16[256,16,256]{2,1,0:T(8,128)(2,1)}) %all-gather.3.cloned.1.call-update) | async-done | bytes 2097168 | tf_op jit(solution)/shard_map/all_gather | solution.py:29
  44.9 2.6 %copy.19 = bf16[32,8,16,256]{3,1,2,0:T(8,128)(2,1)S(1)} copy(bf16[32,8,16,256]{3,2,1,0:T(8,128)(2,1)} %bitcast.126) | data formatting | bytes 4194304
  47.5 2.1 fusion.2
  49.6 0.8 fusion.1
  50.4 2.1 fusion
  52.5 4.1 %copy.15 = bf16[256,4096]{1,0:T(8,128)(2,1)} copy(bf16[256,4096]{0,1:T(8,128)(2,1)} %fusion.2) | data formatting | bytes 4194304 | tf_op jit(solution)/shard_map/convert_element_type | solution.py:36
  56.6 4.2 %reshape.77 = bf16[4096,256]{1,0:T(8,128)(2,1)} reshape(bf16[256,4096]{1,0:T(8,128)(2,1)} %copy.15) | data formatting | bytes 4194304 | tf_op jit(solution)/shard_map/reshape | solution.py:40
  60.8 4.1 %copy.13 = bf16[256,4096]{1,0:T(8,128)(2,1)} copy(bf16[256,4096]{0,1:T(8,128)(2,1)} %fusion) | data formatting | bytes 4194304 | tf_op jit(solution)/shard_map/convert_element_type | solution.py:36
  64.9 4.2 %reshape.73 = bf16[4096,256]{1,0:T(8,128)(2,1)} reshape(bf16[256,4096]{1,0:T(8,128)(2,1)} %copy.13) | data formatting | bytes 4194304 | tf_op jit(solution)/shard_map/reshape | solution.py:40
  69.1 3.8 %convolution_convert_fusion.6 = bf16[4096,256]{1,0:T(8,128)(2,1)} fusion(bf16[4096,256]{1,0:T(8,128)(2,1)} %reshape.77, bf16[1,3,256,256]{3,2,1,0:T(8,128)(2,1)S(1)} %broadcast_select_fusion), kind=kOutput, calls=%fused_computation.6 | convolution fusion | flops 537919488 | bytes 4325376 | tf_op jit(solution)/shard_map/dot_general | solution.py:39
  72.9 2.1 convolution_convert_fusion.10
  75.0 2.9 %copy.14 = bf16[256,4096]{1,0:T(8,128)(2,1)} copy(bf16[256,4096]{0,1:T(8,128)(2,1)S(1)} %fusion.1) | data formatting | bytes 4194304 | tf_op jit(solution)/shard_map/convert_element_type | solution.py:36
  77.9 2.9 %reshape.75 = bf16[4096,256]{1,0:T(8,128)(2,1)S(1)} reshape(bf16[256,4096]{1,0:T(8,128)(2,1)} %copy.14) | data formatting | bytes 4194304 | tf_op jit(solution)/shard_map/reshape | solution.py:40
  80.8 0.0 copy-start.12
  80.8 0.7 convolution_convert_fusion.8
  81.6 0.7 fusion.25
  82.2 0.9 copy-done.5
  83.2 0.7 fusion.29
  83.8 0.9 copy-done.3
  84.7 2.0 fusion.6
  86.8 0.0 reduce-scatter.2.cloned.1.call-update
  86.8 0.0 all-gather.5.cloned.1.call-start
  86.8 31.5 %reduce-scatter.2.cloned.1.call-done = bf16[64,16,256]{2,1,0:T(8,128)(2,1)} async-done(((bf16[256,16,256]{2,1,0:T(8,128)(2,1)}), bf16[64,16,256]{2,1,0:T(8,128)(2,1)}) %reduce-scatter.2.cloned.1.call-update) | async-done | bytes 524304 | tf_op jit(solution)/shard_map/reduce_scatter | solution.py:58
  118.4 2.0 multiply_reduce_fusion.2
  120.4 6.4 %psum.29 = f32[]{:T(128)} all-reduce(f32[]{:T(128)} %multiply_reduce_fusion.2), channel_id=1, replica_groups=mesh['seg'=8,'term'=4] {'term'}, use_global_device_ids=true, to_apply=%region_4.5 | all-reduce | flops 1 | bytes 8 | tf_op jit(solution)/shard_map/psum | solution.py:66
  127.4 1.9 multiply_reduce_fusion.1
  129.3 6.4 %psum.30 = f32[]{:T(128)} all-reduce(f32[]{:T(128)} %multiply_reduce_fusion.1), channel_id=1, replica_groups=mesh['seg'=8,'term'=4] {'term'}, use_global_device_ids=true, to_apply=%region_6.7 | all-reduce | flops 1 | bytes 8 | tf_op jit(solution)/shard_map/psum | solution.py:68
  136.5 1.1 fusion.10
  137.5 0.0 all-gather.5.cloned.1.call-update
  137.6 24.0 %all-gather.5.cloned.1.call-done = bf16[256,16,256]{2,1,0:T(8,128)(2,1)} async-done(((bf16[64,16,256]{2,1,0:T(8,128)(2,1)}), bf16[256,16,256]{2,1,0:T(8,128)(2,1)}) %all-gather.5.cloned.1.call-update) | async-done | bytes 2097168 | tf_op jit(solution)/shard_map/all_gather | solution.py:29
  161.6 2.6 %copy.20 = bf16[32,8,16,256]{3,1,2,0:T(8,128)(2,1)S(1)} copy(bf16[32,8,16,256]{3,2,1,0:T(8,128)(2,1)} %bitcast.125) | data formatting | bytes 4194304
  164.2 2.1 fusion.5
  166.3 0.8 fusion.4
  167.0 2.1 fusion.3
  169.1 4.1 %copy.18 = bf16[256,4096]{1,0:T(8,128)(2,1)} copy(bf16[256,4096]{0,1:T(8,128)(2,1)} %fusion.5) | data formatting | bytes 4194304 | tf_op jit(solution)/shard_map/convert_element_type | solution.py:36
  173.3 4.2 %reshape.84 = bf16[4096,256]{1,0:T(8,128)(2,1)} reshape(bf16[256,4096]{1,0:T(8,128)(2,1)} %copy.18) | data formatting | bytes 4194304 | tf_op jit(solution)/shard_map/reshape | solution.py:40
  177.5 3.6 %convolution_convert_fusion = bf16[4096,256]{1,0:T(8,128)(2,1)} fusion(bf16[4096,256]{1,0:T(8,128)(2,1)} %reshape.84, bf16[1,3,256,256]{3,2,1,0:T(8,128)(2,1)S(1)} %broadcast_select_fusion), kind=kOutput, calls=%fused_computation | convolution fusion | flops 537919488 | bytes 4325376 | tf_op jit(solution)/shard_map/dot_general | solution.py:39
  181.1 4.1 %copy.16 = bf16[256,4096]{1,0:T(8,128)(2,1)} copy(bf16[256,4096]{0,1:T(8,128)(2,1)} %fusion.3) | data formatting | bytes 4194304 | tf_op jit(solution)/shard_map/convert_element_type | solution.py:36
  185.3 4.2 %reshape.80 = bf16[4096,256]{1,0:T(8,128)(2,1)} reshape(bf16[256,4096]{1,0:T(8,128)(2,1)} %copy.16) | data formatting | bytes 4194304 | tf_op jit(solution)/shard_map/reshape | solution.py:40
  189.5 3.7 %convolution_convert_fusion.4 = bf16[4096,256]{1,0:T(8,128)(2,1)} fusion(bf16[4096,256]{1,0:T(8,128)(2,1)} %reshape.80, bf16[1,3,256,256]{3,2,1,0:T(8,128)(2,1)S(1)} %broadcast_select_fusion), kind=kOutput, calls=%fused_computation.4 | convolution fusion | flops 537919488 | bytes 4325376 | tf_op jit(solution)/shard_map/dot_general | solution.py:39
  193.2 3.0 %copy.17 = bf16[256,4096]{1,0:T(8,128)(2,1)} copy(bf16[256,4096]{0,1:T(8,128)(2,1)S(1)} %fusion.4) | data formatting | bytes 4194304 | tf_op jit(solution)/shard_map/convert_element_type | solution.py:36
  196.2 2.9 %reshape.82 = bf16[4096,256]{1,0:T(8,128)(2,1)S(1)} reshape(bf16[256,4096]{1,0:T(8,128)(2,1)} %copy.17) | data formatting | bytes 4194304 | tf_op jit(solution)/shard_map/reshape | solution.py:40
  199.1 0.7 convolution_convert_fusion.2
  199.8 0.0 copy-start.4
  199.8 0.7 fusion.27
  200.5 0.9 copy-done.4
  201.4 0.7 fusion.31
  202.1 0.9 copy-done.2
  203.0 0.7 fusion.7
  203.7 0.9 copy-done.6
  204.6 1.7 multiply_reduce_fusion
  206.3 6.5 %psum.31 = f32[]{:T(128)} all-reduce(f32[]{:T(128)} %multiply_reduce_fusion), channel_id=1, replica_groups=mesh['seg'=8,'term'=4] {'term'}, use_global_device_ids=true, to_apply=%region_8.9 | all-reduce | flops 1 | bytes 8 | tf_op jit(solution)/shard_map/psum | solution.py:76
  213.6 0.0 copy-done.8
  213.6 1.4 divide_bitcast_fusion
  (18 shorter events, 0.1 us)
Async XLA Ops:
  7.2 14.8 %copy-start.11 = (bf16[1,3,256,256]{3,2,1,0:T(8,128)(2,1)S(1)}, bf16[1,3,256,256]{3,2,1,0:T(8,128)(2,1)}, u32[]{:S(2)}) copy-start(bf16[1,3,256,256]{3,2,1,0:T(8,128)(2,1)} %param.7) | copy-start | bytes 1179652
  7.2 37.7 %all-gather.3.cloned.1.call-start = ((), (), s32[]{:S(2)}) async-start(), calls=%async_computation.1 | async-start | bytes 2621440 | tf_op jit(solution)/shard_map/all_gather | solution.py:29
  21.9 96.5 %reduce-scatter.2.cloned.1.call-start = ((), (), s32[]{:S(2)}) async-start(), calls=%async_computation.2 | async-start | bytes 2621440 | tf_op jit(solution)/shard_map/reduce_scatter | solution.py:58
  21.9 11.4 %collective-permute-start = (bf16[1,3,256,256]{3,2,1,0:T(8,128)(2,1)S(1)}, bf16[1,3,256,256]{3,2,1,0:T(8,128)(2,1)S(1)}, u32[]{:S(2)}, u32[]{:S(2)}) collective-permute-start(bf16[1,3,256,256]{3,2,1,0:T(8,128)(2,1)S(1)} %copy-done.11), channel_id=1, source_target_pairs={{4,0},{8,4},{12,8},{16,12},{20,16},{24,20},{28,24},{5,1},{9,5},{13... | collective-permute-start | bytes 1179656 | tf_op jit(solution)/shard_map/ppermute | solution.py:12
  44.9 2.6 %copy-start.9 = (bf16[1,3,256,256]{3,2,1,0:T(8,128)(2,1)S(1)}, bf16[1,3,256,256]{3,2,1,0:T(8,128)(2,1)}, u32[]{:S(2)}) copy-start(bf16[1,3,256,256]{3,2,1,0:T(8,128)(2,1)} %param.6) | copy-start | bytes 1179652
  69.1 3.8 %copy-start.1 = (bf16[4096,256]{1,0:T(8,128)(2,1)S(1)}, bf16[4096,256]{1,0:T(8,128)(2,1)}, u32[]{:S(2)}) copy-start(bf16[4096,256]{1,0:T(8,128)(2,1)} %reshape.73) | copy-start | bytes 6291460
  80.8 0.8 copy-start.12
  81.6 1.6 copy-start.5
  83.1 1.6 copy-start.3
  86.8 31.6 %copy-start = (f32[1,64,16,256]{3,2,1,0:T(8,128)S(1)}, f32[1,64,16,256]{3,2,1,0:T(8,128)}, u32[]{:S(2)}) copy-start(f32[1,64,16,256]{3,2,1,0:T(8,128)} %param.5) | copy-start | bytes 3145732
  86.8 74.8 %all-gather.5.cloned.1.call-start = ((), (), s32[]{:S(2)}) async-start(), calls=%async_computation.3 | async-start | bytes 2621440 | tf_op jit(solution)/shard_map/all_gather | solution.py:29
  118.4 18.1 %copy-start.7 = (bf16[64,16,256]{2,1,0:T(8,128)(2,1)S(1)}, bf16[64,16,256]{2,1,0:T(8,128)(2,1)}, u32[]{:S(2)}) copy-start(bf16[64,16,256]{2,1,0:T(8,128)(2,1)} %reduce-scatter.2.cloned.1.call-done) | copy-start | bytes 1572868
  161.6 2.6 %copy-start.10 = (bf16[1,3,256,256]{3,2,1,0:T(8,128)(2,1)S(1)}, bf16[1,3,256,256]{3,2,1,0:T(8,128)(2,1)}, u32[]{:S(2)}) copy-start(bf16[1,3,256,256]{3,2,1,0:T(8,128)(2,1)} %param.6) | copy-start | bytes 1179652
  199.8 1.6 copy-start.4
  201.4 1.6 copy-start.2
  203.0 1.6 copy-start.6
  204.6 8.9 %copy-start.8 = (bf16[64,16,256]{2,1,0:T(8,128)(2,1)S(1)}, bf16[64,16,256]{2,1,0:T(8,128)(2,1)}, u32[]{:S(2)}) copy-start(bf16[64,16,256]{2,1,0:T(8,128)(2,1)} %reduce-scatter.2.cloned.1.call-done) | copy-start | bytes 1572868
Sparse Core Ops, SparseCore 0:
  22.0 22.8 all-gather.2
  86.9 31.4 reduce-scatter.1
  137.7 23.9 all-gather.4
where the time goes:
time: 224 us; the launch traced here: 223 us
  waiting for transfers between devices  77.2 us (34%)
  local copies, waits for them, and re-layouts  54.8 us (24%)
  matrix products  29.9 us (13%)
  blocking collectives  28.3 us (13%)
  between operations  18.6 us (8%)
  other arithmetic  12.3 us (5%)
    all_gather x2, waiting for transfers between devices, spread(): return lax.all_gather(piece_bf, 'term', axis=0, tiled=True)  35.6 us
    reduce_scatter x1, waiting for transfers between devices, shards(): lax.psum_scatter(group_rows(full_vector, lax.axis_size('term') * row_coun...  31.5 us
    reshape x6, local copies, waits for them, and re-layouts, group_rows(): left_mixed.reshape(row_total * local_states, bond_width)  22.6 us
    convert_element_type x6, local copies, waits for them, and re-layouts, group_rows(): jnp.dot(left_rows, flat_vector, preferred_element_type=jnp.float32)  22.5 us
    dot_general x6, matrix products, group_rows(): jnp.dot(left_mixed.reshape(row_total * local_states, bond_width), right_u...  14.6 us
    ppermute x1, waiting for transfers between devices, shifted(): return lax.ppermute(block, axis, route)  10.1 us
    dot_general x6, matrix products, group_rows(): jnp.dot(left_rows, flat_vector, preferred_element_type=jnp.float32)  9.86 us
    unnamed x28, local copies, waits for them, and re-layouts  9.73 us
  transfers between devices with their start and end apart: 4, of which 4 were waited for; matrix products, arithmetic and copies ran while one was open for 0% of the time, Pallas kernels for 0%

commit v1 on v0

v1 whole, which is shorter than its diff:
```python
import functools

import jax
import jax.numpy as jnp
from jax import lax
from jax.experimental import pallas as pl
from jax.experimental.pallas import tpu as pltpu
from jax.sharding import PartitionSpec as P

epsilon = 1e-06
CORES = 2
TILE = 16
VMEM_LIMIT = 56 * 1024 * 1024
F32 = jnp.float32
BF16 = jnp.bfloat16

vmem = pl.BlockSpec(memory_space=pltpu.VMEM)
smem = pl.BlockSpec(memory_space=pltpu.SMEM)
anywhere = pl.BlockSpec(memory_space=pl.ANY)


def params():
    return pltpu.CompilerParams(vmem_limit_bytes=VMEM_LIMIT)


def cost(flops, moved):
    return pl.CostEstimate(flops=int(flops), bytes_accessed=int(moved), transcendentals=0)


def keep_row(rank, width):
    return (lax.broadcasted_iota(jnp.int32, (1, width), 1) < rank).astype(F32)


def prepare_kernel(rank_ref, guess_ref, x_ref, norm_ref):
    rows, states, width = guess_ref.shape
    masked = guess_ref[...] * keep_row(rank_ref[0], width)[None]
    norm_ref[...] = jnp.full(norm_ref.shape, jnp.sum(masked * masked), F32)
    x_ref[...] = jnp.swapaxes(masked, 0, 1).astype(BF16)


def spread_site(site_ref, kron_ref):
    terms, states, _ = site_ref.shape
    size = states * TILE
    row_state = lax.broadcasted_iota(jnp.int32, (size, states), 0) // TILE
    pick = (row_state == lax.broadcasted_iota(jnp.int32, (size, states), 1)).astype(BF16)
    col_state = lax.broadcasted_iota(jnp.int32, (states, size), 1) // TILE
    pick_t = (col_state == lax.broadcasted_iota(jnp.int32, (states, size), 0)).astype(BF16)
    same = (
        lax.broadcasted_iota(jnp.int32, (size, size), 0) % TILE
        == lax.broadcasted_iota(jnp.int32, (size, size), 1) % TILE
    )
    for k in range(terms):
        tall = jnp.dot(pick, site_ref[k], preferred_element_type=F32).astype(BF16)
        full = jnp.dot(tall, pick_t, preferred_element_type=F32)
        kron_ref[:, k * size : (k + 1) * size] = jnp.where(same, full, 0.0).astype(BF16)


def mix_bonds(block, left_ref, right_ref, both_ref, p):
    terms, width, _ = left_ref.shape
    mixed = jnp.dot(
        left_ref[...].reshape(terms * width, width), block, preferred_element_type=F32
    ).astype(BF16)
    for k in range(terms):
        both_ref[k, p] = jnp.dot(
            mixed[k * width : (k + 1) * width], right_ref[k], preferred_element_type=F32
        ).astype(BF16)


def mix_sites(both_ref, kron_ref, i):
    terms, states, _, width = both_ref.shape
    at = pl.multiple_of(i * TILE, TILE)
    stack = both_ref[:, :, pl.ds(at, TILE), :].reshape(terms * states * TILE, width)
    return jnp.dot(kron_ref[...], stack, preferred_element_type=F32).reshape(states, TILE, width)


def place_pieces(pieces, hops, whole_ref, sems):
    chips = len(hops)
    me = lax.axis_index("term")
    core = me % CORES
    chip = me // CORES
    copies = []
    for n, piece in enumerate(pieces):
        hop = hops[n // 2]
        owner = ((chip - hop + chips) % chips) * CORES + (core if n % 2 == 0 else 1 - core)
        rows = piece.shape[1]
        at = pl.multiple_of(owner * rows, TILE)
        copies.append(pltpu.make_async_copy(piece, whole_ref.at[:, pl.ds(at, rows), :], sems.at[n]))
    for copy in copies:
        copy.start()
    return copies


def apply_kernel(piece_count, hops, *refs):
    pieces = refs[:piece_count]
    left_ref, right_ref, site_ref, partial_ref, stat_ref, whole_ref, both_ref, kron_ref, sems = refs[piece_count:]
    states, width, _ = whole_ref.shape
    copies = place_pieces(pieces, hops, whole_ref, sems)
    spread_site(site_ref, kron_ref)
    for copy in copies:
        copy.wait()

    def bonds(p, carry):
        mix_bonds(whole_ref[p], left_ref, right_ref, both_ref, p)
        return carry

    lax.fori_loop(0, states, bonds, 0, unroll=2)

    def sites(i, total):
        part = mix_sites(both_ref, kron_ref, i).astype(BF16)
        at = pl.multiple_of(i * TILE, TILE)
        partial_ref[:, pl.ds(at, TILE), :] = part
        held = whole_ref[:, pl.ds(at, TILE), :].astype(F32)
        return total + jnp.sum((held * part.astype(F32)).reshape(states * TILE // 8, 8, width), axis=0)

    total = lax.fori_loop(0, width // TILE, sites, jnp.zeros((8, width), F32), unroll=2)
    stat_ref[...] = jnp.full(stat_ref.shape, jnp.sum(total), F32)


def second_kernel(group_count, hops, scale, *refs):
    groups = refs[:group_count]
    stats = refs[group_count : 2 * group_count]
    pieces = refs[2 * group_count : 3 * group_count]
    rest = refs[3 * group_count :]
    (rank_ref, norm_ref, left_ref, right_ref, site_ref, sigma_ref, out_ref) = rest[:7]
    (whole_ref, group_buf, res_ref, both_ref, kron_ref, sems, group_sems) = rest[7:]
    states, width, _ = whole_ref.shape
    rows = sigma_ref.shape[1]
    copies = place_pieces(pieces, hops, whole_ref, sems)
    for p in range(states):
        for g in range(group_count):
            pltpu.make_async_copy(groups[g].at[p], group_buf.at[g, p], group_sems.at[g, p]).start()
    spread_site(site_ref, kron_ref)
    keep = keep_row(rank_ref[0], width)
    inverse = lax.rsqrt(norm_ref[0:1, :] * scale + epsilon)

    def summed(values):
        evens = functools.reduce(jnp.add, values[0::2])
        odds = functools.reduce(jnp.add, values[1::2])
        return evens + odds

    rayleigh = summed([s[0:1, :] for s in stats]) * (inverse * inverse * scale)
    row_scale = keep * inverse
    me = lax.axis_index("term")
    own = pl.multiple_of(me * rows, TILE)
    for copy in copies:
        copy.wait()

    def bonds(p, total):
        for g in range(group_count):
            pltpu.make_async_copy(groups[g].at[p], group_buf.at[g, p], group_sems.at[g, p]).wait()
        sigma = summed([group_buf[g, p].astype(F32) for g in range(group_count)]) * row_scale
        residual = sigma - (rayleigh * inverse) * whole_ref[p].astype(F32)
        rounded = residual.astype(BF16)
        res_ref[p] = rounded
        mine = summed([group_buf[g, p, pl.ds(own, rows), :].astype(F32) for g in range(group_count)])
        sigma_ref[p] = mine * row_scale
        mix_bonds(rounded, left_ref, right_ref, both_ref, p)
        return total + jnp.sum((residual * residual).reshape(width // 8, 8, width), axis=0)

    square = lax.fori_loop(0, states, bonds, jnp.zeros((8, width), F32))

    def sites(i, total):
        image = mix_sites(both_ref, kron_ref, i)
        at = pl.multiple_of(i * TILE, TILE)
        held = res_ref[:, pl.ds(at, TILE), :].astype(F32)
        return total + jnp.sum((held * image).reshape(states * TILE // 8, 8, width), axis=0)

    cross = lax.fori_loop(0, width // TILE, sites, jnp.zeros((8, width), F32), unroll=2)
    share = 1.0 / group_count
    out_ref[0:1, :] = rayleigh * share
    out_ref[1:2, :] = jnp.full((1, width), jnp.sum(square) * (scale * share), F32)
    out_ref[2:3, :] = jnp.full((1, width), jnp.sum(cross) * scale, F32)
    out_ref[3:8, :] = jnp.zeros((5, width), F32)


def finish_kernel(scale, rank_ref, guess_ref, sigma_ref, stat_ref, norm_ref, ritz_ref, energy_ref):
    rows, states, width = guess_ref.shape
    inverse = lax.rsqrt(norm_ref[0:1, :] * scale + epsilon)
    rayleigh = stat_ref[0:1, :]
    res_sq = stat_ref[1:2, :]
    res_var = res_sq + epsilon
    curvature = stat_ref[2:3, :] / res_var
    res_scale = jnp.sqrt(res_var)
    coupling = res_sq / res_scale
    half_gap = 0.5 * (rayleigh - curvature)
    energy = 0.5 * (rayleigh + curvature) - jnp.sqrt(half_gap * half_gap + coupling * coupling)
    coeff_new = energy - rayleigh
    coeff_norm = jnp.sqrt(coupling * coupling + coeff_new * coeff_new + epsilon)
    old = coupling / coeff_norm
    new = coeff_new / (coeff_norm * res_scale)
    vector = guess_ref[...] * (keep_row(rank_ref[0], width) * inverse)[None]
    sigma = jnp.swapaxes(sigma_ref[...], 0, 1)
    ritz_ref[...] = old[None] * vector + new[None] * (sigma - rayleigh[None] * vector)
    energy_ref[0] = energy[0, 0]


def shards(wave_guess, left_env, right_env, site_ops, bond_rank):
    guess = wave_guess[0]
    left = left_env[0]
    site = site_ops[0]
    rows, states, width = guess.shape
    terms = left.shape[0]
    members = lax.axis_size("term")
    chips = members // CORES
    segments = lax.axis_size("seg")
    scale = 1.0 / float(rows * members * states * width)
    hops = tuple(range(chips))

    def to_sibling(block):
        return lax.ppermute(block, "term", [(i, i ^ 1) for i in range(members)])

    def to_next_chip(block):
        return lax.ppermute(block, "term", [(i, (i + CORES) % members) for i in range(members)])

    def around(block):
        found = [block]
        for _ in range(chips - 1):
            found.append(to_next_chip(found[-1]))
        return found

    def total(block):
        bit = 1
        while bit < members:
            block = block + lax.ppermute(block, "term", [(i, i ^ bit) for i in range(members)])
            bit *= 2
        return block

    tile = jax.ShapeDtypeStruct((8, width), F32)
    x_own, norm_part = pl.pallas_call(
        prepare_kernel,
        out_shape=(jax.ShapeDtypeStruct((states, rows, width), BF16), tile),
        in_specs=[smem, vmem],
        out_specs=(vmem, vmem),
        compiler_params=params(),
        cost_estimate=cost(4 * guess.size, 6 * guess.size),
        name="prepare",
    )(bond_rank, guess)

    shift = [(i + 1, i) for i in range(segments - 1)]
    received = lax.ppermute(right_env, "seg", shift)
    right = jnp.where(lax.axis_index("seg") == segments - 1, right_env, received)[0]

    x_hops = around(x_own)
    pieces = []
    for block in x_hops:
        pieces += [block, to_sibling(block)]
    norm = total(norm_part)

    left_hops = around(left)
    right_hops = around(right)
    site_hops = around(site)

    whole = (states, width, width)
    both = (terms, states, width, width)
    kron = (states * TILE, terms * states * TILE)
    apply_flops = 2 * terms * states * width * width * (2 * width + states * TILE)
    apply_call = pl.pallas_call(
        functools.partial(apply_kernel, members, hops),
        out_shape=(jax.ShapeDtypeStruct(whole, BF16), tile),
        in_specs=[anywhere] * members + [vmem] * 3,
        out_specs=(vmem, vmem),
        scratch_shapes=[
            pltpu.VMEM(whole, BF16),
            pltpu.VMEM(both, BF16),
            pltpu.VMEM(kron, BF16),
            pltpu.SemaphoreType.DMA((members,)),
        ],
        compiler_params=params(),
        cost_estimate=cost(apply_flops, 4 * states * width * width),
        name="apply_terms",
    )

    groups = []
    stats = []
    for hop in hops:
        partial, stat = apply_call(*pieces, left_hops[hop], right_hops[hop], site_hops[hop])
        groups += [partial, to_sibling(partial)]
        stats += [stat, to_sibling(stat)]

    sigma_own, share = pl.pallas_call(
        functools.partial(second_kernel, members, hops, scale),
        out_shape=(jax.ShapeDtypeStruct((states, rows, width), F32), tile),
        in_specs=[anywhere] * members + [vmem] * members + [anywhere] * members + [smem] + [vmem] * 4,
        out_specs=(vmem, vmem),
        scratch_shapes=[
            pltpu.VMEM(whole, BF16),
            pltpu.VMEM((members,) + whole, BF16),
            pltpu.VMEM(whole, BF16),
            pltpu.VMEM(both, BF16),
            pltpu.VMEM(kron, BF16),
            pltpu.SemaphoreType.DMA((members,)),
            pltpu.SemaphoreType.DMA((members, states)),
        ],
        compiler_params=params(),
        cost_estimate=cost(apply_flops, 2 * members * states * width * width),
        name="apply_residual",
    )(*groups, *stats, *pieces, bond_rank, norm, left, right, site)

    ritz, energy = pl.pallas_call(
        functools.partial(finish_kernel, scale),
        out_shape=(jax.ShapeDtypeStruct((rows, states, width), F32), jax.ShapeDtypeStruct((1,), F32)),
        in_specs=[smem] + [vmem] * 4,
        out_specs=(vmem, smem),
        compiler_params=params(),
        cost_estimate=cost(4 * guess.size, 12 * guess.size),
        name="finish",
    )(bond_rank, guess, sigma_own, total(share), norm)
    return (ritz[None], energy)


def solution(mesh):
    in_specs = (
        P("seg", "term", None, None),
        P("seg", "term", None, None),
        P("seg", "term", None, None),
        P("seg", "term", None, None),
        P("seg"),
    )
    out_specs = (P("seg", "term", None, None), P("seg"))
    return jax.shard_map(shards, mesh=mesh, in_specs=in_specs, out_specs=out_specs, check_vma=False)
```

time: 224 us -> 93.8 us (0.42)
  waiting for transfers between devices: 77.2 us -> 24.5 us
  Pallas kernels: 0 us -> 49.9 us
  local copies, waits for them, and re-layouts: 54.8 us -> 5.09 us
  matrix products: 29.9 us -> 0 us
  blocking collectives: 28.3 us -> 0 us
  between operations: 18.6 us -> 1.48 us
  other arithmetic: 12.3 us -> 1.95 us
  starting transfers between devices: 1.41 us -> 10.5 us
    pallas_call x0 -> x5, Pallas kernels: none -> 49.9 us  [the longest x2 25.1 us: shards(): apply_call(*pieces, left_hops[hop], right_hops[hop], site_hops[hop])]
    all_gather x2 -> x0, waiting for transfers between devices: 35.6 us -> none  [spread(): return lax.all_gather(piece_bf, 'term', axis=0, tiled=True)]
    reduce_scatter x1 -> x0, waiting for transfers between devices: 31.5 us -> none  [shards(): lax.psum_scatter(group_rows(full_vector, lax.axis_size('term') * row_coun...]
    dot_general x18 -> x0, matrix products: 29.9 us -> none  [the longest x6 14.6 us: group_rows(): jnp.dot(left_mixed.reshape(row_total * local_states, bond_width), right_u...]
    psum x4 -> x0, blocking collectives: 28.3 us -> none  [the longest x1 8.97 us: shards(): norm_sq = lax.psum(jnp.sum(masked * masked), 'term') / entry_count]
    reshape x6 -> x0, local copies, waits for them, and re-layouts: 22.6 us -> none  [group_rows(): left_mixed.reshape(row_total * local_states, bond_width)]
    convert_element_type x6 -> x0, local copies, waits for them, and re-layouts: 22.5 us -> none  [group_rows(): jnp.dot(left_rows, flat_vector, preferred_element_type=jnp.float32)]
    ppermute x1 -> x15, waiting for transfers between devices: 10.1 us -> 24.5 us  [the longest x4 14.1 us: to_next_chip(): lax.ppermute(block, 'term', [(i, (i + CORES) % members) for i in range(me...]
  transfers between devices with their start and end apart: 4 -> 15, of which waited for: 4 -> 6; matrix products, arithmetic and copies ran while one was open for 0% -> 1% of each run, Pallas kernels for 0% -> 27%
where the time goes in v1:
time: 93.8 us; the launch traced here: 93.4 us
  Pallas kernels  49.9 us (53%)
  waiting for transfers between devices  24.5 us (26%)
  starting transfers between devices  10.5 us (11%)
  local copies, waits for them, and re-layouts  5.09 us (5%)
  other arithmetic  1.95 us (2%)
  between operations  1.48 us (2%)
    pallas_call x2, Pallas kernels, shards(): apply_call(*pieces, left_hops[hop], right_hops[hop], site_hops[hop])  25.1 us
    pallas_call x1, Pallas kernels, shards(): pl.pallas_call(functools.partial(second_kernel, members, hops, scale), ou...  19 us
    ppermute x4, waiting for transfers between devices, to_next_chip(): lax.ppermute(block, 'term', [(i, (i + CORES) % members) for i in range(me...  14.1 us
    ppermute x4, waiting for transfers between devices, total(): lax.ppermute(block, 'term', [(i, i ^ bit) for i in range(members)])  10.3 us
    ppermute x4, starting transfers between devices, to_next_chip(): lax.ppermute(block, 'term', [(i, (i + CORES) % members) for i in range(me...  6.83 us
    unnamed x26, local copies, waits for them, and re-layouts  5.09 us
    pallas_call x1, Pallas kernels, shards(): pl.pallas_call(functools.partial(finish_kernel, scale), out_shape=(jax.Sh...  3.15 us
    pallas_call x1, Pallas kernels, shards(): pl.pallas_call(prepare_kernel, out_shape=(jax.ShapeDtypeStruct((states, r...  2.55 us
  transfers between devices with their start and end apart: 15, of which 6 were waited for; matrix products, arithmetic and copies ran while one was open for 1% of the time, Pallas kernels for 27%

profile of v1, /device:TPU:0, one launch (start us, length us, event | category | flops | bytes accessed | tf_op | source)
XLA Modules:
  0.0 93.4 jit_solution(5858368136279623073)
XLA Ops:
  1.3 2.5 %prepare.1 = (bf16[16,64,256]{2,1,0:T(8,128)(2,1)}, f32[8,256]{1,0:T(8,128)}) custom-call(s32[1]{0:T(128)S(6)} %copy.7.rank_ref.refs_12_, f32[64,16,256]{2,1,0:T(8,128)} %bitcast.6), custom_call_target="tpu_custom_call" | custom-call | flops 1048576 | bytes 1572864 | tf_op jit(solution)/shard_map/prepare/pallas_call | solution.py:229
  3.8 3.0 %collective-permute-start.1 = (bf16[16,64,256]{2,1,0:T(8,128)(2,1)}, bf16[16,64,256]{2,1,0:T(8,128)(2,1)S(1)}, u32[]{:S(2)}, u32[]{:S(2)}) collective-permute-start(bf16[16,64,256]{2,1,0:T(8,128)(2,1)} %get-tuple-element.12.refs_0_.refs_8_), channel_id=1, source_target_pairs={{0,2},{1,3},{2,0},{3,1},{4,6},{5,7},{6,4},{7,5},{8,10},{9,11},{10,... | collective-permute-start | bytes 1572872 | tf_op jit(solution)/shard_map/ppermute | solution.py:213
  6.8 1.3 %collective-permute-start.3 = (bf16[1,3,256,256]{3,2,1,0:T(8,128)(2,1)}, bf16[1,3,256,256]{3,2,1,0:T(8,128)(2,1)S(1)}, u32[]{:S(2)}, u32[]{:S(2)}) collective-permute-start(bf16[1,3,256,256]{3,2,1,0:T(8,128)(2,1)} %param.7), channel_id=1, source_target_pairs={{4,0},{8,4},{12,8},{16,12},{20,16},{24,20},{28,24},{5,1},{9,5},{13... | collective-permute-start | bytes 1179656 | tf_op jit(solution)/shard_map/ppermute | solution.py:240
  8.1 0.1 collective-permute-start
  8.2 10.8 %collective-permute-done.1.refs_2_.refs_10_ = bf16[16,64,256]{2,1,0:T(8,128)(2,1)S(1)} collective-permute-done((bf16[16,64,256]{2,1,0:T(8,128)(2,1)}, bf16[16,64,256]{2,1,0:T(8,128)(2,1)S(1)}, u32[]{:S(2)}, u32[]{:S(2)}) %collective-permute-start.1) | collective-permute-done | bytes 524320 | tf_op jit(solution)/shard_map/ppermute | solution.py:213
  18.9 0.0 copy-start.4
  18.9 0.0 collective-permute-start.2
  18.9 1.7 %collective-permute-start.7 = (bf16[3,16,16]{2,1,0:T(8,128)(2,1)}, bf16[3,16,16]{2,1,0:T(8,128)(2,1)S(1)}, u32[]{:S(2)}, u32[]{:S(2)}) collective-permute-start(bf16[3,16,16]{2,1,0:T(8,128)(2,1)} %bitcast.12), channel_id=1, source_target_pairs={{0,2},{1,3},{2,0},{3,1},{4,6},{5,7},{6,4},{7,5},{8,10},{9,11},{10,... | collective-permute-start | bytes 4616 | tf_op jit(solution)/shard_map/ppermute | solution.py:213
  20.7 0.3 collective-permute-start.5
  21.0 0.0 collective-permute-done.3
  21.0 0.0 copy-start
  21.0 1.8 %collective-permute-start.6 = (bf16[3,256,256]{2,1,0:T(8,128)(2,1)S(1)}, bf16[3,256,256]{2,1,0:T(8,128)(2,1)S(1)}, u32[]{:S(2)}, u32[]{:S(2)}) collective-permute-start(bf16[3,256,256]{2,1,0:T(8,128)(2,1)S(1)} %select_bitcast_fusion.refs_5_.refs_15_), channel_id=1, source_target_pairs={{0,2},{1,3},{2,0},{3,1},{4,6},{5,7},{6,4},{7,5},{8,10},{9,11},{10,... | collective-permute-start | bytes 1179656 | tf_op jit(solution)/shard_map/ppermute | solution.py:213
  22.9 0.0 collective-permute-done.refs_1_.refs_9_
  22.9 0.0 copy-start.5
  22.9 0.0 collective-permute-done.2.refs_3_.refs_11_
  22.9 0.0 copy-done.4
  22.9 0.0 copy-done
  22.9 0.8 copy-done.5
  23.6 0.0 copy-start.6
  23.6 0.8 copy-done.6
  24.5 12.6 %apply_terms.2 = (bf16[16,256,256]{2,1,0:T(8,128)(2,1)}, f32[8,256]{1,0:T(8,128)}) custom-call(bf16[16,64,256]{2,1,0:T(8,128)(2,1)} %get-tuple-element.12.refs_0_.refs_8_, bf16[16,64,256]{2,1,0:T(8,128)(2,1)} %copy-done.5, bf16[16,64,256]{2,1,0:T(8,128)(2,1)} %copy-done.4, bf16[16,64,256]{2,1,0:T(8,128)(2,1)} %copy-done.6, bf16[3,256,256]{2,1,0:T(8,128)(2,1)} %bitcast.10, ...), custom_call_target="tpu_custom_call" | custom-call | flops 4831838208 | bytes 4194304 | tf_op jit(solution)/shard_map/apply_terms/pallas_call | solution.py:276
  37.0 0.0 copy-start.1
  37.1 0.0 copy-start.10
  37.1 0.1 collective-permute-start.4
  37.1 0.0 collective-permute-done.7.refs_6_
  37.2 0.0 copy-start.9
  37.2 0.0 collective-permute-done.5.refs_4_
  37.2 0.0 copy-start.7
  37.2 3.4 %collective-permute-done.6.refs_5_ = bf16[3,256,256]{2,1,0:T(8,128)(2,1)S(1)} collective-permute-done((bf16[3,256,256]{2,1,0:T(8,128)(2,1)S(1)}, bf16[3,256,256]{2,1,0:T(8,128)(2,1)S(1)}, u32[]{:S(2)}, u32[]{:S(2)}) %collective-permute-start.6) | collective-permute-done | bytes 393248 | tf_op jit(solution)/shard_map/ppermute | solution.py:213
  40.6 0.0 copy-done.9
  40.6 0.0 copy-done.7
  40.6 0.0 copy-start.8
  40.6 0.8 copy-done.8
  41.3 12.5 %apply_terms.3 = (bf16[16,256,256]{2,1,0:T(8,128)(2,1)}, f32[8,256]{1,0:T(8,128)}) custom-call(bf16[16,64,256]{2,1,0:T(8,128)(2,1)} %get-tuple-element.12.refs_0_.refs_8_, bf16[16,64,256]{2,1,0:T(8,128)(2,1)} %copy-done.5, bf16[16,64,256]{2,1,0:T(8,128)(2,1)} %copy-done.4, bf16[16,64,256]{2,1,0:T(8,128)(2,1)} %copy-done.6, bf16[3,256,256]{2,1,0:T(8,128)(2,1)} %copy-done.7, ...), custom_call_target="tpu_custom_call" | custom-call | flops 4831838208 | bytes 4194304 | tf_op jit(solution)/shard_map/apply_terms/pallas_call | solution.py:276
  53.9 0.1 collective-permute-start.8
  54.0 0.0 copy-done.1
  54.0 0.5 collective-permute-start.11
  54.5 3.3 %collective-permute-done.11 = f32[8,256]{1,0:T(8,128)S(1)} collective-permute-done((f32[8,256]{1,0:T(8,128)S(1)}, f32[8,256]{1,0:T(8,128)S(1)}, u32[]{:S(2)}, u32[]{:S(2)}) %collective-permute-start.11) | collective-permute-done | bytes 8224 | tf_op jit(solution)/shard_map/ppermute | solution.py:224
  57.7 0.6 collective-permute-start.12
  58.3 0.1 collective-permute-start.10
  58.4 0.0 copy-done.10
  58.4 0.4 collective-permute-start.9
  58.8 2.6 %collective-permute-done.12 = f32[8,256]{1,0:T(8,128)S(1)} collective-permute-done((f32[8,256]{1,0:T(8,128)S(1)}, f32[8,256]{1,0:T(8,128)S(1)}, u32[]{:S(2)}, u32[]{:S(2)}) %collective-permute-start.12) | collective-permute-done | bytes 8224 | tf_op jit(solution)/shard_map/ppermute | solution.py:224
  61.4 0.6 add.13.refs_13_.norm_ref
  62.0 0.0 collective-permute-done.10.refs_7_
  62.0 0.0 copy-start.11
  62.0 0.0 collective-permute-done.9.refs_5_
  62.0 0.0 copy-start.12
  62.0 0.0 collective-permute-done.4.refs_1_
  62.0 0.0 copy-start.2
  62.1 0.0 collective-permute-done.8.refs_3_
  62.1 0.5 copy-done.11
  62.6 0.0 copy-done.12
  62.6 0.8 copy-done.2
  63.4 0.0 copy-start.3
  63.4 1.4 %copy-done.3 = bf16[16,256,256]{2,1,0:T(8,128)(2,1)} copy-done((bf16[16,256,256]{2,1,0:T(8,128)(2,1)}, bf16[16,256,256]{2,1,0:T(8,128)(2,1)S(1)}, u32[]{:S(2)}) %copy-start.3) | copy-done | bytes 2097176
  64.8 19.0 %apply_residual.1 = (f32[16,64,256]{2,1,0:T(8,128)}, f32[8,256]{1,0:T(8,128)}) custom-call(bf16[16,256,256]{2,1,0:T(8,128)(2,1)} %get-tuple-element.13.refs_0_, bf16[16,256,256]{2,1,0:T(8,128)(2,1)} %copy-done.2, bf16[16,256,256]{2,1,0:T(8,128)(2,1)} %get-tuple-element.14.refs_2_, bf16[16,256,256]{2,1,0:T(8,128)(2,1)} %copy-done.3, ...), custom_call_target="tpu_custom_call" | custom-call | flops 4831838208 | bytes 8388608 | tf_op jit(solution)/shard_map/apply_residual/pallas_call | solution.py:280
  83.9 0.1 collective-permute-start.13
  83.9 1.4 %collective-permute-done.13 = f32[8,256]{1,0:T(8,128)S(1)} collective-permute-done((f32[8,256]{1,0:T(8,128)}, f32[8,256]{1,0:T(8,128)S(1)}, u32[]{:S(2)}, u32[]{:S(2)}) %collective-permute-start.13) | collective-permute-done | bytes 8224 | tf_op jit(solution)/shard_map/ppermute | solution.py:224
  85.3 0.7 add.14
  86.0 0.6 collective-permute-start.14
  86.6 3.1 %collective-permute-done.14 = f32[8,256]{1,0:T(8,128)S(1)} collective-permute-done((f32[8,256]{1,0:T(8,128)S(1)}, f32[8,256]{1,0:T(8,128)S(1)}, u32[]{:S(2)}, u32[]{:S(2)}) %collective-permute-start.14) | collective-permute-done | bytes 8224 | tf_op jit(solution)/shard_map/ppermute | solution.py:224
  89.7 0.6 add.15.stat_ref
  90.2 3.1 %finish.1 = (f32[64,16,256]{2,1,0:T(8,128)}, f32[1]{0:T(128)}) custom-call(s32[1]{0:T(128)S(6)} %copy.7.rank_ref.refs_12_, f32[64,16,256]{2,1,0:T(8,128)} %bitcast.7, f32[16,64,256]{2,1,0:T(8,128)} %get-tuple-element.18.sigma_ref, f32[8,256]{1,0:T(8,128)} %add.15.stat_ref, f32[8,256]{1,0:T(8,128)} %add.13.refs_13_.norm_ref), custom_call_target="tpu_custom_call" | custom-call | flops 1048576 | bytes 3145728 | tf_op jit(solution)/shard_map/finish/pallas_call | solution.py:299
  (2 shorter events, 0.0 us)
Async XLA Ops:
  3.8 15.1 %collective-permute-start.1 = (bf16[16,64,256]{2,1,0:T(8,128)(2,1)}, bf16[16,64,256]{2,1,0:T(8,128)(2,1)S(1)}, u32[]{:S(2)}, u32[]{:S(2)}) collective-permute-start(bf16[16,64,256]{2,1,0:T(8,128)(2,1)} %get-tuple-element.12.refs_0_.refs_8_), channel_id=1, source_target_pairs={{0,2},{1,3},{2,0},{3,1},{4,6},{5,7},{6,4},{7,5},{8,10},{9,11},{10,... | collective-permute-start | bytes 1572872 | tf_op jit(solution)/shard_map/ppermute | solution.py:213
  6.8 14.2 %collective-permute-start.3 = (bf16[1,3,256,256]{3,2,1,0:T(8,128)(2,1)}, bf16[1,3,256,256]{3,2,1,0:T(8,128)(2,1)S(1)}, u32[]{:S(2)}, u32[]{:S(2)}) collective-permute-start(bf16[1,3,256,256]{3,2,1,0:T(8,128)(2,1)} %param.7), channel_id=1, source_target_pairs={{4,0},{8,4},{12,8},{16,12},{20,16},{24,20},{28,24},{5,1},{9,5},{13... | collective-permute-start | bytes 1179656 | tf_op jit(solution)/shard_map/ppermute | solution.py:240
  8.1 14.8 %collective-permute-start = (bf16[16,64,256]{2,1,0:T(8,128)(2,1)}, bf16[16,64,256]{2,1,0:T(8,128)(2,1)S(1)}, u32[]{:S(2)}, u32[]{:S(2)}) collective-permute-start(bf16[16,64,256]{2,1,0:T(8,128)(2,1)} %get-tuple-element.12.refs_0_.refs_8_), channel_id=1, source_target_pairs={{0,1},{1,0},{2,3},{3,2},{4,5},{5,4},{6,7},{7,6},{8,9},{9,8},{10,11... | collective-permute-start | bytes 1572872 | tf_op jit(solution)/shard_map/ppermute | solution.py:210
  18.9 3.9 %copy-start.4 = (bf16[16,64,256]{2,1,0:T(8,128)(2,1)}, bf16[16,64,256]{2,1,0:T(8,128)(2,1)S(1)}, u32[]{:S(2)}) copy-start(bf16[16,64,256]{2,1,0:T(8,128)(2,1)S(1)} %collective-permute-done.1.refs_2_.refs_10_) | copy-start | bytes 1572868
  18.9 3.9 %collective-permute-start.2 = (bf16[16,64,256]{2,1,0:T(8,128)(2,1)S(1)}, bf16[16,64,256]{2,1,0:T(8,128)(2,1)S(1)}, u32[]{:S(2)}, u32[]{:S(2)}) collective-permute-start(bf16[16,64,256]{2,1,0:T(8,128)(2,1)S(1)} %collective-permute-done.1.refs_2_.refs_10_), channel_id=1, source_target_pairs={{0,1},{1,0},{2,3},{3,2},{4,5},{5,4},{6,7},{7,6},{8,9},{9,8},{10,11... | collective-permute-start | bytes 1572872 | tf_op jit(solution)/shard_map/ppermute | solution.py:210
  18.9 18.2 %collective-permute-start.7 = (bf16[3,16,16]{2,1,0:T(8,128)(2,1)}, bf16[3,16,16]{2,1,0:T(8,128)(2,1)S(1)}, u32[]{:S(2)}, u32[]{:S(2)}) collective-permute-start(bf16[3,16,16]{2,1,0:T(8,128)(2,1)} %bitcast.12), channel_id=1, source_target_pairs={{0,2},{1,3},{2,0},{3,1},{4,6},{5,7},{6,4},{7,5},{8,10},{9,11},{10,... | collective-permute-start | bytes 4616 | tf_op jit(solution)/shard_map/ppermute | solution.py:213
  20.7 16.5 %collective-permute-start.5 = (bf16[3,256,256]{2,1,0:T(8,128)(2,1)}, bf16[3,256,256]{2,1,0:T(8,128)(2,1)S(1)}, u32[]{:S(2)}, u32[]{:S(2)}) collective-permute-start(bf16[3,256,256]{2,1,0:T(8,128)(2,1)} %bitcast.9), channel_id=1, source_target_pairs={{0,2},{1,3},{2,0},{3,1},{4,6},{5,7},{6,4},{7,5},{8,10},{9,11},{10,... | collective-permute-start | bytes 1179656 | tf_op jit(solution)/shard_map/ppermute | solution.py:213
  21.0 1.9 %copy-start = (bf16[3,256,256]{2,1,0:T(8,128)(2,1)}, bf16[3,256,256]{2,1,0:T(8,128)(2,1)S(1)}, u32[]{:S(2)}) copy-start(bf16[3,256,256]{2,1,0:T(8,128)(2,1)S(1)} %select_bitcast_fusion.refs_5_.refs_15_) | copy-start | bytes 1179652
  21.0 19.5 %collective-permute-start.6 = (bf16[3,256,256]{2,1,0:T(8,128)(2,1)S(1)}, bf16[3,256,256]{2,1,0:T(8,128)(2,1)S(1)}, u32[]{:S(2)}, u32[]{:S(2)}) collective-permute-start(bf16[3,256,256]{2,1,0:T(8,128)(2,1)S(1)} %select_bitcast_fusion.refs_5_.refs_15_), channel_id=1, source_target_pairs={{0,2},{1,3},{2,0},{3,1},{4,6},{5,7},{6,4},{7,5},{8,10},{9,11},{10,... | collective-permute-start | bytes 1179656 | tf_op jit(solution)/shard_map/ppermute | solution.py:213
  22.9 0.8 copy-start.5
  23.6 0.8 copy-start.6
  37.0 16.9 %copy-start.1 = (f32[8,256]{1,0:T(8,128)S(1)}, f32[8,256]{1,0:T(8,128)}, u32[]{:S(2)}) copy-start(f32[8,256]{1,0:T(8,128)} %get-tuple-element.17) | copy-start | bytes 24580
  37.1 21.3 %copy-start.10 = (f32[8,256]{1,0:T(8,128)S(1)}, f32[8,256]{1,0:T(8,128)}, u32[]{:S(2)}) copy-start(f32[8,256]{1,0:T(8,128)} %get-tuple-element.15.refs_4_) | copy-start | bytes 24580
  37.1 25.0 %collective-permute-start.4 = (bf16[16,256,256]{2,1,0:T(8,128)(2,1)}, bf16[16,256,256]{2,1,0:T(8,128)(2,1)S(1)}, u32[]{:S(2)}, u32[]{:S(2)}) collective-permute-start(bf16[16,256,256]{2,1,0:T(8,128)(2,1)} %get-tuple-element.13.refs_0_), channel_id=1, source_target_pairs={{0,1},{1,0},{2,3},{3,2},{4,5},{5,4},{6,7},{7,6},{8,9},{9,8},{10,11... | collective-permute-start | bytes 6291464 | tf_op jit(solution)/shard_map/ppermute | solution.py:210
  37.2 3.4 %copy-start.9 = (bf16[3,16,16]{2,1,0:T(8,128)(2,1)}, bf16[3,16,16]{2,1,0:T(8,128)(2,1)S(1)}, u32[]{:S(2)}) copy-start(bf16[3,16,16]{2,1,0:T(8,128)(2,1)S(1)} %collective-permute-done.7.refs_6_) | copy-start | bytes 4612
  37.2 3.4 %copy-start.7 = (bf16[3,256,256]{2,1,0:T(8,128)(2,1)}, bf16[3,256,256]{2,1,0:T(8,128)(2,1)S(1)}, u32[]{:S(2)}) copy-start(bf16[3,256,256]{2,1,0:T(8,128)(2,1)S(1)} %collective-permute-done.5.refs_4_) | copy-start | bytes 1179652
  40.6 0.8 copy-start.8
  53.9 8.2 %collective-permute-start.8 = (bf16[16,256,256]{2,1,0:T(8,128)(2,1)}, bf16[16,256,256]{2,1,0:T(8,128)(2,1)S(1)}, u32[]{:S(2)}, u32[]{:S(2)}) collective-permute-start(bf16[16,256,256]{2,1,0:T(8,128)(2,1)} %get-tuple-element.14.refs_2_), channel_id=1, source_target_pairs={{0,1},{1,0},{2,3},{3,2},{4,5},{5,4},{6,7},{7,6},{8,9},{9,8},{10,11... | collective-permute-start | bytes 6291464 | tf_op jit(solution)/shard_map/ppermute | solution.py:210
  54.0 3.8 %collective-permute-start.11 = (f32[8,256]{1,0:T(8,128)S(1)}, f32[8,256]{1,0:T(8,128)S(1)}, u32[]{:S(2)}, u32[]{:S(2)}) collective-permute-start(f32[8,256]{1,0:T(8,128)S(1)} %copy-done.1), channel_id=1, source_target_pairs={{0,1},{1,0},{2,3},{3,2},{4,5},{5,4},{6,7},{7,6},{8,9},{9,8},{10,11... | collective-permute-start | bytes 24584 | tf_op jit(solution)/shard_map/ppermute | solution.py:224
  57.7 3.7 %collective-permute-start.12 = (f32[8,256]{1,0:T(8,128)S(1)}, f32[8,256]{1,0:T(8,128)S(1)}, u32[]{:S(2)}, u32[]{:S(2)}) collective-permute-start(f32[8,256]{1,0:T(8,128)S(1)} %add.12), channel_id=1, source_target_pairs={{0,2},{1,3},{2,0},{3,1},{4,6},{5,7},{6,4},{7,5},{8,10},{9,11},{10,... | collective-permute-start | bytes 24584 | tf_op jit(solution)/shard_map/ppermute | solution.py:224
  58.3 3.7 %collective-permute-start.10 = (f32[8,256]{1,0:T(8,128)}, f32[8,256]{1,0:T(8,128)S(1)}, u32[]{:S(2)}, u32[]{:S(2)}) collective-permute-start(f32[8,256]{1,0:T(8,128)} %get-tuple-element.16.refs_6_), channel_id=1, source_target_pairs={{0,1},{1,0},{2,3},{3,2},{4,5},{5,4},{6,7},{7,6},{8,9},{9,8},{10,11... | collective-permute-start | bytes 24584 | tf_op jit(solution)/shard_map/ppermute | solution.py:210
  58.4 3.6 %collective-permute-start.9 = (f32[8,256]{1,0:T(8,128)S(1)}, f32[8,256]{1,0:T(8,128)S(1)}, u32[]{:S(2)}, u32[]{:S(2)}) collective-permute-start(f32[8,256]{1,0:T(8,128)S(1)} %copy-done.10), channel_id=1, source_target_pairs={{0,1},{1,0},{2,3},{3,2},{4,5},{5,4},{6,7},{7,6},{8,9},{9,8},{10,11... | collective-permute-start | bytes 24584 | tf_op jit(solution)/shard_map/ppermute | solution.py:210
  62.0 0.6 copy-start.11
  62.0 0.6 copy-start.12
  62.0 1.4 %copy-start.2 = (bf16[16,256,256]{2,1,0:T(8,128)(2,1)}, bf16[16,256,256]{2,1,0:T(8,128)(2,1)S(1)}, u32[]{:S(2)}) copy-start(bf16[16,256,256]{2,1,0:T(8,128)(2,1)S(1)} %collective-permute-done.4.refs_1_) | copy-start | bytes 6291460
  63.4 1.4 %copy-start.3 = (bf16[16,256,256]{2,1,0:T(8,128)(2,1)}, bf16[16,256,256]{2,1,0:T(8,128)(2,1)S(1)}, u32[]{:S(2)}) copy-start(bf16[16,256,256]{2,1,0:T(8,128)(2,1)S(1)} %collective-permute-done.8.refs_3_) | copy-start | bytes 6291460
  83.9 1.4 %collective-permute-start.13 = (f32[8,256]{1,0:T(8,128)}, f32[8,256]{1,0:T(8,128)S(1)}, u32[]{:S(2)}, u32[]{:S(2)}) collective-permute-start(f32[8,256]{1,0:T(8,128)} %get-tuple-element.19), channel_id=1, source_target_pairs={{0,1},{1,0},{2,3},{3,2},{4,5},{5,4},{6,7},{7,6},{8,9},{9,8},{10,11... | collective-permute-start | bytes 24584 | tf_op jit(solution)/shard_map/ppermute | solution.py:224
  86.0 3.7 %collective-permute-start.14 = (f32[8,256]{1,0:T(8,128)S(1)}, f32[8,256]{1,0:T(8,128)S(1)}, u32[]{:S(2)}, u32[]{:S(2)}) collective-permute-start(f32[8,256]{1,0:T(8,128)S(1)} %add.14), channel_id=1, source_target_pairs={{0,2},{1,3},{2,0},{3,1},{4,6},{5,7},{6,4},{7,5},{8,10},{9,11},{10,... | collective-permute-start | bytes 24584 | tf_op jit(solution)/shard_map/ppermute | solution.py:224

commit v2 on v1

v2 whole, which is shorter than its diff:
```python
import functools

import jax
import jax.numpy as jnp
from jax import lax
from jax.experimental import pallas as pl
from jax.experimental.pallas import tpu as pltpu
from jax.sharding import PartitionSpec as P

epsilon = 1e-06
CORES = 2
TILE = 16
VMEM_LIMIT = 28 * 1024 * 1024
F32 = jnp.float32
BF16 = jnp.bfloat16

vmem = pl.BlockSpec(memory_space=pltpu.VMEM)
smem = pl.BlockSpec(memory_space=pltpu.SMEM)
anywhere = pl.BlockSpec(memory_space=pl.ANY)


def params():
    return pltpu.CompilerParams(vmem_limit_bytes=VMEM_LIMIT)


def cost(flops, moved):
    return pl.CostEstimate(flops=int(flops), bytes_accessed=int(moved), transcendentals=0)


def keep_row(rank, width):
    return (lax.broadcasted_iota(jnp.int32, (1, width), 1) < rank).astype(F32)


def prepare_kernel(rank_ref, guess_ref, x_ref, norm_ref):
    rows, states, width = guess_ref.shape
    masked = guess_ref[...] * keep_row(rank_ref[0], width)[None]
    norm_ref[...] = jnp.full(norm_ref.shape, jnp.sum(masked * masked), F32)
    x_ref[...] = jnp.swapaxes(masked, 0, 1).astype(BF16)


def spread_site(site_ref, kron_ref):
    terms, states, _ = site_ref.shape
    size = states * TILE
    row_state = lax.broadcasted_iota(jnp.int32, (size, states), 0) // TILE
    pick = (row_state == lax.broadcasted_iota(jnp.int32, (size, states), 1)).astype(BF16)
    col_state = lax.broadcasted_iota(jnp.int32, (states, size), 1) // TILE
    pick_t = (col_state == lax.broadcasted_iota(jnp.int32, (states, size), 0)).astype(BF16)
    same = (
        lax.broadcasted_iota(jnp.int32, (size, size), 0) % TILE
        == lax.broadcasted_iota(jnp.int32, (size, size), 1) % TILE
    )
    for k in range(terms):
        tall = jnp.dot(pick, site_ref[k], preferred_element_type=F32).astype(BF16)
        full = jnp.dot(tall, pick_t, preferred_element_type=F32)
        kron_ref[k * size : (k + 1) * size, :] = jnp.where(same, full, 0.0).astype(BF16)


def mix_sites(source_ref, kron_ref, rotated_ref):
    terms, states, width, _ = rotated_ref.shape

    def step(i, carry):
        at = pl.multiple_of(i * TILE, TILE)
        stack = source_ref[:, pl.ds(at, TILE), :].reshape(states * TILE, width)
        turned = jnp.dot(kron_ref[...], stack, preferred_element_type=F32).astype(BF16)
        rotated_ref[:, :, pl.ds(at, TILE), :] = turned.reshape(terms, states, TILE, width)
        return carry

    lax.fori_loop(0, width // TILE, step, 0, unroll=4)


def fold(values, width):
    return jnp.sum(values.reshape(values.size // (8 * width), 8, width), axis=0)


def summed(values):
    while len(values) > 1:
        values = [values[n] + values[n + 1] for n in range(0, len(values), 2)]
    return values[0]


def place_pieces(pieces, hops, whole_ref, sems):
    chips = len(hops)
    me = lax.axis_index("term")
    core = me % CORES
    chip = me // CORES
    copies = []
    for n, piece in enumerate(pieces):
        hop = hops[n // 2]
        owner = ((chip - hop + chips) % chips) * CORES + (core if n % 2 == 0 else 1 - core)
        rows = piece.shape[1]
        at = pl.multiple_of(owner * rows, TILE)
        copies.append(pltpu.make_async_copy(piece, whole_ref.at[:, pl.ds(at, rows), :], sems.at[n]))
    for copy in copies:
        copy.start()
    return copies


def apply_terms(left_ref, right_ref, site_ref, whole_ref, partial_ref, rotated_ref, mixed_ref, kron_ref):
    terms, states, width, _ = rotated_ref.shape
    mix_sites(whole_ref, kron_ref, rotated_ref)

    def lefts(p, carry):
        for k in range(terms):
            mixed = jnp.dot(left_ref[k], rotated_ref[k, p], preferred_element_type=F32)
            mixed_ref[p, :, k * width : (k + 1) * width] = mixed.astype(BF16)
        return carry

    lax.fori_loop(0, states, lefts, 0, unroll=4)
    group = 4

    def rights(n, total):
        at = n * group
        rows = mixed_ref[pl.ds(at, group)].reshape(group * width, terms * width)
        stacked = right_ref[...].reshape(terms * width, width)
        part = jnp.dot(rows, stacked, preferred_element_type=F32).astype(BF16)
        part = part.reshape(group, width, width)
        partial_ref[pl.ds(at, group)] = part
        held = whole_ref[pl.ds(at, group)].astype(F32)
        return total + fold(held * part.astype(F32), width)

    total = lax.fori_loop(0, states // group, rights, jnp.zeros((8, width), F32))
    return jnp.sum(total)


def first_kernel(piece_count, hops, *refs):
    pieces = refs[:piece_count]
    norms = refs[piece_count : 2 * piece_count]
    rest = refs[2 * piece_count :]
    left_ref, right_ref, site_ref, whole_ref, partial_ref, stat_ref = rest[:6]
    rotated_ref, mixed_ref, kron_ref, sems = rest[6:]
    width = whole_ref.shape[1]
    copies = place_pieces(pieces, hops, whole_ref, sems)
    spread_site(site_ref, kron_ref)
    for copy in copies:
        copy.wait()
    total = apply_terms(
        left_ref, right_ref, site_ref, whole_ref, partial_ref, rotated_ref, mixed_ref, kron_ref
    )
    stat_ref[0:1, :] = jnp.full((1, width), total, F32)
    stat_ref[1:2, :] = summed([norm[0:1, :] for norm in norms])
    stat_ref[2:8, :] = jnp.zeros((6, width), F32)


def next_kernel(
    whole_ref, before_ref, left_ref, right_ref, site_ref, partial_ref, stat_ref, rotated_ref, mixed_ref, kron_ref
):
    spread_site(site_ref, kron_ref)
    total = apply_terms(
        left_ref, right_ref, site_ref, whole_ref, partial_ref, rotated_ref, mixed_ref, kron_ref
    )
    stat_ref[...] = before_ref[...]
    stat_ref[0:1, :] = before_ref[0:1, :] + total


def second_kernel(group_count, scale, *refs):
    groups = refs[:group_count]
    (rank_ref, mine_ref, theirs_ref, whole_ref, left_ref, right_ref, site_ref) = refs[group_count : group_count + 7]
    (sigma_ref, out_ref, res_ref, rotated_ref, mixed_ref, kron_ref) = refs[group_count + 7 :]
    terms, states, width, _ = rotated_ref.shape
    rows = sigma_ref.shape[1]
    spread_site(site_ref, kron_ref)
    keep = keep_row(rank_ref[0], width)
    inverse = lax.rsqrt(mine_ref[1:2, :] * scale + epsilon)
    rayleigh = (mine_ref[0:1, :] + theirs_ref[0:1, :]) * (inverse * inverse * scale)
    row_scale = keep * inverse
    me = lax.axis_index("term")
    own = pl.multiple_of(me * rows, TILE)

    def group_sum(p, rows_at):
        evens = [group[p, rows_at, :].astype(F32) for group in groups[0::2]]
        odds = [group[p, rows_at, :].astype(F32) for group in groups[1::2]]
        return functools.reduce(jnp.add, evens) + functools.reduce(jnp.add, odds)

    def lefts(p, total):
        sigma = group_sum(p, slice(None)) * row_scale
        residual = sigma - (rayleigh * inverse) * whole_ref[p].astype(F32)
        rounded = residual.astype(BF16)
        res_ref[p] = rounded
        sigma_ref[p] = group_sum(p, pl.ds(own, rows)) * row_scale
        mixed = jnp.dot(
            left_ref[...].reshape(terms * width, width), rounded, preferred_element_type=F32
        ).astype(BF16)
        for k in range(terms):
            mixed_ref[k, p] = mixed[k * width : (k + 1) * width]
        return total + fold(residual * residual, width)

    square = lax.fori_loop(0, states, lefts, jnp.zeros((8, width), F32), unroll=2)
    mix_sites(res_ref, kron_ref, rotated_ref)
    group = 4
    cross = jnp.zeros((8, width), F32)
    for k in range(terms):

        def rights(n, total):
            at = n * group
            turned = rotated_ref[k, pl.ds(at, group)].reshape(group * width, width)
            image = jnp.dot(turned, right_ref[k], preferred_element_type=F32)
            held = mixed_ref[k, pl.ds(at, group)].reshape(group * width, width).astype(F32)
            return total + fold(held * image, width)

        cross = lax.fori_loop(0, states // group, rights, cross)
    share = 1.0 / group_count
    out_ref[0:1, :] = rayleigh * share
    out_ref[1:2, :] = jnp.full((1, width), jnp.sum(square) * (scale * share), F32)
    out_ref[2:3, :] = jnp.full((1, width), jnp.sum(cross) * scale, F32)
    out_ref[3:8, :] = jnp.zeros((5, width), F32)


def finish_kernel(scale, rank_ref, guess_ref, sigma_ref, norm_ref, *refs):
    shares = refs[:-2]
    ritz_ref, energy_ref = refs[-2:]
    rows, states, width = guess_ref.shape
    inverse = lax.rsqrt(norm_ref[1:2, :] * scale + epsilon)
    stat = summed([share[...] for share in shares])
    rayleigh = stat[0:1, :]
    res_sq = stat[1:2, :]
    res_var = res_sq + epsilon
    curvature = stat[2:3, :] / res_var
    res_scale = jnp.sqrt(res_var)
    coupling = res_sq / res_scale
    half_gap = 0.5 * (rayleigh - curvature)
    energy = 0.5 * (rayleigh + curvature) - jnp.sqrt(half_gap * half_gap + coupling * coupling)
    coeff_new = energy - rayleigh
    coeff_norm = jnp.sqrt(coupling * coupling + coeff_new * coeff_new + epsilon)
    old = coupling / coeff_norm
    new = coeff_new / (coeff_norm * res_scale)
    vector = guess_ref[...] * (keep_row(rank_ref[0], width) * inverse)[None]
    sigma = jnp.swapaxes(sigma_ref[...], 0, 1)
    ritz_ref[...] = old[None] * vector + new[None] * (sigma - rayleigh[None] * vector)
    energy_ref[0] = energy[0, 0]


def shards(wave_guess, left_env, right_env, site_ops, bond_rank):
    guess = wave_guess[0]
    left = left_env[0]
    site = site_ops[0]
    rows, states, width = guess.shape
    terms = left.shape[0]
    members = lax.axis_size("term")
    chips = members // CORES
    segments = lax.axis_size("seg")
    scale = 1.0 / float(rows * members * states * width)
    hops = tuple(range(chips))

    def to_sibling(block):
        return lax.ppermute(block, "term", [(i, i ^ 1) for i in range(members)])

    def to_next_chip(block):
        return lax.ppermute(block, "term", [(i, (i + CORES) % members) for i in range(members)])

    def around(block):
        found = [block]
        for _ in range(chips - 1):
            found.append(to_next_chip(found[-1]))
        return found

    def everyone(block):
        others = [
            lax.ppermute(block, "term", [(i, i ^ bits) for i in range(members)]) for bits in range(1, members)
        ]
        return [block] + others

    tile = jax.ShapeDtypeStruct((8, width), F32)
    x_own, norm_part = pl.pallas_call(
        prepare_kernel,
        out_shape=(jax.ShapeDtypeStruct((states, rows, width), BF16), tile),
        in_specs=[smem, vmem],
        out_specs=(vmem, vmem),
        compiler_params=params(),
        cost_estimate=cost(4 * guess.size, 6 * guess.size),
        name="prepare",
    )(bond_rank, guess)

    shift = [(i + 1, i) for i in range(segments - 1)]
    received = lax.ppermute(right_env, "seg", shift)
    right = jnp.where(lax.axis_index("seg") == segments - 1, right_env, received)[0]

    x_hops = around(x_own)
    pieces = []
    for block in x_hops:
        pieces += [block, to_sibling(block)]
    norms = everyone(norm_part)

    left_hops = around(left)
    right_hops = around(right)
    site_hops = around(site)

    whole = (states, width, width)
    rotated = (terms, states, width, width)
    scratch = [
        pltpu.VMEM(rotated, BF16),
        pltpu.VMEM((states, width, terms * width), BF16),
        pltpu.VMEM((terms * states * TILE, states * TILE), BF16),
    ]
    apply_flops = 2 * terms * states * width * width * (2 * width + states * TILE)
    apply_cost = cost(apply_flops, 4 * states * width * width)
    vector, partial, stat = pl.pallas_call(
        functools.partial(first_kernel, members, hops),
        out_shape=(jax.ShapeDtypeStruct(whole, BF16), jax.ShapeDtypeStruct(whole, BF16), tile),
        in_specs=[anywhere] * members + [vmem] * (members + 3),
        out_specs=(vmem, vmem, vmem),
        scratch_shapes=scratch + [pltpu.SemaphoreType.DMA((members,))],
        compiler_params=params(),
        cost_estimate=apply_cost,
        name="apply_own_terms",
    )(*pieces, *norms, left, right, site)
    groups = [partial, to_sibling(partial)]
    for hop in hops[1:]:
        partial, stat = pl.pallas_call(
            next_kernel,
            out_shape=(jax.ShapeDtypeStruct(whole, BF16), tile),
            in_specs=[vmem] * 5,
            out_specs=(vmem, vmem),
            scratch_shapes=scratch,
            compiler_params=params(),
            cost_estimate=apply_cost,
            name="apply_received_terms",
        )(vector, stat, left_hops[hop], right_hops[hop], site_hops[hop])
        groups += [partial, to_sibling(partial)]

    sigma_own, share = pl.pallas_call(
        functools.partial(second_kernel, members, scale),
        out_shape=(jax.ShapeDtypeStruct((states, rows, width), F32), tile),
        in_specs=[vmem] * members + [smem] + [vmem] * 6,
        out_specs=(vmem, vmem),
        scratch_shapes=[
            pltpu.VMEM(whole, BF16),
            pltpu.VMEM(rotated, BF16),
            pltpu.VMEM(rotated, BF16),
            pltpu.VMEM((terms * states * TILE, states * TILE), BF16),
        ],
        compiler_params=params(),
        cost_estimate=cost(apply_flops, 2 * members * states * width * width),
        name="apply_residual",
    )(*groups, bond_rank, stat, to_sibling(stat), vector, left, right, site)

    ritz, energy = pl.pallas_call(
        functools.partial(finish_kernel, scale),
        out_shape=(jax.ShapeDtypeStruct((rows, states, width), F32), jax.ShapeDtypeStruct((1,), F32)),
        in_specs=[smem] + [vmem] * (3 + members),
        out_specs=(vmem, smem),
        compiler_params=params(),
        cost_estimate=cost(4 * guess.size, 12 * guess.size),
        name="finish",
    )(bond_rank, guess, sigma_own, stat, *everyone(share))
    return (ritz[None], energy)


def solution(mesh):
    in_specs = (
        P("seg", "term", None, None),
        P("seg", "term", None, None),
        P("seg", "term", None, None),
        P("seg", "term", None, None),
        P("seg"),
    )
    out_specs = (P("seg", "term", None, None), P("seg"))
    return jax.shard_map(shards, mesh=mesh, in_specs=in_specs, out_specs=out_specs, check_vma=False)
```

time: 93.8 us -> 76.2 us (0.81)
  Pallas kernels: 49.9 us -> 30.9 us
  waiting for transfers between devices: 24.5 us -> 29.8 us
  local copies, waits for them, and re-layouts: 5.09 us -> 1.23 us
  starting transfers between devices: 10.5 us -> 12.7 us
  other arithmetic: 1.95 us -> 0.06 us
    pallas_call x3, Pallas kernels: 44.2 us -> 28.8 us  [the longest x1 12.5 us: shards(): pl.pallas_call(functools.partial(second_kernel, members, scale), out_shap...]
    ppermute x6 -> x5, waiting for transfers between devices: 0.02 us -> 6.59 us  [to_sibling(): return lax.ppermute(block, 'term', [(i, i ^ 1) for i in range(members)])]
    ppermute x4 -> x6, waiting for transfers between devices: 10.3 us -> 3.85 us  [everyone(): lax.ppermute(block, 'term', [(i, i ^ bits) for i in range(members)])]
    ppermute x4, waiting for transfers between devices: 14.1 us -> 19.3 us  [to_next_chip(): lax.ppermute(block, 'term', [(i, (i + CORES) % members) for i in range(me...]
    unnamed x26 -> x8, local copies, waits for them, and re-layouts: 5.09 us -> 1.23 us
    ppermute x4 -> x6, starting transfers between devices: 1.67 us -> 4.07 us  [everyone(): lax.ppermute(block, 'term', [(i, i ^ bits) for i in range(members)])]
    pallas_call x1, Pallas kernels: 2.55 us -> 0.53 us  [shards(): pl.pallas_call(prepare_kernel, out_shape=(jax.ShapeDtypeStruct((states, r...]
    add x4 -> x0, other arithmetic: 1.9 us -> none  [total(): block + lax.ppermute(block, 'term', [(i, i ^ bit) for i in range(members)])]
  transfers between devices with their start and end apart: 15 -> 16, of which waited for: 6 -> 8; matrix products, arithmetic and copies ran while one was open for 1% -> 0% of each run, Pallas kernels for 27% -> 11%
where the time goes in v2:
time: 76.2 us; the launch traced here: 76.1 us
  Pallas kernels  30.9 us (41%)
  waiting for transfers between devices  29.8 us (39%)
  starting transfers between devices  12.7 us (17%)
  between operations  1.37 us (2%)
  local copies, waits for them, and re-layouts  1.23 us (2%)
    ppermute x4, waiting for transfers between devices, to_next_chip(): lax.ppermute(block, 'term', [(i, (i + CORES) % members) for i in range(me...  19.3 us
    pallas_call x1, Pallas kernels, shards(): pl.pallas_call(functools.partial(second_kernel, members, scale), out_shap...  12.5 us
    pallas_call x1, Pallas kernels, shards(): pl.pallas_call(functools.partial(first_kernel, members, hops), out_shape=...  8.18 us
    pallas_call x1, Pallas kernels, shards(): pl.pallas_call(next_kernel, out_shape=(jax.ShapeDtypeStruct(whole, BF16),...  8.03 us
    ppermute x4, starting transfers between devices, to_next_chip(): lax.ppermute(block, 'term', [(i, (i + CORES) % members) for i in range(me...  6.66 us
    ppermute x5, waiting for transfers between devices, to_sibling(): return lax.ppermute(block, 'term', [(i, i ^ 1) for i in range(members)])  6.59 us
    ppermute x6, starting transfers between devices, everyone(): lax.ppermute(block, 'term', [(i, i ^ bits) for i in range(members)])  4.07 us
    ppermute x6, waiting for transfers between devices, everyone(): lax.ppermute(block, 'term', [(i, i ^ bits) for i in range(members)])  3.85 us
  transfers between devices with their start and end apart: 16, of which 8 were waited for; matrix products, arithmetic and copies ran while one was open for 0% of the time, Pallas kernels for 11%

profile of v2, /device:TPU:0, one launch (start us, length us, event | category | flops | bytes accessed | tf_op | source)
XLA Modules:
  0.0 76.1 jit_solution(12133064834716699201)
XLA Ops:
  1.3 0.0 copy-start
  1.3 1.2 %copy-done = f32[1,64,16,256]{3,2,1,0:T(8,128)S(1)} copy-done((f32[1,64,16,256]{3,2,1,0:T(8,128)S(1)}, f32[1,64,16,256]{3,2,1,0:T(8,128)}, u32[]{:S(2)}) %copy-start) | copy-done | bytes 1048600
  2.5 0.0 copy-start.3
  2.5 0.0 copy-start.2
  2.5 0.5 prepare.1
  3.0 3.0 %collective-permute-start.1 = (bf16[16,64,256]{2,1,0:T(8,128)(2,1)S(1)}, bf16[16,64,256]{2,1,0:T(8,128)(2,1)S(1)}, u32[]{:S(2)}, u32[]{:S(2)}) collective-permute-start(bf16[16,64,256]{2,1,0:T(8,128)(2,1)S(1)} %get-tuple-element.13.refs_0_), channel_id=1, source_target_pairs={{0,2},{1,3},{2,0},{3,1},{4,6},{5,7},{6,4},{7,5},{8,10},{9,11},{10,... | collective-permute-start | bytes 1572872 | tf_op jit(solution)/shard_map/ppermute | solution.py:248
  6.1 1.3 %collective-permute-start.6 = (bf16[1,3,256,256]{3,2,1,0:T(8,128)(2,1)}, bf16[1,3,256,256]{3,2,1,0:T(8,128)(2,1)S(1)}, u32[]{:S(2)}, u32[]{:S(2)}) collective-permute-start(bf16[1,3,256,256]{3,2,1,0:T(8,128)(2,1)} %param.7), channel_id=1, source_target_pairs={{4,0},{8,4},{12,8},{16,12},{20,16},{24,20},{28,24},{5,1},{9,5},{13... | collective-permute-start | bytes 1179656 | tf_op jit(solution)/shard_map/ppermute | solution.py:274
  7.4 0.1 collective-permute-start
  7.4 10.6 %collective-permute-done.1.refs_2_ = bf16[16,64,256]{2,1,0:T(8,128)(2,1)S(1)} collective-permute-done((bf16[16,64,256]{2,1,0:T(8,128)(2,1)S(1)}, bf16[16,64,256]{2,1,0:T(8,128)(2,1)S(1)}, u32[]{:S(2)}, u32[]{:S(2)}) %collective-permute-start.1) | collective-permute-done | bytes 524320 | tf_op jit(solution)/shard_map/ppermute | solution.py:248
  18.0 0.0 collective-permute-start.2
  18.0 1.9 %collective-permute-start.5 = (f32[8,256]{1,0:T(8,128)S(1)}, f32[8,256]{1,0:T(8,128)S(1)}, u32[]{:S(2)}, u32[]{:S(2)}) collective-permute-start(f32[8,256]{1,0:T(8,128)S(1)} %get-tuple-element.14.refs_4_), channel_id=1, source_target_pairs={{0,3},{1,2},{2,1},{3,0},{4,7},{5,6},{6,5},{7,4},{8,11},{9,10},{10,... | collective-permute-start | bytes 24584 | tf_op jit(solution)/shard_map/ppermute | solution.py:258
  19.9 0.3 collective-permute-start.4
  20.1 0.0 collective-permute-done.6
  20.1 0.0 collective-permute-start.3
  20.1 0.1 select_bitcast_fusion.refs_9_
  20.2 1.0 %collective-permute-done.5.refs_7_ = f32[8,256]{1,0:T(8,128)S(1)} collective-permute-done((f32[8,256]{1,0:T(8,128)S(1)}, f32[8,256]{1,0:T(8,128)S(1)}, u32[]{:S(2)}, u32[]{:S(2)}) %collective-permute-start.5) | collective-permute-done | bytes 8224 | tf_op jit(solution)/shard_map/ppermute | solution.py:258
  21.2 0.0 copy-done.3
  21.2 1.6 %collective-permute-start.10 = (bf16[3,16,16]{2,1,0:T(8,128)(2,1)S(1)}, bf16[3,16,16]{2,1,0:T(8,128)(2,1)S(1)}, u32[]{:S(2)}, u32[]{:S(2)}) collective-permute-start(bf16[3,16,16]{2,1,0:T(8,128)(2,1)S(1)} %bitcast.11), channel_id=1, source_target_pairs={{0,2},{1,3},{2,0},{3,1},{4,6},{5,7},{6,4},{7,5},{8,10},{9,11},{10,... | collective-permute-start | bytes 4616 | tf_op jit(solution)/shard_map/ppermute | solution.py:248
  22.8 0.7 collective-permute-done.4.refs_6_
  23.5 0.0 copy-done.2
  23.5 0.3 collective-permute-start.8
  23.8 0.0 collective-permute-done.3.refs_5_
  23.8 1.7 %collective-permute-start.9 = (bf16[3,256,256]{2,1,0:T(8,128)(2,1)S(1)}, bf16[3,256,256]{2,1,0:T(8,128)(2,1)S(1)}, u32[]{:S(2)}, u32[]{:S(2)}) collective-permute-start(bf16[3,256,256]{2,1,0:T(8,128)(2,1)S(1)} %select_bitcast_fusion.refs_9_), channel_id=1, source_target_pairs={{0,2},{1,3},{2,0},{3,1},{4,6},{5,7},{6,4},{7,5},{8,10},{9,11},{10,... | collective-permute-start | bytes 1179656 | tf_op jit(solution)/shard_map/ppermute | solution.py:248
  25.5 0.0 collective-permute-done.refs_1_
  25.5 0.0 collective-permute-done.2.refs_3_
  25.5 8.2 %apply_own_terms.1 = (bf16[16,256,256]{2,1,0:T(8,128)(2,1)S(1)}, bf16[16,256,256]{2,1,0:T(8,128)(2,1)S(1)}, f32[8,256]{1,0:T(8,128)S(1)}) custom-call(bf16[16,64,256]{2,1,0:T(8,128)(2,1)S(1)} %get-tuple-element.13.refs_0_, bf16[16,64,256]{2,1,0:T(8,128)(2,1)S(1)} %collective-permute-done.refs_1_, bf16[16,64,256]{2,1,0:T(8,128)(2,1)S(1)} %collective-permute-done.1.refs_2_, ...), custom_call_target="tpu_custom_call" | custom-call | flops 4831838208 | bytes 4194304 | tf_op jit(solution)/shard_map/apply_own_terms/pallas_call | solution.py:296
  33.7 0.0 collective-permute-done.10.site_ref
  33.8 1.8 %collective-permute-done.8.left_ref = bf16[3,256,256]{2,1,0:T(8,128)(2,1)S(1)} collective-permute-done((bf16[3,256,256]{2,1,0:T(8,128)(2,1)S(1)}, bf16[3,256,256]{2,1,0:T(8,128)(2,1)S(1)}, u32[]{:S(2)}, u32[]{:S(2)}) %collective-permute-start.8) | collective-permute-done | bytes 393248 | tf_op jit(solution)/shard_map/ppermute | solution.py:248
  35.6 7.0 %collective-permute-done.9.right_ref = bf16[3,256,256]{2,1,0:T(8,128)(2,1)S(1)} collective-permute-done((bf16[3,256,256]{2,1,0:T(8,128)(2,1)S(1)}, bf16[3,256,256]{2,1,0:T(8,128)(2,1)S(1)}, u32[]{:S(2)}, u32[]{:S(2)}) %collective-permute-start.9) | collective-permute-done | bytes 393248 | tf_op jit(solution)/shard_map/ppermute | solution.py:248
  42.5 8.0 %apply_received_terms.1 = (bf16[16,256,256]{2,1,0:T(8,128)(2,1)S(1)}, f32[8,256]{1,0:T(8,128)S(1)}) custom-call(bf16[16,256,256]{2,1,0:T(8,128)(2,1)S(1)} %get-tuple-element.16.whole_ref.refs_7_, f32[8,256]{1,0:T(8,128)S(1)} %get-tuple-element.17.before_ref, bf16[3,256,256]{2,1,0:T(8,128)(2,1)S(1)} %collective-permute-done.8.left_ref, ...), custom_call_target="tpu_custom_call" | custom-call | flops 4831838208 | bytes 4194304 | tf_op jit(solution)/shard_map/apply_received_terms/pallas_call | solution.py:308
  50.5 0.1 collective-permute-start.11
  50.6 0.5 collective-permute-start.7
  51.1 0.0 copy-start.1
  51.1 0.1 collective-permute-start.12
  51.2 6.6 %collective-permute-done.12.refs_6_ = f32[8,256]{1,0:T(8,128)S(1)} collective-permute-done((f32[8,256]{1,0:T(8,128)S(1)}, f32[8,256]{1,0:T(8,128)S(1)}, u32[]{:S(2)}, u32[]{:S(2)}) %collective-permute-start.12) | collective-permute-done | bytes 8224 | tf_op jit(solution)/shard_map/ppermute | solution.py:245
  57.8 0.0 collective-permute-done.11.refs_3_
  57.8 0.0 collective-permute-done.7.refs_1_
  57.8 12.5 %apply_residual.1 = (f32[16,64,256]{2,1,0:T(8,128)S(1)}, f32[8,256]{1,0:T(8,128)S(1)}) custom-call(bf16[16,256,256]{2,1,0:T(8,128)(2,1)S(1)} %get-tuple-element.15.refs_0_, bf16[16,256,256]{2,1,0:T(8,128)(2,1)S(1)} %collective-permute-done.7.refs_1_, bf16[16,256,256]{2,1,0:T(8,128)(2,1)S(1)} %get-tuple-element.18.refs_2_, ...), custom_call_target="tpu_custom_call" | custom-call | flops 4831838208 | bytes 8388608 | tf_op jit(solution)/shard_map/apply_residual/pallas_call | solution.py:320
  70.3 0.4 collective-permute-start.15
  70.8 1.5 %collective-permute-start.14 = (f32[8,256]{1,0:T(8,128)S(1)}, f32[8,256]{1,0:T(8,128)S(1)}, u32[]{:S(2)}, u32[]{:S(2)}) collective-permute-start(f32[8,256]{1,0:T(8,128)S(1)} %get-tuple-element.21.refs_0_), channel_id=1, source_target_pairs={{0,2},{1,3},{2,0},{3,1},{4,6},{5,7},{6,4},{7,5},{8,10},{9,11},{10,... | collective-permute-start | bytes 24584 | tf_op jit(solution)/shard_map/ppermute | solution.py:258
  72.2 0.0 collective-permute-start.13
  72.3 1.2 %collective-permute-done.15.refs_3_ = f32[8,256]{1,0:T(8,128)S(1)} collective-permute-done((f32[8,256]{1,0:T(8,128)S(1)}, f32[8,256]{1,0:T(8,128)S(1)}, u32[]{:S(2)}, u32[]{:S(2)}) %collective-permute-start.15) | collective-permute-done | bytes 8224 | tf_op jit(solution)/shard_map/ppermute | solution.py:258
  73.5 0.9 %collective-permute-done.14.refs_2_ = f32[8,256]{1,0:T(8,128)S(1)} collective-permute-done((f32[8,256]{1,0:T(8,128)S(1)}, f32[8,256]{1,0:T(8,128)S(1)}, u32[]{:S(2)}, u32[]{:S(2)}) %collective-permute-start.14) | collective-permute-done | bytes 8224 | tf_op jit(solution)/shard_map/ppermute | solution.py:258
  74.4 0.0 collective-permute-done.13.refs_1_
  74.4 0.0 copy-done.1
  74.4 1.6 %finish.1 = (f32[64,16,256]{2,1,0:T(8,128)}, f32[1]{0:T(128)}) custom-call(s32[1]{0:T(128)S(6)} %copy.7.rank_ref.refs_4_, f32[64,16,256]{2,1,0:T(8,128)S(1)} %bitcast.7, f32[16,64,256]{2,1,0:T(8,128)S(1)} %get-tuple-element.20.sigma_ref, f32[8,256]{1,0:T(8,128)S(1)} %get-tuple-element.19.refs_5_.norm_ref, f32[8,256]{1,0:T(8,128)S(1)} %get-tuple-element.21.refs_0_, ...), custom_call_target="tpu_custom_call" | custom-call | flops 1048576 | bytes 3145728 | tf_op jit(solution)/shard_map/finish/pallas_call | solution.py:336
Async XLA Ops:
  1.3 1.2 %copy-start = (f32[1,64,16,256]{3,2,1,0:T(8,128)S(1)}, f32[1,64,16,256]{3,2,1,0:T(8,128)}, u32[]{:S(2)}) copy-start(f32[1,64,16,256]{3,2,1,0:T(8,128)} %param.5) | copy-start | bytes 3145732
  2.5 18.7 %copy-start.3 = (bf16[1,3,16,16]{3,2,1,0:T(8,128)(2,1)S(1)}, bf16[1,3,16,16]{3,2,1,0:T(8,128)(2,1)}, u32[]{:S(2)}) copy-start(bf16[1,3,16,16]{3,2,1,0:T(8,128)(2,1)} %param.8) | copy-start | bytes 4612
  2.5 21.0 %copy-start.2 = (bf16[1,3,256,256]{3,2,1,0:T(8,128)(2,1)S(1)}, bf16[1,3,256,256]{3,2,1,0:T(8,128)(2,1)}, u32[]{:S(2)}) copy-start(bf16[1,3,256,256]{3,2,1,0:T(8,128)(2,1)} %param.6) | copy-start | bytes 1179652
  3.0 15.0 %collective-permute-start.1 = (bf16[16,64,256]{2,1,0:T(8,128)(2,1)S(1)}, bf16[16,64,256]{2,1,0:T(8,128)(2,1)S(1)}, u32[]{:S(2)}, u32[]{:S(2)}) collective-permute-start(bf16[16,64,256]{2,1,0:T(8,128)(2,1)S(1)} %get-tuple-element.13.refs_0_), channel_id=1, source_target_pairs={{0,2},{1,3},{2,0},{3,1},{4,6},{5,7},{6,4},{7,5},{8,10},{9,11},{10,... | collective-permute-start | bytes 1572872 | tf_op jit(solution)/shard_map/ppermute | solution.py:248
  6.1 14.1 %collective-permute-start.6 = (bf16[1,3,256,256]{3,2,1,0:T(8,128)(2,1)}, bf16[1,3,256,256]{3,2,1,0:T(8,128)(2,1)S(1)}, u32[]{:S(2)}, u32[]{:S(2)}) collective-permute-start(bf16[1,3,256,256]{3,2,1,0:T(8,128)(2,1)} %param.7), channel_id=1, source_target_pairs={{4,0},{8,4},{12,8},{16,12},{20,16},{24,20},{28,24},{5,1},{9,5},{13... | collective-permute-start | bytes 1179656 | tf_op jit(solution)/shard_map/ppermute | solution.py:274
  7.4 18.2 %collective-permute-start = (bf16[16,64,256]{2,1,0:T(8,128)(2,1)S(1)}, bf16[16,64,256]{2,1,0:T(8,128)(2,1)S(1)}, u32[]{:S(2)}, u32[]{:S(2)}) collective-permute-start(bf16[16,64,256]{2,1,0:T(8,128)(2,1)S(1)} %get-tuple-element.13.refs_0_), channel_id=1, source_target_pairs={{0,1},{1,0},{2,3},{3,2},{4,5},{5,4},{6,7},{7,6},{8,9},{9,8},{10,11... | collective-permute-start | bytes 1572872 | tf_op jit(solution)/shard_map/ppermute | solution.py:245
  18.0 7.5 %collective-permute-start.2 = (bf16[16,64,256]{2,1,0:T(8,128)(2,1)S(1)}, bf16[16,64,256]{2,1,0:T(8,128)(2,1)S(1)}, u32[]{:S(2)}, u32[]{:S(2)}) collective-permute-start(bf16[16,64,256]{2,1,0:T(8,128)(2,1)S(1)} %collective-permute-done.1.refs_2_), channel_id=1, source_target_pairs={{0,1},{1,0},{2,3},{3,2},{4,5},{5,4},{6,7},{7,6},{8,9},{9,8},{10,11... | collective-permute-start | bytes 1572872 | tf_op jit(solution)/shard_map/ppermute | solution.py:245
  18.0 3.2 %collective-permute-start.5 = (f32[8,256]{1,0:T(8,128)S(1)}, f32[8,256]{1,0:T(8,128)S(1)}, u32[]{:S(2)}, u32[]{:S(2)}) collective-permute-start(f32[8,256]{1,0:T(8,128)S(1)} %get-tuple-element.14.refs_4_), channel_id=1, source_target_pairs={{0,3},{1,2},{2,1},{3,0},{4,7},{5,6},{6,5},{7,4},{8,11},{9,10},{10,... | collective-permute-start | bytes 24584 | tf_op jit(solution)/shard_map/ppermute | solution.py:258
  19.9 3.7 %collective-permute-start.4 = (f32[8,256]{1,0:T(8,128)S(1)}, f32[8,256]{1,0:T(8,128)S(1)}, u32[]{:S(2)}, u32[]{:S(2)}) collective-permute-start(f32[8,256]{1,0:T(8,128)S(1)} %get-tuple-element.14.refs_4_), channel_id=1, source_target_pairs={{0,2},{1,3},{2,0},{3,1},{4,6},{5,7},{6,4},{7,5},{8,10},{9,11},{10,... | collective-permute-start | bytes 24584 | tf_op jit(solution)/shard_map/ppermute | solution.py:258
  20.1 3.7 %collective-permute-start.3 = (f32[8,256]{1,0:T(8,128)S(1)}, f32[8,256]{1,0:T(8,128)S(1)}, u32[]{:S(2)}, u32[]{:S(2)}) collective-permute-start(f32[8,256]{1,0:T(8,128)S(1)} %get-tuple-element.14.refs_4_), channel_id=1, source_target_pairs={{0,1},{1,0},{2,3},{3,2},{4,5},{5,4},{6,7},{7,6},{8,9},{9,8},{10,11... | collective-permute-start | bytes 24584 | tf_op jit(solution)/shard_map/ppermute | solution.py:258
  21.2 12.5 %collective-permute-start.10 = (bf16[3,16,16]{2,1,0:T(8,128)(2,1)S(1)}, bf16[3,16,16]{2,1,0:T(8,128)(2,1)S(1)}, u32[]{:S(2)}, u32[]{:S(2)}) collective-permute-start(bf16[3,16,16]{2,1,0:T(8,128)(2,1)S(1)} %bitcast.11), channel_id=1, source_target_pairs={{0,2},{1,3},{2,0},{3,1},{4,6},{5,7},{6,4},{7,5},{8,10},{9,11},{10,... | collective-permute-start | bytes 4616 | tf_op jit(solution)/shard_map/ppermute | solution.py:248
  23.5 12.0 %collective-permute-start.8 = (bf16[3,256,256]{2,1,0:T(8,128)(2,1)S(1)}, bf16[3,256,256]{2,1,0:T(8,128)(2,1)S(1)}, u32[]{:S(2)}, u32[]{:S(2)}) collective-permute-start(bf16[3,256,256]{2,1,0:T(8,128)(2,1)S(1)} %bitcast.8), channel_id=1, source_target_pairs={{0,2},{1,3},{2,0},{3,1},{4,6},{5,7},{6,4},{7,5},{8,10},{9,11},{10,... | collective-permute-start | bytes 1179656 | tf_op jit(solution)/shard_map/ppermute | solution.py:248
  23.8 18.7 %collective-permute-start.9 = (bf16[3,256,256]{2,1,0:T(8,128)(2,1)S(1)}, bf16[3,256,256]{2,1,0:T(8,128)(2,1)S(1)}, u32[]{:S(2)}, u32[]{:S(2)}) collective-permute-start(bf16[3,256,256]{2,1,0:T(8,128)(2,1)S(1)} %select_bitcast_fusion.refs_9_), channel_id=1, source_target_pairs={{0,2},{1,3},{2,0},{3,1},{4,6},{5,7},{6,4},{7,5},{8,10},{9,11},{10,... | collective-permute-start | bytes 1179656 | tf_op jit(solution)/shard_map/ppermute | solution.py:248
  50.5 7.2 %collective-permute-start.11 = (bf16[16,256,256]{2,1,0:T(8,128)(2,1)S(1)}, bf16[16,256,256]{2,1,0:T(8,128)(2,1)S(1)}, u32[]{:S(2)}, u32[]{:S(2)}) collective-permute-start(bf16[16,256,256]{2,1,0:T(8,128)(2,1)S(1)} %get-tuple-element.18.refs_2_), channel_id=1, source_target_pairs={{0,1},{1,0},{2,3},{3,2},{4,5},{5,4},{6,7},{7,6},{8,9},{9,8},{10,11... | collective-permute-start | bytes 6291464 | tf_op jit(solution)/shard_map/ppermute | solution.py:245
  50.6 7.2 %collective-permute-start.7 = (bf16[16,256,256]{2,1,0:T(8,128)(2,1)S(1)}, bf16[16,256,256]{2,1,0:T(8,128)(2,1)S(1)}, u32[]{:S(2)}, u32[]{:S(2)}) collective-permute-start(bf16[16,256,256]{2,1,0:T(8,128)(2,1)S(1)} %get-tuple-element.15.refs_0_), channel_id=1, source_target_pairs={{0,1},{1,0},{2,3},{3,2},{4,5},{5,4},{6,7},{7,6},{8,9},{9,8},{10,11... | collective-permute-start | bytes 6291464 | tf_op jit(solution)/shard_map/ppermute | solution.py:245
  51.1 23.3 %copy-start.1 = (f32[1,64,16,256]{3,2,1,0:T(8,128)S(1)}, f32[1,64,16,256]{3,2,1,0:T(8,128)}, u32[]{:S(2)}) copy-start(f32[1,64,16,256]{3,2,1,0:T(8,128)} %param.5) | copy-start | bytes 3145732
  51.1 6.7 %collective-permute-start.12 = (f32[8,256]{1,0:T(8,128)S(1)}, f32[8,256]{1,0:T(8,128)S(1)}, u32[]{:S(2)}, u32[]{:S(2)}) collective-permute-start(f32[8,256]{1,0:T(8,128)S(1)} %get-tuple-element.19.refs_5_.norm_ref), channel_id=1, source_target_pairs={{0,1},{1,0},{2,3},{3,2},{4,5},{5,4},{6,7},{7,6},{8,9},{9,8},{10,11... | collective-permute-start | bytes 24584 | tf_op jit(solution)/shard_map/ppermute | solution.py:245
  70.3 3.1 %collective-permute-start.15 = (f32[8,256]{1,0:T(8,128)S(1)}, f32[8,256]{1,0:T(8,128)S(1)}, u32[]{:S(2)}, u32[]{:S(2)}) collective-permute-start(f32[8,256]{1,0:T(8,128)S(1)} %get-tuple-element.21.refs_0_), channel_id=1, source_target_pairs={{0,3},{1,2},{2,1},{3,0},{4,7},{5,6},{6,5},{7,4},{8,11},{9,10},{10,... | collective-permute-start | bytes 24584 | tf_op jit(solution)/shard_map/ppermute | solution.py:258
  70.8 3.7 %collective-permute-start.14 = (f32[8,256]{1,0:T(8,128)S(1)}, f32[8,256]{1,0:T(8,128)S(1)}, u32[]{:S(2)}, u32[]{:S(2)}) collective-permute-start(f32[8,256]{1,0:T(8,128)S(1)} %get-tuple-element.21.refs_0_), channel_id=1, source_target_pairs={{0,2},{1,3},{2,0},{3,1},{4,6},{5,7},{6,4},{7,5},{8,10},{9,11},{10,... | collective-permute-start | bytes 24584 | tf_op jit(solution)/shard_map/ppermute | solution.py:258
  72.2 2.2 %collective-permute-start.13 = (f32[8,256]{1,0:T(8,128)S(1)}, f32[8,256]{1,0:T(8,128)S(1)}, u32[]{:S(2)}, u32[]{:S(2)}) collective-permute-start(f32[8,256]{1,0:T(8,128)S(1)} %get-tuple-element.21.refs_0_), channel_id=1, source_target_pairs={{0,1},{1,0},{2,3},{3,2},{4,5},{5,4},{6,7},{7,6},{8,9},{9,8},{10,11... | collective-permute-start | bytes 24584 | tf_op jit(solution)/shard_map/ppermute | solution.py:258

commit v3 on v2

v3 whole, which is shorter than its diff:
```python
import functools

import jax
import jax.numpy as jnp
from jax import lax
from jax.experimental import pallas as pl
from jax.experimental.pallas import tpu as pltpu
from jax.sharding import PartitionSpec as P

epsilon = 1e-06
CORES = 2
TILE = 16
UNROLL = 4
GROUP = 4
VMEM_LIMIT = 28 * 1024 * 1024
F32 = jnp.float32
BF16 = jnp.bfloat16

vmem = pl.BlockSpec(memory_space=pltpu.VMEM)
smem = pl.BlockSpec(memory_space=pltpu.SMEM)
anywhere = pl.BlockSpec(memory_space=pl.ANY)


def params():
    return pltpu.CompilerParams(vmem_limit_bytes=VMEM_LIMIT)


def cost(flops, moved):
    return pl.CostEstimate(flops=int(flops), bytes_accessed=int(moved), transcendentals=0)


def keep_row(rank, width):
    return (lax.broadcasted_iota(jnp.int32, (1, width), 1) < rank).astype(F32)


def prepare_kernel(rank_ref, guess_ref, x_ref, norm_ref):
    rows, states, width = guess_ref.shape
    masked = guess_ref[...] * keep_row(rank_ref[0], width)[None]
    norm_ref[...] = jnp.full(norm_ref.shape, jnp.sum(masked * masked), F32)
    x_ref[...] = jnp.swapaxes(masked, 0, 1).astype(BF16)


def triangle(half):
    row = lax.broadcasted_iota(jnp.int32, (half, half), 0)
    col = lax.broadcasted_iota(jnp.int32, (half, half), 1)
    return row, col


def pack_kernel(left_ref, right_ref, site_ref, norm_ref, bundle_ref):
    terms, width, _ = left_ref.shape
    states = site_ref.shape[1]
    half = width // 2
    row, col = triangle(half)
    widen = (
        lax.broadcasted_iota(jnp.int32, (states, half), 0) == lax.broadcasted_iota(jnp.int32, (states, half), 1)
    ).astype(BF16)
    norm = norm_ref[0:1, 0:half]
    parts = []
    for _ in range(3):
        parts.append(norm.astype(BF16).astype(F32))
        norm = norm - parts[-1]
    lines = lax.broadcasted_iota(jnp.int32, (TILE, half), 0)
    lines = functools.reduce(jnp.add, [jnp.where(lines == n, parts[n], 0.0) for n in range(3)]).astype(BF16)
    for k in range(terms):
        for m, ref in enumerate((left_ref, right_ref)):
            base = m * (2 * half + TILE)
            upper = ref[k, 0:half, 0:half].astype(F32)
            lower = ref[k, half:width, half:width].astype(F32)
            diagonal = jnp.sum(jnp.where(row == col, lower, 0.0), axis=0, keepdims=True)
            bundle_ref[k, base : base + half, :] = ref[k, 0:half, half:width]
            bundle_ref[k, base + half : base + 2 * half, :] = jnp.where(row <= col, upper, lower).astype(BF16)
            bundle_ref[k, base + 2 * half : base + 2 * half + TILE, :] = jnp.broadcast_to(
                diagonal, (TILE, half)
            ).astype(BF16)
        base = 2 * (2 * half + TILE)
        bundle_ref[k, base : base + states, :] = jnp.dot(
            site_ref[k], widen, preferred_element_type=F32
        ).astype(BF16)
        bundle_ref[k, base + states : base + states + TILE, :] = lines


def unpack(bundle_ref, left_ref, right_ref):
    terms, width, _ = left_ref.shape
    half = width // 2
    row, col = triangle(half)
    for k in range(terms):
        for m, ref in enumerate((left_ref, right_ref)):
            base = m * (2 * half + TILE)
            corner = bundle_ref[k, base : base + half, :]
            mixed = bundle_ref[k, base + half : base + 2 * half, :].astype(F32)
            diagonal = bundle_ref[k, base + 2 * half : base + 2 * half + TILE, :].astype(F32)[0:1]
            turned = mixed.T
            ref[k, 0:half, 0:half] = jnp.where(row <= col, mixed, turned).astype(BF16)
            ref[k, 0:half, half:width] = corner
            ref[k, half:width, 0:half] = corner.astype(F32).T.astype(BF16)
            ref[k, half:width, half:width] = jnp.where(
                row > col, mixed, jnp.where(row == col, diagonal, turned)
            ).astype(BF16)


def spread_site(sites, states, kron_ref):
    size = states * TILE
    lanes = sites[0].shape[1]
    row_state = lax.broadcasted_iota(jnp.int32, (size, states), 0) // TILE
    pick = (row_state == lax.broadcasted_iota(jnp.int32, (size, states), 1)).astype(BF16)
    col_state = lax.broadcasted_iota(jnp.int32, (lanes, size), 1) // TILE
    pick_t = (col_state == lax.broadcasted_iota(jnp.int32, (lanes, size), 0)).astype(BF16)
    same = (
        lax.broadcasted_iota(jnp.int32, (size, size), 0) % TILE
        == lax.broadcasted_iota(jnp.int32, (size, size), 1) % TILE
    )
    for k, site in enumerate(sites):
        tall = jnp.dot(pick, site, preferred_element_type=F32).astype(BF16)
        full = jnp.dot(tall, pick_t, preferred_element_type=F32)
        kron_ref[k * size : (k + 1) * size, :] = jnp.where(same, full, 0.0).astype(BF16)


def mix_sites(source_ref, kron_ref, rotated_ref):
    terms, states, width, _ = rotated_ref.shape

    def step(i, carry):
        at = pl.multiple_of(i * TILE, TILE)
        stack = source_ref[:, pl.ds(at, TILE), :].reshape(states * TILE, width)
        turned = jnp.dot(kron_ref[...], stack, preferred_element_type=F32).astype(BF16)
        rotated_ref[:, :, pl.ds(at, TILE), :] = turned.reshape(terms, states, TILE, width)
        return carry

    lax.fori_loop(0, width // TILE, step, 0, unroll=2 * UNROLL)


def fold(values, width):
    return jnp.sum(values.reshape(values.size // (8 * width), 8, width), axis=0)


def summed(values):
    while len(values) > 1:
        values = [values[n] + values[n + 1] for n in range(0, len(values), 2)]
    return values[0]


def place_pieces(pieces, hops, whole_ref, sems):
    chips = len(hops)
    me = lax.axis_index("term")
    core = me % CORES
    chip = me // CORES
    copies = []
    for n, piece in enumerate(pieces):
        hop = hops[n // 2]
        owner = ((chip - hop + chips) % chips) * CORES + (core if n % 2 == 0 else 1 - core)
        rows = piece.shape[1]
        at = pl.multiple_of(owner * rows, TILE)
        copies.append(pltpu.make_async_copy(piece, whole_ref.at[:, pl.ds(at, rows), :], sems.at[n]))
    for copy in copies:
        copy.start()
    return copies


def rotate_and_mix(left_ref, whole_ref, rotated_ref, mixed_ref, kron_ref):
    terms, states, width, _ = rotated_ref.shape
    mix_sites(whole_ref, kron_ref, rotated_ref)

    def lefts(p, carry):
        for k in range(terms):
            mixed = jnp.dot(left_ref[k], rotated_ref[k, p], preferred_element_type=F32)
            mixed_ref[p, :, k * width : (k + 1) * width] = mixed.astype(BF16)
        return carry

    lax.fori_loop(0, states, lefts, 0, unroll=UNROLL)


def right_rows(right_ref, mixed_ref, at):
    terms, width, _ = right_ref.shape
    rows = mixed_ref[pl.ds(at, GROUP)].reshape(GROUP * width, terms * width)
    stacked = right_ref[...].reshape(terms * width, width)
    return jnp.dot(rows, stacked, preferred_element_type=F32).reshape(GROUP, width, width)


def first_kernel(piece_count, hops, *refs):
    pieces = refs[:piece_count]
    left_ref, right_ref, site_ref, whole_ref, partial_ref = refs[piece_count : piece_count + 5]
    rotated_ref, mixed_ref, kron_ref, sems = refs[piece_count + 5 :]
    terms, states, _, _ = rotated_ref.shape
    copies = place_pieces(pieces, hops, whole_ref, sems)
    spread_site([site_ref[k] for k in range(terms)], states, kron_ref)
    for copy in copies:
        copy.wait()
    rotate_and_mix(left_ref, whole_ref, rotated_ref, mixed_ref, kron_ref)

    def rights(n, carry):
        at = n * GROUP
        partial_ref[pl.ds(at, GROUP)] = right_rows(right_ref, mixed_ref, at).astype(BF16)
        return carry

    lax.fori_loop(0, states // GROUP, rights, 0)


def next_kernel(
    whole_ref,
    before_ref,
    stat_before_ref,
    bundle_ref,
    partial_ref,
    stat_ref,
    rotated_ref,
    mixed_ref,
    kron_ref,
    left_ref,
    right_ref,
):
    terms, states, width, _ = rotated_ref.shape
    base = 2 * (width + TILE)
    spread_site([bundle_ref[k, base : base + states, :] for k in range(terms)], states, kron_ref)
    unpack(bundle_ref, left_ref, right_ref)
    rotate_and_mix(left_ref, whole_ref, rotated_ref, mixed_ref, kron_ref)

    def rights(n, total):
        at = n * GROUP
        before = before_ref[pl.ds(at, GROUP)].astype(F32)
        part = (before + right_rows(right_ref, mixed_ref, at)).astype(BF16)
        partial_ref[pl.ds(at, GROUP)] = part
        held = whole_ref[pl.ds(at, GROUP)].astype(F32)
        return total + fold(held * part.astype(F32), width)

    total = lax.fori_loop(0, states // GROUP, rights, jnp.zeros((8, width), F32))
    lines = bundle_ref[0, base + states : base + states + TILE, :].astype(F32)
    norm = lines[0:1] + lines[1:2] + lines[2:3]
    stat_ref[0:1, :] = jnp.full((1, width), jnp.sum(total), F32)
    stat_ref[1:2, :] = stat_before_ref[1:2, :] + jnp.concatenate([norm, norm], axis=1)
    stat_ref[2:8, :] = jnp.zeros((6, width), F32)


def scales(rank_ref, mine_ref, theirs_ref, scale, width):
    inverse = lax.rsqrt((mine_ref[1:2, :] + theirs_ref[1:2, :]) * scale + epsilon)
    rayleigh = (mine_ref[0:1, :] + theirs_ref[0:1, :]) * (inverse * inverse * scale)
    return inverse, rayleigh, keep_row(rank_ref[0], width) * inverse


def second_kernel(
    scale,
    members,
    rank_ref,
    mine_ref,
    theirs_ref,
    partial_ref,
    other_ref,
    whole_ref,
    left_ref,
    right_ref,
    site_ref,
    out_ref,
    res_ref,
    rotated_ref,
    mixed_ref,
    kron_ref,
):
    terms, states, width, _ = rotated_ref.shape
    spread_site([site_ref[k] for k in range(terms)], states, kron_ref)
    inverse, rayleigh, row_scale = scales(rank_ref, mine_ref, theirs_ref, scale, width)
    back = rayleigh * inverse

    def lefts(p, total):
        sigma = (partial_ref[p].astype(F32) + other_ref[p].astype(F32)) * row_scale
        residual = sigma - back * whole_ref[p].astype(F32)
        rounded = residual.astype(BF16)
        res_ref[p] = rounded
        mixed = jnp.dot(
            left_ref[...].reshape(terms * width, width), rounded, preferred_element_type=F32
        ).astype(BF16)
        for k in range(terms):
            mixed_ref[k, p] = mixed[k * width : (k + 1) * width]
        return total + fold(residual * residual, width)

    square = lax.fori_loop(0, states, lefts, jnp.zeros((8, width), F32), unroll=UNROLL)
    mix_sites(res_ref, kron_ref, rotated_ref)

    def rights(n, total):
        at = n * GROUP
        for k in range(terms):
            turned = rotated_ref[k, pl.ds(at, GROUP)].reshape(GROUP * width, width)
            image = jnp.dot(turned, right_ref[k], preferred_element_type=F32)
            held = mixed_ref[k, pl.ds(at, GROUP)].reshape(GROUP * width, width).astype(F32)
            total = total + fold(held * image, width)
        return total

    cross = lax.fori_loop(0, states // GROUP, rights, jnp.zeros((8, width), F32))
    share = 1.0 / members
    out_ref[0:1, :] = rayleigh * share
    out_ref[1:2, :] = jnp.full((1, width), jnp.sum(square) * (scale * share), F32)
    out_ref[2:3, :] = jnp.full((1, width), jnp.sum(cross) * scale, F32)
    out_ref[3:8, :] = jnp.zeros((5, width), F32)


def own_rows_kernel(
    scale, rank_ref, guess_ref, mine_ref, theirs_ref, partial_ref, other_ref, vector_ref, residual_ref
):
    rows, states, width = guess_ref.shape
    inverse, rayleigh, row_scale = scales(rank_ref, mine_ref, theirs_ref, scale, width)
    own = pl.ds(pl.multiple_of(lax.axis_index("term") * rows, TILE), rows)
    sigma = (partial_ref[:, own, :].astype(F32) + other_ref[:, own, :].astype(F32)) * row_scale[None]
    vector = guess_ref[...] * row_scale[None]
    vector_ref[...] = vector
    residual_ref[...] = jnp.swapaxes(sigma, 0, 1) - rayleigh[None] * vector


def finish_kernel(vector_ref, residual_ref, *refs):
    shares = refs[:-2]
    ritz_ref, energy_ref = refs[-2:]
    stat = summed([share[...] for share in shares])
    rayleigh = stat[0:1, :]
    res_sq = stat[1:2, :]
    res_var = res_sq + epsilon
    curvature = stat[2:3, :] / res_var
    res_scale = jnp.sqrt(res_var)
    coupling = res_sq / res_scale
    half_gap = 0.5 * (rayleigh - curvature)
    energy = 0.5 * (rayleigh + curvature) - jnp.sqrt(half_gap * half_gap + coupling * coupling)
    coeff_new = energy - rayleigh
    coeff_norm = jnp.sqrt(coupling * coupling + coeff_new * coeff_new + epsilon)
    old = coupling / coeff_norm
    new = coeff_new / (coeff_norm * res_scale)
    ritz_ref[...] = old[None] * vector_ref[...] + new[None] * residual_ref[...]
    energy_ref[0] = energy[0, 0]


def shards(wave_guess, left_env, right_env, site_ops, bond_rank):
    guess = wave_guess[0]
    left = left_env[0]
    site = site_ops[0]
    rows, states, width = guess.shape
    terms = left.shape[0]
    members = lax.axis_size("term")
    chips = members // CORES
    segments = lax.axis_size("seg")
    scale = 1.0 / float(rows * members * states * width)
    hops = tuple(range(chips))

    def to_sibling(block):
        return lax.ppermute(block, "term", [(i, i ^ 1) for i in range(members)])

    def to_next_chip(block):
        return lax.ppermute(block, "term", [(i, (i + CORES) % members) for i in range(members)])

    def around(block):
        found = [block]
        for _ in range(chips - 1):
            found.append(to_next_chip(found[-1]))
        return found

    def everyone(block):
        others = [
            lax.ppermute(block, "term", [(i, i ^ bits) for i in range(members)]) for bits in range(1, members)
        ]
        return [block] + others

    tile = jax.ShapeDtypeStruct((8, width), F32)
    x_own, norm_part = pl.pallas_call(
        prepare_kernel,
        out_shape=(jax.ShapeDtypeStruct((states, rows, width), BF16), tile),
        in_specs=[smem, vmem],
        out_specs=(vmem, vmem),
        compiler_params=params(),
        cost_estimate=cost(4 * guess.size, 6 * guess.size),
        name="prepare",
    )(bond_rank, guess)

    shift = [(i + 1, i) for i in range(segments - 1)]
    received = lax.ppermute(right_env, "seg", shift)
    right = jnp.where(lax.axis_index("seg") == segments - 1, right_env, received)[0]

    x_hops = around(x_own)
    pieces = []
    for block in x_hops:
        pieces += [block, to_sibling(block)]
    bundle_rows = 2 * (width + TILE) + states + TILE
    bundle = pl.pallas_call(
        pack_kernel,
        out_shape=jax.ShapeDtypeStruct((terms, bundle_rows, width // 2), BF16),
        in_specs=[vmem] * 4,
        out_specs=vmem,
        compiler_params=params(),
        cost_estimate=cost(8 * left.size, 6 * left.size),
        name="pack",
    )(left, right, site, norm_part)
    bundles = around(bundle)

    whole = (states, width, width)
    rotated = (terms, states, width, width)
    scratch = [
        pltpu.VMEM(rotated, BF16),
        pltpu.VMEM((states, width, terms * width), BF16),
        pltpu.VMEM((terms * states * TILE, states * TILE), BF16),
    ]
    square = pltpu.VMEM((terms, width, width), BF16)
    apply_flops = 2 * terms * states * width * width * (2 * width + states * TILE)
    apply_cost = cost(apply_flops, 4 * states * width * width)
    whole_bf = jax.ShapeDtypeStruct(whole, BF16)
    vector, partial = pl.pallas_call(
        functools.partial(first_kernel, members, hops),
        out_shape=(whole_bf, whole_bf),
        in_specs=[anywhere] * members + [vmem] * 3,
        out_specs=(vmem, vmem),
        scratch_shapes=scratch + [pltpu.SemaphoreType.DMA((members,))],
        compiler_params=params(),
        cost_estimate=apply_cost,
        name="apply_own_terms",
    )(*pieces, left, right, site)
    stat = norm_part
    for hop in hops[1:]:
        partial, stat = pl.pallas_call(
            next_kernel,
            out_shape=(whole_bf, tile),
            in_specs=[vmem] * 4,
            out_specs=(vmem, vmem),
            scratch_shapes=scratch + [square, square],
            compiler_params=params(),
            cost_estimate=apply_cost,
            name="apply_received_terms",
        )(vector, partial, stat, bundles[hop])
    other = to_sibling(partial)
    stat_other = to_sibling(stat)

    share = pl.pallas_call(
        functools.partial(second_kernel, scale, members),
        out_shape=tile,
        in_specs=[smem] + [vmem] * 8,
        out_specs=vmem,
        scratch_shapes=[
            pltpu.VMEM(whole, BF16),
            pltpu.VMEM(rotated, BF16),
            pltpu.VMEM(rotated, BF16),
            pltpu.VMEM((terms * states * TILE, states * TILE), BF16),
        ],
        compiler_params=params(),
        cost_estimate=cost(apply_flops, 6 * states * width * width),
        name="apply_residual",
    )(bond_rank, stat, stat_other, partial, other, vector, left, right, site)
    shares = everyone(share)

    local = jax.ShapeDtypeStruct((rows, states, width), F32)
    vector_own, residual_own = pl.pallas_call(
        functools.partial(own_rows_kernel, scale),
        out_shape=(local, local),
        in_specs=[smem] + [vmem] * 5,
        out_specs=(vmem, vmem),
        compiler_params=params(),
        cost_estimate=cost(8 * guess.size, 16 * guess.size),
        name="own_rows",
    )(bond_rank, guess, stat, stat_other, partial, other)

    ritz, energy = pl.pallas_call(
        finish_kernel,
        out_shape=(local, jax.ShapeDtypeStruct((1,), F32)),
        in_specs=[vmem] * (2 + members),
        out_specs=(vmem, smem),
        compiler_params=params(),
        cost_estimate=cost(3 * guess.size, 12 * guess.size),
        name="finish",
    )(vector_own, residual_own, *shares)
    return (ritz[None], energy)


def solution(mesh):
    in_specs = (
        P("seg", "term", None, None),
        P("seg", "term", None, None),
        P("seg", "term", None, None),
        P("seg", "term", None, None),
        P("seg"),
    )
    out_specs = (P("seg", "term", None, None), P("seg"))
    return jax.shard_map(shards, mesh=mesh, in_specs=in_specs, out_specs=out_specs, check_vma=False)
```

time: 76.2 us -> 57.8 us (0.76)
  waiting for transfers between devices: 29.8 us -> 20.9 us
  Pallas kernels: 30.9 us -> 26.1 us
  starting transfers between devices: 12.7 us -> 7.91 us
    ppermute x4 -> x2, waiting for transfers between devices: 19.3 us -> 13.7 us  [to_next_chip(): lax.ppermute(block, 'term', [(i, (i + CORES) % members) for i in range(me...]
    pallas_call x3 -> x5, Pallas kernels: 22.2 us -> 17.9 us  [the longest x1 8.25 us: shards(): pl.pallas_call(functools.partial(second_kernel, scale, members), out_shap...]
    ppermute x5 -> x4, waiting for transfers between devices: 6.59 us -> 3.67 us  [to_sibling(): return lax.ppermute(block, 'term', [(i, i ^ 1) for i in range(members)])]
    ppermute x4 -> x2, starting transfers between devices: 6.66 us -> 4.04 us  [to_next_chip(): lax.ppermute(block, 'term', [(i, (i + CORES) % members) for i in range(me...]
    ppermute x6 -> x3, starting transfers between devices: 4.07 us -> 1.96 us  [everyone(): lax.ppermute(block, 'term', [(i, i ^ bits) for i in range(members)])]
    ppermute x6 -> x3, waiting for transfers between devices: 3.85 us -> 2.83 us  [everyone(): lax.ppermute(block, 'term', [(i, i ^ bits) for i in range(members)])]
  transfers between devices with their start and end apart: 16 -> 10, of which waited for: 8 -> 6; matrix products, arithmetic and copies ran while one was open for 0% -> 0% of each run, Pallas kernels for 11% -> 15%
where the time goes in v3:
time: 57.8 us; the launch traced here: 57.6 us
  Pallas kernels  26.1 us (45%)
  waiting for transfers between devices  20.9 us (36%)
  starting transfers between devices  7.91 us (14%)
  between operations  1.38 us (2%)
  local copies, waits for them, and re-layouts  1.23 us (2%)
    ppermute x2, waiting for transfers between devices, to_next_chip(): lax.ppermute(block, 'term', [(i, (i + CORES) % members) for i in range(me...  13.7 us
    pallas_call x1, Pallas kernels, shards(): pl.pallas_call(functools.partial(second_kernel, scale, members), out_shap...  8.25 us
    pallas_call x1, Pallas kernels, shards(): pl.pallas_call(functools.partial(first_kernel, members, hops), out_shape=...  7.67 us
    pallas_call x1, Pallas kernels, shards(): pl.pallas_call(next_kernel, out_shape=(whole_bf, tile), in_specs=[vmem] *...  7.65 us
    ppermute x2, starting transfers between devices, to_next_chip(): lax.ppermute(block, 'term', [(i, (i + CORES) % members) for i in range(me...  4.04 us
    ppermute x4, waiting for transfers between devices, to_sibling(): return lax.ppermute(block, 'term', [(i, i ^ 1) for i in range(members)])  3.67 us
    ppermute x3, waiting for transfers between devices, everyone(): lax.ppermute(block, 'term', [(i, i ^ bits) for i in range(members)])  2.83 us
    ppermute x3, starting transfers between devices, everyone(): lax.ppermute(block, 'term', [(i, i ^ bits) for i in range(members)])  1.96 us
  transfers between devices with their start and end apart: 10, of which 6 were waited for; matrix products, arithmetic and copies ran while one was open for 0% of the time, Pallas kernels for 15%

profile of v3, /device:TPU:0, one launch (start us, length us, event | category | flops | bytes accessed | tf_op | source)
XLA Modules:
  0.0 57.6 jit_solution(17138024653987087563)
XLA Ops:
  1.3 0.0 copy-start
  1.3 1.2 %copy-done = f32[1,64,16,256]{3,2,1,0:T(8,128)S(1)} copy-done((f32[1,64,16,256]{3,2,1,0:T(8,128)S(1)}, f32[1,64,16,256]{3,2,1,0:T(8,128)}, u32[]{:S(2)}) %copy-start) | copy-done | bytes 1048600
  2.5 0.0 copy-start.2
  2.5 0.0 copy-start.3
  2.5 0.5 prepare.1
  3.0 3.0 %collective-permute-start.1 = (bf16[16,64,256]{2,1,0:T(8,128)(2,1)S(1)}, bf16[16,64,256]{2,1,0:T(8,128)(2,1)S(1)}, u32[]{:S(2)}, u32[]{:S(2)}) collective-permute-start(bf16[16,64,256]{2,1,0:T(8,128)(2,1)S(1)} %get-tuple-element.12.refs_0_), channel_id=1, source_target_pairs={{0,2},{1,3},{2,0},{3,1},{4,6},{5,7},{6,4},{7,5},{8,10},{9,11},{10,... | collective-permute-start | bytes 1572872 | tf_op jit(solution)/shard_map/ppermute | solution.py:341
  6.1 1.3 %collective-permute-start.3 = (bf16[1,3,256,256]{3,2,1,0:T(8,128)(2,1)}, bf16[1,3,256,256]{3,2,1,0:T(8,128)(2,1)S(1)}, u32[]{:S(2)}, u32[]{:S(2)}) collective-permute-start(bf16[1,3,256,256]{3,2,1,0:T(8,128)(2,1)} %param.7), channel_id=1, source_target_pairs={{4,0},{8,4},{12,8},{16,12},{20,16},{24,20},{28,24},{5,1},{9,5},{13... | collective-permute-start | bytes 1179656 | tf_op jit(solution)/shard_map/ppermute | solution.py:367
  7.4 0.1 collective-permute-start
  7.4 10.6 %collective-permute-done.1.refs_2_ = bf16[16,64,256]{2,1,0:T(8,128)(2,1)S(1)} collective-permute-done((bf16[16,64,256]{2,1,0:T(8,128)(2,1)S(1)}, bf16[16,64,256]{2,1,0:T(8,128)(2,1)S(1)}, u32[]{:S(2)}, u32[]{:S(2)}) %collective-permute-start.1) | collective-permute-done | bytes 524320 | tf_op jit(solution)/shard_map/ppermute | solution.py:341
  18.0 0.0 collective-permute-start.2
  18.0 0.7 %collective-permute-done.3 = bf16[1,3,256,256]{3,2,1,0:T(8,128)(2,1)S(1)} collective-permute-done((bf16[1,3,256,256]{3,2,1,0:T(8,128)(2,1)}, bf16[1,3,256,256]{3,2,1,0:T(8,128)(2,1)S(1)}, u32[]{:S(2)}, u32[]{:S(2)}) %collective-permute-start.3) | collective-permute-done | bytes 393248 | tf_op jit(solution)/shard_map/ppermute | solution.py:367
  18.7 0.1 select_bitcast_fusion.refs_5_.right_ref
  18.8 0.0 copy-done.2
  18.8 0.0 copy-done.3
  18.8 0.2 pack.1
  19.1 1.0 %collective-permute-start.4 = (bf16[3,576,128]{2,1,0:T(8,128)(2,1)S(1)}, bf16[3,576,128]{2,1,0:T(8,128)(2,1)S(1)}, u32[]{:S(2)}, u32[]{:S(2)}) collective-permute-start(bf16[3,576,128]{2,1,0:T(8,128)(2,1)S(1)} %pack.1), channel_id=1, source_target_pairs={{0,2},{1,3},{2,0},{3,1},{4,6},{5,7},{6,4},{7,5},{8,10},{9,11},{10,... | collective-permute-start | bytes 1327112 | tf_op jit(solution)/shard_map/ppermute | solution.py:341
  20.1 0.0 collective-permute-done.refs_1_
  20.1 0.0 collective-permute-done.2.refs_3_
  20.1 7.7 %apply_own_terms.1 = (bf16[16,256,256]{2,1,0:T(8,128)(2,1)S(1)}, bf16[16,256,256]{2,1,0:T(8,128)(2,1)S(1)}) custom-call(bf16[16,64,256]{2,1,0:T(8,128)(2,1)S(1)} %get-tuple-element.12.refs_0_, bf16[16,64,256]{2,1,0:T(8,128)(2,1)S(1)} %collective-permute-done.refs_1_, bf16[16,64,256]{2,1,0:T(8,128)(2,1)S(1)} %collective-permute-done.1.refs_2_, ...), custom_call_target="tpu_custom_call" | custom-call | flops 4831838208 | bytes 4194304 | tf_op jit(solution)/shard_map/apply_own_terms/pallas_call | solution.py:397
  27.8 3.2 %collective-permute-done.4.bundle_ref = bf16[3,576,128]{2,1,0:T(8,128)(2,1)S(1)} collective-permute-done((bf16[3,576,128]{2,1,0:T(8,128)(2,1)S(1)}, bf16[3,576,128]{2,1,0:T(8,128)(2,1)S(1)}, u32[]{:S(2)}, u32[]{:S(2)}) %collective-permute-start.4) | collective-permute-done | bytes 442400 | tf_op jit(solution)/shard_map/ppermute | solution.py:341
  30.9 7.6 %apply_received_terms.1 = (bf16[16,256,256]{2,1,0:T(8,128)(2,1)S(1)}, f32[8,256]{1,0:T(8,128)S(1)}) custom-call(bf16[16,256,256]{2,1,0:T(8,128)(2,1)S(1)} %get-tuple-element.13.whole_ref, bf16[16,256,256]{2,1,0:T(8,128)(2,1)S(1)} %get-tuple-element.14.before_ref, f32[8,256]{1,0:T(8,128)S(1)} %get-tuple-element.15.norm_ref.stat_before_ref, ...), custom_call_target="tpu_custom_call" | custom-call | flops 4831838208 | bytes 4194304 | tf_op jit(solution)/shard_map/apply_received_terms/pallas_call | solution.py:409
  38.6 0.1 collective-permute-start.6
  38.6 0.0 copy-start.1
  38.7 0.5 collective-permute-start.5
  39.1 3.7 %collective-permute-done.5.theirs_ref = f32[8,256]{1,0:T(8,128)S(1)} collective-permute-done((f32[8,256]{1,0:T(8,128)S(1)}, f32[8,256]{1,0:T(8,128)S(1)}, u32[]{:S(2)}, u32[]{:S(2)}) %collective-permute-start.5) | collective-permute-done | bytes 8224 | tf_op jit(solution)/shard_map/ppermute | solution.py:338
  42.8 0.0 collective-permute-done.6.other_ref
  42.8 8.3 %apply_residual.1.refs_0_ = f32[8,256]{1,0:T(8,128)S(1)} custom-call(s32[1]{0:T(128)S(6)} %copy.7.rank_ref, f32[8,256]{1,0:T(8,128)S(1)} %get-tuple-element.16.mine_ref, f32[8,256]{1,0:T(8,128)S(1)} %collective-permute-done.5.theirs_ref, bf16[16,256,256]{2,1,0:T(8,128)(2,1)S(1)} %get-tuple-element.17.partial_ref, ...), custom_call_target="tpu_custom_call" | custom-call | flops 4831838208 | bytes 6291456 | tf_op jit(solution)/shard_map/apply_residual/pallas_call | solution.py:422
  51.1 1.6 %collective-permute-start.9 = (f32[8,256]{1,0:T(8,128)S(1)}, f32[8,256]{1,0:T(8,128)S(1)}, u32[]{:S(2)}, u32[]{:S(2)}) collective-permute-start(f32[8,256]{1,0:T(8,128)S(1)} %apply_residual.1.refs_0_), channel_id=1, source_target_pairs={{0,3},{1,2},{2,1},{3,0},{4,7},{5,6},{6,5},{7,4},{8,11},{9,10},{10,... | collective-permute-start | bytes 24584 | tf_op jit(solution)/shard_map/ppermute | solution.py:351
  52.6 0.3 collective-permute-start.8
  53.0 0.1 collective-permute-start.7
  53.0 0.0 copy-done.1
  53.0 0.5 own_rows.1
  53.5 0.7 %collective-permute-done.9.refs_3_ = f32[8,256]{1,0:T(8,128)S(1)} collective-permute-done((f32[8,256]{1,0:T(8,128)S(1)}, f32[8,256]{1,0:T(8,128)S(1)}, u32[]{:S(2)}, u32[]{:S(2)}) %collective-permute-start.9) | collective-permute-done | bytes 8224 | tf_op jit(solution)/shard_map/ppermute | solution.py:351
  54.2 2.1 %collective-permute-done.8.refs_2_ = f32[8,256]{1,0:T(8,128)S(1)} collective-permute-done((f32[8,256]{1,0:T(8,128)S(1)}, f32[8,256]{1,0:T(8,128)S(1)}, u32[]{:S(2)}, u32[]{:S(2)}) %collective-permute-start.8) | collective-permute-done | bytes 8224 | tf_op jit(solution)/shard_map/ppermute | solution.py:351
  56.3 0.0 collective-permute-done.7.refs_1_
  56.3 1.3 %finish.1 = (f32[64,16,256]{2,1,0:T(8,128)}, f32[1]{0:T(128)}) custom-call(f32[64,16,256]{2,1,0:T(8,128)S(1)} %get-tuple-element.18.vector_ref, f32[64,16,256]{2,1,0:T(8,128)S(1)} %get-tuple-element.19.residual_ref, f32[8,256]{1,0:T(8,128)S(1)} %apply_residual.1.refs_0_, f32[8,256]{1,0:T(8,128)S(1)} %collective-permute-done.7.refs_1_, ...), custom_call_target="tpu_custom_call" | custom-call | flops 786432 | bytes 3145728 | tf_op jit(solution)/shard_map/finish/pallas_call | solution.py:450
Async XLA Ops:
  1.3 1.2 %copy-start = (f32[1,64,16,256]{3,2,1,0:T(8,128)S(1)}, f32[1,64,16,256]{3,2,1,0:T(8,128)}, u32[]{:S(2)}) copy-start(f32[1,64,16,256]{3,2,1,0:T(8,128)} %param.5) | copy-start | bytes 3145732
  2.5 16.3 %copy-start.2 = (bf16[1,3,256,256]{3,2,1,0:T(8,128)(2,1)S(1)}, bf16[1,3,256,256]{3,2,1,0:T(8,128)(2,1)}, u32[]{:S(2)}) copy-start(bf16[1,3,256,256]{3,2,1,0:T(8,128)(2,1)} %param.6) | copy-start | bytes 1179652
  2.5 16.3 %copy-start.3 = (bf16[1,3,16,16]{3,2,1,0:T(8,128)(2,1)S(1)}, bf16[1,3,16,16]{3,2,1,0:T(8,128)(2,1)}, u32[]{:S(2)}) copy-start(bf16[1,3,16,16]{3,2,1,0:T(8,128)(2,1)} %param.8) | copy-start | bytes 4612
  3.0 15.0 %collective-permute-start.1 = (bf16[16,64,256]{2,1,0:T(8,128)(2,1)S(1)}, bf16[16,64,256]{2,1,0:T(8,128)(2,1)S(1)}, u32[]{:S(2)}, u32[]{:S(2)}) collective-permute-start(bf16[16,64,256]{2,1,0:T(8,128)(2,1)S(1)} %get-tuple-element.12.refs_0_), channel_id=1, source_target_pairs={{0,2},{1,3},{2,0},{3,1},{4,6},{5,7},{6,4},{7,5},{8,10},{9,11},{10,... | collective-permute-start | bytes 1572872 | tf_op jit(solution)/shard_map/ppermute | solution.py:341
  6.1 12.7 %collective-permute-start.3 = (bf16[1,3,256,256]{3,2,1,0:T(8,128)(2,1)}, bf16[1,3,256,256]{3,2,1,0:T(8,128)(2,1)S(1)}, u32[]{:S(2)}, u32[]{:S(2)}) collective-permute-start(bf16[1,3,256,256]{3,2,1,0:T(8,128)(2,1)} %param.7), channel_id=1, source_target_pairs={{4,0},{8,4},{12,8},{16,12},{20,16},{24,20},{28,24},{5,1},{9,5},{13... | collective-permute-start | bytes 1179656 | tf_op jit(solution)/shard_map/ppermute | solution.py:367
  7.4 12.7 %collective-permute-start = (bf16[16,64,256]{2,1,0:T(8,128)(2,1)S(1)}, bf16[16,64,256]{2,1,0:T(8,128)(2,1)S(1)}, u32[]{:S(2)}, u32[]{:S(2)}) collective-permute-start(bf16[16,64,256]{2,1,0:T(8,128)(2,1)S(1)} %get-tuple-element.12.refs_0_), channel_id=1, source_target_pairs={{0,1},{1,0},{2,3},{3,2},{4,5},{5,4},{6,7},{7,6},{8,9},{9,8},{10,11... | collective-permute-start | bytes 1572872 | tf_op jit(solution)/shard_map/ppermute | solution.py:338
  18.0 2.1 %collective-permute-start.2 = (bf16[16,64,256]{2,1,0:T(8,128)(2,1)S(1)}, bf16[16,64,256]{2,1,0:T(8,128)(2,1)S(1)}, u32[]{:S(2)}, u32[]{:S(2)}) collective-permute-start(bf16[16,64,256]{2,1,0:T(8,128)(2,1)S(1)} %collective-permute-done.1.refs_2_), channel_id=1, source_target_pairs={{0,1},{1,0},{2,3},{3,2},{4,5},{5,4},{6,7},{7,6},{8,9},{9,8},{10,11... | collective-permute-start | bytes 1572872 | tf_op jit(solution)/shard_map/ppermute | solution.py:338
  19.1 11.8 %collective-permute-start.4 = (bf16[3,576,128]{2,1,0:T(8,128)(2,1)S(1)}, bf16[3,576,128]{2,1,0:T(8,128)(2,1)S(1)}, u32[]{:S(2)}, u32[]{:S(2)}) collective-permute-start(bf16[3,576,128]{2,1,0:T(8,128)(2,1)S(1)} %pack.1), channel_id=1, source_target_pairs={{0,2},{1,3},{2,0},{3,1},{4,6},{5,7},{6,4},{7,5},{8,10},{9,11},{10,... | collective-permute-start | bytes 1327112 | tf_op jit(solution)/shard_map/ppermute | solution.py:341
  38.6 4.2 %collective-permute-start.6 = (bf16[16,256,256]{2,1,0:T(8,128)(2,1)S(1)}, bf16[16,256,256]{2,1,0:T(8,128)(2,1)S(1)}, u32[]{:S(2)}, u32[]{:S(2)}) collective-permute-start(bf16[16,256,256]{2,1,0:T(8,128)(2,1)S(1)} %get-tuple-element.17.partial_ref), channel_id=1, source_target_pairs={{0,1},{1,0},{2,3},{3,2},{4,5},{5,4},{6,7},{7,6},{8,9},{9,8},{10,11... | collective-permute-start | bytes 6291464 | tf_op jit(solution)/shard_map/ppermute | solution.py:338
  38.6 14.4 %copy-start.1 = (f32[1,64,16,256]{3,2,1,0:T(8,128)S(1)}, f32[1,64,16,256]{3,2,1,0:T(8,128)}, u32[]{:S(2)}) copy-start(f32[1,64,16,256]{3,2,1,0:T(8,128)} %param.5) | copy-start | bytes 3145732
  38.7 4.1 %collective-permute-start.5 = (f32[8,256]{1,0:T(8,128)S(1)}, f32[8,256]{1,0:T(8,128)S(1)}, u32[]{:S(2)}, u32[]{:S(2)}) collective-permute-start(f32[8,256]{1,0:T(8,128)S(1)} %get-tuple-element.16.mine_ref), channel_id=1, source_target_pairs={{0,1},{1,0},{2,3},{3,2},{4,5},{5,4},{6,7},{7,6},{8,9},{9,8},{10,11... | collective-permute-start | bytes 24584 | tf_op jit(solution)/shard_map/ppermute | solution.py:338
  51.1 3.1 %collective-permute-start.9 = (f32[8,256]{1,0:T(8,128)S(1)}, f32[8,256]{1,0:T(8,128)S(1)}, u32[]{:S(2)}, u32[]{:S(2)}) collective-permute-start(f32[8,256]{1,0:T(8,128)S(1)} %apply_residual.1.refs_0_), channel_id=1, source_target_pairs={{0,3},{1,2},{2,1},{3,0},{4,7},{5,6},{6,5},{7,4},{8,11},{9,10},{10,... | collective-permute-start | bytes 24584 | tf_op jit(solution)/shard_map/ppermute | solution.py:351
  52.6 3.7 %collective-permute-start.8 = (f32[8,256]{1,0:T(8,128)S(1)}, f32[8,256]{1,0:T(8,128)S(1)}, u32[]{:S(2)}, u32[]{:S(2)}) collective-permute-start(f32[8,256]{1,0:T(8,128)S(1)} %apply_residual.1.refs_0_), channel_id=1, source_target_pairs={{0,2},{1,3},{2,0},{3,1},{4,6},{5,7},{6,4},{7,5},{8,10},{9,11},{10,... | collective-permute-start | bytes 24584 | tf_op jit(solution)/shard_map/ppermute | solution.py:351
  53.0 3.3 %collective-permute-start.7 = (f32[8,256]{1,0:T(8,128)S(1)}, f32[8,256]{1,0:T(8,128)S(1)}, u32[]{:S(2)}, u32[]{:S(2)}) collective-permute-start(f32[8,256]{1,0:T(8,128)S(1)} %apply_residual.1.refs_0_), channel_id=1, source_target_pairs={{0,1},{1,0},{2,3},{3,2},{4,5},{5,4},{6,7},{7,6},{8,9},{9,8},{10,11... | collective-permute-start | bytes 24584 | tf_op jit(solution)/shard_map/ppermute | solution.py:351

commit v4 on v3

--- a/solution.py
+++ b/solution.py
@@ -26,7 +26,7 @@
 
 
 def cost(flops, moved):
-    return pl.CostEstimate(flops=int(flops), bytes_accessed=int(moved), transcendentals=0)
+    return pl.CostEstimate(flops=int(flops) // 100, bytes_accessed=int(moved) // 100, transcendentals=0)
 
 
 def keep_row(rank, width):
@@ -46,11 +46,42 @@
     return row, col
 
 
-def pack_kernel(left_ref, right_ref, site_ref, norm_ref, bundle_ref):
-    terms, width, _ = left_ref.shape
-    states = site_ref.shape[1]
+def pack_symmetric(block_ref, k, out_ref, base):
+    width = block_ref.shape[1]
     half = width // 2
     row, col = triangle(half)
+    upper = block_ref[k, 0:half, 0:half].astype(F32)
+    lower = block_ref[k, half:width, half:width].astype(F32)
+    out_ref[k, base : base + half, :] = block_ref[k, 0:half, half:width]
+    out_ref[k, base + half : base + width, :] = jnp.where(row <= col, upper, lower).astype(BF16)
+    return jnp.sum(jnp.where(row == col, lower, 0.0), axis=0, keepdims=True)
+
+
+def pack_kernel(block_ref, packed_ref):
+    terms, width, _ = block_ref.shape
+    for k in range(terms):
+        diagonal = pack_symmetric(block_ref, k, packed_ref, 0)
+        packed_ref[k, width : width + TILE, :] = jnp.broadcast_to(diagonal, (TILE, width // 2)).astype(BF16)
+
+
+def unpack_symmetric(packed_ref, k, base, diagonal, full_ref):
+    width = full_ref.shape[1]
+    half = width // 2
+    row, col = triangle(half)
+    corner = packed_ref[k, base : base + half, :]
+    mixed = packed_ref[k, base + half : base + width, :].astype(F32)
+    turned = mixed.T
+    full_ref[k, 0:half, 0:half] = jnp.where(row <= col, mixed, turned).astype(BF16)
+    full_ref[k, 0:half, half:width] = corner
+    full_ref[k, half:width, 0:half] = corner.astype(F32).T.astype(BF16)
+    full_ref[k, half:width, half:width] = jnp.where(
+        row > col, mixed, jnp.where(row == col, diagonal, turned)
+    ).astype(BF16)
+
+
+def header_kernel(site_ref, norm_ref, header_ref):
+    terms, states, _ = site_ref.shape
+    half = header_ref.shape[2]
     widen = (
         lax.broadcasted_iota(jnp.int32, (states, half), 0) == lax.broadcasted_iota(jnp.int32, (states, half), 1)
     ).astype(BF16)
@@ -62,45 +93,15 @@
     lines = lax.broadcasted_iota(jnp.int32, (TILE, half), 0)
     lines = functools.reduce(jnp.add, [jnp.where(lines == n, parts[n], 0.0) for n in range(3)]).astype(BF16)
     for k in range(terms):
-        for m, ref in enumerate((left_ref, right_ref)):
-            base = m * (2 * half + TILE)
-            upper = ref[k, 0:half, 0:half].astype(F32)
-            lower = ref[k, half:width, half:width].astype(F32)
-            diagonal = jnp.sum(jnp.where(row == col, lower, 0.0), axis=0, keepdims=True)
-            bundle_ref[k, base : base + half, :] = ref[k, 0:half, half:width]
-            bundle_ref[k, base + half : base + 2 * half, :] = jnp.where(row <= col, upper, lower).astype(BF16)
-            bundle_ref[k, base + 2 * half : base + 2 * half + TILE, :] = jnp.broadcast_to(
-                diagonal, (TILE, half)
-            ).astype(BF16)
-        base = 2 * (2 * half + TILE)
-        bundle_ref[k, base : base + states, :] = jnp.dot(
-            site_ref[k], widen, preferred_element_type=F32
-        ).astype(BF16)
-        bundle_ref[k, base + states : base + states + TILE, :] = lines
-
-
-def unpack(bundle_ref, left_ref, right_ref):
-    terms, width, _ = left_ref.shape
-    half = width // 2
-    row, col = triangle(half)
-    for k in range(terms):
-        for m, ref in enumerate((left_ref, right_ref)):
-            base = m * (2 * half + TILE)
-            corner = bundle_ref[k, base : base + half, :]
-            mixed = bundle_ref[k, base + half : base + 2 * half, :].astype(F32)
-            diagonal = bundle_ref[k, base + 2 * half : base + 2 * half + TILE, :].astype(F32)[0:1]
-            turned = mixed.T
-            ref[k, 0:half, 0:half] = jnp.where(row <= col, mixed, turned).astype(BF16)
-            ref[k, 0:half, half:width] = corner
-            ref[k, half:width, 0:half] = corner.astype(F32).T.astype(BF16)
-            ref[k, half:width, half:width] = jnp.where(
-                row > col, mixed, jnp.where(row == col, diagonal, turned)
-            ).astype(BF16)
-
-
-def spread_site(sites, states, kron_ref):
-    size = states * TILE
-    lanes = sites[0].shape[1]
+        header_ref[k, 0:states, :] = jnp.dot(site_ref[k], widen, preferred_element_type=F32).astype(BF16)
+        header_ref[k, states : states + TILE, :] = lines
+
+
+def spread_kernel(header_ref, kron_ref):
+    terms = header_ref.shape[0]
+    lanes = header_ref.shape[2]
+    size = kron_ref.shape[1]
+    states = size // TILE
     row_state = lax.broadcasted_iota(jnp.int32, (size, states), 0) // TILE
     pick = (row_state == lax.broadcasted_iota(jnp.int32, (size, states), 1)).astype(BF16)
     col_state = lax.broadcasted_iota(jnp.int32, (lanes, size), 1) // TILE
@@ -109,23 +110,25 @@
         lax.broadcasted_iota(jnp.int32, (size, size), 0) % TILE
         == lax.broadcasted_iota(jnp.int32, (size, size), 1) % TILE
     )
-    for k, site in enumerate(sites):
-        tall = jnp.dot(pick, site, preferred_element_type=F32).astype(BF16)
+    for k in range(terms):
+        tall = jnp.dot(pick, header_ref[k, 0:states, :], preferred_element_type=F32).astype(BF16)
         full = jnp.dot(tall, pick_t, preferred_element_type=F32)
         kron_ref[k * size : (k + 1) * size, :] = jnp.where(same, full, 0.0).astype(BF16)
 
 
-def mix_sites(source_ref, kron_ref, rotated_ref):
-    terms, states, width, _ = rotated_ref.shape
+def mix_sites(source_ref, kron_ref, rotated_ref, base, unroll):
+    terms, states, _, width = rotated_ref.shape
+    rows = source_ref.shape[1]
 
     def step(i, carry):
         at = pl.multiple_of(i * TILE, TILE)
+        to = pl.multiple_of(base + i * TILE, TILE)
         stack = source_ref[:, pl.ds(at, TILE), :].reshape(states * TILE, width)
         turned = jnp.dot(kron_ref[...], stack, preferred_element_type=F32).astype(BF16)
-        rotated_ref[:, :, pl.ds(at, TILE), :] = turned.reshape(terms, states, TILE, width)
+        rotated_ref[:, :, pl.ds(to, TILE), :] = turned.reshape(terms, states, TILE, width)
         return carry
 
-    lax.fori_loop(0, width // TILE, step, 0, unroll=2 * UNROLL)
+    lax.fori_loop(0, rows // TILE, step, 0, unroll=min(unroll, rows // TILE))
 
 
 def fold(values, width):
@@ -138,26 +141,92 @@
     return values[0]
 
 
-def place_pieces(pieces, hops, whole_ref, sems):
+def chip_kernel(hop, chips, *refs):
+    own_ref, sib_ref, left_ref, packed_ref, kron_ref = refs[:5]
+    if hop == 0:
+        before_ref = None
+        out_ref, bundle_ref = refs[5:7]
+        rest = refs[7:]
+    else:
+        before_ref, out_ref = refs[5:7]
+        rest = refs[7:]
+    rotated_ref, turned_ref, columns_ref, right_ref = rest
+    terms, states, chip_rows, width = rotated_ref.shape
+    rows = own_ref.shape[1]
+    me = lax.axis_index("term")
+    core = me % CORES
+    chip = (me // CORES - hop + chips) % chips
+    mix_sites(own_ref, kron_ref, rotated_ref, core * rows, UNROLL)
+    mix_sites(sib_ref, kron_ref, rotated_ref, (1 - core) * rows, UNROLL)
+    at = pl.multiple_of(chip * chip_rows, TILE)
+    for k in range(terms):
+        diagonal = packed_ref[k, width : width + TILE, :].astype(F32)[0:1]
+        unpack_symmetric(packed_ref, k, 0, diagonal, right_ref)
+    columns = jnp.concatenate([left_ref[k, pl.ds(at, chip_rows), :] for k in range(terms)], axis=0)
+    columns_ref[...] = columns.astype(F32).T.astype(BF16)
+    if hop == 0:
+        line = lax.broadcasted_iota(jnp.int32, (TILE, width // 2), 0)
+        for k in range(terms):
+            first = packed_ref[k, width : width + TILE, :].astype(F32)
+            second = pack_symmetric(left_ref, k, bundle_ref, width + TILE)
+            bundle_ref[k, 0:width, :] = packed_ref[k, 0:width, :]
+            bundle_ref[k, width : width + TILE, :] = jnp.where(line == 0, first, second).astype(BF16)
+    for k in range(terms):
+        for n in range(0, states, 8):
+            source = rotated_ref[k, n : n + 8].reshape(8 * chip_rows, width)
+            turned = jnp.dot(source, right_ref[k], preferred_element_type=F32).astype(BF16)
+            turned_ref[n : n + 8, k * chip_rows : (k + 1) * chip_rows, :] = turned.reshape(8, chip_rows, width)
+
+    def lefts(p, carry):
+        image = jnp.dot(columns_ref[...], turned_ref[p], preferred_element_type=F32)
+        if before_ref is not None:
+            image = before_ref[p] + image
+        out_ref[p] = image
+        return carry
+
+    lax.fori_loop(0, states, lefts, 0, unroll=UNROLL)
+
+
+def rotate_kernel(piece_count, hops, *refs):
+    pieces = refs[:piece_count]
+    kron_ref, rotated_ref, whole_ref, sems = refs[piece_count:]
     chips = len(hops)
     me = lax.axis_index("term")
     core = me % CORES
     chip = me // CORES
     copies = []
     for n, piece in enumerate(pieces):
-        hop = hops[n // 2]
-        owner = ((chip - hop + chips) % chips) * CORES + (core if n % 2 == 0 else 1 - core)
         rows = piece.shape[1]
+        owner = ((chip - hops[n // 2] + chips) % chips) * CORES + (core if n % 2 == 0 else 1 - core)
         at = pl.multiple_of(owner * rows, TILE)
         copies.append(pltpu.make_async_copy(piece, whole_ref.at[:, pl.ds(at, rows), :], sems.at[n]))
+        copies[-1].start()
+    for n, piece in enumerate(pieces):
+        rows = piece.shape[1]
+        owner = ((chip - hops[n // 2] + chips) % chips) * CORES + (core if n % 2 == 0 else 1 - core)
+        mix_sites(piece, kron_ref, rotated_ref, owner * rows, UNROLL)
     for copy in copies:
-        copy.start()
-    return copies
-
-
-def rotate_and_mix(left_ref, whole_ref, rotated_ref, mixed_ref, kron_ref):
+        copy.wait()
+
+
+def next_kernel(
+    whole_ref,
+    rotated_ref,
+    before_ref,
+    stat_before_ref,
+    header_ref,
+    bundle_ref,
+    partial_ref,
+    stat_ref,
+    mixed_ref,
+    left_ref,
+    right_ref,
+):
     terms, states, width, _ = rotated_ref.shape
-    mix_sites(whole_ref, kron_ref, rotated_ref)
+    for k in range(terms):
+        diagonals = bundle_ref[k, width : width + TILE, :].astype(F32)
+        unpack_symmetric(bundle_ref, k, width + TILE, diagonals[1:2], left_ref)
+        unpack_symmetric(bundle_ref, k, 0, diagonals[0:1], right_ref)
 
     def lefts(p, carry):
         for k in range(terms):
@@ -167,62 +236,18 @@
 
     lax.fori_loop(0, states, lefts, 0, unroll=UNROLL)
 
-
-def right_rows(right_ref, mixed_ref, at):
-    terms, width, _ = right_ref.shape
-    rows = mixed_ref[pl.ds(at, GROUP)].reshape(GROUP * width, terms * width)
-    stacked = right_ref[...].reshape(terms * width, width)
-    return jnp.dot(rows, stacked, preferred_element_type=F32).reshape(GROUP, width, width)
-
-
-def first_kernel(piece_count, hops, *refs):
-    pieces = refs[:piece_count]
-    left_ref, right_ref, site_ref, whole_ref, partial_ref = refs[piece_count : piece_count + 5]
-    rotated_ref, mixed_ref, kron_ref, sems = refs[piece_count + 5 :]
-    terms, states, _, _ = rotated_ref.shape
-    copies = place_pieces(pieces, hops, whole_ref, sems)
-    spread_site([site_ref[k] for k in range(terms)], states, kron_ref)
-    for copy in copies:
-        copy.wait()
-    rotate_and_mix(left_ref, whole_ref, rotated_ref, mixed_ref, kron_ref)
-
-    def rights(n, carry):
-        at = n * GROUP
-        partial_ref[pl.ds(at, GROUP)] = right_rows(right_ref, mixed_ref, at).astype(BF16)
-        return carry
-
-    lax.fori_loop(0, states // GROUP, rights, 0)
-
-
-def next_kernel(
-    whole_ref,
-    before_ref,
-    stat_before_ref,
-    bundle_ref,
-    partial_ref,
-    stat_ref,
-    rotated_ref,
-    mixed_ref,
-    kron_ref,
-    left_ref,
-    right_ref,
-):
-    terms, states, width, _ = rotated_ref.shape
-    base = 2 * (width + TILE)
-    spread_site([bundle_ref[k, base : base + states, :] for k in range(terms)], states, kron_ref)
-    unpack(bundle_ref, left_ref, right_ref)
-    rotate_and_mix(left_ref, whole_ref, rotated_ref, mixed_ref, kron_ref)
-
     def rights(n, total):
         at = n * GROUP
-        before = before_ref[pl.ds(at, GROUP)].astype(F32)
-        part = (before + right_rows(right_ref, mixed_ref, at)).astype(BF16)
+        rows = mixed_ref[pl.ds(at, GROUP)].reshape(GROUP * width, terms * width)
+        stacked = right_ref[...].reshape(terms * width, width)
+        image = jnp.dot(rows, stacked, preferred_element_type=F32).reshape(GROUP, width, width)
+        part = (before_ref[pl.ds(at, GROUP)].astype(F32) + image).astype(partial_ref.dtype)
         partial_ref[pl.ds(at, GROUP)] = part
         held = whole_ref[pl.ds(at, GROUP)].astype(F32)
         return total + fold(held * part.astype(F32), width)
 
     total = lax.fori_loop(0, states // GROUP, rights, jnp.zeros((8, width), F32))
-    lines = bundle_ref[0, base + states : base + states + TILE, :].astype(F32)
+    lines = header_ref[0, states : states + TILE, :].astype(F32)
     norm = lines[0:1] + lines[1:2] + lines[2:3]
     stat_ref[0:1, :] = jnp.full((1, width), jnp.sum(total), F32)
     stat_ref[1:2, :] = stat_before_ref[1:2, :] + jnp.concatenate([norm, norm], axis=1)
@@ -245,16 +270,18 @@
     other_ref,
     whole_ref,
     left_ref,
-    right_ref,
-    site_ref,
+    packed_ref,
+    kron_ref,
     out_ref,
     res_ref,
     rotated_ref,
     mixed_ref,
-    kron_ref,
+    right_ref,
 ):
     terms, states, width, _ = rotated_ref.shape
-    spread_site([site_ref[k] for k in range(terms)], states, kron_ref)
+    for k in range(terms):
+        diagonal = packed_ref[k, width : width + TILE, :].astype(F32)[0:1]
+        unpack_symmetric(packed_ref, k, 0, diagonal, right_ref)
     inverse, rayleigh, row_scale = scales(rank_ref, mine_ref, theirs_ref, scale, width)
     back = rayleigh * inverse
 
@@ -271,7 +298,7 @@
         return total + fold(residual * residual, width)
 
     square = lax.fori_loop(0, states, lefts, jnp.zeros((8, width), F32), unroll=UNROLL)
-    mix_sites(res_ref, kron_ref, rotated_ref)
+    mix_sites(res_ref, kron_ref, rotated_ref, 0, 2 * UNROLL)
 
     def rights(n, total):
         at = n * GROUP
@@ -363,59 +390,104 @@
         name="prepare",
     )(bond_rank, guess)
 
-    shift = [(i + 1, i) for i in range(segments - 1)]
-    received = lax.ppermute(right_env, "seg", shift)
-    right = jnp.where(lax.axis_index("seg") == segments - 1, right_env, received)[0]
-
-    x_hops = around(x_own)
-    pieces = []
-    for block in x_hops:
-        pieces += [block, to_sibling(block)]
-    bundle_rows = 2 * (width + TILE) + states + TILE
-    bundle = pl.pallas_call(
+    packed_own = pl.pallas_call(
         pack_kernel,
-        out_shape=jax.ShapeDtypeStruct((terms, bundle_rows, width // 2), BF16),
-        in_specs=[vmem] * 4,
+        out_shape=jax.ShapeDtypeStruct((terms, width + TILE, width // 2), BF16),
+        in_specs=[vmem],
         out_specs=vmem,
         compiler_params=params(),
-        cost_estimate=cost(8 * left.size, 6 * left.size),
-        name="pack",
-    )(left, right, site, norm_part)
-    bundles = around(bundle)
+        cost_estimate=cost(4 * left.size, 3 * left.size),
+        name="pack_right",
+    )(right_env[0])
+    shift = [(i + 1, i) for i in range(segments - 1)]
+    received = lax.ppermute(packed_own, "seg", shift)
+    packed = jnp.where(lax.axis_index("seg") == segments - 1, packed_own, received)
+
+    x_hops = around(x_own)
+    pieces = [x_own, to_sibling(x_own)]
+
+    headers = around(
+        pl.pallas_call(
+            header_kernel,
+            out_shape=jax.ShapeDtypeStruct((terms, states + TILE, width // 2), BF16),
+            in_specs=[vmem] * 2,
+            out_specs=vmem,
+            compiler_params=params(),
+            cost_estimate=cost(2 * site.size * width, 4 * site.size),
+            name="header",
+        )(site, norm_part)
+    )
+    size = states * TILE
+    krons = [
+        pl.pallas_call(
+            spread_kernel,
+            out_shape=jax.ShapeDtypeStruct((terms * size, size), BF16),
+            in_specs=[vmem],
+            out_specs=vmem,
+            compiler_params=params(),
+            cost_estimate=cost(2 * terms * size * size * width, 2 * terms * size * size),
+            name="spread_site",
+        )(header)
+        for header in headers
+    ]
+
+    left, krons = lax.optimization_barrier((left, krons))
 
     whole = (states, width, width)
+    whole_bf = jax.ShapeDtypeStruct(whole, BF16)
+    whole_f32 = jax.ShapeDtypeStruct(whole, F32)
     rotated = (terms, states, width, width)
-    scratch = [
-        pltpu.VMEM(rotated, BF16),
-        pltpu.VMEM((states, width, terms * width), BF16),
-        pltpu.VMEM((terms * states * TILE, states * TILE), BF16),
-    ]
     square = pltpu.VMEM((terms, width, width), BF16)
-    apply_flops = 2 * terms * states * width * width * (2 * width + states * TILE)
-    apply_cost = cost(apply_flops, 4 * states * width * width)
-    whole_bf = jax.ShapeDtypeStruct(whole, BF16)
-    vector, partial = pl.pallas_call(
-        functools.partial(first_kernel, members, hops),
-        out_shape=(whole_bf, whole_bf),
-        in_specs=[anywhere] * members + [vmem] * 3,
-        out_specs=(vmem, vmem),
-        scratch_shapes=scratch + [pltpu.SemaphoreType.DMA((members,))],
-        compiler_params=params(),
-        cost_estimate=apply_cost,
-        name="apply_own_terms",
-    )(*pieces, left, right, site)
+    chip_rows = CORES * rows
+    stage_flops = 2 * terms * states * width * width * width
+    partial = None
+    for hop in hops:
+        outs = [whole_f32]
+        if hop == 0:
+            outs.append(jax.ShapeDtypeStruct((terms, 2 * width + TILE, width // 2), BF16))
+        result = pl.pallas_call(
+            functools.partial(chip_kernel, hop, chips),
+            out_shape=tuple(outs),
+            in_specs=[vmem] * (5 if hop == 0 else 6),
+            out_specs=tuple([vmem] * len(outs)),
+            scratch_shapes=[
+                pltpu.VMEM((terms, states, chip_rows, width), BF16),
+                pltpu.VMEM((states, terms * chip_rows, width), BF16),
+                pltpu.VMEM((width, terms * chip_rows), BF16),
+                square,
+            ],
+            compiler_params=params(),
+            cost_estimate=cost(3 * stage_flops * chip_rows / width, 8 * states * width * width),
+            name="apply_rows_here" if hop == 0 else "apply_rows_there",
+        )(*pieces[2 * hop : 2 * hop + 2], left, packed, krons[0], *([] if hop == 0 else [partial]))
+        partial = result[0]
+        if hop == 0:
+            bundles = around(result[1])
+            for block in x_hops[1:]:
+                block = lax.optimization_barrier((block, result[1]))[0]
+                pieces += [block, to_sibling(block)]
     stat = norm_part
     for hop in hops[1:]:
+        turned, vector = pl.pallas_call(
+            functools.partial(rotate_kernel, members, hops),
+            out_shape=(jax.ShapeDtypeStruct(rotated, BF16), whole_bf),
+            in_specs=[vmem] * (members + 1),
+            out_specs=(vmem, vmem),
+            scratch_shapes=[pltpu.SemaphoreType.DMA((members,))],
+            compiler_params=params(),
+            cost_estimate=cost(stage_flops, 8 * states * width * width),
+            name="rotate_received",
+        )(*pieces, krons[hop])
         partial, stat = pl.pallas_call(
             next_kernel,
-            out_shape=(whole_bf, tile),
-            in_specs=[vmem] * 4,
+            out_shape=(whole_bf if hop == hops[-1] else whole_f32, tile),
+            in_specs=[vmem] * 6,
             out_specs=(vmem, vmem),
-            scratch_shapes=scratch + [square, square],
+            scratch_shapes=[pltpu.VMEM((states, width, terms * width), BF16), square, square],
             compiler_params=params(),
-            cost_estimate=apply_cost,
+            cost_estimate=cost(2 * stage_flops, 12 * states * width * width),
             name="apply_received_terms",
-        )(vector, partial, stat, bundles[hop])
+        )(vector, turned, partial, stat, headers[hop], bundles[hop])
     other = to_sibling(partial)
     stat_other = to_sibling(stat)
 
@@ -428,12 +500,12 @@
             pltpu.VMEM(whole, BF16),
             pltpu.VMEM(rotated, BF16),
             pltpu.VMEM(rotated, BF16),
-            pltpu.VMEM((terms * states * TILE, states * TILE), BF16),
+            square,
         ],
         compiler_params=params(),
-        cost_estimate=cost(apply_flops, 6 * states * width * width),
+        cost_estimate=cost(3 * stage_flops, 6 * states * width * width),
         name="apply_residual",
-    )(bond_rank, stat, stat_other, partial, other, vector, left, right, site)
+    )(bond_rank, stat, stat_other, partial, other, vector, left, packed, krons[0])
     shares = everyone(share)
 
     local = jax.ShapeDtypeStruct((rows, states, width), F32)

time: 57.8 us -> 60.7 us (1.050)
  local copies, waits for them, and re-layouts: 1.23 us -> 3.92 us
  waiting for transfers between devices: 20.9 us -> 19.7 us
  starting transfers between devices: 7.91 us -> 8.85 us
    unnamed x8 -> x12, local copies, waits for them, and re-layouts: 1.23 us -> 3.92 us
    ppermute x1, waiting for transfers between devices: 0.74 us -> 0.01 us  [shards(): received = lax.ppermute(packed_own, 'seg', shift)]
    pallas_call x3 -> x8, Pallas kernels: 15.6 us -> 16.1 us  [the longest x2 7.45 us: shards(): pl.pallas_call(functools.partial(chip_kernel, hop, chips), out_shape=tupl...]
    ppermute x2 -> x3, waiting for transfers between devices: 13.7 us -> 13.2 us  [to_next_chip(): lax.ppermute(block, 'term', [(i, (i + CORES) % members) for i in range(me...]
    ppermute x2 -> x3, starting transfers between devices: 4.04 us -> 4.44 us  [to_next_chip(): lax.ppermute(block, 'term', [(i, (i + CORES) % members) for i in range(me...]
  transfers between devices with their start and end apart: 10 -> 11, of which waited for: 6 -> 6; matrix products, arithmetic and copies ran while one was open for 0% -> 0% of each run, Pallas kernels for 15% -> 19%
where the time goes in v4:
time: 60.7 us; the launch traced here: 60.4 us
  Pallas kernels  26.3 us (43%)
  waiting for transfers between devices  19.7 us (32%)
  starting transfers between devices  8.85 us (15%)
  local copies, waits for them, and re-layouts  3.92 us (6%)
  between operations  1.6 us (3%)
    ppermute x3, waiting for transfers between devices, to_next_chip(): lax.ppermute(block, 'term', [(i, (i + CORES) % members) for i in range(me...  13.2 us
    pallas_call x1, Pallas kernels, shards(): pl.pallas_call(functools.partial(second_kernel, scale, members), out_shap...  7.94 us
    pallas_call x2, Pallas kernels, shards(): pl.pallas_call(functools.partial(chip_kernel, hop, chips), out_shape=tupl...  7.45 us
    pallas_call x1, Pallas kernels, shards(): pl.pallas_call(next_kernel, out_shape=(whole_bf if hop == hops[-1] else w...  5.1 us
    ppermute x3, starting transfers between devices, to_next_chip(): lax.ppermute(block, 'term', [(i, (i + CORES) % members) for i in range(me...  4.44 us
    unnamed x12, local copies, waits for them, and re-layouts  3.92 us
    ppermute x4, waiting for transfers between devices, to_sibling(): return lax.ppermute(block, 'term', [(i, i ^ 1) for i in range(members)])  3.74 us
    ppermute x3, waiting for transfers between devices, everyone(): lax.ppermute(block, 'term', [(i, i ^ bits) for i in range(members)])  2.79 us
  transfers between devices with their start and end apart: 11, of which 6 were waited for; matrix products, arithmetic and copies ran while one was open for 0% of the time, Pallas kernels for 19%

profile of v4, /device:TPU:0, one launch (start us, length us, event | category | flops | bytes accessed | tf_op | source)
XLA Modules:
  0.0 60.4 jit_solution(131964304465763474)
XLA Ops:
  1.3 0.0 copy-start
  1.3 1.2 %copy-done = f32[1,64,16,256]{3,2,1,0:T(8,128)S(1)} copy-done((f32[1,64,16,256]{3,2,1,0:T(8,128)S(1)}, f32[1,64,16,256]{3,2,1,0:T(8,128)}, u32[]{:S(2)}) %copy-start) | copy-done | bytes 1048600
  2.5 0.0 copy-start.3
  2.5 0.5 prepare.1
  3.0 0.5 collective-permute-start
  3.6 2.6 %collective-permute-start.1 = (bf16[16,64,256]{2,1,0:T(8,128)(2,1)S(1)}, bf16[16,64,256]{2,1,0:T(8,128)(2,1)S(1)}, u32[]{:S(2)}, u32[]{:S(2)}) collective-permute-start(bf16[16,64,256]{2,1,0:T(8,128)(2,1)S(1)} %get-tuple-element.18.refs_0_), channel_id=1, source_target_pairs={{0,2},{1,3},{2,0},{3,1},{4,6},{5,7},{6,4},{7,5},{8,10},{9,11},{10,... | collective-permute-start | bytes 1572872 | tf_op jit(solution)/shard_map/ppermute | solution.py:368
  6.2 0.0 copy-start.4
  6.2 1.0 %copy-done.4 = bf16[1,3,256,256]{3,2,1,0:T(8,128)(2,1)S(1)} copy-done((bf16[1,3,256,256]{3,2,1,0:T(8,128)(2,1)S(1)}, bf16[1,3,256,256]{3,2,1,0:T(8,128)(2,1)}, u32[]{:S(2)}) %copy-start.4) | copy-done | bytes 393240
  7.1 0.1 pack_right.1
  7.2 1.3 %collective-permute-start.3 = (bf16[3,272,128]{2,1,0:T(8,128)(2,1)S(1)}, bf16[3,272,128]{2,1,0:T(8,128)(2,1)S(1)}, u32[]{:S(2)}, u32[]{:S(2)}) collective-permute-start(bf16[3,272,128]{2,1,0:T(8,128)(2,1)S(1)} %pack_right.1), channel_id=1, source_target_pairs={{4,0},{8,4},{12,8},{16,12},{20,16},{24,20},{28,24},{5,1},{9,5},{13... | collective-permute-start | bytes 626696 | tf_op jit(solution)/shard_map/ppermute | solution.py:403
  8.5 0.0 copy-start.5
  8.5 0.7 %copy-done.5 = bf16[1,3,16,16]{3,2,1,0:T(8,128)(2,1)S(1)} copy-done((bf16[1,3,16,16]{3,2,1,0:T(8,128)(2,1)S(1)}, bf16[1,3,16,16]{3,2,1,0:T(8,128)(2,1)}, u32[]{:S(2)}) %copy-start.5) | copy-done | bytes 1560
  9.2 0.1 header.1.header_ref
  9.4 0.0 collective-permute-start.2
  9.4 0.5 spread_site.2.refs_4_.kron_ref
  9.9 9.3 %collective-permute-done.2.header_ref = bf16[3,32,128]{2,1,0:T(8,128)(2,1)S(1)} collective-permute-done((bf16[3,32,128]{2,1,0:T(8,128)(2,1)S(1)}, bf16[3,32,128]{2,1,0:T(8,128)(2,1)S(1)}, u32[]{:S(2)}, u32[]{:S(2)}) %collective-permute-start.2) | collective-permute-done | bytes 24608 | tf_op jit(solution)/shard_map/ppermute | solution.py:368
  19.2 0.5 spread_site.3.refs_4_
  19.7 0.0 collective-permute-done.3
  19.8 0.0 collective-permute-done.refs_1_
  19.8 0.0 copy-start.2
  19.8 1.0 %copy-done.2 = bf16[1,3,256,256]{3,2,1,0:T(8,128)(2,1)S(1)} copy-done((bf16[1,3,256,256]{3,2,1,0:T(8,128)(2,1)S(1)}, bf16[1,3,256,256]{3,2,1,0:T(8,128)(2,1)}, u32[]{:S(2)}) %copy-start.2) | copy-done | bytes 393240
  20.8 3.8 %apply_rows_here.1 = (f32[16,256,256]{2,1,0:T(8,128)S(1)}, bf16[3,528,128]{2,1,0:T(8,128)(2,1)S(1)}) custom-call(bf16[16,64,256]{2,1,0:T(8,128)(2,1)S(1)} %get-tuple-element.18.refs_0_, bf16[16,64,256]{2,1,0:T(8,128)(2,1)S(1)} %collective-permute-done.refs_1_, bf16[3,256,256]{2,1,0:T(8,128)(2,1)S(1)} %bitcast.7, ...), custom_call_target="tpu_custom_call" | custom-call | flops 24159192 | bytes 83886 | tf_op jit(solution)/shard_map/apply_rows_here/pallas_call | solution.py:448
  24.6 0.0 collective-permute-done.1.refs_2_.refs_0_
  24.6 0.1 collective-permute-start.4
  24.7 1.8 %collective-permute-start.5 = (bf16[3,528,128]{2,1,0:T(8,128)(2,1)S(1)}, bf16[3,528,128]{2,1,0:T(8,128)(2,1)S(1)}, u32[]{:S(2)}, u32[]{:S(2)}) collective-permute-start(bf16[3,528,128]{2,1,0:T(8,128)(2,1)S(1)} %get-tuple-element.22), channel_id=1, source_target_pairs={{0,2},{1,3},{2,0},{3,1},{4,6},{5,7},{6,4},{7,5},{8,10},{9,11},{10,... | collective-permute-start | bytes 1216520 | tf_op jit(solution)/shard_map/ppermute | solution.py:368
  26.5 0.1 collective-permute-done.4.refs_3_.refs_1_
  26.6 2.4 %rotate_received.1 = (bf16[3,16,256,256]{3,2,1,0:T(8,128)(2,1)S(1)}, bf16[16,256,256]{2,1,0:T(8,128)(2,1)S(1)}) custom-call(bf16[16,64,256]{2,1,0:T(8,128)(2,1)S(1)} %get-tuple-element.18.refs_0_, bf16[16,64,256]{2,1,0:T(8,128)(2,1)S(1)} %collective-permute-done.refs_1_, bf16[16,64,256]{2,1,0:T(8,128)(2,1)S(1)} %collective-permute-done.1.refs_2_.refs_0_, ...), custom_call_target="tpu_custom_call" | custom-call | flops 16106127 | bytes 83886 | tf_op jit(solution)/shard_map/rotate_received/pallas_call | solution.py:471
  29.0 0.0 copy-done.3
  29.0 3.6 %apply_rows_there.1.before_ref = f32[16,256,256]{2,1,0:T(8,128)S(1)} custom-call(bf16[16,64,256]{2,1,0:T(8,128)(2,1)S(1)} %collective-permute-done.1.refs_2_.refs_0_, bf16[16,64,256]{2,1,0:T(8,128)(2,1)S(1)} %collective-permute-done.4.refs_3_.refs_1_, bf16[3,256,256]{2,1,0:T(8,128)(2,1)S(1)} %bitcast.8, ...), custom_call_target="tpu_custom_call" | custom-call | flops 24159192 | bytes 83886 | tf_op jit(solution)/shard_map/apply_rows_there/pallas_call | solution.py:448
  32.6 3.9 %collective-permute-done.5.bundle_ref = bf16[3,528,128]{2,1,0:T(8,128)(2,1)S(1)} collective-permute-done((bf16[3,528,128]{2,1,0:T(8,128)(2,1)S(1)}, bf16[3,528,128]{2,1,0:T(8,128)(2,1)S(1)}, u32[]{:S(2)}, u32[]{:S(2)}) %collective-permute-start.5) | collective-permute-done | bytes 405536 | tf_op jit(solution)/shard_map/ppermute | solution.py:368
  36.5 5.1 %apply_received_terms.1 = (bf16[16,256,256]{2,1,0:T(8,128)(2,1)S(1)}, f32[8,256]{1,0:T(8,128)S(1)}) custom-call(bf16[16,256,256]{2,1,0:T(8,128)(2,1)S(1)} %get-tuple-element.25.whole_ref, bf16[3,16,256,256]{3,2,1,0:T(8,128)(2,1)S(1)} %get-tuple-element.26.rotated_ref, f32[16,256,256]{2,1,0:T(8,128)S(1)} %apply_rows_there.1.before_ref, ...), custom_call_target="tpu_custom_call" | custom-call | flops 32212254 | bytes 125829 | tf_op jit(solution)/shard_map/apply_received_terms/pallas_call | solution.py:481
  41.6 0.0 copy-start.1
  41.6 0.1 collective-permute-start.7
  41.7 0.5 collective-permute-start.6
  42.2 3.7 %collective-permute-done.6.theirs_ref = f32[8,256]{1,0:T(8,128)S(1)} collective-permute-done((f32[8,256]{1,0:T(8,128)S(1)}, f32[8,256]{1,0:T(8,128)S(1)}, u32[]{:S(2)}, u32[]{:S(2)}) %collective-permute-start.6) | collective-permute-done | bytes 8224 | tf_op jit(solution)/shard_map/ppermute | solution.py:365
  45.8 0.0 collective-permute-done.7.other_ref
  45.8 7.9 %apply_residual.1.refs_0_ = f32[8,256]{1,0:T(8,128)S(1)} custom-call(s32[1]{0:T(128)S(6)} %copy.7.rank_ref, f32[8,256]{1,0:T(8,128)S(1)} %get-tuple-element.28.mine_ref, f32[8,256]{1,0:T(8,128)S(1)} %collective-permute-done.6.theirs_ref, bf16[16,256,256]{2,1,0:T(8,128)(2,1)S(1)} %get-tuple-element.29.partial_ref, ...), custom_call_target="tpu_custom_call" | custom-call | flops 48318384 | bytes 62914 | tf_op jit(solution)/shard_map/apply_residual/pallas_call | solution.py:494
  53.8 1.6 %collective-permute-start.10 = (f32[8,256]{1,0:T(8,128)S(1)}, f32[8,256]{1,0:T(8,128)S(1)}, u32[]{:S(2)}, u32[]{:S(2)}) collective-permute-start(f32[8,256]{1,0:T(8,128)S(1)} %apply_residual.1.refs_0_), channel_id=1, source_target_pairs={{0,3},{1,2},{2,1},{3,0},{4,7},{5,6},{6,5},{7,4},{8,11},{9,10},{10,... | collective-permute-start | bytes 24584 | tf_op jit(solution)/shard_map/ppermute | solution.py:378
  55.4 0.3 collective-permute-start.9
  55.7 0.1 collective-permute-start.8
  55.8 0.0 copy-done.1
  55.8 0.5 own_rows.1
  56.2 0.7 %collective-permute-done.10.refs_3_ = f32[8,256]{1,0:T(8,128)S(1)} collective-permute-done((f32[8,256]{1,0:T(8,128)S(1)}, f32[8,256]{1,0:T(8,128)S(1)}, u32[]{:S(2)}, u32[]{:S(2)}) %collective-permute-start.10) | collective-permute-done | bytes 8224 | tf_op jit(solution)/shard_map/ppermute | solution.py:378
  56.9 2.1 %collective-permute-done.9.refs_2_ = f32[8,256]{1,0:T(8,128)S(1)} collective-permute-done((f32[8,256]{1,0:T(8,128)S(1)}, f32[8,256]{1,0:T(8,128)S(1)}, u32[]{:S(2)}, u32[]{:S(2)}) %collective-permute-start.9) | collective-permute-done | bytes 8224 | tf_op jit(solution)/shard_map/ppermute | solution.py:378
  59.0 0.0 collective-permute-done.8.refs_1_
  59.0 1.3 %finish.1 = (f32[64,16,256]{2,1,0:T(8,128)}, f32[1]{0:T(128)}) custom-call(f32[64,16,256]{2,1,0:T(8,128)S(1)} %get-tuple-element.30.vector_ref, f32[64,16,256]{2,1,0:T(8,128)S(1)} %get-tuple-element.31.residual_ref, f32[8,256]{1,0:T(8,128)S(1)} %apply_residual.1.refs_0_, f32[8,256]{1,0:T(8,128)S(1)} %collective-permute-done.8.refs_1_, ...), custom_call_target="tpu_custom_call" | custom-call | flops 7864 | bytes 31457 | tf_op jit(solution)/shard_map/finish/pallas_call | solution.py:522
  (1 shorter events, 0.0 us)
Async XLA Ops:
  1.3 1.2 %copy-start = (f32[1,64,16,256]{3,2,1,0:T(8,128)S(1)}, f32[1,64,16,256]{3,2,1,0:T(8,128)}, u32[]{:S(2)}) copy-start(f32[1,64,16,256]{3,2,1,0:T(8,128)} %param.5) | copy-start | bytes 3145732
  2.5 26.5 %copy-start.3 = (bf16[1,3,256,256]{3,2,1,0:T(8,128)(2,1)S(1)}, bf16[1,3,256,256]{3,2,1,0:T(8,128)(2,1)}, u32[]{:S(2)}) copy-start(bf16[1,3,256,256]{3,2,1,0:T(8,128)(2,1)} %param.6) | copy-start | bytes 1179652
  3.0 16.7 %collective-permute-start = (bf16[16,64,256]{2,1,0:T(8,128)(2,1)S(1)}, bf16[16,64,256]{2,1,0:T(8,128)(2,1)S(1)}, u32[]{:S(2)}, u32[]{:S(2)}) collective-permute-start(bf16[16,64,256]{2,1,0:T(8,128)(2,1)S(1)} %get-tuple-element.18.refs_0_), channel_id=1, source_target_pairs={{0,1},{1,0},{2,3},{3,2},{4,5},{5,4},{6,7},{7,6},{8,9},{9,8},{10,11... | collective-permute-start | bytes 1572872 | tf_op jit(solution)/shard_map/ppermute | solution.py:365
  3.6 21.0 %collective-permute-start.1 = (bf16[16,64,256]{2,1,0:T(8,128)(2,1)S(1)}, bf16[16,64,256]{2,1,0:T(8,128)(2,1)S(1)}, u32[]{:S(2)}, u32[]{:S(2)}) collective-permute-start(bf16[16,64,256]{2,1,0:T(8,128)(2,1)S(1)} %get-tuple-element.18.refs_0_), channel_id=1, source_target_pairs={{0,2},{1,3},{2,0},{3,1},{4,6},{5,7},{6,4},{7,5},{8,10},{9,11},{10,... | collective-permute-start | bytes 1572872 | tf_op jit(solution)/shard_map/ppermute | solution.py:368
  6.2 1.0 %copy-start.4 = (bf16[1,3,256,256]{3,2,1,0:T(8,128)(2,1)S(1)}, bf16[1,3,256,256]{3,2,1,0:T(8,128)(2,1)}, u32[]{:S(2)}) copy-start(bf16[1,3,256,256]{3,2,1,0:T(8,128)(2,1)} %param.7) | copy-start | bytes 1179652
  7.2 12.5 %collective-permute-start.3 = (bf16[3,272,128]{2,1,0:T(8,128)(2,1)S(1)}, bf16[3,272,128]{2,1,0:T(8,128)(2,1)S(1)}, u32[]{:S(2)}, u32[]{:S(2)}) collective-permute-start(bf16[3,272,128]{2,1,0:T(8,128)(2,1)S(1)} %pack_right.1), channel_id=1, source_target_pairs={{4,0},{8,4},{12,8},{16,12},{20,16},{24,20},{28,24},{5,1},{9,5},{13... | collective-permute-start | bytes 626696 | tf_op jit(solution)/shard_map/ppermute | solution.py:403
  8.5 0.7 %copy-start.5 = (bf16[1,3,16,16]{3,2,1,0:T(8,128)(2,1)S(1)}, bf16[1,3,16,16]{3,2,1,0:T(8,128)(2,1)}, u32[]{:S(2)}) copy-start(bf16[1,3,16,16]{3,2,1,0:T(8,128)(2,1)} %param.8) | copy-start | bytes 4612
  9.4 9.8 %collective-permute-start.2 = (bf16[3,32,128]{2,1,0:T(8,128)(2,1)S(1)}, bf16[3,32,128]{2,1,0:T(8,128)(2,1)S(1)}, u32[]{:S(2)}, u32[]{:S(2)}) collective-permute-start(bf16[3,32,128]{2,1,0:T(8,128)(2,1)S(1)} %header.1.header_ref), channel_id=1, source_target_pairs={{0,2},{1,3},{2,0},{3,1},{4,6},{5,7},{6,4},{7,5},{8,10},{9,11},{10,... | collective-permute-start | bytes 73736 | tf_op jit(solution)/shard_map/ppermute | solution.py:368
  19.8 1.0 %copy-start.2 = (bf16[1,3,256,256]{3,2,1,0:T(8,128)(2,1)S(1)}, bf16[1,3,256,256]{3,2,1,0:T(8,128)(2,1)}, u32[]{:S(2)}) copy-start(bf16[1,3,256,256]{3,2,1,0:T(8,128)(2,1)} %param.6) | copy-start | bytes 1179652
  24.6 2.0 %collective-permute-start.4 = (bf16[16,64,256]{2,1,0:T(8,128)(2,1)S(1)}, bf16[16,64,256]{2,1,0:T(8,128)(2,1)S(1)}, u32[]{:S(2)}, u32[]{:S(2)}) collective-permute-start(bf16[16,64,256]{2,1,0:T(8,128)(2,1)S(1)} %collective-permute-done.1.refs_2_.refs_0_), channel_id=1, source_target_pairs={{0,1},{1,0},{2,3},{3,2},{4,5},{5,4},{6,7},{7,6},{8,9},{9,8},{10,11... | collective-permute-start | bytes 1572872 | tf_op jit(solution)/shard_map/ppermute | solution.py:365
  24.7 11.8 %collective-permute-start.5 = (bf16[3,528,128]{2,1,0:T(8,128)(2,1)S(1)}, bf16[3,528,128]{2,1,0:T(8,128)(2,1)S(1)}, u32[]{:S(2)}, u32[]{:S(2)}) collective-permute-start(bf16[3,528,128]{2,1,0:T(8,128)(2,1)S(1)} %get-tuple-element.22), channel_id=1, source_target_pairs={{0,2},{1,3},{2,0},{3,1},{4,6},{5,7},{6,4},{7,5},{8,10},{9,11},{10,... | collective-permute-start | bytes 1216520 | tf_op jit(solution)/shard_map/ppermute | solution.py:368
  41.6 14.2 %copy-start.1 = (f32[1,64,16,256]{3,2,1,0:T(8,128)S(1)}, f32[1,64,16,256]{3,2,1,0:T(8,128)}, u32[]{:S(2)}) copy-start(f32[1,64,16,256]{3,2,1,0:T(8,128)} %param.5) | copy-start | bytes 3145732
  41.6 4.2 %collective-permute-start.7 = (bf16[16,256,256]{2,1,0:T(8,128)(2,1)S(1)}, bf16[16,256,256]{2,1,0:T(8,128)(2,1)S(1)}, u32[]{:S(2)}, u32[]{:S(2)}) collective-permute-start(bf16[16,256,256]{2,1,0:T(8,128)(2,1)S(1)} %get-tuple-element.29.partial_ref), channel_id=1, source_target_pairs={{0,1},{1,0},{2,3},{3,2},{4,5},{5,4},{6,7},{7,6},{8,9},{9,8},{10,11... | collective-permute-start | bytes 6291464 | tf_op jit(solution)/shard_map/ppermute | solution.py:365
  41.7 4.2 %collective-permute-start.6 = (f32[8,256]{1,0:T(8,128)S(1)}, f32[8,256]{1,0:T(8,128)S(1)}, u32[]{:S(2)}, u32[]{:S(2)}) collective-permute-start(f32[8,256]{1,0:T(8,128)S(1)} %get-tuple-element.28.mine_ref), channel_id=1, source_target_pairs={{0,1},{1,0},{2,3},{3,2},{4,5},{5,4},{6,7},{7,6},{8,9},{9,8},{10,11... | collective-permute-start | bytes 24584 | tf_op jit(solution)/shard_map/ppermute | solution.py:365
  53.8 3.1 %collective-permute-start.10 = (f32[8,256]{1,0:T(8,128)S(1)}, f32[8,256]{1,0:T(8,128)S(1)}, u32[]{:S(2)}, u32[]{:S(2)}) collective-permute-start(f32[8,256]{1,0:T(8,128)S(1)} %apply_residual.1.refs_0_), channel_id=1, source_target_pairs={{0,3},{1,2},{2,1},{3,0},{4,7},{5,6},{6,5},{7,4},{8,11},{9,10},{10,... | collective-permute-start | bytes 24584 | tf_op jit(solution)/shard_map/ppermute | solution.py:378
  55.4 3.7 %collective-permute-start.9 = (f32[8,256]{1,0:T(8,128)S(1)}, f32[8,256]{1,0:T(8,128)S(1)}, u32[]{:S(2)}, u32[]{:S(2)}) collective-permute-start(f32[8,256]{1,0:T(8,128)S(1)} %apply_residual.1.refs_0_), channel_id=1, source_target_pairs={{0,2},{1,3},{2,0},{3,1},{4,6},{5,7},{6,4},{7,5},{8,10},{9,11},{10,... | collective-permute-start | bytes 24584 | tf_op jit(solution)/shard_map/ppermute | solution.py:378
  55.7 3.3 %collective-permute-start.8 = (f32[8,256]{1,0:T(8,128)S(1)}, f32[8,256]{1,0:T(8,128)S(1)}, u32[]{:S(2)}, u32[]{:S(2)}) collective-permute-start(f32[8,256]{1,0:T(8,128)S(1)} %apply_residual.1.refs_0_), channel_id=1, source_target_pairs={{0,1},{1,0},{2,3},{3,2},{4,5},{5,4},{6,7},{7,6},{8,9},{9,8},{10,11... | collective-permute-start | bytes 24584 | tf_op jit(solution)/shard_map/ppermute | solution.py:378

commit v5 on v4

v5 whole, which is shorter than its diff:
```python
import functools

import jax
import jax.numpy as jnp
from jax import lax
from jax.experimental import pallas as pl
from jax.experimental.pallas import tpu as pltpu
from jax.sharding import PartitionSpec as P

epsilon = 1e-06
CORES = 2
TILE = 16
UNROLL = 4
GROUP = 4
VMEM_LIMIT = 20 * 1024 * 1024
F32 = jnp.float32
BF16 = jnp.bfloat16

vmem = pl.BlockSpec(memory_space=pltpu.VMEM)
smem = pl.BlockSpec(memory_space=pltpu.SMEM)
anywhere = pl.BlockSpec(memory_space=pl.ANY)
in_hbm = pl.BlockSpec(memory_space=pltpu.HBM)


def params():
    return pltpu.CompilerParams(vmem_limit_bytes=VMEM_LIMIT)


def cost(flops, moved):
    return pl.CostEstimate(flops=int(flops) // 100, bytes_accessed=int(moved) // 100, transcendentals=0)


def keep_row(rank, width):
    return (lax.broadcasted_iota(jnp.int32, (1, width), 1) < rank).astype(F32)


def prepare_kernel(
    rank_ref,
    guess_in,
    left_in,
    right_in,
    site_in,
    x_ref,
    norm_ref,
    left_packed_ref,
    right_packed_ref,
    left_ref,
    guess_ref,
    right_ref,
    site_ref,
    sems,
):
    rows, states, width = guess_ref.shape
    terms = left_ref.shape[0]
    half = width // 2
    sources = (guess_in, site_in, right_in, left_in)
    targets = (guess_ref, site_ref, right_ref, left_ref)
    copies = [pltpu.make_async_copy(sources[n], targets[n], sems.at[n]) for n in range(4)]
    for copy in copies:
        copy.start()
    copies[0].wait()
    masked = guess_ref[...] * keep_row(rank_ref[0], width)[None]
    total = jnp.sum(masked * masked)
    norm_ref[...] = jnp.full(norm_ref.shape, total, F32)
    x_ref[0:states] = jnp.swapaxes(masked, 0, 1).astype(BF16)
    copies[1].wait()
    widen = (
        lax.broadcasted_iota(jnp.int32, (states, width), 0) == lax.broadcasted_iota(jnp.int32, (states, width), 1)
    ).astype(BF16)
    norm = jnp.full((1, width), total, F32)
    parts = []
    for _ in range(3):
        parts.append(norm.astype(BF16).astype(F32))
        norm = norm - parts[-1]
    lines = lax.broadcasted_iota(jnp.int32, (TILE, width), 0)
    lines = functools.reduce(jnp.add, [jnp.where(lines == n, parts[n], 0.0) for n in range(3)]).astype(BF16)
    for k in range(terms + 1):
        slab, row = divmod(k * TILE, rows)
        sites = lines if k == terms else jnp.dot(site_ref[k], widen, preferred_element_type=F32).astype(BF16)
        x_ref[states + slab, row : row + TILE, :] = sites
    for copy, block_ref, packed_ref in zip(copies[2:], (right_ref, left_ref), (right_packed_ref, left_packed_ref)):
        copy.wait()
        for k in range(terms):
            diagonal = pack_symmetric(block_ref, k, packed_ref)
            packed_ref[k, width : width + TILE, :] = jnp.broadcast_to(diagonal, (TILE, half)).astype(BF16)


def triangle(half):
    row = lax.broadcasted_iota(jnp.int32, (half, half), 0)
    col = lax.broadcasted_iota(jnp.int32, (half, half), 1)
    return row, col


def pack_symmetric(block_ref, k, out_ref):
    width = block_ref.shape[1]
    half = width // 2
    row, col = triangle(half)
    upper = block_ref[k, 0:half, 0:half].astype(F32)
    lower = block_ref[k, half:width, half:width].astype(F32)
    out_ref[k, 0:half, :] = block_ref[k, 0:half, half:width]
    out_ref[k, half:width, :] = jnp.where(row <= col, upper, lower).astype(BF16)
    return jnp.sum(jnp.where(row == col, lower, 0.0), axis=0, keepdims=True)


def unpack_symmetric(packed_ref, full_ref):
    terms, width, _ = full_ref.shape
    half = width // 2
    row, col = triangle(half)
    for k in range(terms):
        corner = packed_ref[k, 0:half, :]
        mixed = packed_ref[k, half:width, :].astype(F32)
        diagonal = packed_ref[k, width : width + TILE, :].astype(F32)[0:1]
        turned = mixed.T
        full_ref[k, 0:half, 0:half] = jnp.where(row <= col, mixed, turned).astype(BF16)
        full_ref[k, 0:half, half:width] = corner
        full_ref[k, half:width, 0:half] = corner.astype(F32).T.astype(BF16)
        full_ref[k, half:width, half:width] = jnp.where(
            row > col, mixed, jnp.where(row == col, diagonal, turned)
        ).astype(BF16)


def spread_kernel(x_ref, kron_ref, norm_ref):
    rows, lanes = x_ref.shape[1:]
    size = kron_ref.shape[1]
    terms = kron_ref.shape[0] // size
    states = size // TILE
    row_state = lax.broadcasted_iota(jnp.int32, (size, states), 0) // TILE
    pick = (row_state == lax.broadcasted_iota(jnp.int32, (size, states), 1)).astype(BF16)
    col_state = lax.broadcasted_iota(jnp.int32, (lanes, size), 1) // TILE
    pick_t = (col_state == lax.broadcasted_iota(jnp.int32, (lanes, size), 0)).astype(BF16)
    same = (
        lax.broadcasted_iota(jnp.int32, (size, size), 0) % TILE
        == lax.broadcasted_iota(jnp.int32, (size, size), 1) % TILE
    )
    for k in range(terms + 1):
        slab, row = divmod(k * TILE, rows)
        sites = x_ref[states + slab, row : row + TILE, :]
        if k == terms:
            lines = sites.astype(F32)
            norm_ref[...] = jnp.broadcast_to(lines[0:1] + lines[1:2] + lines[2:3], norm_ref.shape)
            break
        tall = jnp.dot(pick, sites, preferred_element_type=F32).astype(BF16)
        full = jnp.dot(tall, pick_t, preferred_element_type=F32)
        kron_ref[k * size : (k + 1) * size, :] = jnp.where(same, full, 0.0).astype(BF16)


def mix_sites(source_ref, kron_ref, rotated_ref, base, unroll):
    terms, states, _, width = rotated_ref.shape
    rows = source_ref.shape[1]

    def step(i, carry):
        at = pl.multiple_of(i * TILE, TILE)
        to = pl.multiple_of(base + i * TILE, TILE)
        stack = source_ref[0:states, pl.ds(at, TILE), :].reshape(states * TILE, width)
        turned = jnp.dot(kron_ref[...], stack, preferred_element_type=F32).astype(BF16)
        rotated_ref[:, :, pl.ds(to, TILE), :] = turned.reshape(terms, states, TILE, width)
        return carry

    lax.fori_loop(0, rows // TILE, step, 0, unroll=min(unroll, rows // TILE))


def fold(values, width):
    return jnp.sum(values.reshape(values.size // (8 * width), 8, width), axis=0)


def summed(values):
    while len(values) > 1:
        values = [values[n] + values[n + 1] for n in range(0, len(values), 2)]
    return values[0]


def place(hop, chips):
    me = lax.axis_index("term")
    chip = (me // CORES - hop + chips) % chips
    return chip, me % CORES


def chip_kernel(hop, chips, own_ref, sib_ref, left_ref, packed_ref, kron_ref, *refs):
    before_ref = None if hop == 0 else refs[0]
    out_ref, rotated_ref, turned_ref, columns_ref, right_ref = refs[-5:]
    terms, states, chip_rows, width = rotated_ref.shape
    rows = own_ref.shape[1]
    chip, core = place(hop, chips)
    mix_sites(own_ref, kron_ref, rotated_ref, core * rows, UNROLL)
    mix_sites(sib_ref, kron_ref, rotated_ref, (1 - core) * rows, UNROLL)
    at = pl.multiple_of(chip * chip_rows, TILE)
    unpack_symmetric(packed_ref, right_ref)
    columns = jnp.concatenate([left_ref[k, pl.ds(at, chip_rows), :] for k in range(terms)], axis=0)
    columns_ref[...] = columns.astype(F32).T.astype(BF16)
    for k in range(terms):
        for n in range(0, states, 8):
            source = rotated_ref[k, n : n + 8].reshape(8 * chip_rows, width)
            turned = jnp.dot(source, right_ref[k], preferred_element_type=F32).astype(BF16)
            turned_ref[n : n + 8, k * chip_rows : (k + 1) * chip_rows, :] = turned.reshape(8, chip_rows, width)

    def lefts(p, carry):
        image = jnp.dot(columns_ref[...], turned_ref[p], preferred_element_type=F32)
        if before_ref is not None:
            image = before_ref[p] + image
        out_ref[p] = image
        return carry

    lax.fori_loop(0, states, lefts, 0, unroll=UNROLL)


def rotate_kernel(hops, chips, *refs):
    pieces = refs[: CORES * len(hops)]
    kron_ref = refs[len(pieces)]
    rotated_ref, whole_ref, sems = refs[-3:]
    rows = pieces[0].shape[1]
    copies = []
    for n, piece in enumerate(pieces):
        chip, core = place(hops[n // 2], chips)
        at = (chip * CORES + (core if n % 2 == 0 else 1 - core)) * rows
        copies.append(
            pltpu.make_async_copy(
                piece.at[0 : whole_ref.shape[0]],
                whole_ref.at[:, pl.ds(pl.multiple_of(at, TILE), rows), :],
                sems.at[n],
            )
        )
        copies[-1].start()
    for n, piece in enumerate(pieces):
        chip, core = place(hops[n // 2], chips)
        at = (chip * CORES + (core if n % 2 == 0 else 1 - core)) * rows
        mix_sites(piece, kron_ref, rotated_ref, at, UNROLL)
    for copy in copies:
        copy.wait()


def lefts_kernel(rotated_ref, packed_ref, mixed_ref, left_ref):
    terms, states, width, _ = rotated_ref.shape
    unpack_symmetric(packed_ref, left_ref)

    def lefts(p, carry):
        for k in range(terms):
            mixed = jnp.dot(left_ref[k], rotated_ref[k, p], preferred_element_type=F32)
            mixed_ref[p, :, k * width : (k + 1) * width] = mixed.astype(BF16)
        return carry

    lax.fori_loop(0, states, lefts, 0, unroll=UNROLL)


def rights_kernel(
    mixed_ref, packed_ref, whole_ref, before_ref, stat_before_ref, norm_ref, partial_ref, stat_ref, right_ref
):
    states, width, _ = whole_ref.shape
    terms = right_ref.shape[0]
    unpack_symmetric(packed_ref, right_ref)

    def rights(n, total):
        at = n * GROUP
        rows = mixed_ref[pl.ds(at, GROUP)].reshape(GROUP * width, terms * width)
        stacked = right_ref[...].reshape(terms * width, width)
        image = jnp.dot(rows, stacked, preferred_element_type=F32).reshape(GROUP, width, width)
        part = (before_ref[pl.ds(at, GROUP)].astype(F32) + image).astype(partial_ref.dtype)
        partial_ref[pl.ds(at, GROUP)] = part
        held = whole_ref[pl.ds(at, GROUP)].astype(F32)
        return total + fold(held * part.astype(F32), width)

    total = lax.fori_loop(0, states // GROUP, rights, jnp.zeros((8, width), F32))
    stat_ref[0:1, :] = jnp.full((1, width), jnp.sum(total), F32)
    stat_ref[1:2, :] = stat_before_ref[1:2, :] + norm_ref[1:2, :]
    stat_ref[2:8, :] = jnp.zeros((6, width), F32)


def scales(rank_ref, mine_ref, theirs_ref, scale, width):
    inverse = lax.rsqrt((mine_ref[1:2, :] + theirs_ref[1:2, :]) * scale + epsilon)
    rayleigh = (mine_ref[0:1, :] + theirs_ref[0:1, :]) * (inverse * inverse * scale)
    return inverse, rayleigh, keep_row(rank_ref[0], width) * inverse


def second_kernel(
    scale,
    members,
    rank_ref,
    mine_ref,
    theirs_ref,
    partial_ref,
    other_ref,
    whole_ref,
    left_ref,
    packed_ref,
    kron_ref,
    out_ref,
    res_ref,
    rotated_ref,
    mixed_ref,
    right_ref,
):
    terms, states, width, _ = rotated_ref.shape
    unpack_symmetric(packed_ref, right_ref)
    inverse, rayleigh, row_scale = scales(rank_ref, mine_ref, theirs_ref, scale, width)
    back = rayleigh * inverse

    def lefts(p, total):
        sigma = (partial_ref[p].astype(F32) + other_ref[p].astype(F32)) * row_scale
        residual = sigma - back * whole_ref[p].astype(F32)
        rounded = residual.astype(BF16)
        res_ref[p] = rounded
        mixed = jnp.dot(
            left_ref[...].reshape(terms * width, width), rounded, preferred_element_type=F32
        ).astype(BF16)
        for k in range(terms):
            mixed_ref[k, p] = mixed[k * width : (k + 1) * width]
        return total + fold(residual * residual, width)

    square = lax.fori_loop(0, states, lefts, jnp.zeros((8, width), F32), unroll=UNROLL)
    mix_sites(res_ref, kron_ref, rotated_ref, 0, 2 * UNROLL)

    def rights(n, total):
        at = n * GROUP
        for k in range(terms):
            turned = rotated_ref[k, pl.ds(at, GROUP)].reshape(GROUP * width, width)
            image = jnp.dot(turned, right_ref[k], preferred_element_type=F32)
            held = mixed_ref[k, pl.ds(at, GROUP)].reshape(GROUP * width, width).astype(F32)
            total = total + fold(held * image, width)
        return total

    cross = lax.fori_loop(0, states // GROUP, rights, jnp.zeros((8, width), F32))
    share = 1.0 / members
    out_ref[0:1, :] = rayleigh * share
    out_ref[1:2, :] = jnp.full((1, width), jnp.sum(square) * (scale * share), F32)
    out_ref[2:3, :] = jnp.full((1, width), jnp.sum(cross) * scale, F32)
    out_ref[3:8, :] = jnp.zeros((5, width), F32)


def own_rows_kernel(
    scale, rank_ref, guess_ref, mine_ref, theirs_ref, partial_ref, other_ref, vector_ref, residual_ref
):
    rows, states, width = guess_ref.shape
    inverse, rayleigh, row_scale = scales(rank_ref, mine_ref, theirs_ref, scale, width)
    own = pl.ds(pl.multiple_of(lax.axis_index("term") * rows, TILE), rows)
    sigma = (partial_ref[:, own, :].astype(F32) + other_ref[:, own, :].astype(F32)) * row_scale[None]
    vector = guess_ref[...] * row_scale[None]
    vector_ref[...] = vector
    residual_ref[...] = jnp.swapaxes(sigma, 0, 1) - rayleigh[None] * vector


def finish_kernel(vector_ref, residual_ref, *refs):
    shares = refs[:-2]
    ritz_ref, energy_ref = refs[-2:]
    stat = summed([share[...] for share in shares])
    rayleigh = stat[0:1, :]
    res_sq = stat[1:2, :]
    res_var = res_sq + epsilon
    curvature = stat[2:3, :] / res_var
    res_scale = jnp.sqrt(res_var)
    coupling = res_sq / res_scale
    half_gap = 0.5 * (rayleigh - curvature)
    energy = 0.5 * (rayleigh + curvature) - jnp.sqrt(half_gap * half_gap + coupling * coupling)
    coeff_new = energy - rayleigh
    coeff_norm = jnp.sqrt(coupling * coupling + coeff_new * coeff_new + epsilon)
    old = coupling / coeff_norm
    new = coeff_new / (coeff_norm * res_scale)
    ritz_ref[...] = old[None] * vector_ref[...] + new[None] * residual_ref[...]
    energy_ref[0] = energy[0, 0]


def shards(wave_guess, left_env, right_env, site_ops, bond_rank):
    guess = wave_guess[0]
    left = left_env[0]
    site = site_ops[0]
    rows, states, width = guess.shape
    terms = left.shape[0]
    members = lax.axis_size("term")
    chips = members // CORES
    segments = lax.axis_size("seg")
    scale = 1.0 / float(rows * members * states * width)
    hops = tuple(range(chips))

    def to_sibling(block):
        return lax.ppermute(block, "term", [(i, i ^ 1) for i in range(members)])

    def to_next_chip(block):
        return lax.ppermute(block, "term", [(i, (i + CORES) % members) for i in range(members)])

    def around(block):
        found = [block]
        for _ in range(chips - 1):
            found.append(to_next_chip(found[-1]))
        return found

    def everyone(block):
        others = [
            lax.ppermute(block, "term", [(i, i ^ bits) for i in range(members)]) for bits in range(1, members)
        ]
        return [block] + others

    tile = jax.ShapeDtypeStruct((8, width), F32)
    half = width // 2
    packed_shape = jax.ShapeDtypeStruct((terms, width + TILE, half), BF16)
    slabs = -(-(terms + 1) * TILE // rows)
    x_own, norm_part, left_packed, right_packed, left = pl.pallas_call(
        prepare_kernel,
        out_shape=(
            jax.ShapeDtypeStruct((states + slabs, rows, width), BF16),
            tile,
            packed_shape,
            packed_shape,
            jax.ShapeDtypeStruct(left.shape, BF16),
        ),
        in_specs=[smem] + [in_hbm] * 4,
        out_specs=(vmem,) * 5,
        scratch_shapes=[
            pltpu.VMEM(guess.shape, F32),
            pltpu.VMEM(left.shape, BF16),
            pltpu.VMEM(site.shape, BF16),
            pltpu.SemaphoreType.DMA((4,)),
        ],
        compiler_params=params(),
        cost_estimate=cost(4 * guess.size, 6 * guess.size),
        name="prepare",
    )(bond_rank, *[pltpu.with_memory_space_constraint(a, pltpu.HBM) for a in (guess, left, right_env[0], site)])

    x_hops = around(x_own)
    pieces = [x_own, to_sibling(x_own)]
    lefts = around(left_packed)
    shift = [(i + 1, i) for i in range(segments - 1)]
    received = lax.ppermute(right_packed, "seg", shift)
    packed = jnp.where(lax.axis_index("seg") == segments - 1, right_packed, received)
    rights = around(packed)

    size = states * TILE

    def spread(block):
        return pl.pallas_call(
            spread_kernel,
            out_shape=(jax.ShapeDtypeStruct((terms * size, size), BF16), tile),
            in_specs=[vmem],
            out_specs=(vmem, vmem),
            compiler_params=params(),
            cost_estimate=cost(2 * terms * size * size * width, 2 * terms * size * size),
            name="spread_site",
        )(block)

    kron_own, _ = spread(x_own)

    whole = (states, width, width)
    whole_bf = jax.ShapeDtypeStruct(whole, BF16)
    whole_f32 = jax.ShapeDtypeStruct(whole, F32)
    rotated = (terms, states, width, width)
    rotated_bf = jax.ShapeDtypeStruct(rotated, BF16)
    square = pltpu.VMEM((terms, width, width), BF16)
    chip_rows = CORES * rows
    stage_flops = 2 * terms * states * width * width * width

    def chip_part(hop, before):
        return pl.pallas_call(
            functools.partial(chip_kernel, hop, chips),
            out_shape=whole_f32,
            in_specs=[vmem] * (5 if hop == 0 else 6),
            out_specs=vmem,
            scratch_shapes=[
                pltpu.VMEM((terms, states, chip_rows, width), BF16),
                pltpu.VMEM((states, terms * chip_rows, width), BF16),
                pltpu.VMEM((width, terms * chip_rows), BF16),
                square,
            ],
            compiler_params=params(),
            cost_estimate=cost(3 * stage_flops * chip_rows / width, 8 * states * width * width),
            name="apply_rows_here" if hop == 0 else "apply_rows_there",
        )(*pieces[2 * hop : 2 * hop + 2], left, packed, kron_own, *before)

    def rotate(part, kron, before):
        inputs = pieces[CORES * part[0] : CORES * (part[-1] + 1)]
        return pl.pallas_call(
            functools.partial(rotate_kernel, part, chips),
            out_shape=(rotated_bf, whole_bf),
            in_specs=[vmem] * (len(inputs) + 1) + [anywhere] * len(before),
            out_specs=(vmem, vmem),
            scratch_shapes=[pltpu.SemaphoreType.DMA((len(inputs),))],
            input_output_aliases={len(inputs) + 1 + n: n for n in range(len(before))},
            compiler_params=params(),
            cost_estimate=cost(stage_flops / 2, 8 * states * width * width),
            name="rotate_here" if part[0] == 0 else "rotate_there",
        )(*inputs, kron, *before)

    partial = chip_part(0, ())
    crossed, partial = lax.optimization_barrier((x_hops[1:], partial))
    for block in crossed:
        pieces += [block, to_sibling(block)]
    kron, norm_far = spread(crossed[0])
    turned_here = rotate(hops[:1], kron, ())
    for hop in hops[1:]:
        partial = chip_part(hop, (partial,))
    stat = norm_part
    for hop in hops[1:]:
        if hop > 1:
            block, partial = lax.optimization_barrier((crossed[hop - 1], partial))
            kron, norm_far = spread(block)
            turned_here = rotate(hops[:1], kron, ())
        turned, vector = rotate(hops[1:], kron, turned_here)
        left_far, partial = lax.optimization_barrier((lefts[hop], partial))
        mixed = pl.pallas_call(
            lefts_kernel,
            out_shape=jax.ShapeDtypeStruct((states, width, terms * width), BF16),
            in_specs=[vmem] * 2,
            out_specs=vmem,
            scratch_shapes=[square],
            compiler_params=params(),
            cost_estimate=cost(stage_flops, 12 * states * width * width),
            name="received_lefts",
        )(turned, left_far)
        partial, stat = pl.pallas_call(
            rights_kernel,
            out_shape=(whole_bf if hop == hops[-1] else whole_f32, tile),
            in_specs=[vmem] * 6,
            out_specs=(vmem, vmem),
            scratch_shapes=[square],
            compiler_params=params(),
            cost_estimate=cost(stage_flops, 12 * states * width * width),
            name="received_rights",
        )(mixed, rights[hop], vector, partial, stat, norm_far)
    other = to_sibling(partial)
    stat_other = to_sibling(stat)

    share = pl.pallas_call(
        functools.partial(second_kernel, scale, members),
        out_shape=tile,
        in_specs=[smem] + [vmem] * 8,
        out_specs=vmem,
        scratch_shapes=[
            pltpu.VMEM(whole, BF16),
            pltpu.VMEM(rotated, BF16),
            pltpu.VMEM(rotated, BF16),
            square,
        ],
        compiler_params=params(),
        cost_estimate=cost(3 * stage_flops, 6 * states * width * width),
        name="apply_residual",
    )(bond_rank, stat, stat_other, partial, other, vector, left, packed, kron_own)
    shares = everyone(share)

    local = jax.ShapeDtypeStruct((rows, states, width), F32)
    vector_own, residual_own = pl.pallas_call(
        functools.partial(own_rows_kernel, scale),
        out_shape=(local, local),
        in_specs=[smem] + [vmem] * 5,
        out_specs=(vmem, vmem),
        compiler_params=params(),
        cost_estimate=cost(8 * guess.size, 16 * guess.size),
        name="own_rows",
    )(bond_rank, guess, stat, stat_other, partial, other)

    ritz, energy = pl.pallas_call(
        finish_kernel,
        out_shape=(local, jax.ShapeDtypeStruct((1,), F32)),
        in_specs=[vmem] * (2 + members),
        out_specs=(vmem, smem),
        compiler_params=params(),
        cost_estimate=cost(3 * guess.size, 12 * guess.size),
        name="finish",
    )(vector_own, residual_own, *shares)
    return (ritz[None], energy)


def solution(mesh):
    in_specs = (
        P("seg", "term", None, None),
        P("seg", "term", None, None),
        P("seg", "term", None, None),
        P("seg", "term", None, None),
        P("seg"),
    )
    out_specs = (P("seg", "term", None, None), P("seg"))
    return jax.shard_map(shards, mesh=mesh, in_specs=in_specs, out_specs=out_specs, check_vma=False)
```

time: 60.7 us -> 53.7 us (0.88)
  waiting for transfers between devices: 19.7 us -> 14.4 us
  local copies, waits for them, and re-layouts: 3.92 us -> 0.01 us
  Pallas kernels: 26.3 us -> 28.4 us
    ppermute x3, waiting for transfers between devices: 13.2 us -> 1.04 us  [to_next_chip(): lax.ppermute(block, 'term', [(i, (i + CORES) % members) for i in range(me...]
    ppermute x1, waiting for transfers between devices: 0.01 us -> 6.77 us  [shards(): received = lax.ppermute(right_packed, 'seg', shift)]
    unnamed x12 -> x2, local copies, waits for them, and re-layouts: 3.92 us -> 0.01 us
    pallas_call x9, Pallas kernels: 16.7 us -> 18.7 us  [the longest x2 7.44 us: chip_part(): pl.pallas_call(functools.partial(chip_kernel, hop, chips), out_shape=whol...]
  transfers between devices with their start and end apart: 11 -> 11, of which waited for: 6 -> 7; matrix products, arithmetic and copies ran while one was open for 0% -> 0% of each run, Pallas kernels for 19% -> 27%
where the time goes in v5:
time: 53.7 us; the launch traced here: 53.5 us
  Pallas kernels  28.4 us (53%)
  waiting for transfers between devices  14.4 us (27%)
  starting transfers between devices  9.19 us (17%)
  between operations  1.57 us (3%)
    pallas_call x1, Pallas kernels, shards(): pl.pallas_call(functools.partial(second_kernel, scale, members), out_shap...  7.95 us
    pallas_call x2, Pallas kernels, chip_part(): pl.pallas_call(functools.partial(chip_kernel, hop, chips), out_shape=whol...  7.44 us
    ppermute x1, waiting for transfers between devices, shards(): received = lax.ppermute(right_packed, 'seg', shift)  6.77 us
    ppermute x3, starting transfers between devices, to_next_chip(): lax.ppermute(block, 'term', [(i, (i + CORES) % members) for i in range(me...  4.62 us
    ppermute x4, waiting for transfers between devices, to_sibling(): return lax.ppermute(block, 'term', [(i, i ^ 1) for i in range(members)])  3.67 us
    ppermute x3, waiting for transfers between devices, everyone(): lax.ppermute(block, 'term', [(i, i ^ bits) for i in range(members)])  2.88 us
    pallas_call x1, Pallas kernels, shards(): pl.pallas_call(rights_kernel, out_shape=(whole_bf if hop == hops[-1] else...  2.62 us
    pallas_call x2, Pallas kernels, rotate(): pl.pallas_call(functools.partial(rotate_kernel, part, chips), out_shape=(...  2.57 us
  transfers between devices with their start and end apart: 11, of which 7 were waited for; matrix products, arithmetic and copies ran while one was open for 0% of the time, Pallas kernels for 27%

profile of v5, /device:TPU:0, one launch (start us, length us, event | category | flops | bytes accessed | tf_op | source)
XLA Modules:
  0.0 53.5 jit_solution(9170266241924672300)
XLA Ops:
  1.3 2.1 %prepare.1 = (bf16[17,64,256]{2,1,0:T(8,128)(2,1)S(1)}, f32[8,256]{1,0:T(8,128)S(1)}, bf16[3,272,128]{2,1,0:T(8,128)(2,1)S(1)}, bf16[3,272,128]{2,1,0:T(8,128)(2,1)S(1)}, bf16[3,256,256]{2,1,0:T(8,128)(2,1)S(1)}) custom-call(s32[1]{0:T(128)S(6)} %copy.11.rank_ref, f32[64,16,256]{2,1,0:T(8,128)} %bitcast.5, bf16[3,256,256]{2,1,0:T(8,128)(2,1)} %bitcast.7, ...), custom_call_target="tpu_custom_call" | custom-call | flops 10485 | bytes 15728 | tf_op jit(solution)/shard_map/prepare/pallas_call | solution.py:394
  3.3 0.5 collective-permute-start.1
  3.9 2.6 %collective-permute-start = (bf16[17,64,256]{2,1,0:T(8,128)(2,1)S(1)}, bf16[17,64,256]{2,1,0:T(8,128)(2,1)S(1)}, u32[]{:S(2)}, u32[]{:S(2)}) collective-permute-start(bf16[17,64,256]{2,1,0:T(8,128)(2,1)S(1)} %get-tuple-element.24.x_ref.own_ref.refs_0_), channel_id=1, source_target_pairs={{0,2},{1,3},{2,0},{3,1},{4,6},{5,7},{6,4},{7,5},{8,10},{9,11},{10,... | collective-permute-start | bytes 1671176 | tf_op jit(solution)/shard_map/ppermute | solution.py:376
  6.4 1.3 %collective-permute-start.2 = (bf16[3,272,128]{2,1,0:T(8,128)(2,1)S(1)}, bf16[3,272,128]{2,1,0:T(8,128)(2,1)S(1)}, u32[]{:S(2)}, u32[]{:S(2)}) collective-permute-start(bf16[3,272,128]{2,1,0:T(8,128)(2,1)S(1)} %get-tuple-element.26), channel_id=1, source_target_pairs={{4,0},{8,4},{12,8},{16,12},{20,16},{24,20},{28,24},{5,1},{9,5},{13... | collective-permute-start | bytes 626696 | tf_op jit(solution)/shard_map/ppermute | solution.py:420
  7.7 1.1 %spread_site.2 = (bf16[768,256]{1,0:T(8,128)(2,1)S(1)}, f32[8,256]{1,0:T(8,128)}) custom-call(bf16[17,64,256]{2,1,0:T(8,128)(2,1)S(1)} %get-tuple-element.24.x_ref.own_ref.refs_0_), custom_call_target="tpu_custom_call" | custom-call | flops 1006632 | bytes 3932 | tf_op jit(solution)/shard_map/spread_site/pallas_call | solution.py:427
  8.8 6.8 %collective-permute-done.2 = bf16[3,272,128]{2,1,0:T(8,128)(2,1)S(1)} collective-permute-done((bf16[3,272,128]{2,1,0:T(8,128)(2,1)S(1)}, bf16[3,272,128]{2,1,0:T(8,128)(2,1)S(1)}, u32[]{:S(2)}, u32[]{:S(2)}) %collective-permute-start.2) | collective-permute-done | bytes 208928 | tf_op jit(solution)/shard_map/ppermute | solution.py:420
  15.6 0.0 collective-permute-done.1.sib_ref.refs_1_
  15.6 3.8 %apply_rows_here.1.refs_0_ = f32[16,256,256]{2,1,0:T(8,128)S(1)} custom-call(bf16[17,64,256]{2,1,0:T(8,128)(2,1)S(1)} %get-tuple-element.24.x_ref.own_ref.refs_0_, bf16[17,64,256]{2,1,0:T(8,128)(2,1)S(1)} %collective-permute-done.1.sib_ref.refs_1_, bf16[3,256,256]{2,1,0:T(8,128)(2,1)S(1)} %get-tuple-element.25.left_ref, ...), custom_call_target="tpu_custom_call" | custom-call | flops 24159192 | bytes 83886 | tf_op jit(solution)/shard_map/apply_rows_here/pallas_call | solution.py:449
  19.4 0.3 collective-permute-done.x_ref.refs_0_.own_ref
  19.7 0.0 collective-permute-start.3
  19.7 1.8 %collective-permute-start.4 = (bf16[3,272,128]{2,1,0:T(8,128)(2,1)S(1)}, bf16[3,272,128]{2,1,0:T(8,128)(2,1)S(1)}, u32[]{:S(2)}, u32[]{:S(2)}) collective-permute-start(bf16[3,272,128]{2,1,0:T(8,128)(2,1)S(1)} %get-tuple-element.33), channel_id=1, source_target_pairs={{0,2},{1,3},{2,0},{3,1},{4,6},{5,7},{6,4},{7,5},{8,10},{9,11},{10,... | collective-permute-start | bytes 626696 | tf_op jit(solution)/shard_map/ppermute | solution.py:376
  21.4 0.3 collective-permute-start.5
  21.7 0.5 spread_site.3
  22.2 1.3 %rotate_here.1 = (bf16[3,16,256,256]{3,2,1,0:T(8,128)(2,1)S(1)}, bf16[16,256,256]{2,1,0:T(8,128)(2,1)S(1)}) custom-call(bf16[17,64,256]{2,1,0:T(8,128)(2,1)S(1)} %get-tuple-element.24.x_ref.own_ref.refs_0_, bf16[17,64,256]{2,1,0:T(8,128)(2,1)S(1)} %collective-permute-done.1.sib_ref.refs_1_, bf16[768,256]{1,0:T(8,128)(2,1)S(1)} %get-tuple-element.29.refs_2_), custom_call_target="tpu_custom_call" | custom-call | flops 8053063 | bytes 83886 | tf_op jit(solution)/shard_map/rotate_here/pallas_call | solution.py:467
  23.5 0.0 collective-permute-done.3.refs_1_.sib_ref
  23.5 3.6 %apply_rows_there.1.before_ref = f32[16,256,256]{2,1,0:T(8,128)S(1)} custom-call(bf16[17,64,256]{2,1,0:T(8,128)(2,1)S(1)} %collective-permute-done.x_ref.refs_0_.own_ref, bf16[17,64,256]{2,1,0:T(8,128)(2,1)S(1)} %collective-permute-done.3.refs_1_.sib_ref, bf16[3,256,256]{2,1,0:T(8,128)(2,1)S(1)} %get-tuple-element.25.left_ref, ...), custom_call_target="tpu_custom_call" | custom-call | flops 24159192 | bytes 83886 | tf_op jit(solution)/shard_map/apply_rows_there/pallas_call | solution.py:449
  27.2 0.4 collective-permute-done.4.packed_ref
  27.6 1.3 %rotate_there.1 = (bf16[3,16,256,256]{3,2,1,0:T(8,128)(2,1)S(1)}, bf16[16,256,256]{2,1,0:T(8,128)(2,1)S(1)}) custom-call(bf16[17,64,256]{2,1,0:T(8,128)(2,1)S(1)} %collective-permute-done.x_ref.refs_0_.own_ref, bf16[17,64,256]{2,1,0:T(8,128)(2,1)S(1)} %collective-permute-done.3.refs_1_.sib_ref, ...), custom_call_target="tpu_custom_call", output_to_operand_aliasing={{0}: (3, {}), {1}: (4, {})} | custom-call | flops 8053063 | bytes 83886 | tf_op jit(solution)/shard_map/rotate_there/pallas_call | solution.py:467
  28.9 2.5 %received_lefts.1.mixed_ref = bf16[16,256,768]{2,1,0:T(8,128)(2,1)S(1)} custom-call(bf16[3,16,256,256]{3,2,1,0:T(8,128)(2,1)S(1)} %get-tuple-element.32.rotated_ref, bf16[3,272,128]{2,1,0:T(8,128)(2,1)S(1)} %collective-permute-done.4.packed_ref), custom_call_target="tpu_custom_call" | custom-call | flops 16106127 | bytes 125829 | tf_op jit(solution)/shard_map/received_lefts/pallas_call | solution.py:495
  31.4 0.3 collective-permute-done.5.packed_ref
  31.7 2.6 %received_rights.1 = (bf16[16,256,256]{2,1,0:T(8,128)(2,1)S(1)}, f32[8,256]{1,0:T(8,128)S(1)}) custom-call(bf16[16,256,768]{2,1,0:T(8,128)(2,1)S(1)} %received_lefts.1.mixed_ref, bf16[3,272,128]{2,1,0:T(8,128)(2,1)S(1)} %collective-permute-done.5.packed_ref, bf16[16,256,256]{2,1,0:T(8,128)(2,1)S(1)} %get-tuple-element.36.whole_ref, ...), custom_call_target="tpu_custom_call" | custom-call | flops 16106127 | bytes 125829 | tf_op jit(solution)/shard_map/received_rights/pallas_call | solution.py:505
  34.4 0.0 copy-start
  34.4 0.1 collective-permute-start.7
  34.5 0.5 collective-permute-start.6
  35.0 3.7 %collective-permute-done.6.theirs_ref = f32[8,256]{1,0:T(8,128)S(1)} collective-permute-done((f32[8,256]{1,0:T(8,128)S(1)}, f32[8,256]{1,0:T(8,128)S(1)}, u32[]{:S(2)}, u32[]{:S(2)}) %collective-permute-start.6) | collective-permute-done | bytes 8224 | tf_op jit(solution)/shard_map/ppermute | solution.py:373
  38.6 0.0 collective-permute-done.7.other_ref
  38.6 7.9 %apply_residual.1.refs_0_ = f32[8,256]{1,0:T(8,128)S(1)} custom-call(s32[1]{0:T(128)S(6)} %copy.11.rank_ref, f32[8,256]{1,0:T(8,128)S(1)} %get-tuple-element.40.mine_ref, f32[8,256]{1,0:T(8,128)S(1)} %collective-permute-done.6.theirs_ref, bf16[16,256,256]{2,1,0:T(8,128)(2,1)S(1)} %get-tuple-element.41.partial_ref, ...), custom_call_target="tpu_custom_call" | custom-call | flops 48318384 | bytes 62914 | tf_op jit(solution)/shard_map/apply_residual/pallas_call | solution.py:518
  46.6 1.5 %collective-permute-start.10 = (f32[8,256]{1,0:T(8,128)S(1)}, f32[8,256]{1,0:T(8,128)S(1)}, u32[]{:S(2)}, u32[]{:S(2)}) collective-permute-start(f32[8,256]{1,0:T(8,128)S(1)} %apply_residual.1.refs_0_), channel_id=1, source_target_pairs={{0,3},{1,2},{2,1},{3,0},{4,7},{5,6},{6,5},{7,4},{8,11},{9,10},{10,... | collective-permute-start | bytes 24584 | tf_op jit(solution)/shard_map/ppermute | solution.py:386
  48.1 0.4 collective-permute-start.8
  48.5 0.3 collective-permute-start.9
  48.8 0.0 copy-done
  48.8 0.5 own_rows.1
  49.2 0.5 collective-permute-done.10.refs_3_
  49.7 0.0 collective-permute-done.8.refs_1_
  49.7 2.4 %collective-permute-done.9.refs_2_ = f32[8,256]{1,0:T(8,128)S(1)} collective-permute-done((f32[8,256]{1,0:T(8,128)S(1)}, f32[8,256]{1,0:T(8,128)S(1)}, u32[]{:S(2)}, u32[]{:S(2)}) %collective-permute-start.9) | collective-permute-done | bytes 8224 | tf_op jit(solution)/shard_map/ppermute | solution.py:386
  52.1 1.3 %finish.1 = (f32[64,16,256]{2,1,0:T(8,128)}, f32[1]{0:T(128)}) custom-call(f32[64,16,256]{2,1,0:T(8,128)S(1)} %get-tuple-element.42.vector_ref, f32[64,16,256]{2,1,0:T(8,128)S(1)} %get-tuple-element.43.residual_ref, f32[8,256]{1,0:T(8,128)S(1)} %apply_residual.1.refs_0_, f32[8,256]{1,0:T(8,128)S(1)} %collective-permute-done.8.refs_1_, ...), custom_call_target="tpu_custom_call" | custom-call | flops 7864 | bytes 31457 | tf_op jit(solution)/shard_map/finish/pallas_call | solution.py:546
  (1 shorter events, 0.0 us)
Async XLA Ops:
  3.3 12.3 %collective-permute-start.1 = (bf16[17,64,256]{2,1,0:T(8,128)(2,1)S(1)}, bf16[17,64,256]{2,1,0:T(8,128)(2,1)S(1)}, u32[]{:S(2)}, u32[]{:S(2)}) collective-permute-start(bf16[17,64,256]{2,1,0:T(8,128)(2,1)S(1)} %get-tuple-element.24.x_ref.own_ref.refs_0_), channel_id=1, source_target_pairs={{0,1},{1,0},{2,3},{3,2},{4,5},{5,4},{6,7},{7,6},{8,9},{9,8},{10,11... | collective-permute-start | bytes 1671176 | tf_op jit(solution)/shard_map/ppermute | solution.py:373
  3.9 15.8 %collective-permute-start = (bf16[17,64,256]{2,1,0:T(8,128)(2,1)S(1)}, bf16[17,64,256]{2,1,0:T(8,128)(2,1)S(1)}, u32[]{:S(2)}, u32[]{:S(2)}) collective-permute-start(bf16[17,64,256]{2,1,0:T(8,128)(2,1)S(1)} %get-tuple-element.24.x_ref.own_ref.refs_0_), channel_id=1, source_target_pairs={{0,2},{1,3},{2,0},{3,1},{4,6},{5,7},{6,4},{7,5},{8,10},{9,11},{10,... | collective-permute-start | bytes 1671176 | tf_op jit(solution)/shard_map/ppermute | solution.py:376
  6.4 9.1 %collective-permute-start.2 = (bf16[3,272,128]{2,1,0:T(8,128)(2,1)S(1)}, bf16[3,272,128]{2,1,0:T(8,128)(2,1)S(1)}, u32[]{:S(2)}, u32[]{:S(2)}) collective-permute-start(bf16[3,272,128]{2,1,0:T(8,128)(2,1)S(1)} %get-tuple-element.26), channel_id=1, source_target_pairs={{4,0},{8,4},{12,8},{16,12},{20,16},{24,20},{28,24},{5,1},{9,5},{13... | collective-permute-start | bytes 626696 | tf_op jit(solution)/shard_map/ppermute | solution.py:420
  19.7 3.9 %collective-permute-start.3 = (bf16[17,64,256]{2,1,0:T(8,128)(2,1)S(1)}, bf16[17,64,256]{2,1,0:T(8,128)(2,1)S(1)}, u32[]{:S(2)}, u32[]{:S(2)}) collective-permute-start(bf16[17,64,256]{2,1,0:T(8,128)(2,1)S(1)} %collective-permute-done.x_ref.refs_0_.own_ref), channel_id=1, source_target_pairs={{0,1},{1,0},{2,3},{3,2},{4,5},{5,4},{6,7},{7,6},{8,9},{9,8},{10,11... | collective-permute-start | bytes 1671176 | tf_op jit(solution)/shard_map/ppermute | solution.py:373
  19.7 8.0 %collective-permute-start.4 = (bf16[3,272,128]{2,1,0:T(8,128)(2,1)S(1)}, bf16[3,272,128]{2,1,0:T(8,128)(2,1)S(1)}, u32[]{:S(2)}, u32[]{:S(2)}) collective-permute-start(bf16[3,272,128]{2,1,0:T(8,128)(2,1)S(1)} %get-tuple-element.33), channel_id=1, source_target_pairs={{0,2},{1,3},{2,0},{3,1},{4,6},{5,7},{6,4},{7,5},{8,10},{9,11},{10,... | collective-permute-start | bytes 626696 | tf_op jit(solution)/shard_map/ppermute | solution.py:376
  21.4 10.3 %collective-permute-start.5 = (bf16[3,272,128]{2,1,0:T(8,128)(2,1)S(1)}, bf16[3,272,128]{2,1,0:T(8,128)(2,1)S(1)}, u32[]{:S(2)}, u32[]{:S(2)}) collective-permute-start(bf16[3,272,128]{2,1,0:T(8,128)(2,1)S(1)} %broadcast_select_fusion.packed_ref), channel_id=1, source_target_pairs={{0,2},{1,3},{2,0},{3,1},{4,6},{5,7},{6,4},{7,5},{8,10},{9,11},{10,... | collective-permute-start | bytes 626696 | tf_op jit(solution)/shard_map/ppermute | solution.py:376
  34.4 14.4 %copy-start = (f32[1,64,16,256]{3,2,1,0:T(8,128)S(1)}, f32[1,64,16,256]{3,2,1,0:T(8,128)}, u32[]{:S(2)}) copy-start(f32[1,64,16,256]{3,2,1,0:T(8,128)} %param.5) | copy-start | bytes 3145732
  34.4 4.2 %collective-permute-start.7 = (bf16[16,256,256]{2,1,0:T(8,128)(2,1)S(1)}, bf16[16,256,256]{2,1,0:T(8,128)(2,1)S(1)}, u32[]{:S(2)}, u32[]{:S(2)}) collective-permute-start(bf16[16,256,256]{2,1,0:T(8,128)(2,1)S(1)} %get-tuple-element.41.partial_ref), channel_id=1, source_target_pairs={{0,1},{1,0},{2,3},{3,2},{4,5},{5,4},{6,7},{7,6},{8,9},{9,8},{10,11... | collective-permute-start | bytes 6291464 | tf_op jit(solution)/shard_map/ppermute | solution.py:373
  34.5 4.2 %collective-permute-start.6 = (f32[8,256]{1,0:T(8,128)S(1)}, f32[8,256]{1,0:T(8,128)S(1)}, u32[]{:S(2)}, u32[]{:S(2)}) collective-permute-start(f32[8,256]{1,0:T(8,128)S(1)} %get-tuple-element.40.mine_ref), channel_id=1, source_target_pairs={{0,1},{1,0},{2,3},{3,2},{4,5},{5,4},{6,7},{7,6},{8,9},{9,8},{10,11... | collective-permute-start | bytes 24584 | tf_op jit(solution)/shard_map/ppermute | solution.py:373
  46.6 3.1 %collective-permute-start.10 = (f32[8,256]{1,0:T(8,128)S(1)}, f32[8,256]{1,0:T(8,128)S(1)}, u32[]{:S(2)}, u32[]{:S(2)}) collective-permute-start(f32[8,256]{1,0:T(8,128)S(1)} %apply_residual.1.refs_0_), channel_id=1, source_target_pairs={{0,3},{1,2},{2,1},{3,0},{4,7},{5,6},{6,5},{7,4},{8,11},{9,10},{10,... | collective-permute-start | bytes 24584 | tf_op jit(solution)/shard_map/ppermute | solution.py:386
  48.1 1.6 %collective-permute-start.8 = (f32[8,256]{1,0:T(8,128)S(1)}, f32[8,256]{1,0:T(8,128)S(1)}, u32[]{:S(2)}, u32[]{:S(2)}) collective-permute-start(f32[8,256]{1,0:T(8,128)S(1)} %apply_residual.1.refs_0_), channel_id=1, source_target_pairs={{0,1},{1,0},{2,3},{3,2},{4,5},{5,4},{6,7},{7,6},{8,9},{9,8},{10,11... | collective-permute-start | bytes 24584 | tf_op jit(solution)/shard_map/ppermute | solution.py:386
  48.5 3.7 %collective-permute-start.9 = (f32[8,256]{1,0:T(8,128)S(1)}, f32[8,256]{1,0:T(8,128)S(1)}, u32[]{:S(2)}, u32[]{:S(2)}) collective-permute-start(f32[8,256]{1,0:T(8,128)S(1)} %apply_residual.1.refs_0_), channel_id=1, source_target_pairs={{0,2},{1,3},{2,0},{3,1},{4,6},{5,7},{6,4},{7,5},{8,10},{9,11},{10,... | collective-permute-start | bytes 24584 | tf_op jit(solution)/shard_map/ppermute | solution.py:386

commit v6 on v5

--- a/solution.py
+++ b/solution.py
@@ -10,7 +10,7 @@
 epsilon = 1e-06
 CORES = 2
 TILE = 16
-UNROLL = 4
+UNROLL = 8
 GROUP = 4
 VMEM_LIMIT = 20 * 1024 * 1024
 F32 = jnp.float32
@@ -32,6 +32,10 @@
 
 def keep_row(rank, width):
     return (lax.broadcasted_iota(jnp.int32, (1, width), 1) < rank).astype(F32)
+
+
+def fold(values, width):
+    return jnp.sum(values.reshape(values.size // (8 * width), 8, width), axis=0)
 
 
 def prepare_kernel(
@@ -53,17 +57,25 @@
     rows, states, width = guess_ref.shape
     terms = left_ref.shape[0]
     half = width // 2
-    sources = (guess_in, site_in, right_in, left_in)
-    targets = (guess_ref, site_ref, right_ref, left_ref)
-    copies = [pltpu.make_async_copy(sources[n], targets[n], sems.at[n]) for n in range(4)]
+    parts = [pl.ds(n, TILE) for n in range(0, rows, TILE)]
+    sources = [guess_in.at[part] for part in parts] + [site_in, right_in, left_in]
+    targets = [guess_ref.at[part] for part in parts] + [site_ref, right_ref, left_ref]
+    copies = [
+        pltpu.make_async_copy(source, target, sems.at[n])
+        for n, (source, target) in enumerate(zip(sources, targets))
+    ]
     for copy in copies:
         copy.start()
-    copies[0].wait()
-    masked = guess_ref[...] * keep_row(rank_ref[0], width)[None]
-    total = jnp.sum(masked * masked)
+    keep = keep_row(rank_ref[0], width)[None]
+    squares = jnp.zeros((8, width), F32)
+    for n, part in enumerate(parts):
+        copies[n].wait()
+        masked = guess_ref[part] * keep
+        squares = squares + fold(masked * masked, width)
+        x_ref[0:states, part, :] = jnp.swapaxes(masked, 0, 1).astype(BF16)
+    total = jnp.sum(squares)
     norm_ref[...] = jnp.full(norm_ref.shape, total, F32)
-    x_ref[0:states] = jnp.swapaxes(masked, 0, 1).astype(BF16)
-    copies[1].wait()
+    copies[-3].wait()
     widen = (
         lax.broadcasted_iota(jnp.int32, (states, width), 0) == lax.broadcasted_iota(jnp.int32, (states, width), 1)
     ).astype(BF16)
@@ -78,7 +90,7 @@
         slab, row = divmod(k * TILE, rows)
         sites = lines if k == terms else jnp.dot(site_ref[k], widen, preferred_element_type=F32).astype(BF16)
         x_ref[states + slab, row : row + TILE, :] = sites
-    for copy, block_ref, packed_ref in zip(copies[2:], (right_ref, left_ref), (right_packed_ref, left_packed_ref)):
+    for copy, block_ref, packed_ref in zip(copies[-2:], (right_ref, left_ref), (right_packed_ref, left_packed_ref)):
         copy.wait()
         for k in range(terms):
             diagonal = pack_symmetric(block_ref, k, packed_ref)
@@ -159,10 +171,6 @@
     lax.fori_loop(0, rows // TILE, step, 0, unroll=min(unroll, rows // TILE))
 
 
-def fold(values, width):
-    return jnp.sum(values.reshape(values.size // (8 * width), 8, width), axis=0)
-
-
 def summed(values):
     while len(values) > 1:
         values = [values[n] + values[n + 1] for n in range(0, len(values), 2)]
@@ -175,16 +183,16 @@
     return chip, me % CORES
 
 
-def chip_kernel(hop, chips, own_ref, sib_ref, left_ref, packed_ref, kron_ref, *refs):
-    before_ref = None if hop == 0 else refs[0]
-    out_ref, rotated_ref, turned_ref, columns_ref, right_ref = refs[-5:]
-    terms, states, chip_rows, width = rotated_ref.shape
+def rotate_own_kernel(own_ref, sib_ref, kron_ref, rotated_ref):
     rows = own_ref.shape[1]
-    chip, core = place(hop, chips)
+    _, core = place(0, 1)
     mix_sites(own_ref, kron_ref, rotated_ref, core * rows, UNROLL)
     mix_sites(sib_ref, kron_ref, rotated_ref, (1 - core) * rows, UNROLL)
+
+
+def turn_and_mix(chip, left_ref, right_ref, rotated_ref, before_ref, out_ref, turned_ref, columns_ref):
+    terms, states, chip_rows, width = rotated_ref.shape
     at = pl.multiple_of(chip * chip_rows, TILE)
-    unpack_symmetric(packed_ref, right_ref)
     columns = jnp.concatenate([left_ref[k, pl.ds(at, chip_rows), :] for k in range(terms)], axis=0)
     columns_ref[...] = columns.astype(F32).T.astype(BF16)
     for k in range(terms):
@@ -201,6 +209,19 @@
         return carry
 
     lax.fori_loop(0, states, lefts, 0, unroll=UNROLL)
+
+
+def here_kernel(chips, rotated_ref, left_ref, packed_ref, out_ref, right_ref, turned_ref, columns_ref):
+    chip, _ = place(0, chips)
+    unpack_symmetric(packed_ref, right_ref)
+    turn_and_mix(chip, left_ref, right_ref, rotated_ref, None, out_ref, turned_ref, columns_ref)
+
+
+def there_kernel(hop, chips, own_ref, sib_ref, left_ref, right_ref, kron_ref, before_ref, out_ref, *scratch):
+    rotated_ref, turned_ref, columns_ref = scratch
+    chip, _ = place(hop, chips)
+    rotate_own_kernel(own_ref, sib_ref, kron_ref, rotated_ref)
+    turn_and_mix(chip, left_ref, right_ref, rotated_ref, before_ref, out_ref, turned_ref, columns_ref)
 
 
 def rotate_kernel(hops, chips, *refs):
@@ -228,9 +249,13 @@
         copy.wait()
 
 
-def lefts_kernel(rotated_ref, packed_ref, mixed_ref, left_ref):
+def lefts_kernel(hops, chips, *refs):
+    count = CORES * len(hops)
+    packed_ref = refs[count + 3]
+    mixed_ref, rotated_ref, whole_ref, left_ref, sems = refs[-5:]
     terms, states, width, _ = rotated_ref.shape
     unpack_symmetric(packed_ref, left_ref)
+    rotate_kernel(hops, chips, *refs[: count + 1], rotated_ref, whole_ref, sems)
 
     def lefts(p, carry):
         for k in range(terms):
@@ -241,33 +266,42 @@
     lax.fori_loop(0, states, lefts, 0, unroll=UNROLL)
 
 
-def rights_kernel(
-    mixed_ref, packed_ref, whole_ref, before_ref, stat_before_ref, norm_ref, partial_ref, stat_ref, right_ref
-):
+def rights_kernel(start, stop, packed_ref, mixed_ref, whole_ref, before_ref, *refs):
+    if start == 0:
+        stats = refs[:-3]
+        partial_ref, stat_ref, right_ref = refs[-3:]
+        unpack_symmetric(packed_ref, right_ref)
+    else:
+        stats = refs[:-2]
+        partial_ref, stat_ref = refs[-2:]
+        right_ref = packed_ref
     states, width, _ = whole_ref.shape
     terms = right_ref.shape[0]
-    unpack_symmetric(packed_ref, right_ref)
 
     def rights(n, total):
         at = n * GROUP
-        rows = mixed_ref[pl.ds(at, GROUP)].reshape(GROUP * width, terms * width)
+        rows = mixed_ref[pl.ds(start + at, GROUP)].reshape(GROUP * width, terms * width)
         stacked = right_ref[...].reshape(terms * width, width)
         image = jnp.dot(rows, stacked, preferred_element_type=F32).reshape(GROUP, width, width)
-        part = (before_ref[pl.ds(at, GROUP)].astype(F32) + image).astype(partial_ref.dtype)
+        part = (before_ref[pl.ds(start + at, GROUP)].astype(F32) + image).astype(partial_ref.dtype)
         partial_ref[pl.ds(at, GROUP)] = part
-        held = whole_ref[pl.ds(at, GROUP)].astype(F32)
+        held = whole_ref[pl.ds(start + at, GROUP)].astype(F32)
         return total + fold(held * part.astype(F32), width)
 
-    total = lax.fori_loop(0, states // GROUP, rights, jnp.zeros((8, width), F32))
-    stat_ref[0:1, :] = jnp.full((1, width), jnp.sum(total), F32)
-    stat_ref[1:2, :] = stat_before_ref[1:2, :] + norm_ref[1:2, :]
-    stat_ref[2:8, :] = jnp.zeros((6, width), F32)
+    total = lax.fori_loop(0, (stop - start) // GROUP, rights, jnp.zeros((8, width), F32))
+    stat_ref[...] = functools.reduce(jnp.add, [stat[...] for stat in stats])
+    product = jnp.full((1, width), jnp.sum(total), F32)
+    stat_ref[0:1, :] = product if start == 0 else stats[0][0:1, :] + product
 
 
 def scales(rank_ref, mine_ref, theirs_ref, scale, width):
     inverse = lax.rsqrt((mine_ref[1:2, :] + theirs_ref[1:2, :]) * scale + epsilon)
     rayleigh = (mine_ref[0:1, :] + theirs_ref[0:1, :]) * (inverse * inverse * scale)
     return inverse, rayleigh, keep_row(rank_ref[0], width) * inverse
+
+
+def add_kernel(mine_ref, other_ref, sum_ref):
+    sum_ref[...] = mine_ref[...].astype(F32) + other_ref[...].astype(F32)
 
 
 def second_kernel(
@@ -276,36 +310,39 @@
     rank_ref,
     mine_ref,
     theirs_ref,
-    partial_ref,
-    other_ref,
+    low_ref,
+    high_ref,
+    high_other_ref,
     whole_ref,
     left_ref,
-    packed_ref,
+    right_ref,
     kron_ref,
     out_ref,
     res_ref,
     rotated_ref,
     mixed_ref,
-    right_ref,
 ):
     terms, states, width, _ = rotated_ref.shape
-    unpack_symmetric(packed_ref, right_ref)
     inverse, rayleigh, row_scale = scales(rank_ref, mine_ref, theirs_ref, scale, width)
     back = rayleigh * inverse
 
-    def lefts(p, total):
-        sigma = (partial_ref[p].astype(F32) + other_ref[p].astype(F32)) * row_scale
-        residual = sigma - back * whole_ref[p].astype(F32)
-        rounded = residual.astype(BF16)
-        res_ref[p] = rounded
-        mixed = jnp.dot(
-            left_ref[...].reshape(terms * width, width), rounded, preferred_element_type=F32
-        ).astype(BF16)
-        for k in range(terms):
-            mixed_ref[k, p] = mixed[k * width : (k + 1) * width]
-        return total + fold(residual * residual, width)
-
-    square = lax.fori_loop(0, states, lefts, jnp.zeros((8, width), F32), unroll=UNROLL)
+    square = jnp.zeros((8, width), F32)
+    for start, halves in ((0, (low_ref,)), (states // 2, (high_ref, high_other_ref))):
+
+        def lefts(n, total):
+            p = start + n
+            sigma = functools.reduce(jnp.add, [half[n].astype(F32) for half in halves]) * row_scale
+            residual = sigma - back * whole_ref[p].astype(F32)
+            rounded = residual.astype(BF16)
+            res_ref[p] = rounded
+            mixed = jnp.dot(
+                left_ref[...].reshape(terms * width, width), rounded, preferred_element_type=F32
+            ).astype(BF16)
+            for k in range(terms):
+                mixed_ref[k, p] = mixed[k * width : (k + 1) * width]
+            return total + fold(residual * residual, width)
+
+        square = lax.fori_loop(0, states // 2, lefts, square, unroll=UNROLL)
     mix_sites(res_ref, kron_ref, rotated_ref, 0, 2 * UNROLL)
 
     def rights(n, total):
@@ -325,21 +362,21 @@
     out_ref[3:8, :] = jnp.zeros((5, width), F32)
 
 
-def own_rows_kernel(
-    scale, rank_ref, guess_ref, mine_ref, theirs_ref, partial_ref, other_ref, vector_ref, residual_ref
-):
+def own_rows_kernel(scale, rank_ref, guess_ref, mine_ref, theirs_ref, *refs):
+    low_ref, high_ref, high_other_ref, vector_ref, residual_ref = refs
     rows, states, width = guess_ref.shape
     inverse, rayleigh, row_scale = scales(rank_ref, mine_ref, theirs_ref, scale, width)
     own = pl.ds(pl.multiple_of(lax.axis_index("term") * rows, TILE), rows)
-    sigma = (partial_ref[:, own, :].astype(F32) + other_ref[:, own, :].astype(F32)) * row_scale[None]
     vector = guess_ref[...] * row_scale[None]
     vector_ref[...] = vector
+    high = high_ref[:, own, :].astype(F32) + high_other_ref[:, own, :].astype(F32)
+    sigma = jnp.concatenate([low_ref[:, own, :], high], axis=0) * row_scale[None]
     residual_ref[...] = jnp.swapaxes(sigma, 0, 1) - rayleigh[None] * vector
 
 
 def finish_kernel(vector_ref, residual_ref, *refs):
-    shares = refs[:-2]
-    ritz_ref, energy_ref = refs[-2:]
+    shares = refs[:-4]
+    ritz_hbm, energy_ref, ritz_ref, sems = refs[-4:]
     stat = summed([share[...] for share in shares])
     rayleigh = stat[0:1, :]
     res_sq = stat[1:2, :]
@@ -353,8 +390,16 @@
     coeff_norm = jnp.sqrt(coupling * coupling + coeff_new * coeff_new + epsilon)
     old = coupling / coeff_norm
     new = coeff_new / (coeff_norm * res_scale)
-    ritz_ref[...] = old[None] * vector_ref[...] + new[None] * residual_ref[...]
+    rows = vector_ref.shape[0]
+    copies = []
+    for n in range(0, rows, TILE):
+        part = pl.ds(n, TILE)
+        ritz_ref[part] = old[None] * vector_ref[part] + new[None] * residual_ref[part]
+        copies.append(pltpu.make_async_copy(ritz_ref.at[part], ritz_hbm.at[part], sems.at[n // TILE]))
+        copies[-1].start()
     energy_ref[0] = energy[0, 0]
+    for copy in copies:
+        copy.wait()
 
 
 def shards(wave_guess, left_env, right_env, site_ops, bond_rank):
@@ -406,7 +451,7 @@
             pltpu.VMEM(guess.shape, F32),
             pltpu.VMEM(left.shape, BF16),
             pltpu.VMEM(site.shape, BF16),
-            pltpu.SemaphoreType.DMA((4,)),
+            pltpu.SemaphoreType.DMA((rows // TILE + 3,)),
         ],
         compiler_params=params(),
         cost_estimate=cost(4 * guess.size, 6 * guess.size),
@@ -418,8 +463,6 @@
     lefts = around(left_packed)
     shift = [(i + 1, i) for i in range(segments - 1)]
     received = lax.ppermute(right_packed, "seg", shift)
-    packed = jnp.where(lax.axis_index("seg") == segments - 1, right_packed, received)
-    rights = around(packed)
 
     size = states * TILE
 
@@ -445,109 +488,153 @@
     chip_rows = CORES * rows
     stage_flops = 2 * terms * states * width * width * width
 
-    def chip_part(hop, before):
+    mix_scratch = [
+        pltpu.VMEM((states, terms * chip_rows, width), BF16),
+        pltpu.VMEM((width, terms * chip_rows), BF16),
+    ]
+    chip_rotated = (terms, states, chip_rows, width)
+    chip_cost = cost(3 * stage_flops * chip_rows / width, 8 * states * width * width)
+    rotated_own = pl.pallas_call(
+        rotate_own_kernel,
+        out_shape=jax.ShapeDtypeStruct(chip_rotated, BF16),
+        in_specs=[vmem] * 3,
+        out_specs=vmem,
+        compiler_params=params(),
+        cost_estimate=chip_cost,
+        name="rotate_own",
+    )(*pieces, kron_own)
+    received, rotated_own = lax.optimization_barrier((received, rotated_own))
+    packed = jnp.where(lax.axis_index("seg") == segments - 1, right_packed, received)
+    rights = around(packed)
+    partial, right = pl.pallas_call(
+        functools.partial(here_kernel, chips),
+        out_shape=(whole_f32, jax.ShapeDtypeStruct(left.shape, BF16)),
+        in_specs=[vmem] * 3,
+        out_specs=(vmem, vmem),
+        scratch_shapes=mix_scratch,
+        compiler_params=params(),
+        cost_estimate=chip_cost,
+        name="apply_rows_here",
+    )(rotated_own, left, packed)
+
+    def there(hop, before):
         return pl.pallas_call(
-            functools.partial(chip_kernel, hop, chips),
+            functools.partial(there_kernel, hop, chips),
             out_shape=whole_f32,
-            in_specs=[vmem] * (5 if hop == 0 else 6),
+            in_specs=[vmem] * 6,
             out_specs=vmem,
-            scratch_shapes=[
-                pltpu.VMEM((terms, states, chip_rows, width), BF16),
-                pltpu.VMEM((states, terms * chip_rows, width), BF16),
-                pltpu.VMEM((width, terms * chip_rows), BF16),
-                square,
-            ],
+            scratch_shapes=[pltpu.VMEM(chip_rotated, BF16)] + mix_scratch,
             compiler_params=params(),
-            cost_estimate=cost(3 * stage_flops * chip_rows / width, 8 * states * width * width),
-            name="apply_rows_here" if hop == 0 else "apply_rows_there",
-        )(*pieces[2 * hop : 2 * hop + 2], left, packed, kron_own, *before)
-
-    def rotate(part, kron, before):
-        inputs = pieces[CORES * part[0] : CORES * (part[-1] + 1)]
+            cost_estimate=chip_cost,
+            name="apply_rows_there",
+        )(*pieces[2 * hop : 2 * hop + 2], left, right, kron_own, before)
+
+    def rotate(kron):
         return pl.pallas_call(
-            functools.partial(rotate_kernel, part, chips),
+            functools.partial(rotate_kernel, hops[:1], chips),
             out_shape=(rotated_bf, whole_bf),
-            in_specs=[vmem] * (len(inputs) + 1) + [anywhere] * len(before),
+            in_specs=[vmem] * 3,
             out_specs=(vmem, vmem),
-            scratch_shapes=[pltpu.SemaphoreType.DMA((len(inputs),))],
-            input_output_aliases={len(inputs) + 1 + n: n for n in range(len(before))},
+            scratch_shapes=[pltpu.SemaphoreType.DMA((CORES,))],
             compiler_params=params(),
-            cost_estimate=cost(stage_flops / 2, 8 * states * width * width),
-            name="rotate_here" if part[0] == 0 else "rotate_there",
-        )(*inputs, kron, *before)
-
-    partial = chip_part(0, ())
+            cost_estimate=chip_cost,
+            name="rotate_here",
+        )(*pieces[:CORES], kron)
+
     crossed, partial = lax.optimization_barrier((x_hops[1:], partial))
     for block in crossed:
         pieces += [block, to_sibling(block)]
     kron, norm_far = spread(crossed[0])
-    turned_here = rotate(hops[:1], kron, ())
+    turned = rotate(kron)
     for hop in hops[1:]:
-        partial = chip_part(hop, (partial,))
-    stat = norm_part
+        partial = there(hop, partial)
+    far = pieces[CORES:]
+    norms = [norm_part]
     for hop in hops[1:]:
         if hop > 1:
             block, partial = lax.optimization_barrier((crossed[hop - 1], partial))
             kron, norm_far = spread(block)
-            turned_here = rotate(hops[:1], kron, ())
-        turned, vector = rotate(hops[1:], kron, turned_here)
+            turned = rotate(kron)
+        norms.append(norm_far)
         left_far, partial = lax.optimization_barrier((lefts[hop], partial))
-        mixed = pl.pallas_call(
-            lefts_kernel,
-            out_shape=jax.ShapeDtypeStruct((states, width, terms * width), BF16),
-            in_specs=[vmem] * 2,
-            out_specs=vmem,
-            scratch_shapes=[square],
+        mixed, _, vector = pl.pallas_call(
+            functools.partial(lefts_kernel, hops[1:], chips),
+            out_shape=(jax.ShapeDtypeStruct((states, width, terms * width), BF16), rotated_bf, whole_bf),
+            in_specs=[vmem] * (len(far) + 1) + [anywhere] * 2 + [vmem],
+            out_specs=(vmem,) * 3,
+            scratch_shapes=[square, pltpu.SemaphoreType.DMA((len(far),))],
+            input_output_aliases={len(far) + 1: 1, len(far) + 2: 2},
             compiler_params=params(),
             cost_estimate=cost(stage_flops, 12 * states * width * width),
             name="received_lefts",
-        )(turned, left_far)
-        partial, stat = pl.pallas_call(
-            rights_kernel,
-            out_shape=(whole_bf if hop == hops[-1] else whole_f32, tile),
-            in_specs=[vmem] * 6,
-            out_specs=(vmem, vmem),
-            scratch_shapes=[square],
-            compiler_params=params(),
-            cost_estimate=cost(stage_flops, 12 * states * width * width),
-            name="received_rights",
-        )(mixed, rights[hop], vector, partial, stat, norm_far)
-    other = to_sibling(partial)
+        )(*far, kron, *turned, left_far)
+        last = hop == hops[-1]
+        stats = norms if last else norms[:1]
+        right_far = rights[hop]
+        parts = []
+        bounds = (0, states // 2, states) if last else (0, states)
+        for start, stop in zip(bounds[:-1], bounds[1:]):
+            outs = [jax.ShapeDtypeStruct((stop - start, width, width), BF16 if last else F32), tile]
+            part, stat, *unpacked = pl.pallas_call(
+                functools.partial(rights_kernel, start, stop),
+                out_shape=tuple(outs + ([jax.ShapeDtypeStruct(left.shape, BF16)] if start == 0 else [])),
+                in_specs=[vmem] * (4 + len(stats)),
+                out_specs=(vmem,) * (3 if start == 0 else 2),
+                compiler_params=params(),
+                cost_estimate=cost(stage_flops / 2, 12 * states * width * width),
+                name="received_rights",
+            )(right_far, mixed, vector, partial, *stats)
+            stats = [stat]
+            if unpacked:
+                right_far = unpacked[0]
+            parts.append(part)
+        if not last:
+            partial = parts[0]
+    low = pl.pallas_call(
+        add_kernel,
+        out_shape=jax.ShapeDtypeStruct(parts[0].shape, F32),
+        in_specs=[vmem] * 2,
+        out_specs=vmem,
+        compiler_params=params(),
+        cost_estimate=cost(parts[0].size, 8 * parts[0].size),
+        name="add_low_half",
+    )(parts[0], to_sibling(parts[0]))
+    halves = [low, parts[1], to_sibling(parts[1])]
     stat_other = to_sibling(stat)
 
     share = pl.pallas_call(
         functools.partial(second_kernel, scale, members),
         out_shape=tile,
-        in_specs=[smem] + [vmem] * 8,
+        in_specs=[smem] + [vmem] * 9,
         out_specs=vmem,
         scratch_shapes=[
             pltpu.VMEM(whole, BF16),
             pltpu.VMEM(rotated, BF16),
             pltpu.VMEM(rotated, BF16),
-            square,
         ],
         compiler_params=params(),
         cost_estimate=cost(3 * stage_flops, 6 * states * width * width),
         name="apply_residual",
-    )(bond_rank, stat, stat_other, partial, other, vector, left, packed, kron_own)
+    )(bond_rank, stat, stat_other, *halves, vector, left, right, kron_own)
     shares = everyone(share)
 
     local = jax.ShapeDtypeStruct((rows, states, width), F32)
     vector_own, residual_own = pl.pallas_call(
         functools.partial(own_rows_kernel, scale),
         out_shape=(local, local),
-        in_specs=[smem] + [vmem] * 5,
+        in_specs=[smem] + [vmem] * 6,
         out_specs=(vmem, vmem),
         compiler_params=params(),
         cost_estimate=cost(8 * guess.size, 16 * guess.size),
         name="own_rows",
-    )(bond_rank, guess, stat, stat_other, partial, other)
+    )(bond_rank, guess, stat, stat_other, *halves)
 
     ritz, energy = pl.pallas_call(
         finish_kernel,
         out_shape=(local, jax.ShapeDtypeStruct((1,), F32)),
         in_specs=[vmem] * (2 + members),
-        out_specs=(vmem, smem),
+        out_specs=(anywhere, smem),
+        scratch_shapes=[pltpu.VMEM(guess.shape, F32), pltpu.SemaphoreType.DMA((rows // TILE,))],
         compiler_params=params(),
         cost_estimate=cost(3 * guess.size, 12 * guess.size),
         name="finish",

time: 53.7 us -> 50.7 us (0.944)
  Pallas kernels: 28.4 us -> 26.2 us
  waiting for transfers between devices: 14.4 us -> 13.5 us
    pallas_call x1, Pallas kernels: 7.95 us -> 6.1 us  [shards(): pl.pallas_call(functools.partial(second_kernel, scale, members), out_shap...]
    ppermute x3, waiting for transfers between devices: 1.04 us -> 2.82 us  [to_next_chip(): lax.ppermute(block, 'term', [(i, (i + CORES) % members) for i in range(me...]
    ppermute x4 -> x5, waiting for transfers between devices: 3.67 us -> 2.01 us  [to_sibling(): return lax.ppermute(block, 'term', [(i, i ^ 1) for i in range(members)])]
    ppermute x1, waiting for transfers between devices: 6.77 us -> 5.78 us  [shards(): received = lax.ppermute(right_packed, 'seg', shift)]
    pallas_call x6 -> x8, Pallas kernels: 15.1 us -> 14.8 us  [the longest x1 3.41 us: shards(): pl.pallas_call(functools.partial(lefts_kernel, hops[1:], chips), out_shap...]
    ppermute x4 -> x5, starting transfers between devices: 1.09 us -> 1.23 us  [to_sibling(): return lax.ppermute(block, 'term', [(i, i ^ 1) for i in range(members)])]
  transfers between devices with their start and end apart: 11 -> 12, of which waited for: 7 -> 8; matrix products, arithmetic and copies ran while one was open for 0% -> 0% of each run, Pallas kernels for 27% -> 30%
where the time goes in v6:
time: 50.7 us; the launch traced here: 50.5 us
  Pallas kernels  26.2 us (52%)
  waiting for transfers between devices  13.5 us (27%)
  starting transfers between devices  9.2 us (18%)
  between operations  1.58 us (3%)
    pallas_call x1, Pallas kernels, shards(): pl.pallas_call(functools.partial(second_kernel, scale, members), out_shap...  6.1 us
    ppermute x1, waiting for transfers between devices, shards(): received = lax.ppermute(right_packed, 'seg', shift)  5.78 us
    ppermute x3, starting transfers between devices, to_next_chip(): lax.ppermute(block, 'term', [(i, (i + CORES) % members) for i in range(me...  4.62 us
    pallas_call x1, Pallas kernels, shards(): pl.pallas_call(functools.partial(lefts_kernel, hops[1:], chips), out_shap...  3.41 us
    pallas_call x1, Pallas kernels, there(): pl.pallas_call(functools.partial(there_kernel, hop, chips), out_shape=who...  3.33 us
    ppermute x3, waiting for transfers between devices, everyone(): lax.ppermute(block, 'term', [(i, i ^ bits) for i in range(members)])  2.94 us
    pallas_call x2, Pallas kernels, shards(): pl.pallas_call(functools.partial(rights_kernel, start, stop), out_shape=t...  2.84 us
    ppermute x3, waiting for transfers between devices, to_next_chip(): lax.ppermute(block, 'term', [(i, (i + CORES) % members) for i in range(me...  2.82 us
  transfers between devices with their start and end apart: 12, of which 8 were waited for; matrix products, arithmetic and copies ran while one was open for 0% of the time, Pallas kernels for 30%

profile of v6, /device:TPU:0, one launch (start us, length us, event | category | flops | bytes accessed | tf_op | source)
XLA Modules:
  0.0 50.5 jit_solution(15279580999458754370)
XLA Ops:
  1.3 1.7 %prepare.1 = (bf16[17,64,256]{2,1,0:T(8,128)(2,1)S(1)}, f32[8,256]{1,0:T(8,128)S(1)}, bf16[3,272,128]{2,1,0:T(8,128)(2,1)S(1)}, bf16[3,272,128]{2,1,0:T(8,128)(2,1)S(1)}, bf16[3,256,256]{2,1,0:T(8,128)(2,1)S(1)}) custom-call(s32[1]{0:T(128)S(6)} %copy.11.rank_ref, f32[64,16,256]{2,1,0:T(8,128)} %bitcast.5, bf16[3,256,256]{2,1,0:T(8,128)(2,1)} %bitcast.7, ...), custom_call_target="tpu_custom_call" | custom-call | flops 10485 | bytes 15728 | tf_op jit(solution)/shard_map/prepare/pallas_call | solution.py:439
  3.0 0.5 %collective-permute-start.1 = (bf16[17,64,256]{2,1,0:T(8,128)(2,1)S(1)}, bf16[17,64,256]{2,1,0:T(8,128)(2,1)S(1)}, u32[]{:S(2)}, u32[]{:S(2)}) collective-permute-start(bf16[17,64,256]{2,1,0:T(8,128)(2,1)S(1)} %get-tuple-element.32.x_ref.own_ref.refs_0_), channel_id=1, source_target_pairs={{0,1},{1,0},{2,3},{3,2},{4,5},{5,4},{6,7},{7,6},{8,9},{9,8},{10,11... | collective-permute-start | bytes 1671176 | tf_op jit(solution)/shard_map/ppermute | solution.py:418
  3.5 2.6 %collective-permute-start.3 = (bf16[17,64,256]{2,1,0:T(8,128)(2,1)S(1)}, bf16[17,64,256]{2,1,0:T(8,128)(2,1)S(1)}, u32[]{:S(2)}, u32[]{:S(2)}) collective-permute-start(bf16[17,64,256]{2,1,0:T(8,128)(2,1)S(1)} %get-tuple-element.32.x_ref.own_ref.refs_0_), channel_id=1, source_target_pairs={{0,2},{1,3},{2,0},{3,1},{4,6},{5,7},{6,4},{7,5},{8,10},{9,11},{10,... | collective-permute-start | bytes 1671176 | tf_op jit(solution)/shard_map/ppermute | solution.py:421
  6.1 1.3 %collective-permute-start = (bf16[3,272,128]{2,1,0:T(8,128)(2,1)S(1)}, bf16[3,272,128]{2,1,0:T(8,128)(2,1)S(1)}, u32[]{:S(2)}, u32[]{:S(2)}) collective-permute-start(bf16[3,272,128]{2,1,0:T(8,128)(2,1)S(1)} %get-tuple-element.31), channel_id=1, source_target_pairs={{4,0},{8,4},{12,8},{16,12},{20,16},{24,20},{28,24},{5,1},{9,5},{13... | collective-permute-start | bytes 626696 | tf_op jit(solution)/shard_map/ppermute | solution.py:465
  7.4 1.1 %spread_site.2 = (bf16[768,256]{1,0:T(8,128)(2,1)S(1)}, f32[8,256]{1,0:T(8,128)}) custom-call(bf16[17,64,256]{2,1,0:T(8,128)(2,1)S(1)} %get-tuple-element.32.x_ref.own_ref.refs_0_), custom_call_target="tpu_custom_call" | custom-call | flops 1006632 | bytes 3932 | tf_op jit(solution)/shard_map/spread_site/pallas_call | solution.py:470
  8.5 0.0 collective-permute-done.1.sib_ref.refs_1_
  8.5 1.0 %rotate_own.1.rotated_ref = bf16[3,16,128,256]{3,2,1,0:T(8,128)(2,1)S(1)} custom-call(bf16[17,64,256]{2,1,0:T(8,128)(2,1)S(1)} %get-tuple-element.32.x_ref.own_ref.refs_0_, bf16[17,64,256]{2,1,0:T(8,128)(2,1)S(1)} %collective-permute-done.1.sib_ref.refs_1_, bf16[768,256]{1,0:T(8,128)(2,1)S(1)} %get-tuple-element.33.kron_ref), custom_call_target="tpu_custom_call" | custom-call | flops 24159192 | bytes 83886 | tf_op jit(solution)/shard_map/rotate_own/pallas_call | solution.py:497
  9.5 5.8 %collective-permute-done = bf16[3,272,128]{2,1,0:T(8,128)(2,1)S(1)} collective-permute-done((bf16[3,272,128]{2,1,0:T(8,128)(2,1)S(1)}, bf16[3,272,128]{2,1,0:T(8,128)(2,1)S(1)}, u32[]{:S(2)}, u32[]{:S(2)}) %collective-permute-start) | collective-permute-done | bytes 208928 | tf_op jit(solution)/shard_map/ppermute | solution.py:465
  15.3 2.7 %apply_rows_here.1 = (f32[16,256,256]{2,1,0:T(8,128)S(1)}, bf16[3,256,256]{2,1,0:T(8,128)(2,1)S(1)}) custom-call(bf16[3,16,128,256]{3,2,1,0:T(8,128)(2,1)S(1)} %rotate_own.1.rotated_ref, bf16[3,256,256]{2,1,0:T(8,128)(2,1)S(1)} %get-tuple-element.36.left_ref, bf16[3,272,128]{2,1,0:T(8,128)(2,1)S(1)} %broadcast_select_fusion.packed_ref), custom_call_target="tpu_custom_call" | custom-call | flops 24159192 | bytes 83886 | tf_op jit(solution)/shard_map/apply_rows_here/pallas_call | solution.py:509
  18.0 1.4 %collective-permute-done.3.x_ref.own_ref.refs_0_ = bf16[17,64,256]{2,1,0:T(8,128)(2,1)S(1)} collective-permute-done((bf16[17,64,256]{2,1,0:T(8,128)(2,1)S(1)}, bf16[17,64,256]{2,1,0:T(8,128)(2,1)S(1)}, u32[]{:S(2)}, u32[]{:S(2)}) %collective-permute-start.3) | collective-permute-done | bytes 557088 | tf_op jit(solution)/shard_map/ppermute | solution.py:421
  19.3 0.0 collective-permute-start.4
  19.3 1.8 %collective-permute-start.5 = (bf16[3,272,128]{2,1,0:T(8,128)(2,1)S(1)}, bf16[3,272,128]{2,1,0:T(8,128)(2,1)S(1)}, u32[]{:S(2)}, u32[]{:S(2)}) collective-permute-start(bf16[3,272,128]{2,1,0:T(8,128)(2,1)S(1)} %get-tuple-element.42), channel_id=1, source_target_pairs={{0,2},{1,3},{2,0},{3,1},{4,6},{5,7},{6,4},{7,5},{8,10},{9,11},{10,... | collective-permute-start | bytes 626696 | tf_op jit(solution)/shard_map/ppermute | solution.py:421
  21.1 0.3 collective-permute-start.2
  21.4 0.5 %spread_site.3 = (bf16[768,256]{1,0:T(8,128)(2,1)S(1)}, f32[8,256]{1,0:T(8,128)S(1)}) custom-call(bf16[17,64,256]{2,1,0:T(8,128)(2,1)S(1)} %collective-permute-done.3.x_ref.own_ref.refs_0_), custom_call_target="tpu_custom_call" | custom-call | flops 1006632 | bytes 3932 | tf_op jit(solution)/shard_map/spread_site/pallas_call | solution.py:470
  21.9 1.3 %rotate_here.1 = (bf16[3,16,256,256]{3,2,1,0:T(8,128)(2,1)S(1)}, bf16[16,256,256]{2,1,0:T(8,128)(2,1)S(1)}) custom-call(bf16[17,64,256]{2,1,0:T(8,128)(2,1)S(1)} %get-tuple-element.32.x_ref.own_ref.refs_0_, bf16[17,64,256]{2,1,0:T(8,128)(2,1)S(1)} %collective-permute-done.1.sib_ref.refs_1_, bf16[768,256]{1,0:T(8,128)(2,1)S(1)} %get-tuple-element.39.refs_2_), custom_call_target="tpu_custom_call" | custom-call | flops 24159192 | bytes 83886 | tf_op jit(solution)/shard_map/rotate_here/pallas_call | solution.py:533
  23.2 0.0 collective-permute-done.4.sib_ref.refs_1_
  23.2 3.3 %apply_rows_there.1.before_ref = f32[16,256,256]{2,1,0:T(8,128)S(1)} custom-call(bf16[17,64,256]{2,1,0:T(8,128)(2,1)S(1)} %collective-permute-done.3.x_ref.own_ref.refs_0_, bf16[17,64,256]{2,1,0:T(8,128)(2,1)S(1)} %collective-permute-done.4.sib_ref.refs_1_, bf16[3,256,256]{2,1,0:T(8,128)(2,1)S(1)} %get-tuple-element.36.left_ref, ...), custom_call_target="tpu_custom_call" | custom-call | flops 24159192 | bytes 83886 | tf_op jit(solution)/shard_map/apply_rows_there/pallas_call | solution.py:521
  26.5 0.8 %collective-permute-done.5.refs_5_ = bf16[3,272,128]{2,1,0:T(8,128)(2,1)S(1)} collective-permute-done((bf16[3,272,128]{2,1,0:T(8,128)(2,1)S(1)}, bf16[3,272,128]{2,1,0:T(8,128)(2,1)S(1)}, u32[]{:S(2)}, u32[]{:S(2)}) %collective-permute-start.5) | collective-permute-done | bytes 208928 | tf_op jit(solution)/shard_map/ppermute | solution.py:421
  27.3 3.4 %received_lefts.1 = (bf16[16,256,768]{2,1,0:T(8,128)(2,1)S(1)}, bf16[3,16,256,256]{3,2,1,0:T(8,128)(2,1)S(1)}, bf16[16,256,256]{2,1,0:T(8,128)(2,1)S(1)}) custom-call(bf16[17,64,256]{2,1,0:T(8,128)(2,1)S(1)} %collective-permute-done.3.x_ref.own_ref.refs_0_, ...), custom_call_target="tpu_custom_call", output_to_operand_aliasing={{1}: (3, {}), {2}: (4, {})} | custom-call | flops 16106127 | bytes 125829 | tf_op jit(solution)/shard_map/received_lefts/pallas_call | solution.py:560
  30.7 0.7 %collective-permute-done.2.packed_ref = bf16[3,272,128]{2,1,0:T(8,128)(2,1)S(1)} collective-permute-done((bf16[3,272,128]{2,1,0:T(8,128)(2,1)S(1)}, bf16[3,272,128]{2,1,0:T(8,128)(2,1)S(1)}, u32[]{:S(2)}, u32[]{:S(2)}) %collective-permute-start.2) | collective-permute-done | bytes 208928 | tf_op jit(solution)/shard_map/ppermute | solution.py:421
  31.4 1.5 %received_rights.2 = (bf16[8,256,256]{2,1,0:T(8,128)(2,1)S(1)}, f32[8,256]{1,0:T(8,128)S(1)}, bf16[3,256,256]{2,1,0:T(8,128)(2,1)S(1)}) custom-call(bf16[3,272,128]{2,1,0:T(8,128)(2,1)S(1)} %collective-permute-done.2.packed_ref, bf16[16,256,768]{2,1,0:T(8,128)(2,1)S(1)} %get-tuple-element.46.mixed_ref, ...), custom_call_target="tpu_custom_call" | custom-call | flops 8053063 | bytes 125829 | tf_op jit(solution)/shard_map/received_rights/pallas_call | solution.py:578
  32.9 0.1 collective-permute-start.7
  33.0 1.3 %received_rights.3 = (bf16[8,256,256]{2,1,0:T(8,128)(2,1)S(1)}, f32[8,256]{1,0:T(8,128)S(1)}) custom-call(bf16[3,256,256]{2,1,0:T(8,128)(2,1)S(1)} %get-tuple-element.51.packed_ref, bf16[16,256,768]{2,1,0:T(8,128)(2,1)S(1)} %get-tuple-element.46.mixed_ref, bf16[16,256,256]{2,1,0:T(8,128)(2,1)S(1)} %get-tuple-element.47.whole_ref, ...), custom_call_target="tpu_custom_call" | custom-call | flops 8053063 | bytes 125829 | tf_op jit(solution)/shard_map/received_rights/pallas_call | solution.py:578
  34.3 0.6 %collective-permute-start.8 = (bf16[8,256,256]{2,1,0:T(8,128)(2,1)S(1)}, bf16[8,256,256]{2,1,0:T(8,128)(2,1)S(1)}, u32[]{:S(2)}, u32[]{:S(2)}) collective-permute-start(bf16[8,256,256]{2,1,0:T(8,128)(2,1)S(1)} %get-tuple-element.55.refs_1_.high_ref), channel_id=1, source_target_pairs={{0,1},{1,0},{2,3},{3,2},{4,5},{5,4},{6,7},{7,6},{8,9},{9,8},{10,11... | collective-permute-start | bytes 3145736 | tf_op jit(solution)/shard_map/ppermute | solution.py:418
  34.9 0.1 collective-permute-start.6
  35.0 0.7 %collective-permute-done.7.other_ref = bf16[8,256,256]{2,1,0:T(8,128)(2,1)S(1)} collective-permute-done((bf16[8,256,256]{2,1,0:T(8,128)(2,1)S(1)}, bf16[8,256,256]{2,1,0:T(8,128)(2,1)S(1)}, u32[]{:S(2)}, u32[]{:S(2)}) %collective-permute-start.7) | collective-permute-done | bytes 1048608 | tf_op jit(solution)/shard_map/ppermute | solution.py:418
  35.6 0.2 add_low_half.1.refs_0_.low_ref
  35.8 0.0 copy-start
  35.9 1.3 %collective-permute-done.6.theirs_ref = f32[8,256]{1,0:T(8,128)S(1)} collective-permute-done((f32[8,256]{1,0:T(8,128)S(1)}, f32[8,256]{1,0:T(8,128)S(1)}, u32[]{:S(2)}, u32[]{:S(2)}) %collective-permute-start.6) | collective-permute-done | bytes 8224 | tf_op jit(solution)/shard_map/ppermute | solution.py:418
  37.2 0.0 collective-permute-done.8.refs_2_.high_other_ref
  37.2 6.1 %apply_residual.1.refs_0_ = f32[8,256]{1,0:T(8,128)S(1)} custom-call(s32[1]{0:T(128)S(6)} %copy.11.rank_ref, f32[8,256]{1,0:T(8,128)S(1)} %get-tuple-element.53.mine_ref, f32[8,256]{1,0:T(8,128)S(1)} %collective-permute-done.6.theirs_ref, f32[8,256,256]{2,1,0:T(8,128)S(1)} %add_low_half.1.refs_0_.low_ref, ...), custom_call_target="tpu_custom_call" | custom-call | flops 48318384 | bytes 62914 | tf_op jit(solution)/shard_map/apply_residual/pallas_call | solution.py:605
  43.3 1.8 %collective-permute-start.11 = (f32[8,256]{1,0:T(8,128)S(1)}, f32[8,256]{1,0:T(8,128)S(1)}, u32[]{:S(2)}, u32[]{:S(2)}) collective-permute-start(f32[8,256]{1,0:T(8,128)S(1)} %apply_residual.1.refs_0_), channel_id=1, source_target_pairs={{0,3},{1,2},{2,1},{3,0},{4,7},{5,6},{6,5},{7,4},{8,11},{9,10},{10,... | collective-permute-start | bytes 24584 | tf_op jit(solution)/shard_map/ppermute | solution.py:431
  45.1 0.3 collective-permute-start.10
  45.4 0.0 collective-permute-start.9
  45.4 0.0 copy-done
  45.4 0.4 own_rows.1
  45.8 0.7 %collective-permute-done.11.refs_3_ = f32[8,256]{1,0:T(8,128)S(1)} collective-permute-done((f32[8,256]{1,0:T(8,128)S(1)}, f32[8,256]{1,0:T(8,128)S(1)}, u32[]{:S(2)}, u32[]{:S(2)}) %collective-permute-start.11) | collective-permute-done | bytes 8224 | tf_op jit(solution)/shard_map/ppermute | solution.py:431
  46.5 2.3 %collective-permute-done.10.refs_2_ = f32[8,256]{1,0:T(8,128)S(1)} collective-permute-done((f32[8,256]{1,0:T(8,128)S(1)}, f32[8,256]{1,0:T(8,128)S(1)}, u32[]{:S(2)}, u32[]{:S(2)}) %collective-permute-start.10) | collective-permute-done | bytes 8224 | tf_op jit(solution)/shard_map/ppermute | solution.py:431
  48.8 0.0 collective-permute-done.9.refs_1_
  48.8 1.6 %finish.1 = (f32[64,16,256]{2,1,0:T(8,128)}, f32[1]{0:T(128)}) custom-call(f32[64,16,256]{2,1,0:T(8,128)S(1)} %get-tuple-element.56.vector_ref, f32[64,16,256]{2,1,0:T(8,128)S(1)} %get-tuple-element.57.residual_ref, f32[8,256]{1,0:T(8,128)S(1)} %apply_residual.1.refs_0_, f32[8,256]{1,0:T(8,128)S(1)} %collective-permute-done.9.refs_1_, ...), custom_call_target="tpu_custom_call" | custom-call | flops 7864 | bytes 31457 | tf_op jit(solution)/shard_map/finish/pallas_call | solution.py:632
  (1 shorter events, 0.0 us)
Async XLA Ops:
  3.0 5.5 %collective-permute-start.1 = (bf16[17,64,256]{2,1,0:T(8,128)(2,1)S(1)}, bf16[17,64,256]{2,1,0:T(8,128)(2,1)S(1)}, u32[]{:S(2)}, u32[]{:S(2)}) collective-permute-start(bf16[17,64,256]{2,1,0:T(8,128)(2,1)S(1)} %get-tuple-element.32.x_ref.own_ref.refs_0_), channel_id=1, source_target_pairs={{0,1},{1,0},{2,3},{3,2},{4,5},{5,4},{6,7},{7,6},{8,9},{9,8},{10,11... | collective-permute-start | bytes 1671176 | tf_op jit(solution)/shard_map/ppermute | solution.py:418
  3.5 15.8 %collective-permute-start.3 = (bf16[17,64,256]{2,1,0:T(8,128)(2,1)S(1)}, bf16[17,64,256]{2,1,0:T(8,128)(2,1)S(1)}, u32[]{:S(2)}, u32[]{:S(2)}) collective-permute-start(bf16[17,64,256]{2,1,0:T(8,128)(2,1)S(1)} %get-tuple-element.32.x_ref.own_ref.refs_0_), channel_id=1, source_target_pairs={{0,2},{1,3},{2,0},{3,1},{4,6},{5,7},{6,4},{7,5},{8,10},{9,11},{10,... | collective-permute-start | bytes 1671176 | tf_op jit(solution)/shard_map/ppermute | solution.py:421
  6.1 9.1 %collective-permute-start = (bf16[3,272,128]{2,1,0:T(8,128)(2,1)S(1)}, bf16[3,272,128]{2,1,0:T(8,128)(2,1)S(1)}, u32[]{:S(2)}, u32[]{:S(2)}) collective-permute-start(bf16[3,272,128]{2,1,0:T(8,128)(2,1)S(1)} %get-tuple-element.31), channel_id=1, source_target_pairs={{4,0},{8,4},{12,8},{16,12},{20,16},{24,20},{28,24},{5,1},{9,5},{13... | collective-permute-start | bytes 626696 | tf_op jit(solution)/shard_map/ppermute | solution.py:465
  19.3 3.9 %collective-permute-start.4 = (bf16[17,64,256]{2,1,0:T(8,128)(2,1)S(1)}, bf16[17,64,256]{2,1,0:T(8,128)(2,1)S(1)}, u32[]{:S(2)}, u32[]{:S(2)}) collective-permute-start(bf16[17,64,256]{2,1,0:T(8,128)(2,1)S(1)} %collective-permute-done.3.x_ref.own_ref.refs_0_), channel_id=1, source_target_pairs={{0,1},{1,0},{2,3},{3,2},{4,5},{5,4},{6,7},{7,6},{8,9},{9,8},{10,11... | collective-permute-start | bytes 1671176 | tf_op jit(solution)/shard_map/ppermute | solution.py:418
  19.3 8.0 %collective-permute-start.5 = (bf16[3,272,128]{2,1,0:T(8,128)(2,1)S(1)}, bf16[3,272,128]{2,1,0:T(8,128)(2,1)S(1)}, u32[]{:S(2)}, u32[]{:S(2)}) collective-permute-start(bf16[3,272,128]{2,1,0:T(8,128)(2,1)S(1)} %get-tuple-element.42), channel_id=1, source_target_pairs={{0,2},{1,3},{2,0},{3,1},{4,6},{5,7},{6,4},{7,5},{8,10},{9,11},{10,... | collective-permute-start | bytes 626696 | tf_op jit(solution)/shard_map/ppermute | solution.py:421
  21.1 10.3 %collective-permute-start.2 = (bf16[3,272,128]{2,1,0:T(8,128)(2,1)S(1)}, bf16[3,272,128]{2,1,0:T(8,128)(2,1)S(1)}, u32[]{:S(2)}, u32[]{:S(2)}) collective-permute-start(bf16[3,272,128]{2,1,0:T(8,128)(2,1)S(1)} %broadcast_select_fusion.packed_ref), channel_id=1, source_target_pairs={{0,2},{1,3},{2,0},{3,1},{4,6},{5,7},{6,4},{7,5},{8,10},{9,11},{10,... | collective-permute-start | bytes 626696 | tf_op jit(solution)/shard_map/ppermute | solution.py:421
  32.9 2.7 %collective-permute-start.7 = (bf16[8,256,256]{2,1,0:T(8,128)(2,1)S(1)}, bf16[8,256,256]{2,1,0:T(8,128)(2,1)S(1)}, u32[]{:S(2)}, u32[]{:S(2)}) collective-permute-start(bf16[8,256,256]{2,1,0:T(8,128)(2,1)S(1)} %get-tuple-element.54.mine_ref), channel_id=1, source_target_pairs={{0,1},{1,0},{2,3},{3,2},{4,5},{5,4},{6,7},{7,6},{8,9},{9,8},{10,11... | collective-permute-start | bytes 3145736 | tf_op jit(solution)/shard_map/ppermute | solution.py:418
  34.3 2.9 %collective-permute-start.8 = (bf16[8,256,256]{2,1,0:T(8,128)(2,1)S(1)}, bf16[8,256,256]{2,1,0:T(8,128)(2,1)S(1)}, u32[]{:S(2)}, u32[]{:S(2)}) collective-permute-start(bf16[8,256,256]{2,1,0:T(8,128)(2,1)S(1)} %get-tuple-element.55.refs_1_.high_ref), channel_id=1, source_target_pairs={{0,1},{1,0},{2,3},{3,2},{4,5},{5,4},{6,7},{7,6},{8,9},{9,8},{10,11... | collective-permute-start | bytes 3145736 | tf_op jit(solution)/shard_map/ppermute | solution.py:418
  34.9 2.3 %collective-permute-start.6 = (f32[8,256]{1,0:T(8,128)S(1)}, f32[8,256]{1,0:T(8,128)S(1)}, u32[]{:S(2)}, u32[]{:S(2)}) collective-permute-start(f32[8,256]{1,0:T(8,128)S(1)} %get-tuple-element.53.mine_ref), channel_id=1, source_target_pairs={{0,1},{1,0},{2,3},{3,2},{4,5},{5,4},{6,7},{7,6},{8,9},{9,8},{10,11... | collective-permute-start | bytes 24584 | tf_op jit(solution)/shard_map/ppermute | solution.py:418
  35.8 9.5 %copy-start = (f32[1,64,16,256]{3,2,1,0:T(8,128)S(1)}, f32[1,64,16,256]{3,2,1,0:T(8,128)}, u32[]{:S(2)}) copy-start(f32[1,64,16,256]{3,2,1,0:T(8,128)} %param.5) | copy-start | bytes 3145732
  43.3 3.2 %collective-permute-start.11 = (f32[8,256]{1,0:T(8,128)S(1)}, f32[8,256]{1,0:T(8,128)S(1)}, u32[]{:S(2)}, u32[]{:S(2)}) collective-permute-start(f32[8,256]{1,0:T(8,128)S(1)} %apply_residual.1.refs_0_), channel_id=1, source_target_pairs={{0,3},{1,2},{2,1},{3,0},{4,7},{5,6},{6,5},{7,4},{8,11},{9,10},{10,... | collective-permute-start | bytes 24584 | tf_op jit(solution)/shard_map/ppermute | solution.py:431
  45.1 3.7 %collective-permute-start.10 = (f32[8,256]{1,0:T(8,128)S(1)}, f32[8,256]{1,0:T(8,128)S(1)}, u32[]{:S(2)}, u32[]{:S(2)}) collective-permute-start(f32[8,256]{1,0:T(8,128)S(1)} %apply_residual.1.refs_0_), channel_id=1, source_target_pairs={{0,2},{1,3},{2,0},{3,1},{4,6},{5,7},{6,4},{7,5},{8,10},{9,11},{10,... | collective-permute-start | bytes 24584 | tf_op jit(solution)/shard_map/ppermute | solution.py:431
  45.4 3.4 %collective-permute-start.9 = (f32[8,256]{1,0:T(8,128)S(1)}, f32[8,256]{1,0:T(8,128)S(1)}, u32[]{:S(2)}, u32[]{:S(2)}) collective-permute-start(f32[8,256]{1,0:T(8,128)S(1)} %apply_residual.1.refs_0_), channel_id=1, source_target_pairs={{0,1},{1,0},{2,3},{3,2},{4,5},{5,4},{6,7},{7,6},{8,9},{9,8},{10,11... | collective-permute-start | bytes 24584 | tf_op jit(solution)/shard_map/ppermute | solution.py:431

commit v7 on v6

--- a/solution.py
+++ b/solution.py
@@ -39,6 +39,7 @@
 
 
 def prepare_kernel(
+    starts,
     rank_ref,
     guess_in,
     left_in,
@@ -49,11 +50,10 @@
     left_packed_ref,
     right_packed_ref,
     left_ref,
-    guess_ref,
-    right_ref,
-    site_ref,
-    sems,
+    *refs,
 ):
+    chunk_refs = refs[: len(starts)]
+    guess_ref, right_ref, site_ref, sems = refs[len(starts) :]
     rows, states, width = guess_ref.shape
     terms = left_ref.shape[0]
     half = width // 2
@@ -72,24 +72,26 @@
         copies[n].wait()
         masked = guess_ref[part] * keep
         squares = squares + fold(masked * masked, width)
-        x_ref[0:states, part, :] = jnp.swapaxes(masked, 0, 1).astype(BF16)
+        turned = jnp.swapaxes(masked, 0, 1).astype(BF16)
+        x_ref[:, part, :] = turned
+        chunk = max(c for c, start in enumerate(starts) if start <= n * TILE)
+        at = n * TILE - starts[chunk]
+        chunk_refs[chunk][0:states, at : at + TILE, :] = turned
     total = jnp.sum(squares)
     norm_ref[...] = jnp.full(norm_ref.shape, total, F32)
     copies[-3].wait()
-    widen = (
-        lax.broadcasted_iota(jnp.int32, (states, width), 0) == lax.broadcasted_iota(jnp.int32, (states, width), 1)
-    ).astype(BF16)
-    norm = jnp.full((1, width), total, F32)
-    parts = []
-    for _ in range(3):
-        parts.append(norm.astype(BF16).astype(F32))
-        norm = norm - parts[-1]
-    lines = lax.broadcasted_iota(jnp.int32, (TILE, width), 0)
-    lines = functools.reduce(jnp.add, [jnp.where(lines == n, parts[n], 0.0) for n in range(3)]).astype(BF16)
-    for k in range(terms + 1):
-        slab, row = divmod(k * TILE, rows)
-        sites = lines if k == terms else jnp.dot(site_ref[k], widen, preferred_element_type=F32).astype(BF16)
-        x_ref[states + slab, row : row + TILE, :] = sites
+    line = lax.broadcasted_iota(jnp.int32, (TILE, width), 0)
+    lane = lax.broadcasted_iota(jnp.int32, (TILE, width), 1)
+    norm = jnp.full((TILE, width), total, F32)
+    extra = jnp.zeros((TILE, width), F32)
+    for n in range(3):
+        part = norm.astype(BF16).astype(F32)
+        norm = norm - part
+        extra = jnp.where((line == n) & (lane >= half), part, extra)
+    for k in range(terms):
+        place_at = (lane == line + k * TILE).astype(BF16)
+        extra = extra + jnp.dot(site_ref[k], place_at, preferred_element_type=F32)
+    chunk_refs[0][states, 0:TILE, :] = extra.astype(BF16)
     for copy, block_ref, packed_ref in zip(copies[-2:], (right_ref, left_ref), (right_packed_ref, left_packed_ref)):
         copy.wait()
         for k in range(terms):
@@ -131,27 +133,27 @@
         ).astype(BF16)
 
 
-def spread_kernel(x_ref, kron_ref, norm_ref):
-    rows, lanes = x_ref.shape[1:]
+def spread_kernel(chunk_ref, kron_ref, norm_ref):
+    width = chunk_ref.shape[2]
+    half = width // 2
     size = kron_ref.shape[1]
     terms = kron_ref.shape[0] // size
     states = size // TILE
+    tile = chunk_ref[states, 0:TILE, :]
+    lines = tile.astype(F32)
+    norm = lines[0:1, half:width] + lines[1:2, half:width] + lines[2:3, half:width]
+    norm_ref[...] = jnp.broadcast_to(jnp.concatenate([norm, norm], axis=1), norm_ref.shape)
     row_state = lax.broadcasted_iota(jnp.int32, (size, states), 0) // TILE
     pick = (row_state == lax.broadcasted_iota(jnp.int32, (size, states), 1)).astype(BF16)
-    col_state = lax.broadcasted_iota(jnp.int32, (lanes, size), 1) // TILE
-    pick_t = (col_state == lax.broadcasted_iota(jnp.int32, (lanes, size), 0)).astype(BF16)
+    tall = jnp.dot(pick, tile, preferred_element_type=F32).astype(BF16)
+    lane = lax.broadcasted_iota(jnp.int32, (width, size), 0)
+    col_state = lax.broadcasted_iota(jnp.int32, (width, size), 1) // TILE
     same = (
         lax.broadcasted_iota(jnp.int32, (size, size), 0) % TILE
         == lax.broadcasted_iota(jnp.int32, (size, size), 1) % TILE
     )
-    for k in range(terms + 1):
-        slab, row = divmod(k * TILE, rows)
-        sites = x_ref[states + slab, row : row + TILE, :]
-        if k == terms:
-            lines = sites.astype(F32)
-            norm_ref[...] = jnp.broadcast_to(lines[0:1] + lines[1:2] + lines[2:3], norm_ref.shape)
-            break
-        tall = jnp.dot(pick, sites, preferred_element_type=F32).astype(BF16)
+    for k in range(terms):
+        pick_t = (lane == col_state + k * TILE).astype(BF16)
         full = jnp.dot(tall, pick_t, preferred_element_type=F32)
         kron_ref[k * size : (k + 1) * size, :] = jnp.where(same, full, 0.0).astype(BF16)
 
@@ -183,11 +185,13 @@
     return chip, me % CORES
 
 
-def rotate_own_kernel(own_ref, sib_ref, kron_ref, rotated_ref):
-    rows = own_ref.shape[1]
+def rotate_own_kernel(spots, rows, *refs):
+    pieces = refs[: len(spots)]
+    kron_ref, rotated_ref = refs[len(spots) :]
     _, core = place(0, 1)
-    mix_sites(own_ref, kron_ref, rotated_ref, core * rows, UNROLL)
-    mix_sites(sib_ref, kron_ref, rotated_ref, (1 - core) * rows, UNROLL)
+    for (_, flip, offset), piece in zip(spots, pieces):
+        at = (core if flip == 0 else 1 - core) * rows + offset
+        mix_sites(piece, kron_ref, rotated_ref, at, UNROLL)
 
 
 def turn_and_mix(chip, left_ref, right_ref, rotated_ref, before_ref, out_ref, turned_ref, columns_ref):
@@ -217,45 +221,42 @@
     turn_and_mix(chip, left_ref, right_ref, rotated_ref, None, out_ref, turned_ref, columns_ref)
 
 
-def there_kernel(hop, chips, own_ref, sib_ref, left_ref, right_ref, kron_ref, before_ref, out_ref, *scratch):
-    rotated_ref, turned_ref, columns_ref = scratch
-    chip, _ = place(hop, chips)
-    rotate_own_kernel(own_ref, sib_ref, kron_ref, rotated_ref)
+def there_kernel(spots, rows, chips, *refs):
+    count = len(spots)
+    left_ref, right_ref, kron_ref, before_ref, out_ref = refs[count : count + 5]
+    rotated_ref, turned_ref, columns_ref = refs[count + 5 :]
+    chip, _ = place(spots[0][0], chips)
+    rotate_own_kernel(spots, rows, *refs[:count], kron_ref, rotated_ref)
     turn_and_mix(chip, left_ref, right_ref, rotated_ref, before_ref, out_ref, turned_ref, columns_ref)
 
 
-def rotate_kernel(hops, chips, *refs):
-    pieces = refs[: CORES * len(hops)]
-    kron_ref = refs[len(pieces)]
+def rotate_kernel(spots, rows, chips, *refs):
+    pieces = refs[: len(spots)]
+    kron_ref = refs[len(spots)]
     rotated_ref, whole_ref, sems = refs[-3:]
-    rows = pieces[0].shape[1]
+    states = whole_ref.shape[0]
     copies = []
-    for n, piece in enumerate(pieces):
-        chip, core = place(hops[n // 2], chips)
-        at = (chip * CORES + (core if n % 2 == 0 else 1 - core)) * rows
-        copies.append(
-            pltpu.make_async_copy(
-                piece.at[0 : whole_ref.shape[0]],
-                whole_ref.at[:, pl.ds(pl.multiple_of(at, TILE), rows), :],
-                sems.at[n],
-            )
-        )
+    bases = []
+    for n, ((hop, flip, offset), piece) in enumerate(zip(spots, pieces)):
+        chip, core = place(hop, chips)
+        at = pl.multiple_of((chip * CORES + (core if flip == 0 else 1 - core)) * rows + offset, TILE)
+        bases.append(at)
+        target = whole_ref.at[:, pl.ds(at, piece.shape[1]), :]
+        copies.append(pltpu.make_async_copy(piece.at[0:states], target, sems.at[n]))
         copies[-1].start()
-    for n, piece in enumerate(pieces):
-        chip, core = place(hops[n // 2], chips)
-        at = (chip * CORES + (core if n % 2 == 0 else 1 - core)) * rows
+    for at, piece in zip(bases, pieces):
         mix_sites(piece, kron_ref, rotated_ref, at, UNROLL)
     for copy in copies:
         copy.wait()
 
 
-def lefts_kernel(hops, chips, *refs):
-    count = CORES * len(hops)
+def lefts_kernel(spots, rows, chips, *refs):
+    count = len(spots)
     packed_ref = refs[count + 3]
     mixed_ref, rotated_ref, whole_ref, left_ref, sems = refs[-5:]
     terms, states, width, _ = rotated_ref.shape
     unpack_symmetric(packed_ref, left_ref)
-    rotate_kernel(hops, chips, *refs[: count + 1], rotated_ref, whole_ref, sems)
+    rotate_kernel(spots, rows, chips, *refs[: count + 1], rotated_ref, whole_ref, sems)
 
     def lefts(p, carry):
         for k in range(terms):
@@ -375,8 +376,8 @@
 
 
 def finish_kernel(vector_ref, residual_ref, *refs):
-    shares = refs[:-4]
-    ritz_hbm, energy_ref, ritz_ref, sems = refs[-4:]
+    shares = refs[:-2]
+    ritz_ref, energy_ref = refs[-2:]
     stat = summed([share[...] for share in shares])
     rayleigh = stat[0:1, :]
     res_sq = stat[1:2, :]
@@ -390,16 +391,8 @@
     coeff_norm = jnp.sqrt(coupling * coupling + coeff_new * coeff_new + epsilon)
     old = coupling / coeff_norm
     new = coeff_new / (coeff_norm * res_scale)
-    rows = vector_ref.shape[0]
-    copies = []
-    for n in range(0, rows, TILE):
-        part = pl.ds(n, TILE)
-        ritz_ref[part] = old[None] * vector_ref[part] + new[None] * residual_ref[part]
-        copies.append(pltpu.make_async_copy(ritz_ref.at[part], ritz_hbm.at[part], sems.at[n // TILE]))
-        copies[-1].start()
+    ritz_ref[...] = old[None] * vector_ref[...] + new[None] * residual_ref[...]
     energy_ref[0] = energy[0, 0]
-    for copy in copies:
-        copy.wait()
 
 
 def shards(wave_guess, left_env, right_env, site_ops, bond_rank):
@@ -435,18 +428,23 @@
     tile = jax.ShapeDtypeStruct((8, width), F32)
     half = width // 2
     packed_shape = jax.ShapeDtypeStruct((terms, width + TILE, half), BF16)
-    slabs = -(-(terms + 1) * TILE // rows)
-    x_own, norm_part, left_packed, right_packed, left = pl.pallas_call(
-        prepare_kernel,
+    starts = (0, rows - 2 * TILE, rows - TILE) if rows >= 4 * TILE else (0,)
+    lengths = [stop - start for start, stop in zip(starts, starts[1:] + (rows,))]
+    x_own, norm_part, left_packed, right_packed, left, *chunks = pl.pallas_call(
+        functools.partial(prepare_kernel, starts),
         out_shape=(
-            jax.ShapeDtypeStruct((states + slabs, rows, width), BF16),
+            jax.ShapeDtypeStruct((states, rows, width), BF16),
             tile,
             packed_shape,
             packed_shape,
             jax.ShapeDtypeStruct(left.shape, BF16),
+            *[
+                jax.ShapeDtypeStruct((states + (n == 0), length, width), BF16)
+                for n, length in enumerate(lengths)
+            ],
         ),
         in_specs=[smem] + [in_hbm] * 4,
-        out_specs=(vmem,) * 5,
+        out_specs=(vmem,) * (5 + len(lengths)),
         scratch_shapes=[
             pltpu.VMEM(guess.shape, F32),
             pltpu.VMEM(left.shape, BF16),
@@ -458,8 +456,9 @@
         name="prepare",
     )(bond_rank, *[pltpu.with_memory_space_constraint(a, pltpu.HBM) for a in (guess, left, right_env[0], site)])
 
-    x_hops = around(x_own)
-    pieces = [x_own, to_sibling(x_own)]
+    chunk_hops = [around(chunk) for chunk in chunks]
+    here_pieces = [x_own, to_sibling(x_own)]
+    here_spots = ((0, 0, 0), (0, 1, 0))
     lefts = around(left_packed)
     shift = [(i + 1, i) for i in range(segments - 1)]
     received = lax.ppermute(right_packed, "seg", shift)
@@ -477,7 +476,7 @@
             name="spread_site",
         )(block)
 
-    kron_own, _ = spread(x_own)
+    kron_own, _ = spread(chunks[0])
 
     whole = (states, width, width)
     whole_bf = jax.ShapeDtypeStruct(whole, BF16)
@@ -495,15 +494,44 @@
     chip_rotated = (terms, states, chip_rows, width)
     chip_cost = cost(3 * stage_flops * chip_rows / width, 8 * states * width * width)
     rotated_own = pl.pallas_call(
-        rotate_own_kernel,
+        functools.partial(rotate_own_kernel, here_spots, rows),
         out_shape=jax.ShapeDtypeStruct(chip_rotated, BF16),
         in_specs=[vmem] * 3,
         out_specs=vmem,
         compiler_params=params(),
         cost_estimate=chip_cost,
         name="rotate_own",
-    )(*pieces, kron_own)
-    received, rotated_own = lax.optimization_barrier((received, rotated_own))
+    )(*here_pieces, kron_own)
+    def there(hop, before):
+        spots = tuple(spot for spot in far_spots if spot[0] == hop)
+        pieces = [piece for spot, piece in zip(far_spots, far_pieces) if spot[0] == hop]
+        return pl.pallas_call(
+            functools.partial(there_kernel, spots, rows, chips),
+            out_shape=whole_f32,
+            in_specs=[vmem] * (len(pieces) + 4),
+            out_specs=vmem,
+            scratch_shapes=[pltpu.VMEM(chip_rotated, BF16)] + mix_scratch,
+            compiler_params=params(),
+            cost_estimate=chip_cost,
+            name="apply_rows_there",
+        )(*pieces, left, right, kron_own, before)
+
+    def rotate(kron):
+        return pl.pallas_call(
+            functools.partial(rotate_kernel, here_spots, rows, chips),
+            out_shape=(rotated_bf, whole_bf),
+            in_specs=[vmem] * 3,
+            out_specs=(vmem, vmem),
+            scratch_shapes=[pltpu.SemaphoreType.DMA((CORES,))],
+            compiler_params=params(),
+            cost_estimate=chip_cost,
+            name="rotate_here",
+        )(*here_pieces, kron)
+
+    firsts, rotated_own = lax.optimization_barrier((chunk_hops[0][1:], rotated_own))
+    kron, norm_far = spread(firsts[0])
+    turned = rotate(kron)
+    received, turned = lax.optimization_barrier((received, turned))
     packed = jnp.where(lax.axis_index("seg") == segments - 1, right_packed, received)
     rights = around(packed)
     partial, right = pl.pallas_call(
@@ -517,57 +545,39 @@
         name="apply_rows_here",
     )(rotated_own, left, packed)
 
-    def there(hop, before):
-        return pl.pallas_call(
-            functools.partial(there_kernel, hop, chips),
-            out_shape=whole_f32,
-            in_specs=[vmem] * 6,
-            out_specs=vmem,
-            scratch_shapes=[pltpu.VMEM(chip_rotated, BF16)] + mix_scratch,
-            compiler_params=params(),
-            cost_estimate=chip_cost,
-            name="apply_rows_there",
-        )(*pieces[2 * hop : 2 * hop + 2], left, right, kron_own, before)
-
-    def rotate(kron):
-        return pl.pallas_call(
-            functools.partial(rotate_kernel, hops[:1], chips),
-            out_shape=(rotated_bf, whole_bf),
-            in_specs=[vmem] * 3,
-            out_specs=(vmem, vmem),
-            scratch_shapes=[pltpu.SemaphoreType.DMA((CORES,))],
-            compiler_params=params(),
-            cost_estimate=chip_cost,
-            name="rotate_here",
-        )(*pieces[:CORES], kron)
-
-    crossed, partial = lax.optimization_barrier((x_hops[1:], partial))
-    for block in crossed:
-        pieces += [block, to_sibling(block)]
-    kron, norm_far = spread(crossed[0])
-    turned = rotate(kron)
+    far_pieces = []
+    far_spots = ()
+    for n, start in enumerate(starts):
+        if n == 0:
+            crossed = firsts
+        elif n + 1 < len(starts):
+            crossed, turned = lax.optimization_barrier((chunk_hops[n][1:], turned))
+        else:
+            crossed, partial = lax.optimization_barrier((chunk_hops[n][1:], partial))
+        for hop, block in zip(hops[1:], crossed):
+            far_pieces += [block, to_sibling(block)]
+            far_spots += ((hop, 0, start), (hop, 1, start))
     for hop in hops[1:]:
         partial = there(hop, partial)
-    far = pieces[CORES:]
     norms = [norm_part]
     for hop in hops[1:]:
         if hop > 1:
-            block, partial = lax.optimization_barrier((crossed[hop - 1], partial))
+            block, partial = lax.optimization_barrier((firsts[hop - 1], partial))
             kron, norm_far = spread(block)
             turned = rotate(kron)
         norms.append(norm_far)
         left_far, partial = lax.optimization_barrier((lefts[hop], partial))
         mixed, _, vector = pl.pallas_call(
-            functools.partial(lefts_kernel, hops[1:], chips),
+            functools.partial(lefts_kernel, far_spots, rows, chips),
             out_shape=(jax.ShapeDtypeStruct((states, width, terms * width), BF16), rotated_bf, whole_bf),
-            in_specs=[vmem] * (len(far) + 1) + [anywhere] * 2 + [vmem],
+            in_specs=[vmem] * (len(far_pieces) + 1) + [anywhere] * 2 + [vmem],
             out_specs=(vmem,) * 3,
-            scratch_shapes=[square, pltpu.SemaphoreType.DMA((len(far),))],
-            input_output_aliases={len(far) + 1: 1, len(far) + 2: 2},
+            scratch_shapes=[square, pltpu.SemaphoreType.DMA((len(far_pieces),))],
+            input_output_aliases={len(far_pieces) + 1: 1, len(far_pieces) + 2: 2},
             compiler_params=params(),
             cost_estimate=cost(stage_flops, 12 * states * width * width),
             name="received_lefts",
-        )(*far, kron, *turned, left_far)
+        )(*far_pieces, kron, *turned, left_far)
         last = hop == hops[-1]
         stats = norms if last else norms[:1]
         right_far = rights[hop]
@@ -633,8 +643,7 @@
         finish_kernel,
         out_shape=(local, jax.ShapeDtypeStruct((1,), F32)),
         in_specs=[vmem] * (2 + members),
-        out_specs=(anywhere, smem),
-        scratch_shapes=[pltpu.VMEM(guess.shape, F32), pltpu.SemaphoreType.DMA((rows // TILE,))],
+        out_specs=(vmem, smem),
         compiler_params=params(),
         cost_estimate=cost(3 * guess.size, 12 * guess.size),
         name="finish",

time: 50.7 us -> 47.1 us (0.929)
  waiting for transfers between devices: 13.5 us -> 7.66 us
  starting transfers between devices: 9.2 us -> 12 us
  Pallas kernels: 26.2 us -> 25.6 us
    ppermute x1, waiting for transfers between devices: 5.78 us -> 0.01 us  [shards(): received = lax.ppermute(right_packed, 'seg', shift)]
    ppermute x3 -> x5, starting transfers between devices: 4.62 us -> 6.78 us  [to_next_chip(): lax.ppermute(block, 'term', [(i, (i + CORES) % members) for i in range(me...]
    ppermute x5 -> x7, waiting for transfers between devices: 2.01 us -> 3.01 us  [to_sibling(): return lax.ppermute(block, 'term', [(i, i ^ 1) for i in range(members)])]
    ppermute x5 -> x7, starting transfers between devices: 1.23 us -> 2.02 us  [to_sibling(): return lax.ppermute(block, 'term', [(i, i ^ 1) for i in range(members)])]
    ppermute x3 -> x5, waiting for transfers between devices: 2.82 us -> 2.15 us  [to_next_chip(): lax.ppermute(block, 'term', [(i, (i + CORES) % members) for i in range(me...]
  transfers between devices with their start and end apart: 12 -> 16, of which waited for: 8 -> 6; matrix products, arithmetic and copies ran while one was open for 0% -> 0% of each run, Pallas kernels for 30% -> 32%
where the time goes in v7:
time: 47.1 us; the launch traced here: 46.9 us
  Pallas kernels  25.6 us (54%)
  starting transfers between devices  12 us (25%)
  waiting for transfers between devices  7.66 us (16%)
  between operations  1.6 us (3%)
    ppermute x5, starting transfers between devices, to_next_chip(): lax.ppermute(block, 'term', [(i, (i + CORES) % members) for i in range(me...  6.78 us
    pallas_call x1, Pallas kernels, shards(): pl.pallas_call(functools.partial(second_kernel, scale, members), out_shap...  6.1 us
    pallas_call x1, Pallas kernels, shards(): pl.pallas_call(functools.partial(lefts_kernel, far_spots, rows, chips), o...  3.48 us
    pallas_call x1, Pallas kernels, there(): pl.pallas_call(functools.partial(there_kernel, spots, rows, chips), out_s...  3.33 us
    ppermute x7, waiting for transfers between devices, to_sibling(): return lax.ppermute(block, 'term', [(i, i ^ 1) for i in range(members)])  3.01 us
    pallas_call x2, Pallas kernels, shards(): pl.pallas_call(functools.partial(rights_kernel, start, stop), out_shape=t...  3.01 us
    pallas_call x1, Pallas kernels, shards(): pl.pallas_call(functools.partial(here_kernel, chips), out_shape=(whole_f3...  2.51 us
    ppermute x3, waiting for transfers between devices, everyone(): lax.ppermute(block, 'term', [(i, i ^ bits) for i in range(members)])  2.49 us
  transfers between devices with their start and end apart: 16, of which 6 were waited for; matrix products, arithmetic and copies ran while one was open for 0% of the time, Pallas kernels for 32%

profile of v7, /device:TPU:0, one launch (start us, length us, event | category | flops | bytes accessed | tf_op | source)
XLA Modules:
  0.0 46.9 jit_solution(8930498708940171695)
XLA Ops:
  1.3 1.7 %prepare.1 = (bf16[16,64,256]{2,1,0:T(8,128)(2,1)S(1)}, f32[8,256]{1,0:T(8,128)S(1)}, bf16[3,272,128]{2,1,0:T(8,128)(2,1)S(1)}, bf16[3,272,128]{2,1,0:T(8,128)(2...) custom-call(s32[1]{0:T(128)S(6)} %copy.11.rank_ref, ...), custom_call_target="tpu_custom_call" | custom-call | flops 10485 | bytes 15728 | tf_op jit(solution)/shard_map/prepare/pallas_call | solution.py:433
  3.0 0.5 %collective-permute-start.1 = (bf16[16,64,256]{2,1,0:T(8,128)(2,1)S(1)}, bf16[16,64,256]{2,1,0:T(8,128)(2,1)S(1)}, u32[]{:S(2)}, u32[]{:S(2)}) collective-permute-start(bf16[16,64,256]{2,1,0:T(8,128)(2,1)S(1)} %get-tuple-element.41.refs_0_), channel_id=1, source_target_pairs={{0,1},{1,0},{2,3},{3,2},{4,5},{5,4},{6,7},{7,6},{8,9},{9,8},{10,11... | collective-permute-start | bytes 1572872 | tf_op jit(solution)/shard_map/ppermute | solution.py:411
  3.5 2.6 %collective-permute-start.2 = (bf16[17,32,256]{2,1,0:T(8,128)(2,1)S(1)}, bf16[17,32,256]{2,1,0:T(8,128)(2,1)S(1)}, u32[]{:S(2)}, u32[]{:S(2)}) collective-permute-start(bf16[17,32,256]{2,1,0:T(8,128)(2,1)S(1)} %get-tuple-element.42.chunk_ref), channel_id=1, source_target_pairs={{0,2},{1,3},{2,0},{3,1},{4,6},{5,7},{6,4},{7,5},{8,10},{9,11},{10,... | collective-permute-start | bytes 835592 | tf_op jit(solution)/shard_map/ppermute | solution.py:414
  6.1 1.3 %collective-permute-start = (bf16[3,272,128]{2,1,0:T(8,128)(2,1)S(1)}, bf16[3,272,128]{2,1,0:T(8,128)(2,1)S(1)}, u32[]{:S(2)}, u32[]{:S(2)}) collective-permute-start(bf16[3,272,128]{2,1,0:T(8,128)(2,1)S(1)} %get-tuple-element.40), channel_id=1, source_target_pairs={{4,0},{8,4},{12,8},{16,12},{20,16},{24,20},{28,24},{5,1},{9,5},{13... | collective-permute-start | bytes 626696 | tf_op jit(solution)/shard_map/ppermute | solution.py:464
  7.4 0.1 collective-permute-start.5
  7.5 2.0 %collective-permute-start.7 = (bf16[16,16,256]{2,1,0:T(8,128)(2,1)S(1)}, bf16[16,16,256]{2,1,0:T(8,128)(2,1)S(1)}, u32[]{:S(2)}, u32[]{:S(2)}) collective-permute-start(bf16[16,16,256]{2,1,0:T(8,128)(2,1)S(1)} %get-tuple-element.53), channel_id=1, source_target_pairs={{0,2},{1,3},{2,0},{3,1},{4,6},{5,7},{6,4},{7,5},{8,10},{9,11},{10,... | collective-permute-start | bytes 393224 | tf_op jit(solution)/shard_map/ppermute | solution.py:414
  9.5 0.9 %spread_site.2 = (bf16[768,256]{1,0:T(8,128)(2,1)S(1)}, f32[8,256]{1,0:T(8,128)}) custom-call(bf16[17,32,256]{2,1,0:T(8,128)(2,1)S(1)} %get-tuple-element.42.chunk_ref), custom_call_target="tpu_custom_call" | custom-call | flops 1006632 | bytes 3932 | tf_op jit(solution)/shard_map/spread_site/pallas_call | solution.py:469
  10.4 0.0 collective-permute-done.1.refs_1_
  10.4 0.1 collective-permute-start.9
  10.5 1.0 %rotate_own.1.rotated_ref = bf16[3,16,128,256]{3,2,1,0:T(8,128)(2,1)S(1)} custom-call(bf16[16,64,256]{2,1,0:T(8,128)(2,1)S(1)} %get-tuple-element.41.refs_0_, bf16[16,64,256]{2,1,0:T(8,128)(2,1)S(1)} %collective-permute-done.1.refs_1_, bf16[768,256]{1,0:T(8,128)(2,1)S(1)} %get-tuple-element.43.refs_2_.refs_8_.kron_ref), custom_call_target="tpu_custom_call" | custom-call | flops 24159192 | bytes 83886 | tf_op jit(solution)/shard_map/rotate_own/pallas_call | solution.py:496
  11.5 2.1 %collective-permute-done.2.chunk_ref.refs_0_ = bf16[17,32,256]{2,1,0:T(8,128)(2,1)S(1)} collective-permute-done((bf16[17,32,256]{2,1,0:T(8,128)(2,1)S(1)}, bf16[17,32,256]{2,1,0:T(8,128)(2,1)S(1)}, u32[]{:S(2)}, u32[]{:S(2)}) %collective-permute-start.2) | collective-permute-done | bytes 278560 | tf_op jit(solution)/shard_map/ppermute | solution.py:414
  13.6 0.0 collective-permute-start.4
  13.6 0.4 spread_site.3
  14.0 1.3 %rotate_here.1 = (bf16[3,16,256,256]{3,2,1,0:T(8,128)(2,1)S(1)}, bf16[16,256,256]{2,1,0:T(8,128)(2,1)S(1)}) custom-call(bf16[16,64,256]{2,1,0:T(8,128)(2,1)S(1)} %get-tuple-element.41.refs_0_, bf16[16,64,256]{2,1,0:T(8,128)(2,1)S(1)} %collective-permute-done.1.refs_1_, bf16[768,256]{1,0:T(8,128)(2,1)S(1)} %get-tuple-element.45.refs_2_.refs_6_), custom_call_target="tpu_custom_call" | custom-call | flops 24159192 | bytes 83886 | tf_op jit(solution)/shard_map/rotate_here/pallas_call | solution.py:520
  15.3 0.0 collective-permute-done
  15.4 2.0 %collective-permute-start.3 = (bf16[3,272,128]{2,1,0:T(8,128)(2,1)S(1)}, bf16[3,272,128]{2,1,0:T(8,128)(2,1)S(1)}, u32[]{:S(2)}, u32[]{:S(2)}) collective-permute-start(bf16[3,272,128]{2,1,0:T(8,128)(2,1)S(1)} %broadcast_select_fusion.packed_ref), channel_id=1, source_target_pairs={{0,2},{1,3},{2,0},{3,1},{4,6},{5,7},{6,4},{7,5},{8,10},{9,11},{10,... | collective-permute-start | bytes 626696 | tf_op jit(solution)/shard_map/ppermute | solution.py:414
  17.4 0.0 collective-permute-done.5.refs_2_
  17.4 0.2 collective-permute-start.6
  17.6 2.5 %apply_rows_here.1 = (f32[16,256,256]{2,1,0:T(8,128)S(1)}, bf16[3,256,256]{2,1,0:T(8,128)(2,1)S(1)}) custom-call(bf16[3,16,128,256]{3,2,1,0:T(8,128)(2,1)S(1)} %rotate_own.1.rotated_ref, bf16[3,256,256]{2,1,0:T(8,128)(2,1)S(1)} %get-tuple-element.55.left_ref.refs_6_, bf16[3,272,128]{2,1,0:T(8,128)(2,1)S(1)} %broadcast_select_fusion.packed_ref), custom_call_target="tpu_custom_call" | custom-call | flops 24159192 | bytes 83886 | tf_op jit(solution)/shard_map/apply_rows_here/pallas_call | solution.py:537
  20.1 0.0 collective-permute-done.7.refs_4_
  20.2 0.3 collective-permute-start.8
  20.5 0.0 collective-permute-done.6.refs_3_
  20.5 1.1 %collective-permute-done.8.refs_5_ = bf16[16,16,256]{2,1,0:T(8,128)(2,1)S(1)} collective-permute-done((bf16[16,16,256]{2,1,0:T(8,128)(2,1)S(1)}, bf16[16,16,256]{2,1,0:T(8,128)(2,1)S(1)}, u32[]{:S(2)}, u32[]{:S(2)}) %collective-permute-start.8) | collective-permute-done | bytes 131104 | tf_op jit(solution)/shard_map/ppermute | solution.py:411
  21.6 0.0 collective-permute-done.4.refs_1_
  21.6 3.3 %apply_rows_there.1.before_ref = f32[16,256,256]{2,1,0:T(8,128)S(1)} custom-call(bf16[17,32,256]{2,1,0:T(8,128)(2,1)S(1)} %collective-permute-done.2.chunk_ref.refs_0_, bf16[17,32,256]{2,1,0:T(8,128)(2,1)S(1)} %collective-permute-done.4.refs_1_, bf16[16,16,256]{2,1,0:T(8,128)(2,1)S(1)} %collective-permute-done.5.refs_2_, ...), custom_call_target="tpu_custom_call" | custom-call | flops 24159192 | bytes 83886 | tf_op jit(solution)/shard_map/apply_rows_there/pallas_call | solution.py:508
  24.9 0.0 collective-permute-done.9.refs_9_
  24.9 3.5 %received_lefts.1 = (bf16[16,256,768]{2,1,0:T(8,128)(2,1)S(1)}, bf16[3,16,256,256]{3,2,1,0:T(8,128)(2,1)S(1)}, bf16[16,256,256]{2,1,0:T(8,128)(2,1)S(1)}) custom-call(bf16[17,32,256]{2,1,0:T(8,128)(2,1)S(1)} %collective-permute-done.2.chunk_ref.refs_0_, ...), custom_call_target="tpu_custom_call", output_to_operand_aliasing={{1}: (7, {}), {2}: (8, {})} | custom-call | flops 16106127 | bytes 125829 | tf_op jit(solution)/shard_map/received_lefts/pallas_call | solution.py:570
  28.4 0.0 collective-permute-done.3.packed_ref
  28.4 1.5 %received_rights.2 = (bf16[8,256,256]{2,1,0:T(8,128)(2,1)S(1)}, f32[8,256]{1,0:T(8,128)S(1)}, bf16[3,256,256]{2,1,0:T(8,128)(2,1)S(1)}) custom-call(bf16[3,272,128]{2,1,0:T(8,128)(2,1)S(1)} %collective-permute-done.3.packed_ref, bf16[16,256,768]{2,1,0:T(8,128)(2,1)S(1)} %get-tuple-element.64.mixed_ref, ...), custom_call_target="tpu_custom_call" | custom-call | flops 8053063 | bytes 125829 | tf_op jit(solution)/shard_map/received_rights/pallas_call | solution.py:588
  29.9 0.3 collective-permute-start.11
  30.3 1.5 %received_rights.3 = (bf16[8,256,256]{2,1,0:T(8,128)(2,1)S(1)}, f32[8,256]{1,0:T(8,128)S(1)}) custom-call(bf16[3,256,256]{2,1,0:T(8,128)(2,1)S(1)} %get-tuple-element.69.packed_ref, bf16[16,256,768]{2,1,0:T(8,128)(2,1)S(1)} %get-tuple-element.64.mixed_ref, bf16[16,256,256]{2,1,0:T(8,128)(2,1)S(1)} %get-tuple-element.65.whole_ref, ...), custom_call_target="tpu_custom_call" | custom-call | flops 8053063 | bytes 125829 | tf_op jit(solution)/shard_map/received_rights/pallas_call | solution.py:588
  31.8 0.3 collective-permute-start.12
  32.1 0.3 collective-permute-start.10
  32.4 0.3 collective-permute-done.11.other_ref
  32.6 0.2 add_low_half.1.refs_0_.low_ref
  32.9 0.0 copy-start
  32.9 1.7 %collective-permute-done.10.theirs_ref = f32[8,256]{1,0:T(8,128)S(1)} collective-permute-done((f32[8,256]{1,0:T(8,128)S(1)}, f32[8,256]{1,0:T(8,128)S(1)}, u32[]{:S(2)}, u32[]{:S(2)}) %collective-permute-start.10) | collective-permute-done | bytes 8224 | tf_op jit(solution)/shard_map/ppermute | solution.py:411
  34.5 0.0 collective-permute-done.12.refs_2_.high_other_ref
  34.5 6.1 %apply_residual.1.refs_0_ = f32[8,256]{1,0:T(8,128)S(1)} custom-call(s32[1]{0:T(128)S(6)} %copy.11.rank_ref, f32[8,256]{1,0:T(8,128)S(1)} %get-tuple-element.71.mine_ref, f32[8,256]{1,0:T(8,128)S(1)} %collective-permute-done.10.theirs_ref, f32[8,256,256]{2,1,0:T(8,128)S(1)} %add_low_half.1.refs_0_.low_ref, ...), custom_call_target="tpu_custom_call" | custom-call | flops 48318384 | bytes 62914 | tf_op jit(solution)/shard_map/apply_residual/pallas_call | solution.py:615
  40.7 1.2 %collective-permute-start.15 = (f32[8,256]{1,0:T(8,128)S(1)}, f32[8,256]{1,0:T(8,128)S(1)}, u32[]{:S(2)}, u32[]{:S(2)}) collective-permute-start(f32[8,256]{1,0:T(8,128)S(1)} %apply_residual.1.refs_0_), channel_id=1, source_target_pairs={{0,3},{1,2},{2,1},{3,0},{4,7},{5,6},{6,5},{7,4},{8,11},{9,10},{10,... | collective-permute-start | bytes 24584 | tf_op jit(solution)/shard_map/ppermute | solution.py:424
  41.8 0.7 %collective-permute-start.14 = (f32[8,256]{1,0:T(8,128)S(1)}, f32[8,256]{1,0:T(8,128)S(1)}, u32[]{:S(2)}, u32[]{:S(2)}) collective-permute-start(f32[8,256]{1,0:T(8,128)S(1)} %apply_residual.1.refs_0_), channel_id=1, source_target_pairs={{0,2},{1,3},{2,0},{3,1},{4,6},{5,7},{6,4},{7,5},{8,10},{9,11},{10,... | collective-permute-start | bytes 24584 | tf_op jit(solution)/shard_map/ppermute | solution.py:424
  42.6 0.0 collective-permute-start.13
  42.6 0.0 copy-done
  42.6 0.4 own_rows.1
  43.0 0.8 %collective-permute-done.15.refs_3_ = f32[8,256]{1,0:T(8,128)S(1)} collective-permute-done((f32[8,256]{1,0:T(8,128)S(1)}, f32[8,256]{1,0:T(8,128)S(1)}, u32[]{:S(2)}, u32[]{:S(2)}) %collective-permute-start.15) | collective-permute-done | bytes 8224 | tf_op jit(solution)/shard_map/ppermute | solution.py:424
  43.8 1.7 %collective-permute-done.14.refs_2_ = f32[8,256]{1,0:T(8,128)S(1)} collective-permute-done((f32[8,256]{1,0:T(8,128)S(1)}, f32[8,256]{1,0:T(8,128)S(1)}, u32[]{:S(2)}, u32[]{:S(2)}) %collective-permute-start.14) | collective-permute-done | bytes 8224 | tf_op jit(solution)/shard_map/ppermute | solution.py:424
  45.5 0.0 collective-permute-done.13.refs_1_
  45.5 1.3 %finish.1 = (f32[64,16,256]{2,1,0:T(8,128)}, f32[1]{0:T(128)}) custom-call(f32[64,16,256]{2,1,0:T(8,128)S(1)} %get-tuple-element.74.vector_ref, f32[64,16,256]{2,1,0:T(8,128)S(1)} %get-tuple-element.75.residual_ref, f32[8,256]{1,0:T(8,128)S(1)} %apply_residual.1.refs_0_, f32[8,256]{1,0:T(8,128)S(1)} %collective-permute-done.13.refs_1_, ...), custom_call_target="tpu_custom_call" | custom-call | flops 7864 | bytes 31457 | tf_op jit(solution)/shard_map/finish/pallas_call | solution.py:642
  (1 shorter events, 0.0 us)
Async XLA Ops:
  3.0 7.4 %collective-permute-start.1 = (bf16[16,64,256]{2,1,0:T(8,128)(2,1)S(1)}, bf16[16,64,256]{2,1,0:T(8,128)(2,1)S(1)}, u32[]{:S(2)}, u32[]{:S(2)}) collective-permute-start(bf16[16,64,256]{2,1,0:T(8,128)(2,1)S(1)} %get-tuple-element.41.refs_0_), channel_id=1, source_target_pairs={{0,1},{1,0},{2,3},{3,2},{4,5},{5,4},{6,7},{7,6},{8,9},{9,8},{10,11... | collective-permute-start | bytes 1572872 | tf_op jit(solution)/shard_map/ppermute | solution.py:411
  3.5 10.1 %collective-permute-start.2 = (bf16[17,32,256]{2,1,0:T(8,128)(2,1)S(1)}, bf16[17,32,256]{2,1,0:T(8,128)(2,1)S(1)}, u32[]{:S(2)}, u32[]{:S(2)}) collective-permute-start(bf16[17,32,256]{2,1,0:T(8,128)(2,1)S(1)} %get-tuple-element.42.chunk_ref), channel_id=1, source_target_pairs={{0,2},{1,3},{2,0},{3,1},{4,6},{5,7},{6,4},{7,5},{8,10},{9,11},{10,... | collective-permute-start | bytes 835592 | tf_op jit(solution)/shard_map/ppermute | solution.py:414
  6.1 9.2 %collective-permute-start = (bf16[3,272,128]{2,1,0:T(8,128)(2,1)S(1)}, bf16[3,272,128]{2,1,0:T(8,128)(2,1)S(1)}, u32[]{:S(2)}, u32[]{:S(2)}) collective-permute-start(bf16[3,272,128]{2,1,0:T(8,128)(2,1)S(1)} %get-tuple-element.40), channel_id=1, source_target_pairs={{4,0},{8,4},{12,8},{16,12},{20,16},{24,20},{28,24},{5,1},{9,5},{13... | collective-permute-start | bytes 626696 | tf_op jit(solution)/shard_map/ppermute | solution.py:464
  7.4 10.0 %collective-permute-start.5 = (bf16[16,16,256]{2,1,0:T(8,128)(2,1)S(1)}, bf16[16,16,256]{2,1,0:T(8,128)(2,1)S(1)}, u32[]{:S(2)}, u32[]{:S(2)}) collective-permute-start(bf16[16,16,256]{2,1,0:T(8,128)(2,1)S(1)} %get-tuple-element.49), channel_id=1, source_target_pairs={{0,2},{1,3},{2,0},{3,1},{4,6},{5,7},{6,4},{7,5},{8,10},{9,11},{10,... | collective-permute-start | bytes 393224 | tf_op jit(solution)/shard_map/ppermute | solution.py:414
  7.5 12.6 %collective-permute-start.7 = (bf16[16,16,256]{2,1,0:T(8,128)(2,1)S(1)}, bf16[16,16,256]{2,1,0:T(8,128)(2,1)S(1)}, u32[]{:S(2)}, u32[]{:S(2)}) collective-permute-start(bf16[16,16,256]{2,1,0:T(8,128)(2,1)S(1)} %get-tuple-element.53), channel_id=1, source_target_pairs={{0,2},{1,3},{2,0},{3,1},{4,6},{5,7},{6,4},{7,5},{8,10},{9,11},{10,... | collective-permute-start | bytes 393224 | tf_op jit(solution)/shard_map/ppermute | solution.py:414
  10.4 14.5 %collective-permute-start.9 = (bf16[3,272,128]{2,1,0:T(8,128)(2,1)S(1)}, bf16[3,272,128]{2,1,0:T(8,128)(2,1)S(1)}, u32[]{:S(2)}, u32[]{:S(2)}) collective-permute-start(bf16[3,272,128]{2,1,0:T(8,128)(2,1)S(1)} %get-tuple-element.60), channel_id=1, source_target_pairs={{0,2},{1,3},{2,0},{3,1},{4,6},{5,7},{6,4},{7,5},{8,10},{9,11},{10,... | collective-permute-start | bytes 626696 | tf_op jit(solution)/shard_map/ppermute | solution.py:414
  13.6 7.9 %collective-permute-start.4 = (bf16[17,32,256]{2,1,0:T(8,128)(2,1)S(1)}, bf16[17,32,256]{2,1,0:T(8,128)(2,1)S(1)}, u32[]{:S(2)}, u32[]{:S(2)}) collective-permute-start(bf16[17,32,256]{2,1,0:T(8,128)(2,1)S(1)} %collective-permute-done.2.chunk_ref.refs_0_), channel_id=1, source_target_pairs={{0,1},{1,0},{2,3},{3,2},{4,5},{5,4},{6,7},{7,6},{8,9},{9,8},{10,11... | collective-permute-start | bytes 835592 | tf_op jit(solution)/shard_map/ppermute | solution.py:411
  15.4 13.0 %collective-permute-start.3 = (bf16[3,272,128]{2,1,0:T(8,128)(2,1)S(1)}, bf16[3,272,128]{2,1,0:T(8,128)(2,1)S(1)}, u32[]{:S(2)}, u32[]{:S(2)}) collective-permute-start(bf16[3,272,128]{2,1,0:T(8,128)(2,1)S(1)} %broadcast_select_fusion.packed_ref), channel_id=1, source_target_pairs={{0,2},{1,3},{2,0},{3,1},{4,6},{5,7},{6,4},{7,5},{8,10},{9,11},{10,... | collective-permute-start | bytes 626696 | tf_op jit(solution)/shard_map/ppermute | solution.py:414
  17.4 3.1 %collective-permute-start.6 = (bf16[16,16,256]{2,1,0:T(8,128)(2,1)S(1)}, bf16[16,16,256]{2,1,0:T(8,128)(2,1)S(1)}, u32[]{:S(2)}, u32[]{:S(2)}) collective-permute-start(bf16[16,16,256]{2,1,0:T(8,128)(2,1)S(1)} %collective-permute-done.5.refs_2_), channel_id=1, source_target_pairs={{0,1},{1,0},{2,3},{3,2},{4,5},{5,4},{6,7},{7,6},{8,9},{9,8},{10,11... | collective-permute-start | bytes 393224 | tf_op jit(solution)/shard_map/ppermute | solution.py:411
  20.2 1.4 %collective-permute-start.8 = (bf16[16,16,256]{2,1,0:T(8,128)(2,1)S(1)}, bf16[16,16,256]{2,1,0:T(8,128)(2,1)S(1)}, u32[]{:S(2)}, u32[]{:S(2)}) collective-permute-start(bf16[16,16,256]{2,1,0:T(8,128)(2,1)S(1)} %collective-permute-done.7.refs_4_), channel_id=1, source_target_pairs={{0,1},{1,0},{2,3},{3,2},{4,5},{5,4},{6,7},{7,6},{8,9},{9,8},{10,11... | collective-permute-start | bytes 393224 | tf_op jit(solution)/shard_map/ppermute | solution.py:411
  29.9 2.7 %collective-permute-start.11 = (bf16[8,256,256]{2,1,0:T(8,128)(2,1)S(1)}, bf16[8,256,256]{2,1,0:T(8,128)(2,1)S(1)}, u32[]{:S(2)}, u32[]{:S(2)}) collective-permute-start(bf16[8,256,256]{2,1,0:T(8,128)(2,1)S(1)} %get-tuple-element.72.mine_ref), channel_id=1, source_target_pairs={{0,1},{1,0},{2,3},{3,2},{4,5},{5,4},{6,7},{7,6},{8,9},{9,8},{10,11... | collective-permute-start | bytes 3145736 | tf_op jit(solution)/shard_map/ppermute | solution.py:411
  31.8 2.7 %collective-permute-start.12 = (bf16[8,256,256]{2,1,0:T(8,128)(2,1)S(1)}, bf16[8,256,256]{2,1,0:T(8,128)(2,1)S(1)}, u32[]{:S(2)}, u32[]{:S(2)}) collective-permute-start(bf16[8,256,256]{2,1,0:T(8,128)(2,1)S(1)} %get-tuple-element.73.refs_1_.high_ref), channel_id=1, source_target_pairs={{0,1},{1,0},{2,3},{3,2},{4,5},{5,4},{6,7},{7,6},{8,9},{9,8},{10,11... | collective-permute-start | bytes 3145736 | tf_op jit(solution)/shard_map/ppermute | solution.py:411
  32.1 2.4 %collective-permute-start.10 = (f32[8,256]{1,0:T(8,128)S(1)}, f32[8,256]{1,0:T(8,128)S(1)}, u32[]{:S(2)}, u32[]{:S(2)}) collective-permute-start(f32[8,256]{1,0:T(8,128)S(1)} %get-tuple-element.71.mine_ref), channel_id=1, source_target_pairs={{0,1},{1,0},{2,3},{3,2},{4,5},{5,4},{6,7},{7,6},{8,9},{9,8},{10,11... | collective-permute-start | bytes 24584 | tf_op jit(solution)/shard_map/ppermute | solution.py:411
  32.9 9.7 %copy-start = (f32[1,64,16,256]{3,2,1,0:T(8,128)S(1)}, f32[1,64,16,256]{3,2,1,0:T(8,128)}, u32[]{:S(2)}) copy-start(f32[1,64,16,256]{3,2,1,0:T(8,128)} %param.5) | copy-start | bytes 3145732
  40.7 3.1 %collective-permute-start.15 = (f32[8,256]{1,0:T(8,128)S(1)}, f32[8,256]{1,0:T(8,128)S(1)}, u32[]{:S(2)}, u32[]{:S(2)}) collective-permute-start(f32[8,256]{1,0:T(8,128)S(1)} %apply_residual.1.refs_0_), channel_id=1, source_target_pairs={{0,3},{1,2},{2,1},{3,0},{4,7},{5,6},{6,5},{7,4},{8,11},{9,10},{10,... | collective-permute-start | bytes 24584 | tf_op jit(solution)/shard_map/ppermute | solution.py:424
  41.8 3.7 %collective-permute-start.14 = (f32[8,256]{1,0:T(8,128)S(1)}, f32[8,256]{1,0:T(8,128)S(1)}, u32[]{:S(2)}, u32[]{:S(2)}) collective-permute-start(f32[8,256]{1,0:T(8,128)S(1)} %apply_residual.1.refs_0_), channel_id=1, source_target_pairs={{0,2},{1,3},{2,0},{3,1},{4,6},{5,7},{6,4},{7,5},{8,10},{9,11},{10,... | collective-permute-start | bytes 24584 | tf_op jit(solution)/shard_map/ppermute | solution.py:424
  42.6 2.9 %collective-permute-start.13 = (f32[8,256]{1,0:T(8,128)S(1)}, f32[8,256]{1,0:T(8,128)S(1)}, u32[]{:S(2)}, u32[]{:S(2)}) collective-permute-start(f32[8,256]{1,0:T(8,128)S(1)} %apply_residual.1.refs_0_), channel_id=1, source_target_pairs={{0,1},{1,0},{2,3},{3,2},{4,5},{5,4},{6,7},{7,6},{8,9},{9,8},{10,11... | collective-permute-start | bytes 24584 | tf_op jit(solution)/shard_map/ppermute | solution.py:424

commit v8 on v7

--- a/solution.py
+++ b/solution.py
@@ -11,7 +11,7 @@
 CORES = 2
 TILE = 16
 UNROLL = 8
-GROUP = 4
+GROUP = 8
 VMEM_LIMIT = 20 * 1024 * 1024
 F32 = jnp.float32
 BF16 = jnp.bfloat16
@@ -28,10 +28,6 @@
 
 def cost(flops, moved):
     return pl.CostEstimate(flops=int(flops) // 100, bytes_accessed=int(moved) // 100, transcendentals=0)
-
-
-def keep_row(rank, width):
-    return (lax.broadcasted_iota(jnp.int32, (1, width), 1) < rank).astype(F32)
 
 
 def fold(values, width):
@@ -47,6 +43,7 @@
     site_in,
     x_ref,
     norm_ref,
+    keep_ref,
     left_packed_ref,
     right_packed_ref,
     left_ref,
@@ -66,7 +63,10 @@
     ]
     for copy in copies:
         copy.start()
-    keep = keep_row(rank_ref[0], width)[None]
+    column = lax.broadcasted_iota(jnp.int32, (1, width), 1)
+    keep = (column < rank_ref[...]).astype(F32)
+    keep_ref[...] = jnp.broadcast_to(keep, keep_ref.shape)
+    keep = keep[None]
     squares = jnp.zeros((8, width), F32)
     for n, part in enumerate(parts):
         copies[n].wait()
@@ -185,49 +185,60 @@
     return chip, me % CORES
 
 
-def rotate_own_kernel(spots, rows, *refs):
-    pieces = refs[: len(spots)]
-    kron_ref, rotated_ref = refs[len(spots) :]
+def mix_pieces(spots, rows, pieces, kron_ref, rotated_ref):
     _, core = place(0, 1)
     for (_, flip, offset), piece in zip(spots, pieces):
         at = (core if flip == 0 else 1 - core) * rows + offset
         mix_sites(piece, kron_ref, rotated_ref, at, UNROLL)
 
 
-def turn_and_mix(chip, left_ref, right_ref, rotated_ref, before_ref, out_ref, turned_ref, columns_ref):
+def rotate_own_kernel(spots, rows, chips, *refs):
+    pieces = refs[: len(spots)]
+    kron_ref, left_ref, rotated_ref, columns_ref = refs[len(spots) :]
     terms, states, chip_rows, width = rotated_ref.shape
-    at = pl.multiple_of(chip * chip_rows, TILE)
-    columns = jnp.concatenate([left_ref[k, pl.ds(at, chip_rows), :] for k in range(terms)], axis=0)
-    columns_ref[...] = columns.astype(F32).T.astype(BF16)
+    mix_pieces(spots, rows, pieces, kron_ref, rotated_ref)
+    blocks = []
+    for hop in range(chips):
+        chip, _ = place(hop, chips)
+        at = pl.multiple_of(chip * chip_rows, TILE)
+        blocks += [left_ref[k, pl.ds(at, chip_rows), :] for k in range(terms)]
+    columns_ref[...] = jnp.concatenate(blocks, axis=0).astype(F32).T.astype(BF16)
+
+
+def turn(right_ref, rotated_ref, turned_ref):
+    terms, states, chip_rows, width = rotated_ref.shape
     for k in range(terms):
         for n in range(0, states, 8):
             source = rotated_ref[k, n : n + 8].reshape(8 * chip_rows, width)
             turned = jnp.dot(source, right_ref[k], preferred_element_type=F32).astype(BF16)
             turned_ref[n : n + 8, k * chip_rows : (k + 1) * chip_rows, :] = turned.reshape(8, chip_rows, width)
 
+
+def here_kernel(rotated_ref, packed_ref, turned_ref, right_ref):
+    unpack_symmetric(packed_ref, right_ref)
+    turn(right_ref, rotated_ref, turned_ref)
+
+
+def there_kernel(spots, rows, *refs):
+    count = len(spots)
+    right_ref, kron_ref, turned_ref, rotated_ref = refs[count:]
+    mix_pieces(spots, rows, refs[:count], kron_ref, rotated_ref)
+    turn(right_ref, rotated_ref, turned_ref)
+
+
+def last_kernel(spots, rows, *refs):
+    count = len(spots)
+    right_ref, kron_ref, columns_ref = refs[count : count + 3]
+    out_ref, rotated_ref, turned_ref = refs[-3:]
+    there_kernel(spots, rows, *refs[:count], right_ref, kron_ref, turned_ref, rotated_ref)
+    blocks = list(refs[count + 3 : -3]) + [turned_ref]
+
     def lefts(p, carry):
-        image = jnp.dot(columns_ref[...], turned_ref[p], preferred_element_type=F32)
-        if before_ref is not None:
-            image = before_ref[p] + image
-        out_ref[p] = image
+        stack = jnp.concatenate([block[p] for block in blocks], axis=0)
+        out_ref[p] = jnp.dot(columns_ref[...], stack, preferred_element_type=F32)
         return carry
 
-    lax.fori_loop(0, states, lefts, 0, unroll=UNROLL)
-
-
-def here_kernel(chips, rotated_ref, left_ref, packed_ref, out_ref, right_ref, turned_ref, columns_ref):
-    chip, _ = place(0, chips)
-    unpack_symmetric(packed_ref, right_ref)
-    turn_and_mix(chip, left_ref, right_ref, rotated_ref, None, out_ref, turned_ref, columns_ref)
-
-
-def there_kernel(spots, rows, chips, *refs):
-    count = len(spots)
-    left_ref, right_ref, kron_ref, before_ref, out_ref = refs[count : count + 5]
-    rotated_ref, turned_ref, columns_ref = refs[count + 5 :]
-    chip, _ = place(spots[0][0], chips)
-    rotate_own_kernel(spots, rows, *refs[:count], kron_ref, rotated_ref)
-    turn_and_mix(chip, left_ref, right_ref, rotated_ref, before_ref, out_ref, turned_ref, columns_ref)
+    lax.fori_loop(0, out_ref.shape[0], lefts, 0, unroll=UNROLL)
 
 
 def rotate_kernel(spots, rows, chips, *refs):
@@ -295,10 +306,10 @@
     stat_ref[0:1, :] = product if start == 0 else stats[0][0:1, :] + product
 
 
-def scales(rank_ref, mine_ref, theirs_ref, scale, width):
+def scales(keep_ref, mine_ref, theirs_ref, scale, width):
     inverse = lax.rsqrt((mine_ref[1:2, :] + theirs_ref[1:2, :]) * scale + epsilon)
     rayleigh = (mine_ref[0:1, :] + theirs_ref[0:1, :]) * (inverse * inverse * scale)
-    return inverse, rayleigh, keep_row(rank_ref[0], width) * inverse
+    return inverse, rayleigh, keep_ref[0:1, :] * inverse
 
 
 def add_kernel(mine_ref, other_ref, sum_ref):
@@ -308,7 +319,7 @@
 def second_kernel(
     scale,
     members,
-    rank_ref,
+    keep_ref,
     mine_ref,
     theirs_ref,
     low_ref,
@@ -324,7 +335,7 @@
     mixed_ref,
 ):
     terms, states, width, _ = rotated_ref.shape
-    inverse, rayleigh, row_scale = scales(rank_ref, mine_ref, theirs_ref, scale, width)
+    inverse, rayleigh, row_scale = scales(keep_ref, mine_ref, theirs_ref, scale, width)
     back = rayleigh * inverse
 
     square = jnp.zeros((8, width), F32)
@@ -363,10 +374,10 @@
     out_ref[3:8, :] = jnp.zeros((5, width), F32)
 
 
-def own_rows_kernel(scale, rank_ref, guess_ref, mine_ref, theirs_ref, *refs):
+def own_rows_kernel(scale, keep_ref, guess_ref, mine_ref, theirs_ref, *refs):
     low_ref, high_ref, high_other_ref, vector_ref, residual_ref = refs
     rows, states, width = guess_ref.shape
-    inverse, rayleigh, row_scale = scales(rank_ref, mine_ref, theirs_ref, scale, width)
+    inverse, rayleigh, row_scale = scales(keep_ref, mine_ref, theirs_ref, scale, width)
     own = pl.ds(pl.multiple_of(lax.axis_index("term") * rows, TILE), rows)
     vector = guess_ref[...] * row_scale[None]
     vector_ref[...] = vector
@@ -430,10 +441,11 @@
     packed_shape = jax.ShapeDtypeStruct((terms, width + TILE, half), BF16)
     starts = (0, rows - 2 * TILE, rows - TILE) if rows >= 4 * TILE else (0,)
     lengths = [stop - start for start, stop in zip(starts, starts[1:] + (rows,))]
-    x_own, norm_part, left_packed, right_packed, left, *chunks = pl.pallas_call(
+    x_own, norm_part, keep, left_packed, right_packed, left, *chunks = pl.pallas_call(
         functools.partial(prepare_kernel, starts),
         out_shape=(
             jax.ShapeDtypeStruct((states, rows, width), BF16),
+            tile,
             tile,
             packed_shape,
             packed_shape,
@@ -443,8 +455,8 @@
                 for n, length in enumerate(lengths)
             ],
         ),
-        in_specs=[smem] + [in_hbm] * 4,
-        out_specs=(vmem,) * (5 + len(lengths)),
+        in_specs=[vmem] + [in_hbm] * 4,
+        out_specs=(vmem,) * (6 + len(lengths)),
         scratch_shapes=[
             pltpu.VMEM(guess.shape, F32),
             pltpu.VMEM(left.shape, BF16),
@@ -454,7 +466,7 @@
         compiler_params=params(),
         cost_estimate=cost(4 * guess.size, 6 * guess.size),
         name="prepare",
-    )(bond_rank, *[pltpu.with_memory_space_constraint(a, pltpu.HBM) for a in (guess, left, right_env[0], site)])
+    )(bond_rank.reshape(1, 1), *[pltpu.with_memory_space_constraint(a, pltpu.HBM) for a in (guess, left, right_env[0], site)])
 
     chunk_hops = [around(chunk) for chunk in chunks]
     here_pieces = [x_own, to_sibling(x_own)]
@@ -487,34 +499,37 @@
     chip_rows = CORES * rows
     stage_flops = 2 * terms * states * width * width * width
 
-    mix_scratch = [
-        pltpu.VMEM((states, terms * chip_rows, width), BF16),
-        pltpu.VMEM((width, terms * chip_rows), BF16),
-    ]
     chip_rotated = (terms, states, chip_rows, width)
+    chip_turned = jax.ShapeDtypeStruct((states, terms * chip_rows, width), BF16)
     chip_cost = cost(3 * stage_flops * chip_rows / width, 8 * states * width * width)
-    rotated_own = pl.pallas_call(
-        functools.partial(rotate_own_kernel, here_spots, rows),
-        out_shape=jax.ShapeDtypeStruct(chip_rotated, BF16),
-        in_specs=[vmem] * 3,
-        out_specs=vmem,
+    rotated_own, columns = pl.pallas_call(
+        functools.partial(rotate_own_kernel, here_spots, rows, chips),
+        out_shape=(
+            jax.ShapeDtypeStruct(chip_rotated, BF16),
+            jax.ShapeDtypeStruct((width, terms * width), BF16),
+        ),
+        in_specs=[vmem] * 4,
+        out_specs=(vmem, vmem),
         compiler_params=params(),
         cost_estimate=chip_cost,
         name="rotate_own",
-    )(*here_pieces, kron_own)
+    )(*here_pieces, kron_own, left)
+
     def there(hop, before):
         spots = tuple(spot for spot in far_spots if spot[0] == hop)
         pieces = [piece for spot, piece in zip(far_spots, far_pieces) if spot[0] == hop]
+        last = hop == hops[-1]
         return pl.pallas_call(
-            functools.partial(there_kernel, spots, rows, chips),
-            out_shape=whole_f32,
-            in_specs=[vmem] * (len(pieces) + 4),
+            functools.partial(last_kernel if last else there_kernel, spots, rows),
+            out_shape=whole_f32 if last else chip_turned,
+            in_specs=[vmem] * (len(pieces) + 2 + (1 + len(before) if last else 0)),
             out_specs=vmem,
-            scratch_shapes=[pltpu.VMEM(chip_rotated, BF16)] + mix_scratch,
+            scratch_shapes=[pltpu.VMEM(chip_rotated, BF16)]
+            + ([pltpu.VMEM(chip_turned.shape, BF16)] if last else []),
             compiler_params=params(),
             cost_estimate=chip_cost,
             name="apply_rows_there",
-        )(*pieces, left, right, kron_own, before)
+        )(*pieces, right, kron_own, *([columns] + before if last else []))
 
     def rotate(kron):
         return pl.pallas_call(
@@ -534,17 +549,15 @@
     received, turned = lax.optimization_barrier((received, turned))
     packed = jnp.where(lax.axis_index("seg") == segments - 1, right_packed, received)
     rights = around(packed)
-    partial, right = pl.pallas_call(
-        functools.partial(here_kernel, chips),
-        out_shape=(whole_f32, jax.ShapeDtypeStruct(left.shape, BF16)),
-        in_specs=[vmem] * 3,
+    turned_own, right = pl.pallas_call(
+        here_kernel,
+        out_shape=(chip_turned, jax.ShapeDtypeStruct(left.shape, BF16)),
+        in_specs=[vmem] * 2,
         out_specs=(vmem, vmem),
-        scratch_shapes=mix_scratch,
         compiler_params=params(),
         cost_estimate=chip_cost,
         name="apply_rows_here",
-    )(rotated_own, left, packed)
-
+    )(rotated_own, packed)
     far_pieces = []
     far_spots = ()
     for n, start in enumerate(starts):
@@ -553,12 +566,14 @@
         elif n + 1 < len(starts):
             crossed, turned = lax.optimization_barrier((chunk_hops[n][1:], turned))
         else:
-            crossed, partial = lax.optimization_barrier((chunk_hops[n][1:], partial))
+            crossed, turned_own = lax.optimization_barrier((chunk_hops[n][1:], turned_own))
         for hop, block in zip(hops[1:], crossed):
             far_pieces += [block, to_sibling(block)]
             far_spots += ((hop, 0, start), (hop, 1, start))
+    parts = [turned_own]
     for hop in hops[1:]:
-        partial = there(hop, partial)
+        parts.append(there(hop, parts))
+    partial = parts[-1]
     norms = [norm_part]
     for hop in hops[1:]:
         if hop > 1:
@@ -615,7 +630,7 @@
     share = pl.pallas_call(
         functools.partial(second_kernel, scale, members),
         out_shape=tile,
-        in_specs=[smem] + [vmem] * 9,
+        in_specs=[vmem] * 10,
         out_specs=vmem,
         scratch_shapes=[
             pltpu.VMEM(whole, BF16),
@@ -625,19 +640,19 @@
         compiler_params=params(),
         cost_estimate=cost(3 * stage_flops, 6 * states * width * width),
         name="apply_residual",
-    )(bond_rank, stat, stat_other, *halves, vector, left, right, kron_own)
+    )(keep, stat, stat_other, *halves, vector, left, right, kron_own)
     shares = everyone(share)
 
     local = jax.ShapeDtypeStruct((rows, states, width), F32)
     vector_own, residual_own = pl.pallas_call(
         functools.partial(own_rows_kernel, scale),
         out_shape=(local, local),
-        in_specs=[smem] + [vmem] * 6,
+        in_specs=[vmem] * 7,
         out_specs=(vmem, vmem),
         compiler_params=params(),
         cost_estimate=cost(8 * guess.size, 16 * guess.size),
         name="own_rows",
-    )(bond_rank, guess, stat, stat_other, *halves)
+    )(keep, guess, stat, stat_other, *halves)
 
     ritz, energy = pl.pallas_call(
         finish_kernel,

time: 47.1 us -> 46.5 us (0.987)
  Pallas kernels: 25.6 us -> 24 us
  waiting for transfers between devices: 7.66 us -> 9.07 us
    pallas_call x3, Pallas kernels: 6.82 us -> 5.92 us  [the longest x1 3.84 us: there(): pl.pallas_call(functools.partial(last_kernel if last else there_kernel, s...]
    pallas_call x2, Pallas kernels: 3.01 us -> 2.44 us  [shards(): pl.pallas_call(functools.partial(rights_kernel, start, stop), out_shape=t...]
    ppermute x5, waiting for transfers between devices: 2.15 us -> 2.68 us  [to_next_chip(): lax.ppermute(block, 'term', [(i, (i + CORES) % members) for i in range(me...]
    ppermute x7, starting transfers between devices: 2.02 us -> 1.54 us  [to_sibling(): return lax.ppermute(block, 'term', [(i, i ^ 1) for i in range(members)])]
  transfers between devices with their start and end apart: 16 -> 16, of which waited for: 6 -> 7; matrix products, arithmetic and copies ran while one was open for 0% -> 0% of each run, Pallas kernels for 32% -> 30%
where the time goes in v8:
time: 46.5 us; the launch traced here: 46.4 us
  Pallas kernels  24 us (52%)
  starting transfers between devices  11.7 us (25%)
  waiting for transfers between devices  9.07 us (20%)
  between operations  1.57 us (3%)
    ppermute x5, starting transfers between devices, to_next_chip(): lax.ppermute(block, 'term', [(i, (i + CORES) % members) for i in range(me...  6.78 us
    pallas_call x1, Pallas kernels, shards(): pl.pallas_call(functools.partial(second_kernel, scale, members), out_shap...  5.75 us
    pallas_call x1, Pallas kernels, there(): pl.pallas_call(functools.partial(last_kernel if last else there_kernel, s...  3.84 us
    pallas_call x1, Pallas kernels, shards(): pl.pallas_call(functools.partial(lefts_kernel, far_spots, rows, chips), o...  3.65 us
    ppermute x7, waiting for transfers between devices, to_sibling(): return lax.ppermute(block, 'term', [(i, i ^ 1) for i in range(members)])  3.43 us
    ppermute x3, waiting for transfers between devices, everyone(): lax.ppermute(block, 'term', [(i, i ^ bits) for i in range(members)])  2.95 us
    ppermute x5, waiting for transfers between devices, to_next_chip(): lax.ppermute(block, 'term', [(i, (i + CORES) % members) for i in range(me...  2.68 us
    pallas_call x2, Pallas kernels, shards(): pl.pallas_call(functools.partial(rights_kernel, start, stop), out_shape=t...  2.44 us
  transfers between devices with their start and end apart: 16, of which 7 were waited for; matrix products, arithmetic and copies ran while one was open for 0% of the time, Pallas kernels for 30%

profile of v8, /device:TPU:0, one launch (start us, length us, event | category | flops | bytes accessed | tf_op | source)
XLA Modules:
  0.0 46.4 jit_solution(348384217701279775)
XLA Ops:
  1.3 1.7 %prepare.1 = (bf16[16,64,256]{2,1,0:T(8,128)(2,1)S(1)}, f32[8,256]{1,0:T(8,128)S(1)}, f32[8,256]{1,0:T(8,128)S(1)}, bf16[3,272,128]{2,1,0:T(8,128)(2,1)S(1)}, bf...) custom-call(s32[1,1]{1,0:T(1,128)} %bitcast.6.rank_ref, ...), custom_call_target="tpu_custom_call" | custom-call | flops 10485 | bytes 15728 | tf_op jit(solution)/shard_map/prepare/pallas_call | solution.py:444
  3.0 0.5 %collective-permute-start.1 = (bf16[16,64,256]{2,1,0:T(8,128)(2,1)S(1)}, bf16[16,64,256]{2,1,0:T(8,128)(2,1)S(1)}, u32[]{:S(2)}, u32[]{:S(2)}) collective-permute-start(bf16[16,64,256]{2,1,0:T(8,128)(2,1)S(1)} %get-tuple-element.45.refs_0_), channel_id=1, source_target_pairs={{0,1},{1,0},{2,3},{3,2},{4,5},{5,4},{6,7},{7,6},{8,9},{9,8},{10,11... | collective-permute-start | bytes 1572872 | tf_op jit(solution)/shard_map/ppermute | solution.py:422
  3.5 2.6 %collective-permute-start.2 = (bf16[17,32,256]{2,1,0:T(8,128)(2,1)S(1)}, bf16[17,32,256]{2,1,0:T(8,128)(2,1)S(1)}, u32[]{:S(2)}, u32[]{:S(2)}) collective-permute-start(bf16[17,32,256]{2,1,0:T(8,128)(2,1)S(1)} %get-tuple-element.46.chunk_ref), channel_id=1, source_target_pairs={{0,2},{1,3},{2,0},{3,1},{4,6},{5,7},{6,4},{7,5},{8,10},{9,11},{10,... | collective-permute-start | bytes 835592 | tf_op jit(solution)/shard_map/ppermute | solution.py:425
  6.1 1.3 %collective-permute-start = (bf16[3,272,128]{2,1,0:T(8,128)(2,1)S(1)}, bf16[3,272,128]{2,1,0:T(8,128)(2,1)S(1)}, u32[]{:S(2)}, u32[]{:S(2)}) collective-permute-start(bf16[3,272,128]{2,1,0:T(8,128)(2,1)S(1)} %get-tuple-element.44), channel_id=1, source_target_pairs={{4,0},{8,4},{12,8},{16,12},{20,16},{24,20},{28,24},{5,1},{9,5},{13... | collective-permute-start | bytes 626696 | tf_op jit(solution)/shard_map/ppermute | solution.py:476
  7.4 0.1 collective-permute-start.5
  7.5 2.0 %collective-permute-start.7 = (bf16[16,16,256]{2,1,0:T(8,128)(2,1)S(1)}, bf16[16,16,256]{2,1,0:T(8,128)(2,1)S(1)}, u32[]{:S(2)}, u32[]{:S(2)}) collective-permute-start(bf16[16,16,256]{2,1,0:T(8,128)(2,1)S(1)} %get-tuple-element.59), channel_id=1, source_target_pairs={{0,2},{1,3},{2,0},{3,1},{4,6},{5,7},{6,4},{7,5},{8,10},{9,11},{10,... | collective-permute-start | bytes 393224 | tf_op jit(solution)/shard_map/ppermute | solution.py:425
  9.5 0.9 %spread_site.2 = (bf16[768,256]{1,0:T(8,128)(2,1)S(1)}, f32[8,256]{1,0:T(8,128)}) custom-call(bf16[17,32,256]{2,1,0:T(8,128)(2,1)S(1)} %get-tuple-element.46.chunk_ref), custom_call_target="tpu_custom_call" | custom-call | flops 1006632 | bytes 3932 | tf_op jit(solution)/shard_map/spread_site/pallas_call | solution.py:481
  10.4 0.0 collective-permute-done.1.refs_1_
  10.4 0.1 collective-permute-start.9
  10.5 1.0 %rotate_own.1 = (bf16[3,16,128,256]{3,2,1,0:T(8,128)(2,1)S(1)}, bf16[256,768]{1,0:T(8,128)(2,1)S(1)}) custom-call(bf16[16,64,256]{2,1,0:T(8,128)(2,1)S(1)} %get-tuple-element.45.refs_0_, bf16[16,64,256]{2,1,0:T(8,128)(2,1)S(1)} %collective-permute-done.1.refs_1_, bf16[768,256]{1,0:T(8,128)(2,1)S(1)} %get-tuple-element.47.refs_2_.refs_7_.kron_ref, ...), custom_call_target="tpu_custom_call" | custom-call | flops 24159192 | bytes 83886 | tf_op jit(solution)/shard_map/rotate_own/pallas_call | solution.py:505
  11.5 2.1 %collective-permute-done.2.chunk_ref.refs_0_ = bf16[17,32,256]{2,1,0:T(8,128)(2,1)S(1)} collective-permute-done((bf16[17,32,256]{2,1,0:T(8,128)(2,1)S(1)}, bf16[17,32,256]{2,1,0:T(8,128)(2,1)S(1)}, u32[]{:S(2)}, u32[]{:S(2)}) %collective-permute-start.2) | collective-permute-done | bytes 278560 | tf_op jit(solution)/shard_map/ppermute | solution.py:425
  13.6 0.0 collective-permute-start.4
  13.6 0.4 spread_site.3
  14.0 1.3 %rotate_here.1 = (bf16[3,16,256,256]{3,2,1,0:T(8,128)(2,1)S(1)}, bf16[16,256,256]{2,1,0:T(8,128)(2,1)S(1)}) custom-call(bf16[16,64,256]{2,1,0:T(8,128)(2,1)S(1)} %get-tuple-element.45.refs_0_, bf16[16,64,256]{2,1,0:T(8,128)(2,1)S(1)} %collective-permute-done.1.refs_1_, bf16[768,256]{1,0:T(8,128)(2,1)S(1)} %get-tuple-element.51.refs_2_.refs_6_), custom_call_target="tpu_custom_call" | custom-call | flops 24159192 | bytes 83886 | tf_op jit(solution)/shard_map/rotate_here/pallas_call | solution.py:535
  15.3 0.0 collective-permute-done
  15.4 2.0 %collective-permute-start.3 = (bf16[3,272,128]{2,1,0:T(8,128)(2,1)S(1)}, bf16[3,272,128]{2,1,0:T(8,128)(2,1)S(1)}, u32[]{:S(2)}, u32[]{:S(2)}) collective-permute-start(bf16[3,272,128]{2,1,0:T(8,128)(2,1)S(1)} %broadcast_select_fusion.packed_ref), channel_id=1, source_target_pairs={{0,2},{1,3},{2,0},{3,1},{4,6},{5,7},{6,4},{7,5},{8,10},{9,11},{10,... | collective-permute-start | bytes 626696 | tf_op jit(solution)/shard_map/ppermute | solution.py:425
  17.4 0.0 collective-permute-done.5.refs_2_
  17.4 0.2 collective-permute-start.6
  17.6 1.1 %apply_rows_here.1 = (bf16[16,384,256]{2,1,0:T(8,128)(2,1)S(1)}, bf16[3,256,256]{2,1,0:T(8,128)(2,1)S(1)}) custom-call(bf16[3,16,128,256]{3,2,1,0:T(8,128)(2,1)S(1)} %get-tuple-element.60.rotated_ref, bf16[3,272,128]{2,1,0:T(8,128)(2,1)S(1)} %broadcast_select_fusion.packed_ref), custom_call_target="tpu_custom_call" | custom-call | flops 24159192 | bytes 83886 | tf_op jit(solution)/shard_map/apply_rows_here/pallas_call | solution.py:552
  18.7 0.5 %collective-permute-done.7.refs_4_ = bf16[16,16,256]{2,1,0:T(8,128)(2,1)S(1)} collective-permute-done((bf16[16,16,256]{2,1,0:T(8,128)(2,1)S(1)}, bf16[16,16,256]{2,1,0:T(8,128)(2,1)S(1)}, u32[]{:S(2)}, u32[]{:S(2)}) %collective-permute-start.7) | collective-permute-done | bytes 131104 | tf_op jit(solution)/shard_map/ppermute | solution.py:425
  19.3 0.0 collective-permute-start.8
  19.3 0.0 collective-permute-done.6.refs_3_
  19.3 1.3 %collective-permute-done.8.refs_5_ = bf16[16,16,256]{2,1,0:T(8,128)(2,1)S(1)} collective-permute-done((bf16[16,16,256]{2,1,0:T(8,128)(2,1)S(1)}, bf16[16,16,256]{2,1,0:T(8,128)(2,1)S(1)}, u32[]{:S(2)}, u32[]{:S(2)}) %collective-permute-start.8) | collective-permute-done | bytes 131104 | tf_op jit(solution)/shard_map/ppermute | solution.py:422
  20.6 0.0 collective-permute-done.4.refs_1_
  20.6 3.8 %apply_rows_there.1.before_ref = f32[16,256,256]{2,1,0:T(8,128)S(1)} custom-call(bf16[17,32,256]{2,1,0:T(8,128)(2,1)S(1)} %collective-permute-done.2.chunk_ref.refs_0_, bf16[17,32,256]{2,1,0:T(8,128)(2,1)S(1)} %collective-permute-done.4.refs_1_, bf16[16,16,256]{2,1,0:T(8,128)(2,1)S(1)} %collective-permute-done.5.refs_2_, ...), custom_call_target="tpu_custom_call" | custom-call | flops 24159192 | bytes 83886 | tf_op jit(solution)/shard_map/apply_rows_there/pallas_call | solution.py:522
  24.5 0.0 collective-permute-done.9.refs_9_
  24.5 3.7 %received_lefts.1 = (bf16[16,256,768]{2,1,0:T(8,128)(2,1)S(1)}, bf16[3,16,256,256]{3,2,1,0:T(8,128)(2,1)S(1)}, bf16[16,256,256]{2,1,0:T(8,128)(2,1)S(1)}) custom-call(bf16[17,32,256]{2,1,0:T(8,128)(2,1)S(1)} %collective-permute-done.2.chunk_ref.refs_0_, ...), custom_call_target="tpu_custom_call", output_to_operand_aliasing={{1}: (7, {}), {2}: (8, {})} | custom-call | flops 16106127 | bytes 125829 | tf_op jit(solution)/shard_map/received_lefts/pallas_call | solution.py:585
  28.1 0.0 collective-permute-done.3.packed_ref
  28.1 1.3 %received_rights.2 = (bf16[8,256,256]{2,1,0:T(8,128)(2,1)S(1)}, f32[8,256]{1,0:T(8,128)S(1)}, bf16[3,256,256]{2,1,0:T(8,128)(2,1)S(1)}) custom-call(bf16[3,272,128]{2,1,0:T(8,128)(2,1)S(1)} %collective-permute-done.3.packed_ref, bf16[16,256,768]{2,1,0:T(8,128)(2,1)S(1)} %get-tuple-element.70.mixed_ref, ...), custom_call_target="tpu_custom_call" | custom-call | flops 8053063 | bytes 125829 | tf_op jit(solution)/shard_map/received_rights/pallas_call | solution.py:603
  29.4 0.2 collective-permute-start.11
  29.7 1.2 %received_rights.3 = (bf16[8,256,256]{2,1,0:T(8,128)(2,1)S(1)}, f32[8,256]{1,0:T(8,128)S(1)}) custom-call(bf16[3,256,256]{2,1,0:T(8,128)(2,1)S(1)} %get-tuple-element.75.packed_ref, bf16[16,256,768]{2,1,0:T(8,128)(2,1)S(1)} %get-tuple-element.70.mixed_ref, bf16[16,256,256]{2,1,0:T(8,128)(2,1)S(1)} %get-tuple-element.71.whole_ref, ...), custom_call_target="tpu_custom_call" | custom-call | flops 8053063 | bytes 125829 | tf_op jit(solution)/shard_map/received_rights/pallas_call | solution.py:603
  30.8 0.4 collective-permute-start.12
  31.2 0.1 collective-permute-start.10
  31.4 0.8 %collective-permute-done.11.other_ref = bf16[8,256,256]{2,1,0:T(8,128)(2,1)S(1)} collective-permute-done((bf16[8,256,256]{2,1,0:T(8,128)(2,1)S(1)}, bf16[8,256,256]{2,1,0:T(8,128)(2,1)S(1)}, u32[]{:S(2)}, u32[]{:S(2)}) %collective-permute-start.11) | collective-permute-done | bytes 1048608 | tf_op jit(solution)/shard_map/ppermute | solution.py:422
  32.2 0.2 add_low_half.1.refs_0_.low_ref
  32.4 1.3 %collective-permute-done.10.theirs_ref = f32[8,256]{1,0:T(8,128)S(1)} collective-permute-done((f32[8,256]{1,0:T(8,128)S(1)}, f32[8,256]{1,0:T(8,128)S(1)}, u32[]{:S(2)}, u32[]{:S(2)}) %collective-permute-start.10) | collective-permute-done | bytes 8224 | tf_op jit(solution)/shard_map/ppermute | solution.py:422
  33.7 0.0 collective-permute-done.12.refs_2_.high_other_ref
  33.7 0.0 copy-start
  33.7 5.8 %apply_residual.1.refs_0_ = f32[8,256]{1,0:T(8,128)S(1)} custom-call(f32[8,256]{1,0:T(8,128)S(1)} %get-tuple-element.43.keep_ref, f32[8,256]{1,0:T(8,128)S(1)} %get-tuple-element.77.mine_ref, f32[8,256]{1,0:T(8,128)S(1)} %collective-permute-done.10.theirs_ref, f32[8,256,256]{2,1,0:T(8,128)S(1)} %add_low_half.1.refs_0_.low_ref, ...), custom_call_target="tpu_custom_call" | custom-call | flops 48318384 | bytes 62914 | tf_op jit(solution)/shard_map/apply_residual/pallas_call | solution.py:630
  39.4 1.8 %collective-permute-start.15 = (f32[8,256]{1,0:T(8,128)S(1)}, f32[8,256]{1,0:T(8,128)S(1)}, u32[]{:S(2)}, u32[]{:S(2)}) collective-permute-start(f32[8,256]{1,0:T(8,128)S(1)} %apply_residual.1.refs_0_), channel_id=1, source_target_pairs={{0,3},{1,2},{2,1},{3,0},{4,7},{5,6},{6,5},{7,4},{8,11},{9,10},{10,... | collective-permute-start | bytes 24584 | tf_op jit(solution)/shard_map/ppermute | solution.py:435
  41.3 0.2 collective-permute-start.14
  41.5 0.0 collective-permute-start.13
  41.6 0.0 copy-done
  41.6 0.4 own_rows.1
  42.0 0.7 %collective-permute-done.15.refs_3_ = f32[8,256]{1,0:T(8,128)S(1)} collective-permute-done((f32[8,256]{1,0:T(8,128)S(1)}, f32[8,256]{1,0:T(8,128)S(1)}, u32[]{:S(2)}, u32[]{:S(2)}) %collective-permute-start.15) | collective-permute-done | bytes 8224 | tf_op jit(solution)/shard_map/ppermute | solution.py:435
  42.7 2.3 %collective-permute-done.14.refs_2_ = f32[8,256]{1,0:T(8,128)S(1)} collective-permute-done((f32[8,256]{1,0:T(8,128)S(1)}, f32[8,256]{1,0:T(8,128)S(1)}, u32[]{:S(2)}, u32[]{:S(2)}) %collective-permute-start.14) | collective-permute-done | bytes 8224 | tf_op jit(solution)/shard_map/ppermute | solution.py:435
  44.9 0.0 collective-permute-done.13.refs_1_
  44.9 1.3 %finish.1 = (f32[64,16,256]{2,1,0:T(8,128)}, f32[1]{0:T(128)}) custom-call(f32[64,16,256]{2,1,0:T(8,128)S(1)} %get-tuple-element.80.vector_ref, f32[64,16,256]{2,1,0:T(8,128)S(1)} %get-tuple-element.81.residual_ref, f32[8,256]{1,0:T(8,128)S(1)} %apply_residual.1.refs_0_, f32[8,256]{1,0:T(8,128)S(1)} %collective-permute-done.13.refs_1_, ...), custom_call_target="tpu_custom_call" | custom-call | flops 7864 | bytes 31457 | tf_op jit(solution)/shard_map/finish/pallas_call | solution.py:657
  (1 shorter events, 0.0 us)
Async XLA Ops:
  3.0 7.4 %collective-permute-start.1 = (bf16[16,64,256]{2,1,0:T(8,128)(2,1)S(1)}, bf16[16,64,256]{2,1,0:T(8,128)(2,1)S(1)}, u32[]{:S(2)}, u32[]{:S(2)}) collective-permute-start(bf16[16,64,256]{2,1,0:T(8,128)(2,1)S(1)} %get-tuple-element.45.refs_0_), channel_id=1, source_target_pairs={{0,1},{1,0},{2,3},{3,2},{4,5},{5,4},{6,7},{7,6},{8,9},{9,8},{10,11... | collective-permute-start | bytes 1572872 | tf_op jit(solution)/shard_map/ppermute | solution.py:422
  3.5 10.1 %collective-permute-start.2 = (bf16[17,32,256]{2,1,0:T(8,128)(2,1)S(1)}, bf16[17,32,256]{2,1,0:T(8,128)(2,1)S(1)}, u32[]{:S(2)}, u32[]{:S(2)}) collective-permute-start(bf16[17,32,256]{2,1,0:T(8,128)(2,1)S(1)} %get-tuple-element.46.chunk_ref), channel_id=1, source_target_pairs={{0,2},{1,3},{2,0},{3,1},{4,6},{5,7},{6,4},{7,5},{8,10},{9,11},{10,... | collective-permute-start | bytes 835592 | tf_op jit(solution)/shard_map/ppermute | solution.py:425
  6.1 9.2 %collective-permute-start = (bf16[3,272,128]{2,1,0:T(8,128)(2,1)S(1)}, bf16[3,272,128]{2,1,0:T(8,128)(2,1)S(1)}, u32[]{:S(2)}, u32[]{:S(2)}) collective-permute-start(bf16[3,272,128]{2,1,0:T(8,128)(2,1)S(1)} %get-tuple-element.44), channel_id=1, source_target_pairs={{4,0},{8,4},{12,8},{16,12},{20,16},{24,20},{28,24},{5,1},{9,5},{13... | collective-permute-start | bytes 626696 | tf_op jit(solution)/shard_map/ppermute | solution.py:476
  7.4 10.0 %collective-permute-start.5 = (bf16[16,16,256]{2,1,0:T(8,128)(2,1)S(1)}, bf16[16,16,256]{2,1,0:T(8,128)(2,1)S(1)}, u32[]{:S(2)}, u32[]{:S(2)}) collective-permute-start(bf16[16,16,256]{2,1,0:T(8,128)(2,1)S(1)} %get-tuple-element.55), channel_id=1, source_target_pairs={{0,2},{1,3},{2,0},{3,1},{4,6},{5,7},{6,4},{7,5},{8,10},{9,11},{10,... | collective-permute-start | bytes 393224 | tf_op jit(solution)/shard_map/ppermute | solution.py:425
  7.5 11.7 %collective-permute-start.7 = (bf16[16,16,256]{2,1,0:T(8,128)(2,1)S(1)}, bf16[16,16,256]{2,1,0:T(8,128)(2,1)S(1)}, u32[]{:S(2)}, u32[]{:S(2)}) collective-permute-start(bf16[16,16,256]{2,1,0:T(8,128)(2,1)S(1)} %get-tuple-element.59), channel_id=1, source_target_pairs={{0,2},{1,3},{2,0},{3,1},{4,6},{5,7},{6,4},{7,5},{8,10},{9,11},{10,... | collective-permute-start | bytes 393224 | tf_op jit(solution)/shard_map/ppermute | solution.py:425
  10.4 14.0 %collective-permute-start.9 = (bf16[3,272,128]{2,1,0:T(8,128)(2,1)S(1)}, bf16[3,272,128]{2,1,0:T(8,128)(2,1)S(1)}, u32[]{:S(2)}, u32[]{:S(2)}) collective-permute-start(bf16[3,272,128]{2,1,0:T(8,128)(2,1)S(1)} %get-tuple-element.65), channel_id=1, source_target_pairs={{0,2},{1,3},{2,0},{3,1},{4,6},{5,7},{6,4},{7,5},{8,10},{9,11},{10,... | collective-permute-start | bytes 626696 | tf_op jit(solution)/shard_map/ppermute | solution.py:425
  13.6 7.0 %collective-permute-start.4 = (bf16[17,32,256]{2,1,0:T(8,128)(2,1)S(1)}, bf16[17,32,256]{2,1,0:T(8,128)(2,1)S(1)}, u32[]{:S(2)}, u32[]{:S(2)}) collective-permute-start(bf16[17,32,256]{2,1,0:T(8,128)(2,1)S(1)} %collective-permute-done.2.chunk_ref.refs_0_), channel_id=1, source_target_pairs={{0,1},{1,0},{2,3},{3,2},{4,5},{5,4},{6,7},{7,6},{8,9},{9,8},{10,11... | collective-permute-start | bytes 835592 | tf_op jit(solution)/shard_map/ppermute | solution.py:422
  15.4 12.8 %collective-permute-start.3 = (bf16[3,272,128]{2,1,0:T(8,128)(2,1)S(1)}, bf16[3,272,128]{2,1,0:T(8,128)(2,1)S(1)}, u32[]{:S(2)}, u32[]{:S(2)}) collective-permute-start(bf16[3,272,128]{2,1,0:T(8,128)(2,1)S(1)} %broadcast_select_fusion.packed_ref), channel_id=1, source_target_pairs={{0,2},{1,3},{2,0},{3,1},{4,6},{5,7},{6,4},{7,5},{8,10},{9,11},{10,... | collective-permute-start | bytes 626696 | tf_op jit(solution)/shard_map/ppermute | solution.py:425
  17.4 1.9 %collective-permute-start.6 = (bf16[16,16,256]{2,1,0:T(8,128)(2,1)S(1)}, bf16[16,16,256]{2,1,0:T(8,128)(2,1)S(1)}, u32[]{:S(2)}, u32[]{:S(2)}) collective-permute-start(bf16[16,16,256]{2,1,0:T(8,128)(2,1)S(1)} %collective-permute-done.5.refs_2_), channel_id=1, source_target_pairs={{0,1},{1,0},{2,3},{3,2},{4,5},{5,4},{6,7},{7,6},{8,9},{9,8},{10,11... | collective-permute-start | bytes 393224 | tf_op jit(solution)/shard_map/ppermute | solution.py:422
  19.3 1.3 %collective-permute-start.8 = (bf16[16,16,256]{2,1,0:T(8,128)(2,1)S(1)}, bf16[16,16,256]{2,1,0:T(8,128)(2,1)S(1)}, u32[]{:S(2)}, u32[]{:S(2)}) collective-permute-start(bf16[16,16,256]{2,1,0:T(8,128)(2,1)S(1)} %collective-permute-done.7.refs_4_), channel_id=1, source_target_pairs={{0,1},{1,0},{2,3},{3,2},{4,5},{5,4},{6,7},{7,6},{8,9},{9,8},{10,11... | collective-permute-start | bytes 393224 | tf_op jit(solution)/shard_map/ppermute | solution.py:422
  29.4 2.7 %collective-permute-start.11 = (bf16[8,256,256]{2,1,0:T(8,128)(2,1)S(1)}, bf16[8,256,256]{2,1,0:T(8,128)(2,1)S(1)}, u32[]{:S(2)}, u32[]{:S(2)}) collective-permute-start(bf16[8,256,256]{2,1,0:T(8,128)(2,1)S(1)} %get-tuple-element.78.mine_ref), channel_id=1, source_target_pairs={{0,1},{1,0},{2,3},{3,2},{4,5},{5,4},{6,7},{7,6},{8,9},{9,8},{10,11... | collective-permute-start | bytes 3145736 | tf_op jit(solution)/shard_map/ppermute | solution.py:422
  30.8 2.9 %collective-permute-start.12 = (bf16[8,256,256]{2,1,0:T(8,128)(2,1)S(1)}, bf16[8,256,256]{2,1,0:T(8,128)(2,1)S(1)}, u32[]{:S(2)}, u32[]{:S(2)}) collective-permute-start(bf16[8,256,256]{2,1,0:T(8,128)(2,1)S(1)} %get-tuple-element.79.refs_1_.high_ref), channel_id=1, source_target_pairs={{0,1},{1,0},{2,3},{3,2},{4,5},{5,4},{6,7},{7,6},{8,9},{9,8},{10,11... | collective-permute-start | bytes 3145736 | tf_op jit(solution)/shard_map/ppermute | solution.py:422
  31.2 2.4 %collective-permute-start.10 = (f32[8,256]{1,0:T(8,128)S(1)}, f32[8,256]{1,0:T(8,128)S(1)}, u32[]{:S(2)}, u32[]{:S(2)}) collective-permute-start(f32[8,256]{1,0:T(8,128)S(1)} %get-tuple-element.77.mine_ref), channel_id=1, source_target_pairs={{0,1},{1,0},{2,3},{3,2},{4,5},{5,4},{6,7},{7,6},{8,9},{9,8},{10,11... | collective-permute-start | bytes 24584 | tf_op jit(solution)/shard_map/ppermute | solution.py:422
  33.7 7.9 %copy-start = (f32[1,64,16,256]{3,2,1,0:T(8,128)S(1)}, f32[1,64,16,256]{3,2,1,0:T(8,128)}, u32[]{:S(2)}) copy-start(f32[1,64,16,256]{3,2,1,0:T(8,128)} %param.5) | copy-start | bytes 3145732
  39.4 3.2 %collective-permute-start.15 = (f32[8,256]{1,0:T(8,128)S(1)}, f32[8,256]{1,0:T(8,128)S(1)}, u32[]{:S(2)}, u32[]{:S(2)}) collective-permute-start(f32[8,256]{1,0:T(8,128)S(1)} %apply_residual.1.refs_0_), channel_id=1, source_target_pairs={{0,3},{1,2},{2,1},{3,0},{4,7},{5,6},{6,5},{7,4},{8,11},{9,10},{10,... | collective-permute-start | bytes 24584 | tf_op jit(solution)/shard_map/ppermute | solution.py:435
  41.3 3.7 %collective-permute-start.14 = (f32[8,256]{1,0:T(8,128)S(1)}, f32[8,256]{1,0:T(8,128)S(1)}, u32[]{:S(2)}, u32[]{:S(2)}) collective-permute-start(f32[8,256]{1,0:T(8,128)S(1)} %apply_residual.1.refs_0_), channel_id=1, source_target_pairs={{0,2},{1,3},{2,0},{3,1},{4,6},{5,7},{6,4},{7,5},{8,10},{9,11},{10,... | collective-permute-start | bytes 24584 | tf_op jit(solution)/shard_map/ppermute | solution.py:435
  41.5 3.4 %collective-permute-start.13 = (f32[8,256]{1,0:T(8,128)S(1)}, f32[8,256]{1,0:T(8,128)S(1)}, u32[]{:S(2)}, u32[]{:S(2)}) collective-permute-start(f32[8,256]{1,0:T(8,128)S(1)} %apply_residual.1.refs_0_), channel_id=1, source_target_pairs={{0,1},{1,0},{2,3},{3,2},{4,5},{5,4},{6,7},{7,6},{8,9},{9,8},{10,11... | collective-permute-start | bytes 24584 | tf_op jit(solution)/shard_map/ppermute | solution.py:435

commit v9 on v8

--- a/solution.py
+++ b/solution.py
@@ -34,69 +34,87 @@
     return jnp.sum(values.reshape(values.size // (8 * width), 8, width), axis=0)
 
 
+def chunk_rows_in(guess_in, guess_ref, sems, start, stop):
+    copies = []
+    for n in range(start, stop, TILE):
+        part = pl.ds(n, TILE)
+        copies.append(pltpu.make_async_copy(guess_in.at[part], guess_ref.at[pl.ds(n - start, TILE)], sems.at[n // TILE]))
+        copies[-1].start()
+    return copies
+
+
+def first_chunk_kernel(rank_ref, guess_in, site_ref, x_ref, keep_ref, squares_ref, guess_ref, sems):
+    rows, states, width = guess_ref.shape
+    terms = site_ref.shape[0]
+    copies = chunk_rows_in(guess_in, guess_ref, sems, 0, rows)
+    column = lax.broadcasted_iota(jnp.int32, (1, width), 1)
+    keep = (column < rank_ref[...]).astype(F32)
+    keep_ref[...] = jnp.broadcast_to(keep, keep_ref.shape)
+    line = lax.broadcasted_iota(jnp.int32, (TILE, width), 0)
+    lane = lax.broadcasted_iota(jnp.int32, (TILE, width), 1)
+    extra = jnp.zeros((TILE, width), F32)
+    for k in range(terms):
+        place_at = (lane == line + k * TILE).astype(BF16)
+        extra = extra + jnp.dot(site_ref[k], place_at, preferred_element_type=F32)
+    x_ref[states, 0:TILE, :] = extra.astype(BF16)
+    squares = jnp.zeros((8, width), F32)
+    for n, copy in enumerate(copies):
+        copy.wait()
+        part = pl.ds(n * TILE, TILE)
+        masked = guess_ref[part] * keep[None]
+        squares = squares + fold(masked * masked, width)
+        x_ref[0:states, part, :] = jnp.swapaxes(masked, 0, 1).astype(BF16)
+    squares_ref[...] = squares
+
+
 def prepare_kernel(
     starts,
-    rank_ref,
+    keep_ref,
+    squares_ref,
     guess_in,
     left_in,
     right_in,
-    site_in,
-    x_ref,
     norm_ref,
-    keep_ref,
     left_packed_ref,
     right_packed_ref,
     left_ref,
     *refs,
 ):
-    chunk_refs = refs[: len(starts)]
-    guess_ref, right_ref, site_ref, sems = refs[len(starts) :]
-    rows, states, width = guess_ref.shape
+    x_refs = refs[: len(starts)]
+    guess_ref, right_ref, sems = refs[len(starts) :]
+    rows, states, width = guess_in.shape
     terms = left_ref.shape[0]
     half = width // 2
-    parts = [pl.ds(n, TILE) for n in range(0, rows, TILE)]
-    sources = [guess_in.at[part] for part in parts] + [site_in, right_in, left_in]
-    targets = [guess_ref.at[part] for part in parts] + [site_ref, right_ref, left_ref]
-    copies = [
-        pltpu.make_async_copy(source, target, sems.at[n])
-        for n, (source, target) in enumerate(zip(sources, targets))
-    ]
-    for copy in copies:
-        copy.start()
-    column = lax.broadcasted_iota(jnp.int32, (1, width), 1)
-    keep = (column < rank_ref[...]).astype(F32)
-    keep_ref[...] = jnp.broadcast_to(keep, keep_ref.shape)
-    keep = keep[None]
-    squares = jnp.zeros((8, width), F32)
-    for n, part in enumerate(parts):
+    done = starts[1] if len(starts) > 1 else rows
+    copies = chunk_rows_in(guess_in, guess_ref, sems, done, rows)
+    for source, target in ((right_in, right_ref), (left_in, left_ref)):
+        copies.append(pltpu.make_async_copy(source, target, sems.at[rows // TILE + len(copies) - (rows - done) // TILE]))
+        copies[-1].start()
+    keep = keep_ref[0:1, :][None]
+    squares = squares_ref[...]
+    for n in range((rows - done) // TILE):
         copies[n].wait()
-        masked = guess_ref[part] * keep
+        masked = guess_ref[pl.ds(n * TILE, TILE)] * keep
         squares = squares + fold(masked * masked, width)
         turned = jnp.swapaxes(masked, 0, 1).astype(BF16)
-        x_ref[:, part, :] = turned
-        chunk = max(c for c, start in enumerate(starts) if start <= n * TILE)
-        at = n * TILE - starts[chunk]
-        chunk_refs[chunk][0:states, at : at + TILE, :] = turned
+        x_refs[0][:, n * TILE : (n + 1) * TILE, :] = turned
+        chunk = max(c for c, start in enumerate(starts) if start <= done + n * TILE)
+        at = done + n * TILE - starts[chunk]
+        x_refs[chunk][:, at : at + TILE, :] = turned
     total = jnp.sum(squares)
     norm_ref[...] = jnp.full(norm_ref.shape, total, F32)
-    copies[-3].wait()
-    line = lax.broadcasted_iota(jnp.int32, (TILE, width), 0)
-    lane = lax.broadcasted_iota(jnp.int32, (TILE, width), 1)
-    norm = jnp.full((TILE, width), total, F32)
-    extra = jnp.zeros((TILE, width), F32)
-    for n in range(3):
+    line = lax.broadcasted_iota(jnp.int32, (TILE, half), 0)
+    norm = jnp.full((TILE, half), total, F32)
+    extra = jnp.zeros((TILE, half), F32)
+    for n in range(1, 4):
         part = norm.astype(BF16).astype(F32)
         norm = norm - part
-        extra = jnp.where((line == n) & (lane >= half), part, extra)
-    for k in range(terms):
-        place_at = (lane == line + k * TILE).astype(BF16)
-        extra = extra + jnp.dot(site_ref[k], place_at, preferred_element_type=F32)
-    chunk_refs[0][states, 0:TILE, :] = extra.astype(BF16)
+        extra = jnp.where(line == n, part, extra)
     for copy, block_ref, packed_ref in zip(copies[-2:], (right_ref, left_ref), (right_packed_ref, left_packed_ref)):
         copy.wait()
         for k in range(terms):
             diagonal = pack_symmetric(block_ref, k, packed_ref)
-            packed_ref[k, width : width + TILE, :] = jnp.broadcast_to(diagonal, (TILE, half)).astype(BF16)
+            packed_ref[k, width : width + TILE, :] = jnp.where(line == 0, diagonal, extra).astype(BF16)
 
 
 def triangle(half):
@@ -133,16 +151,12 @@
         ).astype(BF16)
 
 
-def spread_kernel(chunk_ref, kron_ref, norm_ref):
+def spread_kernel(chunk_ref, kron_ref):
     width = chunk_ref.shape[2]
-    half = width // 2
     size = kron_ref.shape[1]
     terms = kron_ref.shape[0] // size
     states = size // TILE
     tile = chunk_ref[states, 0:TILE, :]
-    lines = tile.astype(F32)
-    norm = lines[0:1, half:width] + lines[1:2, half:width] + lines[2:3, half:width]
-    norm_ref[...] = jnp.broadcast_to(jnp.concatenate([norm, norm], axis=1), norm_ref.shape)
     row_state = lax.broadcasted_iota(jnp.int32, (size, states), 0) // TILE
     pick = (row_state == lax.broadcasted_iota(jnp.int32, (size, states), 1)).astype(BF16)
     tall = jnp.dot(pick, tile, preferred_element_type=F32).astype(BF16)
@@ -185,33 +199,35 @@
     return chip, me % CORES
 
 
-def mix_pieces(spots, rows, pieces, kron_ref, rotated_ref):
-    _, core = place(0, 1)
-    for (_, flip, offset), piece in zip(spots, pieces):
-        at = (core if flip == 0 else 1 - core) * rows + offset
+def row_of(spot, rows, chips):
+    chip, core = place(spot[0], chips)
+    return pl.multiple_of((chip * CORES + (core if spot[1] == 0 else 1 - core)) * rows + spot[2], TILE)
+
+
+def mix_pieces(pieces, kron_ref, rotated_ref):
+    at = 0
+    for piece in pieces:
         mix_sites(piece, kron_ref, rotated_ref, at, UNROLL)
-
-
-def rotate_own_kernel(spots, rows, chips, *refs):
-    pieces = refs[: len(spots)]
-    kron_ref, left_ref, rotated_ref, columns_ref = refs[len(spots) :]
-    terms, states, chip_rows, width = rotated_ref.shape
-    mix_pieces(spots, rows, pieces, kron_ref, rotated_ref)
+        at += piece.shape[1]
+
+
+def rotate_own_kernel(groups, rows, chips, *refs):
+    kron_ref, left_ref, rotated_ref, columns_ref = refs[-4:]
+    mix_pieces(refs[:-4], kron_ref, rotated_ref)
     blocks = []
-    for hop in range(chips):
-        chip, _ = place(hop, chips)
-        at = pl.multiple_of(chip * chip_rows, TILE)
-        blocks += [left_ref[k, pl.ds(at, chip_rows), :] for k in range(terms)]
+    for spots in groups:
+        for k in range(left_ref.shape[0]):
+            blocks += [left_ref[k, pl.ds(row_of(spot, rows, chips), spot[3]), :] for spot in spots]
     columns_ref[...] = jnp.concatenate(blocks, axis=0).astype(F32).T.astype(BF16)
 
 
 def turn(right_ref, rotated_ref, turned_ref):
-    terms, states, chip_rows, width = rotated_ref.shape
+    terms, states, count, width = rotated_ref.shape
     for k in range(terms):
         for n in range(0, states, 8):
-            source = rotated_ref[k, n : n + 8].reshape(8 * chip_rows, width)
+            source = rotated_ref[k, n : n + 8].reshape(8 * count, width)
             turned = jnp.dot(source, right_ref[k], preferred_element_type=F32).astype(BF16)
-            turned_ref[n : n + 8, k * chip_rows : (k + 1) * chip_rows, :] = turned.reshape(8, chip_rows, width)
+            turned_ref[n : n + 8, k * count : (k + 1) * count, :] = turned.reshape(8, count, width)
 
 
 def here_kernel(rotated_ref, packed_ref, turned_ref, right_ref):
@@ -219,18 +235,16 @@
     turn(right_ref, rotated_ref, turned_ref)
 
 
-def there_kernel(spots, rows, *refs):
-    count = len(spots)
-    right_ref, kron_ref, turned_ref, rotated_ref = refs[count:]
-    mix_pieces(spots, rows, refs[:count], kron_ref, rotated_ref)
+def there_kernel(*refs):
+    right_ref, kron_ref, turned_ref, rotated_ref = refs[-4:]
+    mix_pieces(refs[:-4], kron_ref, rotated_ref)
     turn(right_ref, rotated_ref, turned_ref)
 
 
-def last_kernel(spots, rows, *refs):
-    count = len(spots)
+def last_kernel(count, *refs):
     right_ref, kron_ref, columns_ref = refs[count : count + 3]
     out_ref, rotated_ref, turned_ref = refs[-3:]
-    there_kernel(spots, rows, *refs[:count], right_ref, kron_ref, turned_ref, rotated_ref)
+    there_kernel(*refs[:count], right_ref, kron_ref, turned_ref, rotated_ref)
     blocks = list(refs[count + 3 : -3]) + [turned_ref]
 
     def lefts(p, carry):
@@ -247,11 +261,8 @@
     rotated_ref, whole_ref, sems = refs[-3:]
     states = whole_ref.shape[0]
     copies = []
-    bases = []
-    for n, ((hop, flip, offset), piece) in enumerate(zip(spots, pieces)):
-        chip, core = place(hop, chips)
-        at = pl.multiple_of((chip * CORES + (core if flip == 0 else 1 - core)) * rows + offset, TILE)
-        bases.append(at)
+    bases = [row_of(spot, rows, chips) for spot in spots]
+    for n, (at, piece) in enumerate(zip(bases, pieces)):
         target = whole_ref.at[:, pl.ds(at, piece.shape[1]), :]
         copies.append(pltpu.make_async_copy(piece.at[0:states], target, sems.at[n]))
         copies[-1].start()
@@ -264,8 +275,11 @@
 def lefts_kernel(spots, rows, chips, *refs):
     count = len(spots)
     packed_ref = refs[count + 3]
-    mixed_ref, rotated_ref, whole_ref, left_ref, sems = refs[-5:]
+    mixed_ref, norm_ref, rotated_ref, whole_ref, left_ref, sems = refs[-6:]
     terms, states, width, _ = rotated_ref.shape
+    lines = packed_ref[0, width : width + TILE, :].astype(F32)
+    norm = lines[1:2] + lines[2:3] + lines[3:4]
+    norm_ref[...] = jnp.broadcast_to(jnp.concatenate([norm, norm], axis=1), norm_ref.shape)
     unpack_symmetric(packed_ref, left_ref)
     rotate_kernel(spots, rows, chips, *refs[: count + 1], rotated_ref, whole_ref, sems)
 
@@ -431,46 +445,69 @@
         return found
 
     def everyone(block):
-        others = [
-            lax.ppermute(block, "term", [(i, i ^ bits) for i in range(members)]) for bits in range(1, members)
+        return [block] + [
+            lax.ppermute(block, "term", [(i, i ^ bits) for i in range(members)])
+            for bits in range(CORES, members, CORES)
         ]
-        return [block] + others
 
     tile = jax.ShapeDtypeStruct((8, width), F32)
     half = width // 2
     packed_shape = jax.ShapeDtypeStruct((terms, width + TILE, half), BF16)
     starts = (0, rows - 2 * TILE, rows - TILE) if rows >= 4 * TILE else (0,)
     lengths = [stop - start for start, stop in zip(starts, starts[1:] + (rows,))]
-    x_own, norm_part, keep, left_packed, right_packed, left, *chunks = pl.pallas_call(
+    in_place = [pltpu.with_memory_space_constraint(a, pltpu.HBM) for a in (guess, left, right_env[0], site)]
+    first_chunk, keep, squares = pl.pallas_call(
+        first_chunk_kernel,
+        out_shape=(jax.ShapeDtypeStruct((states + 1, lengths[0], width), BF16), tile, tile),
+        in_specs=[vmem, in_hbm, vmem],
+        out_specs=(vmem,) * 3,
+        scratch_shapes=[
+            pltpu.VMEM((lengths[0], states, width), F32),
+            pltpu.SemaphoreType.DMA((lengths[0] // TILE,)),
+        ],
+        compiler_params=params(),
+        cost_estimate=cost(2 * guess.size, 3 * guess.size),
+        name="first_chunk",
+    )(bond_rank.reshape(1, 1), in_place[0], in_place[3])
+    rest = rows - lengths[0]
+    norm_part, left_packed, right_packed, left, *chunks = pl.pallas_call(
         functools.partial(prepare_kernel, starts),
         out_shape=(
-            jax.ShapeDtypeStruct((states, rows, width), BF16),
-            tile,
             tile,
             packed_shape,
             packed_shape,
             jax.ShapeDtypeStruct(left.shape, BF16),
             *[
-                jax.ShapeDtypeStruct((states + (n == 0), length, width), BF16)
-                for n, length in enumerate(lengths)
+                jax.ShapeDtypeStruct((states, length, width), BF16)
+                for length in ([rest] + lengths[1:] if rest else [TILE])
             ],
         ),
-        in_specs=[vmem] + [in_hbm] * 4,
-        out_specs=(vmem,) * (6 + len(lengths)),
+        in_specs=[vmem] * 2 + [in_hbm] * 3,
+        out_specs=(vmem,) * (4 + len(lengths)),
         scratch_shapes=[
-            pltpu.VMEM(guess.shape, F32),
+            pltpu.VMEM((max(rest, TILE), states, width), F32),
             pltpu.VMEM(left.shape, BF16),
-            pltpu.VMEM(site.shape, BF16),
-            pltpu.SemaphoreType.DMA((rows // TILE + 3,)),
+            pltpu.SemaphoreType.DMA((rows // TILE + 2,)),
         ],
         compiler_params=params(),
         cost_estimate=cost(4 * guess.size, 6 * guess.size),
         name="prepare",
-    )(bond_rank.reshape(1, 1), *[pltpu.with_memory_space_constraint(a, pltpu.HBM) for a in (guess, left, right_env[0], site)])
+    )(keep, squares, *in_place[:3])
+    own_pieces = [first_chunk] + (chunks[:1] if rest else [])
+    chunks = [first_chunk] + chunks[1:]
 
     chunk_hops = [around(chunk) for chunk in chunks]
-    here_pieces = [x_own, to_sibling(x_own)]
-    here_spots = ((0, 0, 0), (0, 1, 0))
+    here_pieces = own_pieces + [to_sibling(piece) for piece in own_pieces]
+    bounds = (0, lengths[0], rows) if rest else (0, rows)
+    here_spots = tuple(
+        (0, flip, start, stop - start) for flip in range(CORES) for start, stop in zip(bounds[:-1], bounds[1:])
+    )
+    far_spots = [
+        tuple((hop, flip, start, length) for hop in hops[1:] for flip in range(CORES))
+        for start, length in zip(starts, lengths)
+    ]
+    mid_spots = sum(far_spots[:-1], ())
+    groups = [group for group in (here_spots, mid_spots, far_spots[-1]) if group]
     lefts = around(left_packed)
     shift = [(i + 1, i) for i in range(segments - 1)]
     received = lax.ppermute(right_packed, "seg", shift)
@@ -480,15 +517,15 @@
     def spread(block):
         return pl.pallas_call(
             spread_kernel,
-            out_shape=(jax.ShapeDtypeStruct((terms * size, size), BF16), tile),
+            out_shape=jax.ShapeDtypeStruct((terms * size, size), BF16),
             in_specs=[vmem],
-            out_specs=(vmem, vmem),
+            out_specs=vmem,
             compiler_params=params(),
             cost_estimate=cost(2 * terms * size * size * width, 2 * terms * size * size),
             name="spread_site",
         )(block)
 
-    kron_own, _ = spread(chunks[0])
+    kron_own = spread(chunks[0])
 
     whole = (states, width, width)
     whole_bf = jax.ShapeDtypeStruct(whole, BF16)
@@ -499,100 +536,113 @@
     chip_rows = CORES * rows
     stage_flops = 2 * terms * states * width * width * width
 
-    chip_rotated = (terms, states, chip_rows, width)
-    chip_turned = jax.ShapeDtypeStruct((states, terms * chip_rows, width), BF16)
-    chip_cost = cost(3 * stage_flops * chip_rows / width, 8 * states * width * width)
+    def buffers(spots):
+        count = sum(spot[3] for spot in spots)
+        return (terms, states, count, width), (states, terms * count, width)
+
+    here_rotated, here_turned = buffers(here_spots)
+    part_cost = cost(stage_flops, 8 * states * width * width)
     rotated_own, columns = pl.pallas_call(
-        functools.partial(rotate_own_kernel, here_spots, rows, chips),
+        functools.partial(rotate_own_kernel, groups, rows, chips),
         out_shape=(
-            jax.ShapeDtypeStruct(chip_rotated, BF16),
+            jax.ShapeDtypeStruct(here_rotated, BF16),
             jax.ShapeDtypeStruct((width, terms * width), BF16),
         ),
-        in_specs=[vmem] * 4,
+        in_specs=[vmem] * (len(here_pieces) + 2),
         out_specs=(vmem, vmem),
         compiler_params=params(),
-        cost_estimate=chip_cost,
+        cost_estimate=part_cost,
         name="rotate_own",
     )(*here_pieces, kron_own, left)
 
-    def there(hop, before):
-        spots = tuple(spot for spot in far_spots if spot[0] == hop)
-        pieces = [piece for spot, piece in zip(far_spots, far_pieces) if spot[0] == hop]
-        last = hop == hops[-1]
+    def rotate(spots, pieces, kron, before):
         return pl.pallas_call(
-            functools.partial(last_kernel if last else there_kernel, spots, rows),
-            out_shape=whole_f32 if last else chip_turned,
-            in_specs=[vmem] * (len(pieces) + 2 + (1 + len(before) if last else 0)),
-            out_specs=vmem,
-            scratch_shapes=[pltpu.VMEM(chip_rotated, BF16)]
-            + ([pltpu.VMEM(chip_turned.shape, BF16)] if last else []),
+            functools.partial(rotate_kernel, spots, rows, chips),
+            out_shape=(rotated_bf, whole_bf),
+            in_specs=[vmem] * (len(pieces) + 1) + [anywhere] * len(before),
+            out_specs=(vmem, vmem),
+            scratch_shapes=[pltpu.SemaphoreType.DMA((len(pieces),))],
+            input_output_aliases={len(pieces) + 1 + n: n for n in range(len(before))},
             compiler_params=params(),
-            cost_estimate=chip_cost,
-            name="apply_rows_there",
-        )(*pieces, right, kron_own, *([columns] + before if last else []))
-
-    def rotate(kron):
-        return pl.pallas_call(
-            functools.partial(rotate_kernel, here_spots, rows, chips),
-            out_shape=(rotated_bf, whole_bf),
-            in_specs=[vmem] * 3,
-            out_specs=(vmem, vmem),
-            scratch_shapes=[pltpu.SemaphoreType.DMA((CORES,))],
-            compiler_params=params(),
-            cost_estimate=chip_cost,
-            name="rotate_here",
-        )(*here_pieces, kron)
+            cost_estimate=part_cost,
+            name="rotate_crossed" if before else "rotate_here",
+        )(*pieces, kron, *before)
+
+    def relayed(blocks):
+        return [piece for block in blocks for piece in (block, to_sibling(block))]
 
     firsts, rotated_own = lax.optimization_barrier((chunk_hops[0][1:], rotated_own))
-    kron, norm_far = spread(firsts[0])
-    turned = rotate(kron)
+    kron = spread(firsts[0])
+    turned = rotate(here_spots, here_pieces, kron, ())
     received, turned = lax.optimization_barrier((received, turned))
     packed = jnp.where(lax.axis_index("seg") == segments - 1, right_packed, received)
     rights = around(packed)
     turned_own, right = pl.pallas_call(
         here_kernel,
-        out_shape=(chip_turned, jax.ShapeDtypeStruct(left.shape, BF16)),
+        out_shape=(jax.ShapeDtypeStruct(here_turned, BF16), jax.ShapeDtypeStruct(left.shape, BF16)),
         in_specs=[vmem] * 2,
         out_specs=(vmem, vmem),
         compiler_params=params(),
-        cost_estimate=chip_cost,
+        cost_estimate=part_cost,
         name="apply_rows_here",
     )(rotated_own, packed)
-    far_pieces = []
-    far_spots = ()
-    for n, start in enumerate(starts):
-        if n == 0:
-            crossed = firsts
-        elif n + 1 < len(starts):
-            crossed, turned = lax.optimization_barrier((chunk_hops[n][1:], turned))
-        else:
-            crossed, turned_own = lax.optimization_barrier((chunk_hops[n][1:], turned_own))
-        for hop, block in zip(hops[1:], crossed):
-            far_pieces += [block, to_sibling(block)]
-            far_spots += ((hop, 0, start), (hop, 1, start))
     parts = [turned_own]
-    for hop in hops[1:]:
-        parts.append(there(hop, parts))
-    partial = parts[-1]
+    mid_pieces = []
+    if mid_spots:
+        mid_pieces += relayed(firsts)
+        for crossing in chunk_hops[1:-1]:
+            crossed, turned = lax.optimization_barrier((crossing[1:], turned))
+            mid_pieces += relayed(crossed)
+        turned = rotate(mid_spots, mid_pieces, kron, turned)
+        crossed, turned, parts[0] = lax.optimization_barrier((chunk_hops[-1][1:], turned, parts[0]))
+        last_pieces = relayed(crossed)
+        mid_rotated, mid_turned = buffers(mid_spots)
+        parts.append(
+            pl.pallas_call(
+                there_kernel,
+                out_shape=jax.ShapeDtypeStruct(mid_turned, BF16),
+                in_specs=[vmem] * (len(mid_pieces) + 2),
+                out_specs=vmem,
+                scratch_shapes=[pltpu.VMEM(mid_rotated, BF16)],
+                compiler_params=params(),
+                cost_estimate=part_cost,
+                name="apply_rows_crossed",
+            )(*mid_pieces, right, kron_own)
+        )
+    else:
+        last_pieces = relayed(firsts)
+    last_rotated, last_turned = buffers(far_spots[-1])
+    partial = pl.pallas_call(
+        functools.partial(last_kernel, len(last_pieces)),
+        out_shape=whole_f32,
+        in_specs=[vmem] * (len(last_pieces) + 3 + len(parts)),
+        out_specs=vmem,
+        scratch_shapes=[pltpu.VMEM(last_rotated, BF16), pltpu.VMEM(last_turned, BF16)],
+        compiler_params=params(),
+        cost_estimate=part_cost,
+        name="apply_rows_last",
+    )(*last_pieces, right, kron_own, columns, *parts)
     norms = [norm_part]
     for hop in hops[1:]:
         if hop > 1:
             block, partial = lax.optimization_barrier((firsts[hop - 1], partial))
-            kron, norm_far = spread(block)
-            turned = rotate(kron)
-        norms.append(norm_far)
+            kron = spread(block)
+            turned = rotate(here_spots, here_pieces, kron, ())
+            if mid_spots:
+                turned = rotate(mid_spots, mid_pieces, kron, turned)
         left_far, partial = lax.optimization_barrier((lefts[hop], partial))
-        mixed, _, vector = pl.pallas_call(
-            functools.partial(lefts_kernel, far_spots, rows, chips),
-            out_shape=(jax.ShapeDtypeStruct((states, width, terms * width), BF16), rotated_bf, whole_bf),
-            in_specs=[vmem] * (len(far_pieces) + 1) + [anywhere] * 2 + [vmem],
-            out_specs=(vmem,) * 3,
-            scratch_shapes=[square, pltpu.SemaphoreType.DMA((len(far_pieces),))],
-            input_output_aliases={len(far_pieces) + 1: 1, len(far_pieces) + 2: 2},
+        mixed, norm_far, _, vector = pl.pallas_call(
+            functools.partial(lefts_kernel, far_spots[-1], rows, chips),
+            out_shape=(jax.ShapeDtypeStruct((states, width, terms * width), BF16), tile, rotated_bf, whole_bf),
+            in_specs=[vmem] * (len(last_pieces) + 1) + [anywhere] * 2 + [vmem],
+            out_specs=(vmem,) * 4,
+            scratch_shapes=[square, pltpu.SemaphoreType.DMA((len(last_pieces),))],
+            input_output_aliases={len(last_pieces) + 1: 2, len(last_pieces) + 2: 3},
             compiler_params=params(),
             cost_estimate=cost(stage_flops, 12 * states * width * width),
             name="received_lefts",
-        )(*far_pieces, kron, *turned, left_far)
+        )(*last_pieces, kron, *turned, left_far)
+        norms.append(norm_far)
         last = hop == hops[-1]
         stats = norms if last else norms[:1]
         right_far = rights[hop]
@@ -641,7 +691,7 @@
         cost_estimate=cost(3 * stage_flops, 6 * states * width * width),
         name="apply_residual",
     )(keep, stat, stat_other, *halves, vector, left, right, kron_own)
-    shares = everyone(share)
+    crossed = everyone(share)
 
     local = jax.ShapeDtypeStruct((rows, states, width), F32)
     vector_own, residual_own = pl.pallas_call(
@@ -654,6 +704,9 @@
         name="own_rows",
     )(keep, guess, stat, stat_other, *halves)
 
+    shares = [share, to_sibling(share)]
+    gated, residual_own = lax.optimization_barrier((crossed[1:], residual_own))
+    shares += relayed(gated)
     ritz, energy = pl.pallas_call(
         finish_kernel,
         out_shape=(local, jax.ShapeDtypeStruct((1,), F32)),

time: 46.5 us -> 46 us (0.989)
  waiting for transfers between devices: 9.07 us -> 7.43 us
  Pallas kernels: 24 us -> 25.3 us
    ppermute x5, waiting for transfers between devices: 2.68 us -> 0.94 us  [to_next_chip(): lax.ppermute(block, 'term', [(i, (i + CORES) % members) for i in range(me...]
    ppermute x1, waiting for transfers between devices: 0.01 us -> 1.73 us  [shards(): received = lax.ppermute(right_packed, 'seg', shift)]
    ppermute x3 -> x1, waiting for transfers between devices: 2.95 us -> 1.47 us  [everyone(): lax.ppermute(block, 'term', [(i, i ^ bits) for i in range(members)])]
    pallas_call x8 -> x11, Pallas kernels: 13.9 us -> 15.2 us  [the longest x1 2.77 us: shards(): pl.pallas_call(functools.partial(lefts_kernel, far_spots[-1], rows, chips...]
    ppermute x3 -> x1, starting transfers between devices: 2.12 us -> 1.83 us  [everyone(): lax.ppermute(block, 'term', [(i, i ^ bits) for i in range(members)])]
    ppermute x7 -> x10, starting transfers between devices: 1.54 us -> 1.79 us  [to_sibling(): return lax.ppermute(block, 'term', [(i, i ^ 1) for i in range(members)])]
    ppermute x7 -> x10, waiting for transfers between devices: 3.43 us -> 3.29 us  [to_sibling(): return lax.ppermute(block, 'term', [(i, i ^ 1) for i in range(members)])]
  transfers between devices with their start and end apart: 16 -> 17, of which waited for: 7 -> 7; matrix products, arithmetic and copies ran while one was open for 0% -> 0% of each run, Pallas kernels for 30% -> 33%
where the time goes in v9:
time: 46 us; the launch traced here: 45.7 us
  Pallas kernels  25.3 us (55%)
  starting transfers between devices  11.3 us (25%)
  waiting for transfers between devices  7.43 us (16%)
  between operations  1.63 us (4%)
    ppermute x5, starting transfers between devices, to_next_chip(): lax.ppermute(block, 'term', [(i, (i + CORES) % members) for i in range(me...  6.38 us
    pallas_call x1, Pallas kernels, shards(): pl.pallas_call(functools.partial(second_kernel, scale, members), out_shap...  5.78 us
    ppermute x10, waiting for transfers between devices, to_sibling(): return lax.ppermute(block, 'term', [(i, i ^ 1) for i in range(members)])  3.29 us
    pallas_call x1, Pallas kernels, shards(): pl.pallas_call(functools.partial(lefts_kernel, far_spots[-1], rows, chips...  2.77 us
    pallas_call x1, Pallas kernels, shards(): pl.pallas_call(functools.partial(last_kernel, len(last_pieces)), out_shap...  2.54 us
    pallas_call x2, Pallas kernels, shards(): pl.pallas_call(functools.partial(rights_kernel, start, stop), out_shape=t...  2.47 us
    pallas_call x2, Pallas kernels, rotate(): pl.pallas_call(functools.partial(rotate_kernel, spots, rows, chips), out_...  2.38 us
    pallas_call x1, Pallas kernels, shards(): pl.pallas_call(first_chunk_kernel, out_shape=(jax.ShapeDtypeStruct((state...  1.84 us
  transfers between devices with their start and end apart: 17, of which 7 were waited for; matrix products, arithmetic and copies ran while one was open for 0% of the time, Pallas kernels for 33%

profile of v9, /device:TPU:0, one launch (start us, length us, event | category | flops | bytes accessed | tf_op | source)
XLA Modules:
  0.0 45.7 jit_solution(12579094455267496119)
XLA Ops:
  1.3 1.8 %first_chunk.1 = (bf16[17,32,256]{2,1,0:T(8,128)(2,1)S(1)}, f32[8,256]{1,0:T(8,128)S(1)}, f32[8,256]{1,0:T(8,128)S(1)}) custom-call(s32[1,1]{1,0:T(1,128)} %bitcast.6.rank_ref, f32[64,16,256]{2,1,0:T(8,128)} %bitcast.7, bf16[3,16,16]{2,1,0:T(8,128)(2,1)} %bitcast.12), custom_call_target="tpu_custom_call" | custom-call | flops 5242 | bytes 7864 | tf_op jit(solution)/shard_map/first_chunk/pallas_call | solution.py:459
  3.1 0.5 %collective-permute-start.1 = (bf16[17,32,256]{2,1,0:T(8,128)(2,1)S(1)}, bf16[17,32,256]{2,1,0:T(8,128)(2,1)S(1)}, u32[]{:S(2)}, u32[]{:S(2)}) collective-permute-start(bf16[17,32,256]{2,1,0:T(8,128)(2,1)S(1)} %get-tuple-element.51.chunk_ref.refs_0_), channel_id=1, source_target_pairs={{0,1},{1,0},{2,3},{3,2},{4,5},{5,4},{6,7},{7,6},{8,9},{9,8},{10,11... | collective-permute-start | bytes 835592 | tf_op jit(solution)/shard_map/ppermute | solution.py:436
  3.6 2.6 %collective-permute-start.3 = (bf16[17,32,256]{2,1,0:T(8,128)(2,1)S(1)}, bf16[17,32,256]{2,1,0:T(8,128)(2,1)S(1)}, u32[]{:S(2)}, u32[]{:S(2)}) collective-permute-start(bf16[17,32,256]{2,1,0:T(8,128)(2,1)S(1)} %get-tuple-element.51.chunk_ref.refs_0_), channel_id=1, source_target_pairs={{0,2},{1,3},{2,0},{3,1},{4,6},{5,7},{6,4},{7,5},{8,10},{9,11},{10,... | collective-permute-start | bytes 835592 | tf_op jit(solution)/shard_map/ppermute | solution.py:439
  6.2 1.4 %prepare.1 = (f32[8,256]{1,0:T(8,128)S(1)}, bf16[3,272,128]{2,1,0:T(8,128)(2,1)S(1)}, bf16[3,272,128]{2,1,0:T(8,128)(2,1)S(1)}, bf16[3,256,256]{2,1,0:T(8,128)(2...) custom-call(f32[8,256]{1,0:T(8,128)S(1)} %get-tuple-element.48.keep_re, ...), custom_call_target="tpu_custom_call" | custom-call | flops 10485 | bytes 15728 | tf_op jit(solution)/shard_map/prepare/pallas_call | solution.py:473
  7.7 0.2 collective-permute-start.2
  7.9 1.3 %collective-permute-start = (bf16[3,272,128]{2,1,0:T(8,128)(2,1)S(1)}, bf16[3,272,128]{2,1,0:T(8,128)(2,1)S(1)}, u32[]{:S(2)}, u32[]{:S(2)}) collective-permute-start(bf16[3,272,128]{2,1,0:T(8,128)(2,1)S(1)} %get-tuple-element.50), channel_id=1, source_target_pairs={{4,0},{8,4},{12,8},{16,12},{20,16},{24,20},{28,24},{5,1},{9,5},{13... | collective-permute-start | bytes 626696 | tf_op jit(solution)/shard_map/ppermute | solution.py:513
  9.2 0.3 collective-permute-start.7
  9.5 0.4 spread_site.2.refs_4_.refs_5_.refs_3_.kron_ref
  9.9 0.0 collective-permute-done.2.refs_3_
  9.9 1.8 %collective-permute-start.5 = (bf16[16,16,256]{2,1,0:T(8,128)(2,1)S(1)}, bf16[16,16,256]{2,1,0:T(8,128)(2,1)S(1)}, u32[]{:S(2)}, u32[]{:S(2)}) collective-permute-start(bf16[16,16,256]{2,1,0:T(8,128)(2,1)S(1)} %get-tuple-element.59), channel_id=1, source_target_pairs={{0,2},{1,3},{2,0},{3,1},{4,6},{5,7},{6,4},{7,5},{8,10},{9,11},{10,... | collective-permute-start | bytes 393224 | tf_op jit(solution)/shard_map/ppermute | solution.py:439
  11.8 0.0 collective-permute-done.1.refs_2_
  11.8 0.3 collective-permute-start.10
  12.0 1.0 %rotate_own.1 = (bf16[3,16,128,256]{3,2,1,0:T(8,128)(2,1)S(1)}, bf16[256,768]{1,0:T(8,128)(2,1)S(1)}) custom-call(bf16[17,32,256]{2,1,0:T(8,128)(2,1)S(1)} %get-tuple-element.51.chunk_ref.refs_0_, bf16[16,32,256]{2,1,0:T(8,128)(2,1)S(1)} %get-tuple-element.52.refs_1_, bf16[17,32,256]{2,1,0:T(8,128)(2,1)S(1)} %collective-permute-done.1.refs_2_, ...), custom_call_target="tpu_custom_call" | custom-call | flops 16106127 | bytes 83886 | tf_op jit(solution)/shard_map/rotate_own/pallas_call | solution.py:545
  13.0 0.7 %collective-permute-done.3.chunk_ref.refs_0_ = bf16[17,32,256]{2,1,0:T(8,128)(2,1)S(1)} collective-permute-done((bf16[17,32,256]{2,1,0:T(8,128)(2,1)S(1)}, bf16[17,32,256]{2,1,0:T(8,128)(2,1)S(1)}, u32[]{:S(2)}, u32[]{:S(2)}) %collective-permute-start.3) | collective-permute-done | bytes 278560 | tf_op jit(solution)/shard_map/ppermute | solution.py:439
  13.7 0.0 collective-permute-start.6
  13.8 0.4 spread_site.3.refs_4_.refs_2_
  14.1 1.3 %rotate_here.1 = (bf16[3,16,256,256]{3,2,1,0:T(8,128)(2,1)S(1)}, bf16[16,256,256]{2,1,0:T(8,128)(2,1)S(1)}) custom-call(bf16[17,32,256]{2,1,0:T(8,128)(2,1)S(1)} %get-tuple-element.51.chunk_ref.refs_0_, bf16[16,32,256]{2,1,0:T(8,128)(2,1)S(1)} %get-tuple-element.52.refs_1_, bf16[17,32,256]{2,1,0:T(8,128)(2,1)S(1)} %collective-permute-done.1.refs_2_, ...), custom_call_target="tpu_custom_call" | custom-call | flops 16106127 | bytes 83886 | tf_op jit(solution)/shard_map/rotate_here/pallas_call | solution.py:559
  15.5 1.7 %collective-permute-done = bf16[3,272,128]{2,1,0:T(8,128)(2,1)S(1)} collective-permute-done((bf16[3,272,128]{2,1,0:T(8,128)(2,1)S(1)}, bf16[3,272,128]{2,1,0:T(8,128)(2,1)S(1)}, u32[]{:S(2)}, u32[]{:S(2)}) %collective-permute-start) | collective-permute-done | bytes 208928 | tf_op jit(solution)/shard_map/ppermute | solution.py:513
  17.2 0.0 collective-permute-done.7.refs_2_
  17.2 0.0 collective-permute-start.8
  17.2 1.4 %collective-permute-start.4 = (bf16[3,272,128]{2,1,0:T(8,128)(2,1)S(1)}, bf16[3,272,128]{2,1,0:T(8,128)(2,1)S(1)}, u32[]{:S(2)}, u32[]{:S(2)}) collective-permute-start(bf16[3,272,128]{2,1,0:T(8,128)(2,1)S(1)} %broadcast_select_fusion.packed_ref), channel_id=1, source_target_pairs={{0,2},{1,3},{2,0},{3,1},{4,6},{5,7},{6,4},{7,5},{8,10},{9,11},{10,... | collective-permute-start | bytes 626696 | tf_op jit(solution)/shard_map/ppermute | solution.py:439
  18.6 1.1 %apply_rows_here.1 = (bf16[16,384,256]{2,1,0:T(8,128)(2,1)S(1)}, bf16[3,256,256]{2,1,0:T(8,128)(2,1)S(1)}) custom-call(bf16[3,16,128,256]{3,2,1,0:T(8,128)(2,1)S(1)} %get-tuple-element.68.rotated_ref, bf16[3,272,128]{2,1,0:T(8,128)(2,1)S(1)} %broadcast_select_fusion.packed_ref), custom_call_target="tpu_custom_call" | custom-call | flops 16106127 | bytes 83886 | tf_op jit(solution)/shard_map/apply_rows_here/pallas_call | solution.py:580
  19.7 0.0 collective-permute-done.8.refs_3_
  19.7 0.0 collective-permute-done.6.refs_1_
  19.7 1.1 %rotate_crossed.1 = (bf16[3,16,256,256]{3,2,1,0:T(8,128)(2,1)S(1)}, bf16[16,256,256]{2,1,0:T(8,128)(2,1)S(1)}) custom-call(bf16[17,32,256]{2,1,0:T(8,128)(2,1)S(1)} %collective-permute-done.3.chunk_ref.refs_0_, bf16[17,32,256]{2,1,0:T(8,128)(2,1)S(1)} %collective-permute-done.6.refs_1_, ...), custom_call_target="tpu_custom_call", output_to_operand_aliasing={{0}: (5, {}), {1}: (6, {})} | custom-call | flops 16106127 | bytes 83886 | tf_op jit(solution)/shard_map/rotate_crossed/pallas_call | solution.py:559
  20.8 0.0 collective-permute-done.5.refs_0_
  20.8 0.3 collective-permute-start.9
  21.1 1.4 %apply_rows_crossed.1.refs_6_ = bf16[16,288,256]{2,1,0:T(8,128)(2,1)S(1)} custom-call(bf16[17,32,256]{2,1,0:T(8,128)(2,1)S(1)} %collective-permute-done.3.chunk_ref.refs_0_, bf16[17,32,256]{2,1,0:T(8,128)(2,1)S(1)} %collective-permute-done.6.refs_1_, bf16[16,16,256]{2,1,0:T(8,128)(2,1)S(1)} %collective-permute-done.7.refs_2_, ...), custom_call_target="tpu_custom_call" | custom-call | flops 16106127 | bytes 83886 | tf_op jit(solution)/shard_map/apply_rows_crossed/pallas_call | solution.py:601
  22.5 0.0 collective-permute-done.9.refs_1_
  22.5 2.5 %apply_rows_last.1.before_ref = f32[16,256,256]{2,1,0:T(8,128)S(1)} custom-call(bf16[16,16,256]{2,1,0:T(8,128)(2,1)S(1)} %collective-permute-done.5.refs_0_, bf16[16,16,256]{2,1,0:T(8,128)(2,1)S(1)} %collective-permute-done.9.refs_1_, bf16[3,256,256]{2,1,0:T(8,128)(2,1)S(1)} %get-tuple-element.74.refs_4_.refs_2_.right_ref, ...), custom_call_target="tpu_custom_call" | custom-call | flops 16106127 | bytes 83886 | tf_op jit(solution)/shard_map/apply_rows_last/pallas_call | solution.py:615
  25.1 0.0 collective-permute-done.10.refs_5_
  25.1 2.8 %received_lefts.1 = (bf16[16,256,768]{2,1,0:T(8,128)(2,1)S(1)}, f32[8,256]{1,0:T(8,128)S(1)}, bf16[3,16,256,256]{3,2,1,0:T(8,128)(2,1)S(1)}, bf16[16,256,256]{2,1,0:T(8,128)(2,1)S(1)}) custom-call(bf16[16,16,256]{2,1,0:T(8,128)(2,1)S(1)} %collective-permute-done.5.refs_0_, ...), custom_call_target="tpu_custom_call", output_to_operand_aliasing={{2}: (3, {}), {3}: (4, {})} | custom-call | flops 16106127 | bytes 125829 | tf_op jit(solution)/shard_map/received_lefts/pallas_call | solution.py:634
  27.9 0.2 collective-permute-done.4.packed_ref
  28.1 1.3 %received_rights.2 = (bf16[8,256,256]{2,1,0:T(8,128)(2,1)S(1)}, f32[8,256]{1,0:T(8,128)S(1)}, bf16[3,256,256]{2,1,0:T(8,128)(2,1)S(1)}) custom-call(bf16[3,272,128]{2,1,0:T(8,128)(2,1)S(1)} %collective-permute-done.4.packed_ref, bf16[16,256,768]{2,1,0:T(8,128)(2,1)S(1)} %get-tuple-element.78.mixed_ref, ...), custom_call_target="tpu_custom_call" | custom-call | flops 8053063 | bytes 125829 | tf_op jit(solution)/shard_map/received_rights/pallas_call | solution.py:653
  29.4 0.1 collective-permute-start.12
  29.5 1.2 %received_rights.3 = (bf16[8,256,256]{2,1,0:T(8,128)(2,1)S(1)}, f32[8,256]{1,0:T(8,128)S(1)}) custom-call(bf16[3,256,256]{2,1,0:T(8,128)(2,1)S(1)} %get-tuple-element.83.packed_ref, bf16[16,256,768]{2,1,0:T(8,128)(2,1)S(1)} %get-tuple-element.78.mixed_ref, bf16[16,256,256]{2,1,0:T(8,128)(2,1)S(1)} %get-tuple-element.79.whole_ref, ...), custom_call_target="tpu_custom_call" | custom-call | flops 8053063 | bytes 125829 | tf_op jit(solution)/shard_map/received_rights/pallas_call | solution.py:653
  30.7 0.5 %collective-permute-start.13 = (bf16[8,256,256]{2,1,0:T(8,128)(2,1)S(1)}, bf16[8,256,256]{2,1,0:T(8,128)(2,1)S(1)}, u32[]{:S(2)}, u32[]{:S(2)}) collective-permute-start(bf16[8,256,256]{2,1,0:T(8,128)(2,1)S(1)} %get-tuple-element.87.refs_1_.high_ref), channel_id=1, source_target_pairs={{0,1},{1,0},{2,3},{3,2},{4,5},{5,4},{6,7},{7,6},{8,9},{9,8},{10,11... | collective-permute-start | bytes 3145736 | tf_op jit(solution)/shard_map/ppermute | solution.py:436
  31.2 0.1 collective-permute-start.11
  31.3 0.8 %collective-permute-done.12.other_ref = bf16[8,256,256]{2,1,0:T(8,128)(2,1)S(1)} collective-permute-done((bf16[8,256,256]{2,1,0:T(8,128)(2,1)S(1)}, bf16[8,256,256]{2,1,0:T(8,128)(2,1)S(1)}, u32[]{:S(2)}, u32[]{:S(2)}) %collective-permute-start.12) | collective-permute-done | bytes 1048608 | tf_op jit(solution)/shard_map/ppermute | solution.py:436
  32.1 0.2 add_low_half.1.refs_0_.low_ref
  32.3 0.0 copy-start
  32.3 1.3 %collective-permute-done.11.theirs_ref = f32[8,256]{1,0:T(8,128)S(1)} collective-permute-done((f32[8,256]{1,0:T(8,128)S(1)}, f32[8,256]{1,0:T(8,128)S(1)}, u32[]{:S(2)}, u32[]{:S(2)}) %collective-permute-start.11) | collective-permute-done | bytes 8224 | tf_op jit(solution)/shard_map/ppermute | solution.py:436
  33.6 0.0 collective-permute-done.13.refs_2_.high_other_ref
  33.6 5.8 %apply_residual.1.refs_0_ = f32[8,256]{1,0:T(8,128)S(1)} custom-call(f32[8,256]{1,0:T(8,128)S(1)} %get-tuple-element.48.keep_ref, f32[8,256]{1,0:T(8,128)S(1)} %get-tuple-element.85.mine_ref, f32[8,256]{1,0:T(8,128)S(1)} %collective-permute-done.11.theirs_ref, f32[8,256,256]{2,1,0:T(8,128)S(1)} %add_low_half.1.refs_0_.low_ref, ...), custom_call_target="tpu_custom_call" | custom-call | flops 48318384 | bytes 62914 | tf_op jit(solution)/shard_map/apply_residual/pallas_call | solution.py:680
  39.4 1.8 %collective-permute-start.14 = (f32[8,256]{1,0:T(8,128)S(1)}, f32[8,256]{1,0:T(8,128)S(1)}, u32[]{:S(2)}, u32[]{:S(2)}) collective-permute-start(f32[8,256]{1,0:T(8,128)S(1)} %apply_residual.1.refs_0_), channel_id=1, source_target_pairs={{0,2},{1,3},{2,0},{3,1},{4,6},{5,7},{6,4},{7,5},{8,10},{9,11},{10,... | collective-permute-start | bytes 24584 | tf_op jit(solution)/shard_map/ppermute | solution.py:449
  41.2 0.0 collective-permute-start.15
  41.2 0.0 copy-done
  41.2 0.4 own_rows.1
  41.6 1.5 %collective-permute-done.14.refs_2_ = f32[8,256]{1,0:T(8,128)S(1)} collective-permute-done((f32[8,256]{1,0:T(8,128)S(1)}, f32[8,256]{1,0:T(8,128)S(1)}, u32[]{:S(2)}, u32[]{:S(2)}) %collective-permute-start.14) | collective-permute-done | bytes 8224 | tf_op jit(solution)/shard_map/ppermute | solution.py:449
  43.1 0.0 collective-permute-start.16
  43.1 0.0 collective-permute-done.15.refs_1_
  43.1 1.2 %collective-permute-done.16.refs_3_ = f32[8,256]{1,0:T(8,128)S(1)} collective-permute-done((f32[8,256]{1,0:T(8,128)S(1)}, f32[8,256]{1,0:T(8,128)S(1)}, u32[]{:S(2)}, u32[]{:S(2)}) %collective-permute-start.16) | collective-permute-done | bytes 8224 | tf_op jit(solution)/shard_map/ppermute | solution.py:436
  44.3 1.3 %finish.1 = (f32[64,16,256]{2,1,0:T(8,128)}, f32[1]{0:T(128)}) custom-call(f32[64,16,256]{2,1,0:T(8,128)S(1)} %get-tuple-element.88.vector_ref, f32[64,16,256]{2,1,0:T(8,128)S(1)} %get-tuple-element.90.residual_ref, f32[8,256]{1,0:T(8,128)S(1)} %apply_residual.1.refs_0_, f32[8,256]{1,0:T(8,128)S(1)} %collective-permute-done.15.refs_1_, ...), custom_call_target="tpu_custom_call" | custom-call | flops 7864 | bytes 31457 | tf_op jit(solution)/shard_map/finish/pallas_call | solution.py:710
  (1 shorter events, 0.0 us)
Async XLA Ops:
  3.1 8.6 %collective-permute-start.1 = (bf16[17,32,256]{2,1,0:T(8,128)(2,1)S(1)}, bf16[17,32,256]{2,1,0:T(8,128)(2,1)S(1)}, u32[]{:S(2)}, u32[]{:S(2)}) collective-permute-start(bf16[17,32,256]{2,1,0:T(8,128)(2,1)S(1)} %get-tuple-element.51.chunk_ref.refs_0_), channel_id=1, source_target_pairs={{0,1},{1,0},{2,3},{3,2},{4,5},{5,4},{6,7},{7,6},{8,9},{9,8},{10,11... | collective-permute-start | bytes 835592 | tf_op jit(solution)/shard_map/ppermute | solution.py:436
  3.6 10.1 %collective-permute-start.3 = (bf16[17,32,256]{2,1,0:T(8,128)(2,1)S(1)}, bf16[17,32,256]{2,1,0:T(8,128)(2,1)S(1)}, u32[]{:S(2)}, u32[]{:S(2)}) collective-permute-start(bf16[17,32,256]{2,1,0:T(8,128)(2,1)S(1)} %get-tuple-element.51.chunk_ref.refs_0_), channel_id=1, source_target_pairs={{0,2},{1,3},{2,0},{3,1},{4,6},{5,7},{6,4},{7,5},{8,10},{9,11},{10,... | collective-permute-start | bytes 835592 | tf_op jit(solution)/shard_map/ppermute | solution.py:439
  7.7 2.2 %collective-permute-start.2 = (bf16[16,32,256]{2,1,0:T(8,128)(2,1)S(1)}, bf16[16,32,256]{2,1,0:T(8,128)(2,1)S(1)}, u32[]{:S(2)}, u32[]{:S(2)}) collective-permute-start(bf16[16,32,256]{2,1,0:T(8,128)(2,1)S(1)} %get-tuple-element.52.refs_1_), channel_id=1, source_target_pairs={{0,1},{1,0},{2,3},{3,2},{4,5},{5,4},{6,7},{7,6},{8,9},{9,8},{10,11... | collective-permute-start | bytes 786440 | tf_op jit(solution)/shard_map/ppermute | solution.py:436
  7.9 9.3 %collective-permute-start = (bf16[3,272,128]{2,1,0:T(8,128)(2,1)S(1)}, bf16[3,272,128]{2,1,0:T(8,128)(2,1)S(1)}, u32[]{:S(2)}, u32[]{:S(2)}) collective-permute-start(bf16[3,272,128]{2,1,0:T(8,128)(2,1)S(1)} %get-tuple-element.50), channel_id=1, source_target_pairs={{4,0},{8,4},{12,8},{16,12},{20,16},{24,20},{28,24},{5,1},{9,5},{13... | collective-permute-start | bytes 626696 | tf_op jit(solution)/shard_map/ppermute | solution.py:513
  9.2 8.0 %collective-permute-start.7 = (bf16[16,16,256]{2,1,0:T(8,128)(2,1)S(1)}, bf16[16,16,256]{2,1,0:T(8,128)(2,1)S(1)}, u32[]{:S(2)}, u32[]{:S(2)}) collective-permute-start(bf16[16,16,256]{2,1,0:T(8,128)(2,1)S(1)} %get-tuple-element.60), channel_id=1, source_target_pairs={{0,2},{1,3},{2,0},{3,1},{4,6},{5,7},{6,4},{7,5},{8,10},{9,11},{10,... | collective-permute-start | bytes 393224 | tf_op jit(solution)/shard_map/ppermute | solution.py:439
  9.9 10.9 %collective-permute-start.5 = (bf16[16,16,256]{2,1,0:T(8,128)(2,1)S(1)}, bf16[16,16,256]{2,1,0:T(8,128)(2,1)S(1)}, u32[]{:S(2)}, u32[]{:S(2)}) collective-permute-start(bf16[16,16,256]{2,1,0:T(8,128)(2,1)S(1)} %get-tuple-element.59), channel_id=1, source_target_pairs={{0,2},{1,3},{2,0},{3,1},{4,6},{5,7},{6,4},{7,5},{8,10},{9,11},{10,... | collective-permute-start | bytes 393224 | tf_op jit(solution)/shard_map/ppermute | solution.py:439
  11.8 13.3 %collective-permute-start.10 = (bf16[3,272,128]{2,1,0:T(8,128)(2,1)S(1)}, bf16[3,272,128]{2,1,0:T(8,128)(2,1)S(1)}, u32[]{:S(2)}, u32[]{:S(2)}) collective-permute-start(bf16[3,272,128]{2,1,0:T(8,128)(2,1)S(1)} %get-tuple-element.73), channel_id=1, source_target_pairs={{0,2},{1,3},{2,0},{3,1},{4,6},{5,7},{6,4},{7,5},{8,10},{9,11},{10,... | collective-permute-start | bytes 626696 | tf_op jit(solution)/shard_map/ppermute | solution.py:439
  13.7 6.0 %collective-permute-start.6 = (bf16[17,32,256]{2,1,0:T(8,128)(2,1)S(1)}, bf16[17,32,256]{2,1,0:T(8,128)(2,1)S(1)}, u32[]{:S(2)}, u32[]{:S(2)}) collective-permute-start(bf16[17,32,256]{2,1,0:T(8,128)(2,1)S(1)} %collective-permute-done.3.chunk_ref.refs_0_), channel_id=1, source_target_pairs={{0,1},{1,0},{2,3},{3,2},{4,5},{5,4},{6,7},{7,6},{8,9},{9,8},{10,11... | collective-permute-start | bytes 835592 | tf_op jit(solution)/shard_map/ppermute | solution.py:436
  17.2 2.5 %collective-permute-start.8 = (bf16[16,16,256]{2,1,0:T(8,128)(2,1)S(1)}, bf16[16,16,256]{2,1,0:T(8,128)(2,1)S(1)}, u32[]{:S(2)}, u32[]{:S(2)}) collective-permute-start(bf16[16,16,256]{2,1,0:T(8,128)(2,1)S(1)} %collective-permute-done.7.refs_2_), channel_id=1, source_target_pairs={{0,1},{1,0},{2,3},{3,2},{4,5},{5,4},{6,7},{7,6},{8,9},{9,8},{10,11... | collective-permute-start | bytes 393224 | tf_op jit(solution)/shard_map/ppermute | solution.py:436
  17.2 10.8 %collective-permute-start.4 = (bf16[3,272,128]{2,1,0:T(8,128)(2,1)S(1)}, bf16[3,272,128]{2,1,0:T(8,128)(2,1)S(1)}, u32[]{:S(2)}, u32[]{:S(2)}) collective-permute-start(bf16[3,272,128]{2,1,0:T(8,128)(2,1)S(1)} %broadcast_select_fusion.packed_ref), channel_id=1, source_target_pairs={{0,2},{1,3},{2,0},{3,1},{4,6},{5,7},{6,4},{7,5},{8,10},{9,11},{10,... | collective-permute-start | bytes 626696 | tf_op jit(solution)/shard_map/ppermute | solution.py:439
  20.8 1.7 %collective-permute-start.9 = (bf16[16,16,256]{2,1,0:T(8,128)(2,1)S(1)}, bf16[16,16,256]{2,1,0:T(8,128)(2,1)S(1)}, u32[]{:S(2)}, u32[]{:S(2)}) collective-permute-start(bf16[16,16,256]{2,1,0:T(8,128)(2,1)S(1)} %collective-permute-done.5.refs_0_), channel_id=1, source_target_pairs={{0,1},{1,0},{2,3},{3,2},{4,5},{5,4},{6,7},{7,6},{8,9},{9,8},{10,11... | collective-permute-start | bytes 393224 | tf_op jit(solution)/shard_map/ppermute | solution.py:436
  29.4 2.7 %collective-permute-start.12 = (bf16[8,256,256]{2,1,0:T(8,128)(2,1)S(1)}, bf16[8,256,256]{2,1,0:T(8,128)(2,1)S(1)}, u32[]{:S(2)}, u32[]{:S(2)}) collective-permute-start(bf16[8,256,256]{2,1,0:T(8,128)(2,1)S(1)} %get-tuple-element.86.mine_ref), channel_id=1, source_target_pairs={{0,1},{1,0},{2,3},{3,2},{4,5},{5,4},{6,7},{7,6},{8,9},{9,8},{10,11... | collective-permute-start | bytes 3145736 | tf_op jit(solution)/shard_map/ppermute | solution.py:436
  30.7 2.9 %collective-permute-start.13 = (bf16[8,256,256]{2,1,0:T(8,128)(2,1)S(1)}, bf16[8,256,256]{2,1,0:T(8,128)(2,1)S(1)}, u32[]{:S(2)}, u32[]{:S(2)}) collective-permute-start(bf16[8,256,256]{2,1,0:T(8,128)(2,1)S(1)} %get-tuple-element.87.refs_1_.high_ref), channel_id=1, source_target_pairs={{0,1},{1,0},{2,3},{3,2},{4,5},{5,4},{6,7},{7,6},{8,9},{9,8},{10,11... | collective-permute-start | bytes 3145736 | tf_op jit(solution)/shard_map/ppermute | solution.py:436
  31.2 2.4 %collective-permute-start.11 = (f32[8,256]{1,0:T(8,128)S(1)}, f32[8,256]{1,0:T(8,128)S(1)}, u32[]{:S(2)}, u32[]{:S(2)}) collective-permute-start(f32[8,256]{1,0:T(8,128)S(1)} %get-tuple-element.85.mine_ref), channel_id=1, source_target_pairs={{0,1},{1,0},{2,3},{3,2},{4,5},{5,4},{6,7},{7,6},{8,9},{9,8},{10,11... | collective-permute-start | bytes 24584 | tf_op jit(solution)/shard_map/ppermute | solution.py:436
  32.3 8.9 %copy-start = (f32[1,64,16,256]{3,2,1,0:T(8,128)S(1)}, f32[1,64,16,256]{3,2,1,0:T(8,128)}, u32[]{:S(2)}) copy-start(f32[1,64,16,256]{3,2,1,0:T(8,128)} %param.5) | copy-start | bytes 3145732
  39.4 3.7 %collective-permute-start.14 = (f32[8,256]{1,0:T(8,128)S(1)}, f32[8,256]{1,0:T(8,128)S(1)}, u32[]{:S(2)}, u32[]{:S(2)}) collective-permute-start(f32[8,256]{1,0:T(8,128)S(1)} %apply_residual.1.refs_0_), channel_id=1, source_target_pairs={{0,2},{1,3},{2,0},{3,1},{4,6},{5,7},{6,4},{7,5},{8,10},{9,11},{10,... | collective-permute-start | bytes 24584 | tf_op jit(solution)/shard_map/ppermute | solution.py:449
  41.2 1.9 %collective-permute-start.15 = (f32[8,256]{1,0:T(8,128)S(1)}, f32[8,256]{1,0:T(8,128)S(1)}, u32[]{:S(2)}, u32[]{:S(2)}) collective-permute-start(f32[8,256]{1,0:T(8,128)S(1)} %apply_residual.1.refs_0_), channel_id=1, source_target_pairs={{0,1},{1,0},{2,3},{3,2},{4,5},{5,4},{6,7},{7,6},{8,9},{9,8},{10,11... | collective-permute-start | bytes 24584 | tf_op jit(solution)/shard_map/ppermute | solution.py:436
  43.1 1.2 %collective-permute-start.16 = (f32[8,256]{1,0:T(8,128)S(1)}, f32[8,256]{1,0:T(8,128)S(1)}, u32[]{:S(2)}, u32[]{:S(2)}) collective-permute-start(f32[8,256]{1,0:T(8,128)S(1)} %collective-permute-done.14.refs_2_), channel_id=1, source_target_pairs={{0,1},{1,0},{2,3},{3,2},{4,5},{5,4},{6,7},{7,6},{8,9},{9,8},{10,11... | collective-permute-start | bytes 24584 | tf_op jit(solution)/shard_map/ppermute | solution.py:436

commit v10 on v9

--- a/solution.py
+++ b/solution.py
@@ -34,22 +34,53 @@
     return jnp.sum(values.reshape(values.size // (8 * width), 8, width), axis=0)
 
 
-def chunk_rows_in(guess_in, guess_ref, sems, start, stop):
+def chunk_rows_in(guess_in, guess_ref, sems, start, stop, slot):
     copies = []
     for n in range(start, stop, TILE):
-        part = pl.ds(n, TILE)
-        copies.append(pltpu.make_async_copy(guess_in.at[part], guess_ref.at[pl.ds(n - start, TILE)], sems.at[n // TILE]))
+        target = guess_ref.at[pl.ds(n - start, TILE)]
+        copies.append(pltpu.make_async_copy(guess_in.at[pl.ds(n, TILE)], target, sems.at[slot + len(copies)]))
         copies[-1].start()
     return copies
 
 
-def first_chunk_kernel(rank_ref, guess_in, site_ref, x_ref, keep_ref, squares_ref, guess_ref, sems):
+def first_chunk_kernel(
+    rank_in,
+    guess_in,
+    site_in,
+    right_in,
+    x_ref,
+    keep_ref,
+    squares_ref,
+    packed_ref,
+    rank_ref,
+    guess_ref,
+    site_ref,
+    right_ref,
+    sems,
+):
     rows, states, width = guess_ref.shape
     terms = site_ref.shape[0]
-    copies = chunk_rows_in(guess_in, guess_ref, sems, 0, rows)
+    copies = [
+        pltpu.make_async_copy(source, target, sems.at[n])
+        for n, (source, target) in enumerate(((rank_in, rank_ref), (site_in, site_ref), (right_in, right_ref)))
+    ]
+    copies[0].start()
+    parts = chunk_rows_in(guess_in, guess_ref, sems, 0, rows, 3)
+    copies[1].start()
+    copies[2].start()
+    copies[0].wait()
     column = lax.broadcasted_iota(jnp.int32, (1, width), 1)
     keep = (column < rank_ref[...]).astype(F32)
     keep_ref[...] = jnp.broadcast_to(keep, keep_ref.shape)
+    squares = jnp.zeros((8, width), F32)
+    for n, copy in enumerate(parts):
+        copy.wait()
+        part = pl.ds(n * TILE, TILE)
+        masked = guess_ref[part] * keep[None]
+        squares = squares + fold(masked * masked, width)
+        x_ref[0:states, part, :] = jnp.swapaxes(masked, 0, 1).astype(BF16)
+    squares_ref[...] = squares
+    copies[1].wait()
     line = lax.broadcasted_iota(jnp.int32, (TILE, width), 0)
     lane = lax.broadcasted_iota(jnp.int32, (TILE, width), 1)
     extra = jnp.zeros((TILE, width), F32)
@@ -57,50 +88,28 @@
         place_at = (lane == line + k * TILE).astype(BF16)
         extra = extra + jnp.dot(site_ref[k], place_at, preferred_element_type=F32)
     x_ref[states, 0:TILE, :] = extra.astype(BF16)
-    squares = jnp.zeros((8, width), F32)
+    copies[2].wait()
+    pack_blocks(right_ref, None, packed_ref)
+
+
+def prepare_kernel(starts, keep_ref, squares_ref, guess_in, left_in, norm_ref, packed_ref, left_ref, *refs):
+    x_refs = (None,) + refs[: len(starts) - 1]
+    guess_ref, sems = refs[len(starts) - 1 :]
+    rows, states, width = guess_in.shape
+    half = width // 2
+    done = starts[1] if len(starts) > 1 else rows
+    copies = chunk_rows_in(guess_in, guess_ref, sems, done, rows, 1)
+    left_copy = pltpu.make_async_copy(left_in, left_ref, sems.at[0])
+    left_copy.start()
+    keep = keep_ref[0:1, :][None]
+    squares = squares_ref[...]
     for n, copy in enumerate(copies):
         copy.wait()
-        part = pl.ds(n * TILE, TILE)
-        masked = guess_ref[part] * keep[None]
-        squares = squares + fold(masked * masked, width)
-        x_ref[0:states, part, :] = jnp.swapaxes(masked, 0, 1).astype(BF16)
-    squares_ref[...] = squares
-
-
-def prepare_kernel(
-    starts,
-    keep_ref,
-    squares_ref,
-    guess_in,
-    left_in,
-    right_in,
-    norm_ref,
-    left_packed_ref,
-    right_packed_ref,
-    left_ref,
-    *refs,
-):
-    x_refs = refs[: len(starts)]
-    guess_ref, right_ref, sems = refs[len(starts) :]
-    rows, states, width = guess_in.shape
-    terms = left_ref.shape[0]
-    half = width // 2
-    done = starts[1] if len(starts) > 1 else rows
-    copies = chunk_rows_in(guess_in, guess_ref, sems, done, rows)
-    for source, target in ((right_in, right_ref), (left_in, left_ref)):
-        copies.append(pltpu.make_async_copy(source, target, sems.at[rows // TILE + len(copies) - (rows - done) // TILE]))
-        copies[-1].start()
-    keep = keep_ref[0:1, :][None]
-    squares = squares_ref[...]
-    for n in range((rows - done) // TILE):
-        copies[n].wait()
         masked = guess_ref[pl.ds(n * TILE, TILE)] * keep
         squares = squares + fold(masked * masked, width)
-        turned = jnp.swapaxes(masked, 0, 1).astype(BF16)
-        x_refs[0][:, n * TILE : (n + 1) * TILE, :] = turned
         chunk = max(c for c, start in enumerate(starts) if start <= done + n * TILE)
         at = done + n * TILE - starts[chunk]
-        x_refs[chunk][:, at : at + TILE, :] = turned
+        x_refs[chunk][:, at : at + TILE, :] = jnp.swapaxes(masked, 0, 1).astype(BF16)
     total = jnp.sum(squares)
     norm_ref[...] = jnp.full(norm_ref.shape, total, F32)
     line = lax.broadcasted_iota(jnp.int32, (TILE, half), 0)
@@ -110,11 +119,18 @@
         part = norm.astype(BF16).astype(F32)
         norm = norm - part
         extra = jnp.where(line == n, part, extra)
-    for copy, block_ref, packed_ref in zip(copies[-2:], (right_ref, left_ref), (right_packed_ref, left_packed_ref)):
-        copy.wait()
-        for k in range(terms):
-            diagonal = pack_symmetric(block_ref, k, packed_ref)
-            packed_ref[k, width : width + TILE, :] = jnp.where(line == 0, diagonal, extra).astype(BF16)
+    left_copy.wait()
+    pack_blocks(left_ref, extra, packed_ref)
+
+
+def pack_blocks(block_ref, extra, packed_ref):
+    terms, width, _ = block_ref.shape
+    half = width // 2
+    line = lax.broadcasted_iota(jnp.int32, (TILE, half), 0)
+    for k in range(terms):
+        diagonal = pack_symmetric(block_ref, k, packed_ref)
+        lines = jnp.broadcast_to(diagonal, (TILE, half)) if extra is None else jnp.where(line == 0, diagonal, extra)
+        packed_ref[k, width : width + TILE, :] = lines.astype(BF16)
 
 
 def triangle(half):
@@ -456,52 +472,47 @@
     starts = (0, rows - 2 * TILE, rows - TILE) if rows >= 4 * TILE else (0,)
     lengths = [stop - start for start, stop in zip(starts, starts[1:] + (rows,))]
     in_place = [pltpu.with_memory_space_constraint(a, pltpu.HBM) for a in (guess, left, right_env[0], site)]
-    first_chunk, keep, squares = pl.pallas_call(
+    first_chunk, keep, squares, right_packed = pl.pallas_call(
         first_chunk_kernel,
-        out_shape=(jax.ShapeDtypeStruct((states + 1, lengths[0], width), BF16), tile, tile),
-        in_specs=[vmem, in_hbm, vmem],
-        out_specs=(vmem,) * 3,
+        out_shape=(jax.ShapeDtypeStruct((states + 1, lengths[0], width), BF16), tile, tile, packed_shape),
+        in_specs=[anywhere] + [in_hbm] * 3,
+        out_specs=(vmem,) * 4,
         scratch_shapes=[
+            pltpu.VMEM((1, 1), jnp.int32),
             pltpu.VMEM((lengths[0], states, width), F32),
-            pltpu.SemaphoreType.DMA((lengths[0] // TILE,)),
+            pltpu.VMEM(site.shape, BF16),
+            pltpu.VMEM(left.shape, BF16),
+            pltpu.SemaphoreType.DMA((lengths[0] // TILE + 3,)),
         ],
         compiler_params=params(),
         cost_estimate=cost(2 * guess.size, 3 * guess.size),
         name="first_chunk",
-    )(bond_rank.reshape(1, 1), in_place[0], in_place[3])
+    )(bond_rank.reshape(1, 1), in_place[0], in_place[3], in_place[2])
     rest = rows - lengths[0]
-    norm_part, left_packed, right_packed, left, *chunks = pl.pallas_call(
+    squares, first_sibling = lax.optimization_barrier((squares, to_sibling(first_chunk)))
+    norm_part, left_packed, left, *chunks = pl.pallas_call(
         functools.partial(prepare_kernel, starts),
         out_shape=(
             tile,
             packed_shape,
-            packed_shape,
             jax.ShapeDtypeStruct(left.shape, BF16),
-            *[
-                jax.ShapeDtypeStruct((states, length, width), BF16)
-                for length in ([rest] + lengths[1:] if rest else [TILE])
-            ],
+            *[jax.ShapeDtypeStruct((states, length, width), BF16) for length in lengths[1:]],
         ),
-        in_specs=[vmem] * 2 + [in_hbm] * 3,
-        out_specs=(vmem,) * (4 + len(lengths)),
+        in_specs=[vmem] * 2 + [in_hbm] * 2,
+        out_specs=(vmem,) * (2 + len(lengths)),
         scratch_shapes=[
             pltpu.VMEM((max(rest, TILE), states, width), F32),
-            pltpu.VMEM(left.shape, BF16),
-            pltpu.SemaphoreType.DMA((rows // TILE + 2,)),
+            pltpu.SemaphoreType.DMA((rest // TILE + 1,)),
         ],
         compiler_params=params(),
         cost_estimate=cost(4 * guess.size, 6 * guess.size),
         name="prepare",
-    )(keep, squares, *in_place[:3])
-    own_pieces = [first_chunk] + (chunks[:1] if rest else [])
-    chunks = [first_chunk] + chunks[1:]
+    )(keep, squares, *in_place[:2])
+    chunks = [first_chunk] + chunks
 
     chunk_hops = [around(chunk) for chunk in chunks]
-    here_pieces = own_pieces + [to_sibling(piece) for piece in own_pieces]
-    bounds = (0, lengths[0], rows) if rest else (0, rows)
-    here_spots = tuple(
-        (0, flip, start, stop - start) for flip in range(CORES) for start, stop in zip(bounds[:-1], bounds[1:])
-    )
+    here_pieces = chunks + [first_sibling] + [to_sibling(chunk) for chunk in chunks[1:]]
+    here_spots = tuple((0, flip, start, length) for flip in range(CORES) for start, length in zip(starts, lengths))
     far_spots = [
         tuple((hop, flip, start, length) for hop in hops[1:] for flip in range(CORES))
         for start, length in zip(starts, lengths)

time: 46 us -> 45.4 us (0.987)
  waiting for transfers between devices: 7.43 us -> 6.71 us
  starting transfers between devices: 11.3 us -> 12 us
  Pallas kernels: 25.3 us -> 24.8 us
    ppermute x1, waiting for transfers between devices: 1.73 us -> 0.01 us  [shards(): received = lax.ppermute(right_packed, 'seg', shift)]
    ppermute x5, waiting for transfers between devices: 0.94 us -> 1.67 us  [to_next_chip(): lax.ppermute(block, 'term', [(i, (i + CORES) % members) for i in range(me...]
    pallas_call x1, Pallas kernels: 1.84 us -> 1.37 us  [shards(): pl.pallas_call(first_chunk_kernel, out_shape=(jax.ShapeDtypeStruct((state...]
    ppermute x10 -> x11, starting transfers between devices: 1.79 us -> 2.12 us  [to_sibling(): return lax.ppermute(block, 'term', [(i, i ^ 1) for i in range(members)])]
    ppermute x10 -> x11, waiting for transfers between devices: 3.29 us -> 3.55 us  [to_sibling(): return lax.ppermute(block, 'term', [(i, i ^ 1) for i in range(members)])]
  transfers between devices with their start and end apart: 17 -> 18, of which waited for: 7 -> 8; matrix products, arithmetic and copies ran while one was open for 0% -> 0% of each run, Pallas kernels for 33% -> 33%
where the time goes in v10:
time: 45.4 us; the launch traced here: 45.2 us
  Pallas kernels  24.8 us (55%)
  starting transfers between devices  12 us (26%)
  waiting for transfers between devices  6.71 us (15%)
  between operations  1.64 us (4%)
    ppermute x5, starting transfers between devices, to_next_chip(): lax.ppermute(block, 'term', [(i, (i + CORES) % members) for i in range(me...  6.81 us
    pallas_call x1, Pallas kernels, shards(): pl.pallas_call(functools.partial(second_kernel, scale, members), out_shap...  5.78 us
    ppermute x11, waiting for transfers between devices, to_sibling(): return lax.ppermute(block, 'term', [(i, i ^ 1) for i in range(members)])  3.55 us
    pallas_call x1, Pallas kernels, shards(): pl.pallas_call(functools.partial(lefts_kernel, far_spots[-1], rows, chips...  2.77 us
    pallas_call x1, Pallas kernels, shards(): pl.pallas_call(functools.partial(last_kernel, len(last_pieces)), out_shap...  2.54 us
    pallas_call x2, Pallas kernels, shards(): pl.pallas_call(functools.partial(rights_kernel, start, stop), out_shape=t...  2.47 us
    pallas_call x2, Pallas kernels, rotate(): pl.pallas_call(functools.partial(rotate_kernel, spots, rows, chips), out_...  2.43 us
    ppermute x11, starting transfers between devices, to_sibling(): return lax.ppermute(block, 'term', [(i, i ^ 1) for i in range(members)])  2.12 us
  transfers between devices with their start and end apart: 18, of which 8 were waited for; matrix products, arithmetic and copies ran while one was open for 0% of the time, Pallas kernels for 33%

profile of v10, /device:TPU:0, one launch (start us, length us, event | category | flops | bytes accessed | tf_op | source)
XLA Modules:
  0.0 45.2 jit_solution(16477742785097595851)
XLA Ops:
  1.3 1.4 %first_chunk.1 = (bf16[17,32,256]{2,1,0:T(8,128)(2,1)S(1)}, f32[8,256]{1,0:T(8,128)S(1)}, f32[8,256]{1,0:T(8,128)S(1)}, bf16[3,272,128]{2,1,0:T(8,128)(2,1)S(1)}) custom-call(s32[1,1]{1,0:T(1,128)} %bitcast.6.rank_in, f32[64,16,256]{2,1,0:T(8,128)} %bitcast.7, bf16[3,16,16]{2,1,0:T(8,128)(2,1)} %bitcast.12, bf16[3,256,256]{2,1,0:T(8,128)(2,1)} %bitcast.10), custom_call_target="tpu_custom_call" | custom-call | flops 5242 | bytes 7864 | tf_op jit(solution)/shard_map/first_chunk/pallas_call | solution.py:475
  2.7 0.5 %collective-permute-start.1 = (bf16[17,32,256]{2,1,0:T(8,128)(2,1)S(1)}, bf16[17,32,256]{2,1,0:T(8,128)(2,1)S(1)}, u32[]{:S(2)}, u32[]{:S(2)}) collective-permute-start(bf16[17,32,256]{2,1,0:T(8,128)(2,1)S(1)} %get-tuple-element.51.chunk_ref.refs_0_), channel_id=1, source_target_pairs={{0,1},{1,0},{2,3},{3,2},{4,5},{5,4},{6,7},{7,6},{8,9},{9,8},{10,11... | collective-permute-start | bytes 835592 | tf_op jit(solution)/shard_map/ppermute | solution.py:452
  3.2 2.6 %collective-permute-start.4 = (bf16[17,32,256]{2,1,0:T(8,128)(2,1)S(1)}, bf16[17,32,256]{2,1,0:T(8,128)(2,1)S(1)}, u32[]{:S(2)}, u32[]{:S(2)}) collective-permute-start(bf16[17,32,256]{2,1,0:T(8,128)(2,1)S(1)} %get-tuple-element.51.chunk_ref.refs_0_), channel_id=1, source_target_pairs={{0,2},{1,3},{2,0},{3,1},{4,6},{5,7},{6,4},{7,5},{8,10},{9,11},{10,... | collective-permute-start | bytes 835592 | tf_op jit(solution)/shard_map/ppermute | solution.py:455
  5.8 1.3 %collective-permute-start = (bf16[3,272,128]{2,1,0:T(8,128)(2,1)S(1)}, bf16[3,272,128]{2,1,0:T(8,128)(2,1)S(1)}, u32[]{:S(2)}, u32[]{:S(2)}) collective-permute-start(bf16[3,272,128]{2,1,0:T(8,128)(2,1)S(1)} %get-tuple-element.50), channel_id=1, source_target_pairs={{4,0},{8,4},{12,8},{16,12},{20,16},{24,20},{28,24},{5,1},{9,5},{13... | collective-permute-start | bytes 626696 | tf_op jit(solution)/shard_map/ppermute | solution.py:524
  7.1 0.0 collective-permute-done.1.refs_3_
  7.1 1.3 %prepare.1 = (f32[8,256]{1,0:T(8,128)S(1)}, bf16[3,272,128]{2,1,0:T(8,128)(2,1)S(1)}, bf16[3,256,256]{2,1,0:T(8,128)(2,1)S(1)}, bf16[16,16,256]{2,1,0:T(8,128)(2,1)S(1)}, bf16[16,16,256]{2,1,0:T(8,128)(2,1)S(1)}) custom-call(f32[8,256]{1,0:T(8,128)S(1)} %get-tuple-element.49.keep_ref, f32[8,256]{1,0:T(8,128)S(1)} %get-tuple-element.53.squares_ref, ...), custom_call_target="tpu_custom_call" | custom-call | flops 10485 | bytes 15728 | tf_op jit(solution)/shard_map/prepare/pallas_call | solution.py:493
  8.4 0.2 collective-permute-start.2
  8.6 0.3 collective-permute-start.3
  9.0 0.2 collective-permute-start.8
  9.2 0.4 spread_site.2.refs_6_.refs_5_.refs_3_.kron_ref
  9.6 0.3 collective-permute-done.2.refs_4_
  9.8 1.7 %collective-permute-start.6 = (bf16[16,16,256]{2,1,0:T(8,128)(2,1)S(1)}, bf16[16,16,256]{2,1,0:T(8,128)(2,1)S(1)}, u32[]{:S(2)}, u32[]{:S(2)}) collective-permute-start(bf16[16,16,256]{2,1,0:T(8,128)(2,1)S(1)} %get-tuple-element.55.refs_2_), channel_id=1, source_target_pairs={{0,2},{1,3},{2,0},{3,1},{4,6},{5,7},{6,4},{7,5},{8,10},{9,11},{10,... | collective-permute-start | bytes 393224 | tf_op jit(solution)/shard_map/ppermute | solution.py:455
  11.5 0.0 collective-permute-done.3.refs_5_
  11.5 0.4 collective-permute-start.11
  11.9 1.0 %rotate_own.1 = (bf16[3,16,128,256]{3,2,1,0:T(8,128)(2,1)S(1)}, bf16[256,768]{1,0:T(8,128)(2,1)S(1)}) custom-call(bf16[17,32,256]{2,1,0:T(8,128)(2,1)S(1)} %get-tuple-element.51.chunk_ref.refs_0_, bf16[16,16,256]{2,1,0:T(8,128)(2,1)S(1)} %get-tuple-element.54.refs_1_, bf16[16,16,256]{2,1,0:T(8,128)(2,1)S(1)} %get-tuple-element.55.refs_2_, ...), custom_call_target="tpu_custom_call" | custom-call | flops 16106127 | bytes 83886 | tf_op jit(solution)/shard_map/rotate_own/pallas_call | solution.py:556
  12.8 0.4 collective-permute-done.4.chunk_ref.refs_0_
  13.3 0.0 collective-permute-start.7
  13.3 0.4 spread_site.3.refs_6_.refs_4_.refs_2_
  13.7 1.4 %rotate_here.1 = (bf16[3,16,256,256]{3,2,1,0:T(8,128)(2,1)S(1)}, bf16[16,256,256]{2,1,0:T(8,128)(2,1)S(1)}) custom-call(bf16[17,32,256]{2,1,0:T(8,128)(2,1)S(1)} %get-tuple-element.51.chunk_ref.refs_0_, bf16[16,16,256]{2,1,0:T(8,128)(2,1)S(1)} %get-tuple-element.54.refs_1_, bf16[16,16,256]{2,1,0:T(8,128)(2,1)S(1)} %get-tuple-element.55.refs_2_, ...), custom_call_target="tpu_custom_call" | custom-call | flops 16106127 | bytes 83886 | tf_op jit(solution)/shard_map/rotate_here/pallas_call | solution.py:570
  15.0 0.0 collective-permute-done
  15.0 1.0 %collective-permute-done.8.refs_2_ = bf16[16,16,256]{2,1,0:T(8,128)(2,1)S(1)} collective-permute-done((bf16[16,16,256]{2,1,0:T(8,128)(2,1)S(1)}, bf16[16,16,256]{2,1,0:T(8,128)(2,1)S(1)}, u32[]{:S(2)}, u32[]{:S(2)}) %collective-permute-start.8) | collective-permute-done | bytes 131104 | tf_op jit(solution)/shard_map/ppermute | solution.py:455
  16.1 0.0 collective-permute-start.9
  16.1 2.0 %collective-permute-start.5 = (bf16[3,272,128]{2,1,0:T(8,128)(2,1)S(1)}, bf16[3,272,128]{2,1,0:T(8,128)(2,1)S(1)}, u32[]{:S(2)}, u32[]{:S(2)}) collective-permute-start(bf16[3,272,128]{2,1,0:T(8,128)(2,1)S(1)} %broadcast_select_fusion.packed_ref), channel_id=1, source_target_pairs={{0,2},{1,3},{2,0},{3,1},{4,6},{5,7},{6,4},{7,5},{8,10},{9,11},{10,... | collective-permute-start | bytes 626696 | tf_op jit(solution)/shard_map/ppermute | solution.py:455
  18.1 1.1 %apply_rows_here.1 = (bf16[16,384,256]{2,1,0:T(8,128)(2,1)S(1)}, bf16[3,256,256]{2,1,0:T(8,128)(2,1)S(1)}) custom-call(bf16[3,16,128,256]{3,2,1,0:T(8,128)(2,1)S(1)} %get-tuple-element.70.rotated_ref, bf16[3,272,128]{2,1,0:T(8,128)(2,1)S(1)} %broadcast_select_fusion.packed_ref), custom_call_target="tpu_custom_call" | custom-call | flops 16106127 | bytes 83886 | tf_op jit(solution)/shard_map/apply_rows_here/pallas_call | solution.py:591
  19.2 0.0 collective-permute-done.9.refs_3_
  19.2 0.0 collective-permute-done.7.refs_1_
  19.2 1.1 %rotate_crossed.1 = (bf16[3,16,256,256]{3,2,1,0:T(8,128)(2,1)S(1)}, bf16[16,256,256]{2,1,0:T(8,128)(2,1)S(1)}) custom-call(bf16[17,32,256]{2,1,0:T(8,128)(2,1)S(1)} %collective-permute-done.4.chunk_ref.refs_0_, bf16[17,32,256]{2,1,0:T(8,128)(2,1)S(1)} %collective-permute-done.7.refs_1_, ...), custom_call_target="tpu_custom_call", output_to_operand_aliasing={{0}: (5, {}), {1}: (6, {})} | custom-call | flops 16106127 | bytes 83886 | tf_op jit(solution)/shard_map/rotate_crossed/pallas_call | solution.py:570
  20.3 0.0 collective-permute-done.6.refs_0_
  20.3 0.3 collective-permute-start.10
  20.6 1.4 %apply_rows_crossed.1.refs_6_ = bf16[16,288,256]{2,1,0:T(8,128)(2,1)S(1)} custom-call(bf16[17,32,256]{2,1,0:T(8,128)(2,1)S(1)} %collective-permute-done.4.chunk_ref.refs_0_, bf16[17,32,256]{2,1,0:T(8,128)(2,1)S(1)} %collective-permute-done.7.refs_1_, bf16[16,16,256]{2,1,0:T(8,128)(2,1)S(1)} %collective-permute-done.8.refs_2_, ...), custom_call_target="tpu_custom_call" | custom-call | flops 16106127 | bytes 83886 | tf_op jit(solution)/shard_map/apply_rows_crossed/pallas_call | solution.py:612
  22.0 0.0 collective-permute-done.10.refs_1_
  22.0 2.5 %apply_rows_last.1.before_ref = f32[16,256,256]{2,1,0:T(8,128)S(1)} custom-call(bf16[16,16,256]{2,1,0:T(8,128)(2,1)S(1)} %collective-permute-done.6.refs_0_, bf16[16,16,256]{2,1,0:T(8,128)(2,1)S(1)} %collective-permute-done.10.refs_1_, bf16[3,256,256]{2,1,0:T(8,128)(2,1)S(1)} %get-tuple-element.76.refs_4_.refs_2_.right_ref, ...), custom_call_target="tpu_custom_call" | custom-call | flops 16106127 | bytes 83886 | tf_op jit(solution)/shard_map/apply_rows_last/pallas_call | solution.py:626
  24.6 0.0 collective-permute-done.11.refs_5_
  24.6 2.8 %received_lefts.1 = (bf16[16,256,768]{2,1,0:T(8,128)(2,1)S(1)}, f32[8,256]{1,0:T(8,128)S(1)}, bf16[3,16,256,256]{3,2,1,0:T(8,128)(2,1)S(1)}, bf16[16,256,256]{2,1,0:T(8,128)(2,1)S(1)}) custom-call(bf16[16,16,256]{2,1,0:T(8,128)(2,1)S(1)} %collective-permute-done.6.refs_0_, ...), custom_call_target="tpu_custom_call", output_to_operand_aliasing={{2}: (3, {}), {3}: (4, {})} | custom-call | flops 16106127 | bytes 125829 | tf_op jit(solution)/shard_map/received_lefts/pallas_call | solution.py:645
  27.4 0.2 collective-permute-done.5.packed_ref
  27.6 1.3 %received_rights.2 = (bf16[8,256,256]{2,1,0:T(8,128)(2,1)S(1)}, f32[8,256]{1,0:T(8,128)S(1)}, bf16[3,256,256]{2,1,0:T(8,128)(2,1)S(1)}) custom-call(bf16[3,272,128]{2,1,0:T(8,128)(2,1)S(1)} %collective-permute-done.5.packed_ref, bf16[16,256,768]{2,1,0:T(8,128)(2,1)S(1)} %get-tuple-element.80.mixed_ref, ...), custom_call_target="tpu_custom_call" | custom-call | flops 8053063 | bytes 125829 | tf_op jit(solution)/shard_map/received_rights/pallas_call | solution.py:664
  28.9 0.2 collective-permute-start.13
  29.1 1.2 %received_rights.3 = (bf16[8,256,256]{2,1,0:T(8,128)(2,1)S(1)}, f32[8,256]{1,0:T(8,128)S(1)}) custom-call(bf16[3,256,256]{2,1,0:T(8,128)(2,1)S(1)} %get-tuple-element.85.packed_ref, bf16[16,256,768]{2,1,0:T(8,128)(2,1)S(1)} %get-tuple-element.80.mixed_ref, bf16[16,256,256]{2,1,0:T(8,128)(2,1)S(1)} %get-tuple-element.81.whole_ref, ...), custom_call_target="tpu_custom_call" | custom-call | flops 8053063 | bytes 125829 | tf_op jit(solution)/shard_map/received_rights/pallas_call | solution.py:664
  30.2 0.5 %collective-permute-start.14 = (bf16[8,256,256]{2,1,0:T(8,128)(2,1)S(1)}, bf16[8,256,256]{2,1,0:T(8,128)(2,1)S(1)}, u32[]{:S(2)}, u32[]{:S(2)}) collective-permute-start(bf16[8,256,256]{2,1,0:T(8,128)(2,1)S(1)} %get-tuple-element.89.refs_1_.high_ref), channel_id=1, source_target_pairs={{0,1},{1,0},{2,3},{3,2},{4,5},{5,4},{6,7},{7,6},{8,9},{9,8},{10,11... | collective-permute-start | bytes 3145736 | tf_op jit(solution)/shard_map/ppermute | solution.py:452
  30.7 0.1 collective-permute-start.12
  30.8 0.8 %collective-permute-done.13.other_ref = bf16[8,256,256]{2,1,0:T(8,128)(2,1)S(1)} collective-permute-done((bf16[8,256,256]{2,1,0:T(8,128)(2,1)S(1)}, bf16[8,256,256]{2,1,0:T(8,128)(2,1)S(1)}, u32[]{:S(2)}, u32[]{:S(2)}) %collective-permute-start.13) | collective-permute-done | bytes 1048608 | tf_op jit(solution)/shard_map/ppermute | solution.py:452
  31.6 0.2 add_low_half.1.refs_0_.low_ref
  31.8 0.0 copy-start
  31.8 1.3 %collective-permute-done.12.theirs_ref = f32[8,256]{1,0:T(8,128)S(1)} collective-permute-done((f32[8,256]{1,0:T(8,128)S(1)}, f32[8,256]{1,0:T(8,128)S(1)}, u32[]{:S(2)}, u32[]{:S(2)}) %collective-permute-start.12) | collective-permute-done | bytes 8224 | tf_op jit(solution)/shard_map/ppermute | solution.py:452
  33.1 0.0 collective-permute-done.14.refs_2_.high_other_ref
  33.1 5.8 %apply_residual.1.refs_0_ = f32[8,256]{1,0:T(8,128)S(1)} custom-call(f32[8,256]{1,0:T(8,128)S(1)} %get-tuple-element.49.keep_ref, f32[8,256]{1,0:T(8,128)S(1)} %get-tuple-element.87.mine_ref, f32[8,256]{1,0:T(8,128)S(1)} %collective-permute-done.12.theirs_ref, f32[8,256,256]{2,1,0:T(8,128)S(1)} %add_low_half.1.refs_0_.low_ref, ...), custom_call_target="tpu_custom_call" | custom-call | flops 48318384 | bytes 62914 | tf_op jit(solution)/shard_map/apply_residual/pallas_call | solution.py:691
  38.9 1.8 %collective-permute-start.15 = (f32[8,256]{1,0:T(8,128)S(1)}, f32[8,256]{1,0:T(8,128)S(1)}, u32[]{:S(2)}, u32[]{:S(2)}) collective-permute-start(f32[8,256]{1,0:T(8,128)S(1)} %apply_residual.1.refs_0_), channel_id=1, source_target_pairs={{0,2},{1,3},{2,0},{3,1},{4,6},{5,7},{6,4},{7,5},{8,10},{9,11},{10,... | collective-permute-start | bytes 24584 | tf_op jit(solution)/shard_map/ppermute | solution.py:465
  40.7 0.0 collective-permute-start.16
  40.7 0.0 copy-done
  40.7 0.4 own_rows.1
  41.2 1.5 %collective-permute-done.15.refs_2_ = f32[8,256]{1,0:T(8,128)S(1)} collective-permute-done((f32[8,256]{1,0:T(8,128)S(1)}, f32[8,256]{1,0:T(8,128)S(1)}, u32[]{:S(2)}, u32[]{:S(2)}) %collective-permute-start.15) | collective-permute-done | bytes 8224 | tf_op jit(solution)/shard_map/ppermute | solution.py:465
  42.6 0.0 collective-permute-start.17
  42.6 0.0 collective-permute-done.16.refs_1_
  42.6 1.2 %collective-permute-done.17.refs_3_ = f32[8,256]{1,0:T(8,128)S(1)} collective-permute-done((f32[8,256]{1,0:T(8,128)S(1)}, f32[8,256]{1,0:T(8,128)S(1)}, u32[]{:S(2)}, u32[]{:S(2)}) %collective-permute-start.17) | collective-permute-done | bytes 8224 | tf_op jit(solution)/shard_map/ppermute | solution.py:452
  43.8 1.3 %finish.1 = (f32[64,16,256]{2,1,0:T(8,128)}, f32[1]{0:T(128)}) custom-call(f32[64,16,256]{2,1,0:T(8,128)S(1)} %get-tuple-element.90.vector_ref, f32[64,16,256]{2,1,0:T(8,128)S(1)} %get-tuple-element.92.residual_ref, f32[8,256]{1,0:T(8,128)S(1)} %apply_residual.1.refs_0_, f32[8,256]{1,0:T(8,128)S(1)} %collective-permute-done.16.refs_1_, ...), custom_call_target="tpu_custom_call" | custom-call | flops 7864 | bytes 31457 | tf_op jit(solution)/shard_map/finish/pallas_call | solution.py:721
  (1 shorter events, 0.0 us)
Async XLA Ops:
  2.7 4.4 %collective-permute-start.1 = (bf16[17,32,256]{2,1,0:T(8,128)(2,1)S(1)}, bf16[17,32,256]{2,1,0:T(8,128)(2,1)S(1)}, u32[]{:S(2)}, u32[]{:S(2)}) collective-permute-start(bf16[17,32,256]{2,1,0:T(8,128)(2,1)S(1)} %get-tuple-element.51.chunk_ref.refs_0_), channel_id=1, source_target_pairs={{0,1},{1,0},{2,3},{3,2},{4,5},{5,4},{6,7},{7,6},{8,9},{9,8},{10,11... | collective-permute-start | bytes 835592 | tf_op jit(solution)/shard_map/ppermute | solution.py:452
  3.2 10.1 %collective-permute-start.4 = (bf16[17,32,256]{2,1,0:T(8,128)(2,1)S(1)}, bf16[17,32,256]{2,1,0:T(8,128)(2,1)S(1)}, u32[]{:S(2)}, u32[]{:S(2)}) collective-permute-start(bf16[17,32,256]{2,1,0:T(8,128)(2,1)S(1)} %get-tuple-element.51.chunk_ref.refs_0_), channel_id=1, source_target_pairs={{0,2},{1,3},{2,0},{3,1},{4,6},{5,7},{6,4},{7,5},{8,10},{9,11},{10,... | collective-permute-start | bytes 835592 | tf_op jit(solution)/shard_map/ppermute | solution.py:455
  5.8 9.3 %collective-permute-start = (bf16[3,272,128]{2,1,0:T(8,128)(2,1)S(1)}, bf16[3,272,128]{2,1,0:T(8,128)(2,1)S(1)}, u32[]{:S(2)}, u32[]{:S(2)}) collective-permute-start(bf16[3,272,128]{2,1,0:T(8,128)(2,1)S(1)} %get-tuple-element.50), channel_id=1, source_target_pairs={{4,0},{8,4},{12,8},{16,12},{20,16},{24,20},{28,24},{5,1},{9,5},{13... | collective-permute-start | bytes 626696 | tf_op jit(solution)/shard_map/ppermute | solution.py:524
  8.4 1.4 %collective-permute-start.2 = (bf16[16,16,256]{2,1,0:T(8,128)(2,1)S(1)}, bf16[16,16,256]{2,1,0:T(8,128)(2,1)S(1)}, u32[]{:S(2)}, u32[]{:S(2)}) collective-permute-start(bf16[16,16,256]{2,1,0:T(8,128)(2,1)S(1)} %get-tuple-element.54.refs_1_), channel_id=1, source_target_pairs={{0,1},{1,0},{2,3},{3,2},{4,5},{5,4},{6,7},{7,6},{8,9},{9,8},{10,11... | collective-permute-start | bytes 393224 | tf_op jit(solution)/shard_map/ppermute | solution.py:452
  8.6 2.8 %collective-permute-start.3 = (bf16[16,16,256]{2,1,0:T(8,128)(2,1)S(1)}, bf16[16,16,256]{2,1,0:T(8,128)(2,1)S(1)}, u32[]{:S(2)}, u32[]{:S(2)}) collective-permute-start(bf16[16,16,256]{2,1,0:T(8,128)(2,1)S(1)} %get-tuple-element.55.refs_2_), channel_id=1, source_target_pairs={{0,1},{1,0},{2,3},{3,2},{4,5},{5,4},{6,7},{7,6},{8,9},{9,8},{10,11... | collective-permute-start | bytes 393224 | tf_op jit(solution)/shard_map/ppermute | solution.py:452
  9.0 7.1 %collective-permute-start.8 = (bf16[16,16,256]{2,1,0:T(8,128)(2,1)S(1)}, bf16[16,16,256]{2,1,0:T(8,128)(2,1)S(1)}, u32[]{:S(2)}, u32[]{:S(2)}) collective-permute-start(bf16[16,16,256]{2,1,0:T(8,128)(2,1)S(1)} %get-tuple-element.54.refs_1_), channel_id=1, source_target_pairs={{0,2},{1,3},{2,0},{3,1},{4,6},{5,7},{6,4},{7,5},{8,10},{9,11},{10,... | collective-permute-start | bytes 393224 | tf_op jit(solution)/shard_map/ppermute | solution.py:455
  9.8 10.5 %collective-permute-start.6 = (bf16[16,16,256]{2,1,0:T(8,128)(2,1)S(1)}, bf16[16,16,256]{2,1,0:T(8,128)(2,1)S(1)}, u32[]{:S(2)}, u32[]{:S(2)}) collective-permute-start(bf16[16,16,256]{2,1,0:T(8,128)(2,1)S(1)} %get-tuple-element.55.refs_2_), channel_id=1, source_target_pairs={{0,2},{1,3},{2,0},{3,1},{4,6},{5,7},{6,4},{7,5},{8,10},{9,11},{10,... | collective-permute-start | bytes 393224 | tf_op jit(solution)/shard_map/ppermute | solution.py:455
  11.5 13.1 %collective-permute-start.11 = (bf16[3,272,128]{2,1,0:T(8,128)(2,1)S(1)}, bf16[3,272,128]{2,1,0:T(8,128)(2,1)S(1)}, u32[]{:S(2)}, u32[]{:S(2)}) collective-permute-start(bf16[3,272,128]{2,1,0:T(8,128)(2,1)S(1)} %get-tuple-element.75), channel_id=1, source_target_pairs={{0,2},{1,3},{2,0},{3,1},{4,6},{5,7},{6,4},{7,5},{8,10},{9,11},{10,... | collective-permute-start | bytes 626696 | tf_op jit(solution)/shard_map/ppermute | solution.py:455
  13.3 6.0 %collective-permute-start.7 = (bf16[17,32,256]{2,1,0:T(8,128)(2,1)S(1)}, bf16[17,32,256]{2,1,0:T(8,128)(2,1)S(1)}, u32[]{:S(2)}, u32[]{:S(2)}) collective-permute-start(bf16[17,32,256]{2,1,0:T(8,128)(2,1)S(1)} %collective-permute-done.4.chunk_ref.refs_0_), channel_id=1, source_target_pairs={{0,1},{1,0},{2,3},{3,2},{4,5},{5,4},{6,7},{7,6},{8,9},{9,8},{10,11... | collective-permute-start | bytes 835592 | tf_op jit(solution)/shard_map/ppermute | solution.py:452
  16.1 3.2 %collective-permute-start.9 = (bf16[16,16,256]{2,1,0:T(8,128)(2,1)S(1)}, bf16[16,16,256]{2,1,0:T(8,128)(2,1)S(1)}, u32[]{:S(2)}, u32[]{:S(2)}) collective-permute-start(bf16[16,16,256]{2,1,0:T(8,128)(2,1)S(1)} %collective-permute-done.8.refs_2_), channel_id=1, source_target_pairs={{0,1},{1,0},{2,3},{3,2},{4,5},{5,4},{6,7},{7,6},{8,9},{9,8},{10,11... | collective-permute-start | bytes 393224 | tf_op jit(solution)/shard_map/ppermute | solution.py:452
  16.1 11.5 %collective-permute-start.5 = (bf16[3,272,128]{2,1,0:T(8,128)(2,1)S(1)}, bf16[3,272,128]{2,1,0:T(8,128)(2,1)S(1)}, u32[]{:S(2)}, u32[]{:S(2)}) collective-permute-start(bf16[3,272,128]{2,1,0:T(8,128)(2,1)S(1)} %broadcast_select_fusion.packed_ref), channel_id=1, source_target_pairs={{0,2},{1,3},{2,0},{3,1},{4,6},{5,7},{6,4},{7,5},{8,10},{9,11},{10,... | collective-permute-start | bytes 626696 | tf_op jit(solution)/shard_map/ppermute | solution.py:455
  20.3 1.7 %collective-permute-start.10 = (bf16[16,16,256]{2,1,0:T(8,128)(2,1)S(1)}, bf16[16,16,256]{2,1,0:T(8,128)(2,1)S(1)}, u32[]{:S(2)}, u32[]{:S(2)}) collective-permute-start(bf16[16,16,256]{2,1,0:T(8,128)(2,1)S(1)} %collective-permute-done.6.refs_0_), channel_id=1, source_target_pairs={{0,1},{1,0},{2,3},{3,2},{4,5},{5,4},{6,7},{7,6},{8,9},{9,8},{10,11... | collective-permute-start | bytes 393224 | tf_op jit(solution)/shard_map/ppermute | solution.py:452
  28.9 2.7 %collective-permute-start.13 = (bf16[8,256,256]{2,1,0:T(8,128)(2,1)S(1)}, bf16[8,256,256]{2,1,0:T(8,128)(2,1)S(1)}, u32[]{:S(2)}, u32[]{:S(2)}) collective-permute-start(bf16[8,256,256]{2,1,0:T(8,128)(2,1)S(1)} %get-tuple-element.88.mine_ref), channel_id=1, source_target_pairs={{0,1},{1,0},{2,3},{3,2},{4,5},{5,4},{6,7},{7,6},{8,9},{9,8},{10,11... | collective-permute-start | bytes 3145736 | tf_op jit(solution)/shard_map/ppermute | solution.py:452
  30.2 2.9 %collective-permute-start.14 = (bf16[8,256,256]{2,1,0:T(8,128)(2,1)S(1)}, bf16[8,256,256]{2,1,0:T(8,128)(2,1)S(1)}, u32[]{:S(2)}, u32[]{:S(2)}) collective-permute-start(bf16[8,256,256]{2,1,0:T(8,128)(2,1)S(1)} %get-tuple-element.89.refs_1_.high_ref), channel_id=1, source_target_pairs={{0,1},{1,0},{2,3},{3,2},{4,5},{5,4},{6,7},{7,6},{8,9},{9,8},{10,11... | collective-permute-start | bytes 3145736 | tf_op jit(solution)/shard_map/ppermute | solution.py:452
  30.7 2.4 %collective-permute-start.12 = (f32[8,256]{1,0:T(8,128)S(1)}, f32[8,256]{1,0:T(8,128)S(1)}, u32[]{:S(2)}, u32[]{:S(2)}) collective-permute-start(f32[8,256]{1,0:T(8,128)S(1)} %get-tuple-element.87.mine_ref), channel_id=1, source_target_pairs={{0,1},{1,0},{2,3},{3,2},{4,5},{5,4},{6,7},{7,6},{8,9},{9,8},{10,11... | collective-permute-start | bytes 24584 | tf_op jit(solution)/shard_map/ppermute | solution.py:452
  31.8 8.9 %copy-start = (f32[1,64,16,256]{3,2,1,0:T(8,128)S(1)}, f32[1,64,16,256]{3,2,1,0:T(8,128)}, u32[]{:S(2)}) copy-start(f32[1,64,16,256]{3,2,1,0:T(8,128)} %param.5) | copy-start | bytes 3145732
  38.9 3.7 %collective-permute-start.15 = (f32[8,256]{1,0:T(8,128)S(1)}, f32[8,256]{1,0:T(8,128)S(1)}, u32[]{:S(2)}, u32[]{:S(2)}) collective-permute-start(f32[8,256]{1,0:T(8,128)S(1)} %apply_residual.1.refs_0_), channel_id=1, source_target_pairs={{0,2},{1,3},{2,0},{3,1},{4,6},{5,7},{6,4},{7,5},{8,10},{9,11},{10,... | collective-permute-start | bytes 24584 | tf_op jit(solution)/shard_map/ppermute | solution.py:465
  40.7 1.9 %collective-permute-start.16 = (f32[8,256]{1,0:T(8,128)S(1)}, f32[8,256]{1,0:T(8,128)S(1)}, u32[]{:S(2)}, u32[]{:S(2)}) collective-permute-start(f32[8,256]{1,0:T(8,128)S(1)} %apply_residual.1.refs_0_), channel_id=1, source_target_pairs={{0,1},{1,0},{2,3},{3,2},{4,5},{5,4},{6,7},{7,6},{8,9},{9,8},{10,11... | collective-permute-start | bytes 24584 | tf_op jit(solution)/shard_map/ppermute | solution.py:452
  42.6 1.2 %collective-permute-start.17 = (f32[8,256]{1,0:T(8,128)S(1)}, f32[8,256]{1,0:T(8,128)S(1)}, u32[]{:S(2)}, u32[]{:S(2)}) collective-permute-start(f32[8,256]{1,0:T(8,128)S(1)} %collective-permute-done.15.refs_2_), channel_id=1, source_target_pairs={{0,1},{1,0},{2,3},{3,2},{4,5},{5,4},{6,7},{7,6},{8,9},{9,8},{10,11... | collective-permute-start | bytes 24584 | tf_op jit(solution)/shard_map/ppermute | solution.py:452

commit v11 on v10

--- a/solution.py
+++ b/solution.py
@@ -290,12 +290,12 @@
 
 def lefts_kernel(spots, rows, chips, *refs):
     count = len(spots)
-    packed_ref = refs[count + 3]
+    packed_ref, norm_before_ref = refs[count + 3 : count + 5]
     mixed_ref, norm_ref, rotated_ref, whole_ref, left_ref, sems = refs[-6:]
     terms, states, width, _ = rotated_ref.shape
     lines = packed_ref[0, width : width + TILE, :].astype(F32)
     norm = lines[1:2] + lines[2:3] + lines[3:4]
-    norm_ref[...] = jnp.broadcast_to(jnp.concatenate([norm, norm], axis=1), norm_ref.shape)
+    norm_ref[...] = norm_before_ref[...] + jnp.concatenate([norm, norm], axis=1)
     unpack_symmetric(packed_ref, left_ref)
     rotate_kernel(spots, rows, chips, *refs[: count + 1], rotated_ref, whole_ref, sems)
 
@@ -308,112 +308,159 @@
     lax.fori_loop(0, states, lefts, 0, unroll=UNROLL)
 
 
-def rights_kernel(start, stop, packed_ref, mixed_ref, whole_ref, before_ref, *refs):
+def rights_kernel(start, stop, packed_ref, mixed_ref, before_ref, partial_ref, *refs):
     if start == 0:
-        stats = refs[:-3]
-        partial_ref, stat_ref, right_ref = refs[-3:]
+        right_ref = refs[0]
         unpack_symmetric(packed_ref, right_ref)
     else:
-        stats = refs[:-2]
-        partial_ref, stat_ref = refs[-2:]
         right_ref = packed_ref
-    states, width, _ = whole_ref.shape
-    terms = right_ref.shape[0]
-
-    def rights(n, total):
+    terms, width, _ = right_ref.shape
+
+    def rights(n, carry):
         at = n * GROUP
         rows = mixed_ref[pl.ds(start + at, GROUP)].reshape(GROUP * width, terms * width)
         stacked = right_ref[...].reshape(terms * width, width)
         image = jnp.dot(rows, stacked, preferred_element_type=F32).reshape(GROUP, width, width)
-        part = (before_ref[pl.ds(start + at, GROUP)].astype(F32) + image).astype(partial_ref.dtype)
-        partial_ref[pl.ds(at, GROUP)] = part
-        held = whole_ref[pl.ds(start + at, GROUP)].astype(F32)
-        return total + fold(held * part.astype(F32), width)
-
-    total = lax.fori_loop(0, (stop - start) // GROUP, rights, jnp.zeros((8, width), F32))
-    stat_ref[...] = functools.reduce(jnp.add, [stat[...] for stat in stats])
-    product = jnp.full((1, width), jnp.sum(total), F32)
-    stat_ref[0:1, :] = product if start == 0 else stats[0][0:1, :] + product
-
-
-def scales(keep_ref, mine_ref, theirs_ref, scale, width):
-    inverse = lax.rsqrt((mine_ref[1:2, :] + theirs_ref[1:2, :]) * scale + epsilon)
-    rayleigh = (mine_ref[0:1, :] + theirs_ref[0:1, :]) * (inverse * inverse * scale)
-    return inverse, rayleigh, keep_ref[0:1, :] * inverse
-
-
-def add_kernel(mine_ref, other_ref, sum_ref):
-    sum_ref[...] = mine_ref[...].astype(F32) + other_ref[...].astype(F32)
-
-
-def second_kernel(
+        partial_ref[pl.ds(at, GROUP)] = (before_ref[pl.ds(start + at, GROUP)] + image).astype(partial_ref.dtype)
+        return carry
+
+    lax.fori_loop(0, (stop - start) // GROUP, rights, 0)
+
+
+def shifted_residual(start, shift, keep, mine_ref, other_ref, whole_ref, left_ref, res_ref, mixed_ref):
+    count, width, _ = res_ref.shape
+    terms = left_ref.shape[0]
+    zero = jnp.zeros((8, width), F32)
+
+    def lefts(n, sums):
+        held = whole_ref[start + n].astype(F32)
+        sigma = (mine_ref[n].astype(F32) + other_ref[n].astype(F32)) * keep
+        residual = sigma - shift * held
+        rounded = residual.astype(BF16)
+        res_ref[n] = rounded
+        mixed = jnp.dot(
+            left_ref[...].reshape(terms * width, width), rounded, preferred_element_type=F32
+        ).astype(BF16)
+        for k in range(terms):
+            mixed_ref[k, n] = mixed[k * width : (k + 1) * width]
+        return (
+            sums[0] + fold(residual * residual, width),
+            sums[1] + fold(residual * held, width),
+            sums[2] + fold(held * held, width),
+        )
+
+    sums = lax.fori_loop(0, count, lefts, (zero, zero, zero), unroll=UNROLL)
+    return [jnp.sum(total) for total in sums]
+
+
+def low_kernel(
+    keep_ref,
+    norm_ref,
+    norm_other_ref,
+    low_ref,
+    low_other_ref,
+    whole_ref,
+    left_ref,
+    res_ref,
+    mixed_ref,
+    out_ref,
+):
+    count, width, _ = low_ref.shape
+    keep = keep_ref[0:1, :]
+    zero = jnp.zeros((8, width), F32)
+
+    def products(n, sums):
+        held = whole_ref[n].astype(F32)
+        sigma = low_ref[n].astype(F32) + low_other_ref[n].astype(F32)
+        return sums[0] + fold(sigma * held, width), sums[1] + fold(held * held, width)
+
+    cross, square = lax.fori_loop(0, count, products, (zero, zero), unroll=UNROLL)
+    total = norm_ref[0:1, :] + norm_other_ref[0:1, :]
+    floor = jnp.maximum(jnp.maximum(jnp.full((1, width), jnp.sum(square), F32), 0.25 * total), 1e-30)
+    shift = jnp.sum(cross) / floor
+    sums = shifted_residual(0, shift, keep, low_ref, low_other_ref, whole_ref, left_ref, res_ref, mixed_ref)
+    out_ref[0:1, :] = shift
+    for n, value in enumerate(sums):
+        out_ref[n + 1 : n + 2, :] = jnp.full((1, width), value, F32)
+    out_ref[4:8, :] = jnp.zeros((4, width), F32)
+
+
+def high_kernel(
     scale,
     members,
     keep_ref,
-    mine_ref,
-    theirs_ref,
-    low_ref,
+    norm_ref,
+    norm_other_ref,
+    sums_ref,
     high_ref,
     high_other_ref,
     whole_ref,
     left_ref,
     right_ref,
     kron_ref,
+    res_low_ref,
+    mixed_low_ref,
     out_ref,
     res_ref,
     rotated_ref,
     mixed_ref,
 ):
     terms, states, width, _ = rotated_ref.shape
-    inverse, rayleigh, row_scale = scales(keep_ref, mine_ref, theirs_ref, scale, width)
-    back = rayleigh * inverse
-
-    square = jnp.zeros((8, width), F32)
-    for start, halves in ((0, (low_ref,)), (states // 2, (high_ref, high_other_ref))):
-
-        def lefts(n, total):
-            p = start + n
-            sigma = functools.reduce(jnp.add, [half[n].astype(F32) for half in halves]) * row_scale
-            residual = sigma - back * whole_ref[p].astype(F32)
-            rounded = residual.astype(BF16)
-            res_ref[p] = rounded
-            mixed = jnp.dot(
-                left_ref[...].reshape(terms * width, width), rounded, preferred_element_type=F32
-            ).astype(BF16)
-            for k in range(terms):
-                mixed_ref[k, p] = mixed[k * width : (k + 1) * width]
-            return total + fold(residual * residual, width)
-
-        square = lax.fori_loop(0, states // 2, lefts, square, unroll=UNROLL)
-    mix_sites(res_ref, kron_ref, rotated_ref, 0, 2 * UNROLL)
-
-    def rights(n, total):
-        at = n * GROUP
+    half = states // 2
+    shift = sums_ref[0:1, :]
+    keep = keep_ref[0:1, :]
+    sums = shifted_residual(
+        half, shift, keep, high_ref, high_other_ref, whole_ref, left_ref, res_ref, mixed_ref
+    )
+
+    def sites(i, carry):
+        at = pl.ds(pl.multiple_of(i * TILE, TILE), TILE)
+        stack = jnp.concatenate([res_low_ref[:, at, :], res_ref[:, at, :]], axis=0).reshape(states * TILE, width)
+        turned = jnp.dot(kron_ref[...], stack, preferred_element_type=F32).astype(BF16)
+        rotated_ref[:, :, at, :] = turned.reshape(terms, states, TILE, width)
+        return carry
+
+    lax.fori_loop(0, width // TILE, sites, 0, unroll=UNROLL)
+    cross = jnp.zeros((8, width), F32)
+    for start, left_mixed_ref in ((0, mixed_low_ref), (half, mixed_ref)):
         for k in range(terms):
-            turned = rotated_ref[k, pl.ds(at, GROUP)].reshape(GROUP * width, width)
+            turned = rotated_ref[k, start : start + half].reshape(half * width, width)
             image = jnp.dot(turned, right_ref[k], preferred_element_type=F32)
-            held = mixed_ref[k, pl.ds(at, GROUP)].reshape(GROUP * width, width).astype(F32)
-            total = total + fold(held * image, width)
-        return total
-
-    cross = lax.fori_loop(0, states // GROUP, rights, jnp.zeros((8, width), F32))
+            held = left_mixed_ref[k].reshape(half * width, width).astype(F32)
+            cross = cross + fold(held * image, width)
+    res_square = sums_ref[1:2, :] + sums[0]
+    res_vector = sums_ref[2:3, :] + sums[1]
+    vector_square = sums_ref[3:4, :] + sums[2]
+    total = norm_ref[0:1, :] + norm_other_ref[0:1, :]
+    factor = scale / (total * scale + epsilon)
+    rayleigh = factor * (res_vector + shift * vector_square)
+    gap = rayleigh - shift
+    res_sq = factor * (res_square - 2.0 * gap * res_vector + gap * gap * vector_square)
+    change = gap * gap * (res_vector + shift * vector_square) - 2.0 * gap * (res_square + shift * res_vector)
     share = 1.0 / members
     out_ref[0:1, :] = rayleigh * share
-    out_ref[1:2, :] = jnp.full((1, width), jnp.sum(square) * (scale * share), F32)
-    out_ref[2:3, :] = jnp.full((1, width), jnp.sum(cross) * scale, F32)
+    out_ref[1:2, :] = jnp.maximum(res_sq, 0.0) * share
+    out_ref[2:3, :] = factor * (jnp.sum(cross) + share * change)
     out_ref[3:8, :] = jnp.zeros((5, width), F32)
 
 
-def own_rows_kernel(scale, keep_ref, guess_ref, mine_ref, theirs_ref, *refs):
-    low_ref, high_ref, high_other_ref, vector_ref, residual_ref = refs
+def own_rows_kernel(scale, members, keep_ref, norm_ref, norm_other_ref, share_ref, guess_ref, *refs):
+    low_ref, low_other_ref, high_ref, high_other_ref, vector_ref, residual_ref = refs
     rows, states, width = guess_ref.shape
-    inverse, rayleigh, row_scale = scales(keep_ref, mine_ref, theirs_ref, scale, width)
+    inverse = lax.rsqrt((norm_ref[0:1, :] + norm_other_ref[0:1, :]) * scale + epsilon)
+    row_scale = keep_ref[0:1, :] * inverse
+    rayleigh = share_ref[0:1, :] * members
     own = pl.ds(pl.multiple_of(lax.axis_index("term") * rows, TILE), rows)
     vector = guess_ref[...] * row_scale[None]
     vector_ref[...] = vector
-    high = high_ref[:, own, :].astype(F32) + high_other_ref[:, own, :].astype(F32)
-    sigma = jnp.concatenate([low_ref[:, own, :], high], axis=0) * row_scale[None]
-    residual_ref[...] = jnp.swapaxes(sigma, 0, 1) - rayleigh[None] * vector
+    sigma = jnp.concatenate(
+        [
+            mine_ref[:, own, :].astype(F32) + other_ref[:, own, :].astype(F32)
+            for mine_ref, other_ref in ((low_ref, low_other_ref), (high_ref, high_other_ref))
+        ],
+        axis=0,
+    )
+    residual_ref[...] = jnp.swapaxes(sigma * row_scale[None], 0, 1) - rayleigh[None] * vector
 
 
 def finish_kernel(vector_ref, residual_ref, *refs):
@@ -633,7 +680,7 @@
         cost_estimate=part_cost,
         name="apply_rows_last",
     )(*last_pieces, right, kron_own, columns, *parts)
-    norms = [norm_part]
+    norm = norm_part
     for hop in hops[1:]:
         if hop > 1:
             block, partial = lax.optimization_barrier((firsts[hop - 1], partial))
@@ -642,78 +689,77 @@
             if mid_spots:
                 turned = rotate(mid_spots, mid_pieces, kron, turned)
         left_far, partial = lax.optimization_barrier((lefts[hop], partial))
-        mixed, norm_far, _, vector = pl.pallas_call(
+        mixed, norm, _, vector = pl.pallas_call(
             functools.partial(lefts_kernel, far_spots[-1], rows, chips),
             out_shape=(jax.ShapeDtypeStruct((states, width, terms * width), BF16), tile, rotated_bf, whole_bf),
-            in_specs=[vmem] * (len(last_pieces) + 1) + [anywhere] * 2 + [vmem],
+            in_specs=[vmem] * (len(last_pieces) + 1) + [anywhere] * 2 + [vmem] * 2,
             out_specs=(vmem,) * 4,
             scratch_shapes=[square, pltpu.SemaphoreType.DMA((len(last_pieces),))],
             input_output_aliases={len(last_pieces) + 1: 2, len(last_pieces) + 2: 3},
             compiler_params=params(),
             cost_estimate=cost(stage_flops, 12 * states * width * width),
             name="received_lefts",
-        )(*last_pieces, kron, *turned, left_far)
-        norms.append(norm_far)
+        )(*last_pieces, kron, *turned, left_far, norm)
         last = hop == hops[-1]
-        stats = norms if last else norms[:1]
         right_far = rights[hop]
         parts = []
         bounds = (0, states // 2, states) if last else (0, states)
         for start, stop in zip(bounds[:-1], bounds[1:]):
-            outs = [jax.ShapeDtypeStruct((stop - start, width, width), BF16 if last else F32), tile]
-            part, stat, *unpacked = pl.pallas_call(
+            part_shape = jax.ShapeDtypeStruct((stop - start, width, width), BF16 if last else F32)
+            part, *unpacked = pl.pallas_call(
                 functools.partial(rights_kernel, start, stop),
-                out_shape=tuple(outs + ([jax.ShapeDtypeStruct(left.shape, BF16)] if start == 0 else [])),
-                in_specs=[vmem] * (4 + len(stats)),
-                out_specs=(vmem,) * (3 if start == 0 else 2),
+                out_shape=(part_shape,) + ((jax.ShapeDtypeStruct(left.shape, BF16),) if start == 0 else ()),
+                in_specs=[vmem] * 3,
+                out_specs=(vmem,) * (2 if start == 0 else 1),
                 compiler_params=params(),
                 cost_estimate=cost(stage_flops / 2, 12 * states * width * width),
                 name="received_rights",
-            )(right_far, mixed, vector, partial, *stats)
-            stats = [stat]
+            )(right_far, mixed, partial)
             if unpacked:
-                right_far = unpacked[0]
+                right_far, norm_other = lax.optimization_barrier((unpacked[0], to_sibling(norm)))
             parts.append(part)
         if not last:
             partial = parts[0]
-    low = pl.pallas_call(
-        add_kernel,
-        out_shape=jax.ShapeDtypeStruct(parts[0].shape, F32),
-        in_specs=[vmem] * 2,
-        out_specs=vmem,
-        compiler_params=params(),
-        cost_estimate=cost(parts[0].size, 8 * parts[0].size),
-        name="add_low_half",
-    )(parts[0], to_sibling(parts[0]))
-    halves = [low, parts[1], to_sibling(parts[1])]
-    stat_other = to_sibling(stat)
-
+    halves = []
+    for part in parts:
+        halves += [part, to_sibling(part)]
+    half_bf = jax.ShapeDtypeStruct((states // 2, width, width), BF16)
+    half_mixed = (terms, states // 2, width, width)
+    res_low, mixed_low, sums = pl.pallas_call(
+        low_kernel,
+        out_shape=(half_bf, jax.ShapeDtypeStruct(half_mixed, BF16), tile),
+        in_specs=[vmem] * 7,
+        out_specs=(vmem,) * 3,
+        compiler_params=params(),
+        cost_estimate=cost(stage_flops / 2, 3 * states * width * width),
+        name="residual_low",
+    )(keep, norm, norm_other, *halves[:2], vector, left)
     share = pl.pallas_call(
-        functools.partial(second_kernel, scale, members),
+        functools.partial(high_kernel, scale, members),
         out_shape=tile,
-        in_specs=[vmem] * 10,
+        in_specs=[vmem] * 12,
         out_specs=vmem,
         scratch_shapes=[
-            pltpu.VMEM(whole, BF16),
+            pltpu.VMEM(half_bf.shape, BF16),
             pltpu.VMEM(rotated, BF16),
-            pltpu.VMEM(rotated, BF16),
+            pltpu.VMEM(half_mixed, BF16),
         ],
         compiler_params=params(),
         cost_estimate=cost(3 * stage_flops, 6 * states * width * width),
-        name="apply_residual",
-    )(keep, stat, stat_other, *halves, vector, left, right, kron_own)
+        name="residual_high",
+    )(keep, norm, norm_other, sums, *halves[2:], vector, left, right, kron_own, res_low, mixed_low)
     crossed = everyone(share)
 
     local = jax.ShapeDtypeStruct((rows, states, width), F32)
     vector_own, residual_own = pl.pallas_call(
-        functools.partial(own_rows_kernel, scale),
+        functools.partial(own_rows_kernel, scale, members),
         out_shape=(local, local),
-        in_specs=[vmem] * 7,
+        in_specs=[vmem] * 9,
         out_specs=(vmem, vmem),
         compiler_params=params(),
         cost_estimate=cost(8 * guess.size, 16 * guess.size),
         name="own_rows",
-    )(keep, guess, stat, stat_other, *halves)
+    )(keep, norm, norm_other, share, guess, *halves)
 
     shares = [share, to_sibling(share)]
     gated, residual_own = lax.optimization_barrier((crossed[1:], residual_own))

time: 45.4 us -> 46.4 us (1.022)
  Pallas kernels: 24.8 us -> 26.8 us
  waiting for transfers between devices: 6.71 us -> 5.52 us
    pallas_call x5, Pallas kernels: 8.87 us -> 10.9 us  [the longest x1 5.7 us: shards(): pl.pallas_call(functools.partial(high_kernel, scale, members), out_shape=...]
    ppermute x11, waiting for transfers between devices: 3.55 us -> 2.48 us  [to_sibling(): return lax.ppermute(block, 'term', [(i, i ^ 1) for i in range(members)])]
  transfers between devices with their start and end apart: 18 -> 18, of which waited for: 8 -> 6; matrix products, arithmetic and copies ran while one was open for 0% -> 0% of each run, Pallas kernels for 33% -> 40%
where the time goes in v11:
time: 46.4 us; the launch traced here: 46.2 us
  Pallas kernels  26.8 us (58%)
  starting transfers between devices  12.2 us (26%)
  waiting for transfers between devices  5.52 us (12%)
  between operations  1.64 us (4%)
    ppermute x5, starting transfers between devices, to_next_chip(): lax.ppermute(block, 'term', [(i, (i + CORES) % members) for i in range(me...  6.81 us
    pallas_call x1, Pallas kernels, shards(): pl.pallas_call(functools.partial(high_kernel, scale, members), out_shape=...  5.7 us
    pallas_call x1, Pallas kernels, shards(): pl.pallas_call(functools.partial(lefts_kernel, far_spots[-1], rows, chips...  2.76 us
    pallas_call x1, Pallas kernels, shards(): pl.pallas_call(functools.partial(last_kernel, len(last_pieces)), out_shap...  2.54 us
    pallas_call x1, Pallas kernels, shards(): pl.pallas_call(low_kernel, out_shape=(half_bf, jax.ShapeDtypeStruct(half_...  2.52 us
    ppermute x11, waiting for transfers between devices, to_sibling(): return lax.ppermute(block, 'term', [(i, i ^ 1) for i in range(members)])  2.48 us
    pallas_call x2, Pallas kernels, rotate(): pl.pallas_call(functools.partial(rotate_kernel, spots, rows, chips), out_...  2.42 us
    ppermute x11, starting transfers between devices, to_sibling(): return lax.ppermute(block, 'term', [(i, i ^ 1) for i in range(members)])  2.39 us
  transfers between devices with their start and end apart: 18, of which 6 were waited for; matrix products, arithmetic and copies ran while one was open for 0% of the time, Pallas kernels for 40%

profile of v11, /device:TPU:0, one launch (start us, length us, event | category | flops | bytes accessed | tf_op | source)
XLA Modules:
  0.0 46.2 jit_solution(15400490713678280944)
XLA Ops:
  1.3 1.4 %first_chunk.1 = (bf16[17,32,256]{2,1,0:T(8,128)(2,1)S(1)}, f32[8,256]{1,0:T(8,128)S(1)}, f32[8,256]{1,0:T(8,128)S(1)}, bf16[3,272,128]{2,1,0:T(8,128)(2,1)S(1)}) custom-call(s32[1,1]{1,0:T(1,128)} %bitcast.6.rank_in, f32[64,16,256]{2,1,0:T(8,128)} %bitcast.7, bf16[3,16,16]{2,1,0:T(8,128)(2,1)} %bitcast.12, bf16[3,256,256]{2,1,0:T(8,128)(2,1)} %bitcast.10), custom_call_target="tpu_custom_call" | custom-call | flops 5242 | bytes 7864 | tf_op jit(solution)/shard_map/first_chunk/pallas_call | solution.py:522
  2.7 0.5 %collective-permute-start = (bf16[17,32,256]{2,1,0:T(8,128)(2,1)S(1)}, bf16[17,32,256]{2,1,0:T(8,128)(2,1)S(1)}, u32[]{:S(2)}, u32[]{:S(2)}) collective-permute-start(bf16[17,32,256]{2,1,0:T(8,128)(2,1)S(1)} %get-tuple-element.53.chunk_ref.refs_0_), channel_id=1, source_target_pairs={{0,1},{1,0},{2,3},{3,2},{4,5},{5,4},{6,7},{7,6},{8,9},{9,8},{10,11... | collective-permute-start | bytes 835592 | tf_op jit(solution)/shard_map/ppermute | solution.py:499
  3.2 2.6 %collective-permute-start.2 = (bf16[17,32,256]{2,1,0:T(8,128)(2,1)S(1)}, bf16[17,32,256]{2,1,0:T(8,128)(2,1)S(1)}, u32[]{:S(2)}, u32[]{:S(2)}) collective-permute-start(bf16[17,32,256]{2,1,0:T(8,128)(2,1)S(1)} %get-tuple-element.53.chunk_ref.refs_0_), channel_id=1, source_target_pairs={{0,2},{1,3},{2,0},{3,1},{4,6},{5,7},{6,4},{7,5},{8,10},{9,11},{10,... | collective-permute-start | bytes 835592 | tf_op jit(solution)/shard_map/ppermute | solution.py:502
  5.8 1.3 %collective-permute-start.7 = (bf16[3,272,128]{2,1,0:T(8,128)(2,1)S(1)}, bf16[3,272,128]{2,1,0:T(8,128)(2,1)S(1)}, u32[]{:S(2)}, u32[]{:S(2)}) collective-permute-start(bf16[3,272,128]{2,1,0:T(8,128)(2,1)S(1)} %get-tuple-element.61), channel_id=1, source_target_pairs={{4,0},{8,4},{12,8},{16,12},{20,16},{24,20},{28,24},{5,1},{9,5},{13... | collective-permute-start | bytes 626696 | tf_op jit(solution)/shard_map/ppermute | solution.py:571
  7.1 0.0 collective-permute-done.refs_3_
  7.1 1.3 %prepare.1 = (f32[8,256]{1,0:T(8,128)S(1)}, bf16[3,272,128]{2,1,0:T(8,128)(2,1)S(1)}, bf16[3,256,256]{2,1,0:T(8,128)(2,1)S(1)}, bf16[16,16,256]{2,1,0:T(8,128)(2,1)S(1)}, bf16[16,16,256]{2,1,0:T(8,128)(2,1)S(1)}) custom-call(f32[8,256]{1,0:T(8,128)S(1)} %get-tuple-element.51.keep_ref, f32[8,256]{1,0:T(8,128)S(1)} %get-tuple-element.54.squares_ref, ...), custom_call_target="tpu_custom_call" | custom-call | flops 10485 | bytes 15728 | tf_op jit(solution)/shard_map/prepare/pallas_call | solution.py:540
  8.4 0.2 collective-permute-start.4
  8.6 0.3 collective-permute-start.3
  9.0 0.2 collective-permute-start.6
  9.2 0.4 spread_site.2.refs_6_.refs_5_.refs_3_.kron_ref
  9.6 0.3 collective-permute-done.4.refs_5_
  9.8 1.7 %collective-permute-start.1 = (bf16[16,16,256]{2,1,0:T(8,128)(2,1)S(1)}, bf16[16,16,256]{2,1,0:T(8,128)(2,1)S(1)}, u32[]{:S(2)}, u32[]{:S(2)}) collective-permute-start(bf16[16,16,256]{2,1,0:T(8,128)(2,1)S(1)} %get-tuple-element.55.refs_2_), channel_id=1, source_target_pairs={{0,2},{1,3},{2,0},{3,1},{4,6},{5,7},{6,4},{7,5},{8,10},{9,11},{10,... | collective-permute-start | bytes 393224 | tf_op jit(solution)/shard_map/ppermute | solution.py:502
  11.5 0.0 collective-permute-done.3.refs_4_
  11.5 0.4 collective-permute-start.10
  11.9 1.0 %rotate_own.1 = (bf16[3,16,128,256]{3,2,1,0:T(8,128)(2,1)S(1)}, bf16[256,768]{1,0:T(8,128)(2,1)S(1)}) custom-call(bf16[17,32,256]{2,1,0:T(8,128)(2,1)S(1)} %get-tuple-element.53.chunk_ref.refs_0_, bf16[16,16,256]{2,1,0:T(8,128)(2,1)S(1)} %get-tuple-element.56.refs_1_, bf16[16,16,256]{2,1,0:T(8,128)(2,1)S(1)} %get-tuple-element.55.refs_2_, ...), custom_call_target="tpu_custom_call" | custom-call | flops 16106127 | bytes 83886 | tf_op jit(solution)/shard_map/rotate_own/pallas_call | solution.py:603
  12.8 0.4 collective-permute-done.2.chunk_ref.refs_0_
  13.3 0.0 collective-permute-start.5
  13.3 0.4 spread_site.3.refs_6_.refs_4_.refs_2_
  13.7 1.4 %rotate_here.1 = (bf16[3,16,256,256]{3,2,1,0:T(8,128)(2,1)S(1)}, bf16[16,256,256]{2,1,0:T(8,128)(2,1)S(1)}) custom-call(bf16[17,32,256]{2,1,0:T(8,128)(2,1)S(1)} %get-tuple-element.53.chunk_ref.refs_0_, bf16[16,16,256]{2,1,0:T(8,128)(2,1)S(1)} %get-tuple-element.56.refs_1_, bf16[16,16,256]{2,1,0:T(8,128)(2,1)S(1)} %get-tuple-element.55.refs_2_, ...), custom_call_target="tpu_custom_call" | custom-call | flops 16106127 | bytes 83886 | tf_op jit(solution)/shard_map/rotate_here/pallas_call | solution.py:617
  15.0 0.0 collective-permute-done.7
  15.0 1.0 %collective-permute-done.6.refs_2_ = bf16[16,16,256]{2,1,0:T(8,128)(2,1)S(1)} collective-permute-done((bf16[16,16,256]{2,1,0:T(8,128)(2,1)S(1)}, bf16[16,16,256]{2,1,0:T(8,128)(2,1)S(1)}, u32[]{:S(2)}, u32[]{:S(2)}) %collective-permute-start.6) | collective-permute-done | bytes 131104 | tf_op jit(solution)/shard_map/ppermute | solution.py:502
  16.1 0.0 collective-permute-start.8
  16.1 2.0 %collective-permute-start.11 = (bf16[3,272,128]{2,1,0:T(8,128)(2,1)S(1)}, bf16[3,272,128]{2,1,0:T(8,128)(2,1)S(1)}, u32[]{:S(2)}, u32[]{:S(2)}) collective-permute-start(bf16[3,272,128]{2,1,0:T(8,128)(2,1)S(1)} %broadcast_select_fusion.packed_ref), channel_id=1, source_target_pairs={{0,2},{1,3},{2,0},{3,1},{4,6},{5,7},{6,4},{7,5},{8,10},{9,11},{10,... | collective-permute-start | bytes 626696 | tf_op jit(solution)/shard_map/ppermute | solution.py:502
  18.1 1.1 %apply_rows_here.1 = (bf16[16,384,256]{2,1,0:T(8,128)(2,1)S(1)}, bf16[3,256,256]{2,1,0:T(8,128)(2,1)S(1)}) custom-call(bf16[3,16,128,256]{3,2,1,0:T(8,128)(2,1)S(1)} %get-tuple-element.71.rotated_ref, bf16[3,272,128]{2,1,0:T(8,128)(2,1)S(1)} %broadcast_select_fusion.packed_ref), custom_call_target="tpu_custom_call" | custom-call | flops 16106127 | bytes 83886 | tf_op jit(solution)/shard_map/apply_rows_here/pallas_call | solution.py:638
  19.2 0.0 collective-permute-done.8.refs_3_
  19.2 0.0 collective-permute-done.5.refs_1_
  19.3 1.1 %rotate_crossed.1 = (bf16[3,16,256,256]{3,2,1,0:T(8,128)(2,1)S(1)}, bf16[16,256,256]{2,1,0:T(8,128)(2,1)S(1)}) custom-call(bf16[17,32,256]{2,1,0:T(8,128)(2,1)S(1)} %collective-permute-done.2.chunk_ref.refs_0_, bf16[17,32,256]{2,1,0:T(8,128)(2,1)S(1)} %collective-permute-done.5.refs_1_, ...), custom_call_target="tpu_custom_call", output_to_operand_aliasing={{0}: (5, {}), {1}: (6, {})} | custom-call | flops 16106127 | bytes 83886 | tf_op jit(solution)/shard_map/rotate_crossed/pallas_call | solution.py:617
  20.3 0.0 collective-permute-done.1.refs_0_
  20.3 0.3 collective-permute-start.9
  20.6 1.4 %apply_rows_crossed.1.refs_6_ = bf16[16,288,256]{2,1,0:T(8,128)(2,1)S(1)} custom-call(bf16[17,32,256]{2,1,0:T(8,128)(2,1)S(1)} %collective-permute-done.2.chunk_ref.refs_0_, bf16[17,32,256]{2,1,0:T(8,128)(2,1)S(1)} %collective-permute-done.5.refs_1_, bf16[16,16,256]{2,1,0:T(8,128)(2,1)S(1)} %collective-permute-done.6.refs_2_, ...), custom_call_target="tpu_custom_call" | custom-call | flops 16106127 | bytes 83886 | tf_op jit(solution)/shard_map/apply_rows_crossed/pallas_call | solution.py:659
  22.0 0.0 collective-permute-done.9.refs_1_
  22.0 2.5 %apply_rows_last.1.before_ref = f32[16,256,256]{2,1,0:T(8,128)S(1)} custom-call(bf16[16,16,256]{2,1,0:T(8,128)(2,1)S(1)} %collective-permute-done.1.refs_0_, bf16[16,16,256]{2,1,0:T(8,128)(2,1)S(1)} %collective-permute-done.9.refs_1_, bf16[3,256,256]{2,1,0:T(8,128)(2,1)S(1)} %get-tuple-element.78.refs_4_.refs_2_.right_ref, ...), custom_call_target="tpu_custom_call" | custom-call | flops 16106127 | bytes 83886 | tf_op jit(solution)/shard_map/apply_rows_last/pallas_call | solution.py:673
  24.6 0.0 collective-permute-done.10.refs_5_
  24.6 2.8 %received_lefts.1 = (bf16[16,256,768]{2,1,0:T(8,128)(2,1)S(1)}, f32[8,256]{1,0:T(8,128)S(1)}, bf16[3,16,256,256]{3,2,1,0:T(8,128)(2,1)S(1)}, bf16[16,256,256]{2,1,0:T(8,128)(2,1)S(1)}) custom-call(bf16[16,16,256]{2,1,0:T(8,128)(2,1)S(1)} %collective-permute-done.1.refs_0_, ...), custom_call_target="tpu_custom_call", output_to_operand_aliasing={{2}: (3, {}), {3}: (4, {})} | custom-call | flops 16106127 | bytes 125829 | tf_op jit(solution)/shard_map/received_lefts/pallas_call | solution.py:692
  27.4 0.4 collective-permute-start.12
  27.7 0.0 collective-permute-done.11.packed_ref
  27.7 1.2 %received_rights.2 = (bf16[8,256,256]{2,1,0:T(8,128)(2,1)S(1)}, bf16[3,256,256]{2,1,0:T(8,128)(2,1)S(1)}) custom-call(bf16[3,272,128]{2,1,0:T(8,128)(2,1)S(1)} %collective-permute-done.11.packed_ref, bf16[16,256,768]{2,1,0:T(8,128)(2,1)S(1)} %get-tuple-element.84.mixed_ref, f32[16,256,256]{2,1,0:T(8,128)S(1)} %apply_rows_last.1.before_ref), custom_call_target="tpu_custom_call" | custom-call | flops 8053063 | bytes 125829 | tf_op jit(solution)/shard_map/received_rights/pallas_call | solution.py:709
  28.9 0.3 collective-permute-start.13
  29.2 0.0 collective-permute-done.12.norm_other_ref
  29.2 1.1 %received_rights.3.high_ref.refs_2_ = bf16[8,256,256]{2,1,0:T(8,128)(2,1)S(1)} custom-call(bf16[3,256,256]{2,1,0:T(8,128)(2,1)S(1)} %get-tuple-element.91.packed_ref, bf16[16,256,768]{2,1,0:T(8,128)(2,1)S(1)} %get-tuple-element.84.mixed_ref, f32[16,256,256]{2,1,0:T(8,128)S(1)} %apply_rows_last.1.before_ref), custom_call_target="tpu_custom_call" | custom-call | flops 8053063 | bytes 125829 | tf_op jit(solution)/shard_map/received_rights/pallas_call | solution.py:709
  30.2 0.4 collective-permute-start.14
  30.6 1.0 %collective-permute-done.13.low_other_ref.refs_1_ = bf16[8,256,256]{2,1,0:T(8,128)(2,1)S(1)} collective-permute-done((bf16[8,256,256]{2,1,0:T(8,128)(2,1)S(1)}, bf16[8,256,256]{2,1,0:T(8,128)(2,1)S(1)}, u32[]{:S(2)}, u32[]{:S(2)}) %collective-permute-start.13) | collective-permute-done | bytes 1048608 | tf_op jit(solution)/shard_map/ppermute | solution.py:499
  31.6 2.5 %residual_low.1 = (bf16[8,256,256]{2,1,0:T(8,128)(2,1)S(1)}, bf16[3,8,256,256]{3,2,1,0:T(8,128)(2,1)S(1)}, f32[8,256]{1,0:T(8,128)S(1)}) custom-call(f32[8,256]{1,0:T(8,128)S(1)} %get-tuple-element.51.keep_ref, f32[8,256]{1,0:T(8,128)S(1)} %get-tuple-element.83.norm_ref, f32[8,256]{1,0:T(8,128)S(1)} %collective-permute-done.12.norm_other_ref, ...), custom_call_target="tpu_custom_call" | custom-call | flops 8053063 | bytes 31457 | tf_op jit(solution)/shard_map/residual_low/pallas_call | solution.py:728
  34.1 0.0 collective-permute-done.14.high_other_ref.refs_3_
  34.1 0.0 copy-start
  34.2 5.7 %residual_high.1.share_ref.refs_0_ = f32[8,256]{1,0:T(8,128)S(1)} custom-call(f32[8,256]{1,0:T(8,128)S(1)} %get-tuple-element.51.keep_ref, f32[8,256]{1,0:T(8,128)S(1)} %get-tuple-element.83.norm_ref, f32[8,256]{1,0:T(8,128)S(1)} %collective-permute-done.12.norm_other_ref, f32[8,256]{1,0:T(8,128)S(1)} %get-tuple-element.90.sums_ref, ...), custom_call_target="tpu_custom_call" | custom-call | flops 48318384 | bytes 62914 | tf_op jit(solution)/shard_map/residual_high/pallas_call | solution.py:737
  39.9 1.7 %collective-permute-start.15 = (f32[8,256]{1,0:T(8,128)S(1)}, f32[8,256]{1,0:T(8,128)S(1)}, u32[]{:S(2)}, u32[]{:S(2)}) collective-permute-start(f32[8,256]{1,0:T(8,128)S(1)} %residual_high.1.share_ref.refs_0_), channel_id=1, source_target_pairs={{0,2},{1,3},{2,0},{3,1},{4,6},{5,7},{6,4},{7,5},{8,10},{9,11},{10,... | collective-permute-start | bytes 24584 | tf_op jit(solution)/shard_map/ppermute | solution.py:512
  41.5 0.0 collective-permute-start.16
  41.5 0.0 copy-done
  41.5 0.5 own_rows.1
  42.0 1.6 %collective-permute-done.15.refs_2_ = f32[8,256]{1,0:T(8,128)S(1)} collective-permute-done((f32[8,256]{1,0:T(8,128)S(1)}, f32[8,256]{1,0:T(8,128)S(1)}, u32[]{:S(2)}, u32[]{:S(2)}) %collective-permute-start.15) | collective-permute-done | bytes 8224 | tf_op jit(solution)/shard_map/ppermute | solution.py:512
  43.6 0.0 collective-permute-start.17
  43.6 0.0 collective-permute-done.16.refs_1_
  43.6 1.2 %collective-permute-done.17.refs_3_ = f32[8,256]{1,0:T(8,128)S(1)} collective-permute-done((f32[8,256]{1,0:T(8,128)S(1)}, f32[8,256]{1,0:T(8,128)S(1)}, u32[]{:S(2)}, u32[]{:S(2)}) %collective-permute-start.17) | collective-permute-done | bytes 8224 | tf_op jit(solution)/shard_map/ppermute | solution.py:499
  44.8 1.3 %finish.1 = (f32[64,16,256]{2,1,0:T(8,128)}, f32[1]{0:T(128)}) custom-call(f32[64,16,256]{2,1,0:T(8,128)S(1)} %get-tuple-element.94.vector_ref, f32[64,16,256]{2,1,0:T(8,128)S(1)} %get-tuple-element.96.residual_ref, f32[8,256]{1,0:T(8,128)S(1)} %residual_high.1.share_ref.refs_0_, f32[8,256]{1,0:T(8,128)S(1)} %collective-permute-done.16.refs_1_, ...), custom_call_target="tpu_custom_call" | custom-call | flops 7864 | bytes 31457 | tf_op jit(solution)/shard_map/finish/pallas_call | solution.py:767
  (1 shorter events, 0.0 us)
Async XLA Ops:
  2.7 4.4 %collective-permute-start = (bf16[17,32,256]{2,1,0:T(8,128)(2,1)S(1)}, bf16[17,32,256]{2,1,0:T(8,128)(2,1)S(1)}, u32[]{:S(2)}, u32[]{:S(2)}) collective-permute-start(bf16[17,32,256]{2,1,0:T(8,128)(2,1)S(1)} %get-tuple-element.53.chunk_ref.refs_0_), channel_id=1, source_target_pairs={{0,1},{1,0},{2,3},{3,2},{4,5},{5,4},{6,7},{7,6},{8,9},{9,8},{10,11... | collective-permute-start | bytes 835592 | tf_op jit(solution)/shard_map/ppermute | solution.py:499
  3.2 10.1 %collective-permute-start.2 = (bf16[17,32,256]{2,1,0:T(8,128)(2,1)S(1)}, bf16[17,32,256]{2,1,0:T(8,128)(2,1)S(1)}, u32[]{:S(2)}, u32[]{:S(2)}) collective-permute-start(bf16[17,32,256]{2,1,0:T(8,128)(2,1)S(1)} %get-tuple-element.53.chunk_ref.refs_0_), channel_id=1, source_target_pairs={{0,2},{1,3},{2,0},{3,1},{4,6},{5,7},{6,4},{7,5},{8,10},{9,11},{10,... | collective-permute-start | bytes 835592 | tf_op jit(solution)/shard_map/ppermute | solution.py:502
  5.8 9.3 %collective-permute-start.7 = (bf16[3,272,128]{2,1,0:T(8,128)(2,1)S(1)}, bf16[3,272,128]{2,1,0:T(8,128)(2,1)S(1)}, u32[]{:S(2)}, u32[]{:S(2)}) collective-permute-start(bf16[3,272,128]{2,1,0:T(8,128)(2,1)S(1)} %get-tuple-element.61), channel_id=1, source_target_pairs={{4,0},{8,4},{12,8},{16,12},{20,16},{24,20},{28,24},{5,1},{9,5},{13... | collective-permute-start | bytes 626696 | tf_op jit(solution)/shard_map/ppermute | solution.py:571
  8.4 1.4 %collective-permute-start.4 = (bf16[16,16,256]{2,1,0:T(8,128)(2,1)S(1)}, bf16[16,16,256]{2,1,0:T(8,128)(2,1)S(1)}, u32[]{:S(2)}, u32[]{:S(2)}) collective-permute-start(bf16[16,16,256]{2,1,0:T(8,128)(2,1)S(1)} %get-tuple-element.55.refs_2_), channel_id=1, source_target_pairs={{0,1},{1,0},{2,3},{3,2},{4,5},{5,4},{6,7},{7,6},{8,9},{9,8},{10,11... | collective-permute-start | bytes 393224 | tf_op jit(solution)/shard_map/ppermute | solution.py:499
  8.6 2.8 %collective-permute-start.3 = (bf16[16,16,256]{2,1,0:T(8,128)(2,1)S(1)}, bf16[16,16,256]{2,1,0:T(8,128)(2,1)S(1)}, u32[]{:S(2)}, u32[]{:S(2)}) collective-permute-start(bf16[16,16,256]{2,1,0:T(8,128)(2,1)S(1)} %get-tuple-element.56.refs_1_), channel_id=1, source_target_pairs={{0,1},{1,0},{2,3},{3,2},{4,5},{5,4},{6,7},{7,6},{8,9},{9,8},{10,11... | collective-permute-start | bytes 393224 | tf_op jit(solution)/shard_map/ppermute | solution.py:499
  9.0 7.1 %collective-permute-start.6 = (bf16[16,16,256]{2,1,0:T(8,128)(2,1)S(1)}, bf16[16,16,256]{2,1,0:T(8,128)(2,1)S(1)}, u32[]{:S(2)}, u32[]{:S(2)}) collective-permute-start(bf16[16,16,256]{2,1,0:T(8,128)(2,1)S(1)} %get-tuple-element.56.refs_1_), channel_id=1, source_target_pairs={{0,2},{1,3},{2,0},{3,1},{4,6},{5,7},{6,4},{7,5},{8,10},{9,11},{10,... | collective-permute-start | bytes 393224 | tf_op jit(solution)/shard_map/ppermute | solution.py:502
  9.8 10.5 %collective-permute-start.1 = (bf16[16,16,256]{2,1,0:T(8,128)(2,1)S(1)}, bf16[16,16,256]{2,1,0:T(8,128)(2,1)S(1)}, u32[]{:S(2)}, u32[]{:S(2)}) collective-permute-start(bf16[16,16,256]{2,1,0:T(8,128)(2,1)S(1)} %get-tuple-element.55.refs_2_), channel_id=1, source_target_pairs={{0,2},{1,3},{2,0},{3,1},{4,6},{5,7},{6,4},{7,5},{8,10},{9,11},{10,... | collective-permute-start | bytes 393224 | tf_op jit(solution)/shard_map/ppermute | solution.py:502
  11.5 13.1 %collective-permute-start.10 = (bf16[3,272,128]{2,1,0:T(8,128)(2,1)S(1)}, bf16[3,272,128]{2,1,0:T(8,128)(2,1)S(1)}, u32[]{:S(2)}, u32[]{:S(2)}) collective-permute-start(bf16[3,272,128]{2,1,0:T(8,128)(2,1)S(1)} %get-tuple-element.77), channel_id=1, source_target_pairs={{0,2},{1,3},{2,0},{3,1},{4,6},{5,7},{6,4},{7,5},{8,10},{9,11},{10,... | collective-permute-start | bytes 626696 | tf_op jit(solution)/shard_map/ppermute | solution.py:502
  13.3 6.0 %collective-permute-start.5 = (bf16[17,32,256]{2,1,0:T(8,128)(2,1)S(1)}, bf16[17,32,256]{2,1,0:T(8,128)(2,1)S(1)}, u32[]{:S(2)}, u32[]{:S(2)}) collective-permute-start(bf16[17,32,256]{2,1,0:T(8,128)(2,1)S(1)} %collective-permute-done.2.chunk_ref.refs_0_), channel_id=1, source_target_pairs={{0,1},{1,0},{2,3},{3,2},{4,5},{5,4},{6,7},{7,6},{8,9},{9,8},{10,11... | collective-permute-start | bytes 835592 | tf_op jit(solution)/shard_map/ppermute | solution.py:499
  16.1 3.2 %collective-permute-start.8 = (bf16[16,16,256]{2,1,0:T(8,128)(2,1)S(1)}, bf16[16,16,256]{2,1,0:T(8,128)(2,1)S(1)}, u32[]{:S(2)}, u32[]{:S(2)}) collective-permute-start(bf16[16,16,256]{2,1,0:T(8,128)(2,1)S(1)} %collective-permute-done.6.refs_2_), channel_id=1, source_target_pairs={{0,1},{1,0},{2,3},{3,2},{4,5},{5,4},{6,7},{7,6},{8,9},{9,8},{10,11... | collective-permute-start | bytes 393224 | tf_op jit(solution)/shard_map/ppermute | solution.py:499
  16.1 11.6 %collective-permute-start.11 = (bf16[3,272,128]{2,1,0:T(8,128)(2,1)S(1)}, bf16[3,272,128]{2,1,0:T(8,128)(2,1)S(1)}, u32[]{:S(2)}, u32[]{:S(2)}) collective-permute-start(bf16[3,272,128]{2,1,0:T(8,128)(2,1)S(1)} %broadcast_select_fusion.packed_ref), channel_id=1, source_target_pairs={{0,2},{1,3},{2,0},{3,1},{4,6},{5,7},{6,4},{7,5},{8,10},{9,11},{10,... | collective-permute-start | bytes 626696 | tf_op jit(solution)/shard_map/ppermute | solution.py:502
  20.3 1.7 %collective-permute-start.9 = (bf16[16,16,256]{2,1,0:T(8,128)(2,1)S(1)}, bf16[16,16,256]{2,1,0:T(8,128)(2,1)S(1)}, u32[]{:S(2)}, u32[]{:S(2)}) collective-permute-start(bf16[16,16,256]{2,1,0:T(8,128)(2,1)S(1)} %collective-permute-done.1.refs_0_), channel_id=1, source_target_pairs={{0,1},{1,0},{2,3},{3,2},{4,5},{5,4},{6,7},{7,6},{8,9},{9,8},{10,11... | collective-permute-start | bytes 393224 | tf_op jit(solution)/shard_map/ppermute | solution.py:499
  27.4 1.8 %collective-permute-start.12 = (f32[8,256]{1,0:T(8,128)S(1)}, f32[8,256]{1,0:T(8,128)S(1)}, u32[]{:S(2)}, u32[]{:S(2)}) collective-permute-start(f32[8,256]{1,0:T(8,128)S(1)} %get-tuple-element.83.norm_ref), channel_id=1, source_target_pairs={{0,1},{1,0},{2,3},{3,2},{4,5},{5,4},{6,7},{7,6},{8,9},{9,8},{10,11... | collective-permute-start | bytes 24584 | tf_op jit(solution)/shard_map/ppermute | solution.py:499
  28.9 2.7 %collective-permute-start.13 = (bf16[8,256,256]{2,1,0:T(8,128)(2,1)S(1)}, bf16[8,256,256]{2,1,0:T(8,128)(2,1)S(1)}, u32[]{:S(2)}, u32[]{:S(2)}) collective-permute-start(bf16[8,256,256]{2,1,0:T(8,128)(2,1)S(1)} %get-tuple-element.88.low_ref.refs_0_), channel_id=1, source_target_pairs={{0,1},{1,0},{2,3},{3,2},{4,5},{5,4},{6,7},{7,6},{8,9},{9,8},{10,11... | collective-permute-start | bytes 3145736 | tf_op jit(solution)/shard_map/ppermute | solution.py:499
  30.2 3.9 %collective-permute-start.14 = (bf16[8,256,256]{2,1,0:T(8,128)(2,1)S(1)}, bf16[8,256,256]{2,1,0:T(8,128)(2,1)S(1)}, u32[]{:S(2)}, u32[]{:S(2)}) collective-permute-start(bf16[8,256,256]{2,1,0:T(8,128)(2,1)S(1)} %received_rights.3.high_ref.refs_2_), channel_id=1, source_target_pairs={{0,1},{1,0},{2,3},{3,2},{4,5},{5,4},{6,7},{7,6},{8,9},{9,8},{10,11... | collective-permute-start | bytes 3145736 | tf_op jit(solution)/shard_map/ppermute | solution.py:499
  34.1 7.4 %copy-start = (f32[1,64,16,256]{3,2,1,0:T(8,128)S(1)}, f32[1,64,16,256]{3,2,1,0:T(8,128)}, u32[]{:S(2)}) copy-start(f32[1,64,16,256]{3,2,1,0:T(8,128)} %param.5) | copy-start | bytes 3145732
  39.9 3.7 %collective-permute-start.15 = (f32[8,256]{1,0:T(8,128)S(1)}, f32[8,256]{1,0:T(8,128)S(1)}, u32[]{:S(2)}, u32[]{:S(2)}) collective-permute-start(f32[8,256]{1,0:T(8,128)S(1)} %residual_high.1.share_ref.refs_0_), channel_id=1, source_target_pairs={{0,2},{1,3},{2,0},{3,1},{4,6},{5,7},{6,4},{7,5},{8,10},{9,11},{10,... | collective-permute-start | bytes 24584 | tf_op jit(solution)/shard_map/ppermute | solution.py:512
  41.5 2.0 %collective-permute-start.16 = (f32[8,256]{1,0:T(8,128)S(1)}, f32[8,256]{1,0:T(8,128)S(1)}, u32[]{:S(2)}, u32[]{:S(2)}) collective-permute-start(f32[8,256]{1,0:T(8,128)S(1)} %residual_high.1.share_ref.refs_0_), channel_id=1, source_target_pairs={{0,1},{1,0},{2,3},{3,2},{4,5},{5,4},{6,7},{7,6},{8,9},{9,8},{10,11... | collective-permute-start | bytes 24584 | tf_op jit(solution)/shard_map/ppermute | solution.py:499
  43.6 1.2 %collective-permute-start.17 = (f32[8,256]{1,0:T(8,128)S(1)}, f32[8,256]{1,0:T(8,128)S(1)}, u32[]{:S(2)}, u32[]{:S(2)}) collective-permute-start(f32[8,256]{1,0:T(8,128)S(1)} %collective-permute-done.15.refs_2_), channel_id=1, source_target_pairs={{0,1},{1,0},{2,3},{3,2},{4,5},{5,4},{6,7},{7,6},{8,9},{9,8},{10,11... | collective-permute-start | bytes 24584 | tf_op jit(solution)/shard_map/ppermute | solution.py:499

commit v12 on v11

--- a/solution.py
+++ b/solution.py
@@ -10,8 +10,8 @@
 epsilon = 1e-06
 CORES = 2
 TILE = 16
-UNROLL = 8
-GROUP = 8
+UNROLL = 2
+GROUP = 2
 VMEM_LIMIT = 20 * 1024 * 1024
 F32 = jnp.float32
 BF16 = jnp.bfloat16
@@ -239,11 +239,16 @@
 
 def turn(right_ref, rotated_ref, turned_ref):
     terms, states, count, width = rotated_ref.shape
-    for k in range(terms):
-        for n in range(0, states, 8):
-            source = rotated_ref[k, n : n + 8].reshape(8 * count, width)
+
+    def step(n, carry):
+        at = n * 4
+        for k in range(terms):
+            source = rotated_ref[k, pl.ds(at, 4)].reshape(4 * count, width)
             turned = jnp.dot(source, right_ref[k], preferred_element_type=F32).astype(BF16)
-            turned_ref[n : n + 8, k * count : (k + 1) * count, :] = turned.reshape(8, count, width)
+            turned_ref[pl.ds(at, 4), k * count : (k + 1) * count, :] = turned.reshape(4, count, width)
+        return carry
+
+    lax.fori_loop(0, states // 4, step, 0)
 
 
 def here_kernel(rotated_ref, packed_ref, turned_ref, right_ref):
@@ -327,7 +332,7 @@
     lax.fori_loop(0, (stop - start) // GROUP, rights, 0)
 
 
-def shifted_residual(start, shift, keep, mine_ref, other_ref, whole_ref, left_ref, res_ref, mixed_ref):
+def shifted_residual(products, start, shift, keep, mine_ref, other_ref, whole_ref, left_ref, res_ref, mixed_ref):
     count, width, _ = res_ref.shape
     terms = left_ref.shape[0]
     zero = jnp.zeros((8, width), F32)
@@ -343,13 +348,10 @@
         ).astype(BF16)
         for k in range(terms):
             mixed_ref[k, n] = mixed[k * width : (k + 1) * width]
-        return (
-            sums[0] + fold(residual * residual, width),
-            sums[1] + fold(residual * held, width),
-            sums[2] + fold(held * held, width),
-        )
-
-    sums = lax.fori_loop(0, count, lefts, (zero, zero, zero), unroll=UNROLL)
+        square = sums[0] + fold(residual * residual, width)
+        return (square, sums[1] + fold(sigma * held, width)) if products else (square,)
+
+    sums = lax.fori_loop(0, count, lefts, (zero,) * (2 if products else 1), unroll=UNROLL)
     return [jnp.sum(total) for total in sums]
 
 
@@ -374,15 +376,16 @@
         sigma = low_ref[n].astype(F32) + low_other_ref[n].astype(F32)
         return sums[0] + fold(sigma * held, width), sums[1] + fold(held * held, width)
 
-    cross, square = lax.fori_loop(0, count, products, (zero, zero), unroll=UNROLL)
+    cross, square = lax.fori_loop(0, count, products, (zero, zero), unroll=4)
+    cross = jnp.sum(cross)
     total = norm_ref[0:1, :] + norm_other_ref[0:1, :]
     floor = jnp.maximum(jnp.maximum(jnp.full((1, width), jnp.sum(square), F32), 0.25 * total), 1e-30)
-    shift = jnp.sum(cross) / floor
-    sums = shifted_residual(0, shift, keep, low_ref, low_other_ref, whole_ref, left_ref, res_ref, mixed_ref)
+    shift = cross / floor
+    sums = shifted_residual(False, 0, shift, keep, low_ref, low_other_ref, whole_ref, left_ref, res_ref, mixed_ref)
     out_ref[0:1, :] = shift
-    for n, value in enumerate(sums):
-        out_ref[n + 1 : n + 2, :] = jnp.full((1, width), value, F32)
-    out_ref[4:8, :] = jnp.zeros((4, width), F32)
+    out_ref[1:2, :] = jnp.full((1, width), sums[0], F32)
+    out_ref[2:3, :] = jnp.full((1, width), cross, F32)
+    out_ref[3:8, :] = jnp.zeros((5, width), F32)
 
 
 def high_kernel(
@@ -410,7 +413,7 @@
     shift = sums_ref[0:1, :]
     keep = keep_ref[0:1, :]
     sums = shifted_residual(
-        half, shift, keep, high_ref, high_other_ref, whole_ref, left_ref, res_ref, mixed_ref
+        True, half, shift, keep, high_ref, high_other_ref, whole_ref, left_ref, res_ref, mixed_ref
     )
 
     def sites(i, carry):
@@ -423,20 +426,26 @@
     lax.fori_loop(0, width // TILE, sites, 0, unroll=UNROLL)
     cross = jnp.zeros((8, width), F32)
     for start, left_mixed_ref in ((0, mixed_low_ref), (half, mixed_ref)):
-        for k in range(terms):
-            turned = rotated_ref[k, start : start + half].reshape(half * width, width)
-            image = jnp.dot(turned, right_ref[k], preferred_element_type=F32)
-            held = left_mixed_ref[k].reshape(half * width, width).astype(F32)
-            cross = cross + fold(held * image, width)
+
+        def rights(n, cross):
+            at = n * 4
+            for k in range(terms):
+                turned = rotated_ref[k, pl.ds(start + at, 4)].reshape(4 * width, width)
+                image = jnp.dot(turned, right_ref[k], preferred_element_type=F32)
+                held = left_mixed_ref[k, pl.ds(at, 4)].reshape(4 * width, width).astype(F32)
+                cross = cross + fold(held * image, width)
+            return cross
+
+        cross = lax.fori_loop(0, half // 4, rights, cross)
     res_square = sums_ref[1:2, :] + sums[0]
-    res_vector = sums_ref[2:3, :] + sums[1]
-    vector_square = sums_ref[3:4, :] + sums[2]
+    product = sums_ref[2:3, :] + sums[1]
     total = norm_ref[0:1, :] + norm_other_ref[0:1, :]
     factor = scale / (total * scale + epsilon)
-    rayleigh = factor * (res_vector + shift * vector_square)
+    rayleigh = factor * product
     gap = rayleigh - shift
-    res_sq = factor * (res_square - 2.0 * gap * res_vector + gap * gap * vector_square)
-    change = gap * gap * (res_vector + shift * vector_square) - 2.0 * gap * (res_square + shift * res_vector)
+    res_vector = product - shift * total
+    res_sq = factor * (res_square - 2.0 * gap * res_vector + gap * gap * total)
+    change = gap * gap * product - 2.0 * gap * (res_square + shift * res_vector)
     share = 1.0 / members
     out_ref[0:1, :] = rayleigh * share
     out_ref[1:2, :] = jnp.maximum(res_sq, 0.0) * share

time: 46.4 us -> 53 us (1.14)
  Pallas kernels: 26.8 us -> 34.1 us
  starting transfers between devices: 12.2 us -> 10.8 us
  waiting for transfers between devices: 5.52 us -> 6.38 us
    pallas_call x1, Pallas kernels: 5.7 us -> 8.05 us  [shards(): pl.pallas_call(functools.partial(high_kernel, scale, members), out_shape=...]
    pallas_call x1, Pallas kernels: 2.54 us -> 4.22 us  [shards(): pl.pallas_call(functools.partial(last_kernel, len(last_pieces)), out_shap...]
    ppermute x1, starting transfers between devices: 1.68 us -> 0.23 us  [everyone(): lax.ppermute(block, 'term', [(i, i ^ bits) for i in range(members)])]
    ppermute x1, waiting for transfers between devices: 1.57 us -> 2.89 us  [everyone(): lax.ppermute(block, 'term', [(i, i ^ bits) for i in range(members)])]
    pallas_call x2, Pallas kernels: 2.21 us -> 3.17 us  [shards(): pl.pallas_call(functools.partial(rights_kernel, start, stop), out_shape=(...]
    pallas_call x1, Pallas kernels: 2.76 us -> 3.63 us  [shards(): pl.pallas_call(functools.partial(lefts_kernel, far_spots[-1], rows, chips...]
    pallas_call x1, Pallas kernels: 1.4 us -> 2.07 us  [shards(): pl.pallas_call(there_kernel, out_shape=jax.ShapeDtypeStruct(mid_turned, B...]
    pallas_call x1, Pallas kernels: 1.1 us -> 1.66 us  [shards(): pl.pallas_call(here_kernel, out_shape=(jax.ShapeDtypeStruct(here_turned,...]
  transfers between devices with their start and end apart: 18 -> 18, of which waited for: 6 -> 6; matrix products, arithmetic and copies ran while one was open for 0% -> 0% of each run, Pallas kernels for 40% -> 44%
where the time goes in v12:
time: 53 us; the launch traced here: 52.9 us
  Pallas kernels  34.1 us (64%)
  starting transfers between devices  10.8 us (20%)
  waiting for transfers between devices  6.38 us (12%)
  between operations  1.49 us (3%)
    pallas_call x1, Pallas kernels, shards(): pl.pallas_call(functools.partial(high_kernel, scale, members), out_shape=...  8.05 us
    ppermute x5, starting transfers between devices, to_next_chip(): lax.ppermute(block, 'term', [(i, (i + CORES) % members) for i in range(me...  6.81 us
    pallas_call x1, Pallas kernels, shards(): pl.pallas_call(functools.partial(last_kernel, len(last_pieces)), out_shap...  4.22 us
    pallas_call x1, Pallas kernels, shards(): pl.pallas_call(functools.partial(lefts_kernel, far_spots[-1], rows, chips...  3.63 us
    pallas_call x2, Pallas kernels, shards(): pl.pallas_call(functools.partial(rights_kernel, start, stop), out_shape=(...  3.17 us
    ppermute x1, waiting for transfers between devices, everyone(): lax.ppermute(block, 'term', [(i, i ^ bits) for i in range(members)])  2.89 us
    pallas_call x1, Pallas kernels, shards(): pl.pallas_call(low_kernel, out_shape=(half_bf, jax.ShapeDtypeStruct(half_...  2.72 us
    ppermute x11, starting transfers between devices, to_sibling(): return lax.ppermute(block, 'term', [(i, i ^ 1) for i in range(members)])  2.51 us
  transfers between devices with their start and end apart: 18, of which 6 were waited for; matrix products, arithmetic and copies ran while one was open for 0% of the time, Pallas kernels for 44%

profile of v12, /device:TPU:0, one launch (start us, length us, event | category | flops | bytes accessed | tf_op | source)
XLA Modules:
  0.0 52.9 jit_solution(3753178857723602865)
XLA Ops:
  1.3 1.4 %first_chunk.1 = (bf16[17,32,256]{2,1,0:T(8,128)(2,1)S(1)}, f32[8,256]{1,0:T(8,128)S(1)}, f32[8,256]{1,0:T(8,128)S(1)}, bf16[3,272,128]{2,1,0:T(8,128)(2,1)S(1)}) custom-call(s32[1,1]{1,0:T(1,128)} %bitcast.6.rank_in, f32[64,16,256]{2,1,0:T(8,128)} %bitcast.7, bf16[3,16,16]{2,1,0:T(8,128)(2,1)} %bitcast.12, bf16[3,256,256]{2,1,0:T(8,128)(2,1)} %bitcast.10), custom_call_target="tpu_custom_call" | custom-call | flops 5242 | bytes 7864 | tf_op jit(solution)/shard_map/first_chunk/pallas_call | solution.py:531
  2.7 0.5 collective-permute-start
  3.2 2.6 %collective-permute-start.2 = (bf16[17,32,256]{2,1,0:T(8,128)(2,1)S(1)}, bf16[17,32,256]{2,1,0:T(8,128)(2,1)S(1)}, u32[]{:S(2)}, u32[]{:S(2)}) collective-permute-start(bf16[17,32,256]{2,1,0:T(8,128)(2,1)S(1)} %get-tuple-element.53.chunk_ref.refs_0_), channel_id=1, source_target_pairs={{0,2},{1,3},{2,0},{3,1},{4,6},{5,7},{6,4},{7,5},{8,10},{9,11},{10,... | collective-permute-start | bytes 835592 | tf_op jit(solution)/shard_map/ppermute | solution.py:511
  5.8 1.3 %collective-permute-start.7 = (bf16[3,272,128]{2,1,0:T(8,128)(2,1)S(1)}, bf16[3,272,128]{2,1,0:T(8,128)(2,1)S(1)}, u32[]{:S(2)}, u32[]{:S(2)}) collective-permute-start(bf16[3,272,128]{2,1,0:T(8,128)(2,1)S(1)} %get-tuple-element.61), channel_id=1, source_target_pairs={{4,0},{8,4},{12,8},{16,12},{20,16},{24,20},{28,24},{5,1},{9,5},{13... | collective-permute-start | bytes 626696 | tf_op jit(solution)/shard_map/ppermute | solution.py:580
  7.1 0.0 collective-permute-done.refs_3_
  7.1 1.3 %prepare.1 = (f32[8,256]{1,0:T(8,128)S(1)}, bf16[3,272,128]{2,1,0:T(8,128)(2,1)S(1)}, bf16[3,256,256]{2,1,0:T(8,128)(2,1)S(1)}, bf16[16,16,256]{2,1,0:T(8,128)(2,1)S(1)}, bf16[16,16,256]{2,1,0:T(8,128)(2,1)S(1)}) custom-call(f32[8,256]{1,0:T(8,128)S(1)} %get-tuple-element.51.keep_ref, f32[8,256]{1,0:T(8,128)S(1)} %get-tuple-element.54.squares_ref, ...), custom_call_target="tpu_custom_call" | custom-call | flops 10485 | bytes 15728 | tf_op jit(solution)/shard_map/prepare/pallas_call | solution.py:549
  8.4 0.2 collective-permute-start.4
  8.6 0.3 collective-permute-start.3
  9.0 0.2 collective-permute-start.6
  9.2 0.4 spread_site.2.refs_6_.refs_5_.refs_3_.kron_ref
  9.6 0.3 collective-permute-done.4.refs_5_
  9.8 1.7 %collective-permute-start.1 = (bf16[16,16,256]{2,1,0:T(8,128)(2,1)S(1)}, bf16[16,16,256]{2,1,0:T(8,128)(2,1)S(1)}, u32[]{:S(2)}, u32[]{:S(2)}) collective-permute-start(bf16[16,16,256]{2,1,0:T(8,128)(2,1)S(1)} %get-tuple-element.55.refs_2_), channel_id=1, source_target_pairs={{0,2},{1,3},{2,0},{3,1},{4,6},{5,7},{6,4},{7,5},{8,10},{9,11},{10,... | collective-permute-start | bytes 393224 | tf_op jit(solution)/shard_map/ppermute | solution.py:511
  11.5 0.0 collective-permute-done.3.refs_4_
  11.5 0.4 collective-permute-start.10
  11.9 1.0 %rotate_own.1 = (bf16[3,16,128,256]{3,2,1,0:T(8,128)(2,1)S(1)}, bf16[256,768]{1,0:T(8,128)(2,1)S(1)}) custom-call(bf16[17,32,256]{2,1,0:T(8,128)(2,1)S(1)} %get-tuple-element.53.chunk_ref.refs_0_, bf16[16,16,256]{2,1,0:T(8,128)(2,1)S(1)} %get-tuple-element.56.refs_1_, bf16[16,16,256]{2,1,0:T(8,128)(2,1)S(1)} %get-tuple-element.55.refs_2_, ...), custom_call_target="tpu_custom_call" | custom-call | flops 16106127 | bytes 83886 | tf_op jit(solution)/shard_map/rotate_own/pallas_call | solution.py:612
  12.8 0.4 collective-permute-done.2.chunk_ref.refs_0_
  13.3 0.0 collective-permute-start.5
  13.3 0.4 spread_site.3.refs_6_.refs_4_.refs_2_
  13.7 1.4 %rotate_here.1 = (bf16[3,16,256,256]{3,2,1,0:T(8,128)(2,1)S(1)}, bf16[16,256,256]{2,1,0:T(8,128)(2,1)S(1)}) custom-call(bf16[17,32,256]{2,1,0:T(8,128)(2,1)S(1)} %get-tuple-element.53.chunk_ref.refs_0_, bf16[16,16,256]{2,1,0:T(8,128)(2,1)S(1)} %get-tuple-element.56.refs_1_, bf16[16,16,256]{2,1,0:T(8,128)(2,1)S(1)} %get-tuple-element.55.refs_2_, ...), custom_call_target="tpu_custom_call" | custom-call | flops 16106127 | bytes 83886 | tf_op jit(solution)/shard_map/rotate_here/pallas_call | solution.py:626
  15.0 0.0 collective-permute-done.7
  15.0 1.0 %collective-permute-done.6.refs_2_ = bf16[16,16,256]{2,1,0:T(8,128)(2,1)S(1)} collective-permute-done((bf16[16,16,256]{2,1,0:T(8,128)(2,1)S(1)}, bf16[16,16,256]{2,1,0:T(8,128)(2,1)S(1)}, u32[]{:S(2)}, u32[]{:S(2)}) %collective-permute-start.6) | collective-permute-done | bytes 131104 | tf_op jit(solution)/shard_map/ppermute | solution.py:511
  16.1 0.0 collective-permute-start.8
  16.1 2.0 %collective-permute-start.11 = (bf16[3,272,128]{2,1,0:T(8,128)(2,1)S(1)}, bf16[3,272,128]{2,1,0:T(8,128)(2,1)S(1)}, u32[]{:S(2)}, u32[]{:S(2)}) collective-permute-start(bf16[3,272,128]{2,1,0:T(8,128)(2,1)S(1)} %broadcast_select_fusion.packed_ref), channel_id=1, source_target_pairs={{0,2},{1,3},{2,0},{3,1},{4,6},{5,7},{6,4},{7,5},{8,10},{9,11},{10,... | collective-permute-start | bytes 626696 | tf_op jit(solution)/shard_map/ppermute | solution.py:511
  18.1 1.7 %apply_rows_here.1 = (bf16[16,384,256]{2,1,0:T(8,128)(2,1)S(1)}, bf16[3,256,256]{2,1,0:T(8,128)(2,1)S(1)}) custom-call(bf16[3,16,128,256]{3,2,1,0:T(8,128)(2,1)S(1)} %get-tuple-element.71.rotated_ref, bf16[3,272,128]{2,1,0:T(8,128)(2,1)S(1)} %broadcast_select_fusion.packed_ref), custom_call_target="tpu_custom_call" | custom-call | flops 16106127 | bytes 83886 | tf_op jit(solution)/shard_map/apply_rows_here/pallas_call | solution.py:647
  19.8 0.0 collective-permute-done.8.refs_3_
  19.8 0.0 collective-permute-done.5.refs_1_
  19.8 1.1 %rotate_crossed.1 = (bf16[3,16,256,256]{3,2,1,0:T(8,128)(2,1)S(1)}, bf16[16,256,256]{2,1,0:T(8,128)(2,1)S(1)}) custom-call(bf16[17,32,256]{2,1,0:T(8,128)(2,1)S(1)} %collective-permute-done.2.chunk_ref.refs_0_, bf16[17,32,256]{2,1,0:T(8,128)(2,1)S(1)} %collective-permute-done.5.refs_1_, ...), custom_call_target="tpu_custom_call", output_to_operand_aliasing={{0}: (5, {}), {1}: (6, {})} | custom-call | flops 16106127 | bytes 83886 | tf_op jit(solution)/shard_map/rotate_crossed/pallas_call | solution.py:626
  20.9 0.0 collective-permute-done.1.refs_0_
  20.9 0.3 collective-permute-start.9
  21.2 2.1 %apply_rows_crossed.1.refs_6_ = bf16[16,288,256]{2,1,0:T(8,128)(2,1)S(1)} custom-call(bf16[17,32,256]{2,1,0:T(8,128)(2,1)S(1)} %collective-permute-done.2.chunk_ref.refs_0_, bf16[17,32,256]{2,1,0:T(8,128)(2,1)S(1)} %collective-permute-done.5.refs_1_, bf16[16,16,256]{2,1,0:T(8,128)(2,1)S(1)} %collective-permute-done.6.refs_2_, ...), custom_call_target="tpu_custom_call" | custom-call | flops 16106127 | bytes 83886 | tf_op jit(solution)/shard_map/apply_rows_crossed/pallas_call | solution.py:668
  23.3 0.0 collective-permute-done.9.refs_1_
  23.3 4.2 %apply_rows_last.1.before_ref = f32[16,256,256]{2,1,0:T(8,128)S(1)} custom-call(bf16[16,16,256]{2,1,0:T(8,128)(2,1)S(1)} %collective-permute-done.1.refs_0_, bf16[16,16,256]{2,1,0:T(8,128)(2,1)S(1)} %collective-permute-done.9.refs_1_, bf16[3,256,256]{2,1,0:T(8,128)(2,1)S(1)} %get-tuple-element.78.refs_4_.refs_2_.right_ref, ...), custom_call_target="tpu_custom_call" | custom-call | flops 16106127 | bytes 83886 | tf_op jit(solution)/shard_map/apply_rows_last/pallas_call | solution.py:682
  27.5 0.0 collective-permute-done.10.refs_5_
  27.5 3.6 %received_lefts.1 = (bf16[16,256,768]{2,1,0:T(8,128)(2,1)S(1)}, f32[8,256]{1,0:T(8,128)S(1)}, bf16[3,16,256,256]{3,2,1,0:T(8,128)(2,1)S(1)}, bf16[16,256,256]{2,1,0:T(8,128)(2,1)S(1)}) custom-call(bf16[16,16,256]{2,1,0:T(8,128)(2,1)S(1)} %collective-permute-done.1.refs_0_, ...), custom_call_target="tpu_custom_call", output_to_operand_aliasing={{2}: (3, {}), {3}: (4, {})} | custom-call | flops 16106127 | bytes 125829 | tf_op jit(solution)/shard_map/received_lefts/pallas_call | solution.py:701
  31.1 0.4 collective-permute-start.12
  31.5 0.0 collective-permute-done.11.packed_ref
  31.5 1.7 %received_rights.2 = (bf16[8,256,256]{2,1,0:T(8,128)(2,1)S(1)}, bf16[3,256,256]{2,1,0:T(8,128)(2,1)S(1)}) custom-call(bf16[3,272,128]{2,1,0:T(8,128)(2,1)S(1)} %collective-permute-done.11.packed_ref, bf16[16,256,768]{2,1,0:T(8,128)(2,1)S(1)} %get-tuple-element.84.mixed_ref, f32[16,256,256]{2,1,0:T(8,128)S(1)} %apply_rows_last.1.before_ref), custom_call_target="tpu_custom_call" | custom-call | flops 8053063 | bytes 125829 | tf_op jit(solution)/shard_map/received_rights/pallas_call | solution.py:718
  33.2 0.3 collective-permute-start.13
  33.4 0.0 collective-permute-done.12.norm_other_ref
  33.5 1.5 %received_rights.3.high_ref.refs_2_ = bf16[8,256,256]{2,1,0:T(8,128)(2,1)S(1)} custom-call(bf16[3,256,256]{2,1,0:T(8,128)(2,1)S(1)} %get-tuple-element.91.packed_ref, bf16[16,256,768]{2,1,0:T(8,128)(2,1)S(1)} %get-tuple-element.84.mixed_ref, f32[16,256,256]{2,1,0:T(8,128)S(1)} %apply_rows_last.1.before_ref), custom_call_target="tpu_custom_call" | custom-call | flops 8053063 | bytes 125829 | tf_op jit(solution)/shard_map/received_rights/pallas_call | solution.py:718
  35.0 0.4 collective-permute-start.14
  35.3 0.6 %collective-permute-done.13.low_other_ref.refs_1_ = bf16[8,256,256]{2,1,0:T(8,128)(2,1)S(1)} collective-permute-done((bf16[8,256,256]{2,1,0:T(8,128)(2,1)S(1)}, bf16[8,256,256]{2,1,0:T(8,128)(2,1)S(1)}, u32[]{:S(2)}, u32[]{:S(2)}) %collective-permute-start.13) | collective-permute-done | bytes 1048608 | tf_op jit(solution)/shard_map/ppermute | solution.py:508
  35.9 2.7 %residual_low.1 = (bf16[8,256,256]{2,1,0:T(8,128)(2,1)S(1)}, bf16[3,8,256,256]{3,2,1,0:T(8,128)(2,1)S(1)}, f32[8,256]{1,0:T(8,128)S(1)}) custom-call(f32[8,256]{1,0:T(8,128)S(1)} %get-tuple-element.51.keep_ref, f32[8,256]{1,0:T(8,128)S(1)} %get-tuple-element.83.norm_ref, f32[8,256]{1,0:T(8,128)S(1)} %collective-permute-done.12.norm_other_ref, ...), custom_call_target="tpu_custom_call" | custom-call | flops 8053063 | bytes 31457 | tf_op jit(solution)/shard_map/residual_low/pallas_call | solution.py:737
  38.6 0.0 collective-permute-done.14.high_other_ref.refs_3_
  38.6 0.0 copy-start
  38.6 8.1 %residual_high.1.share_ref.refs_0_ = f32[8,256]{1,0:T(8,128)S(1)} custom-call(f32[8,256]{1,0:T(8,128)S(1)} %get-tuple-element.51.keep_ref, f32[8,256]{1,0:T(8,128)S(1)} %get-tuple-element.83.norm_ref, f32[8,256]{1,0:T(8,128)S(1)} %collective-permute-done.12.norm_other_ref, f32[8,256]{1,0:T(8,128)S(1)} %get-tuple-element.90.sums_ref, ...), custom_call_target="tpu_custom_call" | custom-call | flops 48318384 | bytes 62914 | tf_op jit(solution)/shard_map/residual_high/pallas_call | solution.py:746
  46.7 0.2 collective-permute-start.15
  46.9 0.1 collective-permute-start.16
  47.1 0.0 copy-done
  47.1 0.5 own_rows.1
  47.5 2.9 %collective-permute-done.15.refs_2_ = f32[8,256]{1,0:T(8,128)S(1)} collective-permute-done((f32[8,256]{1,0:T(8,128)S(1)}, f32[8,256]{1,0:T(8,128)S(1)}, u32[]{:S(2)}, u32[]{:S(2)}) %collective-permute-start.15) | collective-permute-done | bytes 8224 | tf_op jit(solution)/shard_map/ppermute | solution.py:521
  50.4 0.0 collective-permute-start.17
  50.4 0.0 collective-permute-done.16.refs_1_
  50.4 1.2 %collective-permute-done.17.refs_3_ = f32[8,256]{1,0:T(8,128)S(1)} collective-permute-done((f32[8,256]{1,0:T(8,128)S(1)}, f32[8,256]{1,0:T(8,128)S(1)}, u32[]{:S(2)}, u32[]{:S(2)}) %collective-permute-start.17) | collective-permute-done | bytes 8224 | tf_op jit(solution)/shard_map/ppermute | solution.py:508
  51.6 1.3 %finish.1 = (f32[64,16,256]{2,1,0:T(8,128)}, f32[1]{0:T(128)}) custom-call(f32[64,16,256]{2,1,0:T(8,128)S(1)} %get-tuple-element.94.vector_ref, f32[64,16,256]{2,1,0:T(8,128)S(1)} %get-tuple-element.96.residual_ref, f32[8,256]{1,0:T(8,128)S(1)} %residual_high.1.share_ref.refs_0_, f32[8,256]{1,0:T(8,128)S(1)} %collective-permute-done.16.refs_1_, ...), custom_call_target="tpu_custom_call" | custom-call | flops 7864 | bytes 31457 | tf_op jit(solution)/shard_map/finish/pallas_call | solution.py:776
  (1 shorter events, 0.0 us)
Async XLA Ops:
  2.7 4.4 %collective-permute-start = (bf16[17,32,256]{2,1,0:T(8,128)(2,1)S(1)}, bf16[17,32,256]{2,1,0:T(8,128)(2,1)S(1)}, u32[]{:S(2)}, u32[]{:S(2)}) collective-permute-start(bf16[17,32,256]{2,1,0:T(8,128)(2,1)S(1)} %get-tuple-element.53.chunk_ref.refs_0_), channel_id=1, source_target_pairs={{0,1},{1,0},{2,3},{3,2},{4,5},{5,4},{6,7},{7,6},{8,9},{9,8},{10,11... | collective-permute-start | bytes 835592 | tf_op jit(solution)/shard_map/ppermute | solution.py:508
  3.2 10.1 %collective-permute-start.2 = (bf16[17,32,256]{2,1,0:T(8,128)(2,1)S(1)}, bf16[17,32,256]{2,1,0:T(8,128)(2,1)S(1)}, u32[]{:S(2)}, u32[]{:S(2)}) collective-permute-start(bf16[17,32,256]{2,1,0:T(8,128)(2,1)S(1)} %get-tuple-element.53.chunk_ref.refs_0_), channel_id=1, source_target_pairs={{0,2},{1,3},{2,0},{3,1},{4,6},{5,7},{6,4},{7,5},{8,10},{9,11},{10,... | collective-permute-start | bytes 835592 | tf_op jit(solution)/shard_map/ppermute | solution.py:511
  5.8 9.3 %collective-permute-start.7 = (bf16[3,272,128]{2,1,0:T(8,128)(2,1)S(1)}, bf16[3,272,128]{2,1,0:T(8,128)(2,1)S(1)}, u32[]{:S(2)}, u32[]{:S(2)}) collective-permute-start(bf16[3,272,128]{2,1,0:T(8,128)(2,1)S(1)} %get-tuple-element.61), channel_id=1, source_target_pairs={{4,0},{8,4},{12,8},{16,12},{20,16},{24,20},{28,24},{5,1},{9,5},{13... | collective-permute-start | bytes 626696 | tf_op jit(solution)/shard_map/ppermute | solution.py:580
  8.4 1.4 %collective-permute-start.4 = (bf16[16,16,256]{2,1,0:T(8,128)(2,1)S(1)}, bf16[16,16,256]{2,1,0:T(8,128)(2,1)S(1)}, u32[]{:S(2)}, u32[]{:S(2)}) collective-permute-start(bf16[16,16,256]{2,1,0:T(8,128)(2,1)S(1)} %get-tuple-element.55.refs_2_), channel_id=1, source_target_pairs={{0,1},{1,0},{2,3},{3,2},{4,5},{5,4},{6,7},{7,6},{8,9},{9,8},{10,11... | collective-permute-start | bytes 393224 | tf_op jit(solution)/shard_map/ppermute | solution.py:508
  8.6 2.8 %collective-permute-start.3 = (bf16[16,16,256]{2,1,0:T(8,128)(2,1)S(1)}, bf16[16,16,256]{2,1,0:T(8,128)(2,1)S(1)}, u32[]{:S(2)}, u32[]{:S(2)}) collective-permute-start(bf16[16,16,256]{2,1,0:T(8,128)(2,1)S(1)} %get-tuple-element.56.refs_1_), channel_id=1, source_target_pairs={{0,1},{1,0},{2,3},{3,2},{4,5},{5,4},{6,7},{7,6},{8,9},{9,8},{10,11... | collective-permute-start | bytes 393224 | tf_op jit(solution)/shard_map/ppermute | solution.py:508
  9.0 7.1 %collective-permute-start.6 = (bf16[16,16,256]{2,1,0:T(8,128)(2,1)S(1)}, bf16[16,16,256]{2,1,0:T(8,128)(2,1)S(1)}, u32[]{:S(2)}, u32[]{:S(2)}) collective-permute-start(bf16[16,16,256]{2,1,0:T(8,128)(2,1)S(1)} %get-tuple-element.56.refs_1_), channel_id=1, source_target_pairs={{0,2},{1,3},{2,0},{3,1},{4,6},{5,7},{6,4},{7,5},{8,10},{9,11},{10,... | collective-permute-start | bytes 393224 | tf_op jit(solution)/shard_map/ppermute | solution.py:511
  9.8 11.1 %collective-permute-start.1 = (bf16[16,16,256]{2,1,0:T(8,128)(2,1)S(1)}, bf16[16,16,256]{2,1,0:T(8,128)(2,1)S(1)}, u32[]{:S(2)}, u32[]{:S(2)}) collective-permute-start(bf16[16,16,256]{2,1,0:T(8,128)(2,1)S(1)} %get-tuple-element.55.refs_2_), channel_id=1, source_target_pairs={{0,2},{1,3},{2,0},{3,1},{4,6},{5,7},{6,4},{7,5},{8,10},{9,11},{10,... | collective-permute-start | bytes 393224 | tf_op jit(solution)/shard_map/ppermute | solution.py:511
  11.5 16.0 %collective-permute-start.10 = (bf16[3,272,128]{2,1,0:T(8,128)(2,1)S(1)}, bf16[3,272,128]{2,1,0:T(8,128)(2,1)S(1)}, u32[]{:S(2)}, u32[]{:S(2)}) collective-permute-start(bf16[3,272,128]{2,1,0:T(8,128)(2,1)S(1)} %get-tuple-element.77), channel_id=1, source_target_pairs={{0,2},{1,3},{2,0},{3,1},{4,6},{5,7},{6,4},{7,5},{8,10},{9,11},{10,... | collective-permute-start | bytes 626696 | tf_op jit(solution)/shard_map/ppermute | solution.py:511
  13.3 6.5 %collective-permute-start.5 = (bf16[17,32,256]{2,1,0:T(8,128)(2,1)S(1)}, bf16[17,32,256]{2,1,0:T(8,128)(2,1)S(1)}, u32[]{:S(2)}, u32[]{:S(2)}) collective-permute-start(bf16[17,32,256]{2,1,0:T(8,128)(2,1)S(1)} %collective-permute-done.2.chunk_ref.refs_0_), channel_id=1, source_target_pairs={{0,1},{1,0},{2,3},{3,2},{4,5},{5,4},{6,7},{7,6},{8,9},{9,8},{10,11... | collective-permute-start | bytes 835592 | tf_op jit(solution)/shard_map/ppermute | solution.py:508
  16.1 3.7 %collective-permute-start.8 = (bf16[16,16,256]{2,1,0:T(8,128)(2,1)S(1)}, bf16[16,16,256]{2,1,0:T(8,128)(2,1)S(1)}, u32[]{:S(2)}, u32[]{:S(2)}) collective-permute-start(bf16[16,16,256]{2,1,0:T(8,128)(2,1)S(1)} %collective-permute-done.6.refs_2_), channel_id=1, source_target_pairs={{0,1},{1,0},{2,3},{3,2},{4,5},{5,4},{6,7},{7,6},{8,9},{9,8},{10,11... | collective-permute-start | bytes 393224 | tf_op jit(solution)/shard_map/ppermute | solution.py:508
  16.1 15.4 %collective-permute-start.11 = (bf16[3,272,128]{2,1,0:T(8,128)(2,1)S(1)}, bf16[3,272,128]{2,1,0:T(8,128)(2,1)S(1)}, u32[]{:S(2)}, u32[]{:S(2)}) collective-permute-start(bf16[3,272,128]{2,1,0:T(8,128)(2,1)S(1)} %broadcast_select_fusion.packed_ref), channel_id=1, source_target_pairs={{0,2},{1,3},{2,0},{3,1},{4,6},{5,7},{6,4},{7,5},{8,10},{9,11},{10,... | collective-permute-start | bytes 626696 | tf_op jit(solution)/shard_map/ppermute | solution.py:511
  20.9 2.4 %collective-permute-start.9 = (bf16[16,16,256]{2,1,0:T(8,128)(2,1)S(1)}, bf16[16,16,256]{2,1,0:T(8,128)(2,1)S(1)}, u32[]{:S(2)}, u32[]{:S(2)}) collective-permute-start(bf16[16,16,256]{2,1,0:T(8,128)(2,1)S(1)} %collective-permute-done.1.refs_0_), channel_id=1, source_target_pairs={{0,1},{1,0},{2,3},{3,2},{4,5},{5,4},{6,7},{7,6},{8,9},{9,8},{10,11... | collective-permute-start | bytes 393224 | tf_op jit(solution)/shard_map/ppermute | solution.py:508
  31.1 2.3 %collective-permute-start.12 = (f32[8,256]{1,0:T(8,128)S(1)}, f32[8,256]{1,0:T(8,128)S(1)}, u32[]{:S(2)}, u32[]{:S(2)}) collective-permute-start(f32[8,256]{1,0:T(8,128)S(1)} %get-tuple-element.83.norm_ref), channel_id=1, source_target_pairs={{0,1},{1,0},{2,3},{3,2},{4,5},{5,4},{6,7},{7,6},{8,9},{9,8},{10,11... | collective-permute-start | bytes 24584 | tf_op jit(solution)/shard_map/ppermute | solution.py:508
  33.2 2.7 %collective-permute-start.13 = (bf16[8,256,256]{2,1,0:T(8,128)(2,1)S(1)}, bf16[8,256,256]{2,1,0:T(8,128)(2,1)S(1)}, u32[]{:S(2)}, u32[]{:S(2)}) collective-permute-start(bf16[8,256,256]{2,1,0:T(8,128)(2,1)S(1)} %get-tuple-element.88.low_ref.refs_0_), channel_id=1, source_target_pairs={{0,1},{1,0},{2,3},{3,2},{4,5},{5,4},{6,7},{7,6},{8,9},{9,8},{10,11... | collective-permute-start | bytes 3145736 | tf_op jit(solution)/shard_map/ppermute | solution.py:508
  35.0 3.7 %collective-permute-start.14 = (bf16[8,256,256]{2,1,0:T(8,128)(2,1)S(1)}, bf16[8,256,256]{2,1,0:T(8,128)(2,1)S(1)}, u32[]{:S(2)}, u32[]{:S(2)}) collective-permute-start(bf16[8,256,256]{2,1,0:T(8,128)(2,1)S(1)} %received_rights.3.high_ref.refs_2_), channel_id=1, source_target_pairs={{0,1},{1,0},{2,3},{3,2},{4,5},{5,4},{6,7},{7,6},{8,9},{9,8},{10,11... | collective-permute-start | bytes 3145736 | tf_op jit(solution)/shard_map/ppermute | solution.py:508
  38.6 8.4 %copy-start = (f32[1,64,16,256]{3,2,1,0:T(8,128)S(1)}, f32[1,64,16,256]{3,2,1,0:T(8,128)}, u32[]{:S(2)}) copy-start(f32[1,64,16,256]{3,2,1,0:T(8,128)} %param.5) | copy-start | bytes 3145732
  46.7 3.7 %collective-permute-start.15 = (f32[8,256]{1,0:T(8,128)S(1)}, f32[8,256]{1,0:T(8,128)S(1)}, u32[]{:S(2)}, u32[]{:S(2)}) collective-permute-start(f32[8,256]{1,0:T(8,128)S(1)} %residual_high.1.share_ref.refs_0_), channel_id=1, source_target_pairs={{0,2},{1,3},{2,0},{3,1},{4,6},{5,7},{6,4},{7,5},{8,10},{9,11},{10,... | collective-permute-start | bytes 24584 | tf_op jit(solution)/shard_map/ppermute | solution.py:521
  46.9 3.5 %collective-permute-start.16 = (f32[8,256]{1,0:T(8,128)S(1)}, f32[8,256]{1,0:T(8,128)S(1)}, u32[]{:S(2)}, u32[]{:S(2)}) collective-permute-start(f32[8,256]{1,0:T(8,128)S(1)} %residual_high.1.share_ref.refs_0_), channel_id=1, source_target_pairs={{0,1},{1,0},{2,3},{3,2},{4,5},{5,4},{6,7},{7,6},{8,9},{9,8},{10,11... | collective-permute-start | bytes 24584 | tf_op jit(solution)/shard_map/ppermute | solution.py:508
  50.4 1.2 %collective-permute-start.17 = (f32[8,256]{1,0:T(8,128)S(1)}, f32[8,256]{1,0:T(8,128)S(1)}, u32[]{:S(2)}, u32[]{:S(2)}) collective-permute-start(f32[8,256]{1,0:T(8,128)S(1)} %collective-permute-done.15.refs_2_), channel_id=1, source_target_pairs={{0,1},{1,0},{2,3},{3,2},{4,5},{5,4},{6,7},{7,6},{8,9},{9,8},{10,11... | collective-permute-start | bytes 24584 | tf_op jit(solution)/shard_map/ppermute | solution.py:508

commit v13 on v11

--- a/solution.py
+++ b/solution.py
@@ -10,7 +10,7 @@
 epsilon = 1e-06
 CORES = 2
 TILE = 16
-UNROLL = 8
+UNROLL = 16
 GROUP = 8
 VMEM_LIMIT = 20 * 1024 * 1024
 F32 = jnp.float32
@@ -150,21 +150,24 @@
     return jnp.sum(jnp.where(row == col, lower, 0.0), axis=0, keepdims=True)
 
 
-def unpack_symmetric(packed_ref, full_ref):
+def unpack_symmetric(packed_ref, full_ref, keep=None):
     terms, width, _ = full_ref.shape
     half = width // 2
     row, col = triangle(half)
+
+    def kept(block, start):
+        return block if keep is None else block * keep[:, start : start + half]
+
     for k in range(terms):
-        corner = packed_ref[k, 0:half, :]
+        corner = packed_ref[k, 0:half, :].astype(F32)
         mixed = packed_ref[k, half:width, :].astype(F32)
         diagonal = packed_ref[k, width : width + TILE, :].astype(F32)[0:1]
         turned = mixed.T
-        full_ref[k, 0:half, 0:half] = jnp.where(row <= col, mixed, turned).astype(BF16)
-        full_ref[k, 0:half, half:width] = corner
-        full_ref[k, half:width, 0:half] = corner.astype(F32).T.astype(BF16)
-        full_ref[k, half:width, half:width] = jnp.where(
-            row > col, mixed, jnp.where(row == col, diagonal, turned)
-        ).astype(BF16)
+        lower = jnp.where(row > col, mixed, jnp.where(row == col, diagonal, turned))
+        full_ref[k, 0:half, 0:half] = kept(jnp.where(row <= col, mixed, turned), 0).astype(BF16)
+        full_ref[k, 0:half, half:width] = kept(corner, half).astype(BF16)
+        full_ref[k, half:width, 0:half] = kept(corner.T, 0).astype(BF16)
+        full_ref[k, half:width, half:width] = kept(lower, half).astype(BF16)
 
 
 def spread_kernel(chunk_ref, kron_ref):
@@ -246,8 +249,8 @@
             turned_ref[n : n + 8, k * count : (k + 1) * count, :] = turned.reshape(8, count, width)
 
 
-def here_kernel(rotated_ref, packed_ref, turned_ref, right_ref):
-    unpack_symmetric(packed_ref, right_ref)
+def here_kernel(rotated_ref, packed_ref, keep_ref, turned_ref, right_ref):
+    unpack_symmetric(packed_ref, right_ref, keep_ref[0:1, :])
     turn(right_ref, rotated_ref, turned_ref)
 
 
@@ -308,10 +311,10 @@
     lax.fori_loop(0, states, lefts, 0, unroll=UNROLL)
 
 
-def rights_kernel(start, stop, packed_ref, mixed_ref, before_ref, partial_ref, *refs):
+def rights_kernel(start, stop, packed_ref, mixed_ref, before_ref, keep_ref, partial_ref, *refs):
     if start == 0:
         right_ref = refs[0]
-        unpack_symmetric(packed_ref, right_ref)
+        unpack_symmetric(packed_ref, right_ref, keep_ref[0:1, :])
     else:
         right_ref = packed_ref
     terms, width, _ = right_ref.shape
@@ -327,14 +330,14 @@
     lax.fori_loop(0, (stop - start) // GROUP, rights, 0)
 
 
-def shifted_residual(start, shift, keep, mine_ref, other_ref, whole_ref, left_ref, res_ref, mixed_ref):
+def shifted_residual(start, shift, mine_ref, other_ref, whole_ref, left_ref, res_ref, mixed_ref):
     count, width, _ = res_ref.shape
     terms = left_ref.shape[0]
     zero = jnp.zeros((8, width), F32)
 
     def lefts(n, sums):
         held = whole_ref[start + n].astype(F32)
-        sigma = (mine_ref[n].astype(F32) + other_ref[n].astype(F32)) * keep
+        sigma = mine_ref[n].astype(F32) + other_ref[n].astype(F32)
         residual = sigma - shift * held
         rounded = residual.astype(BF16)
         res_ref[n] = rounded
@@ -343,18 +346,13 @@
         ).astype(BF16)
         for k in range(terms):
             mixed_ref[k, n] = mixed[k * width : (k + 1) * width]
-        return (
-            sums[0] + fold(residual * residual, width),
-            sums[1] + fold(residual * held, width),
-            sums[2] + fold(held * held, width),
-        )
-
-    sums = lax.fori_loop(0, count, lefts, (zero, zero, zero), unroll=UNROLL)
-    return [jnp.sum(total) for total in sums]
+        return sums[0] + fold(residual * residual, width), sums[1] + fold(sigma * held, width)
+
+    square, product = lax.fori_loop(0, count, lefts, (zero, zero), unroll=UNROLL)
+    return jnp.sum(square), jnp.sum(product)
 
 
 def low_kernel(
-    keep_ref,
     norm_ref,
     norm_other_ref,
     low_ref,
@@ -366,29 +364,26 @@
     out_ref,
 ):
     count, width, _ = low_ref.shape
-    keep = keep_ref[0:1, :]
-    zero = jnp.zeros((8, width), F32)
-
-    def products(n, sums):
-        held = whole_ref[n].astype(F32)
-        sigma = low_ref[n].astype(F32) + low_other_ref[n].astype(F32)
-        return sums[0] + fold(sigma * held, width), sums[1] + fold(held * held, width)
-
-    cross, square = lax.fori_loop(0, count, products, (zero, zero), unroll=UNROLL)
+    states = whole_ref.shape[0]
+    held = whole_ref[0].astype(F32)
+    sigma = low_ref[0].astype(F32) + low_other_ref[0].astype(F32)
+    product = jnp.sum(fold(sigma * held, width))
+    square = jnp.sum(fold(held * held, width))
     total = norm_ref[0:1, :] + norm_other_ref[0:1, :]
-    floor = jnp.maximum(jnp.maximum(jnp.full((1, width), jnp.sum(square), F32), 0.25 * total), 1e-30)
-    shift = jnp.sum(cross) / floor
-    sums = shifted_residual(0, shift, keep, low_ref, low_other_ref, whole_ref, left_ref, res_ref, mixed_ref)
+    floor = jnp.maximum(jnp.maximum(square, (0.25 / states) * total), 1e-30)
+    shift = product / floor
+    square, product = shifted_residual(
+        0, shift, low_ref, low_other_ref, whole_ref, left_ref, res_ref, mixed_ref
+    )
     out_ref[0:1, :] = shift
-    for n, value in enumerate(sums):
-        out_ref[n + 1 : n + 2, :] = jnp.full((1, width), value, F32)
-    out_ref[4:8, :] = jnp.zeros((4, width), F32)
+    out_ref[1:2, :] = jnp.full((1, width), square, F32)
+    out_ref[2:3, :] = jnp.full((1, width), product, F32)
+    out_ref[3:8, :] = jnp.zeros((5, width), F32)
 
 
 def high_kernel(
     scale,
     members,
-    keep_ref,
     norm_ref,
     norm_other_ref,
     sums_ref,
@@ -408,9 +403,8 @@
     terms, states, width, _ = rotated_ref.shape
     half = states // 2
     shift = sums_ref[0:1, :]
-    keep = keep_ref[0:1, :]
-    sums = shifted_residual(
-        half, shift, keep, high_ref, high_other_ref, whole_ref, left_ref, res_ref, mixed_ref
+    square, product = shifted_residual(
+        half, shift, high_ref, high_other_ref, whole_ref, left_ref, res_ref, mixed_ref
     )
 
     def sites(i, carry):
@@ -428,15 +422,15 @@
             image = jnp.dot(turned, right_ref[k], preferred_element_type=F32)
             held = left_mixed_ref[k].reshape(half * width, width).astype(F32)
             cross = cross + fold(held * image, width)
-    res_square = sums_ref[1:2, :] + sums[0]
-    res_vector = sums_ref[2:3, :] + sums[1]
-    vector_square = sums_ref[3:4, :] + sums[2]
+    res_square = sums_ref[1:2, :] + square
+    product = sums_ref[2:3, :] + product
     total = norm_ref[0:1, :] + norm_other_ref[0:1, :]
     factor = scale / (total * scale + epsilon)
-    rayleigh = factor * (res_vector + shift * vector_square)
+    rayleigh = factor * product
     gap = rayleigh - shift
-    res_sq = factor * (res_square - 2.0 * gap * res_vector + gap * gap * vector_square)
-    change = gap * gap * (res_vector + shift * vector_square) - 2.0 * gap * (res_square + shift * res_vector)
+    res_vector = product - shift * total
+    res_sq = factor * (res_square - 2.0 * gap * res_vector + gap * gap * total)
+    change = gap * gap * product - 2.0 * gap * (res_square + shift * res_vector)
     share = 1.0 / members
     out_ref[0:1, :] = rayleigh * share
     out_ref[1:2, :] = jnp.maximum(res_sq, 0.0) * share
@@ -638,12 +632,12 @@
     turned_own, right = pl.pallas_call(
         here_kernel,
         out_shape=(jax.ShapeDtypeStruct(here_turned, BF16), jax.ShapeDtypeStruct(left.shape, BF16)),
-        in_specs=[vmem] * 2,
+        in_specs=[vmem] * 3,
         out_specs=(vmem, vmem),
         compiler_params=params(),
         cost_estimate=part_cost,
         name="apply_rows_here",
-    )(rotated_own, packed)
+    )(rotated_own, packed, keep)
     parts = [turned_own]
     mid_pieces = []
     if mid_spots:
@@ -709,12 +703,12 @@
             part, *unpacked = pl.pallas_call(
                 functools.partial(rights_kernel, start, stop),
                 out_shape=(part_shape,) + ((jax.ShapeDtypeStruct(left.shape, BF16),) if start == 0 else ()),
-                in_specs=[vmem] * 3,
+                in_specs=[vmem] * 4,
                 out_specs=(vmem,) * (2 if start == 0 else 1),
                 compiler_params=params(),
                 cost_estimate=cost(stage_flops / 2, 12 * states * width * width),
                 name="received_rights",
-            )(right_far, mixed, partial)
+            )(right_far, mixed, partial, keep)
             if unpacked:
                 right_far, norm_other = lax.optimization_barrier((unpacked[0], to_sibling(norm)))
             parts.append(part)
@@ -728,16 +722,16 @@
     res_low, mixed_low, sums = pl.pallas_call(
         low_kernel,
         out_shape=(half_bf, jax.ShapeDtypeStruct(half_mixed, BF16), tile),
-        in_specs=[vmem] * 7,
+        in_specs=[vmem] * 6,
         out_specs=(vmem,) * 3,
         compiler_params=params(),
         cost_estimate=cost(stage_flops / 2, 3 * states * width * width),
         name="residual_low",
-    )(keep, norm, norm_other, *halves[:2], vector, left)
+    )(norm, norm_other, *halves[:2], vector, left)
     share = pl.pallas_call(
         functools.partial(high_kernel, scale, members),
         out_shape=tile,
-        in_specs=[vmem] * 12,
+        in_specs=[vmem] * 11,
         out_specs=vmem,
         scratch_shapes=[
             pltpu.VMEM(half_bf.shape, BF16),
@@ -747,7 +741,7 @@
         compiler_params=params(),
         cost_estimate=cost(3 * stage_flops, 6 * states * width * width),
         name="residual_high",
-    )(keep, norm, norm_other, sums, *halves[2:], vector, left, right, kron_own, res_low, mixed_low)
+    )(norm, norm_other, sums, *halves[2:], vector, left, right, kron_own, res_low, mixed_low)
     crossed = everyone(share)
 
     local = jax.ShapeDtypeStruct((rows, states, width), F32)

time: 46.4 us -> 47.4 us (1.022)
  Pallas kernels: 26.8 us -> 27.5 us
    pallas_call x1, Pallas kernels: 5.7 us -> 6.41 us  [shards(): pl.pallas_call(functools.partial(high_kernel, scale, members), out_shape=...]
  transfers between devices with their start and end apart: 18 -> 18, of which waited for: 6 -> 7; matrix products, arithmetic and copies ran while one was open for 0% -> 0% of each run, Pallas kernels for 40% -> 39%
where the time goes in v13:
time: 47.4 us; the launch traced here: 47.2 us
  Pallas kernels  27.5 us (58%)
  starting transfers between devices  12.3 us (26%)
  waiting for transfers between devices  5.75 us (12%)
  between operations  1.68 us (4%)
    ppermute x5, starting transfers between devices, to_next_chip(): lax.ppermute(block, 'term', [(i, (i + CORES) % members) for i in range(me...  6.81 us
    pallas_call x1, Pallas kernels, shards(): pl.pallas_call(functools.partial(high_kernel, scale, members), out_shape=...  6.41 us
    pallas_call x1, Pallas kernels, shards(): pl.pallas_call(low_kernel, out_shape=(half_bf, jax.ShapeDtypeStruct(half_...  2.92 us
    pallas_call x2, Pallas kernels, rotate(): pl.pallas_call(functools.partial(rotate_kernel, spots, rows, chips), out_...  2.59 us
    ppermute x11, waiting for transfers between devices, to_sibling(): return lax.ppermute(block, 'term', [(i, i ^ 1) for i in range(members)])  2.48 us
    pallas_call x1, Pallas kernels, shards(): pl.pallas_call(functools.partial(lefts_kernel, far_spots[-1], rows, chips...  2.42 us
    ppermute x11, starting transfers between devices, to_sibling(): return lax.ppermute(block, 'term', [(i, i ^ 1) for i in range(members)])  2.36 us
    pallas_call x2, Pallas kernels, shards(): pl.pallas_call(functools.partial(rights_kernel, start, stop), out_shape=(...  2.25 us
  transfers between devices with their start and end apart: 18, of which 7 were waited for; matrix products, arithmetic and copies ran while one was open for 0% of the time, Pallas kernels for 39%

profile of v13, /device:TPU:0, one launch (start us, length us, event | category | flops | bytes accessed | tf_op | source)
XLA Modules:
  0.0 47.2 jit_solution(6005004044020741903)
XLA Ops:
  1.3 1.4 %first_chunk.1 = (bf16[17,32,256]{2,1,0:T(8,128)(2,1)S(1)}, f32[8,256]{1,0:T(8,128)S(1)}, f32[8,256]{1,0:T(8,128)S(1)}, bf16[3,272,128]{2,1,0:T(8,128)(2,1)S(1)}) custom-call(s32[1,1]{1,0:T(1,128)} %bitcast.6.rank_in, f32[64,16,256]{2,1,0:T(8,128)} %bitcast.7, bf16[3,16,16]{2,1,0:T(8,128)(2,1)} %bitcast.12, bf16[3,256,256]{2,1,0:T(8,128)(2,1)} %bitcast.10), custom_call_target="tpu_custom_call" | custom-call | flops 5242 | bytes 7864 | tf_op jit(solution)/shard_map/first_chunk/pallas_call | solution.py:516
  2.7 0.5 %collective-permute-start = (bf16[17,32,256]{2,1,0:T(8,128)(2,1)S(1)}, bf16[17,32,256]{2,1,0:T(8,128)(2,1)S(1)}, u32[]{:S(2)}, u32[]{:S(2)}) collective-permute-start(bf16[17,32,256]{2,1,0:T(8,128)(2,1)S(1)} %get-tuple-element.53.chunk_ref.refs_0_), channel_id=1, source_target_pairs={{0,1},{1,0},{2,3},{3,2},{4,5},{5,4},{6,7},{7,6},{8,9},{9,8},{10,11... | collective-permute-start | bytes 835592 | tf_op jit(solution)/shard_map/ppermute | solution.py:493
  3.2 2.6 %collective-permute-start.2 = (bf16[17,32,256]{2,1,0:T(8,128)(2,1)S(1)}, bf16[17,32,256]{2,1,0:T(8,128)(2,1)S(1)}, u32[]{:S(2)}, u32[]{:S(2)}) collective-permute-start(bf16[17,32,256]{2,1,0:T(8,128)(2,1)S(1)} %get-tuple-element.53.chunk_ref.refs_0_), channel_id=1, source_target_pairs={{0,2},{1,3},{2,0},{3,1},{4,6},{5,7},{6,4},{7,5},{8,10},{9,11},{10,... | collective-permute-start | bytes 835592 | tf_op jit(solution)/shard_map/ppermute | solution.py:496
  5.8 1.3 %collective-permute-start.7 = (bf16[3,272,128]{2,1,0:T(8,128)(2,1)S(1)}, bf16[3,272,128]{2,1,0:T(8,128)(2,1)S(1)}, u32[]{:S(2)}, u32[]{:S(2)}) collective-permute-start(bf16[3,272,128]{2,1,0:T(8,128)(2,1)S(1)} %get-tuple-element.61), channel_id=1, source_target_pairs={{4,0},{8,4},{12,8},{16,12},{20,16},{24,20},{28,24},{5,1},{9,5},{13... | collective-permute-start | bytes 626696 | tf_op jit(solution)/shard_map/ppermute | solution.py:565
  7.1 0.0 collective-permute-done.refs_3_
  7.1 1.3 %prepare.1 = (f32[8,256]{1,0:T(8,128)S(1)}, bf16[3,272,128]{2,1,0:T(8,128)(2,1)S(1)}, bf16[3,256,256]{2,1,0:T(8,128)(2,1)S(1)}, bf16[16,16,256]{2,1,0:T(8,128)(2,1)S(1)}, bf16[16,16,256]{2,1,0:T(8,128)(2,1)S(1)}) custom-call(f32[8,256]{1,0:T(8,128)S(1)} %get-tuple-element.51.keep_ref, f32[8,256]{1,0:T(8,128)S(1)} %get-tuple-element.54.squares_ref, ...), custom_call_target="tpu_custom_call" | custom-call | flops 10485 | bytes 15728 | tf_op jit(solution)/shard_map/prepare/pallas_call | solution.py:534
  8.4 0.2 collective-permute-start.4
  8.6 0.3 collective-permute-start.3
  9.0 0.2 collective-permute-start.6
  9.2 0.4 spread_site.2.refs_6_.refs_5_.refs_3_.kron_ref
  9.6 0.3 collective-permute-done.4.refs_5_
  9.8 1.7 %collective-permute-start.1 = (bf16[16,16,256]{2,1,0:T(8,128)(2,1)S(1)}, bf16[16,16,256]{2,1,0:T(8,128)(2,1)S(1)}, u32[]{:S(2)}, u32[]{:S(2)}) collective-permute-start(bf16[16,16,256]{2,1,0:T(8,128)(2,1)S(1)} %get-tuple-element.55.refs_2_), channel_id=1, source_target_pairs={{0,2},{1,3},{2,0},{3,1},{4,6},{5,7},{6,4},{7,5},{8,10},{9,11},{10,... | collective-permute-start | bytes 393224 | tf_op jit(solution)/shard_map/ppermute | solution.py:496
  11.5 0.0 collective-permute-done.3.refs_4_
  11.5 0.4 collective-permute-start.10
  11.9 1.0 %rotate_own.1 = (bf16[3,16,128,256]{3,2,1,0:T(8,128)(2,1)S(1)}, bf16[256,768]{1,0:T(8,128)(2,1)S(1)}) custom-call(bf16[17,32,256]{2,1,0:T(8,128)(2,1)S(1)} %get-tuple-element.53.chunk_ref.refs_0_, bf16[16,16,256]{2,1,0:T(8,128)(2,1)S(1)} %get-tuple-element.56.refs_1_, bf16[16,16,256]{2,1,0:T(8,128)(2,1)S(1)} %get-tuple-element.55.refs_2_, ...), custom_call_target="tpu_custom_call" | custom-call | flops 16106127 | bytes 83886 | tf_op jit(solution)/shard_map/rotate_own/pallas_call | solution.py:597
  12.8 0.4 collective-permute-done.2.chunk_ref.refs_0_
  13.3 0.0 collective-permute-start.5
  13.3 0.4 spread_site.3.refs_6_.refs_4_.refs_2_
  13.7 1.5 %rotate_here.1 = (bf16[3,16,256,256]{3,2,1,0:T(8,128)(2,1)S(1)}, bf16[16,256,256]{2,1,0:T(8,128)(2,1)S(1)}) custom-call(bf16[17,32,256]{2,1,0:T(8,128)(2,1)S(1)} %get-tuple-element.53.chunk_ref.refs_0_, bf16[16,16,256]{2,1,0:T(8,128)(2,1)S(1)} %get-tuple-element.56.refs_1_, bf16[16,16,256]{2,1,0:T(8,128)(2,1)S(1)} %get-tuple-element.55.refs_2_, ...), custom_call_target="tpu_custom_call" | custom-call | flops 16106127 | bytes 83886 | tf_op jit(solution)/shard_map/rotate_here/pallas_call | solution.py:611
  15.2 0.0 collective-permute-done.7
  15.2 0.9 %collective-permute-done.6.refs_2_ = bf16[16,16,256]{2,1,0:T(8,128)(2,1)S(1)} collective-permute-done((bf16[16,16,256]{2,1,0:T(8,128)(2,1)S(1)}, bf16[16,16,256]{2,1,0:T(8,128)(2,1)S(1)}, u32[]{:S(2)}, u32[]{:S(2)}) %collective-permute-start.6) | collective-permute-done | bytes 131104 | tf_op jit(solution)/shard_map/ppermute | solution.py:496
  16.1 0.0 collective-permute-start.8
  16.1 2.0 %collective-permute-start.11 = (bf16[3,272,128]{2,1,0:T(8,128)(2,1)S(1)}, bf16[3,272,128]{2,1,0:T(8,128)(2,1)S(1)}, u32[]{:S(2)}, u32[]{:S(2)}) collective-permute-start(bf16[3,272,128]{2,1,0:T(8,128)(2,1)S(1)} %broadcast_select_fusion.packed_ref), channel_id=1, source_target_pairs={{0,2},{1,3},{2,0},{3,1},{4,6},{5,7},{6,4},{7,5},{8,10},{9,11},{10,... | collective-permute-start | bytes 626696 | tf_op jit(solution)/shard_map/ppermute | solution.py:496
  18.1 1.1 %apply_rows_here.1 = (bf16[16,384,256]{2,1,0:T(8,128)(2,1)S(1)}, bf16[3,256,256]{2,1,0:T(8,128)(2,1)S(1)}) custom-call(bf16[3,16,128,256]{3,2,1,0:T(8,128)(2,1)S(1)} %get-tuple-element.71.rotated_ref, bf16[3,272,128]{2,1,0:T(8,128)(2,1)S(1)} %broadcast_select_fusion.packed_ref, f32[8,256]{1,0:T(8,128)S(1)} %get-tuple-element.51.keep_ref), custom_call_target="tpu_custom_call" | custom-call | flops 16106127 | bytes 83886 | tf_op jit(solution)/shard_map/apply_rows_here/pallas_call | solution.py:632
  19.2 0.0 collective-permute-done.8.refs_3_
  19.2 0.0 collective-permute-done.5.refs_1_
  19.3 1.1 %rotate_crossed.1 = (bf16[3,16,256,256]{3,2,1,0:T(8,128)(2,1)S(1)}, bf16[16,256,256]{2,1,0:T(8,128)(2,1)S(1)}) custom-call(bf16[17,32,256]{2,1,0:T(8,128)(2,1)S(1)} %collective-permute-done.2.chunk_ref.refs_0_, bf16[17,32,256]{2,1,0:T(8,128)(2,1)S(1)} %collective-permute-done.5.refs_1_, ...), custom_call_target="tpu_custom_call", output_to_operand_aliasing={{0}: (5, {}), {1}: (6, {})} | custom-call | flops 16106127 | bytes 83886 | tf_op jit(solution)/shard_map/rotate_crossed/pallas_call | solution.py:611
  20.3 0.0 collective-permute-done.1.refs_0_
  20.3 0.3 collective-permute-start.9
  20.6 1.4 %apply_rows_crossed.1.refs_6_ = bf16[16,288,256]{2,1,0:T(8,128)(2,1)S(1)} custom-call(bf16[17,32,256]{2,1,0:T(8,128)(2,1)S(1)} %collective-permute-done.2.chunk_ref.refs_0_, bf16[17,32,256]{2,1,0:T(8,128)(2,1)S(1)} %collective-permute-done.5.refs_1_, bf16[16,16,256]{2,1,0:T(8,128)(2,1)S(1)} %collective-permute-done.6.refs_2_, ...), custom_call_target="tpu_custom_call" | custom-call | flops 16106127 | bytes 83886 | tf_op jit(solution)/shard_map/apply_rows_crossed/pallas_call | solution.py:653
  22.0 0.0 collective-permute-done.9.refs_1_
  22.0 2.2 %apply_rows_last.1.before_ref = f32[16,256,256]{2,1,0:T(8,128)S(1)} custom-call(bf16[16,16,256]{2,1,0:T(8,128)(2,1)S(1)} %collective-permute-done.1.refs_0_, bf16[16,16,256]{2,1,0:T(8,128)(2,1)S(1)} %collective-permute-done.9.refs_1_, bf16[3,256,256]{2,1,0:T(8,128)(2,1)S(1)} %get-tuple-element.78.refs_4_.refs_2_.right_ref, ...), custom_call_target="tpu_custom_call" | custom-call | flops 16106127 | bytes 83886 | tf_op jit(solution)/shard_map/apply_rows_last/pallas_call | solution.py:667
  24.3 0.0 collective-permute-done.10.refs_5_
  24.3 2.4 %received_lefts.1 = (bf16[16,256,768]{2,1,0:T(8,128)(2,1)S(1)}, f32[8,256]{1,0:T(8,128)S(1)}, bf16[3,16,256,256]{3,2,1,0:T(8,128)(2,1)S(1)}, bf16[16,256,256]{2,1,0:T(8,128)(2,1)S(1)}) custom-call(bf16[16,16,256]{2,1,0:T(8,128)(2,1)S(1)} %collective-permute-done.1.refs_0_, ...), custom_call_target="tpu_custom_call", output_to_operand_aliasing={{2}: (3, {}), {3}: (4, {})} | custom-call | flops 16106127 | bytes 125829 | tf_op jit(solution)/shard_map/received_lefts/pallas_call | solution.py:686
  26.7 0.3 collective-permute-start.12
  27.0 0.5 %collective-permute-done.11.packed_ref = bf16[3,272,128]{2,1,0:T(8,128)(2,1)S(1)} collective-permute-done((bf16[3,272,128]{2,1,0:T(8,128)(2,1)S(1)}, bf16[3,272,128]{2,1,0:T(8,128)(2,1)S(1)}, u32[]{:S(2)}, u32[]{:S(2)}) %collective-permute-start.11) | collective-permute-done | bytes 208928 | tf_op jit(solution)/shard_map/ppermute | solution.py:496
  27.6 1.2 %received_rights.2 = (bf16[8,256,256]{2,1,0:T(8,128)(2,1)S(1)}, bf16[3,256,256]{2,1,0:T(8,128)(2,1)S(1)}) custom-call(bf16[3,272,128]{2,1,0:T(8,128)(2,1)S(1)} %collective-permute-done.11.packed_ref, bf16[16,256,768]{2,1,0:T(8,128)(2,1)S(1)} %get-tuple-element.84.mixed_ref, f32[16,256,256]{2,1,0:T(8,128)S(1)} %apply_rows_last.1.before_ref, ...), custom_call_target="tpu_custom_call" | custom-call | flops 8053063 | bytes 125829 | tf_op jit(solution)/shard_map/received_rights/pallas_call | solution.py:703
  28.8 0.1 collective-permute-start.13
  28.9 0.0 collective-permute-done.12.norm_other_ref
  28.9 1.1 %received_rights.3.high_ref.refs_2_ = bf16[8,256,256]{2,1,0:T(8,128)(2,1)S(1)} custom-call(bf16[3,256,256]{2,1,0:T(8,128)(2,1)S(1)} %get-tuple-element.91.packed_ref, bf16[16,256,768]{2,1,0:T(8,128)(2,1)S(1)} %get-tuple-element.84.mixed_ref, f32[16,256,256]{2,1,0:T(8,128)S(1)} %apply_rows_last.1.before_ref, f32[8,256]{1,0:T(8,128)S(1)} %get-tuple-element.51.keep_ref), custom_call_target="tpu_custom_call" | custom-call | flops 8053063 | bytes 125829 | tf_op jit(solution)/shard_map/received_rights/pallas_call | solution.py:703
  29.9 0.6 %collective-permute-start.14 = (bf16[8,256,256]{2,1,0:T(8,128)(2,1)S(1)}, bf16[8,256,256]{2,1,0:T(8,128)(2,1)S(1)}, u32[]{:S(2)}, u32[]{:S(2)}) collective-permute-start(bf16[8,256,256]{2,1,0:T(8,128)(2,1)S(1)} %received_rights.3.high_ref.refs_2_), channel_id=1, source_target_pairs={{0,1},{1,0},{2,3},{3,2},{4,5},{5,4},{6,7},{7,6},{8,9},{9,8},{10,11... | collective-permute-start | bytes 3145736 | tf_op jit(solution)/shard_map/ppermute | solution.py:493
  30.5 1.0 %collective-permute-done.13.low_other_ref.refs_1_ = bf16[8,256,256]{2,1,0:T(8,128)(2,1)S(1)} collective-permute-done((bf16[8,256,256]{2,1,0:T(8,128)(2,1)S(1)}, bf16[8,256,256]{2,1,0:T(8,128)(2,1)S(1)}, u32[]{:S(2)}, u32[]{:S(2)}) %collective-permute-start.13) | collective-permute-done | bytes 1048608 | tf_op jit(solution)/shard_map/ppermute | solution.py:493
  31.5 2.9 %residual_low.1 = (bf16[8,256,256]{2,1,0:T(8,128)(2,1)S(1)}, bf16[3,8,256,256]{3,2,1,0:T(8,128)(2,1)S(1)}, f32[8,256]{1,0:T(8,128)S(1)}) custom-call(f32[8,256]{1,0:T(8,128)S(1)} %get-tuple-element.83.norm_ref, f32[8,256]{1,0:T(8,128)S(1)} %collective-permute-done.12.norm_other_ref, bf16[8,256,256]{2,1,0:T(8,128)(2,1)S(1)} %get-tuple-element.88.low_ref.refs_0_, ...), custom_call_target="tpu_custom_call" | custom-call | flops 8053063 | bytes 31457 | tf_op jit(solution)/shard_map/residual_low/pallas_call | solution.py:722
  34.4 0.0 collective-permute-done.14.high_other_ref.refs_3_
  34.4 0.0 copy-start
  34.5 6.4 %residual_high.1.share_ref.refs_0_ = f32[8,256]{1,0:T(8,128)S(1)} custom-call(f32[8,256]{1,0:T(8,128)S(1)} %get-tuple-element.83.norm_ref, f32[8,256]{1,0:T(8,128)S(1)} %collective-permute-done.12.norm_other_ref, f32[8,256]{1,0:T(8,128)S(1)} %get-tuple-element.90.sums_ref, bf16[8,256,256]{2,1,0:T(8,128)(2,1)S(1)} %received_rights.3.high_ref.refs_2_, ...), custom_call_target="tpu_custom_call" | custom-call | flops 48318384 | bytes 62914 | tf_op jit(solution)/shard_map/residual_high/pallas_call | solution.py:731
  40.9 1.8 %collective-permute-start.15 = (f32[8,256]{1,0:T(8,128)S(1)}, f32[8,256]{1,0:T(8,128)S(1)}, u32[]{:S(2)}, u32[]{:S(2)}) collective-permute-start(f32[8,256]{1,0:T(8,128)S(1)} %residual_high.1.share_ref.refs_0_), channel_id=1, source_target_pairs={{0,2},{1,3},{2,0},{3,1},{4,6},{5,7},{6,4},{7,5},{8,10},{9,11},{10,... | collective-permute-start | bytes 24584 | tf_op jit(solution)/shard_map/ppermute | solution.py:506
  42.7 0.0 collective-permute-start.16
  42.7 0.0 copy-done
  42.7 0.5 own_rows.1
  43.2 1.4 %collective-permute-done.15.refs_2_ = f32[8,256]{1,0:T(8,128)S(1)} collective-permute-done((f32[8,256]{1,0:T(8,128)S(1)}, f32[8,256]{1,0:T(8,128)S(1)}, u32[]{:S(2)}, u32[]{:S(2)}) %collective-permute-start.15) | collective-permute-done | bytes 8224 | tf_op jit(solution)/shard_map/ppermute | solution.py:506
  44.6 0.0 collective-permute-start.17
  44.6 0.0 collective-permute-done.16.refs_1_
  44.6 1.2 %collective-permute-done.17.refs_3_ = f32[8,256]{1,0:T(8,128)S(1)} collective-permute-done((f32[8,256]{1,0:T(8,128)S(1)}, f32[8,256]{1,0:T(8,128)S(1)}, u32[]{:S(2)}, u32[]{:S(2)}) %collective-permute-start.17) | collective-permute-done | bytes 8224 | tf_op jit(solution)/shard_map/ppermute | solution.py:493
  45.8 1.3 %finish.1 = (f32[64,16,256]{2,1,0:T(8,128)}, f32[1]{0:T(128)}) custom-call(f32[64,16,256]{2,1,0:T(8,128)S(1)} %get-tuple-element.94.vector_ref, f32[64,16,256]{2,1,0:T(8,128)S(1)} %get-tuple-element.96.residual_ref, f32[8,256]{1,0:T(8,128)S(1)} %residual_high.1.share_ref.refs_0_, f32[8,256]{1,0:T(8,128)S(1)} %collective-permute-done.16.refs_1_, ...), custom_call_target="tpu_custom_call" | custom-call | flops 7864 | bytes 31457 | tf_op jit(solution)/shard_map/finish/pallas_call | solution.py:761
  (1 shorter events, 0.0 us)
Async XLA Ops:
  2.7 4.4 %collective-permute-start = (bf16[17,32,256]{2,1,0:T(8,128)(2,1)S(1)}, bf16[17,32,256]{2,1,0:T(8,128)(2,1)S(1)}, u32[]{:S(2)}, u32[]{:S(2)}) collective-permute-start(bf16[17,32,256]{2,1,0:T(8,128)(2,1)S(1)} %get-tuple-element.53.chunk_ref.refs_0_), channel_id=1, source_target_pairs={{0,1},{1,0},{2,3},{3,2},{4,5},{5,4},{6,7},{7,6},{8,9},{9,8},{10,11... | collective-permute-start | bytes 835592 | tf_op jit(solution)/shard_map/ppermute | solution.py:493
  3.2 10.1 %collective-permute-start.2 = (bf16[17,32,256]{2,1,0:T(8,128)(2,1)S(1)}, bf16[17,32,256]{2,1,0:T(8,128)(2,1)S(1)}, u32[]{:S(2)}, u32[]{:S(2)}) collective-permute-start(bf16[17,32,256]{2,1,0:T(8,128)(2,1)S(1)} %get-tuple-element.53.chunk_ref.refs_0_), channel_id=1, source_target_pairs={{0,2},{1,3},{2,0},{3,1},{4,6},{5,7},{6,4},{7,5},{8,10},{9,11},{10,... | collective-permute-start | bytes 835592 | tf_op jit(solution)/shard_map/ppermute | solution.py:496
  5.8 9.4 %collective-permute-start.7 = (bf16[3,272,128]{2,1,0:T(8,128)(2,1)S(1)}, bf16[3,272,128]{2,1,0:T(8,128)(2,1)S(1)}, u32[]{:S(2)}, u32[]{:S(2)}) collective-permute-start(bf16[3,272,128]{2,1,0:T(8,128)(2,1)S(1)} %get-tuple-element.61), channel_id=1, source_target_pairs={{4,0},{8,4},{12,8},{16,12},{20,16},{24,20},{28,24},{5,1},{9,5},{13... | collective-permute-start | bytes 626696 | tf_op jit(solution)/shard_map/ppermute | solution.py:565
  8.4 1.4 %collective-permute-start.4 = (bf16[16,16,256]{2,1,0:T(8,128)(2,1)S(1)}, bf16[16,16,256]{2,1,0:T(8,128)(2,1)S(1)}, u32[]{:S(2)}, u32[]{:S(2)}) collective-permute-start(bf16[16,16,256]{2,1,0:T(8,128)(2,1)S(1)} %get-tuple-element.55.refs_2_), channel_id=1, source_target_pairs={{0,1},{1,0},{2,3},{3,2},{4,5},{5,4},{6,7},{7,6},{8,9},{9,8},{10,11... | collective-permute-start | bytes 393224 | tf_op jit(solution)/shard_map/ppermute | solution.py:493
  8.6 2.8 %collective-permute-start.3 = (bf16[16,16,256]{2,1,0:T(8,128)(2,1)S(1)}, bf16[16,16,256]{2,1,0:T(8,128)(2,1)S(1)}, u32[]{:S(2)}, u32[]{:S(2)}) collective-permute-start(bf16[16,16,256]{2,1,0:T(8,128)(2,1)S(1)} %get-tuple-element.56.refs_1_), channel_id=1, source_target_pairs={{0,1},{1,0},{2,3},{3,2},{4,5},{5,4},{6,7},{7,6},{8,9},{9,8},{10,11... | collective-permute-start | bytes 393224 | tf_op jit(solution)/shard_map/ppermute | solution.py:493
  9.0 7.1 %collective-permute-start.6 = (bf16[16,16,256]{2,1,0:T(8,128)(2,1)S(1)}, bf16[16,16,256]{2,1,0:T(8,128)(2,1)S(1)}, u32[]{:S(2)}, u32[]{:S(2)}) collective-permute-start(bf16[16,16,256]{2,1,0:T(8,128)(2,1)S(1)} %get-tuple-element.56.refs_1_), channel_id=1, source_target_pairs={{0,2},{1,3},{2,0},{3,1},{4,6},{5,7},{6,4},{7,5},{8,10},{9,11},{10,... | collective-permute-start | bytes 393224 | tf_op jit(solution)/shard_map/ppermute | solution.py:496
  9.8 10.5 %collective-permute-start.1 = (bf16[16,16,256]{2,1,0:T(8,128)(2,1)S(1)}, bf16[16,16,256]{2,1,0:T(8,128)(2,1)S(1)}, u32[]{:S(2)}, u32[]{:S(2)}) collective-permute-start(bf16[16,16,256]{2,1,0:T(8,128)(2,1)S(1)} %get-tuple-element.55.refs_2_), channel_id=1, source_target_pairs={{0,2},{1,3},{2,0},{3,1},{4,6},{5,7},{6,4},{7,5},{8,10},{9,11},{10,... | collective-permute-start | bytes 393224 | tf_op jit(solution)/shard_map/ppermute | solution.py:496
  11.5 12.8 %collective-permute-start.10 = (bf16[3,272,128]{2,1,0:T(8,128)(2,1)S(1)}, bf16[3,272,128]{2,1,0:T(8,128)(2,1)S(1)}, u32[]{:S(2)}, u32[]{:S(2)}) collective-permute-start(bf16[3,272,128]{2,1,0:T(8,128)(2,1)S(1)} %get-tuple-element.77), channel_id=1, source_target_pairs={{0,2},{1,3},{2,0},{3,1},{4,6},{5,7},{6,4},{7,5},{8,10},{9,11},{10,... | collective-permute-start | bytes 626696 | tf_op jit(solution)/shard_map/ppermute | solution.py:496
  13.3 6.0 %collective-permute-start.5 = (bf16[17,32,256]{2,1,0:T(8,128)(2,1)S(1)}, bf16[17,32,256]{2,1,0:T(8,128)(2,1)S(1)}, u32[]{:S(2)}, u32[]{:S(2)}) collective-permute-start(bf16[17,32,256]{2,1,0:T(8,128)(2,1)S(1)} %collective-permute-done.2.chunk_ref.refs_0_), channel_id=1, source_target_pairs={{0,1},{1,0},{2,3},{3,2},{4,5},{5,4},{6,7},{7,6},{8,9},{9,8},{10,11... | collective-permute-start | bytes 835592 | tf_op jit(solution)/shard_map/ppermute | solution.py:493
  16.1 3.2 %collective-permute-start.8 = (bf16[16,16,256]{2,1,0:T(8,128)(2,1)S(1)}, bf16[16,16,256]{2,1,0:T(8,128)(2,1)S(1)}, u32[]{:S(2)}, u32[]{:S(2)}) collective-permute-start(bf16[16,16,256]{2,1,0:T(8,128)(2,1)S(1)} %collective-permute-done.6.refs_2_), channel_id=1, source_target_pairs={{0,1},{1,0},{2,3},{3,2},{4,5},{5,4},{6,7},{7,6},{8,9},{9,8},{10,11... | collective-permute-start | bytes 393224 | tf_op jit(solution)/shard_map/ppermute | solution.py:493
  16.1 11.5 %collective-permute-start.11 = (bf16[3,272,128]{2,1,0:T(8,128)(2,1)S(1)}, bf16[3,272,128]{2,1,0:T(8,128)(2,1)S(1)}, u32[]{:S(2)}, u32[]{:S(2)}) collective-permute-start(bf16[3,272,128]{2,1,0:T(8,128)(2,1)S(1)} %broadcast_select_fusion.packed_ref), channel_id=1, source_target_pairs={{0,2},{1,3},{2,0},{3,1},{4,6},{5,7},{6,4},{7,5},{8,10},{9,11},{10,... | collective-permute-start | bytes 626696 | tf_op jit(solution)/shard_map/ppermute | solution.py:496
  20.3 1.7 %collective-permute-start.9 = (bf16[16,16,256]{2,1,0:T(8,128)(2,1)S(1)}, bf16[16,16,256]{2,1,0:T(8,128)(2,1)S(1)}, u32[]{:S(2)}, u32[]{:S(2)}) collective-permute-start(bf16[16,16,256]{2,1,0:T(8,128)(2,1)S(1)} %collective-permute-done.1.refs_0_), channel_id=1, source_target_pairs={{0,1},{1,0},{2,3},{3,2},{4,5},{5,4},{6,7},{7,6},{8,9},{9,8},{10,11... | collective-permute-start | bytes 393224 | tf_op jit(solution)/shard_map/ppermute | solution.py:493
  26.7 2.2 %collective-permute-start.12 = (f32[8,256]{1,0:T(8,128)S(1)}, f32[8,256]{1,0:T(8,128)S(1)}, u32[]{:S(2)}, u32[]{:S(2)}) collective-permute-start(f32[8,256]{1,0:T(8,128)S(1)} %get-tuple-element.83.norm_ref), channel_id=1, source_target_pairs={{0,1},{1,0},{2,3},{3,2},{4,5},{5,4},{6,7},{7,6},{8,9},{9,8},{10,11... | collective-permute-start | bytes 24584 | tf_op jit(solution)/shard_map/ppermute | solution.py:493
  28.8 2.7 %collective-permute-start.13 = (bf16[8,256,256]{2,1,0:T(8,128)(2,1)S(1)}, bf16[8,256,256]{2,1,0:T(8,128)(2,1)S(1)}, u32[]{:S(2)}, u32[]{:S(2)}) collective-permute-start(bf16[8,256,256]{2,1,0:T(8,128)(2,1)S(1)} %get-tuple-element.88.low_ref.refs_0_), channel_id=1, source_target_pairs={{0,1},{1,0},{2,3},{3,2},{4,5},{5,4},{6,7},{7,6},{8,9},{9,8},{10,11... | collective-permute-start | bytes 3145736 | tf_op jit(solution)/shard_map/ppermute | solution.py:493
  29.9 4.5 %collective-permute-start.14 = (bf16[8,256,256]{2,1,0:T(8,128)(2,1)S(1)}, bf16[8,256,256]{2,1,0:T(8,128)(2,1)S(1)}, u32[]{:S(2)}, u32[]{:S(2)}) collective-permute-start(bf16[8,256,256]{2,1,0:T(8,128)(2,1)S(1)} %received_rights.3.high_ref.refs_2_), channel_id=1, source_target_pairs={{0,1},{1,0},{2,3},{3,2},{4,5},{5,4},{6,7},{7,6},{8,9},{9,8},{10,11... | collective-permute-start | bytes 3145736 | tf_op jit(solution)/shard_map/ppermute | solution.py:493
  34.4 8.3 %copy-start = (f32[1,64,16,256]{3,2,1,0:T(8,128)S(1)}, f32[1,64,16,256]{3,2,1,0:T(8,128)}, u32[]{:S(2)}) copy-start(f32[1,64,16,256]{3,2,1,0:T(8,128)} %param.5) | copy-start | bytes 3145732
  40.9 3.7 %collective-permute-start.15 = (f32[8,256]{1,0:T(8,128)S(1)}, f32[8,256]{1,0:T(8,128)S(1)}, u32[]{:S(2)}, u32[]{:S(2)}) collective-permute-start(f32[8,256]{1,0:T(8,128)S(1)} %residual_high.1.share_ref.refs_0_), channel_id=1, source_target_pairs={{0,2},{1,3},{2,0},{3,1},{4,6},{5,7},{6,4},{7,5},{8,10},{9,11},{10,... | collective-permute-start | bytes 24584 | tf_op jit(solution)/shard_map/ppermute | solution.py:506
  42.7 1.9 %collective-permute-start.16 = (f32[8,256]{1,0:T(8,128)S(1)}, f32[8,256]{1,0:T(8,128)S(1)}, u32[]{:S(2)}, u32[]{:S(2)}) collective-permute-start(f32[8,256]{1,0:T(8,128)S(1)} %residual_high.1.share_ref.refs_0_), channel_id=1, source_target_pairs={{0,1},{1,0},{2,3},{3,2},{4,5},{5,4},{6,7},{7,6},{8,9},{9,8},{10,11... | collective-permute-start | bytes 24584 | tf_op jit(solution)/shard_map/ppermute | solution.py:493
  44.6 1.2 %collective-permute-start.17 = (f32[8,256]{1,0:T(8,128)S(1)}, f32[8,256]{1,0:T(8,128)S(1)}, u32[]{:S(2)}, u32[]{:S(2)}) collective-permute-start(f32[8,256]{1,0:T(8,128)S(1)} %collective-permute-done.15.refs_2_), channel_id=1, source_target_pairs={{0,1},{1,0},{2,3},{3,2},{4,5},{5,4},{6,7},{7,6},{8,9},{9,8},{10,11... | collective-permute-start | bytes 24584 | tf_op jit(solution)/shard_map/ppermute | solution.py:493

commit v14 on v13

--- a/solution.py
+++ b/solution.py
@@ -11,6 +11,7 @@
 CORES = 2
 TILE = 16
 UNROLL = 16
+STRIP = 32
 GROUP = 8
 VMEM_LIMIT = 20 * 1024 * 1024
 F32 = jnp.float32
@@ -336,17 +337,21 @@
     zero = jnp.zeros((8, width), F32)
 
     def lefts(n, sums):
-        held = whole_ref[start + n].astype(F32)
-        sigma = mine_ref[n].astype(F32) + other_ref[n].astype(F32)
-        residual = sigma - shift * held
-        rounded = residual.astype(BF16)
-        res_ref[n] = rounded
+        square, product = sums
+        for row in range(0, width, STRIP):
+            strip = pl.ds(row, STRIP)
+            held = whole_ref[start + n, strip, :].astype(F32)
+            sigma = mine_ref[n, strip, :].astype(F32) + other_ref[n, strip, :].astype(F32)
+            residual = sigma - shift * held
+            res_ref[n, strip, :] = residual.astype(BF16)
+            square = square + fold(residual * residual, width)
+            product = product + fold(sigma * held, width)
         mixed = jnp.dot(
-            left_ref[...].reshape(terms * width, width), rounded, preferred_element_type=F32
+            left_ref[...].reshape(terms * width, width), res_ref[n], preferred_element_type=F32
         ).astype(BF16)
         for k in range(terms):
             mixed_ref[k, n] = mixed[k * width : (k + 1) * width]
-        return sums[0] + fold(residual * residual, width), sums[1] + fold(sigma * held, width)
+        return square, product
 
     square, product = lax.fori_loop(0, count, lefts, (zero, zero), unroll=UNROLL)
     return jnp.sum(square), jnp.sum(product)
@@ -418,10 +423,9 @@
     cross = jnp.zeros((8, width), F32)
     for start, left_mixed_ref in ((0, mixed_low_ref), (half, mixed_ref)):
         for k in range(terms):
-            turned = rotated_ref[k, start : start + half].reshape(half * width, width)
-            image = jnp.dot(turned, right_ref[k], preferred_element_type=F32)
-            held = left_mixed_ref[k].reshape(half * width, width).astype(F32)
-            cross = cross + fold(held * image, width)
+            for n in range(half):
+                image = jnp.dot(rotated_ref[k, start + n], right_ref[k], preferred_element_type=F32)
+                cross = cross + fold(left_mixed_ref[k, n].astype(F32) * image, width)
     res_square = sums_ref[1:2, :] + square
     product = sums_ref[2:3, :] + product
     total = norm_ref[0:1, :] + norm_other_ref[0:1, :]

time: 47.4 us -> 47.5 us (level)
  no operation moved by 1% of the time
where the time goes in v14:
time: 47.5 us; the launch traced here: 47.3 us
  Pallas kernels  27.5 us (58%)
  starting transfers between devices  12.3 us (26%)
  waiting for transfers between devices  5.75 us (12%)
  between operations  1.68 us (4%)
    ppermute x5, starting transfers between devices, to_next_chip(): lax.ppermute(block, 'term', [(i, (i + CORES) % members) for i in range(me...  6.81 us
    pallas_call x1, Pallas kernels, shards(): pl.pallas_call(functools.partial(high_kernel, scale, members), out_shape=...  6.48 us
    pallas_call x1, Pallas kernels, shards(): pl.pallas_call(low_kernel, out_shape=(half_bf, jax.ShapeDtypeStruct(half_...  2.92 us
    pallas_call x2, Pallas kernels, rotate(): pl.pallas_call(functools.partial(rotate_kernel, spots, rows, chips), out_...  2.59 us
    ppermute x11, waiting for transfers between devices, to_sibling(): return lax.ppermute(block, 'term', [(i, i ^ 1) for i in range(members)])  2.48 us
    pallas_call x1, Pallas kernels, shards(): pl.pallas_call(functools.partial(lefts_kernel, far_spots[-1], rows, chips...  2.42 us
    ppermute x11, starting transfers between devices, to_sibling(): return lax.ppermute(block, 'term', [(i, i ^ 1) for i in range(members)])  2.36 us
    pallas_call x2, Pallas kernels, shards(): pl.pallas_call(functools.partial(rights_kernel, start, stop), out_shape=(...  2.25 us
  transfers between devices with their start and end apart: 18, of which 7 were waited for; matrix products, arithmetic and copies ran while one was open for 0% of the time, Pallas kernels for 39%

profile of v14, /device:TPU:0, one launch (start us, length us, event | category | flops | bytes accessed | tf_op | source)
XLA Modules:
  0.0 47.3 jit_solution(14913732376954719000)
XLA Ops:
  1.3 1.4 %first_chunk.1 = (bf16[17,32,256]{2,1,0:T(8,128)(2,1)S(1)}, f32[8,256]{1,0:T(8,128)S(1)}, f32[8,256]{1,0:T(8,128)S(1)}, bf16[3,272,128]{2,1,0:T(8,128)(2,1)S(1)}) custom-call(s32[1,1]{1,0:T(1,128)} %bitcast.6.rank_in, f32[64,16,256]{2,1,0:T(8,128)} %bitcast.7, bf16[3,16,16]{2,1,0:T(8,128)(2,1)} %bitcast.12, bf16[3,256,256]{2,1,0:T(8,128)(2,1)} %bitcast.10), custom_call_target="tpu_custom_call" | custom-call | flops 5242 | bytes 7864 | tf_op jit(solution)/shard_map/first_chunk/pallas_call | solution.py:520
  2.7 0.5 %collective-permute-start = (bf16[17,32,256]{2,1,0:T(8,128)(2,1)S(1)}, bf16[17,32,256]{2,1,0:T(8,128)(2,1)S(1)}, u32[]{:S(2)}, u32[]{:S(2)}) collective-permute-start(bf16[17,32,256]{2,1,0:T(8,128)(2,1)S(1)} %get-tuple-element.53.chunk_ref.refs_0_), channel_id=1, source_target_pairs={{0,1},{1,0},{2,3},{3,2},{4,5},{5,4},{6,7},{7,6},{8,9},{9,8},{10,11... | collective-permute-start | bytes 835592 | tf_op jit(solution)/shard_map/ppermute | solution.py:497
  3.2 2.6 %collective-permute-start.2 = (bf16[17,32,256]{2,1,0:T(8,128)(2,1)S(1)}, bf16[17,32,256]{2,1,0:T(8,128)(2,1)S(1)}, u32[]{:S(2)}, u32[]{:S(2)}) collective-permute-start(bf16[17,32,256]{2,1,0:T(8,128)(2,1)S(1)} %get-tuple-element.53.chunk_ref.refs_0_), channel_id=1, source_target_pairs={{0,2},{1,3},{2,0},{3,1},{4,6},{5,7},{6,4},{7,5},{8,10},{9,11},{10,... | collective-permute-start | bytes 835592 | tf_op jit(solution)/shard_map/ppermute | solution.py:500
  5.8 1.3 %collective-permute-start.7 = (bf16[3,272,128]{2,1,0:T(8,128)(2,1)S(1)}, bf16[3,272,128]{2,1,0:T(8,128)(2,1)S(1)}, u32[]{:S(2)}, u32[]{:S(2)}) collective-permute-start(bf16[3,272,128]{2,1,0:T(8,128)(2,1)S(1)} %get-tuple-element.61), channel_id=1, source_target_pairs={{4,0},{8,4},{12,8},{16,12},{20,16},{24,20},{28,24},{5,1},{9,5},{13... | collective-permute-start | bytes 626696 | tf_op jit(solution)/shard_map/ppermute | solution.py:569
  7.1 0.0 collective-permute-done.refs_3_
  7.1 1.3 %prepare.1 = (f32[8,256]{1,0:T(8,128)S(1)}, bf16[3,272,128]{2,1,0:T(8,128)(2,1)S(1)}, bf16[3,256,256]{2,1,0:T(8,128)(2,1)S(1)}, bf16[16,16,256]{2,1,0:T(8,128)(2,1)S(1)}, bf16[16,16,256]{2,1,0:T(8,128)(2,1)S(1)}) custom-call(f32[8,256]{1,0:T(8,128)S(1)} %get-tuple-element.51.keep_ref, f32[8,256]{1,0:T(8,128)S(1)} %get-tuple-element.54.squares_ref, ...), custom_call_target="tpu_custom_call" | custom-call | flops 10485 | bytes 15728 | tf_op jit(solution)/shard_map/prepare/pallas_call | solution.py:538
  8.4 0.2 collective-permute-start.4
  8.6 0.3 collective-permute-start.3
  9.0 0.2 collective-permute-start.6
  9.2 0.4 spread_site.2.refs_6_.refs_5_.refs_3_.kron_ref
  9.6 0.3 collective-permute-done.4.refs_5_
  9.8 1.7 %collective-permute-start.1 = (bf16[16,16,256]{2,1,0:T(8,128)(2,1)S(1)}, bf16[16,16,256]{2,1,0:T(8,128)(2,1)S(1)}, u32[]{:S(2)}, u32[]{:S(2)}) collective-permute-start(bf16[16,16,256]{2,1,0:T(8,128)(2,1)S(1)} %get-tuple-element.55.refs_2_), channel_id=1, source_target_pairs={{0,2},{1,3},{2,0},{3,1},{4,6},{5,7},{6,4},{7,5},{8,10},{9,11},{10,... | collective-permute-start | bytes 393224 | tf_op jit(solution)/shard_map/ppermute | solution.py:500
  11.5 0.0 collective-permute-done.3.refs_4_
  11.5 0.4 collective-permute-start.10
  11.9 1.0 %rotate_own.1 = (bf16[3,16,128,256]{3,2,1,0:T(8,128)(2,1)S(1)}, bf16[256,768]{1,0:T(8,128)(2,1)S(1)}) custom-call(bf16[17,32,256]{2,1,0:T(8,128)(2,1)S(1)} %get-tuple-element.53.chunk_ref.refs_0_, bf16[16,16,256]{2,1,0:T(8,128)(2,1)S(1)} %get-tuple-element.56.refs_1_, bf16[16,16,256]{2,1,0:T(8,128)(2,1)S(1)} %get-tuple-element.55.refs_2_, ...), custom_call_target="tpu_custom_call" | custom-call | flops 16106127 | bytes 83886 | tf_op jit(solution)/shard_map/rotate_own/pallas_call | solution.py:601
  12.8 0.4 collective-permute-done.2.chunk_ref.refs_0_
  13.3 0.0 collective-permute-start.5
  13.3 0.4 spread_site.3.refs_6_.refs_4_.refs_2_
  13.7 1.5 %rotate_here.1 = (bf16[3,16,256,256]{3,2,1,0:T(8,128)(2,1)S(1)}, bf16[16,256,256]{2,1,0:T(8,128)(2,1)S(1)}) custom-call(bf16[17,32,256]{2,1,0:T(8,128)(2,1)S(1)} %get-tuple-element.53.chunk_ref.refs_0_, bf16[16,16,256]{2,1,0:T(8,128)(2,1)S(1)} %get-tuple-element.56.refs_1_, bf16[16,16,256]{2,1,0:T(8,128)(2,1)S(1)} %get-tuple-element.55.refs_2_, ...), custom_call_target="tpu_custom_call" | custom-call | flops 16106127 | bytes 83886 | tf_op jit(solution)/shard_map/rotate_here/pallas_call | solution.py:615
  15.2 0.0 collective-permute-done.7
  15.2 0.9 %collective-permute-done.6.refs_2_ = bf16[16,16,256]{2,1,0:T(8,128)(2,1)S(1)} collective-permute-done((bf16[16,16,256]{2,1,0:T(8,128)(2,1)S(1)}, bf16[16,16,256]{2,1,0:T(8,128)(2,1)S(1)}, u32[]{:S(2)}, u32[]{:S(2)}) %collective-permute-start.6) | collective-permute-done | bytes 131104 | tf_op jit(solution)/shard_map/ppermute | solution.py:500
  16.1 0.0 collective-permute-start.8
  16.1 2.0 %collective-permute-start.11 = (bf16[3,272,128]{2,1,0:T(8,128)(2,1)S(1)}, bf16[3,272,128]{2,1,0:T(8,128)(2,1)S(1)}, u32[]{:S(2)}, u32[]{:S(2)}) collective-permute-start(bf16[3,272,128]{2,1,0:T(8,128)(2,1)S(1)} %broadcast_select_fusion.packed_ref), channel_id=1, source_target_pairs={{0,2},{1,3},{2,0},{3,1},{4,6},{5,7},{6,4},{7,5},{8,10},{9,11},{10,... | collective-permute-start | bytes 626696 | tf_op jit(solution)/shard_map/ppermute | solution.py:500
  18.1 1.1 %apply_rows_here.1 = (bf16[16,384,256]{2,1,0:T(8,128)(2,1)S(1)}, bf16[3,256,256]{2,1,0:T(8,128)(2,1)S(1)}) custom-call(bf16[3,16,128,256]{3,2,1,0:T(8,128)(2,1)S(1)} %get-tuple-element.71.rotated_ref, bf16[3,272,128]{2,1,0:T(8,128)(2,1)S(1)} %broadcast_select_fusion.packed_ref, f32[8,256]{1,0:T(8,128)S(1)} %get-tuple-element.51.keep_ref), custom_call_target="tpu_custom_call" | custom-call | flops 16106127 | bytes 83886 | tf_op jit(solution)/shard_map/apply_rows_here/pallas_call | solution.py:636
  19.2 0.0 collective-permute-done.8.refs_3_
  19.2 0.0 collective-permute-done.5.refs_1_
  19.3 1.1 %rotate_crossed.1 = (bf16[3,16,256,256]{3,2,1,0:T(8,128)(2,1)S(1)}, bf16[16,256,256]{2,1,0:T(8,128)(2,1)S(1)}) custom-call(bf16[17,32,256]{2,1,0:T(8,128)(2,1)S(1)} %collective-permute-done.2.chunk_ref.refs_0_, bf16[17,32,256]{2,1,0:T(8,128)(2,1)S(1)} %collective-permute-done.5.refs_1_, ...), custom_call_target="tpu_custom_call", output_to_operand_aliasing={{0}: (5, {}), {1}: (6, {})} | custom-call | flops 16106127 | bytes 83886 | tf_op jit(solution)/shard_map/rotate_crossed/pallas_call | solution.py:615
  20.3 0.0 collective-permute-done.1.refs_0_
  20.3 0.3 collective-permute-start.9
  20.6 1.4 %apply_rows_crossed.1.refs_6_ = bf16[16,288,256]{2,1,0:T(8,128)(2,1)S(1)} custom-call(bf16[17,32,256]{2,1,0:T(8,128)(2,1)S(1)} %collective-permute-done.2.chunk_ref.refs_0_, bf16[17,32,256]{2,1,0:T(8,128)(2,1)S(1)} %collective-permute-done.5.refs_1_, bf16[16,16,256]{2,1,0:T(8,128)(2,1)S(1)} %collective-permute-done.6.refs_2_, ...), custom_call_target="tpu_custom_call" | custom-call | flops 16106127 | bytes 83886 | tf_op jit(solution)/shard_map/apply_rows_crossed/pallas_call | solution.py:657
  22.0 0.0 collective-permute-done.9.refs_1_
  22.0 2.2 %apply_rows_last.1.before_ref = f32[16,256,256]{2,1,0:T(8,128)S(1)} custom-call(bf16[16,16,256]{2,1,0:T(8,128)(2,1)S(1)} %collective-permute-done.1.refs_0_, bf16[16,16,256]{2,1,0:T(8,128)(2,1)S(1)} %collective-permute-done.9.refs_1_, bf16[3,256,256]{2,1,0:T(8,128)(2,1)S(1)} %get-tuple-element.78.refs_4_.refs_2_.right_ref, ...), custom_call_target="tpu_custom_call" | custom-call | flops 16106127 | bytes 83886 | tf_op jit(solution)/shard_map/apply_rows_last/pallas_call | solution.py:671
  24.3 0.0 collective-permute-done.10.refs_5_
  24.3 2.4 %received_lefts.1 = (bf16[16,256,768]{2,1,0:T(8,128)(2,1)S(1)}, f32[8,256]{1,0:T(8,128)S(1)}, bf16[3,16,256,256]{3,2,1,0:T(8,128)(2,1)S(1)}, bf16[16,256,256]{2,1,0:T(8,128)(2,1)S(1)}) custom-call(bf16[16,16,256]{2,1,0:T(8,128)(2,1)S(1)} %collective-permute-done.1.refs_0_, ...), custom_call_target="tpu_custom_call", output_to_operand_aliasing={{2}: (3, {}), {3}: (4, {})} | custom-call | flops 16106127 | bytes 125829 | tf_op jit(solution)/shard_map/received_lefts/pallas_call | solution.py:690
  26.7 0.3 collective-permute-start.12
  27.0 0.5 %collective-permute-done.11.packed_ref = bf16[3,272,128]{2,1,0:T(8,128)(2,1)S(1)} collective-permute-done((bf16[3,272,128]{2,1,0:T(8,128)(2,1)S(1)}, bf16[3,272,128]{2,1,0:T(8,128)(2,1)S(1)}, u32[]{:S(2)}, u32[]{:S(2)}) %collective-permute-start.11) | collective-permute-done | bytes 208928 | tf_op jit(solution)/shard_map/ppermute | solution.py:500
  27.6 1.2 %received_rights.2 = (bf16[8,256,256]{2,1,0:T(8,128)(2,1)S(1)}, bf16[3,256,256]{2,1,0:T(8,128)(2,1)S(1)}) custom-call(bf16[3,272,128]{2,1,0:T(8,128)(2,1)S(1)} %collective-permute-done.11.packed_ref, bf16[16,256,768]{2,1,0:T(8,128)(2,1)S(1)} %get-tuple-element.84.mixed_ref, f32[16,256,256]{2,1,0:T(8,128)S(1)} %apply_rows_last.1.before_ref, ...), custom_call_target="tpu_custom_call" | custom-call | flops 8053063 | bytes 125829 | tf_op jit(solution)/shard_map/received_rights/pallas_call | solution.py:707
  28.8 0.1 collective-permute-start.13
  28.9 0.0 collective-permute-done.12.norm_other_ref
  28.9 1.1 %received_rights.3.high_ref.refs_2_ = bf16[8,256,256]{2,1,0:T(8,128)(2,1)S(1)} custom-call(bf16[3,256,256]{2,1,0:T(8,128)(2,1)S(1)} %get-tuple-element.91.packed_ref, bf16[16,256,768]{2,1,0:T(8,128)(2,1)S(1)} %get-tuple-element.84.mixed_ref, f32[16,256,256]{2,1,0:T(8,128)S(1)} %apply_rows_last.1.before_ref, f32[8,256]{1,0:T(8,128)S(1)} %get-tuple-element.51.keep_ref), custom_call_target="tpu_custom_call" | custom-call | flops 8053063 | bytes 125829 | tf_op jit(solution)/shard_map/received_rights/pallas_call | solution.py:707
  29.9 0.6 %collective-permute-start.14 = (bf16[8,256,256]{2,1,0:T(8,128)(2,1)S(1)}, bf16[8,256,256]{2,1,0:T(8,128)(2,1)S(1)}, u32[]{:S(2)}, u32[]{:S(2)}) collective-permute-start(bf16[8,256,256]{2,1,0:T(8,128)(2,1)S(1)} %received_rights.3.high_ref.refs_2_), channel_id=1, source_target_pairs={{0,1},{1,0},{2,3},{3,2},{4,5},{5,4},{6,7},{7,6},{8,9},{9,8},{10,11... | collective-permute-start | bytes 3145736 | tf_op jit(solution)/shard_map/ppermute | solution.py:497
  30.5 1.0 %collective-permute-done.13.low_other_ref.refs_1_ = bf16[8,256,256]{2,1,0:T(8,128)(2,1)S(1)} collective-permute-done((bf16[8,256,256]{2,1,0:T(8,128)(2,1)S(1)}, bf16[8,256,256]{2,1,0:T(8,128)(2,1)S(1)}, u32[]{:S(2)}, u32[]{:S(2)}) %collective-permute-start.13) | collective-permute-done | bytes 1048608 | tf_op jit(solution)/shard_map/ppermute | solution.py:497
  31.5 2.9 %residual_low.1 = (bf16[8,256,256]{2,1,0:T(8,128)(2,1)S(1)}, bf16[3,8,256,256]{3,2,1,0:T(8,128)(2,1)S(1)}, f32[8,256]{1,0:T(8,128)S(1)}) custom-call(f32[8,256]{1,0:T(8,128)S(1)} %get-tuple-element.83.norm_ref, f32[8,256]{1,0:T(8,128)S(1)} %collective-permute-done.12.norm_other_ref, bf16[8,256,256]{2,1,0:T(8,128)(2,1)S(1)} %get-tuple-element.88.low_ref.refs_0_, ...), custom_call_target="tpu_custom_call" | custom-call | flops 8053063 | bytes 31457 | tf_op jit(solution)/shard_map/residual_low/pallas_call | solution.py:726
  34.4 0.0 collective-permute-done.14.high_other_ref.refs_3_
  34.4 0.0 copy-start
  34.5 6.5 %residual_high.1.share_ref.refs_0_ = f32[8,256]{1,0:T(8,128)S(1)} custom-call(f32[8,256]{1,0:T(8,128)S(1)} %get-tuple-element.83.norm_ref, f32[8,256]{1,0:T(8,128)S(1)} %collective-permute-done.12.norm_other_ref, f32[8,256]{1,0:T(8,128)S(1)} %get-tuple-element.90.sums_ref, bf16[8,256,256]{2,1,0:T(8,128)(2,1)S(1)} %received_rights.3.high_ref.refs_2_, ...), custom_call_target="tpu_custom_call" | custom-call | flops 48318384 | bytes 62914 | tf_op jit(solution)/shard_map/residual_high/pallas_call | solution.py:735
  40.9 1.8 %collective-permute-start.15 = (f32[8,256]{1,0:T(8,128)S(1)}, f32[8,256]{1,0:T(8,128)S(1)}, u32[]{:S(2)}, u32[]{:S(2)}) collective-permute-start(f32[8,256]{1,0:T(8,128)S(1)} %residual_high.1.share_ref.refs_0_), channel_id=1, source_target_pairs={{0,2},{1,3},{2,0},{3,1},{4,6},{5,7},{6,4},{7,5},{8,10},{9,11},{10,... | collective-permute-start | bytes 24584 | tf_op jit(solution)/shard_map/ppermute | solution.py:510
  42.8 0.0 collective-permute-start.16
  42.8 0.0 copy-done
  42.8 0.5 own_rows.1
  43.2 1.4 %collective-permute-done.15.refs_2_ = f32[8,256]{1,0:T(8,128)S(1)} collective-permute-done((f32[8,256]{1,0:T(8,128)S(1)}, f32[8,256]{1,0:T(8,128)S(1)}, u32[]{:S(2)}, u32[]{:S(2)}) %collective-permute-start.15) | collective-permute-done | bytes 8224 | tf_op jit(solution)/shard_map/ppermute | solution.py:510
  44.7 0.0 collective-permute-start.17
  44.7 0.0 collective-permute-done.16.refs_1_
  44.7 1.2 %collective-permute-done.17.refs_3_ = f32[8,256]{1,0:T(8,128)S(1)} collective-permute-done((f32[8,256]{1,0:T(8,128)S(1)}, f32[8,256]{1,0:T(8,128)S(1)}, u32[]{:S(2)}, u32[]{:S(2)}) %collective-permute-start.17) | collective-permute-done | bytes 8224 | tf_op jit(solution)/shard_map/ppermute | solution.py:497
  45.8 1.3 %finish.1 = (f32[64,16,256]{2,1,0:T(8,128)}, f32[1]{0:T(128)}) custom-call(f32[64,16,256]{2,1,0:T(8,128)S(1)} %get-tuple-element.94.vector_ref, f32[64,16,256]{2,1,0:T(8,128)S(1)} %get-tuple-element.96.residual_ref, f32[8,256]{1,0:T(8,128)S(1)} %residual_high.1.share_ref.refs_0_, f32[8,256]{1,0:T(8,128)S(1)} %collective-permute-done.16.refs_1_, ...), custom_call_target="tpu_custom_call" | custom-call | flops 7864 | bytes 31457 | tf_op jit(solution)/shard_map/finish/pallas_call | solution.py:765
  (1 shorter events, 0.0 us)
Async XLA Ops:
  2.7 4.4 %collective-permute-start = (bf16[17,32,256]{2,1,0:T(8,128)(2,1)S(1)}, bf16[17,32,256]{2,1,0:T(8,128)(2,1)S(1)}, u32[]{:S(2)}, u32[]{:S(2)}) collective-permute-start(bf16[17,32,256]{2,1,0:T(8,128)(2,1)S(1)} %get-tuple-element.53.chunk_ref.refs_0_), channel_id=1, source_target_pairs={{0,1},{1,0},{2,3},{3,2},{4,5},{5,4},{6,7},{7,6},{8,9},{9,8},{10,11... | collective-permute-start | bytes 835592 | tf_op jit(solution)/shard_map/ppermute | solution.py:497
  3.2 10.1 %collective-permute-start.2 = (bf16[17,32,256]{2,1,0:T(8,128)(2,1)S(1)}, bf16[17,32,256]{2,1,0:T(8,128)(2,1)S(1)}, u32[]{:S(2)}, u32[]{:S(2)}) collective-permute-start(bf16[17,32,256]{2,1,0:T(8,128)(2,1)S(1)} %get-tuple-element.53.chunk_ref.refs_0_), channel_id=1, source_target_pairs={{0,2},{1,3},{2,0},{3,1},{4,6},{5,7},{6,4},{7,5},{8,10},{9,11},{10,... | collective-permute-start | bytes 835592 | tf_op jit(solution)/shard_map/ppermute | solution.py:500
  5.8 9.4 %collective-permute-start.7 = (bf16[3,272,128]{2,1,0:T(8,128)(2,1)S(1)}, bf16[3,272,128]{2,1,0:T(8,128)(2,1)S(1)}, u32[]{:S(2)}, u32[]{:S(2)}) collective-permute-start(bf16[3,272,128]{2,1,0:T(8,128)(2,1)S(1)} %get-tuple-element.61), channel_id=1, source_target_pairs={{4,0},{8,4},{12,8},{16,12},{20,16},{24,20},{28,24},{5,1},{9,5},{13... | collective-permute-start | bytes 626696 | tf_op jit(solution)/shard_map/ppermute | solution.py:569
  8.4 1.4 %collective-permute-start.4 = (bf16[16,16,256]{2,1,0:T(8,128)(2,1)S(1)}, bf16[16,16,256]{2,1,0:T(8,128)(2,1)S(1)}, u32[]{:S(2)}, u32[]{:S(2)}) collective-permute-start(bf16[16,16,256]{2,1,0:T(8,128)(2,1)S(1)} %get-tuple-element.55.refs_2_), channel_id=1, source_target_pairs={{0,1},{1,0},{2,3},{3,2},{4,5},{5,4},{6,7},{7,6},{8,9},{9,8},{10,11... | collective-permute-start | bytes 393224 | tf_op jit(solution)/shard_map/ppermute | solution.py:497
  8.6 2.8 %collective-permute-start.3 = (bf16[16,16,256]{2,1,0:T(8,128)(2,1)S(1)}, bf16[16,16,256]{2,1,0:T(8,128)(2,1)S(1)}, u32[]{:S(2)}, u32[]{:S(2)}) collective-permute-start(bf16[16,16,256]{2,1,0:T(8,128)(2,1)S(1)} %get-tuple-element.56.refs_1_), channel_id=1, source_target_pairs={{0,1},{1,0},{2,3},{3,2},{4,5},{5,4},{6,7},{7,6},{8,9},{9,8},{10,11... | collective-permute-start | bytes 393224 | tf_op jit(solution)/shard_map/ppermute | solution.py:497
  9.0 7.1 %collective-permute-start.6 = (bf16[16,16,256]{2,1,0:T(8,128)(2,1)S(1)}, bf16[16,16,256]{2,1,0:T(8,128)(2,1)S(1)}, u32[]{:S(2)}, u32[]{:S(2)}) collective-permute-start(bf16[16,16,256]{2,1,0:T(8,128)(2,1)S(1)} %get-tuple-element.56.refs_1_), channel_id=1, source_target_pairs={{0,2},{1,3},{2,0},{3,1},{4,6},{5,7},{6,4},{7,5},{8,10},{9,11},{10,... | collective-permute-start | bytes 393224 | tf_op jit(solution)/shard_map/ppermute | solution.py:500
  9.8 10.5 %collective-permute-start.1 = (bf16[16,16,256]{2,1,0:T(8,128)(2,1)S(1)}, bf16[16,16,256]{2,1,0:T(8,128)(2,1)S(1)}, u32[]{:S(2)}, u32[]{:S(2)}) collective-permute-start(bf16[16,16,256]{2,1,0:T(8,128)(2,1)S(1)} %get-tuple-element.55.refs_2_), channel_id=1, source_target_pairs={{0,2},{1,3},{2,0},{3,1},{4,6},{5,7},{6,4},{7,5},{8,10},{9,11},{10,... | collective-permute-start | bytes 393224 | tf_op jit(solution)/shard_map/ppermute | solution.py:500
  11.5 12.8 %collective-permute-start.10 = (bf16[3,272,128]{2,1,0:T(8,128)(2,1)S(1)}, bf16[3,272,128]{2,1,0:T(8,128)(2,1)S(1)}, u32[]{:S(2)}, u32[]{:S(2)}) collective-permute-start(bf16[3,272,128]{2,1,0:T(8,128)(2,1)S(1)} %get-tuple-element.77), channel_id=1, source_target_pairs={{0,2},{1,3},{2,0},{3,1},{4,6},{5,7},{6,4},{7,5},{8,10},{9,11},{10,... | collective-permute-start | bytes 626696 | tf_op jit(solution)/shard_map/ppermute | solution.py:500
  13.3 6.0 %collective-permute-start.5 = (bf16[17,32,256]{2,1,0:T(8,128)(2,1)S(1)}, bf16[17,32,256]{2,1,0:T(8,128)(2,1)S(1)}, u32[]{:S(2)}, u32[]{:S(2)}) collective-permute-start(bf16[17,32,256]{2,1,0:T(8,128)(2,1)S(1)} %collective-permute-done.2.chunk_ref.refs_0_), channel_id=1, source_target_pairs={{0,1},{1,0},{2,3},{3,2},{4,5},{5,4},{6,7},{7,6},{8,9},{9,8},{10,11... | collective-permute-start | bytes 835592 | tf_op jit(solution)/shard_map/ppermute | solution.py:497
  16.1 3.2 %collective-permute-start.8 = (bf16[16,16,256]{2,1,0:T(8,128)(2,1)S(1)}, bf16[16,16,256]{2,1,0:T(8,128)(2,1)S(1)}, u32[]{:S(2)}, u32[]{:S(2)}) collective-permute-start(bf16[16,16,256]{2,1,0:T(8,128)(2,1)S(1)} %collective-permute-done.6.refs_2_), channel_id=1, source_target_pairs={{0,1},{1,0},{2,3},{3,2},{4,5},{5,4},{6,7},{7,6},{8,9},{9,8},{10,11... | collective-permute-start | bytes 393224 | tf_op jit(solution)/shard_map/ppermute | solution.py:497
  16.1 11.5 %collective-permute-start.11 = (bf16[3,272,128]{2,1,0:T(8,128)(2,1)S(1)}, bf16[3,272,128]{2,1,0:T(8,128)(2,1)S(1)}, u32[]{:S(2)}, u32[]{:S(2)}) collective-permute-start(bf16[3,272,128]{2,1,0:T(8,128)(2,1)S(1)} %broadcast_select_fusion.packed_ref), channel_id=1, source_target_pairs={{0,2},{1,3},{2,0},{3,1},{4,6},{5,7},{6,4},{7,5},{8,10},{9,11},{10,... | collective-permute-start | bytes 626696 | tf_op jit(solution)/shard_map/ppermute | solution.py:500
  20.3 1.7 %collective-permute-start.9 = (bf16[16,16,256]{2,1,0:T(8,128)(2,1)S(1)}, bf16[16,16,256]{2,1,0:T(8,128)(2,1)S(1)}, u32[]{:S(2)}, u32[]{:S(2)}) collective-permute-start(bf16[16,16,256]{2,1,0:T(8,128)(2,1)S(1)} %collective-permute-done.1.refs_0_), channel_id=1, source_target_pairs={{0,1},{1,0},{2,3},{3,2},{4,5},{5,4},{6,7},{7,6},{8,9},{9,8},{10,11... | collective-permute-start | bytes 393224 | tf_op jit(solution)/shard_map/ppermute | solution.py:497
  26.7 2.2 %collective-permute-start.12 = (f32[8,256]{1,0:T(8,128)S(1)}, f32[8,256]{1,0:T(8,128)S(1)}, u32[]{:S(2)}, u32[]{:S(2)}) collective-permute-start(f32[8,256]{1,0:T(8,128)S(1)} %get-tuple-element.83.norm_ref), channel_id=1, source_target_pairs={{0,1},{1,0},{2,3},{3,2},{4,5},{5,4},{6,7},{7,6},{8,9},{9,8},{10,11... | collective-permute-start | bytes 24584 | tf_op jit(solution)/shard_map/ppermute | solution.py:497
  28.8 2.7 %collective-permute-start.13 = (bf16[8,256,256]{2,1,0:T(8,128)(2,1)S(1)}, bf16[8,256,256]{2,1,0:T(8,128)(2,1)S(1)}, u32[]{:S(2)}, u32[]{:S(2)}) collective-permute-start(bf16[8,256,256]{2,1,0:T(8,128)(2,1)S(1)} %get-tuple-element.88.low_ref.refs_0_), channel_id=1, source_target_pairs={{0,1},{1,0},{2,3},{3,2},{4,5},{5,4},{6,7},{7,6},{8,9},{9,8},{10,11... | collective-permute-start | bytes 3145736 | tf_op jit(solution)/shard_map/ppermute | solution.py:497
  29.9 4.5 %collective-permute-start.14 = (bf16[8,256,256]{2,1,0:T(8,128)(2,1)S(1)}, bf16[8,256,256]{2,1,0:T(8,128)(2,1)S(1)}, u32[]{:S(2)}, u32[]{:S(2)}) collective-permute-start(bf16[8,256,256]{2,1,0:T(8,128)(2,1)S(1)} %received_rights.3.high_ref.refs_2_), channel_id=1, source_target_pairs={{0,1},{1,0},{2,3},{3,2},{4,5},{5,4},{6,7},{7,6},{8,9},{9,8},{10,11... | collective-permute-start | bytes 3145736 | tf_op jit(solution)/shard_map/ppermute | solution.py:497
  34.4 8.3 %copy-start = (f32[1,64,16,256]{3,2,1,0:T(8,128)S(1)}, f32[1,64,16,256]{3,2,1,0:T(8,128)}, u32[]{:S(2)}) copy-start(f32[1,64,16,256]{3,2,1,0:T(8,128)} %param.5) | copy-start | bytes 3145732
  40.9 3.7 %collective-permute-start.15 = (f32[8,256]{1,0:T(8,128)S(1)}, f32[8,256]{1,0:T(8,128)S(1)}, u32[]{:S(2)}, u32[]{:S(2)}) collective-permute-start(f32[8,256]{1,0:T(8,128)S(1)} %residual_high.1.share_ref.refs_0_), channel_id=1, source_target_pairs={{0,2},{1,3},{2,0},{3,1},{4,6},{5,7},{6,4},{7,5},{8,10},{9,11},{10,... | collective-permute-start | bytes 24584 | tf_op jit(solution)/shard_map/ppermute | solution.py:510
  42.8 1.9 %collective-permute-start.16 = (f32[8,256]{1,0:T(8,128)S(1)}, f32[8,256]{1,0:T(8,128)S(1)}, u32[]{:S(2)}, u32[]{:S(2)}) collective-permute-start(f32[8,256]{1,0:T(8,128)S(1)} %residual_high.1.share_ref.refs_0_), channel_id=1, source_target_pairs={{0,1},{1,0},{2,3},{3,2},{4,5},{5,4},{6,7},{7,6},{8,9},{9,8},{10,11... | collective-permute-start | bytes 24584 | tf_op jit(solution)/shard_map/ppermute | solution.py:497
  44.7 1.2 %collective-permute-start.17 = (f32[8,256]{1,0:T(8,128)S(1)}, f32[8,256]{1,0:T(8,128)S(1)}, u32[]{:S(2)}, u32[]{:S(2)}) collective-permute-start(f32[8,256]{1,0:T(8,128)S(1)} %collective-permute-done.15.refs_2_), channel_id=1, source_target_pairs={{0,1},{1,0},{2,3},{3,2},{4,5},{5,4},{6,7},{7,6},{8,9},{9,8},{10,11... | collective-permute-start | bytes 24584 | tf_op jit(solution)/shard_map/ppermute | solution.py:497

commit v15 on v14

--- a/solution.py
+++ b/solution.py
@@ -272,7 +272,7 @@
         out_ref[p] = jnp.dot(columns_ref[...], stack, preferred_element_type=F32)
         return carry
 
-    lax.fori_loop(0, out_ref.shape[0], lefts, 0, unroll=UNROLL)
+    lax.fori_loop(0, out_ref.shape[0], lefts, 0, unroll=out_ref.shape[0])
 
 
 def rotate_kernel(spots, rows, chips, *refs):
@@ -309,7 +309,7 @@
             mixed_ref[p, :, k * width : (k + 1) * width] = mixed.astype(BF16)
         return carry
 
-    lax.fori_loop(0, states, lefts, 0, unroll=UNROLL)
+    lax.fori_loop(0, states, lefts, 0, unroll=states)
 
 
 def rights_kernel(start, stop, packed_ref, mixed_ref, before_ref, keep_ref, partial_ref, *refs):
@@ -353,7 +353,7 @@
             mixed_ref[k, n] = mixed[k * width : (k + 1) * width]
         return square, product
 
-    square, product = lax.fori_loop(0, count, lefts, (zero, zero), unroll=UNROLL)
+    square, product = lax.fori_loop(0, count, lefts, (zero, zero), unroll=count)
     return jnp.sum(square), jnp.sum(product)
 
 
@@ -419,13 +419,14 @@
         rotated_ref[:, :, at, :] = turned.reshape(terms, states, TILE, width)
         return carry
 
-    lax.fori_loop(0, width // TILE, sites, 0, unroll=UNROLL)
+    lax.fori_loop(0, width // TILE, sites, 0, unroll=width // TILE)
     cross = jnp.zeros((8, width), F32)
     for start, left_mixed_ref in ((0, mixed_low_ref), (half, mixed_ref)):
         for k in range(terms):
-            for n in range(half):
-                image = jnp.dot(rotated_ref[k, start + n], right_ref[k], preferred_element_type=F32)
-                cross = cross + fold(left_mixed_ref[k, n].astype(F32) * image, width)
+            turned = rotated_ref[k, start : start + half].reshape(half * width, width)
+            image = jnp.dot(turned, right_ref[k], preferred_element_type=F32)
+            held = left_mixed_ref[k].reshape(half * width, width).astype(F32)
+            cross = cross + fold(held * image, width)
     res_square = sums_ref[1:2, :] + square
     product = sums_ref[2:3, :] + product
     total = norm_ref[0:1, :] + norm_other_ref[0:1, :]

time: 47.5 us -> 44.5 us (0.937)
  Pallas kernels: 27.5 us -> 24.6 us
    pallas_call x1, Pallas kernels: 6.48 us -> 4.76 us  [shards(): pl.pallas_call(functools.partial(high_kernel, scale, members), out_shape=...]
    pallas_call x1, Pallas kernels: 2.92 us -> 1.72 us  [shards(): pl.pallas_call(low_kernel, out_shape=(half_bf, jax.ShapeDtypeStruct(half_...]
where the time goes in v15:
time: 44.5 us; the launch traced here: 44.3 us
  Pallas kernels  24.6 us (55%)
  starting transfers between devices  12.3 us (28%)
  waiting for transfers between devices  5.75 us (13%)
  between operations  1.66 us (4%)
    ppermute x5, starting transfers between devices, to_next_chip(): lax.ppermute(block, 'term', [(i, (i + CORES) % members) for i in range(me...  6.81 us
    pallas_call x1, Pallas kernels, shards(): pl.pallas_call(functools.partial(high_kernel, scale, members), out_shape=...  4.76 us
    pallas_call x1, Pallas kernels, shards(): pl.pallas_call(functools.partial(lefts_kernel, far_spots[-1], rows, chips...  2.59 us
    ppermute x11, waiting for transfers between devices, to_sibling(): return lax.ppermute(block, 'term', [(i, i ^ 1) for i in range(members)])  2.48 us
    pallas_call x2, Pallas kernels, rotate(): pl.pallas_call(functools.partial(rotate_kernel, spots, rows, chips), out_...  2.42 us
    ppermute x11, starting transfers between devices, to_sibling(): return lax.ppermute(block, 'term', [(i, i ^ 1) for i in range(members)])  2.36 us
    pallas_call x2, Pallas kernels, shards(): pl.pallas_call(functools.partial(rights_kernel, start, stop), out_shape=(...  2.25 us
    pallas_call x1, Pallas kernels, shards(): pl.pallas_call(functools.partial(last_kernel, len(last_pieces)), out_shap...  2.21 us
  transfers between devices with their start and end apart: 18, of which 7 were waited for; matrix products, arithmetic and copies ran while one was open for 0% of the time, Pallas kernels for 39%

profile of v15, /device:TPU:0, one launch (start us, length us, event | category | flops | bytes accessed | tf_op | source)
XLA Modules:
  0.0 44.3 jit_solution(17335803615011857793)
XLA Ops:
  1.3 1.4 %first_chunk.1 = (bf16[17,32,256]{2,1,0:T(8,128)(2,1)S(1)}, f32[8,256]{1,0:T(8,128)S(1)}, f32[8,256]{1,0:T(8,128)S(1)}, bf16[3,272,128]{2,1,0:T(8,128)(2,1)S(1)}) custom-call(s32[1,1]{1,0:T(1,128)} %bitcast.6.rank_in, f32[64,16,256]{2,1,0:T(8,128)} %bitcast.7, bf16[3,16,16]{2,1,0:T(8,128)(2,1)} %bitcast.12, bf16[3,256,256]{2,1,0:T(8,128)(2,1)} %bitcast.10), custom_call_target="tpu_custom_call" | custom-call | flops 5242 | bytes 7864 | tf_op jit(solution)/shard_map/first_chunk/pallas_call | solution.py:521
  2.7 0.5 %collective-permute-start = (bf16[17,32,256]{2,1,0:T(8,128)(2,1)S(1)}, bf16[17,32,256]{2,1,0:T(8,128)(2,1)S(1)}, u32[]{:S(2)}, u32[]{:S(2)}) collective-permute-start(bf16[17,32,256]{2,1,0:T(8,128)(2,1)S(1)} %get-tuple-element.53.chunk_ref.refs_0_), channel_id=1, source_target_pairs={{0,1},{1,0},{2,3},{3,2},{4,5},{5,4},{6,7},{7,6},{8,9},{9,8},{10,11... | collective-permute-start | bytes 835592 | tf_op jit(solution)/shard_map/ppermute | solution.py:498
  3.2 2.6 %collective-permute-start.2 = (bf16[17,32,256]{2,1,0:T(8,128)(2,1)S(1)}, bf16[17,32,256]{2,1,0:T(8,128)(2,1)S(1)}, u32[]{:S(2)}, u32[]{:S(2)}) collective-permute-start(bf16[17,32,256]{2,1,0:T(8,128)(2,1)S(1)} %get-tuple-element.53.chunk_ref.refs_0_), channel_id=1, source_target_pairs={{0,2},{1,3},{2,0},{3,1},{4,6},{5,7},{6,4},{7,5},{8,10},{9,11},{10,... | collective-permute-start | bytes 835592 | tf_op jit(solution)/shard_map/ppermute | solution.py:501
  5.8 1.3 %collective-permute-start.7 = (bf16[3,272,128]{2,1,0:T(8,128)(2,1)S(1)}, bf16[3,272,128]{2,1,0:T(8,128)(2,1)S(1)}, u32[]{:S(2)}, u32[]{:S(2)}) collective-permute-start(bf16[3,272,128]{2,1,0:T(8,128)(2,1)S(1)} %get-tuple-element.61), channel_id=1, source_target_pairs={{4,0},{8,4},{12,8},{16,12},{20,16},{24,20},{28,24},{5,1},{9,5},{13... | collective-permute-start | bytes 626696 | tf_op jit(solution)/shard_map/ppermute | solution.py:570
  7.1 0.0 collective-permute-done.refs_3_
  7.1 1.3 %prepare.1 = (f32[8,256]{1,0:T(8,128)S(1)}, bf16[3,272,128]{2,1,0:T(8,128)(2,1)S(1)}, bf16[3,256,256]{2,1,0:T(8,128)(2,1)S(1)}, bf16[16,16,256]{2,1,0:T(8,128)(2,1)S(1)}, bf16[16,16,256]{2,1,0:T(8,128)(2,1)S(1)}) custom-call(f32[8,256]{1,0:T(8,128)S(1)} %get-tuple-element.51.keep_ref, f32[8,256]{1,0:T(8,128)S(1)} %get-tuple-element.54.squares_ref, ...), custom_call_target="tpu_custom_call" | custom-call | flops 10485 | bytes 15728 | tf_op jit(solution)/shard_map/prepare/pallas_call | solution.py:539
  8.4 0.2 collective-permute-start.4
  8.6 0.3 collective-permute-start.3
  9.0 0.2 collective-permute-start.6
  9.2 0.4 spread_site.2.refs_6_.refs_5_.refs_3_.kron_ref
  9.6 0.3 collective-permute-done.4.refs_5_
  9.8 1.7 %collective-permute-start.1 = (bf16[16,16,256]{2,1,0:T(8,128)(2,1)S(1)}, bf16[16,16,256]{2,1,0:T(8,128)(2,1)S(1)}, u32[]{:S(2)}, u32[]{:S(2)}) collective-permute-start(bf16[16,16,256]{2,1,0:T(8,128)(2,1)S(1)} %get-tuple-element.55.refs_2_), channel_id=1, source_target_pairs={{0,2},{1,3},{2,0},{3,1},{4,6},{5,7},{6,4},{7,5},{8,10},{9,11},{10,... | collective-permute-start | bytes 393224 | tf_op jit(solution)/shard_map/ppermute | solution.py:501
  11.5 0.0 collective-permute-done.3.refs_4_
  11.5 0.4 collective-permute-start.10
  11.9 1.0 %rotate_own.1 = (bf16[3,16,128,256]{3,2,1,0:T(8,128)(2,1)S(1)}, bf16[256,768]{1,0:T(8,128)(2,1)S(1)}) custom-call(bf16[17,32,256]{2,1,0:T(8,128)(2,1)S(1)} %get-tuple-element.53.chunk_ref.refs_0_, bf16[16,16,256]{2,1,0:T(8,128)(2,1)S(1)} %get-tuple-element.56.refs_1_, bf16[16,16,256]{2,1,0:T(8,128)(2,1)S(1)} %get-tuple-element.55.refs_2_, ...), custom_call_target="tpu_custom_call" | custom-call | flops 16106127 | bytes 83886 | tf_op jit(solution)/shard_map/rotate_own/pallas_call | solution.py:602
  12.8 0.4 collective-permute-done.2.chunk_ref.refs_0_
  13.3 0.0 collective-permute-start.5
  13.3 0.4 spread_site.3.refs_6_.refs_4_.refs_2_
  13.7 1.4 %rotate_here.1 = (bf16[3,16,256,256]{3,2,1,0:T(8,128)(2,1)S(1)}, bf16[16,256,256]{2,1,0:T(8,128)(2,1)S(1)}) custom-call(bf16[17,32,256]{2,1,0:T(8,128)(2,1)S(1)} %get-tuple-element.53.chunk_ref.refs_0_, bf16[16,16,256]{2,1,0:T(8,128)(2,1)S(1)} %get-tuple-element.56.refs_1_, bf16[16,16,256]{2,1,0:T(8,128)(2,1)S(1)} %get-tuple-element.55.refs_2_, ...), custom_call_target="tpu_custom_call" | custom-call | flops 16106127 | bytes 83886 | tf_op jit(solution)/shard_map/rotate_here/pallas_call | solution.py:616
  15.0 0.0 collective-permute-done.7
  15.0 1.0 %collective-permute-done.6.refs_2_ = bf16[16,16,256]{2,1,0:T(8,128)(2,1)S(1)} collective-permute-done((bf16[16,16,256]{2,1,0:T(8,128)(2,1)S(1)}, bf16[16,16,256]{2,1,0:T(8,128)(2,1)S(1)}, u32[]{:S(2)}, u32[]{:S(2)}) %collective-permute-start.6) | collective-permute-done | bytes 131104 | tf_op jit(solution)/shard_map/ppermute | solution.py:501
  16.1 0.0 collective-permute-start.8
  16.1 2.0 %collective-permute-start.11 = (bf16[3,272,128]{2,1,0:T(8,128)(2,1)S(1)}, bf16[3,272,128]{2,1,0:T(8,128)(2,1)S(1)}, u32[]{:S(2)}, u32[]{:S(2)}) collective-permute-start(bf16[3,272,128]{2,1,0:T(8,128)(2,1)S(1)} %broadcast_select_fusion.packed_ref), channel_id=1, source_target_pairs={{0,2},{1,3},{2,0},{3,1},{4,6},{5,7},{6,4},{7,5},{8,10},{9,11},{10,... | collective-permute-start | bytes 626696 | tf_op jit(solution)/shard_map/ppermute | solution.py:501
  18.1 1.1 %apply_rows_here.1 = (bf16[16,384,256]{2,1,0:T(8,128)(2,1)S(1)}, bf16[3,256,256]{2,1,0:T(8,128)(2,1)S(1)}) custom-call(bf16[3,16,128,256]{3,2,1,0:T(8,128)(2,1)S(1)} %get-tuple-element.71.rotated_ref, bf16[3,272,128]{2,1,0:T(8,128)(2,1)S(1)} %broadcast_select_fusion.packed_ref, f32[8,256]{1,0:T(8,128)S(1)} %get-tuple-element.51.keep_ref), custom_call_target="tpu_custom_call" | custom-call | flops 16106127 | bytes 83886 | tf_op jit(solution)/shard_map/apply_rows_here/pallas_call | solution.py:637
  19.2 0.0 collective-permute-done.8.refs_3_
  19.2 0.0 collective-permute-done.5.refs_1_
  19.3 1.1 %rotate_crossed.1 = (bf16[3,16,256,256]{3,2,1,0:T(8,128)(2,1)S(1)}, bf16[16,256,256]{2,1,0:T(8,128)(2,1)S(1)}) custom-call(bf16[17,32,256]{2,1,0:T(8,128)(2,1)S(1)} %collective-permute-done.2.chunk_ref.refs_0_, bf16[17,32,256]{2,1,0:T(8,128)(2,1)S(1)} %collective-permute-done.5.refs_1_, ...), custom_call_target="tpu_custom_call", output_to_operand_aliasing={{0}: (5, {}), {1}: (6, {})} | custom-call | flops 16106127 | bytes 83886 | tf_op jit(solution)/shard_map/rotate_crossed/pallas_call | solution.py:616
  20.3 0.0 collective-permute-done.1.refs_0_
  20.3 0.3 collective-permute-start.9
  20.6 1.4 %apply_rows_crossed.1.refs_6_ = bf16[16,288,256]{2,1,0:T(8,128)(2,1)S(1)} custom-call(bf16[17,32,256]{2,1,0:T(8,128)(2,1)S(1)} %collective-permute-done.2.chunk_ref.refs_0_, bf16[17,32,256]{2,1,0:T(8,128)(2,1)S(1)} %collective-permute-done.5.refs_1_, bf16[16,16,256]{2,1,0:T(8,128)(2,1)S(1)} %collective-permute-done.6.refs_2_, ...), custom_call_target="tpu_custom_call" | custom-call | flops 16106127 | bytes 83886 | tf_op jit(solution)/shard_map/apply_rows_crossed/pallas_call | solution.py:658
  22.0 0.0 collective-permute-done.9.refs_1_
  22.0 2.2 %apply_rows_last.1.before_ref = f32[16,256,256]{2,1,0:T(8,128)S(1)} custom-call(bf16[16,16,256]{2,1,0:T(8,128)(2,1)S(1)} %collective-permute-done.1.refs_0_, bf16[16,16,256]{2,1,0:T(8,128)(2,1)S(1)} %collective-permute-done.9.refs_1_, bf16[3,256,256]{2,1,0:T(8,128)(2,1)S(1)} %get-tuple-element.78.refs_4_.refs_2_.right_ref, ...), custom_call_target="tpu_custom_call" | custom-call | flops 16106127 | bytes 83886 | tf_op jit(solution)/shard_map/apply_rows_last/pallas_call | solution.py:672
  24.3 0.0 collective-permute-done.10.refs_5_
  24.3 2.6 %received_lefts.1 = (bf16[16,256,768]{2,1,0:T(8,128)(2,1)S(1)}, f32[8,256]{1,0:T(8,128)S(1)}, bf16[3,16,256,256]{3,2,1,0:T(8,128)(2,1)S(1)}, bf16[16,256,256]{2,1,0:T(8,128)(2,1)S(1)}) custom-call(bf16[16,16,256]{2,1,0:T(8,128)(2,1)S(1)} %collective-permute-done.1.refs_0_, ...), custom_call_target="tpu_custom_call", output_to_operand_aliasing={{2}: (3, {}), {3}: (4, {})} | custom-call | flops 16106127 | bytes 125829 | tf_op jit(solution)/shard_map/received_lefts/pallas_call | solution.py:691
  26.9 0.3 collective-permute-start.12
  27.2 0.4 collective-permute-done.11.packed_ref
  27.6 1.2 %received_rights.2 = (bf16[8,256,256]{2,1,0:T(8,128)(2,1)S(1)}, bf16[3,256,256]{2,1,0:T(8,128)(2,1)S(1)}) custom-call(bf16[3,272,128]{2,1,0:T(8,128)(2,1)S(1)} %collective-permute-done.11.packed_ref, bf16[16,256,768]{2,1,0:T(8,128)(2,1)S(1)} %get-tuple-element.84.mixed_ref, f32[16,256,256]{2,1,0:T(8,128)S(1)} %apply_rows_last.1.before_ref, ...), custom_call_target="tpu_custom_call" | custom-call | flops 8053063 | bytes 125829 | tf_op jit(solution)/shard_map/received_rights/pallas_call | solution.py:708
  28.8 0.1 collective-permute-start.13
  28.9 0.0 collective-permute-done.12.norm_other_ref
  28.9 1.1 %received_rights.3.high_ref.refs_2_ = bf16[8,256,256]{2,1,0:T(8,128)(2,1)S(1)} custom-call(bf16[3,256,256]{2,1,0:T(8,128)(2,1)S(1)} %get-tuple-element.91.packed_ref, bf16[16,256,768]{2,1,0:T(8,128)(2,1)S(1)} %get-tuple-element.84.mixed_ref, f32[16,256,256]{2,1,0:T(8,128)S(1)} %apply_rows_last.1.before_ref, f32[8,256]{1,0:T(8,128)S(1)} %get-tuple-element.51.keep_ref), custom_call_target="tpu_custom_call" | custom-call | flops 8053063 | bytes 125829 | tf_op jit(solution)/shard_map/received_rights/pallas_call | solution.py:708
  29.9 0.6 %collective-permute-start.14 = (bf16[8,256,256]{2,1,0:T(8,128)(2,1)S(1)}, bf16[8,256,256]{2,1,0:T(8,128)(2,1)S(1)}, u32[]{:S(2)}, u32[]{:S(2)}) collective-permute-start(bf16[8,256,256]{2,1,0:T(8,128)(2,1)S(1)} %received_rights.3.high_ref.refs_2_), channel_id=1, source_target_pairs={{0,1},{1,0},{2,3},{3,2},{4,5},{5,4},{6,7},{7,6},{8,9},{9,8},{10,11... | collective-permute-start | bytes 3145736 | tf_op jit(solution)/shard_map/ppermute | solution.py:498
  30.5 1.0 %collective-permute-done.13.low_other_ref.refs_1_ = bf16[8,256,256]{2,1,0:T(8,128)(2,1)S(1)} collective-permute-done((bf16[8,256,256]{2,1,0:T(8,128)(2,1)S(1)}, bf16[8,256,256]{2,1,0:T(8,128)(2,1)S(1)}, u32[]{:S(2)}, u32[]{:S(2)}) %collective-permute-start.13) | collective-permute-done | bytes 1048608 | tf_op jit(solution)/shard_map/ppermute | solution.py:498
  31.5 1.7 %residual_low.1 = (bf16[8,256,256]{2,1,0:T(8,128)(2,1)S(1)}, bf16[3,8,256,256]{3,2,1,0:T(8,128)(2,1)S(1)}, f32[8,256]{1,0:T(8,128)S(1)}) custom-call(f32[8,256]{1,0:T(8,128)S(1)} %get-tuple-element.83.norm_ref, f32[8,256]{1,0:T(8,128)S(1)} %collective-permute-done.12.norm_other_ref, bf16[8,256,256]{2,1,0:T(8,128)(2,1)S(1)} %get-tuple-element.88.low_ref.refs_0_, ...), custom_call_target="tpu_custom_call" | custom-call | flops 8053063 | bytes 31457 | tf_op jit(solution)/shard_map/residual_low/pallas_call | solution.py:727
  33.2 0.0 collective-permute-done.14.high_other_ref.refs_3_
  33.3 0.0 copy-start
  33.3 4.8 %residual_high.1.share_ref.refs_0_ = f32[8,256]{1,0:T(8,128)S(1)} custom-call(f32[8,256]{1,0:T(8,128)S(1)} %get-tuple-element.83.norm_ref, f32[8,256]{1,0:T(8,128)S(1)} %collective-permute-done.12.norm_other_ref, f32[8,256]{1,0:T(8,128)S(1)} %get-tuple-element.90.sums_ref, bf16[8,256,256]{2,1,0:T(8,128)(2,1)S(1)} %received_rights.3.high_ref.refs_2_, ...), custom_call_target="tpu_custom_call" | custom-call | flops 48318384 | bytes 62914 | tf_op jit(solution)/shard_map/residual_high/pallas_call | solution.py:736
  38.0 1.8 %collective-permute-start.15 = (f32[8,256]{1,0:T(8,128)S(1)}, f32[8,256]{1,0:T(8,128)S(1)}, u32[]{:S(2)}, u32[]{:S(2)}) collective-permute-start(f32[8,256]{1,0:T(8,128)S(1)} %residual_high.1.share_ref.refs_0_), channel_id=1, source_target_pairs={{0,2},{1,3},{2,0},{3,1},{4,6},{5,7},{6,4},{7,5},{8,10},{9,11},{10,... | collective-permute-start | bytes 24584 | tf_op jit(solution)/shard_map/ppermute | solution.py:511
  39.9 0.0 collective-permute-start.16
  39.9 0.0 copy-done
  39.9 0.5 %own_rows.1 = (f32[64,16,256]{2,1,0:T(8,128)S(1)}, f32[64,16,256]{2,1,0:T(8,128)S(1)}) custom-call(f32[8,256]{1,0:T(8,128)S(1)} %get-tuple-element.51.keep_ref, f32[8,256]{1,0:T(8,128)S(1)} %get-tuple-element.83.norm_ref, f32[8,256]{1,0:T(8,128)S(1)} %collective-permute-done.12.norm_other_ref, f32[8,256]{1,0:T(8,128)S(1)} %residual_high.1.share_ref.refs_0_, ...), custom_call_target="tpu_custom_call" | custom-call | flops 20971 | bytes 41943 | tf_op jit(solution)/shard_map/own_rows/pallas_call | solution.py:753
  40.3 1.4 %collective-permute-done.15.refs_2_ = f32[8,256]{1,0:T(8,128)S(1)} collective-permute-done((f32[8,256]{1,0:T(8,128)S(1)}, f32[8,256]{1,0:T(8,128)S(1)}, u32[]{:S(2)}, u32[]{:S(2)}) %collective-permute-start.15) | collective-permute-done | bytes 8224 | tf_op jit(solution)/shard_map/ppermute | solution.py:511
  41.7 0.0 collective-permute-start.17
  41.8 0.0 collective-permute-done.16.refs_1_
  41.8 1.2 %collective-permute-done.17.refs_3_ = f32[8,256]{1,0:T(8,128)S(1)} collective-permute-done((f32[8,256]{1,0:T(8,128)S(1)}, f32[8,256]{1,0:T(8,128)S(1)}, u32[]{:S(2)}, u32[]{:S(2)}) %collective-permute-start.17) | collective-permute-done | bytes 8224 | tf_op jit(solution)/shard_map/ppermute | solution.py:498
  42.9 1.3 %finish.1 = (f32[64,16,256]{2,1,0:T(8,128)}, f32[1]{0:T(128)}) custom-call(f32[64,16,256]{2,1,0:T(8,128)S(1)} %get-tuple-element.94.vector_ref, f32[64,16,256]{2,1,0:T(8,128)S(1)} %get-tuple-element.96.residual_ref, f32[8,256]{1,0:T(8,128)S(1)} %residual_high.1.share_ref.refs_0_, f32[8,256]{1,0:T(8,128)S(1)} %collective-permute-done.16.refs_1_, ...), custom_call_target="tpu_custom_call" | custom-call | flops 7864 | bytes 31457 | tf_op jit(solution)/shard_map/finish/pallas_call | solution.py:766
  (1 shorter events, 0.0 us)
Async XLA Ops:
  2.7 4.4 %collective-permute-start = (bf16[17,32,256]{2,1,0:T(8,128)(2,1)S(1)}, bf16[17,32,256]{2,1,0:T(8,128)(2,1)S(1)}, u32[]{:S(2)}, u32[]{:S(2)}) collective-permute-start(bf16[17,32,256]{2,1,0:T(8,128)(2,1)S(1)} %get-tuple-element.53.chunk_ref.refs_0_), channel_id=1, source_target_pairs={{0,1},{1,0},{2,3},{3,2},{4,5},{5,4},{6,7},{7,6},{8,9},{9,8},{10,11... | collective-permute-start | bytes 835592 | tf_op jit(solution)/shard_map/ppermute | solution.py:498
  3.2 10.1 %collective-permute-start.2 = (bf16[17,32,256]{2,1,0:T(8,128)(2,1)S(1)}, bf16[17,32,256]{2,1,0:T(8,128)(2,1)S(1)}, u32[]{:S(2)}, u32[]{:S(2)}) collective-permute-start(bf16[17,32,256]{2,1,0:T(8,128)(2,1)S(1)} %get-tuple-element.53.chunk_ref.refs_0_), channel_id=1, source_target_pairs={{0,2},{1,3},{2,0},{3,1},{4,6},{5,7},{6,4},{7,5},{8,10},{9,11},{10,... | collective-permute-start | bytes 835592 | tf_op jit(solution)/shard_map/ppermute | solution.py:501
  5.8 9.3 %collective-permute-start.7 = (bf16[3,272,128]{2,1,0:T(8,128)(2,1)S(1)}, bf16[3,272,128]{2,1,0:T(8,128)(2,1)S(1)}, u32[]{:S(2)}, u32[]{:S(2)}) collective-permute-start(bf16[3,272,128]{2,1,0:T(8,128)(2,1)S(1)} %get-tuple-element.61), channel_id=1, source_target_pairs={{4,0},{8,4},{12,8},{16,12},{20,16},{24,20},{28,24},{5,1},{9,5},{13... | collective-permute-start | bytes 626696 | tf_op jit(solution)/shard_map/ppermute | solution.py:570
  8.4 1.4 %collective-permute-start.4 = (bf16[16,16,256]{2,1,0:T(8,128)(2,1)S(1)}, bf16[16,16,256]{2,1,0:T(8,128)(2,1)S(1)}, u32[]{:S(2)}, u32[]{:S(2)}) collective-permute-start(bf16[16,16,256]{2,1,0:T(8,128)(2,1)S(1)} %get-tuple-element.55.refs_2_), channel_id=1, source_target_pairs={{0,1},{1,0},{2,3},{3,2},{4,5},{5,4},{6,7},{7,6},{8,9},{9,8},{10,11... | collective-permute-start | bytes 393224 | tf_op jit(solution)/shard_map/ppermute | solution.py:498
  8.6 2.8 %collective-permute-start.3 = (bf16[16,16,256]{2,1,0:T(8,128)(2,1)S(1)}, bf16[16,16,256]{2,1,0:T(8,128)(2,1)S(1)}, u32[]{:S(2)}, u32[]{:S(2)}) collective-permute-start(bf16[16,16,256]{2,1,0:T(8,128)(2,1)S(1)} %get-tuple-element.56.refs_1_), channel_id=1, source_target_pairs={{0,1},{1,0},{2,3},{3,2},{4,5},{5,4},{6,7},{7,6},{8,9},{9,8},{10,11... | collective-permute-start | bytes 393224 | tf_op jit(solution)/shard_map/ppermute | solution.py:498
  9.0 7.1 %collective-permute-start.6 = (bf16[16,16,256]{2,1,0:T(8,128)(2,1)S(1)}, bf16[16,16,256]{2,1,0:T(8,128)(2,1)S(1)}, u32[]{:S(2)}, u32[]{:S(2)}) collective-permute-start(bf16[16,16,256]{2,1,0:T(8,128)(2,1)S(1)} %get-tuple-element.56.refs_1_), channel_id=1, source_target_pairs={{0,2},{1,3},{2,0},{3,1},{4,6},{5,7},{6,4},{7,5},{8,10},{9,11},{10,... | collective-permute-start | bytes 393224 | tf_op jit(solution)/shard_map/ppermute | solution.py:501
  9.8 10.5 %collective-permute-start.1 = (bf16[16,16,256]{2,1,0:T(8,128)(2,1)S(1)}, bf16[16,16,256]{2,1,0:T(8,128)(2,1)S(1)}, u32[]{:S(2)}, u32[]{:S(2)}) collective-permute-start(bf16[16,16,256]{2,1,0:T(8,128)(2,1)S(1)} %get-tuple-element.55.refs_2_), channel_id=1, source_target_pairs={{0,2},{1,3},{2,0},{3,1},{4,6},{5,7},{6,4},{7,5},{8,10},{9,11},{10,... | collective-permute-start | bytes 393224 | tf_op jit(solution)/shard_map/ppermute | solution.py:501
  11.5 12.8 %collective-permute-start.10 = (bf16[3,272,128]{2,1,0:T(8,128)(2,1)S(1)}, bf16[3,272,128]{2,1,0:T(8,128)(2,1)S(1)}, u32[]{:S(2)}, u32[]{:S(2)}) collective-permute-start(bf16[3,272,128]{2,1,0:T(8,128)(2,1)S(1)} %get-tuple-element.77), channel_id=1, source_target_pairs={{0,2},{1,3},{2,0},{3,1},{4,6},{5,7},{6,4},{7,5},{8,10},{9,11},{10,... | collective-permute-start | bytes 626696 | tf_op jit(solution)/shard_map/ppermute | solution.py:501
  13.3 6.0 %collective-permute-start.5 = (bf16[17,32,256]{2,1,0:T(8,128)(2,1)S(1)}, bf16[17,32,256]{2,1,0:T(8,128)(2,1)S(1)}, u32[]{:S(2)}, u32[]{:S(2)}) collective-permute-start(bf16[17,32,256]{2,1,0:T(8,128)(2,1)S(1)} %collective-permute-done.2.chunk_ref.refs_0_), channel_id=1, source_target_pairs={{0,1},{1,0},{2,3},{3,2},{4,5},{5,4},{6,7},{7,6},{8,9},{9,8},{10,11... | collective-permute-start | bytes 835592 | tf_op jit(solution)/shard_map/ppermute | solution.py:498
  16.1 3.2 %collective-permute-start.8 = (bf16[16,16,256]{2,1,0:T(8,128)(2,1)S(1)}, bf16[16,16,256]{2,1,0:T(8,128)(2,1)S(1)}, u32[]{:S(2)}, u32[]{:S(2)}) collective-permute-start(bf16[16,16,256]{2,1,0:T(8,128)(2,1)S(1)} %collective-permute-done.6.refs_2_), channel_id=1, source_target_pairs={{0,1},{1,0},{2,3},{3,2},{4,5},{5,4},{6,7},{7,6},{8,9},{9,8},{10,11... | collective-permute-start | bytes 393224 | tf_op jit(solution)/shard_map/ppermute | solution.py:498
  16.1 11.5 %collective-permute-start.11 = (bf16[3,272,128]{2,1,0:T(8,128)(2,1)S(1)}, bf16[3,272,128]{2,1,0:T(8,128)(2,1)S(1)}, u32[]{:S(2)}, u32[]{:S(2)}) collective-permute-start(bf16[3,272,128]{2,1,0:T(8,128)(2,1)S(1)} %broadcast_select_fusion.packed_ref), channel_id=1, source_target_pairs={{0,2},{1,3},{2,0},{3,1},{4,6},{5,7},{6,4},{7,5},{8,10},{9,11},{10,... | collective-permute-start | bytes 626696 | tf_op jit(solution)/shard_map/ppermute | solution.py:501
  20.3 1.7 %collective-permute-start.9 = (bf16[16,16,256]{2,1,0:T(8,128)(2,1)S(1)}, bf16[16,16,256]{2,1,0:T(8,128)(2,1)S(1)}, u32[]{:S(2)}, u32[]{:S(2)}) collective-permute-start(bf16[16,16,256]{2,1,0:T(8,128)(2,1)S(1)} %collective-permute-done.1.refs_0_), channel_id=1, source_target_pairs={{0,1},{1,0},{2,3},{3,2},{4,5},{5,4},{6,7},{7,6},{8,9},{9,8},{10,11... | collective-permute-start | bytes 393224 | tf_op jit(solution)/shard_map/ppermute | solution.py:498
  26.9 2.0 %collective-permute-start.12 = (f32[8,256]{1,0:T(8,128)S(1)}, f32[8,256]{1,0:T(8,128)S(1)}, u32[]{:S(2)}, u32[]{:S(2)}) collective-permute-start(f32[8,256]{1,0:T(8,128)S(1)} %get-tuple-element.83.norm_ref), channel_id=1, source_target_pairs={{0,1},{1,0},{2,3},{3,2},{4,5},{5,4},{6,7},{7,6},{8,9},{9,8},{10,11... | collective-permute-start | bytes 24584 | tf_op jit(solution)/shard_map/ppermute | solution.py:498
  28.8 2.7 %collective-permute-start.13 = (bf16[8,256,256]{2,1,0:T(8,128)(2,1)S(1)}, bf16[8,256,256]{2,1,0:T(8,128)(2,1)S(1)}, u32[]{:S(2)}, u32[]{:S(2)}) collective-permute-start(bf16[8,256,256]{2,1,0:T(8,128)(2,1)S(1)} %get-tuple-element.88.low_ref.refs_0_), channel_id=1, source_target_pairs={{0,1},{1,0},{2,3},{3,2},{4,5},{5,4},{6,7},{7,6},{8,9},{9,8},{10,11... | collective-permute-start | bytes 3145736 | tf_op jit(solution)/shard_map/ppermute | solution.py:498
  29.9 3.3 %collective-permute-start.14 = (bf16[8,256,256]{2,1,0:T(8,128)(2,1)S(1)}, bf16[8,256,256]{2,1,0:T(8,128)(2,1)S(1)}, u32[]{:S(2)}, u32[]{:S(2)}) collective-permute-start(bf16[8,256,256]{2,1,0:T(8,128)(2,1)S(1)} %received_rights.3.high_ref.refs_2_), channel_id=1, source_target_pairs={{0,1},{1,0},{2,3},{3,2},{4,5},{5,4},{6,7},{7,6},{8,9},{9,8},{10,11... | collective-permute-start | bytes 3145736 | tf_op jit(solution)/shard_map/ppermute | solution.py:498
  33.3 6.6 %copy-start = (f32[1,64,16,256]{3,2,1,0:T(8,128)S(1)}, f32[1,64,16,256]{3,2,1,0:T(8,128)}, u32[]{:S(2)}) copy-start(f32[1,64,16,256]{3,2,1,0:T(8,128)} %param.5) | copy-start | bytes 3145732
  38.0 3.7 %collective-permute-start.15 = (f32[8,256]{1,0:T(8,128)S(1)}, f32[8,256]{1,0:T(8,128)S(1)}, u32[]{:S(2)}, u32[]{:S(2)}) collective-permute-start(f32[8,256]{1,0:T(8,128)S(1)} %residual_high.1.share_ref.refs_0_), channel_id=1, source_target_pairs={{0,2},{1,3},{2,0},{3,1},{4,6},{5,7},{6,4},{7,5},{8,10},{9,11},{10,... | collective-permute-start | bytes 24584 | tf_op jit(solution)/shard_map/ppermute | solution.py:511
  39.9 1.9 %collective-permute-start.16 = (f32[8,256]{1,0:T(8,128)S(1)}, f32[8,256]{1,0:T(8,128)S(1)}, u32[]{:S(2)}, u32[]{:S(2)}) collective-permute-start(f32[8,256]{1,0:T(8,128)S(1)} %residual_high.1.share_ref.refs_0_), channel_id=1, source_target_pairs={{0,1},{1,0},{2,3},{3,2},{4,5},{5,4},{6,7},{7,6},{8,9},{9,8},{10,11... | collective-permute-start | bytes 24584 | tf_op jit(solution)/shard_map/ppermute | solution.py:498
  41.7 1.2 %collective-permute-start.17 = (f32[8,256]{1,0:T(8,128)S(1)}, f32[8,256]{1,0:T(8,128)S(1)}, u32[]{:S(2)}, u32[]{:S(2)}) collective-permute-start(f32[8,256]{1,0:T(8,128)S(1)} %collective-permute-done.15.refs_2_), channel_id=1, source_target_pairs={{0,1},{1,0},{2,3},{3,2},{4,5},{5,4},{6,7},{7,6},{8,9},{9,8},{10,11... | collective-permute-start | bytes 24584 | tf_op jit(solution)/shard_map/ppermute | solution.py:498

commit v16 on v15

--- a/solution.py
+++ b/solution.py
@@ -10,7 +10,6 @@
 epsilon = 1e-06
 CORES = 2
 TILE = 16
-UNROLL = 16
 STRIP = 32
 GROUP = 8
 VMEM_LIMIT = 20 * 1024 * 1024
@@ -61,6 +60,7 @@
 ):
     rows, states, width = guess_ref.shape
     terms = site_ref.shape[0]
+    blocks = rows // TILE
     copies = [
         pltpu.make_async_copy(source, target, sems.at[n])
         for n, (source, target) in enumerate(((rank_in, rank_ref), (site_in, site_ref), (right_in, right_ref)))
@@ -76,10 +76,9 @@
     squares = jnp.zeros((8, width), F32)
     for n, copy in enumerate(parts):
         copy.wait()
-        part = pl.ds(n * TILE, TILE)
-        masked = guess_ref[part] * keep[None]
+        masked = guess_ref[pl.ds(n * TILE, TILE)] * keep[None]
         squares = squares + fold(masked * masked, width)
-        x_ref[0:states, part, :] = jnp.swapaxes(masked, 0, 1).astype(BF16)
+        x_ref[n * states : (n + 1) * states] = jnp.swapaxes(masked, 0, 1).astype(BF16)
     squares_ref[...] = squares
     copies[1].wait()
     line = lax.broadcasted_iota(jnp.int32, (TILE, width), 0)
@@ -88,7 +87,7 @@
     for k in range(terms):
         place_at = (lane == line + k * TILE).astype(BF16)
         extra = extra + jnp.dot(site_ref[k], place_at, preferred_element_type=F32)
-    x_ref[states, 0:TILE, :] = extra.astype(BF16)
+    x_ref[blocks * states] = extra.astype(BF16)
     copies[2].wait()
     pack_blocks(right_ref, None, packed_ref)
 
@@ -110,16 +109,17 @@
         squares = squares + fold(masked * masked, width)
         chunk = max(c for c, start in enumerate(starts) if start <= done + n * TILE)
         at = done + n * TILE - starts[chunk]
-        x_refs[chunk][:, at : at + TILE, :] = jnp.swapaxes(masked, 0, 1).astype(BF16)
+        block = at // TILE
+        x_refs[chunk][block * states : (block + 1) * states] = jnp.swapaxes(masked, 0, 1).astype(BF16)
     total = jnp.sum(squares)
     norm_ref[...] = jnp.full(norm_ref.shape, total, F32)
     line = lax.broadcasted_iota(jnp.int32, (TILE, half), 0)
     norm = jnp.full((TILE, half), total, F32)
     extra = jnp.zeros((TILE, half), F32)
-    for n in range(1, 4):
+    for n in range(3):
         part = norm.astype(BF16).astype(F32)
         norm = norm - part
-        extra = jnp.where(line == n, part, extra)
+        extra = jnp.where(line == left_ref.shape[0] + n, part, extra)
     left_copy.wait()
     pack_blocks(left_ref, extra, packed_ref)
 
@@ -128,10 +128,17 @@
     terms, width, _ = block_ref.shape
     half = width // 2
     line = lax.broadcasted_iota(jnp.int32, (TILE, half), 0)
+    row, col = triangle(half)
+    lines = jnp.zeros((TILE, half), F32) if extra is None else extra
     for k in range(terms):
-        diagonal = pack_symmetric(block_ref, k, packed_ref)
-        lines = jnp.broadcast_to(diagonal, (TILE, half)) if extra is None else jnp.where(line == 0, diagonal, extra)
-        packed_ref[k, width : width + TILE, :] = lines.astype(BF16)
+        upper = block_ref[k, 0:half, 0:half].astype(F32)
+        lower = block_ref[k, half:width, half:width].astype(F32)
+        diagonal = jnp.sum(jnp.where(row == col, lower, 0.0), axis=0, keepdims=True)
+        lines = jnp.where(line == k, diagonal, lines)
+        base = k * width
+        packed_ref[base : base + half, :] = block_ref[k, 0:half, half:width]
+        packed_ref[base + half : base + width, :] = jnp.where(row <= col, upper, lower).astype(BF16)
+    packed_ref[terms * width : terms * width + TILE, :] = lines.astype(BF16)
 
 
 def triangle(half):
@@ -140,17 +147,6 @@
     return row, col
 
 
-def pack_symmetric(block_ref, k, out_ref):
-    width = block_ref.shape[1]
-    half = width // 2
-    row, col = triangle(half)
-    upper = block_ref[k, 0:half, 0:half].astype(F32)
-    lower = block_ref[k, half:width, half:width].astype(F32)
-    out_ref[k, 0:half, :] = block_ref[k, 0:half, half:width]
-    out_ref[k, half:width, :] = jnp.where(row <= col, upper, lower).astype(BF16)
-    return jnp.sum(jnp.where(row == col, lower, 0.0), axis=0, keepdims=True)
-
-
 def unpack_symmetric(packed_ref, full_ref, keep=None):
     terms, width, _ = full_ref.shape
     half = width // 2
@@ -159,10 +155,12 @@
     def kept(block, start):
         return block if keep is None else block * keep[:, start : start + half]
 
+    diagonals = packed_ref[terms * width : terms * width + TILE, :].astype(F32)
     for k in range(terms):
-        corner = packed_ref[k, 0:half, :].astype(F32)
-        mixed = packed_ref[k, half:width, :].astype(F32)
-        diagonal = packed_ref[k, width : width + TILE, :].astype(F32)[0:1]
+        base = k * width
+        corner = packed_ref[base : base + half, :].astype(F32)
+        mixed = packed_ref[base + half : base + width, :].astype(F32)
+        diagonal = diagonals[k : k + 1]
         turned = mixed.T
         lower = jnp.where(row > col, mixed, jnp.where(row == col, diagonal, turned))
         full_ref[k, 0:half, 0:half] = kept(jnp.where(row <= col, mixed, turned), 0).astype(BF16)
@@ -176,7 +174,7 @@
     size = kron_ref.shape[1]
     terms = kron_ref.shape[0] // size
     states = size // TILE
-    tile = chunk_ref[states, 0:TILE, :]
+    tile = chunk_ref[chunk_ref.shape[0] - 1]
     row_state = lax.broadcasted_iota(jnp.int32, (size, states), 0) // TILE
     pick = (row_state == lax.broadcasted_iota(jnp.int32, (size, states), 1)).astype(BF16)
     tall = jnp.dot(pick, tile, preferred_element_type=F32).astype(BF16)
@@ -192,19 +190,13 @@
         kron_ref[k * size : (k + 1) * size, :] = jnp.where(same, full, 0.0).astype(BF16)
 
 
-def mix_sites(source_ref, kron_ref, rotated_ref, base, unroll):
+def mix_sites(source_ref, kron_ref, rotated_ref, base):
     terms, states, _, width = rotated_ref.shape
-    rows = source_ref.shape[1]
-
-    def step(i, carry):
-        at = pl.multiple_of(i * TILE, TILE)
-        to = pl.multiple_of(base + i * TILE, TILE)
-        stack = source_ref[0:states, pl.ds(at, TILE), :].reshape(states * TILE, width)
+    for i in range(source_ref.shape[0] // states):
+        to = pl.ds(pl.multiple_of(base + i * TILE, TILE), TILE)
+        stack = source_ref[i * states : (i + 1) * states].reshape(states * TILE, width)
         turned = jnp.dot(kron_ref[...], stack, preferred_element_type=F32).astype(BF16)
-        rotated_ref[:, :, pl.ds(to, TILE), :] = turned.reshape(terms, states, TILE, width)
-        return carry
-
-    lax.fori_loop(0, rows // TILE, step, 0, unroll=min(unroll, rows // TILE))
+        rotated_ref[:, :, to, :] = turned.reshape(terms, states, TILE, width)
 
 
 def summed(values):
@@ -227,8 +219,8 @@
 def mix_pieces(pieces, kron_ref, rotated_ref):
     at = 0
     for piece in pieces:
-        mix_sites(piece, kron_ref, rotated_ref, at, UNROLL)
-        at += piece.shape[1]
+        mix_sites(piece, kron_ref, rotated_ref, at)
+        at += piece.shape[0] // rotated_ref.shape[1] * TILE
 
 
 def rotate_own_kernel(groups, rows, chips, *refs):
@@ -282,12 +274,14 @@
     states = whole_ref.shape[0]
     copies = []
     bases = [row_of(spot, rows, chips) for spot in spots]
-    for n, (at, piece) in enumerate(zip(bases, pieces)):
-        target = whole_ref.at[:, pl.ds(at, piece.shape[1]), :]
-        copies.append(pltpu.make_async_copy(piece.at[0:states], target, sems.at[n]))
-        copies[-1].start()
     for at, piece in zip(bases, pieces):
-        mix_sites(piece, kron_ref, rotated_ref, at, UNROLL)
+        for i in range(piece.shape[0] // states):
+            target = whole_ref.at[:, pl.ds(pl.multiple_of(at + i * TILE, TILE), TILE), :]
+            source = piece.at[i * states : (i + 1) * states]
+            copies.append(pltpu.make_async_copy(source, target, sems.at[len(copies)]))
+            copies[-1].start()
+    for at, piece in zip(bases, pieces):
+        mix_sites(piece, kron_ref, rotated_ref, at)
     for copy in copies:
         copy.wait()
 
@@ -297,8 +291,8 @@
     packed_ref, norm_before_ref = refs[count + 3 : count + 5]
     mixed_ref, norm_ref, rotated_ref, whole_ref, left_ref, sems = refs[-6:]
     terms, states, width, _ = rotated_ref.shape
-    lines = packed_ref[0, width : width + TILE, :].astype(F32)
-    norm = lines[1:2] + lines[2:3] + lines[3:4]
+    lines = packed_ref[terms * width : terms * width + TILE, :].astype(F32)
+    norm = lines[terms : terms + 1] + lines[terms + 1 : terms + 2] + lines[terms + 2 : terms + 3]
     norm_ref[...] = norm_before_ref[...] + jnp.concatenate([norm, norm], axis=1)
     unpack_symmetric(packed_ref, left_ref)
     rotate_kernel(spots, rows, chips, *refs[: count + 1], rotated_ref, whole_ref, sems)
@@ -514,13 +508,13 @@
 
     tile = jax.ShapeDtypeStruct((8, width), F32)
     half = width // 2
-    packed_shape = jax.ShapeDtypeStruct((terms, width + TILE, half), BF16)
+    packed_shape = jax.ShapeDtypeStruct((terms * width + TILE, half), BF16)
     starts = (0, rows - 2 * TILE, rows - TILE) if rows >= 4 * TILE else (0,)
     lengths = [stop - start for start, stop in zip(starts, starts[1:] + (rows,))]
     in_place = [pltpu.with_memory_space_constraint(a, pltpu.HBM) for a in (guess, left, right_env[0], site)]
     first_chunk, keep, squares, right_packed = pl.pallas_call(
         first_chunk_kernel,
-        out_shape=(jax.ShapeDtypeStruct((states + 1, lengths[0], width), BF16), tile, tile, packed_shape),
+        out_shape=(jax.ShapeDtypeStruct((lengths[0] // TILE * states + 1, TILE, width), BF16), tile, tile, packed_shape),
         in_specs=[anywhere] + [in_hbm] * 3,
         out_specs=(vmem,) * 4,
         scratch_shapes=[
@@ -542,7 +536,7 @@
             tile,
             packed_shape,
             jax.ShapeDtypeStruct(left.shape, BF16),
-            *[jax.ShapeDtypeStruct((states, length, width), BF16) for length in lengths[1:]],
+            *[jax.ShapeDtypeStruct((length // TILE * states, TILE, width), BF16) for length in lengths[1:]],
         ),
         in_specs=[vmem] * 2 + [in_hbm] * 2,
         out_specs=(vmem,) * (2 + len(lengths)),
@@ -618,7 +612,7 @@
             out_shape=(rotated_bf, whole_bf),
             in_specs=[vmem] * (len(pieces) + 1) + [anywhere] * len(before),
             out_specs=(vmem, vmem),
-            scratch_shapes=[pltpu.SemaphoreType.DMA((len(pieces),))],
+            scratch_shapes=[pltpu.SemaphoreType.DMA((sum(spot[3] for spot in spots) // TILE,))],
             input_output_aliases={len(pieces) + 1 + n: n for n in range(len(before))},
             compiler_params=params(),
             cost_estimate=part_cost,
@@ -693,7 +687,10 @@
             out_shape=(jax.ShapeDtypeStruct((states, width, terms * width), BF16), tile, rotated_bf, whole_bf),
             in_specs=[vmem] * (len(last_pieces) + 1) + [anywhere] * 2 + [vmem] * 2,
             out_specs=(vmem,) * 4,
-            scratch_shapes=[square, pltpu.SemaphoreType.DMA((len(last_pieces),))],
+            scratch_shapes=[
+                square,
+                pltpu.SemaphoreType.DMA((sum(spot[3] for spot in far_spots[-1]) // TILE,)),
+            ],
             input_output_aliases={len(last_pieces) + 1: 2, len(last_pieces) + 2: 3},
             compiler_params=params(),
             cost_estimate=cost(stage_flops, 12 * states * width * width),

time: 44.5 us -> 44 us (0.989)
  waiting for transfers between devices: 5.75 us -> 5.26 us
    ppermute x5, waiting for transfers between devices: 1.84 us -> 1.26 us  [to_next_chip(): lax.ppermute(block, 'term', [(i, (i + CORES) % members) for i in range(me...]
  transfers between devices with their start and end apart: 18 -> 18, of which waited for: 7 -> 6; matrix products, arithmetic and copies ran while one was open for 0% -> 0% of each run, Pallas kernels for 39% -> 39%
where the time goes in v16:
time: 44 us; the launch traced here: 43.8 us
  Pallas kernels  24.7 us (56%)
  starting transfers between devices  12.2 us (28%)
  waiting for transfers between devices  5.26 us (12%)
  between operations  1.65 us (4%)
    ppermute x5, starting transfers between devices, to_next_chip(): lax.ppermute(block, 'term', [(i, (i + CORES) % members) for i in range(me...  6.8 us
    pallas_call x1, Pallas kernels, shards(): pl.pallas_call(functools.partial(high_kernel, scale, members), out_shape=...  4.76 us
    pallas_call x1, Pallas kernels, shards(): pl.pallas_call(functools.partial(lefts_kernel, far_spots[-1], rows, chips...  2.6 us
    ppermute x11, waiting for transfers between devices, to_sibling(): return lax.ppermute(block, 'term', [(i, i ^ 1) for i in range(members)])  2.51 us
    pallas_call x2, Pallas kernels, rotate(): pl.pallas_call(functools.partial(rotate_kernel, spots, rows, chips), out_...  2.5 us
    ppermute x11, starting transfers between devices, to_sibling(): return lax.ppermute(block, 'term', [(i, i ^ 1) for i in range(members)])  2.38 us
    pallas_call x1, Pallas kernels, shards(): pl.pallas_call(functools.partial(last_kernel, len(last_pieces)), out_shap...  2.22 us
    pallas_call x2, Pallas kernels, shards(): pl.pallas_call(functools.partial(rights_kernel, start, stop), out_shape=(...  2.21 us
  transfers between devices with their start and end apart: 18, of which 6 were waited for; matrix products, arithmetic and copies ran while one was open for 0% of the time, Pallas kernels for 39%

profile of v16, /device:TPU:0, one launch (start us, length us, event | category | flops | bytes accessed | tf_op | source)
XLA Modules:
  0.0 43.8 jit_solution(6426851991007277939)
XLA Ops:
  1.3 1.4 %first_chunk.1 = (bf16[33,16,256]{2,1,0:T(8,128)(2,1)S(1)}, f32[8,256]{1,0:T(8,128)S(1)}, f32[8,256]{1,0:T(8,128)S(1)}, bf16[784,128]{1,0:T(8,128)(2,1)S(1)}) custom-call(s32[1,1]{1,0:T(1,128)} %bitcast.6.rank_in, f32[64,16,256]{2,1,0:T(8,128)} %bitcast.7, bf16[3,16,16]{2,1,0:T(8,128)(2,1)} %bitcast.12, bf16[3,256,256]{2,1,0:T(8,128)(2,1)} %bitcast.10), custom_call_target="tpu_custom_call" | custom-call | flops 5242 | bytes 7864 | tf_op jit(solution)/shard_map/first_chunk/pallas_call | solution.py:515
  2.7 0.5 %collective-permute-start = (bf16[33,16,256]{2,1,0:T(8,128)(2,1)S(1)}, bf16[33,16,256]{2,1,0:T(8,128)(2,1)S(1)}, u32[]{:S(2)}, u32[]{:S(2)}) collective-permute-start(bf16[33,16,256]{2,1,0:T(8,128)(2,1)S(1)} %get-tuple-element.53.chunk_ref.refs_0_), channel_id=1, source_target_pairs={{0,1},{1,0},{2,3},{3,2},{4,5},{5,4},{6,7},{7,6},{8,9},{9,8},{10,11... | collective-permute-start | bytes 811016 | tf_op jit(solution)/shard_map/ppermute | solution.py:492
  3.2 2.6 %collective-permute-start.2 = (bf16[33,16,256]{2,1,0:T(8,128)(2,1)S(1)}, bf16[33,16,256]{2,1,0:T(8,128)(2,1)S(1)}, u32[]{:S(2)}, u32[]{:S(2)}) collective-permute-start(bf16[33,16,256]{2,1,0:T(8,128)(2,1)S(1)} %get-tuple-element.53.chunk_ref.refs_0_), channel_id=1, source_target_pairs={{0,2},{1,3},{2,0},{3,1},{4,6},{5,7},{6,4},{7,5},{8,10},{9,11},{10,... | collective-permute-start | bytes 811016 | tf_op jit(solution)/shard_map/ppermute | solution.py:495
  5.8 1.3 %collective-permute-start.7 = (bf16[784,128]{1,0:T(8,128)(2,1)S(1)}, bf16[784,128]{1,0:T(8,128)(2,1)S(1)}, u32[]{:S(2)}, u32[]{:S(2)}) collective-permute-start(bf16[784,128]{1,0:T(8,128)(2,1)S(1)} %get-tuple-element.61), channel_id=1, source_target_pairs={{4,0},{8,4},{12,8},{16,12},{20,16},{24,20},{28,24},{5,1},{9,5},{13... | collective-permute-start | bytes 602120 | tf_op jit(solution)/shard_map/ppermute | solution.py:564
  7.0 0.0 collective-permute-done.refs_3_
  7.1 1.3 %prepare.1 = (f32[8,256]{1,0:T(8,128)S(1)}, bf16[784,128]{1,0:T(8,128)(2,1)S(1)}, bf16[3,256,256]{2,1,0:T(8,128)(2,1)S(1)}, bf16[16,16,256]{2,1,0:T(8,128)(2,1)S(1)}, bf16[16,16,256]{2,1,0:T(8,128)(2,1)S(1)}) custom-call(f32[8,256]{1,0:T(8,128)S(1)} %get-tuple-element.51.keep_ref, f32[8,256]{1,0:T(8,128)S(1)} %get-tuple-element.54.squares_ref, ...), custom_call_target="tpu_custom_call" | custom-call | flops 10485 | bytes 15728 | tf_op jit(solution)/shard_map/prepare/pallas_call | solution.py:533
  8.4 0.2 collective-permute-start.4
  8.6 0.3 collective-permute-start.3
  9.0 0.2 collective-permute-start.6
  9.2 0.4 spread_site.2.refs_6_.refs_5_.refs_3_.kron_ref
  9.5 0.3 collective-permute-done.4.refs_5_
  9.8 1.7 %collective-permute-start.1 = (bf16[16,16,256]{2,1,0:T(8,128)(2,1)S(1)}, bf16[16,16,256]{2,1,0:T(8,128)(2,1)S(1)}, u32[]{:S(2)}, u32[]{:S(2)}) collective-permute-start(bf16[16,16,256]{2,1,0:T(8,128)(2,1)S(1)} %get-tuple-element.55.refs_2_), channel_id=1, source_target_pairs={{0,2},{1,3},{2,0},{3,1},{4,6},{5,7},{6,4},{7,5},{8,10},{9,11},{10,... | collective-permute-start | bytes 393224 | tf_op jit(solution)/shard_map/ppermute | solution.py:495
  11.5 0.0 collective-permute-done.3.refs_4_
  11.5 0.4 collective-permute-start.10
  11.9 1.0 %rotate_own.1 = (bf16[3,16,128,256]{3,2,1,0:T(8,128)(2,1)S(1)}, bf16[256,768]{1,0:T(8,128)(2,1)S(1)}) custom-call(bf16[33,16,256]{2,1,0:T(8,128)(2,1)S(1)} %get-tuple-element.53.chunk_ref.refs_0_, bf16[16,16,256]{2,1,0:T(8,128)(2,1)S(1)} %get-tuple-element.56.refs_1_, bf16[16,16,256]{2,1,0:T(8,128)(2,1)S(1)} %get-tuple-element.55.refs_2_, ...), custom_call_target="tpu_custom_call" | custom-call | flops 16106127 | bytes 83886 | tf_op jit(solution)/shard_map/rotate_own/pallas_call | solution.py:596
  12.8 0.2 collective-permute-done.2.chunk_ref.refs_0_
  13.1 0.0 collective-permute-start.5
  13.1 0.4 spread_site.3.refs_6_.refs_4_.refs_2_
  13.5 1.4 %rotate_here.1 = (bf16[3,16,256,256]{3,2,1,0:T(8,128)(2,1)S(1)}, bf16[16,256,256]{2,1,0:T(8,128)(2,1)S(1)}) custom-call(bf16[33,16,256]{2,1,0:T(8,128)(2,1)S(1)} %get-tuple-element.53.chunk_ref.refs_0_, bf16[16,16,256]{2,1,0:T(8,128)(2,1)S(1)} %get-tuple-element.56.refs_1_, bf16[16,16,256]{2,1,0:T(8,128)(2,1)S(1)} %get-tuple-element.55.refs_2_, ...), custom_call_target="tpu_custom_call" | custom-call | flops 16106127 | bytes 83886 | tf_op jit(solution)/shard_map/rotate_here/pallas_call | solution.py:610
  14.9 0.0 collective-permute-done.7
  14.9 1.0 %collective-permute-done.6.refs_2_ = bf16[16,16,256]{2,1,0:T(8,128)(2,1)S(1)} collective-permute-done((bf16[16,16,256]{2,1,0:T(8,128)(2,1)S(1)}, bf16[16,16,256]{2,1,0:T(8,128)(2,1)S(1)}, u32[]{:S(2)}, u32[]{:S(2)}) %collective-permute-start.6) | collective-permute-done | bytes 131104 | tf_op jit(solution)/shard_map/ppermute | solution.py:495
  15.9 0.0 collective-permute-start.8
  15.9 2.0 %collective-permute-start.11 = (bf16[784,128]{1,0:T(8,128)(2,1)S(1)}, bf16[784,128]{1,0:T(8,128)(2,1)S(1)}, u32[]{:S(2)}, u32[]{:S(2)}) collective-permute-start(bf16[784,128]{1,0:T(8,128)(2,1)S(1)} %broadcast_select_fusion.packed_ref), channel_id=1, source_target_pairs={{0,2},{1,3},{2,0},{3,1},{4,6},{5,7},{6,4},{7,5},{8,10},{9,11},{10,... | collective-permute-start | bytes 602120 | tf_op jit(solution)/shard_map/ppermute | solution.py:495
  17.9 1.1 %apply_rows_here.1 = (bf16[16,384,256]{2,1,0:T(8,128)(2,1)S(1)}, bf16[3,256,256]{2,1,0:T(8,128)(2,1)S(1)}) custom-call(bf16[3,16,128,256]{3,2,1,0:T(8,128)(2,1)S(1)} %get-tuple-element.71.rotated_ref, bf16[784,128]{1,0:T(8,128)(2,1)S(1)} %broadcast_select_fusion.packed_ref, f32[8,256]{1,0:T(8,128)S(1)} %get-tuple-element.51.keep_ref), custom_call_target="tpu_custom_call" | custom-call | flops 16106127 | bytes 83886 | tf_op jit(solution)/shard_map/apply_rows_here/pallas_call | solution.py:631
  19.1 0.0 collective-permute-done.8.refs_3_
  19.1 0.0 collective-permute-done.5.refs_1_
  19.1 1.1 %rotate_crossed.1 = (bf16[3,16,256,256]{3,2,1,0:T(8,128)(2,1)S(1)}, bf16[16,256,256]{2,1,0:T(8,128)(2,1)S(1)}) custom-call(bf16[33,16,256]{2,1,0:T(8,128)(2,1)S(1)} %collective-permute-done.2.chunk_ref.refs_0_, bf16[33,16,256]{2,1,0:T(8,128)(2,1)S(1)} %collective-permute-done.5.refs_1_, ...), custom_call_target="tpu_custom_call", output_to_operand_aliasing={{0}: (5, {}), {1}: (6, {})} | custom-call | flops 16106127 | bytes 83886 | tf_op jit(solution)/shard_map/rotate_crossed/pallas_call | solution.py:610
  20.2 0.0 collective-permute-done.1.refs_0_
  20.2 0.3 collective-permute-start.9
  20.5 1.4 %apply_rows_crossed.1.refs_6_ = bf16[16,288,256]{2,1,0:T(8,128)(2,1)S(1)} custom-call(bf16[33,16,256]{2,1,0:T(8,128)(2,1)S(1)} %collective-permute-done.2.chunk_ref.refs_0_, bf16[33,16,256]{2,1,0:T(8,128)(2,1)S(1)} %collective-permute-done.5.refs_1_, bf16[16,16,256]{2,1,0:T(8,128)(2,1)S(1)} %collective-permute-done.6.refs_2_, ...), custom_call_target="tpu_custom_call" | custom-call | flops 16106127 | bytes 83886 | tf_op jit(solution)/shard_map/apply_rows_crossed/pallas_call | solution.py:652
  21.9 0.0 collective-permute-done.9.refs_1_
  21.9 2.2 %apply_rows_last.1.before_ref = f32[16,256,256]{2,1,0:T(8,128)S(1)} custom-call(bf16[16,16,256]{2,1,0:T(8,128)(2,1)S(1)} %collective-permute-done.1.refs_0_, bf16[16,16,256]{2,1,0:T(8,128)(2,1)S(1)} %collective-permute-done.9.refs_1_, bf16[3,256,256]{2,1,0:T(8,128)(2,1)S(1)} %get-tuple-element.78.refs_4_.refs_2_.right_ref, ...), custom_call_target="tpu_custom_call" | custom-call | flops 16106127 | bytes 83886 | tf_op jit(solution)/shard_map/apply_rows_last/pallas_call | solution.py:666
  24.1 0.0 collective-permute-done.10.refs_5_
  24.1 2.6 %received_lefts.1 = (bf16[16,256,768]{2,1,0:T(8,128)(2,1)S(1)}, f32[8,256]{1,0:T(8,128)S(1)}, bf16[3,16,256,256]{3,2,1,0:T(8,128)(2,1)S(1)}, bf16[16,256,256]{2,1,0:T(8,128)(2,1)S(1)}) custom-call(bf16[16,16,256]{2,1,0:T(8,128)(2,1)S(1)} %collective-permute-done.1.refs_0_, ...), custom_call_target="tpu_custom_call", output_to_operand_aliasing={{2}: (3, {}), {3}: (4, {})} | custom-call | flops 16106127 | bytes 125829 | tf_op jit(solution)/shard_map/received_lefts/pallas_call | solution.py:685
  26.7 0.4 collective-permute-start.12
  27.1 0.0 collective-permute-done.11.packed_ref
  27.1 1.2 %received_rights.2 = (bf16[8,256,256]{2,1,0:T(8,128)(2,1)S(1)}, bf16[3,256,256]{2,1,0:T(8,128)(2,1)S(1)}) custom-call(bf16[784,128]{1,0:T(8,128)(2,1)S(1)} %collective-permute-done.11.packed_ref, bf16[16,256,768]{2,1,0:T(8,128)(2,1)S(1)} %get-tuple-element.84.mixed_ref, f32[16,256,256]{2,1,0:T(8,128)S(1)} %apply_rows_last.1.before_ref, ...), custom_call_target="tpu_custom_call" | custom-call | flops 8053063 | bytes 125829 | tf_op jit(solution)/shard_map/received_rights/pallas_call | solution.py:705
  28.3 0.3 collective-permute-start.13
  28.6 0.0 collective-permute-done.12.norm_other_ref
  28.6 1.0 %received_rights.3.high_ref.refs_2_ = bf16[8,256,256]{2,1,0:T(8,128)(2,1)S(1)} custom-call(bf16[3,256,256]{2,1,0:T(8,128)(2,1)S(1)} %get-tuple-element.91.packed_ref, bf16[16,256,768]{2,1,0:T(8,128)(2,1)S(1)} %get-tuple-element.84.mixed_ref, f32[16,256,256]{2,1,0:T(8,128)S(1)} %apply_rows_last.1.before_ref, f32[8,256]{1,0:T(8,128)S(1)} %get-tuple-element.51.keep_ref), custom_call_target="tpu_custom_call" | custom-call | flops 8053063 | bytes 125829 | tf_op jit(solution)/shard_map/received_rights/pallas_call | solution.py:705
  29.6 0.4 collective-permute-start.14
  30.0 1.0 %collective-permute-done.13.low_other_ref.refs_1_ = bf16[8,256,256]{2,1,0:T(8,128)(2,1)S(1)} collective-permute-done((bf16[8,256,256]{2,1,0:T(8,128)(2,1)S(1)}, bf16[8,256,256]{2,1,0:T(8,128)(2,1)S(1)}, u32[]{:S(2)}, u32[]{:S(2)}) %collective-permute-start.13) | collective-permute-done | bytes 1048608 | tf_op jit(solution)/shard_map/ppermute | solution.py:492
  31.0 1.7 %residual_low.1 = (bf16[8,256,256]{2,1,0:T(8,128)(2,1)S(1)}, bf16[3,8,256,256]{3,2,1,0:T(8,128)(2,1)S(1)}, f32[8,256]{1,0:T(8,128)S(1)}) custom-call(f32[8,256]{1,0:T(8,128)S(1)} %get-tuple-element.83.norm_ref, f32[8,256]{1,0:T(8,128)S(1)} %collective-permute-done.12.norm_other_ref, bf16[8,256,256]{2,1,0:T(8,128)(2,1)S(1)} %get-tuple-element.88.low_ref.refs_0_, ...), custom_call_target="tpu_custom_call" | custom-call | flops 8053063 | bytes 31457 | tf_op jit(solution)/shard_map/residual_low/pallas_call | solution.py:724
  32.7 0.0 collective-permute-done.14.high_other_ref.refs_3_
  32.7 0.0 copy-start
  32.8 4.8 %residual_high.1.share_ref.refs_0_ = f32[8,256]{1,0:T(8,128)S(1)} custom-call(f32[8,256]{1,0:T(8,128)S(1)} %get-tuple-element.83.norm_ref, f32[8,256]{1,0:T(8,128)S(1)} %collective-permute-done.12.norm_other_ref, f32[8,256]{1,0:T(8,128)S(1)} %get-tuple-element.90.sums_ref, bf16[8,256,256]{2,1,0:T(8,128)(2,1)S(1)} %received_rights.3.high_ref.refs_2_, ...), custom_call_target="tpu_custom_call" | custom-call | flops 48318384 | bytes 62914 | tf_op jit(solution)/shard_map/residual_high/pallas_call | solution.py:733
  37.5 1.8 %collective-permute-start.15 = (f32[8,256]{1,0:T(8,128)S(1)}, f32[8,256]{1,0:T(8,128)S(1)}, u32[]{:S(2)}, u32[]{:S(2)}) collective-permute-start(f32[8,256]{1,0:T(8,128)S(1)} %residual_high.1.share_ref.refs_0_), channel_id=1, source_target_pairs={{0,2},{1,3},{2,0},{3,1},{4,6},{5,7},{6,4},{7,5},{8,10},{9,11},{10,... | collective-permute-start | bytes 24584 | tf_op jit(solution)/shard_map/ppermute | solution.py:505
  39.3 0.0 collective-permute-start.16
  39.3 0.0 copy-done
  39.3 0.5 %own_rows.1 = (f32[64,16,256]{2,1,0:T(8,128)S(1)}, f32[64,16,256]{2,1,0:T(8,128)S(1)}) custom-call(f32[8,256]{1,0:T(8,128)S(1)} %get-tuple-element.51.keep_ref, f32[8,256]{1,0:T(8,128)S(1)} %get-tuple-element.83.norm_ref, f32[8,256]{1,0:T(8,128)S(1)} %collective-permute-done.12.norm_other_ref, f32[8,256]{1,0:T(8,128)S(1)} %residual_high.1.share_ref.refs_0_, ...), custom_call_target="tpu_custom_call" | custom-call | flops 20971 | bytes 41943 | tf_op jit(solution)/shard_map/own_rows/pallas_call | solution.py:750
  39.8 1.5 %collective-permute-done.15.refs_2_ = f32[8,256]{1,0:T(8,128)S(1)} collective-permute-done((f32[8,256]{1,0:T(8,128)S(1)}, f32[8,256]{1,0:T(8,128)S(1)}, u32[]{:S(2)}, u32[]{:S(2)}) %collective-permute-start.15) | collective-permute-done | bytes 8224 | tf_op jit(solution)/shard_map/ppermute | solution.py:505
  41.2 0.0 collective-permute-start.17
  41.2 0.0 collective-permute-done.16.refs_1_
  41.3 1.2 %collective-permute-done.17.refs_3_ = f32[8,256]{1,0:T(8,128)S(1)} collective-permute-done((f32[8,256]{1,0:T(8,128)S(1)}, f32[8,256]{1,0:T(8,128)S(1)}, u32[]{:S(2)}, u32[]{:S(2)}) %collective-permute-start.17) | collective-permute-done | bytes 8224 | tf_op jit(solution)/shard_map/ppermute | solution.py:492
  42.4 1.3 %finish.1 = (f32[64,16,256]{2,1,0:T(8,128)}, f32[1]{0:T(128)}) custom-call(f32[64,16,256]{2,1,0:T(8,128)S(1)} %get-tuple-element.94.vector_ref, f32[64,16,256]{2,1,0:T(8,128)S(1)} %get-tuple-element.96.residual_ref, f32[8,256]{1,0:T(8,128)S(1)} %residual_high.1.share_ref.refs_0_, f32[8,256]{1,0:T(8,128)S(1)} %collective-permute-done.16.refs_1_, ...), custom_call_target="tpu_custom_call" | custom-call | flops 7864 | bytes 31457 | tf_op jit(solution)/shard_map/finish/pallas_call | solution.py:763
  (1 shorter events, 0.0 us)
Async XLA Ops:
  2.7 4.4 %collective-permute-start = (bf16[33,16,256]{2,1,0:T(8,128)(2,1)S(1)}, bf16[33,16,256]{2,1,0:T(8,128)(2,1)S(1)}, u32[]{:S(2)}, u32[]{:S(2)}) collective-permute-start(bf16[33,16,256]{2,1,0:T(8,128)(2,1)S(1)} %get-tuple-element.53.chunk_ref.refs_0_), channel_id=1, source_target_pairs={{0,1},{1,0},{2,3},{3,2},{4,5},{5,4},{6,7},{7,6},{8,9},{9,8},{10,11... | collective-permute-start | bytes 811016 | tf_op jit(solution)/shard_map/ppermute | solution.py:492
  3.2 9.9 %collective-permute-start.2 = (bf16[33,16,256]{2,1,0:T(8,128)(2,1)S(1)}, bf16[33,16,256]{2,1,0:T(8,128)(2,1)S(1)}, u32[]{:S(2)}, u32[]{:S(2)}) collective-permute-start(bf16[33,16,256]{2,1,0:T(8,128)(2,1)S(1)} %get-tuple-element.53.chunk_ref.refs_0_), channel_id=1, source_target_pairs={{0,2},{1,3},{2,0},{3,1},{4,6},{5,7},{6,4},{7,5},{8,10},{9,11},{10,... | collective-permute-start | bytes 811016 | tf_op jit(solution)/shard_map/ppermute | solution.py:495
  5.8 9.1 %collective-permute-start.7 = (bf16[784,128]{1,0:T(8,128)(2,1)S(1)}, bf16[784,128]{1,0:T(8,128)(2,1)S(1)}, u32[]{:S(2)}, u32[]{:S(2)}) collective-permute-start(bf16[784,128]{1,0:T(8,128)(2,1)S(1)} %get-tuple-element.61), channel_id=1, source_target_pairs={{4,0},{8,4},{12,8},{16,12},{20,16},{24,20},{28,24},{5,1},{9,5},{13... | collective-permute-start | bytes 602120 | tf_op jit(solution)/shard_map/ppermute | solution.py:564
  8.4 1.4 %collective-permute-start.4 = (bf16[16,16,256]{2,1,0:T(8,128)(2,1)S(1)}, bf16[16,16,256]{2,1,0:T(8,128)(2,1)S(1)}, u32[]{:S(2)}, u32[]{:S(2)}) collective-permute-start(bf16[16,16,256]{2,1,0:T(8,128)(2,1)S(1)} %get-tuple-element.55.refs_2_), channel_id=1, source_target_pairs={{0,1},{1,0},{2,3},{3,2},{4,5},{5,4},{6,7},{7,6},{8,9},{9,8},{10,11... | collective-permute-start | bytes 393224 | tf_op jit(solution)/shard_map/ppermute | solution.py:492
  8.6 2.8 %collective-permute-start.3 = (bf16[16,16,256]{2,1,0:T(8,128)(2,1)S(1)}, bf16[16,16,256]{2,1,0:T(8,128)(2,1)S(1)}, u32[]{:S(2)}, u32[]{:S(2)}) collective-permute-start(bf16[16,16,256]{2,1,0:T(8,128)(2,1)S(1)} %get-tuple-element.56.refs_1_), channel_id=1, source_target_pairs={{0,1},{1,0},{2,3},{3,2},{4,5},{5,4},{6,7},{7,6},{8,9},{9,8},{10,11... | collective-permute-start | bytes 393224 | tf_op jit(solution)/shard_map/ppermute | solution.py:492
  9.0 6.9 %collective-permute-start.6 = (bf16[16,16,256]{2,1,0:T(8,128)(2,1)S(1)}, bf16[16,16,256]{2,1,0:T(8,128)(2,1)S(1)}, u32[]{:S(2)}, u32[]{:S(2)}) collective-permute-start(bf16[16,16,256]{2,1,0:T(8,128)(2,1)S(1)} %get-tuple-element.56.refs_1_), channel_id=1, source_target_pairs={{0,2},{1,3},{2,0},{3,1},{4,6},{5,7},{6,4},{7,5},{8,10},{9,11},{10,... | collective-permute-start | bytes 393224 | tf_op jit(solution)/shard_map/ppermute | solution.py:495
  9.8 10.4 %collective-permute-start.1 = (bf16[16,16,256]{2,1,0:T(8,128)(2,1)S(1)}, bf16[16,16,256]{2,1,0:T(8,128)(2,1)S(1)}, u32[]{:S(2)}, u32[]{:S(2)}) collective-permute-start(bf16[16,16,256]{2,1,0:T(8,128)(2,1)S(1)} %get-tuple-element.55.refs_2_), channel_id=1, source_target_pairs={{0,2},{1,3},{2,0},{3,1},{4,6},{5,7},{6,4},{7,5},{8,10},{9,11},{10,... | collective-permute-start | bytes 393224 | tf_op jit(solution)/shard_map/ppermute | solution.py:495
  11.5 12.6 %collective-permute-start.10 = (bf16[784,128]{1,0:T(8,128)(2,1)S(1)}, bf16[784,128]{1,0:T(8,128)(2,1)S(1)}, u32[]{:S(2)}, u32[]{:S(2)}) collective-permute-start(bf16[784,128]{1,0:T(8,128)(2,1)S(1)} %get-tuple-element.77), channel_id=1, source_target_pairs={{0,2},{1,3},{2,0},{3,1},{4,6},{5,7},{6,4},{7,5},{8,10},{9,11},{10,... | collective-permute-start | bytes 602120 | tf_op jit(solution)/shard_map/ppermute | solution.py:495
  13.1 6.0 %collective-permute-start.5 = (bf16[33,16,256]{2,1,0:T(8,128)(2,1)S(1)}, bf16[33,16,256]{2,1,0:T(8,128)(2,1)S(1)}, u32[]{:S(2)}, u32[]{:S(2)}) collective-permute-start(bf16[33,16,256]{2,1,0:T(8,128)(2,1)S(1)} %collective-permute-done.2.chunk_ref.refs_0_), channel_id=1, source_target_pairs={{0,1},{1,0},{2,3},{3,2},{4,5},{5,4},{6,7},{7,6},{8,9},{9,8},{10,11... | collective-permute-start | bytes 811016 | tf_op jit(solution)/shard_map/ppermute | solution.py:492
  15.9 3.2 %collective-permute-start.8 = (bf16[16,16,256]{2,1,0:T(8,128)(2,1)S(1)}, bf16[16,16,256]{2,1,0:T(8,128)(2,1)S(1)}, u32[]{:S(2)}, u32[]{:S(2)}) collective-permute-start(bf16[16,16,256]{2,1,0:T(8,128)(2,1)S(1)} %collective-permute-done.6.refs_2_), channel_id=1, source_target_pairs={{0,1},{1,0},{2,3},{3,2},{4,5},{5,4},{6,7},{7,6},{8,9},{9,8},{10,11... | collective-permute-start | bytes 393224 | tf_op jit(solution)/shard_map/ppermute | solution.py:492
  15.9 11.2 %collective-permute-start.11 = (bf16[784,128]{1,0:T(8,128)(2,1)S(1)}, bf16[784,128]{1,0:T(8,128)(2,1)S(1)}, u32[]{:S(2)}, u32[]{:S(2)}) collective-permute-start(bf16[784,128]{1,0:T(8,128)(2,1)S(1)} %broadcast_select_fusion.packed_ref), channel_id=1, source_target_pairs={{0,2},{1,3},{2,0},{3,1},{4,6},{5,7},{6,4},{7,5},{8,10},{9,11},{10,... | collective-permute-start | bytes 602120 | tf_op jit(solution)/shard_map/ppermute | solution.py:495
  20.2 1.7 %collective-permute-start.9 = (bf16[16,16,256]{2,1,0:T(8,128)(2,1)S(1)}, bf16[16,16,256]{2,1,0:T(8,128)(2,1)S(1)}, u32[]{:S(2)}, u32[]{:S(2)}) collective-permute-start(bf16[16,16,256]{2,1,0:T(8,128)(2,1)S(1)} %collective-permute-done.1.refs_0_), channel_id=1, source_target_pairs={{0,1},{1,0},{2,3},{3,2},{4,5},{5,4},{6,7},{7,6},{8,9},{9,8},{10,11... | collective-permute-start | bytes 393224 | tf_op jit(solution)/shard_map/ppermute | solution.py:492
  26.7 1.8 %collective-permute-start.12 = (f32[8,256]{1,0:T(8,128)S(1)}, f32[8,256]{1,0:T(8,128)S(1)}, u32[]{:S(2)}, u32[]{:S(2)}) collective-permute-start(f32[8,256]{1,0:T(8,128)S(1)} %get-tuple-element.83.norm_ref), channel_id=1, source_target_pairs={{0,1},{1,0},{2,3},{3,2},{4,5},{5,4},{6,7},{7,6},{8,9},{9,8},{10,11... | collective-permute-start | bytes 24584 | tf_op jit(solution)/shard_map/ppermute | solution.py:492
  28.3 2.7 %collective-permute-start.13 = (bf16[8,256,256]{2,1,0:T(8,128)(2,1)S(1)}, bf16[8,256,256]{2,1,0:T(8,128)(2,1)S(1)}, u32[]{:S(2)}, u32[]{:S(2)}) collective-permute-start(bf16[8,256,256]{2,1,0:T(8,128)(2,1)S(1)} %get-tuple-element.88.low_ref.refs_0_), channel_id=1, source_target_pairs={{0,1},{1,0},{2,3},{3,2},{4,5},{5,4},{6,7},{7,6},{8,9},{9,8},{10,11... | collective-permute-start | bytes 3145736 | tf_op jit(solution)/shard_map/ppermute | solution.py:492
  29.6 3.1 %collective-permute-start.14 = (bf16[8,256,256]{2,1,0:T(8,128)(2,1)S(1)}, bf16[8,256,256]{2,1,0:T(8,128)(2,1)S(1)}, u32[]{:S(2)}, u32[]{:S(2)}) collective-permute-start(bf16[8,256,256]{2,1,0:T(8,128)(2,1)S(1)} %received_rights.3.high_ref.refs_2_), channel_id=1, source_target_pairs={{0,1},{1,0},{2,3},{3,2},{4,5},{5,4},{6,7},{7,6},{8,9},{9,8},{10,11... | collective-permute-start | bytes 3145736 | tf_op jit(solution)/shard_map/ppermute | solution.py:492
  32.7 6.5 %copy-start = (f32[1,64,16,256]{3,2,1,0:T(8,128)S(1)}, f32[1,64,16,256]{3,2,1,0:T(8,128)}, u32[]{:S(2)}) copy-start(f32[1,64,16,256]{3,2,1,0:T(8,128)} %param.5) | copy-start | bytes 3145732
  37.5 3.7 %collective-permute-start.15 = (f32[8,256]{1,0:T(8,128)S(1)}, f32[8,256]{1,0:T(8,128)S(1)}, u32[]{:S(2)}, u32[]{:S(2)}) collective-permute-start(f32[8,256]{1,0:T(8,128)S(1)} %residual_high.1.share_ref.refs_0_), channel_id=1, source_target_pairs={{0,2},{1,3},{2,0},{3,1},{4,6},{5,7},{6,4},{7,5},{8,10},{9,11},{10,... | collective-permute-start | bytes 24584 | tf_op jit(solution)/shard_map/ppermute | solution.py:505
  39.3 2.0 %collective-permute-start.16 = (f32[8,256]{1,0:T(8,128)S(1)}, f32[8,256]{1,0:T(8,128)S(1)}, u32[]{:S(2)}, u32[]{:S(2)}) collective-permute-start(f32[8,256]{1,0:T(8,128)S(1)} %residual_high.1.share_ref.refs_0_), channel_id=1, source_target_pairs={{0,1},{1,0},{2,3},{3,2},{4,5},{5,4},{6,7},{7,6},{8,9},{9,8},{10,11... | collective-permute-start | bytes 24584 | tf_op jit(solution)/shard_map/ppermute | solution.py:492
  41.2 1.2 %collective-permute-start.17 = (f32[8,256]{1,0:T(8,128)S(1)}, f32[8,256]{1,0:T(8,128)S(1)}, u32[]{:S(2)}, u32[]{:S(2)}) collective-permute-start(f32[8,256]{1,0:T(8,128)S(1)} %collective-permute-done.15.refs_2_), channel_id=1, source_target_pairs={{0,1},{1,0},{2,3},{3,2},{4,5},{5,4},{6,7},{7,6},{8,9},{9,8},{10,11... | collective-permute-start | bytes 24584 | tf_op jit(solution)/shard_map/ppermute | solution.py:492

commit v17 on v16

--- a/solution.py
+++ b/solution.py
@@ -44,15 +44,12 @@
 
 
 def first_chunk_kernel(
-    rank_in,
     guess_in,
     site_in,
     right_in,
     x_ref,
-    keep_ref,
     squares_ref,
     packed_ref,
-    rank_ref,
     guess_ref,
     site_ref,
     right_ref,
@@ -63,24 +60,19 @@
     blocks = rows // TILE
     copies = [
         pltpu.make_async_copy(source, target, sems.at[n])
-        for n, (source, target) in enumerate(((rank_in, rank_ref), (site_in, site_ref), (right_in, right_ref)))
+        for n, (source, target) in enumerate(((site_in, site_ref), (right_in, right_ref)))
     ]
+    parts = chunk_rows_in(guess_in, guess_ref, sems, 0, rows, 2)
     copies[0].start()
-    parts = chunk_rows_in(guess_in, guess_ref, sems, 0, rows, 3)
     copies[1].start()
-    copies[2].start()
-    copies[0].wait()
-    column = lax.broadcasted_iota(jnp.int32, (1, width), 1)
-    keep = (column < rank_ref[...]).astype(F32)
-    keep_ref[...] = jnp.broadcast_to(keep, keep_ref.shape)
     squares = jnp.zeros((8, width), F32)
     for n, copy in enumerate(parts):
         copy.wait()
-        masked = guess_ref[pl.ds(n * TILE, TILE)] * keep[None]
-        squares = squares + fold(masked * masked, width)
-        x_ref[n * states : (n + 1) * states] = jnp.swapaxes(masked, 0, 1).astype(BF16)
+        whole = guess_ref[pl.ds(n * TILE, TILE)]
+        squares = squares + fold(whole * whole, width)
+        x_ref[n * states : (n + 1) * states] = jnp.swapaxes(whole, 0, 1).astype(BF16)
     squares_ref[...] = squares
-    copies[1].wait()
+    copies[0].wait()
     line = lax.broadcasted_iota(jnp.int32, (TILE, width), 0)
     lane = lax.broadcasted_iota(jnp.int32, (TILE, width), 1)
     extra = jnp.zeros((TILE, width), F32)
@@ -88,11 +80,13 @@
         place_at = (lane == line + k * TILE).astype(BF16)
         extra = extra + jnp.dot(site_ref[k], place_at, preferred_element_type=F32)
     x_ref[blocks * states] = extra.astype(BF16)
-    copies[2].wait()
+    copies[1].wait()
     pack_blocks(right_ref, None, packed_ref)
 
 
-def prepare_kernel(starts, keep_ref, squares_ref, guess_in, left_in, norm_ref, packed_ref, left_ref, *refs):
+def prepare_kernel(
+    starts, rank_ref, squares_ref, guess_in, left_in, norm_ref, keep_ref, packed_ref, left_ref, *refs
+):
     x_refs = (None,) + refs[: len(starts) - 1]
     guess_ref, sems = refs[len(starts) - 1 :]
     rows, states, width = guess_in.shape
@@ -101,8 +95,11 @@
     copies = chunk_rows_in(guess_in, guess_ref, sems, done, rows, 1)
     left_copy = pltpu.make_async_copy(left_in, left_ref, sems.at[0])
     left_copy.start()
-    keep = keep_ref[0:1, :][None]
-    squares = squares_ref[...]
+    column = lax.broadcasted_iota(jnp.int32, (1, width), 1)
+    keep = (column < rank_ref[...]).astype(F32)
+    keep_ref[...] = jnp.broadcast_to(keep, keep_ref.shape)
+    squares = squares_ref[...] * keep
+    keep = keep[None]
     for n, copy in enumerate(copies):
         copy.wait()
         masked = guess_ref[pl.ds(n * TILE, TILE)] * keep
@@ -152,8 +149,13 @@
     half = width // 2
     row, col = triangle(half)
 
-    def kept(block, start):
-        return block if keep is None else block * keep[:, start : start + half]
+    rank = width if keep is None else jnp.sum(keep)
+    row_index = row.astype(F32)
+
+    def kept(block, top, start):
+        if keep is None:
+            return block
+        return jnp.where(row_index < rank - top, block * keep[:, start : start + half], 0.0)
 
     diagonals = packed_ref[terms * width : terms * width + TILE, :].astype(F32)
     for k in range(terms):
@@ -163,10 +165,10 @@
         diagonal = diagonals[k : k + 1]
         turned = mixed.T
         lower = jnp.where(row > col, mixed, jnp.where(row == col, diagonal, turned))
-        full_ref[k, 0:half, 0:half] = kept(jnp.where(row <= col, mixed, turned), 0).astype(BF16)
-        full_ref[k, 0:half, half:width] = kept(corner, half).astype(BF16)
-        full_ref[k, half:width, 0:half] = kept(corner.T, 0).astype(BF16)
-        full_ref[k, half:width, half:width] = kept(lower, half).astype(BF16)
+        full_ref[k, 0:half, 0:half] = kept(jnp.where(row <= col, mixed, turned), 0, 0).astype(BF16)
+        full_ref[k, 0:half, half:width] = kept(corner, 0, half).astype(BF16)
+        full_ref[k, half:width, 0:half] = kept(corner.T, half, 0).astype(BF16)
+        full_ref[k, half:width, half:width] = kept(lower, half, half).astype(BF16)
 
 
 def spread_kernel(chunk_ref, kron_ref):
@@ -325,7 +327,7 @@
     lax.fori_loop(0, (stop - start) // GROUP, rights, 0)
 
 
-def shifted_residual(start, shift, mine_ref, other_ref, whole_ref, left_ref, res_ref, mixed_ref):
+def shifted_residual(start, shift, keep, mine_ref, other_ref, whole_ref, left_ref, res_ref, mixed_ref):
     count, width, _ = res_ref.shape
     terms = left_ref.shape[0]
     zero = jnp.zeros((8, width), F32)
@@ -334,7 +336,7 @@
         square, product = sums
         for row in range(0, width, STRIP):
             strip = pl.ds(row, STRIP)
-            held = whole_ref[start + n, strip, :].astype(F32)
+            held = whole_ref[start + n, strip, :].astype(F32) * keep
             sigma = mine_ref[n, strip, :].astype(F32) + other_ref[n, strip, :].astype(F32)
             residual = sigma - shift * held
             res_ref[n, strip, :] = residual.astype(BF16)
@@ -352,6 +354,7 @@
 
 
 def low_kernel(
+    keep_ref,
     norm_ref,
     norm_other_ref,
     low_ref,
@@ -364,7 +367,8 @@
 ):
     count, width, _ = low_ref.shape
     states = whole_ref.shape[0]
-    held = whole_ref[0].astype(F32)
+    keep = keep_ref[0:1, :]
+    held = whole_ref[0].astype(F32) * keep
     sigma = low_ref[0].astype(F32) + low_other_ref[0].astype(F32)
     product = jnp.sum(fold(sigma * held, width))
     square = jnp.sum(fold(held * held, width))
@@ -372,7 +376,7 @@
     floor = jnp.maximum(jnp.maximum(square, (0.25 / states) * total), 1e-30)
     shift = product / floor
     square, product = shifted_residual(
-        0, shift, low_ref, low_other_ref, whole_ref, left_ref, res_ref, mixed_ref
+        0, shift, keep, low_ref, low_other_ref, whole_ref, left_ref, res_ref, mixed_ref
     )
     out_ref[0:1, :] = shift
     out_ref[1:2, :] = jnp.full((1, width), square, F32)
@@ -383,6 +387,7 @@
 def high_kernel(
     scale,
     members,
+    keep_ref,
     norm_ref,
     norm_other_ref,
     sums_ref,
@@ -403,7 +408,7 @@
     half = states // 2
     shift = sums_ref[0:1, :]
     square, product = shifted_residual(
-        half, shift, high_ref, high_other_ref, whole_ref, left_ref, res_ref, mixed_ref
+        half, shift, keep_ref[0:1, :], high_ref, high_other_ref, whole_ref, left_ref, res_ref, mixed_ref
     )
 
     def sites(i, carry):
@@ -512,34 +517,34 @@
     starts = (0, rows - 2 * TILE, rows - TILE) if rows >= 4 * TILE else (0,)
     lengths = [stop - start for start, stop in zip(starts, starts[1:] + (rows,))]
     in_place = [pltpu.with_memory_space_constraint(a, pltpu.HBM) for a in (guess, left, right_env[0], site)]
-    first_chunk, keep, squares, right_packed = pl.pallas_call(
+    first_chunk, squares, right_packed = pl.pallas_call(
         first_chunk_kernel,
-        out_shape=(jax.ShapeDtypeStruct((lengths[0] // TILE * states + 1, TILE, width), BF16), tile, tile, packed_shape),
-        in_specs=[anywhere] + [in_hbm] * 3,
-        out_specs=(vmem,) * 4,
+        out_shape=(jax.ShapeDtypeStruct((lengths[0] // TILE * states + 1, TILE, width), BF16), tile, packed_shape),
+        in_specs=[in_hbm] * 3,
+        out_specs=(vmem,) * 3,
         scratch_shapes=[
-            pltpu.VMEM((1, 1), jnp.int32),
             pltpu.VMEM((lengths[0], states, width), F32),
             pltpu.VMEM(site.shape, BF16),
             pltpu.VMEM(left.shape, BF16),
-            pltpu.SemaphoreType.DMA((lengths[0] // TILE + 3,)),
+            pltpu.SemaphoreType.DMA((lengths[0] // TILE + 2,)),
         ],
         compiler_params=params(),
         cost_estimate=cost(2 * guess.size, 3 * guess.size),
         name="first_chunk",
-    )(bond_rank.reshape(1, 1), in_place[0], in_place[3], in_place[2])
+    )(in_place[0], in_place[3], in_place[2])
     rest = rows - lengths[0]
     squares, first_sibling = lax.optimization_barrier((squares, to_sibling(first_chunk)))
-    norm_part, left_packed, left, *chunks = pl.pallas_call(
+    norm_part, keep, left_packed, left, *chunks = pl.pallas_call(
         functools.partial(prepare_kernel, starts),
         out_shape=(
+            tile,
             tile,
             packed_shape,
             jax.ShapeDtypeStruct(left.shape, BF16),
             *[jax.ShapeDtypeStruct((length // TILE * states, TILE, width), BF16) for length in lengths[1:]],
         ),
         in_specs=[vmem] * 2 + [in_hbm] * 2,
-        out_specs=(vmem,) * (2 + len(lengths)),
+        out_specs=(vmem,) * (3 + len(lengths)),
         scratch_shapes=[
             pltpu.VMEM((max(rest, TILE), states, width), F32),
             pltpu.SemaphoreType.DMA((rest // TILE + 1,)),
@@ -547,7 +552,7 @@
         compiler_params=params(),
         cost_estimate=cost(4 * guess.size, 6 * guess.size),
         name="prepare",
-    )(keep, squares, *in_place[:2])
+    )(bond_rank.reshape(1, 1), squares, *in_place[:2])
     chunks = [first_chunk] + chunks
 
     chunk_hops = [around(chunk) for chunk in chunks]
@@ -724,16 +729,16 @@
     res_low, mixed_low, sums = pl.pallas_call(
         low_kernel,
         out_shape=(half_bf, jax.ShapeDtypeStruct(half_mixed, BF16), tile),
-        in_specs=[vmem] * 6,
+        in_specs=[vmem] * 7,
         out_specs=(vmem,) * 3,
         compiler_params=params(),
         cost_estimate=cost(stage_flops / 2, 3 * states * width * width),
         name="residual_low",
-    )(norm, norm_other, *halves[:2], vector, left)
+    )(keep, norm, norm_other, *halves[:2], vector, left)
     share = pl.pallas_call(
         functools.partial(high_kernel, scale, members),
         out_shape=tile,
-        in_specs=[vmem] * 11,
+        in_specs=[vmem] * 12,
         out_specs=vmem,
         scratch_shapes=[
             pltpu.VMEM(half_bf.shape, BF16),
@@ -743,7 +748,7 @@
         compiler_params=params(),
         cost_estimate=cost(3 * stage_flops, 6 * states * width * width),
         name="residual_high",
-    )(norm, norm_other, sums, *halves[2:], vector, left, right, kron_own, res_low, mixed_low)
+    )(keep, norm, norm_other, sums, *halves[2:], vector, left, right, kron_own, res_low, mixed_low)
     crossed = everyone(share)
 
     local = jax.ShapeDtypeStruct((rows, states, width), F32)

time: 44 us -> 44.3 us (level); the launches traced: 43.8 us -> 43.5 us
    ppermute x5, waiting for transfers between devices: 1.26 us -> 0.7 us  [to_next_chip(): lax.ppermute(block, 'term', [(i, (i + CORES) % members) for i in range(me...]
  transfers between devices with their start and end apart: 18 -> 18, of which waited for: 6 -> 5; matrix products, arithmetic and copies ran while one was open for 0% -> 0% of each run, Pallas kernels for 39% -> 40%
where the time goes in v17:
time: 44.3 us; the launch traced here: 43.5 us
  Pallas kernels  25 us (56%)
  starting transfers between devices  11.9 us (27%)
  waiting for transfers between devices  4.88 us (11%)
  between operations  1.66 us (4%)
    ppermute x5, starting transfers between devices, to_next_chip(): lax.ppermute(block, 'term', [(i, (i + CORES) % members) for i in range(me...  6.49 us
    pallas_call x1, Pallas kernels, shards(): pl.pallas_call(functools.partial(high_kernel, scale, members), out_shape=...  4.88 us
    ppermute x11, waiting for transfers between devices, to_sibling(): return lax.ppermute(block, 'term', [(i, i ^ 1) for i in range(members)])  2.65 us
    pallas_call x1, Pallas kernels, shards(): pl.pallas_call(functools.partial(lefts_kernel, far_spots[-1], rows, chips...  2.6 us
    pallas_call x2, Pallas kernels, rotate(): pl.pallas_call(functools.partial(rotate_kernel, spots, rows, chips), out_...  2.47 us
    ppermute x11, starting transfers between devices, to_sibling(): return lax.ppermute(block, 'term', [(i, i ^ 1) for i in range(members)])  2.45 us
    pallas_call x2, Pallas kernels, shards(): pl.pallas_call(functools.partial(rights_kernel, start, stop), out_shape=(...  2.27 us
    pallas_call x1, Pallas kernels, shards(): pl.pallas_call(functools.partial(last_kernel, len(last_pieces)), out_shap...  2.22 us
  transfers between devices with their start and end apart: 18, of which 5 were waited for; matrix products, arithmetic and copies ran while one was open for 0% of the time, Pallas kernels for 40%

profile of v17, /device:TPU:0, one launch (start us, length us, event | category | flops | bytes accessed | tf_op | source)
XLA Modules:
  0.0 43.5 jit_solution(10348041547514739868)
XLA Ops:
  0.6 1.3 %first_chunk.1 = (bf16[33,16,256]{2,1,0:T(8,128)(2,1)S(1)}, f32[8,256]{1,0:T(8,128)S(1)}, bf16[784,128]{1,0:T(8,128)(2,1)S(1)}) custom-call(f32[64,16,256]{2,1,0:T(8,128)} %bitcast.7, bf16[3,16,16]{2,1,0:T(8,128)(2,1)} %bitcast.12, bf16[3,256,256]{2,1,0:T(8,128)(2,1)} %bitcast.10), custom_call_target="tpu_custom_call" | custom-call | flops 5242 | bytes 7864 | tf_op jit(solution)/shard_map/first_chunk/pallas_call | solution.py:520
  2.0 0.5 %collective-permute-start = (bf16[33,16,256]{2,1,0:T(8,128)(2,1)S(1)}, bf16[33,16,256]{2,1,0:T(8,128)(2,1)S(1)}, u32[]{:S(2)}, u32[]{:S(2)}) collective-permute-start(bf16[33,16,256]{2,1,0:T(8,128)(2,1)S(1)} %get-tuple-element.52.chunk_ref.refs_0_), channel_id=1, source_target_pairs={{0,1},{1,0},{2,3},{3,2},{4,5},{5,4},{6,7},{7,6},{8,9},{9,8},{10,11... | collective-permute-start | bytes 811016 | tf_op jit(solution)/shard_map/ppermute | solution.py:497
  2.5 2.6 %collective-permute-start.2 = (bf16[33,16,256]{2,1,0:T(8,128)(2,1)S(1)}, bf16[33,16,256]{2,1,0:T(8,128)(2,1)S(1)}, u32[]{:S(2)}, u32[]{:S(2)}) collective-permute-start(bf16[33,16,256]{2,1,0:T(8,128)(2,1)S(1)} %get-tuple-element.52.chunk_ref.refs_0_), channel_id=1, source_target_pairs={{0,2},{1,3},{2,0},{3,1},{4,6},{5,7},{6,4},{7,5},{8,10},{9,11},{10,... | collective-permute-start | bytes 811016 | tf_op jit(solution)/shard_map/ppermute | solution.py:500
  5.1 1.3 %collective-permute-start.7 = (bf16[784,128]{1,0:T(8,128)(2,1)S(1)}, bf16[784,128]{1,0:T(8,128)(2,1)S(1)}, u32[]{:S(2)}, u32[]{:S(2)}) collective-permute-start(bf16[784,128]{1,0:T(8,128)(2,1)S(1)} %get-tuple-element.61), channel_id=1, source_target_pairs={{4,0},{8,4},{12,8},{16,12},{20,16},{24,20},{28,24},{5,1},{9,5},{13... | collective-permute-start | bytes 602120 | tf_op jit(solution)/shard_map/ppermute | solution.py:569
  7.0 0.0 collective-permute-done.refs_3_
  7.0 1.3 %prepare.1 = (f32[8,256]{1,0:T(8,128)S(1)}, f32[8,256]{1,0:T(8,128)S(1)}, bf16[784,128]{1,0:T(8,128)(2,1)S(1)}, bf16[3,256,256]{2,1,0:T(8,128)(2,1)S(1)}, bf16[1...) custom-call(s32[1,1]{1,0:T(1,128)} %bitcast.6.rank_ref, f32[8,256]{1,0:T(8,128)S(1)} %get-tuple-element.53.squares_ref, ...), custom_call_target="tpu_custom_call" | custom-call | flops 10485 | bytes 15728 | tf_op jit(solution)/shard_map/prepare/pallas_call | solution.py:537
  8.4 0.2 collective-permute-start.4
  8.6 0.3 collective-permute-start.3
  9.0 0.0 collective-permute-start.6
  9.0 0.4 spread_site.2.refs_6_.refs_5_.refs_3_.kron_ref
  9.4 0.4 collective-permute-done.4.refs_5_
  9.8 1.7 %collective-permute-start.1 = (bf16[16,16,256]{2,1,0:T(8,128)(2,1)S(1)}, bf16[16,16,256]{2,1,0:T(8,128)(2,1)S(1)}, u32[]{:S(2)}, u32[]{:S(2)}) collective-permute-start(bf16[16,16,256]{2,1,0:T(8,128)(2,1)S(1)} %get-tuple-element.55.refs_2_), channel_id=1, source_target_pairs={{0,2},{1,3},{2,0},{3,1},{4,6},{5,7},{6,4},{7,5},{8,10},{9,11},{10,... | collective-permute-start | bytes 393224 | tf_op jit(solution)/shard_map/ppermute | solution.py:500
  11.4 0.0 collective-permute-done.3.refs_4_
  11.5 0.4 collective-permute-start.10
  11.8 1.0 %rotate_own.1 = (bf16[3,16,128,256]{3,2,1,0:T(8,128)(2,1)S(1)}, bf16[256,768]{1,0:T(8,128)(2,1)S(1)}) custom-call(bf16[33,16,256]{2,1,0:T(8,128)(2,1)S(1)} %get-tuple-element.52.chunk_ref.refs_0_, bf16[16,16,256]{2,1,0:T(8,128)(2,1)S(1)} %get-tuple-element.56.refs_1_, bf16[16,16,256]{2,1,0:T(8,128)(2,1)S(1)} %get-tuple-element.55.refs_2_, ...), custom_call_target="tpu_custom_call" | custom-call | flops 16106127 | bytes 83886 | tf_op jit(solution)/shard_map/rotate_own/pallas_call | solution.py:601
  12.8 0.0 collective-permute-done.2.chunk_ref.refs_0_
  12.8 0.1 collective-permute-start.5
  12.9 0.4 spread_site.3.refs_6_.refs_4_.refs_2_
  13.3 1.4 %rotate_here.1 = (bf16[3,16,256,256]{3,2,1,0:T(8,128)(2,1)S(1)}, bf16[16,256,256]{2,1,0:T(8,128)(2,1)S(1)}) custom-call(bf16[33,16,256]{2,1,0:T(8,128)(2,1)S(1)} %get-tuple-element.52.chunk_ref.refs_0_, bf16[16,16,256]{2,1,0:T(8,128)(2,1)S(1)} %get-tuple-element.56.refs_1_, bf16[16,16,256]{2,1,0:T(8,128)(2,1)S(1)} %get-tuple-element.55.refs_2_, ...), custom_call_target="tpu_custom_call" | custom-call | flops 16106127 | bytes 83886 | tf_op jit(solution)/shard_map/rotate_here/pallas_call | solution.py:615
  14.7 0.0 collective-permute-done.7
  14.7 0.7 %collective-permute-done.6.refs_2_ = bf16[16,16,256]{2,1,0:T(8,128)(2,1)S(1)} collective-permute-done((bf16[16,16,256]{2,1,0:T(8,128)(2,1)S(1)}, bf16[16,16,256]{2,1,0:T(8,128)(2,1)S(1)}, u32[]{:S(2)}, u32[]{:S(2)}) %collective-permute-start.6) | collective-permute-done | bytes 131104 | tf_op jit(solution)/shard_map/ppermute | solution.py:500
  15.4 0.0 collective-permute-start.8
  15.4 1.9 %collective-permute-start.11 = (bf16[784,128]{1,0:T(8,128)(2,1)S(1)}, bf16[784,128]{1,0:T(8,128)(2,1)S(1)}, u32[]{:S(2)}, u32[]{:S(2)}) collective-permute-start(bf16[784,128]{1,0:T(8,128)(2,1)S(1)} %broadcast_select_fusion.packed_ref), channel_id=1, source_target_pairs={{0,2},{1,3},{2,0},{3,1},{4,6},{5,7},{6,4},{7,5},{8,10},{9,11},{10,... | collective-permute-start | bytes 602120 | tf_op jit(solution)/shard_map/ppermute | solution.py:500
  17.3 1.2 %apply_rows_here.1 = (bf16[16,384,256]{2,1,0:T(8,128)(2,1)S(1)}, bf16[3,256,256]{2,1,0:T(8,128)(2,1)S(1)}) custom-call(bf16[3,16,128,256]{3,2,1,0:T(8,128)(2,1)S(1)} %get-tuple-element.71.rotated_ref, bf16[784,128]{1,0:T(8,128)(2,1)S(1)} %broadcast_select_fusion.packed_ref, f32[8,256]{1,0:T(8,128)S(1)} %get-tuple-element.54.keep_ref), custom_call_target="tpu_custom_call" | custom-call | flops 16106127 | bytes 83886 | tf_op jit(solution)/shard_map/apply_rows_here/pallas_call | solution.py:636
  18.5 0.0 collective-permute-done.8.refs_3_
  18.5 0.0 collective-permute-done.5.refs_1_
  18.5 1.1 %rotate_crossed.1 = (bf16[3,16,256,256]{3,2,1,0:T(8,128)(2,1)S(1)}, bf16[16,256,256]{2,1,0:T(8,128)(2,1)S(1)}) custom-call(bf16[33,16,256]{2,1,0:T(8,128)(2,1)S(1)} %collective-permute-done.2.chunk_ref.refs_0_, bf16[33,16,256]{2,1,0:T(8,128)(2,1)S(1)} %collective-permute-done.5.refs_1_, ...), custom_call_target="tpu_custom_call", output_to_operand_aliasing={{0}: (5, {}), {1}: (6, {})} | custom-call | flops 16106127 | bytes 83886 | tf_op jit(solution)/shard_map/rotate_crossed/pallas_call | solution.py:615
  19.6 0.0 collective-permute-done.1.refs_0_
  19.6 0.3 collective-permute-start.9
  19.9 1.4 %apply_rows_crossed.1.refs_6_ = bf16[16,288,256]{2,1,0:T(8,128)(2,1)S(1)} custom-call(bf16[33,16,256]{2,1,0:T(8,128)(2,1)S(1)} %collective-permute-done.2.chunk_ref.refs_0_, bf16[33,16,256]{2,1,0:T(8,128)(2,1)S(1)} %collective-permute-done.5.refs_1_, bf16[16,16,256]{2,1,0:T(8,128)(2,1)S(1)} %collective-permute-done.6.refs_2_, ...), custom_call_target="tpu_custom_call" | custom-call | flops 16106127 | bytes 83886 | tf_op jit(solution)/shard_map/apply_rows_crossed/pallas_call | solution.py:657
  21.3 0.0 collective-permute-done.9.refs_1_
  21.3 2.2 %apply_rows_last.1.before_ref = f32[16,256,256]{2,1,0:T(8,128)S(1)} custom-call(bf16[16,16,256]{2,1,0:T(8,128)(2,1)S(1)} %collective-permute-done.1.refs_0_, bf16[16,16,256]{2,1,0:T(8,128)(2,1)S(1)} %collective-permute-done.9.refs_1_, bf16[3,256,256]{2,1,0:T(8,128)(2,1)S(1)} %get-tuple-element.78.refs_4_.refs_2_.right_ref, ...), custom_call_target="tpu_custom_call" | custom-call | flops 16106127 | bytes 83886 | tf_op jit(solution)/shard_map/apply_rows_last/pallas_call | solution.py:671
  23.5 0.0 collective-permute-done.10.refs_5_
  23.6 2.6 %received_lefts.1 = (bf16[16,256,768]{2,1,0:T(8,128)(2,1)S(1)}, f32[8,256]{1,0:T(8,128)S(1)}, bf16[3,16,256,256]{3,2,1,0:T(8,128)(2,1)S(1)}, bf16[16,256,256]{2,1,0:T(8,128)(2,1)S(1)}) custom-call(bf16[16,16,256]{2,1,0:T(8,128)(2,1)S(1)} %collective-permute-done.1.refs_0_, ...), custom_call_target="tpu_custom_call", output_to_operand_aliasing={{2}: (3, {}), {3}: (4, {})} | custom-call | flops 16106127 | bytes 125829 | tf_op jit(solution)/shard_map/received_lefts/pallas_call | solution.py:690
  26.2 0.3 collective-permute-start.12
  26.5 0.0 collective-permute-done.11.packed_ref
  26.5 1.2 %received_rights.2 = (bf16[8,256,256]{2,1,0:T(8,128)(2,1)S(1)}, bf16[3,256,256]{2,1,0:T(8,128)(2,1)S(1)}) custom-call(bf16[784,128]{1,0:T(8,128)(2,1)S(1)} %collective-permute-done.11.packed_ref, bf16[16,256,768]{2,1,0:T(8,128)(2,1)S(1)} %get-tuple-element.84.mixed_ref, f32[16,256,256]{2,1,0:T(8,128)S(1)} %apply_rows_last.1.before_ref, ...), custom_call_target="tpu_custom_call" | custom-call | flops 8053063 | bytes 125829 | tf_op jit(solution)/shard_map/received_rights/pallas_call | solution.py:710
  27.7 0.3 collective-permute-start.13
  28.0 0.0 collective-permute-done.12.norm_other_ref
  28.1 1.0 %received_rights.3.high_ref.refs_2_ = bf16[8,256,256]{2,1,0:T(8,128)(2,1)S(1)} custom-call(bf16[3,256,256]{2,1,0:T(8,128)(2,1)S(1)} %get-tuple-element.91.packed_ref, bf16[16,256,768]{2,1,0:T(8,128)(2,1)S(1)} %get-tuple-element.84.mixed_ref, f32[16,256,256]{2,1,0:T(8,128)S(1)} %apply_rows_last.1.before_ref, f32[8,256]{1,0:T(8,128)S(1)} %get-tuple-element.54.keep_ref), custom_call_target="tpu_custom_call" | custom-call | flops 8053063 | bytes 125829 | tf_op jit(solution)/shard_map/received_rights/pallas_call | solution.py:710
  29.1 0.3 collective-permute-start.14
  29.4 1.0 %collective-permute-done.13.low_other_ref.refs_1_ = bf16[8,256,256]{2,1,0:T(8,128)(2,1)S(1)} collective-permute-done((bf16[8,256,256]{2,1,0:T(8,128)(2,1)S(1)}, bf16[8,256,256]{2,1,0:T(8,128)(2,1)S(1)}, u32[]{:S(2)}, u32[]{:S(2)}) %collective-permute-start.13) | collective-permute-done | bytes 1048608 | tf_op jit(solution)/shard_map/ppermute | solution.py:497
  30.5 1.8 %residual_low.1 = (bf16[8,256,256]{2,1,0:T(8,128)(2,1)S(1)}, bf16[3,8,256,256]{3,2,1,0:T(8,128)(2,1)S(1)}, f32[8,256]{1,0:T(8,128)S(1)}) custom-call(f32[8,256]{1,0:T(8,128)S(1)} %get-tuple-element.54.keep_ref, f32[8,256]{1,0:T(8,128)S(1)} %get-tuple-element.83.norm_ref, f32[8,256]{1,0:T(8,128)S(1)} %collective-permute-done.12.norm_other_ref, ...), custom_call_target="tpu_custom_call" | custom-call | flops 8053063 | bytes 31457 | tf_op jit(solution)/shard_map/residual_low/pallas_call | solution.py:729
  32.3 0.0 collective-permute-done.14.high_other_ref.refs_3_
  32.3 0.0 copy-start
  32.3 4.9 %residual_high.1.share_ref.refs_0_ = f32[8,256]{1,0:T(8,128)S(1)} custom-call(f32[8,256]{1,0:T(8,128)S(1)} %get-tuple-element.54.keep_ref, f32[8,256]{1,0:T(8,128)S(1)} %get-tuple-element.83.norm_ref, f32[8,256]{1,0:T(8,128)S(1)} %collective-permute-done.12.norm_other_ref, f32[8,256]{1,0:T(8,128)S(1)} %get-tuple-element.90.sums_ref, ...), custom_call_target="tpu_custom_call" | custom-call | flops 48318384 | bytes 62914 | tf_op jit(solution)/shard_map/residual_high/pallas_call | solution.py:738
  37.2 1.7 %collective-permute-start.15 = (f32[8,256]{1,0:T(8,128)S(1)}, f32[8,256]{1,0:T(8,128)S(1)}, u32[]{:S(2)}, u32[]{:S(2)}) collective-permute-start(f32[8,256]{1,0:T(8,128)S(1)} %residual_high.1.share_ref.refs_0_), channel_id=1, source_target_pairs={{0,2},{1,3},{2,0},{3,1},{4,6},{5,7},{6,4},{7,5},{8,10},{9,11},{10,... | collective-permute-start | bytes 24584 | tf_op jit(solution)/shard_map/ppermute | solution.py:510
  38.9 0.0 collective-permute-start.16
  38.9 0.0 copy-done
  38.9 0.5 %own_rows.1 = (f32[64,16,256]{2,1,0:T(8,128)S(1)}, f32[64,16,256]{2,1,0:T(8,128)S(1)}) custom-call(f32[8,256]{1,0:T(8,128)S(1)} %get-tuple-element.54.keep_ref, f32[8,256]{1,0:T(8,128)S(1)} %get-tuple-element.83.norm_ref, f32[8,256]{1,0:T(8,128)S(1)} %collective-permute-done.12.norm_other_ref, f32[8,256]{1,0:T(8,128)S(1)} %residual_high.1.share_ref.refs_0_, ...), custom_call_target="tpu_custom_call" | custom-call | flops 20971 | bytes 41943 | tf_op jit(solution)/shard_map/own_rows/pallas_call | solution.py:755
  39.4 1.5 %collective-permute-done.15.refs_2_ = f32[8,256]{1,0:T(8,128)S(1)} collective-permute-done((f32[8,256]{1,0:T(8,128)S(1)}, f32[8,256]{1,0:T(8,128)S(1)}, u32[]{:S(2)}, u32[]{:S(2)}) %collective-permute-start.15) | collective-permute-done | bytes 8224 | tf_op jit(solution)/shard_map/ppermute | solution.py:510
  40.9 0.0 collective-permute-start.17
  40.9 0.0 collective-permute-done.16.refs_1_
  40.9 1.2 %collective-permute-done.17.refs_3_ = f32[8,256]{1,0:T(8,128)S(1)} collective-permute-done((f32[8,256]{1,0:T(8,128)S(1)}, f32[8,256]{1,0:T(8,128)S(1)}, u32[]{:S(2)}, u32[]{:S(2)}) %collective-permute-start.17) | collective-permute-done | bytes 8224 | tf_op jit(solution)/shard_map/ppermute | solution.py:497
  42.1 1.3 %finish.1 = (f32[64,16,256]{2,1,0:T(8,128)}, f32[1]{0:T(128)}) custom-call(f32[64,16,256]{2,1,0:T(8,128)S(1)} %get-tuple-element.94.vector_ref, f32[64,16,256]{2,1,0:T(8,128)S(1)} %get-tuple-element.96.residual_ref, f32[8,256]{1,0:T(8,128)S(1)} %residual_high.1.share_ref.refs_0_, f32[8,256]{1,0:T(8,128)S(1)} %collective-permute-done.16.refs_1_, ...), custom_call_target="tpu_custom_call" | custom-call | flops 7864 | bytes 31457 | tf_op jit(solution)/shard_map/finish/pallas_call | solution.py:768
  (1 shorter events, 0.0 us)
Async XLA Ops:
  2.0 5.0 %collective-permute-start = (bf16[33,16,256]{2,1,0:T(8,128)(2,1)S(1)}, bf16[33,16,256]{2,1,0:T(8,128)(2,1)S(1)}, u32[]{:S(2)}, u32[]{:S(2)}) collective-permute-start(bf16[33,16,256]{2,1,0:T(8,128)(2,1)S(1)} %get-tuple-element.52.chunk_ref.refs_0_), channel_id=1, source_target_pairs={{0,1},{1,0},{2,3},{3,2},{4,5},{5,4},{6,7},{7,6},{8,9},{9,8},{10,11... | collective-permute-start | bytes 811016 | tf_op jit(solution)/shard_map/ppermute | solution.py:497
  2.5 10.3 %collective-permute-start.2 = (bf16[33,16,256]{2,1,0:T(8,128)(2,1)S(1)}, bf16[33,16,256]{2,1,0:T(8,128)(2,1)S(1)}, u32[]{:S(2)}, u32[]{:S(2)}) collective-permute-start(bf16[33,16,256]{2,1,0:T(8,128)(2,1)S(1)} %get-tuple-element.52.chunk_ref.refs_0_), channel_id=1, source_target_pairs={{0,2},{1,3},{2,0},{3,1},{4,6},{5,7},{6,4},{7,5},{8,10},{9,11},{10,... | collective-permute-start | bytes 811016 | tf_op jit(solution)/shard_map/ppermute | solution.py:500
  5.1 9.6 %collective-permute-start.7 = (bf16[784,128]{1,0:T(8,128)(2,1)S(1)}, bf16[784,128]{1,0:T(8,128)(2,1)S(1)}, u32[]{:S(2)}, u32[]{:S(2)}) collective-permute-start(bf16[784,128]{1,0:T(8,128)(2,1)S(1)} %get-tuple-element.61), channel_id=1, source_target_pairs={{4,0},{8,4},{12,8},{16,12},{20,16},{24,20},{28,24},{5,1},{9,5},{13... | collective-permute-start | bytes 602120 | tf_op jit(solution)/shard_map/ppermute | solution.py:569
  8.4 1.4 %collective-permute-start.4 = (bf16[16,16,256]{2,1,0:T(8,128)(2,1)S(1)}, bf16[16,16,256]{2,1,0:T(8,128)(2,1)S(1)}, u32[]{:S(2)}, u32[]{:S(2)}) collective-permute-start(bf16[16,16,256]{2,1,0:T(8,128)(2,1)S(1)} %get-tuple-element.55.refs_2_), channel_id=1, source_target_pairs={{0,1},{1,0},{2,3},{3,2},{4,5},{5,4},{6,7},{7,6},{8,9},{9,8},{10,11... | collective-permute-start | bytes 393224 | tf_op jit(solution)/shard_map/ppermute | solution.py:497
  8.6 2.8 %collective-permute-start.3 = (bf16[16,16,256]{2,1,0:T(8,128)(2,1)S(1)}, bf16[16,16,256]{2,1,0:T(8,128)(2,1)S(1)}, u32[]{:S(2)}, u32[]{:S(2)}) collective-permute-start(bf16[16,16,256]{2,1,0:T(8,128)(2,1)S(1)} %get-tuple-element.56.refs_1_), channel_id=1, source_target_pairs={{0,1},{1,0},{2,3},{3,2},{4,5},{5,4},{6,7},{7,6},{8,9},{9,8},{10,11... | collective-permute-start | bytes 393224 | tf_op jit(solution)/shard_map/ppermute | solution.py:497
  9.0 6.4 %collective-permute-start.6 = (bf16[16,16,256]{2,1,0:T(8,128)(2,1)S(1)}, bf16[16,16,256]{2,1,0:T(8,128)(2,1)S(1)}, u32[]{:S(2)}, u32[]{:S(2)}) collective-permute-start(bf16[16,16,256]{2,1,0:T(8,128)(2,1)S(1)} %get-tuple-element.56.refs_1_), channel_id=1, source_target_pairs={{0,2},{1,3},{2,0},{3,1},{4,6},{5,7},{6,4},{7,5},{8,10},{9,11},{10,... | collective-permute-start | bytes 393224 | tf_op jit(solution)/shard_map/ppermute | solution.py:500
  9.8 9.8 %collective-permute-start.1 = (bf16[16,16,256]{2,1,0:T(8,128)(2,1)S(1)}, bf16[16,16,256]{2,1,0:T(8,128)(2,1)S(1)}, u32[]{:S(2)}, u32[]{:S(2)}) collective-permute-start(bf16[16,16,256]{2,1,0:T(8,128)(2,1)S(1)} %get-tuple-element.55.refs_2_), channel_id=1, source_target_pairs={{0,2},{1,3},{2,0},{3,1},{4,6},{5,7},{6,4},{7,5},{8,10},{9,11},{10,... | collective-permute-start | bytes 393224 | tf_op jit(solution)/shard_map/ppermute | solution.py:500
  11.5 12.1 %collective-permute-start.10 = (bf16[784,128]{1,0:T(8,128)(2,1)S(1)}, bf16[784,128]{1,0:T(8,128)(2,1)S(1)}, u32[]{:S(2)}, u32[]{:S(2)}) collective-permute-start(bf16[784,128]{1,0:T(8,128)(2,1)S(1)} %get-tuple-element.77), channel_id=1, source_target_pairs={{0,2},{1,3},{2,0},{3,1},{4,6},{5,7},{6,4},{7,5},{8,10},{9,11},{10,... | collective-permute-start | bytes 602120 | tf_op jit(solution)/shard_map/ppermute | solution.py:500
  12.8 5.7 %collective-permute-start.5 = (bf16[33,16,256]{2,1,0:T(8,128)(2,1)S(1)}, bf16[33,16,256]{2,1,0:T(8,128)(2,1)S(1)}, u32[]{:S(2)}, u32[]{:S(2)}) collective-permute-start(bf16[33,16,256]{2,1,0:T(8,128)(2,1)S(1)} %collective-permute-done.2.chunk_ref.refs_0_), channel_id=1, source_target_pairs={{0,1},{1,0},{2,3},{3,2},{4,5},{5,4},{6,7},{7,6},{8,9},{9,8},{10,11... | collective-permute-start | bytes 811016 | tf_op jit(solution)/shard_map/ppermute | solution.py:497
  15.4 3.1 %collective-permute-start.8 = (bf16[16,16,256]{2,1,0:T(8,128)(2,1)S(1)}, bf16[16,16,256]{2,1,0:T(8,128)(2,1)S(1)}, u32[]{:S(2)}, u32[]{:S(2)}) collective-permute-start(bf16[16,16,256]{2,1,0:T(8,128)(2,1)S(1)} %collective-permute-done.6.refs_2_), channel_id=1, source_target_pairs={{0,1},{1,0},{2,3},{3,2},{4,5},{5,4},{6,7},{7,6},{8,9},{9,8},{10,11... | collective-permute-start | bytes 393224 | tf_op jit(solution)/shard_map/ppermute | solution.py:497
  15.4 11.1 %collective-permute-start.11 = (bf16[784,128]{1,0:T(8,128)(2,1)S(1)}, bf16[784,128]{1,0:T(8,128)(2,1)S(1)}, u32[]{:S(2)}, u32[]{:S(2)}) collective-permute-start(bf16[784,128]{1,0:T(8,128)(2,1)S(1)} %broadcast_select_fusion.packed_ref), channel_id=1, source_target_pairs={{0,2},{1,3},{2,0},{3,1},{4,6},{5,7},{6,4},{7,5},{8,10},{9,11},{10,... | collective-permute-start | bytes 602120 | tf_op jit(solution)/shard_map/ppermute | solution.py:500
  19.6 1.7 %collective-permute-start.9 = (bf16[16,16,256]{2,1,0:T(8,128)(2,1)S(1)}, bf16[16,16,256]{2,1,0:T(8,128)(2,1)S(1)}, u32[]{:S(2)}, u32[]{:S(2)}) collective-permute-start(bf16[16,16,256]{2,1,0:T(8,128)(2,1)S(1)} %collective-permute-done.1.refs_0_), channel_id=1, source_target_pairs={{0,1},{1,0},{2,3},{3,2},{4,5},{5,4},{6,7},{7,6},{8,9},{9,8},{10,11... | collective-permute-start | bytes 393224 | tf_op jit(solution)/shard_map/ppermute | solution.py:497
  26.2 1.9 %collective-permute-start.12 = (f32[8,256]{1,0:T(8,128)S(1)}, f32[8,256]{1,0:T(8,128)S(1)}, u32[]{:S(2)}, u32[]{:S(2)}) collective-permute-start(f32[8,256]{1,0:T(8,128)S(1)} %get-tuple-element.83.norm_ref), channel_id=1, source_target_pairs={{0,1},{1,0},{2,3},{3,2},{4,5},{5,4},{6,7},{7,6},{8,9},{9,8},{10,11... | collective-permute-start | bytes 24584 | tf_op jit(solution)/shard_map/ppermute | solution.py:497
  27.7 2.7 %collective-permute-start.13 = (bf16[8,256,256]{2,1,0:T(8,128)(2,1)S(1)}, bf16[8,256,256]{2,1,0:T(8,128)(2,1)S(1)}, u32[]{:S(2)}, u32[]{:S(2)}) collective-permute-start(bf16[8,256,256]{2,1,0:T(8,128)(2,1)S(1)} %get-tuple-element.88.low_ref.refs_0_), channel_id=1, source_target_pairs={{0,1},{1,0},{2,3},{3,2},{4,5},{5,4},{6,7},{7,6},{8,9},{9,8},{10,11... | collective-permute-start | bytes 3145736 | tf_op jit(solution)/shard_map/ppermute | solution.py:497
  29.1 3.2 %collective-permute-start.14 = (bf16[8,256,256]{2,1,0:T(8,128)(2,1)S(1)}, bf16[8,256,256]{2,1,0:T(8,128)(2,1)S(1)}, u32[]{:S(2)}, u32[]{:S(2)}) collective-permute-start(bf16[8,256,256]{2,1,0:T(8,128)(2,1)S(1)} %received_rights.3.high_ref.refs_2_), channel_id=1, source_target_pairs={{0,1},{1,0},{2,3},{3,2},{4,5},{5,4},{6,7},{7,6},{8,9},{9,8},{10,11... | collective-permute-start | bytes 3145736 | tf_op jit(solution)/shard_map/ppermute | solution.py:497
  32.3 6.6 %copy-start = (f32[1,64,16,256]{3,2,1,0:T(8,128)S(1)}, f32[1,64,16,256]{3,2,1,0:T(8,128)}, u32[]{:S(2)}) copy-start(f32[1,64,16,256]{3,2,1,0:T(8,128)} %param.5) | copy-start | bytes 3145732
  37.2 3.7 %collective-permute-start.15 = (f32[8,256]{1,0:T(8,128)S(1)}, f32[8,256]{1,0:T(8,128)S(1)}, u32[]{:S(2)}, u32[]{:S(2)}) collective-permute-start(f32[8,256]{1,0:T(8,128)S(1)} %residual_high.1.share_ref.refs_0_), channel_id=1, source_target_pairs={{0,2},{1,3},{2,0},{3,1},{4,6},{5,7},{6,4},{7,5},{8,10},{9,11},{10,... | collective-permute-start | bytes 24584 | tf_op jit(solution)/shard_map/ppermute | solution.py:510
  38.9 2.0 %collective-permute-start.16 = (f32[8,256]{1,0:T(8,128)S(1)}, f32[8,256]{1,0:T(8,128)S(1)}, u32[]{:S(2)}, u32[]{:S(2)}) collective-permute-start(f32[8,256]{1,0:T(8,128)S(1)} %residual_high.1.share_ref.refs_0_), channel_id=1, source_target_pairs={{0,1},{1,0},{2,3},{3,2},{4,5},{5,4},{6,7},{7,6},{8,9},{9,8},{10,11... | collective-permute-start | bytes 24584 | tf_op jit(solution)/shard_map/ppermute | solution.py:497
  40.9 1.2 %collective-permute-start.17 = (f32[8,256]{1,0:T(8,128)S(1)}, f32[8,256]{1,0:T(8,128)S(1)}, u32[]{:S(2)}, u32[]{:S(2)}) collective-permute-start(f32[8,256]{1,0:T(8,128)S(1)} %collective-permute-done.15.refs_2_), channel_id=1, source_target_pairs={{0,1},{1,0},{2,3},{3,2},{4,5},{5,4},{6,7},{7,6},{8,9},{9,8},{10,11... | collective-permute-start | bytes 24584 | tf_op jit(solution)/shard_map/ppermute | solution.py:497

commit v18 on v17

--- a/solution.py
+++ b/solution.py
@@ -255,49 +255,56 @@
     turn(right_ref, rotated_ref, turned_ref)
 
 
-def last_kernel(count, *refs):
-    right_ref, kron_ref, columns_ref = refs[count : count + 3]
-    out_ref, rotated_ref, turned_ref = refs[-3:]
-    there_kernel(*refs[:count], right_ref, kron_ref, turned_ref, rotated_ref)
-    blocks = list(refs[count + 3 : -3]) + [turned_ref]
-
-    def lefts(p, carry):
-        stack = jnp.concatenate([block[p] for block in blocks], axis=0)
-        out_ref[p] = jnp.dot(columns_ref[...], stack, preferred_element_type=F32)
-        return carry
-
-    lax.fori_loop(0, out_ref.shape[0], lefts, 0, unroll=out_ref.shape[0])
-
-
-def rotate_kernel(spots, rows, chips, *refs):
-    pieces = refs[: len(spots)]
-    kron_ref = refs[len(spots)]
-    rotated_ref, whole_ref, sems = refs[-3:]
+def assemble(spots, rows, chips, pieces, whole_ref, sems):
     states = whole_ref.shape[0]
     copies = []
-    bases = [row_of(spot, rows, chips) for spot in spots]
-    for at, piece in zip(bases, pieces):
+    for spot, piece in zip(spots, pieces):
+        at = row_of(spot, rows, chips)
         for i in range(piece.shape[0] // states):
             target = whole_ref.at[:, pl.ds(pl.multiple_of(at + i * TILE, TILE), TILE), :]
             source = piece.at[i * states : (i + 1) * states]
             copies.append(pltpu.make_async_copy(source, target, sems.at[len(copies)]))
             copies[-1].start()
-    for at, piece in zip(bases, pieces):
-        mix_sites(piece, kron_ref, rotated_ref, at)
+    return copies
+
+
+def last_kernel(count, spots, rows, chips, *refs):
+    far = refs[: len(spots)]
+    right_ref, kron_ref, columns_ref = refs[len(spots) : len(spots) + 3]
+    out_ref, whole_ref, rotated_ref, turned_ref, sems = refs[-5:]
+    copies = assemble(spots, rows, chips, far, whole_ref, sems)
+    there_kernel(*far[:count], right_ref, kron_ref, turned_ref, rotated_ref)
+    blocks = list(refs[len(spots) + 3 : -5]) + [turned_ref]
+
+    def lefts(p, carry):
+        stack = jnp.concatenate([block[p] for block in blocks], axis=0)
+        out_ref[p] = jnp.dot(columns_ref[...], stack, preferred_element_type=F32)
+        return carry
+
+    lax.fori_loop(0, out_ref.shape[0], lefts, 0, unroll=out_ref.shape[0])
     for copy in copies:
         copy.wait()
 
 
-def lefts_kernel(spots, rows, chips, *refs):
+def rotate_kernel(spots, rows, chips, *refs):
+    pieces = refs[: len(spots)]
+    kron_ref, rotated_ref = refs[len(spots)], refs[-1]
+    for spot, piece in zip(spots, pieces):
+        mix_sites(piece, kron_ref, rotated_ref, row_of(spot, rows, chips))
+
+
+def lefts_kernel(spots, here_spots, rows, chips, *refs):
     count = len(spots)
     packed_ref, norm_before_ref = refs[count + 3 : count + 5]
+    here = refs[count + 5 : count + 5 + len(here_spots)]
     mixed_ref, norm_ref, rotated_ref, whole_ref, left_ref, sems = refs[-6:]
     terms, states, width, _ = rotated_ref.shape
+    copies = assemble(here_spots, rows, chips, here, whole_ref, sems)
     lines = packed_ref[terms * width : terms * width + TILE, :].astype(F32)
     norm = lines[terms : terms + 1] + lines[terms + 1 : terms + 2] + lines[terms + 2 : terms + 3]
     norm_ref[...] = norm_before_ref[...] + jnp.concatenate([norm, norm], axis=1)
     unpack_symmetric(packed_ref, left_ref)
-    rotate_kernel(spots, rows, chips, *refs[: count + 1], rotated_ref, whole_ref, sems)
+    rotate_kernel(spots, rows, chips, *refs[: count + 1], rotated_ref)
 
     def lefts(p, carry):
         for k in range(terms):
@@ -306,6 +313,8 @@
         return carry
 
     lax.fori_loop(0, states, lefts, 0, unroll=states)
+    for copy in copies:
+        copy.wait()
 
 
 def rights_kernel(start, stop, packed_ref, mixed_ref, before_ref, keep_ref, partial_ref, *refs):
@@ -331,14 +340,15 @@
     count, width, _ = res_ref.shape
     terms = left_ref.shape[0]
     zero = jnp.zeros((8, width), F32)
+    shift_keep = shift * keep
 
     def lefts(n, sums):
         square, product = sums
         for row in range(0, width, STRIP):
             strip = pl.ds(row, STRIP)
-            held = whole_ref[start + n, strip, :].astype(F32) * keep
+            held = whole_ref[start + n, strip, :].astype(F32)
             sigma = mine_ref[n, strip, :].astype(F32) + other_ref[n, strip, :].astype(F32)
-            residual = sigma - shift * held
+            residual = sigma - shift_keep * held
             res_ref[n, strip, :] = residual.astype(BF16)
             square = square + fold(residual * residual, width)
             product = product + fold(sigma * held, width)
@@ -614,15 +624,17 @@
     def rotate(spots, pieces, kron, before):
         return pl.pallas_call(
             functools.partial(rotate_kernel, spots, rows, chips),
-            out_shape=(rotated_bf, whole_bf),
+            out_shape=rotated_bf,
             in_specs=[vmem] * (len(pieces) + 1) + [anywhere] * len(before),
-            out_specs=(vmem, vmem),
-            scratch_shapes=[pltpu.SemaphoreType.DMA((sum(spot[3] for spot in spots) // TILE,))],
+            out_specs=vmem,
             input_output_aliases={len(pieces) + 1 + n: n for n in range(len(before))},
             compiler_params=params(),
             cost_estimate=part_cost,
             name="rotate_crossed" if before else "rotate_here",
         )(*pieces, kron, *before)
+
+    def tiles(spots):
+        return pltpu.SemaphoreType.DMA((sum(spot[3] for spot in spots) // TILE,))
 
     def relayed(blocks):
         return [piece for block in blocks for piece in (block, to_sibling(block))]
@@ -649,7 +661,7 @@
         for crossing in chunk_hops[1:-1]:
             crossed, turned = lax.optimization_barrier((crossing[1:], turned))
             mid_pieces += relayed(crossed)
-        turned = rotate(mid_spots, mid_pieces, kron, turned)
+        turned = rotate(mid_spots, mid_pieces, kron, (turned,))
         crossed, turned, parts[0] = lax.optimization_barrier((chunk_hops[-1][1:], turned, parts[0]))
         last_pieces = relayed(crossed)
         mid_rotated, mid_turned = buffers(mid_spots)
@@ -668,16 +680,17 @@
     else:
         last_pieces = relayed(firsts)
     last_rotated, last_turned = buffers(far_spots[-1])
-    partial = pl.pallas_call(
-        functools.partial(last_kernel, len(last_pieces)),
-        out_shape=whole_f32,
-        in_specs=[vmem] * (len(last_pieces) + 3 + len(parts)),
-        out_specs=vmem,
-        scratch_shapes=[pltpu.VMEM(last_rotated, BF16), pltpu.VMEM(last_turned, BF16)],
+    all_spots = far_spots[-1] + mid_spots
+    partial, vector = pl.pallas_call(
+        functools.partial(last_kernel, len(last_pieces), all_spots, rows, chips),
+        out_shape=(whole_f32, whole_bf),
+        in_specs=[vmem] * (len(all_spots) + 3 + len(parts)),
+        out_specs=(vmem, vmem),
+        scratch_shapes=[pltpu.VMEM(last_rotated, BF16), pltpu.VMEM(last_turned, BF16), tiles(all_spots)],
         compiler_params=params(),
         cost_estimate=part_cost,
         name="apply_rows_last",
-    )(*last_pieces, right, kron_own, columns, *parts)
+    )(*last_pieces, *mid_pieces, right, kron_own, columns, *parts)
     norm = norm_part
     for hop in hops[1:]:
         if hop > 1:
@@ -685,22 +698,19 @@
             kron = spread(block)
             turned = rotate(here_spots, here_pieces, kron, ())
             if mid_spots:
-                turned = rotate(mid_spots, mid_pieces, kron, turned)
+                turned = rotate(mid_spots, mid_pieces, kron, (turned,))
         left_far, partial = lax.optimization_barrier((lefts[hop], partial))
         mixed, norm, _, vector = pl.pallas_call(
-            functools.partial(lefts_kernel, far_spots[-1], rows, chips),
+            functools.partial(lefts_kernel, far_spots[-1], here_spots, rows, chips),
             out_shape=(jax.ShapeDtypeStruct((states, width, terms * width), BF16), tile, rotated_bf, whole_bf),
-            in_specs=[vmem] * (len(last_pieces) + 1) + [anywhere] * 2 + [vmem] * 2,
+            in_specs=[vmem] * (len(last_pieces) + 1) + [anywhere] * 2 + [vmem] * (2 + len(here_pieces)),
             out_specs=(vmem,) * 4,
-            scratch_shapes=[
-                square,
-                pltpu.SemaphoreType.DMA((sum(spot[3] for spot in far_spots[-1]) // TILE,)),
-            ],
+            scratch_shapes=[square, tiles(here_spots)],
             input_output_aliases={len(last_pieces) + 1: 2, len(last_pieces) + 2: 3},
             compiler_params=params(),
             cost_estimate=cost(stage_flops, 12 * states * width * width),
             name="received_lefts",
-        )(*last_pieces, kron, *turned, left_far, norm)
+        )(*last_pieces, kron, turned, vector, left_far, norm, *here_pieces)
         last = hop == hops[-1]
         right_far = rights[hop]
         parts = []

time: 44.3 us -> 44.1 us (level)
  no operation moved by 1% of the time
where the time goes in v18:
time: 44.1 us; the launch traced here: 43.5 us
  Pallas kernels  24.8 us (56%)
  starting transfers between devices  11.8 us (27%)
  waiting for transfers between devices  5.27 us (12%)
  between operations  1.66 us (4%)
    ppermute x5, starting transfers between devices, to_next_chip(): lax.ppermute(block, 'term', [(i, (i + CORES) % members) for i in range(me...  6.49 us
    pallas_call x1, Pallas kernels, shards(): pl.pallas_call(functools.partial(high_kernel, scale, members), out_shape=...  4.78 us
    pallas_call x1, Pallas kernels, shards(): pl.pallas_call(functools.partial(lefts_kernel, far_spots[-1], here_spots,...  2.69 us
    ppermute x11, waiting for transfers between devices, to_sibling(): return lax.ppermute(block, 'term', [(i, i ^ 1) for i in range(members)])  2.65 us
    pallas_call x1, Pallas kernels, shards(): pl.pallas_call(functools.partial(last_kernel, len(last_pieces), all_spots...  2.47 us
    ppermute x11, starting transfers between devices, to_sibling(): return lax.ppermute(block, 'term', [(i, i ^ 1) for i in range(members)])  2.45 us
    pallas_call x2, Pallas kernels, shards(): pl.pallas_call(functools.partial(rights_kernel, start, stop), out_shape=(...  2.26 us
    pallas_call x2, Pallas kernels, rotate(): pl.pallas_call(functools.partial(rotate_kernel, spots, rows, chips), out_...  2.1 us
  transfers between devices with their start and end apart: 18, of which 5 were waited for; matrix products, arithmetic and copies ran while one was open for 0% of the time, Pallas kernels for 40%

profile of v18, /device:TPU:0, one launch (start us, length us, event | category | flops | bytes accessed | tf_op | source)
XLA Modules:
  0.0 43.5 jit_solution(10175064347233602814)
XLA Ops:
  0.6 1.3 %first_chunk.1 = (bf16[33,16,256]{2,1,0:T(8,128)(2,1)S(1)}, f32[8,256]{1,0:T(8,128)S(1)}, bf16[784,128]{1,0:T(8,128)(2,1)S(1)}) custom-call(f32[64,16,256]{2,1,0:T(8,128)} %bitcast.7, bf16[3,16,16]{2,1,0:T(8,128)(2,1)} %bitcast.12, bf16[3,256,256]{2,1,0:T(8,128)(2,1)} %bitcast.10), custom_call_target="tpu_custom_call" | custom-call | flops 5242 | bytes 7864 | tf_op jit(solution)/shard_map/first_chunk/pallas_call | solution.py:530
  2.0 0.5 %collective-permute-start = (bf16[33,16,256]{2,1,0:T(8,128)(2,1)S(1)}, bf16[33,16,256]{2,1,0:T(8,128)(2,1)S(1)}, u32[]{:S(2)}, u32[]{:S(2)}) collective-permute-start(bf16[33,16,256]{2,1,0:T(8,128)(2,1)S(1)} %get-tuple-element.47.chunk_ref.refs_0_.refs_7_), channel_id=1, source_target_pairs={{0,1},{1,0},{2,3},{3,2},{4,5},{5,4},{6,7},{7,6},{8,9},{9,8},{10,11... | collective-permute-start | bytes 811016 | tf_op jit(solution)/shard_map/ppermute | solution.py:507
  2.5 2.6 %collective-permute-start.2 = (bf16[33,16,256]{2,1,0:T(8,128)(2,1)S(1)}, bf16[33,16,256]{2,1,0:T(8,128)(2,1)S(1)}, u32[]{:S(2)}, u32[]{:S(2)}) collective-permute-start(bf16[33,16,256]{2,1,0:T(8,128)(2,1)S(1)} %get-tuple-element.47.chunk_ref.refs_0_.refs_7_), channel_id=1, source_target_pairs={{0,2},{1,3},{2,0},{3,1},{4,6},{5,7},{6,4},{7,5},{8,10},{9,11},{10,... | collective-permute-start | bytes 811016 | tf_op jit(solution)/shard_map/ppermute | solution.py:510
  5.1 1.3 %collective-permute-start.7 = (bf16[784,128]{1,0:T(8,128)(2,1)S(1)}, bf16[784,128]{1,0:T(8,128)(2,1)S(1)}, u32[]{:S(2)}, u32[]{:S(2)}) collective-permute-start(bf16[784,128]{1,0:T(8,128)(2,1)S(1)} %get-tuple-element.56), channel_id=1, source_target_pairs={{4,0},{8,4},{12,8},{16,12},{20,16},{24,20},{28,24},{5,1},{9,5},{13... | collective-permute-start | bytes 602120 | tf_op jit(solution)/shard_map/ppermute | solution.py:579
  7.0 0.0 collective-permute-done.refs_3_.refs_10_
  7.0 1.3 %prepare.1 = (f32[8,256]{1,0:T(8,128)S(1)}, f32[8,256]{1,0:T(8,128)S(1)}, bf16[784,128]{1,0:T(8,128)(2,1)S(1)}, bf16[3,256,256]{2,1,0:T(8,128)(2,1)S(1)}, bf16[1...) custom-call(s32[1,1]{1,0:T(1,128)} %bitcast.6.rank_ref, f32[8,256]{1,0:T(8,128)S(1)} %get-tuple-element.48.squares_ref, ...), custom_call_target="tpu_custom_call" | custom-call | flops 10485 | bytes 15728 | tf_op jit(solution)/shard_map/prepare/pallas_call | solution.py:547
  8.4 0.2 collective-permute-start.4
  8.6 0.3 collective-permute-start.3
  9.0 0.0 collective-permute-start.6
  9.0 0.4 spread_site.2.refs_6_.refs_5_.refs_7_.kron_ref
  9.4 0.4 collective-permute-done.4.refs_5_.refs_12_
  9.8 1.7 %collective-permute-start.1 = (bf16[16,16,256]{2,1,0:T(8,128)(2,1)S(1)}, bf16[16,16,256]{2,1,0:T(8,128)(2,1)S(1)}, u32[]{:S(2)}, u32[]{:S(2)}) collective-permute-start(bf16[16,16,256]{2,1,0:T(8,128)(2,1)S(1)} %get-tuple-element.50.refs_2_.refs_9_), channel_id=1, source_target_pairs={{0,2},{1,3},{2,0},{3,1},{4,6},{5,7},{6,4},{7,5},{8,10},{9,11},{10,... | collective-permute-start | bytes 393224 | tf_op jit(solution)/shard_map/ppermute | solution.py:510
  11.4 0.0 collective-permute-done.3.refs_4_.refs_11_
  11.5 0.4 collective-permute-start.10
  11.8 1.0 %rotate_own.1 = (bf16[3,16,128,256]{3,2,1,0:T(8,128)(2,1)S(1)}, bf16[256,768]{1,0:T(8,128)(2,1)S(1)}) custom-call(bf16[33,16,256]{2,1,0:T(8,128)(2,1)S(1)} %get-tuple-element.47.chunk_ref.refs_0_.refs_7_, bf16[16,16,256]{2,1,0:T(8,128)(2,1)S(1)} %get-tuple-element.51.refs_1_.refs_8_, bf16[16,16,256]{2,1,0:T(8,128)(2,1)S(1)} %get-tuple-element.50.refs_2_.refs_9_, ...), custom_call_target="tpu_custom_call" | custom-call | flops 16106127 | bytes 83886 | tf_op jit(solution)/shard_map/rotate_own/pallas_call | solution.py:611
  12.8 0.0 collective-permute-done.2.chunk_ref.refs_0_.refs_2_
  12.8 0.1 collective-permute-start.5
  12.9 0.4 spread_site.3.refs_6_.refs_4_.refs_2_
  13.3 1.2 %rotate_here.1.refs_5_ = bf16[3,16,256,256]{3,2,1,0:T(8,128)(2,1)S(1)} custom-call(bf16[33,16,256]{2,1,0:T(8,128)(2,1)S(1)} %get-tuple-element.47.chunk_ref.refs_0_.refs_7_, bf16[16,16,256]{2,1,0:T(8,128)(2,1)S(1)} %get-tuple-element.51.refs_1_.refs_8_, bf16[16,16,256]{2,1,0:T(8,128)(2,1)S(1)} %get-tuple-element.50.refs_2_.refs_9_, ...), custom_call_target="tpu_custom_call" | custom-call | flops 16106127 | bytes 83886 | tf_op jit(solution)/shard_map/rotate_here/pallas_call | solution.py:625
  14.5 0.0 collective-permute-done.7
  14.5 0.9 %collective-permute-done.6.refs_2_.refs_4_ = bf16[16,16,256]{2,1,0:T(8,128)(2,1)S(1)} collective-permute-done((bf16[16,16,256]{2,1,0:T(8,128)(2,1)S(1)}, bf16[16,16,256]{2,1,0:T(8,128)(2,1)S(1)}, u32[]{:S(2)}, u32[]{:S(2)}) %collective-permute-start.6) | collective-permute-done | bytes 131104 | tf_op jit(solution)/shard_map/ppermute | solution.py:510
  15.4 0.0 collective-permute-start.8
  15.4 1.9 %collective-permute-start.11 = (bf16[784,128]{1,0:T(8,128)(2,1)S(1)}, bf16[784,128]{1,0:T(8,128)(2,1)S(1)}, u32[]{:S(2)}, u32[]{:S(2)}) collective-permute-start(bf16[784,128]{1,0:T(8,128)(2,1)S(1)} %broadcast_select_fusion.packed_ref), channel_id=1, source_target_pairs={{0,2},{1,3},{2,0},{3,1},{4,6},{5,7},{6,4},{7,5},{8,10},{9,11},{10,... | collective-permute-start | bytes 602120 | tf_op jit(solution)/shard_map/ppermute | solution.py:510
  17.3 1.2 %apply_rows_here.1 = (bf16[16,384,256]{2,1,0:T(8,128)(2,1)S(1)}, bf16[3,256,256]{2,1,0:T(8,128)(2,1)S(1)}) custom-call(bf16[3,16,128,256]{3,2,1,0:T(8,128)(2,1)S(1)} %get-tuple-element.60.rotated_ref, bf16[784,128]{1,0:T(8,128)(2,1)S(1)} %broadcast_select_fusion.packed_ref, f32[8,256]{1,0:T(8,128)S(1)} %get-tuple-element.49.keep_ref), custom_call_target="tpu_custom_call" | custom-call | flops 16106127 | bytes 83886 | tf_op jit(solution)/shard_map/apply_rows_here/pallas_call | solution.py:648
  18.5 0.0 collective-permute-done.8.refs_3_.refs_5_
  18.5 0.0 collective-permute-done.5.refs_1_.refs_3_
  18.5 0.9 %rotate_crossed.1.refs_3_ = bf16[3,16,256,256]{3,2,1,0:T(8,128)(2,1)S(1)} custom-call(bf16[33,16,256]{2,1,0:T(8,128)(2,1)S(1)} %collective-permute-done.2.chunk_ref.refs_0_.refs_2_, bf16[33,16,256]{2,1,0:T(8,128)(2,1)S(1)} %collective-permute-done.5.refs_1_.refs_3_, ...), custom_call_target="tpu_custom_call", output_to_operand_aliasing={{}: (5, {})} | custom-call | flops 16106127 | bytes 83886 | tf_op jit(solution)/shard_map/rotate_crossed/pallas_call | solution.py:625
  19.4 0.0 collective-permute-done.1.refs_0_
  19.4 0.3 collective-permute-start.9
  19.7 1.4 %apply_rows_crossed.1.refs_10_ = bf16[16,288,256]{2,1,0:T(8,128)(2,1)S(1)} custom-call(bf16[33,16,256]{2,1,0:T(8,128)(2,1)S(1)} %collective-permute-done.2.chunk_ref.refs_0_.refs_2_, bf16[33,16,256]{2,1,0:T(8,128)(2,1)S(1)} %collective-permute-done.5.refs_1_.refs_3_, bf16[16,16,256]{2,1,0:T(8,128)(2,1)S(1)} %collective-permute-done.6.refs_2_.refs_4_, ...), custom_call_target="tpu_custom_call" | custom-call | flops 16106127 | bytes 83886 | tf_op jit(solution)/shard_map/apply_rows_crossed/pallas_call | solution.py:669
  21.1 0.0 collective-permute-done.9.refs_1_
  21.1 2.5 %apply_rows_last.1 = (f32[16,256,256]{2,1,0:T(8,128)S(1)}, bf16[16,256,256]{2,1,0:T(8,128)(2,1)S(1)}) custom-call(bf16[16,16,256]{2,1,0:T(8,128)(2,1)S(1)} %collective-permute-done.1.refs_0_, bf16[16,16,256]{2,1,0:T(8,128)(2,1)S(1)} %collective-permute-done.9.refs_1_, bf16[33,16,256]{2,1,0:T(8,128)(2,1)S(1)} %collective-permute-done.2.chunk_ref.refs_0_.refs_2_, ...), custom_call_target="tpu_custom_call" | custom-call | flops 16106127 | bytes 83886 | tf_op jit(solution)/shard_map/apply_rows_last/pallas_call | solution.py:684
  23.6 0.0 collective-permute-done.10.refs_5_
  23.6 2.7 %received_lefts.1 = (bf16[16,256,768]{2,1,0:T(8,128)(2,1)S(1)}, f32[8,256]{1,0:T(8,128)S(1)}, bf16[3,16,256,256]{3,2,1,0:T(8,128)(2,1)S(1)}, bf16[16,256,256]{2,1,0:T(8,128)(2,1)S(1)}) custom-call(bf16[16,16,256]{2,1,0:T(8,128)(2,1)S(1)} %collective-permute-done.1.refs_0_, ...), custom_call_target="tpu_custom_call", output_to_operand_aliasing={{2}: (3, {}), {3}: (4, {})} | custom-call | flops 16106127 | bytes 125829 | tf_op jit(solution)/shard_map/received_lefts/pallas_call | solution.py:703
  26.3 0.3 collective-permute-start.12
  26.7 0.0 collective-permute-done.11.packed_ref
  26.7 1.2 %received_rights.2 = (bf16[8,256,256]{2,1,0:T(8,128)(2,1)S(1)}, bf16[3,256,256]{2,1,0:T(8,128)(2,1)S(1)}) custom-call(bf16[784,128]{1,0:T(8,128)(2,1)S(1)} %collective-permute-done.11.packed_ref, bf16[16,256,768]{2,1,0:T(8,128)(2,1)S(1)} %get-tuple-element.74.mixed_ref, f32[16,256,256]{2,1,0:T(8,128)S(1)} %get-tuple-element.75.before_ref, ...), custom_call_target="tpu_custom_call" | custom-call | flops 8053063 | bytes 125829 | tf_op jit(solution)/shard_map/received_rights/pallas_call | solution.py:720
  27.9 0.3 collective-permute-start.13
  28.2 0.0 collective-permute-done.12.norm_other_ref
  28.2 1.0 %received_rights.3.high_ref.refs_2_ = bf16[8,256,256]{2,1,0:T(8,128)(2,1)S(1)} custom-call(bf16[3,256,256]{2,1,0:T(8,128)(2,1)S(1)} %get-tuple-element.81.packed_ref, bf16[16,256,768]{2,1,0:T(8,128)(2,1)S(1)} %get-tuple-element.74.mixed_ref, f32[16,256,256]{2,1,0:T(8,128)S(1)} %get-tuple-element.75.before_ref, f32[8,256]{1,0:T(8,128)S(1)} %get-tuple-element.49.keep_ref), custom_call_target="tpu_custom_call" | custom-call | flops 8053063 | bytes 125829 | tf_op jit(solution)/shard_map/received_rights/pallas_call | solution.py:720
  29.2 0.3 collective-permute-start.14
  29.6 1.0 %collective-permute-done.13.low_other_ref.refs_1_ = bf16[8,256,256]{2,1,0:T(8,128)(2,1)S(1)} collective-permute-done((bf16[8,256,256]{2,1,0:T(8,128)(2,1)S(1)}, bf16[8,256,256]{2,1,0:T(8,128)(2,1)S(1)}, u32[]{:S(2)}, u32[]{:S(2)}) %collective-permute-start.13) | collective-permute-done | bytes 1048608 | tf_op jit(solution)/shard_map/ppermute | solution.py:507
  30.6 1.8 %residual_low.1 = (bf16[8,256,256]{2,1,0:T(8,128)(2,1)S(1)}, bf16[3,8,256,256]{3,2,1,0:T(8,128)(2,1)S(1)}, f32[8,256]{1,0:T(8,128)S(1)}) custom-call(f32[8,256]{1,0:T(8,128)S(1)} %get-tuple-element.49.keep_ref, f32[8,256]{1,0:T(8,128)S(1)} %get-tuple-element.73.norm_ref, f32[8,256]{1,0:T(8,128)S(1)} %collective-permute-done.12.norm_other_ref, ...), custom_call_target="tpu_custom_call" | custom-call | flops 8053063 | bytes 31457 | tf_op jit(solution)/shard_map/residual_low/pallas_call | solution.py:739
  32.4 0.0 collective-permute-done.14.high_other_ref.refs_3_
  32.4 0.0 copy-start
  32.4 4.8 %residual_high.1.share_ref.refs_0_ = f32[8,256]{1,0:T(8,128)S(1)} custom-call(f32[8,256]{1,0:T(8,128)S(1)} %get-tuple-element.49.keep_ref, f32[8,256]{1,0:T(8,128)S(1)} %get-tuple-element.73.norm_ref, f32[8,256]{1,0:T(8,128)S(1)} %collective-permute-done.12.norm_other_ref, f32[8,256]{1,0:T(8,128)S(1)} %get-tuple-element.80.sums_ref, ...), custom_call_target="tpu_custom_call" | custom-call | flops 48318384 | bytes 62914 | tf_op jit(solution)/shard_map/residual_high/pallas_call | solution.py:748
  37.2 1.5 %collective-permute-start.15 = (f32[8,256]{1,0:T(8,128)S(1)}, f32[8,256]{1,0:T(8,128)S(1)}, u32[]{:S(2)}, u32[]{:S(2)}) collective-permute-start(f32[8,256]{1,0:T(8,128)S(1)} %residual_high.1.share_ref.refs_0_), channel_id=1, source_target_pairs={{0,2},{1,3},{2,0},{3,1},{4,6},{5,7},{6,4},{7,5},{8,10},{9,11},{10,... | collective-permute-start | bytes 24584 | tf_op jit(solution)/shard_map/ppermute | solution.py:520
  38.7 0.0 collective-permute-start.16
  38.7 0.0 copy-done
  38.7 0.5 %own_rows.1 = (f32[64,16,256]{2,1,0:T(8,128)S(1)}, f32[64,16,256]{2,1,0:T(8,128)S(1)}) custom-call(f32[8,256]{1,0:T(8,128)S(1)} %get-tuple-element.49.keep_ref, f32[8,256]{1,0:T(8,128)S(1)} %get-tuple-element.73.norm_ref, f32[8,256]{1,0:T(8,128)S(1)} %collective-permute-done.12.norm_other_ref, f32[8,256]{1,0:T(8,128)S(1)} %residual_high.1.share_ref.refs_0_, ...), custom_call_target="tpu_custom_call" | custom-call | flops 20971 | bytes 41943 | tf_op jit(solution)/shard_map/own_rows/pallas_call | solution.py:765
  39.2 1.7 %collective-permute-done.15.refs_2_ = f32[8,256]{1,0:T(8,128)S(1)} collective-permute-done((f32[8,256]{1,0:T(8,128)S(1)}, f32[8,256]{1,0:T(8,128)S(1)}, u32[]{:S(2)}, u32[]{:S(2)}) %collective-permute-start.15) | collective-permute-done | bytes 8224 | tf_op jit(solution)/shard_map/ppermute | solution.py:520
  40.9 0.0 collective-permute-start.17
  40.9 0.0 collective-permute-done.16.refs_1_
  40.9 1.2 %collective-permute-done.17.refs_3_ = f32[8,256]{1,0:T(8,128)S(1)} collective-permute-done((f32[8,256]{1,0:T(8,128)S(1)}, f32[8,256]{1,0:T(8,128)S(1)}, u32[]{:S(2)}, u32[]{:S(2)}) %collective-permute-start.17) | collective-permute-done | bytes 8224 | tf_op jit(solution)/shard_map/ppermute | solution.py:507
  42.1 1.3 %finish.1 = (f32[64,16,256]{2,1,0:T(8,128)}, f32[1]{0:T(128)}) custom-call(f32[64,16,256]{2,1,0:T(8,128)S(1)} %get-tuple-element.84.vector_ref, f32[64,16,256]{2,1,0:T(8,128)S(1)} %get-tuple-element.86.residual_ref, f32[8,256]{1,0:T(8,128)S(1)} %residual_high.1.share_ref.refs_0_, f32[8,256]{1,0:T(8,128)S(1)} %collective-permute-done.16.refs_1_, ...), custom_call_target="tpu_custom_call" | custom-call | flops 7864 | bytes 31457 | tf_op jit(solution)/shard_map/finish/pallas_call | solution.py:778
  (1 shorter events, 0.0 us)
Async XLA Ops:
  2.0 5.0 %collective-permute-start = (bf16[33,16,256]{2,1,0:T(8,128)(2,1)S(1)}, bf16[33,16,256]{2,1,0:T(8,128)(2,1)S(1)}, u32[]{:S(2)}, u32[]{:S(2)}) collective-permute-start(bf16[33,16,256]{2,1,0:T(8,128)(2,1)S(1)} %get-tuple-element.47.chunk_ref.refs_0_.refs_7_), channel_id=1, source_target_pairs={{0,1},{1,0},{2,3},{3,2},{4,5},{5,4},{6,7},{7,6},{8,9},{9,8},{10,11... | collective-permute-start | bytes 811016 | tf_op jit(solution)/shard_map/ppermute | solution.py:507
  2.5 10.3 %collective-permute-start.2 = (bf16[33,16,256]{2,1,0:T(8,128)(2,1)S(1)}, bf16[33,16,256]{2,1,0:T(8,128)(2,1)S(1)}, u32[]{:S(2)}, u32[]{:S(2)}) collective-permute-start(bf16[33,16,256]{2,1,0:T(8,128)(2,1)S(1)} %get-tuple-element.47.chunk_ref.refs_0_.refs_7_), channel_id=1, source_target_pairs={{0,2},{1,3},{2,0},{3,1},{4,6},{5,7},{6,4},{7,5},{8,10},{9,11},{10,... | collective-permute-start | bytes 811016 | tf_op jit(solution)/shard_map/ppermute | solution.py:510
  5.1 9.4 %collective-permute-start.7 = (bf16[784,128]{1,0:T(8,128)(2,1)S(1)}, bf16[784,128]{1,0:T(8,128)(2,1)S(1)}, u32[]{:S(2)}, u32[]{:S(2)}) collective-permute-start(bf16[784,128]{1,0:T(8,128)(2,1)S(1)} %get-tuple-element.56), channel_id=1, source_target_pairs={{4,0},{8,4},{12,8},{16,12},{20,16},{24,20},{28,24},{5,1},{9,5},{13... | collective-permute-start | bytes 602120 | tf_op jit(solution)/shard_map/ppermute | solution.py:579
  8.4 1.4 %collective-permute-start.4 = (bf16[16,16,256]{2,1,0:T(8,128)(2,1)S(1)}, bf16[16,16,256]{2,1,0:T(8,128)(2,1)S(1)}, u32[]{:S(2)}, u32[]{:S(2)}) collective-permute-start(bf16[16,16,256]{2,1,0:T(8,128)(2,1)S(1)} %get-tuple-element.50.refs_2_.refs_9_), channel_id=1, source_target_pairs={{0,1},{1,0},{2,3},{3,2},{4,5},{5,4},{6,7},{7,6},{8,9},{9,8},{10,11... | collective-permute-start | bytes 393224 | tf_op jit(solution)/shard_map/ppermute | solution.py:507
  8.6 2.8 %collective-permute-start.3 = (bf16[16,16,256]{2,1,0:T(8,128)(2,1)S(1)}, bf16[16,16,256]{2,1,0:T(8,128)(2,1)S(1)}, u32[]{:S(2)}, u32[]{:S(2)}) collective-permute-start(bf16[16,16,256]{2,1,0:T(8,128)(2,1)S(1)} %get-tuple-element.51.refs_1_.refs_8_), channel_id=1, source_target_pairs={{0,1},{1,0},{2,3},{3,2},{4,5},{5,4},{6,7},{7,6},{8,9},{9,8},{10,11... | collective-permute-start | bytes 393224 | tf_op jit(solution)/shard_map/ppermute | solution.py:507
  9.0 6.4 %collective-permute-start.6 = (bf16[16,16,256]{2,1,0:T(8,128)(2,1)S(1)}, bf16[16,16,256]{2,1,0:T(8,128)(2,1)S(1)}, u32[]{:S(2)}, u32[]{:S(2)}) collective-permute-start(bf16[16,16,256]{2,1,0:T(8,128)(2,1)S(1)} %get-tuple-element.51.refs_1_.refs_8_), channel_id=1, source_target_pairs={{0,2},{1,3},{2,0},{3,1},{4,6},{5,7},{6,4},{7,5},{8,10},{9,11},{10,... | collective-permute-start | bytes 393224 | tf_op jit(solution)/shard_map/ppermute | solution.py:510
  9.8 9.6 %collective-permute-start.1 = (bf16[16,16,256]{2,1,0:T(8,128)(2,1)S(1)}, bf16[16,16,256]{2,1,0:T(8,128)(2,1)S(1)}, u32[]{:S(2)}, u32[]{:S(2)}) collective-permute-start(bf16[16,16,256]{2,1,0:T(8,128)(2,1)S(1)} %get-tuple-element.50.refs_2_.refs_9_), channel_id=1, source_target_pairs={{0,2},{1,3},{2,0},{3,1},{4,6},{5,7},{6,4},{7,5},{8,10},{9,11},{10,... | collective-permute-start | bytes 393224 | tf_op jit(solution)/shard_map/ppermute | solution.py:510
  11.5 12.2 %collective-permute-start.10 = (bf16[784,128]{1,0:T(8,128)(2,1)S(1)}, bf16[784,128]{1,0:T(8,128)(2,1)S(1)}, u32[]{:S(2)}, u32[]{:S(2)}) collective-permute-start(bf16[784,128]{1,0:T(8,128)(2,1)S(1)} %get-tuple-element.69), channel_id=1, source_target_pairs={{0,2},{1,3},{2,0},{3,1},{4,6},{5,7},{6,4},{7,5},{8,10},{9,11},{10,... | collective-permute-start | bytes 602120 | tf_op jit(solution)/shard_map/ppermute | solution.py:510
  12.8 5.7 %collective-permute-start.5 = (bf16[33,16,256]{2,1,0:T(8,128)(2,1)S(1)}, bf16[33,16,256]{2,1,0:T(8,128)(2,1)S(1)}, u32[]{:S(2)}, u32[]{:S(2)}) collective-permute-start(bf16[33,16,256]{2,1,0:T(8,128)(2,1)S(1)} %collective-permute-done.2.chunk_ref.refs_0_.refs_2_), channel_id=1, source_target_pairs={{0,1},{1,0},{2,3},{3,2},{4,5},{5,4},{6,7},{7,6},{8,9},{9,8},{10,11... | collective-permute-start | bytes 811016 | tf_op jit(solution)/shard_map/ppermute | solution.py:507
  15.4 3.1 %collective-permute-start.8 = (bf16[16,16,256]{2,1,0:T(8,128)(2,1)S(1)}, bf16[16,16,256]{2,1,0:T(8,128)(2,1)S(1)}, u32[]{:S(2)}, u32[]{:S(2)}) collective-permute-start(bf16[16,16,256]{2,1,0:T(8,128)(2,1)S(1)} %collective-permute-done.6.refs_2_.refs_4_), channel_id=1, source_target_pairs={{0,1},{1,0},{2,3},{3,2},{4,5},{5,4},{6,7},{7,6},{8,9},{9,8},{10,11... | collective-permute-start | bytes 393224 | tf_op jit(solution)/shard_map/ppermute | solution.py:507
  15.4 11.2 %collective-permute-start.11 = (bf16[784,128]{1,0:T(8,128)(2,1)S(1)}, bf16[784,128]{1,0:T(8,128)(2,1)S(1)}, u32[]{:S(2)}, u32[]{:S(2)}) collective-permute-start(bf16[784,128]{1,0:T(8,128)(2,1)S(1)} %broadcast_select_fusion.packed_ref), channel_id=1, source_target_pairs={{0,2},{1,3},{2,0},{3,1},{4,6},{5,7},{6,4},{7,5},{8,10},{9,11},{10,... | collective-permute-start | bytes 602120 | tf_op jit(solution)/shard_map/ppermute | solution.py:510
  19.4 1.7 %collective-permute-start.9 = (bf16[16,16,256]{2,1,0:T(8,128)(2,1)S(1)}, bf16[16,16,256]{2,1,0:T(8,128)(2,1)S(1)}, u32[]{:S(2)}, u32[]{:S(2)}) collective-permute-start(bf16[16,16,256]{2,1,0:T(8,128)(2,1)S(1)} %collective-permute-done.1.refs_0_), channel_id=1, source_target_pairs={{0,1},{1,0},{2,3},{3,2},{4,5},{5,4},{6,7},{7,6},{8,9},{9,8},{10,11... | collective-permute-start | bytes 393224 | tf_op jit(solution)/shard_map/ppermute | solution.py:507
  26.3 1.9 %collective-permute-start.12 = (f32[8,256]{1,0:T(8,128)S(1)}, f32[8,256]{1,0:T(8,128)S(1)}, u32[]{:S(2)}, u32[]{:S(2)}) collective-permute-start(f32[8,256]{1,0:T(8,128)S(1)} %get-tuple-element.73.norm_ref), channel_id=1, source_target_pairs={{0,1},{1,0},{2,3},{3,2},{4,5},{5,4},{6,7},{7,6},{8,9},{9,8},{10,11... | collective-permute-start | bytes 24584 | tf_op jit(solution)/shard_map/ppermute | solution.py:507
  27.9 2.7 %collective-permute-start.13 = (bf16[8,256,256]{2,1,0:T(8,128)(2,1)S(1)}, bf16[8,256,256]{2,1,0:T(8,128)(2,1)S(1)}, u32[]{:S(2)}, u32[]{:S(2)}) collective-permute-start(bf16[8,256,256]{2,1,0:T(8,128)(2,1)S(1)} %get-tuple-element.78.low_ref.refs_0_), channel_id=1, source_target_pairs={{0,1},{1,0},{2,3},{3,2},{4,5},{5,4},{6,7},{7,6},{8,9},{9,8},{10,11... | collective-permute-start | bytes 3145736 | tf_op jit(solution)/shard_map/ppermute | solution.py:507
  29.2 3.2 %collective-permute-start.14 = (bf16[8,256,256]{2,1,0:T(8,128)(2,1)S(1)}, bf16[8,256,256]{2,1,0:T(8,128)(2,1)S(1)}, u32[]{:S(2)}, u32[]{:S(2)}) collective-permute-start(bf16[8,256,256]{2,1,0:T(8,128)(2,1)S(1)} %received_rights.3.high_ref.refs_2_), channel_id=1, source_target_pairs={{0,1},{1,0},{2,3},{3,2},{4,5},{5,4},{6,7},{7,6},{8,9},{9,8},{10,11... | collective-permute-start | bytes 3145736 | tf_op jit(solution)/shard_map/ppermute | solution.py:507
  32.4 6.3 %copy-start = (f32[1,64,16,256]{3,2,1,0:T(8,128)S(1)}, f32[1,64,16,256]{3,2,1,0:T(8,128)}, u32[]{:S(2)}) copy-start(f32[1,64,16,256]{3,2,1,0:T(8,128)} %param.5) | copy-start | bytes 3145732
  37.2 3.7 %collective-permute-start.15 = (f32[8,256]{1,0:T(8,128)S(1)}, f32[8,256]{1,0:T(8,128)S(1)}, u32[]{:S(2)}, u32[]{:S(2)}) collective-permute-start(f32[8,256]{1,0:T(8,128)S(1)} %residual_high.1.share_ref.refs_0_), channel_id=1, source_target_pairs={{0,2},{1,3},{2,0},{3,1},{4,6},{5,7},{6,4},{7,5},{8,10},{9,11},{10,... | collective-permute-start | bytes 24584 | tf_op jit(solution)/shard_map/ppermute | solution.py:520
  38.7 2.2 %collective-permute-start.16 = (f32[8,256]{1,0:T(8,128)S(1)}, f32[8,256]{1,0:T(8,128)S(1)}, u32[]{:S(2)}, u32[]{:S(2)}) collective-permute-start(f32[8,256]{1,0:T(8,128)S(1)} %residual_high.1.share_ref.refs_0_), channel_id=1, source_target_pairs={{0,1},{1,0},{2,3},{3,2},{4,5},{5,4},{6,7},{7,6},{8,9},{9,8},{10,11... | collective-permute-start | bytes 24584 | tf_op jit(solution)/shard_map/ppermute | solution.py:507
  40.9 1.2 %collective-permute-start.17 = (f32[8,256]{1,0:T(8,128)S(1)}, f32[8,256]{1,0:T(8,128)S(1)}, u32[]{:S(2)}, u32[]{:S(2)}) collective-permute-start(f32[8,256]{1,0:T(8,128)S(1)} %collective-permute-done.15.refs_2_), channel_id=1, source_target_pairs={{0,1},{1,0},{2,3},{3,2},{4,5},{5,4},{6,7},{7,6},{8,9},{9,8},{10,11... | collective-permute-start | bytes 24584 | tf_op jit(solution)/shard_map/ppermute | solution.py:507

commit v19 on v16

--- a/solution.py
+++ b/solution.py
@@ -236,10 +236,9 @@
 def turn(right_ref, rotated_ref, turned_ref):
     terms, states, count, width = rotated_ref.shape
     for k in range(terms):
-        for n in range(0, states, 8):
-            source = rotated_ref[k, n : n + 8].reshape(8 * count, width)
-            turned = jnp.dot(source, right_ref[k], preferred_element_type=F32).astype(BF16)
-            turned_ref[n : n + 8, k * count : (k + 1) * count, :] = turned.reshape(8, count, width)
+        source = rotated_ref[k].reshape(states * count, width)
+        turned = jnp.dot(source, right_ref[k], preferred_element_type=F32).astype(BF16)
+        turned_ref[:, k * count : (k + 1) * count, :] = turned.reshape(states, count, width)
 
 
 def here_kernel(rotated_ref, packed_ref, keep_ref, turned_ref, right_ref):

time: 44 us -> 44.4 us (level)
  transfers between devices with their start and end apart: 18 -> 18, of which waited for: 6 -> 6; matrix products, arithmetic and copies ran while one was open for 0% -> 0% of each run, Pallas kernels for 39% -> 40%
where the time goes in v19:
time: 44.4 us; the launch traced here: 44.2 us
  Pallas kernels  25 us (56%)
  starting transfers between devices  11.9 us (27%)
  waiting for transfers between devices  5.6 us (13%)
  between operations  1.64 us (4%)
    ppermute x5, starting transfers between devices, to_next_chip(): lax.ppermute(block, 'term', [(i, (i + CORES) % members) for i in range(me...  6.8 us
    pallas_call x1, Pallas kernels, shards(): pl.pallas_call(functools.partial(high_kernel, scale, members), out_shape=...  4.76 us
    pallas_call x1, Pallas kernels, shards(): pl.pallas_call(functools.partial(lefts_kernel, far_spots[-1], rows, chips...  2.6 us
    ppermute x11, waiting for transfers between devices, to_sibling(): return lax.ppermute(block, 'term', [(i, i ^ 1) for i in range(members)])  2.51 us
    pallas_call x2, Pallas kernels, rotate(): pl.pallas_call(functools.partial(rotate_kernel, spots, rows, chips), out_...  2.48 us
    ppermute x11, starting transfers between devices, to_sibling(): return lax.ppermute(block, 'term', [(i, i ^ 1) for i in range(members)])  2.38 us
    pallas_call x1, Pallas kernels, shards(): pl.pallas_call(functools.partial(last_kernel, len(last_pieces)), out_shap...  2.28 us
    pallas_call x2, Pallas kernels, shards(): pl.pallas_call(functools.partial(rights_kernel, start, stop), out_shape=(...  2.21 us
  transfers between devices with their start and end apart: 18, of which 6 were waited for; matrix products, arithmetic and copies ran while one was open for 0% of the time, Pallas kernels for 40%

profile of v19, /device:TPU:0, one launch (start us, length us, event | category | flops | bytes accessed | tf_op | source)
XLA Modules:
  0.0 44.2 jit_solution(18188381201221436162)
XLA Ops:
  1.3 1.4 %first_chunk.1 = (bf16[33,16,256]{2,1,0:T(8,128)(2,1)S(1)}, f32[8,256]{1,0:T(8,128)S(1)}, f32[8,256]{1,0:T(8,128)S(1)}, bf16[784,128]{1,0:T(8,128)(2,1)S(1)}) custom-call(s32[1,1]{1,0:T(1,128)} %bitcast.6.rank_in, f32[64,16,256]{2,1,0:T(8,128)} %bitcast.7, bf16[3,16,16]{2,1,0:T(8,128)(2,1)} %bitcast.12, bf16[3,256,256]{2,1,0:T(8,128)(2,1)} %bitcast.10), custom_call_target="tpu_custom_call" | custom-call | flops 5242 | bytes 7864 | tf_op jit(solution)/shard_map/first_chunk/pallas_call | solution.py:514
  2.7 0.5 %collective-permute-start = (bf16[33,16,256]{2,1,0:T(8,128)(2,1)S(1)}, bf16[33,16,256]{2,1,0:T(8,128)(2,1)S(1)}, u32[]{:S(2)}, u32[]{:S(2)}) collective-permute-start(bf16[33,16,256]{2,1,0:T(8,128)(2,1)S(1)} %get-tuple-element.53.chunk_ref.refs_0_), channel_id=1, source_target_pairs={{0,1},{1,0},{2,3},{3,2},{4,5},{5,4},{6,7},{7,6},{8,9},{9,8},{10,11... | collective-permute-start | bytes 811016 | tf_op jit(solution)/shard_map/ppermute | solution.py:491
  3.2 2.6 %collective-permute-start.2 = (bf16[33,16,256]{2,1,0:T(8,128)(2,1)S(1)}, bf16[33,16,256]{2,1,0:T(8,128)(2,1)S(1)}, u32[]{:S(2)}, u32[]{:S(2)}) collective-permute-start(bf16[33,16,256]{2,1,0:T(8,128)(2,1)S(1)} %get-tuple-element.53.chunk_ref.refs_0_), channel_id=1, source_target_pairs={{0,2},{1,3},{2,0},{3,1},{4,6},{5,7},{6,4},{7,5},{8,10},{9,11},{10,... | collective-permute-start | bytes 811016 | tf_op jit(solution)/shard_map/ppermute | solution.py:494
  5.8 1.3 %collective-permute-start.7 = (bf16[784,128]{1,0:T(8,128)(2,1)S(1)}, bf16[784,128]{1,0:T(8,128)(2,1)S(1)}, u32[]{:S(2)}, u32[]{:S(2)}) collective-permute-start(bf16[784,128]{1,0:T(8,128)(2,1)S(1)} %get-tuple-element.61), channel_id=1, source_target_pairs={{4,0},{8,4},{12,8},{16,12},{20,16},{24,20},{28,24},{5,1},{9,5},{13... | collective-permute-start | bytes 602120 | tf_op jit(solution)/shard_map/ppermute | solution.py:563
  7.0 0.0 collective-permute-done.refs_3_
  7.1 1.3 %prepare.1 = (f32[8,256]{1,0:T(8,128)S(1)}, bf16[784,128]{1,0:T(8,128)(2,1)S(1)}, bf16[3,256,256]{2,1,0:T(8,128)(2,1)S(1)}, bf16[16,16,256]{2,1,0:T(8,128)(2,1)S(1)}, bf16[16,16,256]{2,1,0:T(8,128)(2,1)S(1)}) custom-call(f32[8,256]{1,0:T(8,128)S(1)} %get-tuple-element.51.keep_ref, f32[8,256]{1,0:T(8,128)S(1)} %get-tuple-element.54.squares_ref, ...), custom_call_target="tpu_custom_call" | custom-call | flops 10485 | bytes 15728 | tf_op jit(solution)/shard_map/prepare/pallas_call | solution.py:532
  8.4 0.2 collective-permute-start.4
  8.6 0.3 collective-permute-start.3
  9.0 0.2 collective-permute-start.6
  9.2 0.4 spread_site.2.refs_6_.refs_5_.refs_3_.kron_ref
  9.5 0.3 collective-permute-done.4.refs_5_
  9.8 1.7 %collective-permute-start.1 = (bf16[16,16,256]{2,1,0:T(8,128)(2,1)S(1)}, bf16[16,16,256]{2,1,0:T(8,128)(2,1)S(1)}, u32[]{:S(2)}, u32[]{:S(2)}) collective-permute-start(bf16[16,16,256]{2,1,0:T(8,128)(2,1)S(1)} %get-tuple-element.55.refs_2_), channel_id=1, source_target_pairs={{0,2},{1,3},{2,0},{3,1},{4,6},{5,7},{6,4},{7,5},{8,10},{9,11},{10,... | collective-permute-start | bytes 393224 | tf_op jit(solution)/shard_map/ppermute | solution.py:494
  11.5 0.0 collective-permute-done.3.refs_4_
  11.5 0.4 collective-permute-start.10
  11.9 1.0 %rotate_own.1 = (bf16[3,16,128,256]{3,2,1,0:T(8,128)(2,1)S(1)}, bf16[256,768]{1,0:T(8,128)(2,1)S(1)}) custom-call(bf16[33,16,256]{2,1,0:T(8,128)(2,1)S(1)} %get-tuple-element.53.chunk_ref.refs_0_, bf16[16,16,256]{2,1,0:T(8,128)(2,1)S(1)} %get-tuple-element.56.refs_1_, bf16[16,16,256]{2,1,0:T(8,128)(2,1)S(1)} %get-tuple-element.55.refs_2_, ...), custom_call_target="tpu_custom_call" | custom-call | flops 16106127 | bytes 83886 | tf_op jit(solution)/shard_map/rotate_own/pallas_call | solution.py:595
  12.8 0.2 collective-permute-done.2.chunk_ref.refs_0_
  13.1 0.0 collective-permute-start.5
  13.1 0.4 spread_site.3.refs_6_.refs_4_.refs_2_
  13.5 1.4 %rotate_here.1 = (bf16[3,16,256,256]{3,2,1,0:T(8,128)(2,1)S(1)}, bf16[16,256,256]{2,1,0:T(8,128)(2,1)S(1)}) custom-call(bf16[33,16,256]{2,1,0:T(8,128)(2,1)S(1)} %get-tuple-element.53.chunk_ref.refs_0_, bf16[16,16,256]{2,1,0:T(8,128)(2,1)S(1)} %get-tuple-element.56.refs_1_, bf16[16,16,256]{2,1,0:T(8,128)(2,1)S(1)} %get-tuple-element.55.refs_2_, ...), custom_call_target="tpu_custom_call" | custom-call | flops 16106127 | bytes 83886 | tf_op jit(solution)/shard_map/rotate_here/pallas_call | solution.py:609
  14.9 0.0 collective-permute-done.7
  14.9 1.0 %collective-permute-done.6.refs_2_ = bf16[16,16,256]{2,1,0:T(8,128)(2,1)S(1)} collective-permute-done((bf16[16,16,256]{2,1,0:T(8,128)(2,1)S(1)}, bf16[16,16,256]{2,1,0:T(8,128)(2,1)S(1)}, u32[]{:S(2)}, u32[]{:S(2)}) %collective-permute-start.6) | collective-permute-done | bytes 131104 | tf_op jit(solution)/shard_map/ppermute | solution.py:494
  15.9 0.0 collective-permute-start.8
  15.9 2.0 %collective-permute-start.11 = (bf16[784,128]{1,0:T(8,128)(2,1)S(1)}, bf16[784,128]{1,0:T(8,128)(2,1)S(1)}, u32[]{:S(2)}, u32[]{:S(2)}) collective-permute-start(bf16[784,128]{1,0:T(8,128)(2,1)S(1)} %broadcast_select_fusion.packed_ref), channel_id=1, source_target_pairs={{0,2},{1,3},{2,0},{3,1},{4,6},{5,7},{6,4},{7,5},{8,10},{9,11},{10,... | collective-permute-start | bytes 602120 | tf_op jit(solution)/shard_map/ppermute | solution.py:494
  17.9 1.1 %apply_rows_here.1 = (bf16[16,384,256]{2,1,0:T(8,128)(2,1)S(1)}, bf16[3,256,256]{2,1,0:T(8,128)(2,1)S(1)}) custom-call(bf16[3,16,128,256]{3,2,1,0:T(8,128)(2,1)S(1)} %get-tuple-element.71.rotated_ref, bf16[784,128]{1,0:T(8,128)(2,1)S(1)} %broadcast_select_fusion.packed_ref, f32[8,256]{1,0:T(8,128)S(1)} %get-tuple-element.51.keep_ref), custom_call_target="tpu_custom_call" | custom-call | flops 16106127 | bytes 83886 | tf_op jit(solution)/shard_map/apply_rows_here/pallas_call | solution.py:630
  19.1 0.0 collective-permute-done.8.refs_3_
  19.1 0.0 collective-permute-done.5.refs_1_
  19.1 1.1 %rotate_crossed.1 = (bf16[3,16,256,256]{3,2,1,0:T(8,128)(2,1)S(1)}, bf16[16,256,256]{2,1,0:T(8,128)(2,1)S(1)}) custom-call(bf16[33,16,256]{2,1,0:T(8,128)(2,1)S(1)} %collective-permute-done.2.chunk_ref.refs_0_, bf16[33,16,256]{2,1,0:T(8,128)(2,1)S(1)} %collective-permute-done.5.refs_1_, ...), custom_call_target="tpu_custom_call", output_to_operand_aliasing={{0}: (5, {}), {1}: (6, {})} | custom-call | flops 16106127 | bytes 83886 | tf_op jit(solution)/shard_map/rotate_crossed/pallas_call | solution.py:609
  20.2 0.0 collective-permute-done.1.refs_0_
  20.2 0.3 collective-permute-start.9
  20.5 1.7 %apply_rows_crossed.1.refs_6_ = bf16[16,288,256]{2,1,0:T(8,128)(2,1)S(1)} custom-call(bf16[33,16,256]{2,1,0:T(8,128)(2,1)S(1)} %collective-permute-done.2.chunk_ref.refs_0_, bf16[33,16,256]{2,1,0:T(8,128)(2,1)S(1)} %collective-permute-done.5.refs_1_, bf16[16,16,256]{2,1,0:T(8,128)(2,1)S(1)} %collective-permute-done.6.refs_2_, ...), custom_call_target="tpu_custom_call" | custom-call | flops 16106127 | bytes 83886 | tf_op jit(solution)/shard_map/apply_rows_crossed/pallas_call | solution.py:651
  22.2 0.0 collective-permute-done.9.refs_1_
  22.2 2.3 %apply_rows_last.1.before_ref = f32[16,256,256]{2,1,0:T(8,128)S(1)} custom-call(bf16[16,16,256]{2,1,0:T(8,128)(2,1)S(1)} %collective-permute-done.1.refs_0_, bf16[16,16,256]{2,1,0:T(8,128)(2,1)S(1)} %collective-permute-done.9.refs_1_, bf16[3,256,256]{2,1,0:T(8,128)(2,1)S(1)} %get-tuple-element.78.refs_4_.refs_2_.right_ref, ...), custom_call_target="tpu_custom_call" | custom-call | flops 16106127 | bytes 83886 | tf_op jit(solution)/shard_map/apply_rows_last/pallas_call | solution.py:665
  24.5 0.0 collective-permute-done.10.refs_5_
  24.5 2.6 %received_lefts.1 = (bf16[16,256,768]{2,1,0:T(8,128)(2,1)S(1)}, f32[8,256]{1,0:T(8,128)S(1)}, bf16[3,16,256,256]{3,2,1,0:T(8,128)(2,1)S(1)}, bf16[16,256,256]{2,1,0:T(8,128)(2,1)S(1)}) custom-call(bf16[16,16,256]{2,1,0:T(8,128)(2,1)S(1)} %collective-permute-done.1.refs_0_, ...), custom_call_target="tpu_custom_call", output_to_operand_aliasing={{2}: (3, {}), {3}: (4, {})} | custom-call | flops 16106127 | bytes 125829 | tf_op jit(solution)/shard_map/received_lefts/pallas_call | solution.py:684
  27.1 0.4 collective-permute-start.12
  27.4 0.0 collective-permute-done.11.packed_ref
  27.4 1.2 %received_rights.2 = (bf16[8,256,256]{2,1,0:T(8,128)(2,1)S(1)}, bf16[3,256,256]{2,1,0:T(8,128)(2,1)S(1)}) custom-call(bf16[784,128]{1,0:T(8,128)(2,1)S(1)} %collective-permute-done.11.packed_ref, bf16[16,256,768]{2,1,0:T(8,128)(2,1)S(1)} %get-tuple-element.84.mixed_ref, f32[16,256,256]{2,1,0:T(8,128)S(1)} %apply_rows_last.1.before_ref, ...), custom_call_target="tpu_custom_call" | custom-call | flops 8053063 | bytes 125829 | tf_op jit(solution)/shard_map/received_rights/pallas_call | solution.py:704
  28.6 0.3 collective-permute-start.13
  28.9 0.0 collective-permute-done.12.norm_other_ref
  28.9 1.0 %received_rights.3.high_ref.refs_2_ = bf16[8,256,256]{2,1,0:T(8,128)(2,1)S(1)} custom-call(bf16[3,256,256]{2,1,0:T(8,128)(2,1)S(1)} %get-tuple-element.91.packed_ref, bf16[16,256,768]{2,1,0:T(8,128)(2,1)S(1)} %get-tuple-element.84.mixed_ref, f32[16,256,256]{2,1,0:T(8,128)S(1)} %apply_rows_last.1.before_ref, f32[8,256]{1,0:T(8,128)S(1)} %get-tuple-element.51.keep_ref), custom_call_target="tpu_custom_call" | custom-call | flops 8053063 | bytes 125829 | tf_op jit(solution)/shard_map/received_rights/pallas_call | solution.py:704
  30.0 0.4 collective-permute-start.14
  30.3 1.0 %collective-permute-done.13.low_other_ref.refs_1_ = bf16[8,256,256]{2,1,0:T(8,128)(2,1)S(1)} collective-permute-done((bf16[8,256,256]{2,1,0:T(8,128)(2,1)S(1)}, bf16[8,256,256]{2,1,0:T(8,128)(2,1)S(1)}, u32[]{:S(2)}, u32[]{:S(2)}) %collective-permute-start.13) | collective-permute-done | bytes 1048608 | tf_op jit(solution)/shard_map/ppermute | solution.py:491
  31.3 1.7 %residual_low.1 = (bf16[8,256,256]{2,1,0:T(8,128)(2,1)S(1)}, bf16[3,8,256,256]{3,2,1,0:T(8,128)(2,1)S(1)}, f32[8,256]{1,0:T(8,128)S(1)}) custom-call(f32[8,256]{1,0:T(8,128)S(1)} %get-tuple-element.83.norm_ref, f32[8,256]{1,0:T(8,128)S(1)} %collective-permute-done.12.norm_other_ref, bf16[8,256,256]{2,1,0:T(8,128)(2,1)S(1)} %get-tuple-element.88.low_ref.refs_0_, ...), custom_call_target="tpu_custom_call" | custom-call | flops 8053063 | bytes 31457 | tf_op jit(solution)/shard_map/residual_low/pallas_call | solution.py:723
  33.1 0.0 collective-permute-done.14.high_other_ref.refs_3_
  33.1 0.0 copy-start
  33.1 4.8 %residual_high.1.share_ref.refs_0_ = f32[8,256]{1,0:T(8,128)S(1)} custom-call(f32[8,256]{1,0:T(8,128)S(1)} %get-tuple-element.83.norm_ref, f32[8,256]{1,0:T(8,128)S(1)} %collective-permute-done.12.norm_other_ref, f32[8,256]{1,0:T(8,128)S(1)} %get-tuple-element.90.sums_ref, bf16[8,256,256]{2,1,0:T(8,128)(2,1)S(1)} %received_rights.3.high_ref.refs_2_, ...), custom_call_target="tpu_custom_call" | custom-call | flops 48318384 | bytes 62914 | tf_op jit(solution)/shard_map/residual_high/pallas_call | solution.py:732
  37.9 1.4 %collective-permute-start.15 = (f32[8,256]{1,0:T(8,128)S(1)}, f32[8,256]{1,0:T(8,128)S(1)}, u32[]{:S(2)}, u32[]{:S(2)}) collective-permute-start(f32[8,256]{1,0:T(8,128)S(1)} %residual_high.1.share_ref.refs_0_), channel_id=1, source_target_pairs={{0,2},{1,3},{2,0},{3,1},{4,6},{5,7},{6,4},{7,5},{8,10},{9,11},{10,... | collective-permute-start | bytes 24584 | tf_op jit(solution)/shard_map/ppermute | solution.py:504
  39.3 0.0 collective-permute-start.16
  39.3 0.0 copy-done
  39.3 0.5 %own_rows.1 = (f32[64,16,256]{2,1,0:T(8,128)S(1)}, f32[64,16,256]{2,1,0:T(8,128)S(1)}) custom-call(f32[8,256]{1,0:T(8,128)S(1)} %get-tuple-element.51.keep_ref, f32[8,256]{1,0:T(8,128)S(1)} %get-tuple-element.83.norm_ref, f32[8,256]{1,0:T(8,128)S(1)} %collective-permute-done.12.norm_other_ref, f32[8,256]{1,0:T(8,128)S(1)} %residual_high.1.share_ref.refs_0_, ...), custom_call_target="tpu_custom_call" | custom-call | flops 20971 | bytes 41943 | tf_op jit(solution)/shard_map/own_rows/pallas_call | solution.py:749
  39.8 1.8 %collective-permute-done.15.refs_2_ = f32[8,256]{1,0:T(8,128)S(1)} collective-permute-done((f32[8,256]{1,0:T(8,128)S(1)}, f32[8,256]{1,0:T(8,128)S(1)}, u32[]{:S(2)}, u32[]{:S(2)}) %collective-permute-start.15) | collective-permute-done | bytes 8224 | tf_op jit(solution)/shard_map/ppermute | solution.py:504
  41.6 0.0 collective-permute-start.17
  41.6 0.0 collective-permute-done.16.refs_1_
  41.6 1.2 %collective-permute-done.17.refs_3_ = f32[8,256]{1,0:T(8,128)S(1)} collective-permute-done((f32[8,256]{1,0:T(8,128)S(1)}, f32[8,256]{1,0:T(8,128)S(1)}, u32[]{:S(2)}, u32[]{:S(2)}) %collective-permute-start.17) | collective-permute-done | bytes 8224 | tf_op jit(solution)/shard_map/ppermute | solution.py:491
  42.8 1.3 %finish.1 = (f32[64,16,256]{2,1,0:T(8,128)}, f32[1]{0:T(128)}) custom-call(f32[64,16,256]{2,1,0:T(8,128)S(1)} %get-tuple-element.94.vector_ref, f32[64,16,256]{2,1,0:T(8,128)S(1)} %get-tuple-element.96.residual_ref, f32[8,256]{1,0:T(8,128)S(1)} %residual_high.1.share_ref.refs_0_, f32[8,256]{1,0:T(8,128)S(1)} %collective-permute-done.16.refs_1_, ...), custom_call_target="tpu_custom_call" | custom-call | flops 7864 | bytes 31457 | tf_op jit(solution)/shard_map/finish/pallas_call | solution.py:762
  (1 shorter events, 0.0 us)
Async XLA Ops:
  2.7 4.4 %collective-permute-start = (bf16[33,16,256]{2,1,0:T(8,128)(2,1)S(1)}, bf16[33,16,256]{2,1,0:T(8,128)(2,1)S(1)}, u32[]{:S(2)}, u32[]{:S(2)}) collective-permute-start(bf16[33,16,256]{2,1,0:T(8,128)(2,1)S(1)} %get-tuple-element.53.chunk_ref.refs_0_), channel_id=1, source_target_pairs={{0,1},{1,0},{2,3},{3,2},{4,5},{5,4},{6,7},{7,6},{8,9},{9,8},{10,11... | collective-permute-start | bytes 811016 | tf_op jit(solution)/shard_map/ppermute | solution.py:491
  3.2 9.9 %collective-permute-start.2 = (bf16[33,16,256]{2,1,0:T(8,128)(2,1)S(1)}, bf16[33,16,256]{2,1,0:T(8,128)(2,1)S(1)}, u32[]{:S(2)}, u32[]{:S(2)}) collective-permute-start(bf16[33,16,256]{2,1,0:T(8,128)(2,1)S(1)} %get-tuple-element.53.chunk_ref.refs_0_), channel_id=1, source_target_pairs={{0,2},{1,3},{2,0},{3,1},{4,6},{5,7},{6,4},{7,5},{8,10},{9,11},{10,... | collective-permute-start | bytes 811016 | tf_op jit(solution)/shard_map/ppermute | solution.py:494
  5.8 9.1 %collective-permute-start.7 = (bf16[784,128]{1,0:T(8,128)(2,1)S(1)}, bf16[784,128]{1,0:T(8,128)(2,1)S(1)}, u32[]{:S(2)}, u32[]{:S(2)}) collective-permute-start(bf16[784,128]{1,0:T(8,128)(2,1)S(1)} %get-tuple-element.61), channel_id=1, source_target_pairs={{4,0},{8,4},{12,8},{16,12},{20,16},{24,20},{28,24},{5,1},{9,5},{13... | collective-permute-start | bytes 602120 | tf_op jit(solution)/shard_map/ppermute | solution.py:563
  8.4 1.4 %collective-permute-start.4 = (bf16[16,16,256]{2,1,0:T(8,128)(2,1)S(1)}, bf16[16,16,256]{2,1,0:T(8,128)(2,1)S(1)}, u32[]{:S(2)}, u32[]{:S(2)}) collective-permute-start(bf16[16,16,256]{2,1,0:T(8,128)(2,1)S(1)} %get-tuple-element.55.refs_2_), channel_id=1, source_target_pairs={{0,1},{1,0},{2,3},{3,2},{4,5},{5,4},{6,7},{7,6},{8,9},{9,8},{10,11... | collective-permute-start | bytes 393224 | tf_op jit(solution)/shard_map/ppermute | solution.py:491
  8.6 2.8 %collective-permute-start.3 = (bf16[16,16,256]{2,1,0:T(8,128)(2,1)S(1)}, bf16[16,16,256]{2,1,0:T(8,128)(2,1)S(1)}, u32[]{:S(2)}, u32[]{:S(2)}) collective-permute-start(bf16[16,16,256]{2,1,0:T(8,128)(2,1)S(1)} %get-tuple-element.56.refs_1_), channel_id=1, source_target_pairs={{0,1},{1,0},{2,3},{3,2},{4,5},{5,4},{6,7},{7,6},{8,9},{9,8},{10,11... | collective-permute-start | bytes 393224 | tf_op jit(solution)/shard_map/ppermute | solution.py:491
  9.0 6.9 %collective-permute-start.6 = (bf16[16,16,256]{2,1,0:T(8,128)(2,1)S(1)}, bf16[16,16,256]{2,1,0:T(8,128)(2,1)S(1)}, u32[]{:S(2)}, u32[]{:S(2)}) collective-permute-start(bf16[16,16,256]{2,1,0:T(8,128)(2,1)S(1)} %get-tuple-element.56.refs_1_), channel_id=1, source_target_pairs={{0,2},{1,3},{2,0},{3,1},{4,6},{5,7},{6,4},{7,5},{8,10},{9,11},{10,... | collective-permute-start | bytes 393224 | tf_op jit(solution)/shard_map/ppermute | solution.py:494
  9.8 10.4 %collective-permute-start.1 = (bf16[16,16,256]{2,1,0:T(8,128)(2,1)S(1)}, bf16[16,16,256]{2,1,0:T(8,128)(2,1)S(1)}, u32[]{:S(2)}, u32[]{:S(2)}) collective-permute-start(bf16[16,16,256]{2,1,0:T(8,128)(2,1)S(1)} %get-tuple-element.55.refs_2_), channel_id=1, source_target_pairs={{0,2},{1,3},{2,0},{3,1},{4,6},{5,7},{6,4},{7,5},{8,10},{9,11},{10,... | collective-permute-start | bytes 393224 | tf_op jit(solution)/shard_map/ppermute | solution.py:494
  11.5 13.0 %collective-permute-start.10 = (bf16[784,128]{1,0:T(8,128)(2,1)S(1)}, bf16[784,128]{1,0:T(8,128)(2,1)S(1)}, u32[]{:S(2)}, u32[]{:S(2)}) collective-permute-start(bf16[784,128]{1,0:T(8,128)(2,1)S(1)} %get-tuple-element.77), channel_id=1, source_target_pairs={{0,2},{1,3},{2,0},{3,1},{4,6},{5,7},{6,4},{7,5},{8,10},{9,11},{10,... | collective-permute-start | bytes 602120 | tf_op jit(solution)/shard_map/ppermute | solution.py:494
  13.1 6.0 %collective-permute-start.5 = (bf16[33,16,256]{2,1,0:T(8,128)(2,1)S(1)}, bf16[33,16,256]{2,1,0:T(8,128)(2,1)S(1)}, u32[]{:S(2)}, u32[]{:S(2)}) collective-permute-start(bf16[33,16,256]{2,1,0:T(8,128)(2,1)S(1)} %collective-permute-done.2.chunk_ref.refs_0_), channel_id=1, source_target_pairs={{0,1},{1,0},{2,3},{3,2},{4,5},{5,4},{6,7},{7,6},{8,9},{9,8},{10,11... | collective-permute-start | bytes 811016 | tf_op jit(solution)/shard_map/ppermute | solution.py:491
  15.9 3.2 %collective-permute-start.8 = (bf16[16,16,256]{2,1,0:T(8,128)(2,1)S(1)}, bf16[16,16,256]{2,1,0:T(8,128)(2,1)S(1)}, u32[]{:S(2)}, u32[]{:S(2)}) collective-permute-start(bf16[16,16,256]{2,1,0:T(8,128)(2,1)S(1)} %collective-permute-done.6.refs_2_), channel_id=1, source_target_pairs={{0,1},{1,0},{2,3},{3,2},{4,5},{5,4},{6,7},{7,6},{8,9},{9,8},{10,11... | collective-permute-start | bytes 393224 | tf_op jit(solution)/shard_map/ppermute | solution.py:491
  15.9 11.5 %collective-permute-start.11 = (bf16[784,128]{1,0:T(8,128)(2,1)S(1)}, bf16[784,128]{1,0:T(8,128)(2,1)S(1)}, u32[]{:S(2)}, u32[]{:S(2)}) collective-permute-start(bf16[784,128]{1,0:T(8,128)(2,1)S(1)} %broadcast_select_fusion.packed_ref), channel_id=1, source_target_pairs={{0,2},{1,3},{2,0},{3,1},{4,6},{5,7},{6,4},{7,5},{8,10},{9,11},{10,... | collective-permute-start | bytes 602120 | tf_op jit(solution)/shard_map/ppermute | solution.py:494
  20.2 2.0 %collective-permute-start.9 = (bf16[16,16,256]{2,1,0:T(8,128)(2,1)S(1)}, bf16[16,16,256]{2,1,0:T(8,128)(2,1)S(1)}, u32[]{:S(2)}, u32[]{:S(2)}) collective-permute-start(bf16[16,16,256]{2,1,0:T(8,128)(2,1)S(1)} %collective-permute-done.1.refs_0_), channel_id=1, source_target_pairs={{0,1},{1,0},{2,3},{3,2},{4,5},{5,4},{6,7},{7,6},{8,9},{9,8},{10,11... | collective-permute-start | bytes 393224 | tf_op jit(solution)/shard_map/ppermute | solution.py:491
  27.1 1.8 %collective-permute-start.12 = (f32[8,256]{1,0:T(8,128)S(1)}, f32[8,256]{1,0:T(8,128)S(1)}, u32[]{:S(2)}, u32[]{:S(2)}) collective-permute-start(f32[8,256]{1,0:T(8,128)S(1)} %get-tuple-element.83.norm_ref), channel_id=1, source_target_pairs={{0,1},{1,0},{2,3},{3,2},{4,5},{5,4},{6,7},{7,6},{8,9},{9,8},{10,11... | collective-permute-start | bytes 24584 | tf_op jit(solution)/shard_map/ppermute | solution.py:491
  28.6 2.7 %collective-permute-start.13 = (bf16[8,256,256]{2,1,0:T(8,128)(2,1)S(1)}, bf16[8,256,256]{2,1,0:T(8,128)(2,1)S(1)}, u32[]{:S(2)}, u32[]{:S(2)}) collective-permute-start(bf16[8,256,256]{2,1,0:T(8,128)(2,1)S(1)} %get-tuple-element.88.low_ref.refs_0_), channel_id=1, source_target_pairs={{0,1},{1,0},{2,3},{3,2},{4,5},{5,4},{6,7},{7,6},{8,9},{9,8},{10,11... | collective-permute-start | bytes 3145736 | tf_op jit(solution)/shard_map/ppermute | solution.py:491
  30.0 3.1 %collective-permute-start.14 = (bf16[8,256,256]{2,1,0:T(8,128)(2,1)S(1)}, bf16[8,256,256]{2,1,0:T(8,128)(2,1)S(1)}, u32[]{:S(2)}, u32[]{:S(2)}) collective-permute-start(bf16[8,256,256]{2,1,0:T(8,128)(2,1)S(1)} %received_rights.3.high_ref.refs_2_), channel_id=1, source_target_pairs={{0,1},{1,0},{2,3},{3,2},{4,5},{5,4},{6,7},{7,6},{8,9},{9,8},{10,11... | collective-permute-start | bytes 3145736 | tf_op jit(solution)/shard_map/ppermute | solution.py:491
  33.1 6.2 %copy-start = (f32[1,64,16,256]{3,2,1,0:T(8,128)S(1)}, f32[1,64,16,256]{3,2,1,0:T(8,128)}, u32[]{:S(2)}) copy-start(f32[1,64,16,256]{3,2,1,0:T(8,128)} %param.5) | copy-start | bytes 3145732
  37.9 3.7 %collective-permute-start.15 = (f32[8,256]{1,0:T(8,128)S(1)}, f32[8,256]{1,0:T(8,128)S(1)}, u32[]{:S(2)}, u32[]{:S(2)}) collective-permute-start(f32[8,256]{1,0:T(8,128)S(1)} %residual_high.1.share_ref.refs_0_), channel_id=1, source_target_pairs={{0,2},{1,3},{2,0},{3,1},{4,6},{5,7},{6,4},{7,5},{8,10},{9,11},{10,... | collective-permute-start | bytes 24584 | tf_op jit(solution)/shard_map/ppermute | solution.py:504
  39.3 2.3 %collective-permute-start.16 = (f32[8,256]{1,0:T(8,128)S(1)}, f32[8,256]{1,0:T(8,128)S(1)}, u32[]{:S(2)}, u32[]{:S(2)}) collective-permute-start(f32[8,256]{1,0:T(8,128)S(1)} %residual_high.1.share_ref.refs_0_), channel_id=1, source_target_pairs={{0,1},{1,0},{2,3},{3,2},{4,5},{5,4},{6,7},{7,6},{8,9},{9,8},{10,11... | collective-permute-start | bytes 24584 | tf_op jit(solution)/shard_map/ppermute | solution.py:491
  41.6 1.2 %collective-permute-start.17 = (f32[8,256]{1,0:T(8,128)S(1)}, f32[8,256]{1,0:T(8,128)S(1)}, u32[]{:S(2)}, u32[]{:S(2)}) collective-permute-start(f32[8,256]{1,0:T(8,128)S(1)} %collective-permute-done.15.refs_2_), channel_id=1, source_target_pairs={{0,1},{1,0},{2,3},{3,2},{4,5},{5,4},{6,7},{7,6},{8,9},{9,8},{10,11... | collective-permute-start | bytes 24584 | tf_op jit(solution)/shard_map/ppermute | solution.py:491

commit v20 on v16

--- a/solution.py
+++ b/solution.py
@@ -10,7 +10,7 @@
 epsilon = 1e-06
 CORES = 2
 TILE = 16
-STRIP = 32
+STRIP = 16
 GROUP = 8
 VMEM_LIMIT = 20 * 1024 * 1024
 F32 = jnp.float32

time: 44 us -> 44.1 us (level)
  transfers between devices with their start and end apart: 18 -> 18, of which waited for: 6 -> 6; matrix products, arithmetic and copies ran while one was open for 0% -> 0% of each run, Pallas kernels for 39% -> 40%
where the time goes in v20:
time: 44.1 us; the launch traced here: 43.9 us
  Pallas kernels  24.7 us (56%)
  starting transfers between devices  12.2 us (28%)
  waiting for transfers between devices  5.25 us (12%)
  between operations  1.65 us (4%)
    ppermute x5, starting transfers between devices, to_next_chip(): lax.ppermute(block, 'term', [(i, (i + CORES) % members) for i in range(me...  6.8 us
    pallas_call x1, Pallas kernels, shards(): pl.pallas_call(functools.partial(high_kernel, scale, members), out_shape=...  4.76 us
    pallas_call x1, Pallas kernels, shards(): pl.pallas_call(functools.partial(lefts_kernel, far_spots[-1], rows, chips...  2.6 us
    ppermute x11, waiting for transfers between devices, to_sibling(): return lax.ppermute(block, 'term', [(i, i ^ 1) for i in range(members)])  2.51 us
    pallas_call x2, Pallas kernels, rotate(): pl.pallas_call(functools.partial(rotate_kernel, spots, rows, chips), out_...  2.5 us
    ppermute x11, starting transfers between devices, to_sibling(): return lax.ppermute(block, 'term', [(i, i ^ 1) for i in range(members)])  2.38 us
    pallas_call x1, Pallas kernels, shards(): pl.pallas_call(functools.partial(last_kernel, len(last_pieces)), out_shap...  2.22 us
    pallas_call x2, Pallas kernels, shards(): pl.pallas_call(functools.partial(rights_kernel, start, stop), out_shape=(...  2.21 us
  transfers between devices with their start and end apart: 18, of which 6 were waited for; matrix products, arithmetic and copies ran while one was open for 0% of the time, Pallas kernels for 40%

profile of v20, /device:TPU:0, one launch (start us, length us, event | category | flops | bytes accessed | tf_op | source)
XLA Modules:
  0.0 43.9 jit_solution(14841751039954106409)
XLA Ops:
  1.3 1.4 %first_chunk.1 = (bf16[33,16,256]{2,1,0:T(8,128)(2,1)S(1)}, f32[8,256]{1,0:T(8,128)S(1)}, f32[8,256]{1,0:T(8,128)S(1)}, bf16[784,128]{1,0:T(8,128)(2,1)S(1)}) custom-call(s32[1,1]{1,0:T(1,128)} %bitcast.6.rank_in, f32[64,16,256]{2,1,0:T(8,128)} %bitcast.7, bf16[3,16,16]{2,1,0:T(8,128)(2,1)} %bitcast.12, bf16[3,256,256]{2,1,0:T(8,128)(2,1)} %bitcast.10), custom_call_target="tpu_custom_call" | custom-call | flops 5242 | bytes 7864 | tf_op jit(solution)/shard_map/first_chunk/pallas_call | solution.py:515
  2.7 0.5 %collective-permute-start = (bf16[33,16,256]{2,1,0:T(8,128)(2,1)S(1)}, bf16[33,16,256]{2,1,0:T(8,128)(2,1)S(1)}, u32[]{:S(2)}, u32[]{:S(2)}) collective-permute-start(bf16[33,16,256]{2,1,0:T(8,128)(2,1)S(1)} %get-tuple-element.53.chunk_ref.refs_0_), channel_id=1, source_target_pairs={{0,1},{1,0},{2,3},{3,2},{4,5},{5,4},{6,7},{7,6},{8,9},{9,8},{10,11... | collective-permute-start | bytes 811016 | tf_op jit(solution)/shard_map/ppermute | solution.py:492
  3.2 2.6 %collective-permute-start.2 = (bf16[33,16,256]{2,1,0:T(8,128)(2,1)S(1)}, bf16[33,16,256]{2,1,0:T(8,128)(2,1)S(1)}, u32[]{:S(2)}, u32[]{:S(2)}) collective-permute-start(bf16[33,16,256]{2,1,0:T(8,128)(2,1)S(1)} %get-tuple-element.53.chunk_ref.refs_0_), channel_id=1, source_target_pairs={{0,2},{1,3},{2,0},{3,1},{4,6},{5,7},{6,4},{7,5},{8,10},{9,11},{10,... | collective-permute-start | bytes 811016 | tf_op jit(solution)/shard_map/ppermute | solution.py:495
  5.8 1.3 %collective-permute-start.7 = (bf16[784,128]{1,0:T(8,128)(2,1)S(1)}, bf16[784,128]{1,0:T(8,128)(2,1)S(1)}, u32[]{:S(2)}, u32[]{:S(2)}) collective-permute-start(bf16[784,128]{1,0:T(8,128)(2,1)S(1)} %get-tuple-element.61), channel_id=1, source_target_pairs={{4,0},{8,4},{12,8},{16,12},{20,16},{24,20},{28,24},{5,1},{9,5},{13... | collective-permute-start | bytes 602120 | tf_op jit(solution)/shard_map/ppermute | solution.py:564
  7.0 0.0 collective-permute-done.refs_3_
  7.1 1.3 %prepare.1 = (f32[8,256]{1,0:T(8,128)S(1)}, bf16[784,128]{1,0:T(8,128)(2,1)S(1)}, bf16[3,256,256]{2,1,0:T(8,128)(2,1)S(1)}, bf16[16,16,256]{2,1,0:T(8,128)(2,1)S(1)}, bf16[16,16,256]{2,1,0:T(8,128)(2,1)S(1)}) custom-call(f32[8,256]{1,0:T(8,128)S(1)} %get-tuple-element.51.keep_ref, f32[8,256]{1,0:T(8,128)S(1)} %get-tuple-element.54.squares_ref, ...), custom_call_target="tpu_custom_call" | custom-call | flops 10485 | bytes 15728 | tf_op jit(solution)/shard_map/prepare/pallas_call | solution.py:533
  8.4 0.2 collective-permute-start.4
  8.6 0.3 collective-permute-start.3
  9.0 0.2 collective-permute-start.6
  9.2 0.4 spread_site.2.refs_6_.refs_5_.refs_3_.kron_ref
  9.5 0.3 collective-permute-done.4.refs_5_
  9.8 1.7 %collective-permute-start.1 = (bf16[16,16,256]{2,1,0:T(8,128)(2,1)S(1)}, bf16[16,16,256]{2,1,0:T(8,128)(2,1)S(1)}, u32[]{:S(2)}, u32[]{:S(2)}) collective-permute-start(bf16[16,16,256]{2,1,0:T(8,128)(2,1)S(1)} %get-tuple-element.55.refs_2_), channel_id=1, source_target_pairs={{0,2},{1,3},{2,0},{3,1},{4,6},{5,7},{6,4},{7,5},{8,10},{9,11},{10,... | collective-permute-start | bytes 393224 | tf_op jit(solution)/shard_map/ppermute | solution.py:495
  11.5 0.0 collective-permute-done.3.refs_4_
  11.5 0.4 collective-permute-start.10
  11.9 1.0 %rotate_own.1 = (bf16[3,16,128,256]{3,2,1,0:T(8,128)(2,1)S(1)}, bf16[256,768]{1,0:T(8,128)(2,1)S(1)}) custom-call(bf16[33,16,256]{2,1,0:T(8,128)(2,1)S(1)} %get-tuple-element.53.chunk_ref.refs_0_, bf16[16,16,256]{2,1,0:T(8,128)(2,1)S(1)} %get-tuple-element.56.refs_1_, bf16[16,16,256]{2,1,0:T(8,128)(2,1)S(1)} %get-tuple-element.55.refs_2_, ...), custom_call_target="tpu_custom_call" | custom-call | flops 16106127 | bytes 83886 | tf_op jit(solution)/shard_map/rotate_own/pallas_call | solution.py:596
  12.8 0.2 collective-permute-done.2.chunk_ref.refs_0_
  13.1 0.0 collective-permute-start.5
  13.1 0.4 spread_site.3.refs_6_.refs_4_.refs_2_
  13.5 1.4 %rotate_here.1 = (bf16[3,16,256,256]{3,2,1,0:T(8,128)(2,1)S(1)}, bf16[16,256,256]{2,1,0:T(8,128)(2,1)S(1)}) custom-call(bf16[33,16,256]{2,1,0:T(8,128)(2,1)S(1)} %get-tuple-element.53.chunk_ref.refs_0_, bf16[16,16,256]{2,1,0:T(8,128)(2,1)S(1)} %get-tuple-element.56.refs_1_, bf16[16,16,256]{2,1,0:T(8,128)(2,1)S(1)} %get-tuple-element.55.refs_2_, ...), custom_call_target="tpu_custom_call" | custom-call | flops 16106127 | bytes 83886 | tf_op jit(solution)/shard_map/rotate_here/pallas_call | solution.py:610
  14.9 0.0 collective-permute-done.7
  14.9 1.0 %collective-permute-done.6.refs_2_ = bf16[16,16,256]{2,1,0:T(8,128)(2,1)S(1)} collective-permute-done((bf16[16,16,256]{2,1,0:T(8,128)(2,1)S(1)}, bf16[16,16,256]{2,1,0:T(8,128)(2,1)S(1)}, u32[]{:S(2)}, u32[]{:S(2)}) %collective-permute-start.6) | collective-permute-done | bytes 131104 | tf_op jit(solution)/shard_map/ppermute | solution.py:495
  15.9 0.0 collective-permute-start.8
  15.9 2.0 %collective-permute-start.11 = (bf16[784,128]{1,0:T(8,128)(2,1)S(1)}, bf16[784,128]{1,0:T(8,128)(2,1)S(1)}, u32[]{:S(2)}, u32[]{:S(2)}) collective-permute-start(bf16[784,128]{1,0:T(8,128)(2,1)S(1)} %broadcast_select_fusion.packed_ref), channel_id=1, source_target_pairs={{0,2},{1,3},{2,0},{3,1},{4,6},{5,7},{6,4},{7,5},{8,10},{9,11},{10,... | collective-permute-start | bytes 602120 | tf_op jit(solution)/shard_map/ppermute | solution.py:495
  17.9 1.1 %apply_rows_here.1 = (bf16[16,384,256]{2,1,0:T(8,128)(2,1)S(1)}, bf16[3,256,256]{2,1,0:T(8,128)(2,1)S(1)}) custom-call(bf16[3,16,128,256]{3,2,1,0:T(8,128)(2,1)S(1)} %get-tuple-element.71.rotated_ref, bf16[784,128]{1,0:T(8,128)(2,1)S(1)} %broadcast_select_fusion.packed_ref, f32[8,256]{1,0:T(8,128)S(1)} %get-tuple-element.51.keep_ref), custom_call_target="tpu_custom_call" | custom-call | flops 16106127 | bytes 83886 | tf_op jit(solution)/shard_map/apply_rows_here/pallas_call | solution.py:631
  19.1 0.0 collective-permute-done.8.refs_3_
  19.1 0.0 collective-permute-done.5.refs_1_
  19.1 1.1 %rotate_crossed.1 = (bf16[3,16,256,256]{3,2,1,0:T(8,128)(2,1)S(1)}, bf16[16,256,256]{2,1,0:T(8,128)(2,1)S(1)}) custom-call(bf16[33,16,256]{2,1,0:T(8,128)(2,1)S(1)} %collective-permute-done.2.chunk_ref.refs_0_, bf16[33,16,256]{2,1,0:T(8,128)(2,1)S(1)} %collective-permute-done.5.refs_1_, ...), custom_call_target="tpu_custom_call", output_to_operand_aliasing={{0}: (5, {}), {1}: (6, {})} | custom-call | flops 16106127 | bytes 83886 | tf_op jit(solution)/shard_map/rotate_crossed/pallas_call | solution.py:610
  20.2 0.0 collective-permute-done.1.refs_0_
  20.2 0.3 collective-permute-start.9
  20.5 1.4 %apply_rows_crossed.1.refs_6_ = bf16[16,288,256]{2,1,0:T(8,128)(2,1)S(1)} custom-call(bf16[33,16,256]{2,1,0:T(8,128)(2,1)S(1)} %collective-permute-done.2.chunk_ref.refs_0_, bf16[33,16,256]{2,1,0:T(8,128)(2,1)S(1)} %collective-permute-done.5.refs_1_, bf16[16,16,256]{2,1,0:T(8,128)(2,1)S(1)} %collective-permute-done.6.refs_2_, ...), custom_call_target="tpu_custom_call" | custom-call | flops 16106127 | bytes 83886 | tf_op jit(solution)/shard_map/apply_rows_crossed/pallas_call | solution.py:652
  21.9 0.0 collective-permute-done.9.refs_1_
  21.9 2.2 %apply_rows_last.1.before_ref = f32[16,256,256]{2,1,0:T(8,128)S(1)} custom-call(bf16[16,16,256]{2,1,0:T(8,128)(2,1)S(1)} %collective-permute-done.1.refs_0_, bf16[16,16,256]{2,1,0:T(8,128)(2,1)S(1)} %collective-permute-done.9.refs_1_, bf16[3,256,256]{2,1,0:T(8,128)(2,1)S(1)} %get-tuple-element.78.refs_4_.refs_2_.right_ref, ...), custom_call_target="tpu_custom_call" | custom-call | flops 16106127 | bytes 83886 | tf_op jit(solution)/shard_map/apply_rows_last/pallas_call | solution.py:666
  24.1 0.0 collective-permute-done.10.refs_5_
  24.1 2.6 %received_lefts.1 = (bf16[16,256,768]{2,1,0:T(8,128)(2,1)S(1)}, f32[8,256]{1,0:T(8,128)S(1)}, bf16[3,16,256,256]{3,2,1,0:T(8,128)(2,1)S(1)}, bf16[16,256,256]{2,1,0:T(8,128)(2,1)S(1)}) custom-call(bf16[16,16,256]{2,1,0:T(8,128)(2,1)S(1)} %collective-permute-done.1.refs_0_, ...), custom_call_target="tpu_custom_call", output_to_operand_aliasing={{2}: (3, {}), {3}: (4, {})} | custom-call | flops 16106127 | bytes 125829 | tf_op jit(solution)/shard_map/received_lefts/pallas_call | solution.py:685
  26.7 0.4 collective-permute-start.12
  27.1 0.0 collective-permute-done.11.packed_ref
  27.1 1.2 %received_rights.2 = (bf16[8,256,256]{2,1,0:T(8,128)(2,1)S(1)}, bf16[3,256,256]{2,1,0:T(8,128)(2,1)S(1)}) custom-call(bf16[784,128]{1,0:T(8,128)(2,1)S(1)} %collective-permute-done.11.packed_ref, bf16[16,256,768]{2,1,0:T(8,128)(2,1)S(1)} %get-tuple-element.84.mixed_ref, f32[16,256,256]{2,1,0:T(8,128)S(1)} %apply_rows_last.1.before_ref, ...), custom_call_target="tpu_custom_call" | custom-call | flops 8053063 | bytes 125829 | tf_op jit(solution)/shard_map/received_rights/pallas_call | solution.py:705
  28.3 0.3 collective-permute-start.13
  28.6 0.0 collective-permute-done.12.norm_other_ref
  28.6 1.0 %received_rights.3.high_ref.refs_2_ = bf16[8,256,256]{2,1,0:T(8,128)(2,1)S(1)} custom-call(bf16[3,256,256]{2,1,0:T(8,128)(2,1)S(1)} %get-tuple-element.91.packed_ref, bf16[16,256,768]{2,1,0:T(8,128)(2,1)S(1)} %get-tuple-element.84.mixed_ref, f32[16,256,256]{2,1,0:T(8,128)S(1)} %apply_rows_last.1.before_ref, f32[8,256]{1,0:T(8,128)S(1)} %get-tuple-element.51.keep_ref), custom_call_target="tpu_custom_call" | custom-call | flops 8053063 | bytes 125829 | tf_op jit(solution)/shard_map/received_rights/pallas_call | solution.py:705
  29.6 0.4 collective-permute-start.14
  30.0 1.0 %collective-permute-done.13.low_other_ref.refs_1_ = bf16[8,256,256]{2,1,0:T(8,128)(2,1)S(1)} collective-permute-done((bf16[8,256,256]{2,1,0:T(8,128)(2,1)S(1)}, bf16[8,256,256]{2,1,0:T(8,128)(2,1)S(1)}, u32[]{:S(2)}, u32[]{:S(2)}) %collective-permute-start.13) | collective-permute-done | bytes 1048608 | tf_op jit(solution)/shard_map/ppermute | solution.py:492
  31.0 1.8 %residual_low.1 = (bf16[8,256,256]{2,1,0:T(8,128)(2,1)S(1)}, bf16[3,8,256,256]{3,2,1,0:T(8,128)(2,1)S(1)}, f32[8,256]{1,0:T(8,128)S(1)}) custom-call(f32[8,256]{1,0:T(8,128)S(1)} %get-tuple-element.83.norm_ref, f32[8,256]{1,0:T(8,128)S(1)} %collective-permute-done.12.norm_other_ref, bf16[8,256,256]{2,1,0:T(8,128)(2,1)S(1)} %get-tuple-element.88.low_ref.refs_0_, ...), custom_call_target="tpu_custom_call" | custom-call | flops 8053063 | bytes 31457 | tf_op jit(solution)/shard_map/residual_low/pallas_call | solution.py:724
  32.8 0.0 collective-permute-done.14.high_other_ref.refs_3_
  32.8 0.0 copy-start
  32.8 4.8 %residual_high.1.share_ref.refs_0_ = f32[8,256]{1,0:T(8,128)S(1)} custom-call(f32[8,256]{1,0:T(8,128)S(1)} %get-tuple-element.83.norm_ref, f32[8,256]{1,0:T(8,128)S(1)} %collective-permute-done.12.norm_other_ref, f32[8,256]{1,0:T(8,128)S(1)} %get-tuple-element.90.sums_ref, bf16[8,256,256]{2,1,0:T(8,128)(2,1)S(1)} %received_rights.3.high_ref.refs_2_, ...), custom_call_target="tpu_custom_call" | custom-call | flops 48318384 | bytes 62914 | tf_op jit(solution)/shard_map/residual_high/pallas_call | solution.py:733
  37.6 1.8 %collective-permute-start.15 = (f32[8,256]{1,0:T(8,128)S(1)}, f32[8,256]{1,0:T(8,128)S(1)}, u32[]{:S(2)}, u32[]{:S(2)}) collective-permute-start(f32[8,256]{1,0:T(8,128)S(1)} %residual_high.1.share_ref.refs_0_), channel_id=1, source_target_pairs={{0,2},{1,3},{2,0},{3,1},{4,6},{5,7},{6,4},{7,5},{8,10},{9,11},{10,... | collective-permute-start | bytes 24584 | tf_op jit(solution)/shard_map/ppermute | solution.py:505
  39.4 0.0 collective-permute-start.16
  39.4 0.0 copy-done
  39.4 0.5 %own_rows.1 = (f32[64,16,256]{2,1,0:T(8,128)S(1)}, f32[64,16,256]{2,1,0:T(8,128)S(1)}) custom-call(f32[8,256]{1,0:T(8,128)S(1)} %get-tuple-element.51.keep_ref, f32[8,256]{1,0:T(8,128)S(1)} %get-tuple-element.83.norm_ref, f32[8,256]{1,0:T(8,128)S(1)} %collective-permute-done.12.norm_other_ref, f32[8,256]{1,0:T(8,128)S(1)} %residual_high.1.share_ref.refs_0_, ...), custom_call_target="tpu_custom_call" | custom-call | flops 20971 | bytes 41943 | tf_op jit(solution)/shard_map/own_rows/pallas_call | solution.py:750
  39.8 1.5 %collective-permute-done.15.refs_2_ = f32[8,256]{1,0:T(8,128)S(1)} collective-permute-done((f32[8,256]{1,0:T(8,128)S(1)}, f32[8,256]{1,0:T(8,128)S(1)}, u32[]{:S(2)}, u32[]{:S(2)}) %collective-permute-start.15) | collective-permute-done | bytes 8224 | tf_op jit(solution)/shard_map/ppermute | solution.py:505
  41.3 0.0 collective-permute-start.17
  41.3 0.0 collective-permute-done.16.refs_1_
  41.3 1.2 %collective-permute-done.17.refs_3_ = f32[8,256]{1,0:T(8,128)S(1)} collective-permute-done((f32[8,256]{1,0:T(8,128)S(1)}, f32[8,256]{1,0:T(8,128)S(1)}, u32[]{:S(2)}, u32[]{:S(2)}) %collective-permute-start.17) | collective-permute-done | bytes 8224 | tf_op jit(solution)/shard_map/ppermute | solution.py:492
  42.5 1.3 %finish.1 = (f32[64,16,256]{2,1,0:T(8,128)}, f32[1]{0:T(128)}) custom-call(f32[64,16,256]{2,1,0:T(8,128)S(1)} %get-tuple-element.94.vector_ref, f32[64,16,256]{2,1,0:T(8,128)S(1)} %get-tuple-element.96.residual_ref, f32[8,256]{1,0:T(8,128)S(1)} %residual_high.1.share_ref.refs_0_, f32[8,256]{1,0:T(8,128)S(1)} %collective-permute-done.16.refs_1_, ...), custom_call_target="tpu_custom_call" | custom-call | flops 7864 | bytes 31457 | tf_op jit(solution)/shard_map/finish/pallas_call | solution.py:763
  (1 shorter events, 0.0 us)
Async XLA Ops:
  2.7 4.4 %collective-permute-start = (bf16[33,16,256]{2,1,0:T(8,128)(2,1)S(1)}, bf16[33,16,256]{2,1,0:T(8,128)(2,1)S(1)}, u32[]{:S(2)}, u32[]{:S(2)}) collective-permute-start(bf16[33,16,256]{2,1,0:T(8,128)(2,1)S(1)} %get-tuple-element.53.chunk_ref.refs_0_), channel_id=1, source_target_pairs={{0,1},{1,0},{2,3},{3,2},{4,5},{5,4},{6,7},{7,6},{8,9},{9,8},{10,11... | collective-permute-start | bytes 811016 | tf_op jit(solution)/shard_map/ppermute | solution.py:492
  3.2 9.9 %collective-permute-start.2 = (bf16[33,16,256]{2,1,0:T(8,128)(2,1)S(1)}, bf16[33,16,256]{2,1,0:T(8,128)(2,1)S(1)}, u32[]{:S(2)}, u32[]{:S(2)}) collective-permute-start(bf16[33,16,256]{2,1,0:T(8,128)(2,1)S(1)} %get-tuple-element.53.chunk_ref.refs_0_), channel_id=1, source_target_pairs={{0,2},{1,3},{2,0},{3,1},{4,6},{5,7},{6,4},{7,5},{8,10},{9,11},{10,... | collective-permute-start | bytes 811016 | tf_op jit(solution)/shard_map/ppermute | solution.py:495
  5.8 9.1 %collective-permute-start.7 = (bf16[784,128]{1,0:T(8,128)(2,1)S(1)}, bf16[784,128]{1,0:T(8,128)(2,1)S(1)}, u32[]{:S(2)}, u32[]{:S(2)}) collective-permute-start(bf16[784,128]{1,0:T(8,128)(2,1)S(1)} %get-tuple-element.61), channel_id=1, source_target_pairs={{4,0},{8,4},{12,8},{16,12},{20,16},{24,20},{28,24},{5,1},{9,5},{13... | collective-permute-start | bytes 602120 | tf_op jit(solution)/shard_map/ppermute | solution.py:564
  8.4 1.4 %collective-permute-start.4 = (bf16[16,16,256]{2,1,0:T(8,128)(2,1)S(1)}, bf16[16,16,256]{2,1,0:T(8,128)(2,1)S(1)}, u32[]{:S(2)}, u32[]{:S(2)}) collective-permute-start(bf16[16,16,256]{2,1,0:T(8,128)(2,1)S(1)} %get-tuple-element.55.refs_2_), channel_id=1, source_target_pairs={{0,1},{1,0},{2,3},{3,2},{4,5},{5,4},{6,7},{7,6},{8,9},{9,8},{10,11... | collective-permute-start | bytes 393224 | tf_op jit(solution)/shard_map/ppermute | solution.py:492
  8.6 2.8 %collective-permute-start.3 = (bf16[16,16,256]{2,1,0:T(8,128)(2,1)S(1)}, bf16[16,16,256]{2,1,0:T(8,128)(2,1)S(1)}, u32[]{:S(2)}, u32[]{:S(2)}) collective-permute-start(bf16[16,16,256]{2,1,0:T(8,128)(2,1)S(1)} %get-tuple-element.56.refs_1_), channel_id=1, source_target_pairs={{0,1},{1,0},{2,3},{3,2},{4,5},{5,4},{6,7},{7,6},{8,9},{9,8},{10,11... | collective-permute-start | bytes 393224 | tf_op jit(solution)/shard_map/ppermute | solution.py:492
  9.0 6.9 %collective-permute-start.6 = (bf16[16,16,256]{2,1,0:T(8,128)(2,1)S(1)}, bf16[16,16,256]{2,1,0:T(8,128)(2,1)S(1)}, u32[]{:S(2)}, u32[]{:S(2)}) collective-permute-start(bf16[16,16,256]{2,1,0:T(8,128)(2,1)S(1)} %get-tuple-element.56.refs_1_), channel_id=1, source_target_pairs={{0,2},{1,3},{2,0},{3,1},{4,6},{5,7},{6,4},{7,5},{8,10},{9,11},{10,... | collective-permute-start | bytes 393224 | tf_op jit(solution)/shard_map/ppermute | solution.py:495
  9.8 10.4 %collective-permute-start.1 = (bf16[16,16,256]{2,1,0:T(8,128)(2,1)S(1)}, bf16[16,16,256]{2,1,0:T(8,128)(2,1)S(1)}, u32[]{:S(2)}, u32[]{:S(2)}) collective-permute-start(bf16[16,16,256]{2,1,0:T(8,128)(2,1)S(1)} %get-tuple-element.55.refs_2_), channel_id=1, source_target_pairs={{0,2},{1,3},{2,0},{3,1},{4,6},{5,7},{6,4},{7,5},{8,10},{9,11},{10,... | collective-permute-start | bytes 393224 | tf_op jit(solution)/shard_map/ppermute | solution.py:495
  11.5 12.6 %collective-permute-start.10 = (bf16[784,128]{1,0:T(8,128)(2,1)S(1)}, bf16[784,128]{1,0:T(8,128)(2,1)S(1)}, u32[]{:S(2)}, u32[]{:S(2)}) collective-permute-start(bf16[784,128]{1,0:T(8,128)(2,1)S(1)} %get-tuple-element.77), channel_id=1, source_target_pairs={{0,2},{1,3},{2,0},{3,1},{4,6},{5,7},{6,4},{7,5},{8,10},{9,11},{10,... | collective-permute-start | bytes 602120 | tf_op jit(solution)/shard_map/ppermute | solution.py:495
  13.1 6.0 %collective-permute-start.5 = (bf16[33,16,256]{2,1,0:T(8,128)(2,1)S(1)}, bf16[33,16,256]{2,1,0:T(8,128)(2,1)S(1)}, u32[]{:S(2)}, u32[]{:S(2)}) collective-permute-start(bf16[33,16,256]{2,1,0:T(8,128)(2,1)S(1)} %collective-permute-done.2.chunk_ref.refs_0_), channel_id=1, source_target_pairs={{0,1},{1,0},{2,3},{3,2},{4,5},{5,4},{6,7},{7,6},{8,9},{9,8},{10,11... | collective-permute-start | bytes 811016 | tf_op jit(solution)/shard_map/ppermute | solution.py:492
  15.9 3.2 %collective-permute-start.8 = (bf16[16,16,256]{2,1,0:T(8,128)(2,1)S(1)}, bf16[16,16,256]{2,1,0:T(8,128)(2,1)S(1)}, u32[]{:S(2)}, u32[]{:S(2)}) collective-permute-start(bf16[16,16,256]{2,1,0:T(8,128)(2,1)S(1)} %collective-permute-done.6.refs_2_), channel_id=1, source_target_pairs={{0,1},{1,0},{2,3},{3,2},{4,5},{5,4},{6,7},{7,6},{8,9},{9,8},{10,11... | collective-permute-start | bytes 393224 | tf_op jit(solution)/shard_map/ppermute | solution.py:492
  15.9 11.2 %collective-permute-start.11 = (bf16[784,128]{1,0:T(8,128)(2,1)S(1)}, bf16[784,128]{1,0:T(8,128)(2,1)S(1)}, u32[]{:S(2)}, u32[]{:S(2)}) collective-permute-start(bf16[784,128]{1,0:T(8,128)(2,1)S(1)} %broadcast_select_fusion.packed_ref), channel_id=1, source_target_pairs={{0,2},{1,3},{2,0},{3,1},{4,6},{5,7},{6,4},{7,5},{8,10},{9,11},{10,... | collective-permute-start | bytes 602120 | tf_op jit(solution)/shard_map/ppermute | solution.py:495
  20.2 1.7 %collective-permute-start.9 = (bf16[16,16,256]{2,1,0:T(8,128)(2,1)S(1)}, bf16[16,16,256]{2,1,0:T(8,128)(2,1)S(1)}, u32[]{:S(2)}, u32[]{:S(2)}) collective-permute-start(bf16[16,16,256]{2,1,0:T(8,128)(2,1)S(1)} %collective-permute-done.1.refs_0_), channel_id=1, source_target_pairs={{0,1},{1,0},{2,3},{3,2},{4,5},{5,4},{6,7},{7,6},{8,9},{9,8},{10,11... | collective-permute-start | bytes 393224 | tf_op jit(solution)/shard_map/ppermute | solution.py:492
  26.7 1.8 %collective-permute-start.12 = (f32[8,256]{1,0:T(8,128)S(1)}, f32[8,256]{1,0:T(8,128)S(1)}, u32[]{:S(2)}, u32[]{:S(2)}) collective-permute-start(f32[8,256]{1,0:T(8,128)S(1)} %get-tuple-element.83.norm_ref), channel_id=1, source_target_pairs={{0,1},{1,0},{2,3},{3,2},{4,5},{5,4},{6,7},{7,6},{8,9},{9,8},{10,11... | collective-permute-start | bytes 24584 | tf_op jit(solution)/shard_map/ppermute | solution.py:492
  28.3 2.7 %collective-permute-start.13 = (bf16[8,256,256]{2,1,0:T(8,128)(2,1)S(1)}, bf16[8,256,256]{2,1,0:T(8,128)(2,1)S(1)}, u32[]{:S(2)}, u32[]{:S(2)}) collective-permute-start(bf16[8,256,256]{2,1,0:T(8,128)(2,1)S(1)} %get-tuple-element.88.low_ref.refs_0_), channel_id=1, source_target_pairs={{0,1},{1,0},{2,3},{3,2},{4,5},{5,4},{6,7},{7,6},{8,9},{9,8},{10,11... | collective-permute-start | bytes 3145736 | tf_op jit(solution)/shard_map/ppermute | solution.py:492
  29.6 3.2 %collective-permute-start.14 = (bf16[8,256,256]{2,1,0:T(8,128)(2,1)S(1)}, bf16[8,256,256]{2,1,0:T(8,128)(2,1)S(1)}, u32[]{:S(2)}, u32[]{:S(2)}) collective-permute-start(bf16[8,256,256]{2,1,0:T(8,128)(2,1)S(1)} %received_rights.3.high_ref.refs_2_), channel_id=1, source_target_pairs={{0,1},{1,0},{2,3},{3,2},{4,5},{5,4},{6,7},{7,6},{8,9},{9,8},{10,11... | collective-permute-start | bytes 3145736 | tf_op jit(solution)/shard_map/ppermute | solution.py:492
  32.8 6.6 %copy-start = (f32[1,64,16,256]{3,2,1,0:T(8,128)S(1)}, f32[1,64,16,256]{3,2,1,0:T(8,128)}, u32[]{:S(2)}) copy-start(f32[1,64,16,256]{3,2,1,0:T(8,128)} %param.5) | copy-start | bytes 3145732
  37.6 3.7 %collective-permute-start.15 = (f32[8,256]{1,0:T(8,128)S(1)}, f32[8,256]{1,0:T(8,128)S(1)}, u32[]{:S(2)}, u32[]{:S(2)}) collective-permute-start(f32[8,256]{1,0:T(8,128)S(1)} %residual_high.1.share_ref.refs_0_), channel_id=1, source_target_pairs={{0,2},{1,3},{2,0},{3,1},{4,6},{5,7},{6,4},{7,5},{8,10},{9,11},{10,... | collective-permute-start | bytes 24584 | tf_op jit(solution)/shard_map/ppermute | solution.py:505
  39.4 1.9 %collective-permute-start.16 = (f32[8,256]{1,0:T(8,128)S(1)}, f32[8,256]{1,0:T(8,128)S(1)}, u32[]{:S(2)}, u32[]{:S(2)}) collective-permute-start(f32[8,256]{1,0:T(8,128)S(1)} %residual_high.1.share_ref.refs_0_), channel_id=1, source_target_pairs={{0,1},{1,0},{2,3},{3,2},{4,5},{5,4},{6,7},{7,6},{8,9},{9,8},{10,11... | collective-permute-start | bytes 24584 | tf_op jit(solution)/shard_map/ppermute | solution.py:492
  41.3 1.2 %collective-permute-start.17 = (f32[8,256]{1,0:T(8,128)S(1)}, f32[8,256]{1,0:T(8,128)S(1)}, u32[]{:S(2)}, u32[]{:S(2)}) collective-permute-start(f32[8,256]{1,0:T(8,128)S(1)} %collective-permute-done.15.refs_2_), channel_id=1, source_target_pairs={{0,1},{1,0},{2,3},{3,2},{4,5},{5,4},{6,7},{7,6},{8,9},{9,8},{10,11... | collective-permute-start | bytes 24584 | tf_op jit(solution)/shard_map/ppermute | solution.py:492
